TPU v7x, 32 devices: a whole 2x2x4 slice. The times are simulated.
32 devices in a mesh: dom: 4 (over z), four: 8 (over y, x, core).
Axes of the slice: x: 2, y: 2, z: 4, core: 2. Of those that a mesh axis runs over, the one named last changes fastest.
Arguments:
- adjoint: float32 [3, 256, 64, 1024], P(None, 'four', None, 'dom'), may hold values from -6 to 6
- base_bank: float32 [4, 2, 64, 1024], P(None, None, None, 'dom'), may hold values from -6 to 6
- snapshot: int32 [1024], P('dom'), may hold values from 0 to 3
- geometry: float32 [2, 1024], P(None, 'dom'), may hold values from 0.5 to 4
- diff_r: float32 [64, 64], replicated, may hold values from -0.75 to 0.75
- diff_s: float32 [64, 64], replicated, may hold values from -0.75 to 0.75
- stiffness: float32 [64, 64], replicated, as said below
- upper_list: int32 [4, 512], P('dom'), may hold values from 7 to 16383, as said below
- lower_list: int32 [4, 512], P('dom'), may hold values from 0 to 14591, as said below
Outputs:
- advanced: float32 [3, 256, 64, 1024], P(None, 'four', None, 'dom')
Inputs may be any that keep to these rules, and one draw needn't show every extreme that they name: `upper_list`: row p lists 64 distinct elements e of partition p, each with its eight nodes n = 8 s + 7, s = 0 .. 7, as n * 256 + e; element 256 - 1 is always among them. `lower_list`: row p lists 64 distinct elements e of partition p, each with its eight nodes n = 8 s, s = 0 .. 7, as n * 256 + e; elements 0 and 255 are always among them. `stiffness`: Symmetric. An off-diagonal entry (n, m) is negative where n and m lie on one line of the 8 x 8 node grid (n // 8 == m // 8 or n % 8 == m % 8) and zero elsewhere; the off-diagonal magnitudes of each row sum to less than its diagonal entry, which is positive.
All inputs are finite; a program needn't handle non-finite values.
Results may differ from a plain program's by a relative error of at most 0.0001.
Values sent between devices are 32-bit elements; how exact they have to be, the bound alone decides.
No kernel may reach another device: no remote copies, remote signals or barrier semaphores. Data moves between devices by JAX's collectives and lax.ppermute only.
A program may use at most 128 MiB of HBM per device.

v0:
```python
import math

import jax
import jax.numpy as jnp
from jax import lax
from jax.sharding import PartitionSpec as P

PLANES = 256
SWEEPS = 6


HIGHEST = lax.Precision.HIGHEST
PENALTY = 0.5
RELAXATION = 0.8
TIME_STEP = 0.2
INTERACTION = 2.0


def with_halo(x, sides, width):
    for axis, dim in sides:
        peers, length = (lax.axis_size(axis), x.shape[dim])
        up = [(i, (i + 1) % peers) for i in range(peers)]
        down = [(j, i) for i, j in up]
        last = lax.slice_in_dim(x, length - width, length, axis=dim)
        first = lax.slice_in_dim(x, 0, width, axis=dim)
        before = lax.ppermute(last, axis, up)
        after = lax.ppermute(first, axis, down)
        x = jnp.concatenate([before, x, after], axis=dim)
    return x


def along_nodes(matrix, field):
    return jnp.einsum("mn,...ne->...me", matrix, field, precision=HIGHEST)


def pick_base(base_bank, snapshot):
    levels = lax.iota(jnp.int32, base_bank.shape[0])
    chosen = (snapshot[None, :] == levels[:, None]).astype(base_bank.dtype)
    return jnp.sum(chosen[:, None, None, :] * base_bank, 0)


def advect(velocity, base_flow, grad_x, grad_y, diff_r, diff_s, scale_r, scale_s):
    slope_x = scale_r * along_nodes(diff_r, velocity)
    slope_y = scale_s * along_nodes(diff_s, velocity)
    transport = base_flow[0] * slope_x + base_flow[1] * slope_y
    product_x = velocity[0] * grad_x[0] + velocity[1] * grad_x[1]
    product_y = velocity[0] * grad_y[0] + velocity[1] * grad_y[1]
    return jnp.stack([product_x - transport[0], product_y - transport[1], -transport[2]])


def coef_table(length):
    row_index = lax.iota(jnp.int32, length)
    column_index = lax.iota(jnp.int32, length)
    phase = row_index[:, None] // 2 * column_index[None, :] % length
    angle = phase.astype(jnp.float32) * (2.0 * math.pi / length)
    weights_table = jnp.where(
        row_index[:, None] % 2 == 1, jnp.sin(angle), jnp.cos(angle)
    ) * math.sqrt(2.0 / length)
    alternate = jnp.where(column_index % 2 == 0, 1.0, -1.0).astype(jnp.float32) / math.sqrt(length)
    weights_table = weights_table.at[0].set(
        jnp.full((length,), 1.0 / math.sqrt(length), jnp.float32)
    )
    return weights_table.at[1].set(alternate)


def spectral(columns):
    weights_table = coef_table(columns.shape[1])
    coefficients = jnp.einsum("cj,fjne->fcne", weights_table, columns, precision=HIGHEST)
    return lax.all_to_all(coefficients, "four", split_axis=1, concat_axis=2, tiled=True)


def derivative_z(field, waves):
    lead = field.shape[0]
    pairs = field.reshape((lead // 2, 2) + field.shape[1:])
    factor = waves[:, None, None]
    return jnp.stack([factor * pairs[:, 1], -factor * pairs[:, 0]], 1).reshape(field.shape)


def face_penalty(field, upper_idx, lower_idx):
    planes_dev, nodes, elements = field.shape
    flat_field = field.reshape(planes_dev, nodes * elements)
    upper_vals = flat_field[:, upper_idx]
    lower_vals = flat_field[:, lower_idx]
    extended = with_halo(jnp.stack([lower_vals, upper_vals]), (("dom", 0),), 1)
    penalty = jnp.zeros_like(flat_field).at[:, upper_idx].add(PENALTY * (upper_vals - extended[3]))
    penalty = penalty.at[:, lower_idx].add(PENALTY * (lower_vals - extended[0]))
    return penalty.reshape(field.shape)


def per_device(
    adjoint, base_bank, snapshot, geometry, diff_r, diff_s, stiffness, upper_list, lower_list
):
    planes_dev = adjoint.shape[1]
    nodes = adjoint.shape[2]
    elements = adjoint.shape[3]
    base_flow = pick_base(base_bank, snapshot)
    scale_r = geometry[0]
    scale_s = geometry[1]
    grad_x = scale_r * along_nodes(diff_r, base_flow)
    grad_y = scale_s * along_nodes(diff_s, base_flow)
    rates = advect(adjoint, base_flow, grad_x, grad_y, diff_r, diff_s, scale_r, scale_s)
    stacked = spectral(
        lax.all_to_all(
            jnp.concatenate([adjoint, rates], 0), "four", split_axis=2, concat_axis=1, tiled=True
        )
    )
    spectra = stacked[:3]
    spectral_rates = stacked[3:]
    beta = 4.0 / PLANES
    position = lax.axis_index("four")
    pair_index = position * (planes_dev // 2) + lax.iota(jnp.int32, planes_dev // 2)
    waves = beta * pair_index.astype(jnp.float32)
    coef_index = position * planes_dev + lax.iota(jnp.int32, planes_dev)
    wave_number = jnp.where(coef_index == 1, PLANES // 2, coef_index // 2).astype(jnp.float32)
    shift = (beta * wave_number) ** 2
    source = -(scale_r * along_nodes(diff_r, spectra[2])) + derivative_z(spectra[0], waves)
    mass = 1.0 / (scale_r * scale_s)
    upper_idx = upper_list[0]
    lower_idx = lower_list[0]
    ones_flat = (
        jnp.zeros((nodes * elements,), jnp.float32).at[upper_idx].add(1.0).at[lower_idx].add(1.0)
    )
    shifted_mass = shift[:, None, None] * mass[None, None, :]
    diagonal_part = (
        jnp.diagonal(stiffness)[None, :, None]
        + shifted_mass
        + PENALTY * ones_flat.reshape(nodes, elements)[None]
    )
    potential = RELAXATION * source / diagonal_part
    for sweep_index in range(SWEEPS - 1):
        applied = along_nodes(stiffness, potential) + shifted_mass * potential
        applied = applied + face_penalty(potential, upper_idx, lower_idx)
        potential = potential + RELAXATION * (source - applied) / diagonal_part
    force_x = derivative_z(potential, waves) - spectra[0]
    force_z = -(scale_r * along_nodes(diff_r, potential)) - spectra[2]
    advanced_x = spectra[0] + TIME_STEP * (spectral_rates[0] + INTERACTION * force_x)
    advanced_y = spectra[1] + TIME_STEP * (spectral_rates[1] + INTERACTION * 0.0)
    advanced_z = spectra[2] + TIME_STEP * (spectral_rates[2] + INTERACTION * force_z)
    return jnp.stack([advanced_x, advanced_y, advanced_z])


def solution(mesh):
    in_specs = (
        P(None, "four", None, "dom"),
        P(None, None, None, "dom"),
        P("dom"),
        P(None, "dom"),
        P(),
        P(),
        P(),
        P("dom", None),
        P("dom", None),
    )
    out_specs = P(None, "four", None, "dom")
    return jax.shard_map(
        per_device, mesh=mesh, in_specs=in_specs, out_specs=out_specs, check_vma=False
    )
```

profile of v0, /device:TPU:0, one launch (start us, length us, event | category | flops | bytes accessed | tf_op | source)
XLA Modules:
  0.0 685.8 jit_solution(3767072238360900375)
XLA Ops:
  2.6 6.6 copy.78
  9.2 6.4 fusion.122
  16.2 7.8 %fusion.2 = f32[3,32,64,256]{3,2,1,0:T(8,128)S(1)} fusion(f32[3,32,256,64]{2,3,1,0:T(8,128)S(1)} %fusion.122, f32[256]{0:T(256)S(1)} %bitcast.417, f32[64,256]{1,0:T(8,128)S(1)} %get-tuple-element.46, f32[256]{0:T(256)S(1)} %bitcast.412, f32[64,256]{1,0:T(8,128)S(1)} %get-tuple-element.45, f32[3,32,64,256]{3,2,1,0:T(8,128)S(1)} %bitcast.379, ...), kind=kOutput, calls=%fused_computation.28 | convolution fusion | flops 1215823872 | bytes 19023872 | tf_op jit(solution)/shard_map/mn,...ne->...me/dot_general | solution.py:33
  33.0 5.0 pad_maximum_fusion
  38.0 5.3 all-to-all-start
  44.8 138.2 %all-to-all-done = f32[6,32,64,256]{3,1,0,2:T(8,128)} async-done(((f32[6,32,64,256]{3,1,0,2:T(8,128)}), f32[6,32,64,256]{3,1,0,2:T(8,128)}, u32[]{:S(2)}, u32[]{:S(2)}) %all-to-all-start) | async-done | bytes 12582944 | tf_op jit(solution)/shard_map/all_to_all | solution.py:103
  183.0 21.7 %copy.83 = f32[6,8,32,8,256]{4,3,2,1,0:T(8,128)} copy(f32[6,8,32,8,256]{4,2,0,3,1:T(8,128)} %bitcast.20) | data formatting | bytes 25165824 | tf_op jit(solution)/shard_map/all_to_all | solution.py:103
  204.6 27.0 %fusion.3 = f32[6,256,8,256]{1,3,2,0:T(8,128)} fusion(f32[6,256,8,256]{3,2,1,0:T(8,128)} %bitcast.380, f32[256,256]{1,0:T(8,128)S(1)} %scatter.9), kind=kOutput, calls=%fused_computation.30 | convolution fusion | flops 9663676416 | bytes 25427968 | tf_op jit(solution)/shard_map/cj,fjne->fcne/dot_general | solution.py:68
  231.6 12.8 %copy.85 = f32[6,256,8,256]{3,2,0,1:T(8,128)} copy(f32[6,256,8,256]{1,3,2,0:T(8,128)} %fusion.3) | data formatting | bytes 25165824 | tf_op jit(solution)/shard_map/cj,fjne->fcne/transpose | solution.py:68
  244.4 5.7 all-to-all-start.1
  257.9 131.2 %all-to-all-done.1 = f32[6,256,8,256]{3,2,0,1:T(8,128)} async-done(((f32[6,256,8,256]{3,2,0,1:T(8,128)}), f32[6,256,8,256]{3,2,0,1:T(8,128)}, u32[]{:S(2)}, u32[]{:S(2)}) %all-to-all-start.1) | async-done | bytes 12582944 | tf_op jit(solution)/shard_map/all_to_all | solution.py:69
  389.1 10.4 %copy.86 = f32[6,256,8,256]{3,2,1,0:T(8,128)} copy(f32[6,256,8,256]{3,2,0,1:T(8,128)} %all-to-all-done.1) | data formatting | bytes 25165824 | tf_op jit(solution)/shard_map/all_to_all | solution.py:69
  399.5 7.8 %fusion.141 = (f32[1,32,8,8,256]{4,3,1,2,0:T(8,128)}, f32[1,32,8,8,256]{4,3,1,2,0:T(8,128)}, f32[1,32,8,8,256]{4,3,1,2,0:T(8,128)}, f32[1,32,8,8,256]{4,3,1,2,0:T(8,128)S(1)}, f32[1,32,8,8,256]{4,3,1,2,0:T(8,128)S(1)}) fusion(f32[6,32,8,8,256]{4,3,1,2,0:T(8,128)} %bitcast.381), kind=kLoop, calls=%fused_computation.219 | loop fusion | flops 1048576 | bytes 23068672 | tf_op jit(solution)/shard_map/slice | solution.py:136
  408.7 4.5 fusion.53
  413.2 6.3 copy.117
  423.9 4.5 collective-permute-start
  428.4 4.4 gather_fusion.1
  434.8 6.0 scatter_custom_fusion.2
  441.0 9.8 %scatter_custom_fusion.3 = f32[32,16384]{0,1:T(8,128)} fusion(f32[32,16384]{0,1:T(8,128)} %scatter_custom_fusion.2, s32[512]{0:T(512)S(1)} %bitcast.421, f32[1,32,512]{1,2,0:T(8,128)S(1)} %collective-permute-done.1, f32[512,32]{1,0:T(8,128)S(1)} %gather_fusion.2, f32[]{:T(128)} %constant.163.clone.1), kind=kCustom, calls=%fused_computation.148 | custom fusion | flops 49152 | bytes 2621952 | tf_op jit(solution)/shard_map/scatter-add | solution.py:86
  450.9 6.5 copy.112
  457.3 7.5 %fusion.50 = f32[32,64,256]{2,1,0:T(8,128)} fusion(f32[32,64,256]{2,1,0:T(8,128)} %get-tuple-element.50, f32[32,64,256]{2,1,0:T(8,128)} %copy.112, f32[64,256]{1,0:T(8,128)S(1)} %mul.432, f32[32,256]{1,0:T(8,128)S(1)} %broadcast_multiply_fusion.1, f32[64]{0:T(128)S(1)} %gather_fusion, f32[64,64]{1,0:T(8,128)S(1)} %copy-done.1), kind=kOutput, calls=%fused_computation.88 | convolution fusion | flops 410517504 | bytes 6406400 | tf_op jit(solution)/shard_map/mn,...ne->...me/dot_general | solution.py:33
  464.8 6.3 copy.118
  475.5 4.4 gather_fusion.3
  487.9 6.0 scatter_custom_fusion.4
  493.9 9.6 %scatter_custom_fusion.5 = f32[32,16384]{0,1:T(8,128)} fusion(f32[32,16384]{0,1:T(8,128)} %scatter_custom_fusion.4, s32[512]{0:T(512)S(1)} %bitcast.422, f32[1,32,512]{1,2,0:T(8,128)S(1)} %collective-permute-done.3, f32[512,32]{1,0:T(8,128)S(1)} %gather_fusion.4, f32[]{:T(128)} %constant.163.clone.1), kind=kCustom, calls=%fused_computation.139 | custom fusion | flops 49152 | bytes 2621952 | tf_op jit(solution)/shard_map/scatter-add | solution.py:86
  503.6 6.9 copy.113
  510.4 7.4 %fusion.45 = f32[32,64,256]{2,1,0:T(8,128)} fusion(f32[32,64,256]{2,1,0:T(8,128)} %fusion.50, f32[32,64,256]{2,1,0:T(8,128)} %get-tuple-element.50, f32[32,64,256]{2,1,0:T(8,128)} %copy.113, f32[64,256]{1,0:T(8,128)S(1)} %mul.432, f32[32,256]{1,0:T(8,128)S(1)} %broadcast_multiply_fusion.1, f32[64]{0:T(128)S(1)} %gather_fusion, f32[64,64]{1,0:T(8,128)S(1)} %copy-done.1), kind=kOutput, calls=%fused_computation.82 | convolution fusion | flops 407371776 | bytes 8503552 | tf_op jit(solution)/shard_map/mn,...ne->...me/dot_general | solution.py:33
  517.8 6.3 copy.119
  528.5 4.4 gather_fusion.5
  532.9 4.4 collective-permute-start.4
  541.3 6.0 scatter_custom_fusion.6
  547.2 9.6 %scatter_custom_fusion.7 = f32[32,16384]{0,1:T(8,128)} fusion(f32[32,16384]{0,1:T(8,128)} %scatter_custom_fusion.6, s32[512]{0:T(512)S(1)} %bitcast.423, f32[1,32,512]{1,2,0:T(8,128)S(1)} %collective-permute-done.5, f32[512,32]{1,0:T(8,128)S(1)} %gather_fusion.6, f32[]{:T(128)} %constant.163.clone.1), kind=kCustom, calls=%fused_computation.130 | custom fusion | flops 49152 | bytes 2621952 | tf_op jit(solution)/shard_map/scatter-add | solution.py:86
  556.9 6.6 copy.114
  563.5 7.4 %fusion.40 = f32[32,64,256]{2,1,0:T(8,128)} fusion(f32[32,64,256]{2,1,0:T(8,128)} %fusion.45, f32[32,64,256]{2,1,0:T(8,128)} %get-tuple-element.50, f32[32,64,256]{2,1,0:T(8,128)} %copy.114, f32[64,256]{1,0:T(8,128)S(1)} %mul.432, f32[32,256]{1,0:T(8,128)S(1)} %broadcast_multiply_fusion.1, f32[64]{0:T(128)S(1)} %gather_fusion, f32[64,64]{1,0:T(8,128)S(1)} %copy-done.1), kind=kOutput, calls=%fused_computation.76 | convolution fusion | flops 407371776 | bytes 8503552 | tf_op jit(solution)/shard_map/mn,...ne->...me/dot_general | solution.py:33
  570.9 6.3 copy.120
  581.6 4.4 gather_fusion.7
  586.0 4.4 collective-permute-start.6
  594.4 6.0 scatter_custom_fusion.8
  600.4 9.6 %scatter_custom_fusion.9 = f32[32,16384]{0,1:T(8,128)} fusion(f32[32,16384]{0,1:T(8,128)} %scatter_custom_fusion.8, s32[512]{0:T(512)S(1)} %bitcast.424, f32[1,32,512]{1,2,0:T(8,128)S(1)} %collective-permute-done.7, f32[512,32]{1,0:T(8,128)S(1)} %gather_fusion.8, f32[]{:T(128)} %constant.163.clone.1), kind=kCustom, calls=%fused_computation.121 | custom fusion | flops 49152 | bytes 2621952 | tf_op jit(solution)/shard_map/scatter-add | solution.py:86
  610.0 6.7 copy.115
  616.6 7.3 %fusion.35 = f32[32,64,256]{2,1,0:T(8,128)} fusion(f32[32,64,256]{2,1,0:T(8,128)} %fusion.40, f32[32,64,256]{2,1,0:T(8,128)} %get-tuple-element.50, f32[32,64,256]{2,1,0:T(8,128)} %copy.115, f32[64,256]{1,0:T(8,128)S(1)} %mul.432, f32[32,256]{1,0:T(8,128)S(1)} %broadcast_multiply_fusion.1, f32[64]{0:T(128)S(1)} %gather_fusion, f32[64,64]{1,0:T(8,128)S(1)} %copy-done.1), kind=kOutput, calls=%fused_computation.70 | convolution fusion | flops 407371776 | bytes 8503552 | tf_op jit(solution)/shard_map/mn,...ne->...me/dot_general | solution.py:33
  624.0 6.3 copy.121
  634.7 4.4 gather_fusion.9
  639.1 4.4 collective-permute-start.8
  647.5 6.0 scatter_custom_fusion.10
  653.4 9.6 %scatter_custom_fusion.11 = f32[32,16384]{0,1:T(8,128)} fusion(f32[32,16384]{0,1:T(8,128)} %scatter_custom_fusion.10, s32[512]{0:T(512)S(1)} %bitcast.425, f32[1,32,512]{1,2,0:T(8,128)S(1)} %collective-permute-done.9, f32[512,32]{1,0:T(8,128)S(1)} %gather_fusion.10, f32[]{:T(128)} %constant.163.clone.1), kind=kCustom, calls=%fused_computation.112 | custom fusion | flops 49152 | bytes 2621952 | tf_op jit(solution)/shard_map/scatter-add | solution.py:86
  663.1 6.7 copy.116
  669.8 6.2 fusion.30
  (90 shorter events, 75.7 us)
Async XLA Ops:
  0.0 9.2 %copy-start = (f32[64,64]{1,0:T(8,128)S(1)}, f32[64,64]{1,0:T(8,128)}, u32[]{:S(2)}) copy-start(f32[64,64]{1,0:T(8,128)} %param.17) | copy-start | bytes 49156
  2.5 6.6 slice-start
  2.6 6.6 slice-start.1
  9.2 6.7 copy-start.8
  27.5 3.0 copy-start.6
  38.0 145.0 %all-to-all-start = ((f32[6,32,64,256]{3,1,0,2:T(8,128)}), f32[6,32,64,256]{3,1,0,2:T(8,128)}, u32[]{:S(2)}, u32[]{:S(2)}) async-start(f32[6,32,64,256]{3,1,0,2:T(8,128)} %pad_maximum_fusion), calls=%async_computation | async-start | bytes 25165824 | tf_op jit(solution)/shard_map/all_to_all | solution.py:103
  244.4 5.7 copy-start.9
  244.4 9.0 %copy-start.10 = (s32[1,512]{1,0:T(1,128)S(1)}, s32[1,512]{1,0:T(1,128)}, u32[]{:S(2)}) copy-start(s32[1,512]{1,0:T(1,128)} %param.21) | copy-start | bytes 6148
  244.4 144.7 %all-to-all-start.1 = ((f32[6,256,8,256]{3,2,0,1:T(8,128)}), f32[6,256,8,256]{3,2,0,1:T(8,128)}, u32[]{:S(2)}, u32[]{:S(2)}) async-start(f32[6,256,8,256]{3,2,0,1:T(8,128)} %copy.85), calls=%async_computation.1 | async-start | bytes 25165824 | tf_op jit(solution)/shard_map/all_to_all | solution.py:69
  253.5 3.5 copy-start.1
  407.3 1.4 copy-start.4
  423.9 10.9 %collective-permute-start = (f32[1,32,512]{1,2,0:T(8,128)S(1)}, f32[1,32,512]{1,2,0:T(8,128)S(1)}, u32[]{:S(2)}, u32[]{:S(2)}) collective-permute-start(f32[1,32,512]{1,2,0:T(8,128)S(1)} %bitcast.402), channel_id=1, source_target_pairs={{8,0},{16,8},{24,16},{0,24},{9,1},{17,9},{25,17},{1,25},{10,2},{18... | collective-permute-start | bytes 196616 | tf_op jit(solution)/shard_map/ppermute | solution.py:27
  432.8 8.2 %collective-permute-start.1 = (f32[1,32,512]{1,2,0:T(8,128)S(1)}, f32[1,32,512]{1,2,0:T(8,128)S(1)}, u32[]{:S(2)}, u32[]{:S(2)}) collective-permute-start(f32[1,32,512]{1,2,0:T(8,128)S(1)} %bitcast.410), channel_id=1, source_target_pairs={{0,8},{8,16},{16,24},{24,0},{1,9},{9,17},{17,25},{25,1},{2,10},{10... | collective-permute-start | bytes 196616 | tf_op jit(solution)/shard_map/ppermute | solution.py:26
  479.9 8.0 %collective-permute-start.2 = (f32[1,32,512]{1,2,0:T(8,128)S(1)}, f32[1,32,512]{1,2,0:T(8,128)S(1)}, u32[]{:S(2)}, u32[]{:S(2)}) collective-permute-start(f32[1,32,512]{1,2,0:T(8,128)S(1)} %bitcast.403), channel_id=1, source_target_pairs={{8,0},{16,8},{24,16},{0,24},{9,1},{17,9},{25,17},{1,25},{10,2},{18... | collective-permute-start | bytes 196616 | tf_op jit(solution)/shard_map/ppermute | solution.py:27
  484.0 9.9 %collective-permute-start.3 = (f32[1,32,512]{1,2,0:T(8,128)S(1)}, f32[1,32,512]{1,2,0:T(8,128)S(1)}, u32[]{:S(2)}, u32[]{:S(2)}) collective-permute-start(f32[1,32,512]{1,2,0:T(8,128)S(1)} %bitcast.407), channel_id=1, source_target_pairs={{0,8},{8,16},{16,24},{24,0},{1,9},{9,17},{17,25},{25,1},{2,10},{10... | collective-permute-start | bytes 196616 | tf_op jit(solution)/shard_map/ppermute | solution.py:26
  532.9 8.3 %collective-permute-start.4 = (f32[1,32,512]{1,2,0:T(8,128)S(1)}, f32[1,32,512]{1,2,0:T(8,128)S(1)}, u32[]{:S(2)}, u32[]{:S(2)}) collective-permute-start(f32[1,32,512]{1,2,0:T(8,128)S(1)} %bitcast.404), channel_id=1, source_target_pairs={{8,0},{16,8},{24,16},{0,24},{9,1},{17,9},{25,17},{1,25},{10,2},{18... | collective-permute-start | bytes 196616 | tf_op jit(solution)/shard_map/ppermute | solution.py:27
  537.4 9.9 %collective-permute-start.5 = (f32[1,32,512]{1,2,0:T(8,128)S(1)}, f32[1,32,512]{1,2,0:T(8,128)S(1)}, u32[]{:S(2)}, u32[]{:S(2)}) collective-permute-start(f32[1,32,512]{1,2,0:T(8,128)S(1)} %bitcast.408), channel_id=1, source_target_pairs={{0,8},{8,16},{16,24},{24,0},{1,9},{9,17},{17,25},{25,1},{2,10},{10... | collective-permute-start | bytes 196616 | tf_op jit(solution)/shard_map/ppermute | solution.py:26
  586.0 8.3 %collective-permute-start.6 = (f32[1,32,512]{1,2,0:T(8,128)S(1)}, f32[1,32,512]{1,2,0:T(8,128)S(1)}, u32[]{:S(2)}, u32[]{:S(2)}) collective-permute-start(f32[1,32,512]{1,2,0:T(8,128)S(1)} %bitcast.405), channel_id=1, source_target_pairs={{8,0},{16,8},{24,16},{0,24},{9,1},{17,9},{25,17},{1,25},{10,2},{18... | collective-permute-start | bytes 196616 | tf_op jit(solution)/shard_map/ppermute | solution.py:27
  590.5 9.9 %collective-permute-start.7 = (f32[1,32,512]{1,2,0:T(8,128)S(1)}, f32[1,32,512]{1,2,0:T(8,128)S(1)}, u32[]{:S(2)}, u32[]{:S(2)}) collective-permute-start(f32[1,32,512]{1,2,0:T(8,128)S(1)} %bitcast.409), channel_id=1, source_target_pairs={{0,8},{8,16},{16,24},{24,0},{1,9},{9,17},{17,25},{25,1},{2,10},{10... | collective-permute-start | bytes 196616 | tf_op jit(solution)/shard_map/ppermute | solution.py:26
  639.1 8.3 %collective-permute-start.8 = (f32[1,32,512]{1,2,0:T(8,128)S(1)}, f32[1,32,512]{1,2,0:T(8,128)S(1)}, u32[]{:S(2)}, u32[]{:S(2)}) collective-permute-start(f32[1,32,512]{1,2,0:T(8,128)S(1)} %bitcast.401), channel_id=1, source_target_pairs={{8,0},{16,8},{24,16},{0,24},{9,1},{17,9},{25,17},{1,25},{10,2},{18... | collective-permute-start | bytes 196616 | tf_op jit(solution)/shard_map/ppermute | solution.py:27
  643.6 9.9 %collective-permute-start.9 = (f32[1,32,512]{1,2,0:T(8,128)S(1)}, f32[1,32,512]{1,2,0:T(8,128)S(1)}, u32[]{:S(2)}, u32[]{:S(2)}) collective-permute-start(f32[1,32,512]{1,2,0:T(8,128)S(1)} %bitcast.406), channel_id=1, source_target_pairs={{0,8},{8,16},{16,24},{24,0},{1,9},{9,17},{17,25},{25,1},{2,10},{10... | collective-permute-start | bytes 196616 | tf_op jit(solution)/shard_map/ppermute | solution.py:26
  669.8 6.2 copy-start.3
  669.8 6.2 copy-start.5
  678.7 1.6 copy-start.7
  680.3 1.6 copy-start.2
where the time goes:
time: 698 us; the launch traced here: 686 us
  waiting for transfers between devices  284 us (41%)
  local copies, waits for them, and re-layouts  174 us (25%)
  other arithmetic  109 us (16%)
  matrix products  84.7 us (12%)
  starting transfers between devices  33 us (5%)
    all_to_all x1, waiting for transfers between devices, per_device(): lax.all_to_all(jnp.concatenate([adjoint, rates], 0), 'four', split_axis=2...  138 us
    all_to_all x1, waiting for transfers between devices, spectral(): lax.all_to_all(coefficients, 'four', split_axis=1, concat_axis=2, tiled=T...  131 us
    dot_general x11, matrix products, along_nodes(): return jnp.einsum('mn,...ne->...me', matrix, field, precision=HIGHEST)  57.7 us
    scatter-add x5, other arithmetic, face_penalty(): penalty = penalty.at[:, lower_idx].add(PENALTY * (lower_vals - extended[0]))  48.3 us
    reshape x5, local copies, waits for them, and re-layouts, face_penalty(): return penalty.reshape(field.shape)  33.3 us
    reshape x5, local copies, waits for them, and re-layouts, face_penalty(): flat_field = field.reshape(planes_dev, nodes * elements)  31.5 us
    scatter-add x5, other arithmetic, face_penalty(): jnp.zeros_like(flat_field).at[:, upper_idx]  29.9 us
    dot_general x1, matrix products, spectral(): jnp.einsum('cj,fjne->fcne', weights_table, columns, precision=HIGHEST)  27 us
  transfers between devices with their start and end apart: 12, of which 8 were waited for; matrix products, arithmetic and copies ran while one was open for 7% of the time, Pallas kernels for 0%

commit v1 on v0

v1 whole, which is shorter than its diff:
```python
import functools
import math

import jax
import jax.numpy as jnp
import ml_dtypes
import numpy as np
from jax import lax
from jax.experimental import pallas as pl
from jax.experimental.pallas import tpu as pltpu
from jax.sharding import PartitionSpec as P

PLANES = 256
PENALTY = 0.5
RELAXATION = 0.8
TIME_STEP = 0.2
INTERACTION = 2.0
LINE = 8

F32 = jnp.float32
BF16 = jnp.bfloat16
VMEM_LIMIT = 48 * 1024 * 1024


def params():
    return pltpu.CompilerParams(vmem_limit_bytes=VMEM_LIMIT)


def cost(flops, moved):
    return pl.CostEstimate(flops=int(flops), bytes_accessed=int(moved), transcendentals=0)


def split(x):
    high = x.astype(BF16)
    low = (x - high.astype(F32)).astype(BF16)
    return high, low


def dot(a, b):
    return lax.dot_general(a, b, (((1,), (0,)), ((), ())), preferred_element_type=F32)


def pack_matrix(m):
    high, low = split(m)
    return jnp.concatenate([high, low, high], axis=1)


def pack_field(v):
    high, low = split(v)
    return jnp.concatenate([high, high, low], axis=0)


def coef_table(length):
    c = np.arange(length)[:, None]
    j = np.arange(length)[None, :]
    angle = ((c // 2) * j % length) * (2.0 * math.pi / length)
    table = np.where(c % 2 == 1, np.sin(angle), np.cos(angle)) * math.sqrt(2.0 / length)
    table[0] = 1.0 / math.sqrt(length)
    table[1] = np.where(np.arange(length) % 2 == 0, 1.0, -1.0) / math.sqrt(length)
    high = table.astype(ml_dtypes.bfloat16)
    low = (table - high.astype(np.float64)).astype(ml_dtypes.bfloat16)
    return np.concatenate([high, low], axis=0)


def transform_kernel(nodes, table_ref, x_ref, o_ref):
    planes = table_ref.shape[1]
    both = table_ref[...]
    high_table = both[:planes]
    for n in range(nodes):
        rows = pl.ds(n, planes, stride=nodes) if nodes > 1 else pl.ds(0, planes)
        high, low = split(x_ref[rows, :])
        wide = dot(both, high)
        o_ref[rows, :] = wide[:planes] + (wide[planes:] + dot(high_table, low))


def transform(columns, table):
    peers, per, nodes, elements = columns.shape
    rows = peers * per * nodes
    width = 128
    flat = columns.reshape(rows, elements)
    out = pl.pallas_call(
        functools.partial(transform_kernel, nodes),
        out_shape=jax.ShapeDtypeStruct((rows, elements), F32),
        grid=(elements // width,),
        in_specs=[
            pl.BlockSpec(table.shape, lambda i: (0, 0)),
            pl.BlockSpec((rows, width), lambda i: (0, i)),
        ],
        out_specs=pl.BlockSpec((rows, width), lambda i: (0, i)),
        compiler_params=params(),
        cost_estimate=cost(6 * PLANES * rows * elements, 8 * rows * elements),
        name="transform",
    )(table, flat)
    return out.reshape(columns.shape)


BXR, BYS, DXBX, DXBY, DYBX, DYBY, DIAG = range(7)


def prep_kernel(
    bank_ref, snap_ref, geo_ref, dr_ref, ds_ref, st_ref, up_ref, lo_ref,
    coef_ref, dpack_ref, spack_ref, gather_ref, scatter_ref, mask_ref,
):
    elements = geo_ref.shape[1]
    nodes = dr_ref.shape[0]
    snap = snap_ref[...]
    base = [
        sum(jnp.where(snap == k, bank_ref[k, i], 0.0) for k in range(bank_ref.shape[0]))
        for i in range(2)
    ]
    rx = geo_ref[0:1, :]
    sy = geo_ref[1:2, :]
    dpack = pack_matrix(jnp.concatenate([dr_ref[...], ds_ref[...]], axis=0))
    dpack_ref[...] = dpack
    bx = dot(dpack, pack_field(base[0]))
    by = dot(dpack, pack_field(base[1]))
    coef_ref[BXR] = base[0] * rx
    coef_ref[BYS] = base[1] * sy
    coef_ref[DXBX] = rx * bx[:nodes]
    coef_ref[DXBY] = rx * by[:nodes]
    coef_ref[DYBX] = sy * bx[nodes:]
    coef_ref[DYBY] = sy * by[nodes:]
    row = lax.broadcasted_iota(jnp.int32, (nodes, nodes), 0)
    col = lax.broadcasted_iota(jnp.int32, (nodes, nodes), 1)
    stiff = st_ref[...]
    spack_ref[...] = pack_matrix(jnp.where(row == col, 0.0, stiff))
    diag = jnp.sum(jnp.where(row == col, stiff, 0.0), axis=1, keepdims=True)
    coef_ref[DIAG] = jnp.broadcast_to(diag, (nodes, elements))
    shared = up_ref.shape[1]
    lines = nodes // LINE
    for side, (ref, first) in enumerate(((up_ref, LINE - 1), (lo_ref, 0))):
        index = ref[...]
        node = index // elements
        element = index - node * elements
        hot = lax.broadcasted_iota(jnp.int32, (elements, shared), 0) == element
        hot = jnp.where(hot, 1.0, 0.0)
        gather_ref[side] = hot.astype(BF16)
        back = hot.T.astype(BF16)
        scatter_ref[side] = back
        mask = lax.broadcasted_iota(jnp.int32, (lines, shared), 0) == node // LINE
        mask = jnp.where(mask, 1.0, 0.0)
        mask_ref[side] = mask
        count = dot(mask.astype(BF16), back)
        for s in range(lines):
            n = s * LINE + first
            coef_ref[DIAG, n : n + 1, :] = coef_ref[DIAG, n : n + 1, :] + PENALTY * count[s : s + 1]


def prepare(base_bank, snapshot, geometry, diff_r, diff_s, stiffness, upper, lower):
    nodes = diff_r.shape[0]
    elements = geometry.shape[1]
    shared = upper.shape[1]
    return pl.pallas_call(
        prep_kernel,
        out_shape=[
            jax.ShapeDtypeStruct((7, nodes, elements), F32),
            jax.ShapeDtypeStruct((2 * nodes, 3 * nodes), BF16),
            jax.ShapeDtypeStruct((nodes, 3 * nodes), BF16),
            jax.ShapeDtypeStruct((2, elements, shared), BF16),
            jax.ShapeDtypeStruct((2, shared, elements), BF16),
            jax.ShapeDtypeStruct((2, nodes // LINE, shared), F32),
        ],
        compiler_params=params(),
        cost_estimate=cost(1e7, 4e6),
        name="prepare",
    )(base_bank, snapshot.reshape(1, elements), geometry, diff_r, diff_s, stiffness, upper, lower)


def face_of(ref, side):
    rows, elements = ref.shape
    return ref.reshape(rows // LINE, LINE, elements).at[:, LINE - 1 if side == 0 else 0, :]


def gather_faces(side, fields, gather_ref, mask_ref):
    lines = mask_ref.shape[1]
    high, low = split(jnp.concatenate(fields, axis=0))
    rows = high.shape[0]
    both = dot(jnp.concatenate([high, low], axis=0), gather_ref[side])
    picked = both[:rows] + both[rows:]
    shared = picked.shape[1]
    return jnp.sum(picked.reshape(rows // lines, lines, shared) * mask_ref[side][None], axis=1)


def scatter_faces(side, values, scatter_ref, mask_ref):
    mask = mask_ref[side]
    coefs, shared = values.shape
    spread = (values[:, None, :] * mask[None]).reshape(coefs * mask.shape[0], shared)
    high, low = split(spread)
    rows = high.shape[0]
    both = dot(jnp.concatenate([high, low], axis=0), scatter_ref[side])
    return both[:rows] + both[rows:]


def local_sweep(pot, source, inverse, spack):
    applied = dot(spack, pack_field(pot))
    return (1.0 - RELAXATION) * pot + inverse * (source - applied)


def coef_block(coefs):
    return 8 if coefs % 8 == 0 else coefs


def start_kernel(
    block, pos_ref, z_ref, x_ref, geo_ref, diag_ref, dpack_ref, spack_ref, gather_ref, mask_ref,
    source_ref, inverse_ref, local_ref, up_ref, lo_ref, pot_ref,
):
    nodes, elements = diag_ref.shape[1:]
    beta = 4.0 / PLANES
    first = pos_ref[0] * (block * pl.num_programs(0)) + pl.program_id(0) * block
    rx = geo_ref[0:1, :]
    mass = 1.0 / (rx * geo_ref[1:2, :])
    diag = diag_ref[0]
    drpack = dpack_ref[:nodes]
    spack = spack_ref[...]
    for c in range(block):
        index = first + c
        wave = beta * (index // 2).astype(F32)
        shift = beta * jnp.where(index == 1, PLANES // 2, index // 2).astype(F32)
        shift = shift * shift
        z = z_ref[:, c].reshape(nodes, elements)
        other = x_ref[:, c + 1 if c % 2 == 0 else c - 1].reshape(nodes, elements)
        turned = (wave if c % 2 == 0 else -wave) * other
        source = turned - rx * dot(drpack, pack_field(z))
        inverse = RELAXATION / (diag + shift * mass)
        pot = inverse * source
        rows = pl.ds(c * nodes, nodes)
        source_ref[rows, :] = source
        inverse_ref[rows, :] = inverse
        pot_ref[rows, :] = pot
        local_ref[rows, :] = local_sweep(pot, source, inverse, spack)
    for side, out in ((0, up_ref), (1, lo_ref)):
        fields = [face_of(ref, side)[...] for ref in (pot_ref, local_ref, inverse_ref)]
        picked = gather_faces(side, fields, gather_ref, mask_ref)
        for k in range(3):
            out[k] = picked[k * block : (k + 1) * block]


def whole(shape):
    return pl.BlockSpec(shape, lambda *i: (0,) * len(shape))


SMEM_SPEC = pl.BlockSpec(memory_space=pltpu.SMEM)


def start_solve(position, z, x, geometry, coef, dpack, spack, gather, mask):
    groups, coefs, part, elements = z.shape
    nodes = groups * part
    shared = gather.shape[2]
    block = coef_block(coefs)
    field = pl.BlockSpec((groups, block, part, elements), lambda i: (0, i, 0, 0))
    flat = pl.BlockSpec((block * nodes, elements), lambda i: (i, 0))
    face = pl.BlockSpec((3, block, shared), lambda i: (0, i, 0))
    size = coefs * nodes * elements
    return pl.pallas_call(
        functools.partial(start_kernel, block),
        out_shape=[jax.ShapeDtypeStruct((coefs * nodes, elements), F32)] * 3
        + [jax.ShapeDtypeStruct((3, coefs, shared), F32)] * 2,
        grid=(coefs // block,),
        in_specs=[
            SMEM_SPEC, field, field, whole(geometry.shape),
            pl.BlockSpec((1, nodes, elements), lambda i: (DIAG, 0, 0)),
            whole(dpack.shape), whole(spack.shape), whole(gather.shape), whole(mask.shape),
        ],
        out_specs=[flat, flat, flat, face, face],
        scratch_shapes=[pltpu.VMEM((block * nodes, elements), F32)],
        compiler_params=params(),
        cost_estimate=cost(12 * nodes * size, 20 * size),
        name="start_solve",
    )(position, z, x, geometry, coef, dpack, spack, gather, mask)


def sweeps_kernel(
    block, keep, local_ref, source_ref, inverse_ref, own_up_ref, own_lo_ref,
    got_up_ref, got_lo_ref, inv_up_ref, inv_lo_ref, spack_ref, gather_ref, scatter_ref, mask_ref,
    next_ref, up_ref, lo_ref, pot_ref,
):
    nodes = spack_ref.shape[0]
    spack = spack_ref[...]
    lines = block * (nodes // LINE)
    partners = []
    for side, own, got, inv in (
        (0, own_up_ref, got_up_ref, inv_up_ref),
        (1, own_lo_ref, got_lo_ref, inv_lo_ref),
    ):
        now = got[0]
        later = got[1] + PENALTY * inv[0] * own[0]
        both = scatter_faces(side, jnp.concatenate([now, later], axis=0), scatter_ref, mask_ref)
        scale = PENALTY * face_of(inverse_ref, side)[...]
        partners.append((scale * both[:lines], scale * both[lines:]))
    pot_ref[...] = local_ref[...]
    for side in range(2):
        face = face_of(pot_ref, side)
        face[...] = face[...] + partners[side][0]
    for c in range(block):
        rows = pl.ds(c * nodes, nodes)
        pot_ref[rows, :] = local_sweep(pot_ref[rows, :], source_ref[rows, :], inverse_ref[rows, :], spack)
    for side in range(2):
        face = face_of(pot_ref, side)
        face[...] = face[...] + partners[side][1]
    for c in range(block):
        rows = pl.ds(c * nodes, nodes)
        next_ref[rows, :] = local_sweep(pot_ref[rows, :], source_ref[rows, :], inverse_ref[rows, :], spack)
    for side, out in ((0, up_ref), (1, lo_ref)):
        fields = [face_of(ref, side)[...] for ref in (pot_ref, next_ref)[:keep]]
        picked = gather_faces(side, fields, gather_ref, mask_ref)
        for k in range(keep):
            out[k] = picked[k * block : (k + 1) * block]


def two_sweeps(keep, local, source, inverse, own, got, inv, spack, gather, scatter, mask):
    nodes = spack.shape[0]
    elements = local.shape[1]
    coefs = local.shape[0] // nodes
    shared = gather.shape[2]
    block = coef_block(coefs)
    flat = pl.BlockSpec((block * nodes, elements), lambda i: (i, 0))
    one = pl.BlockSpec((1, block, shared), lambda i: (0, i, 0))
    two = pl.BlockSpec((2, block, shared), lambda i: (0, i, 0))
    third = pl.BlockSpec((1, block, shared), lambda i: (2, i, 0))
    face = pl.BlockSpec((keep, block, shared), lambda i: (0, i, 0))
    size = coefs * nodes * elements
    return pl.pallas_call(
        functools.partial(sweeps_kernel, block, keep),
        out_shape=[jax.ShapeDtypeStruct(local.shape, F32)]
        + [jax.ShapeDtypeStruct((keep, coefs, shared), F32)] * 2,
        grid=(coefs // block,),
        in_specs=[
            flat, flat, flat, one, one, two, two, third, third,
            whole(spack.shape), whole(gather.shape), whole(scatter.shape), whole(mask.shape),
        ],
        out_specs=[flat, face, face],
        scratch_shapes=[pltpu.VMEM((block * nodes, elements), F32)],
        compiler_params=params(),
        cost_estimate=cost(12 * nodes * size, 16 * size),
        name="two_sweeps",
    )(local, source, inverse, *own, *got, *inv, spack, gather, scatter, mask)


def partial_kernel(block, z_ref, x_ref, coef_ref, dpack_ref, o_ref):
    nodes, elements = coef_ref.shape[1:]
    dpack = dpack_ref[...]
    for c in range(block):
        z = z_ref[:, c].reshape(nodes, elements)
        slopes = dot(dpack, pack_field(z))
        moved = coef_ref[BXR] * slopes[:nodes] + coef_ref[BYS] * slopes[nodes:]
        o_ref[2, c] = z - TIME_STEP * (moved + INTERACTION * z)
        x = x_ref[:, c].reshape(nodes, elements)
        slopes = dot(dpack, pack_field(x))
        moved = coef_ref[BXR] * slopes[:nodes] + coef_ref[BYS] * slopes[nodes:]
        o_ref[0, c] = x + TIME_STEP * (x * coef_ref[DXBX] - moved - INTERACTION * x)
        o_ref[1, c] = TIME_STEP * (x * coef_ref[DYBX])


def partial_update(z, x, coef, dpack):
    groups, coefs, part, elements = z.shape
    nodes = groups * part
    block = coef_block(coefs)
    field = pl.BlockSpec((groups, block, part, elements), lambda i: (0, i, 0, 0))
    size = coefs * nodes * elements
    return pl.pallas_call(
        functools.partial(partial_kernel, block),
        out_shape=jax.ShapeDtypeStruct((3, coefs, nodes, elements), F32),
        grid=(coefs // block,),
        in_specs=[field, field, whole(coef.shape), whole(dpack.shape)],
        out_specs=pl.BlockSpec((3, block, nodes, elements), lambda i: (0, i, 0, 0)),
        compiler_params=params(),
        cost_estimate=cost(24 * nodes * size, 20 * size),
        name="partial_update",
    )(z, x, coef, dpack)


def force_kernel(
    block, pos_ref, local_ref, inverse_ref, got_up_ref, got_lo_ref, geo_ref, dpack_ref, scatter_ref,
    mask_ref, part_ref, o_ref, pot_ref,
):
    nodes = dpack_ref.shape[0] // 2
    scale = TIME_STEP * INTERACTION
    which = pl.program_id(1)

    @pl.when(which == 0)
    def _():
        pot_ref[...] = local_ref[...]
        for side, got in ((0, got_up_ref), (1, got_lo_ref)):
            face = face_of(pot_ref, side)
            partner = scatter_faces(side, got[0], scatter_ref, mask_ref)
            face[...] = face[...] + PENALTY * face_of(inverse_ref, side)[...] * partner
        first = pos_ref[0] * (block * pl.num_programs(0)) + pl.program_id(0) * block
        for c in range(block):
            wave = (4.0 / PLANES) * ((first + c) // 2).astype(F32)
            factor = scale * (wave if c % 2 == 0 else -wave)
            other = c + 1 if c % 2 == 0 else c - 1
            o_ref[0, c] = part_ref[0, c] + factor * pot_ref[pl.ds(other * nodes, nodes), :]

    @pl.when(which == 1)
    def _():
        drpack = dpack_ref[:nodes]
        factor = scale * geo_ref[0:1, :]
        for c in range(block):
            slope = dot(drpack, pack_field(pot_ref[pl.ds(c * nodes, nodes), :]))
            o_ref[0, c] = part_ref[0, c] - factor * slope


def add_force(position, local, inverse, got, geometry, dpack, scatter, mask, partial):
    _, coefs, nodes, elements = partial.shape
    shared = scatter.shape[1]
    block = coef_block(coefs)
    flat = pl.BlockSpec((block * nodes, elements), lambda i, j: (i, 0))
    one = pl.BlockSpec((1, block, shared), lambda i, j: (0, i, 0))
    comp = pl.BlockSpec((1, block, nodes, elements), lambda i, j: (2 * j, i, 0, 0))
    size = coefs * nodes * elements
    return pl.pallas_call(
        functools.partial(force_kernel, block),
        out_shape=jax.ShapeDtypeStruct(partial.shape, F32),
        grid=(coefs // block, 2),
        in_specs=[
            SMEM_SPEC, flat, flat, one, one, whole(geometry.shape), whole(dpack.shape),
            whole(scatter.shape), whole(mask.shape), comp,
        ],
        out_specs=comp,
        scratch_shapes=[pltpu.VMEM((block * nodes, elements), F32)],
        input_output_aliases={9: 0},
        compiler_params=params(),
        cost_estimate=cost(6 * nodes * size, 24 * size),
        name="add_force",
    )(position, local, inverse, *got, geometry, dpack, scatter, mask, partial)


def finish_kernel(block, y_ref, coef_ref, dpack_ref, part_ref, o_ref):
    nodes, elements = coef_ref.shape[1:]
    which = pl.program_id(1)

    @pl.when(which == 0)
    def _():
        for c in range(block):
            y = y_ref[:, c].reshape(nodes, elements)
            o_ref[0, c] = part_ref[0, c] + TIME_STEP * (y * coef_ref[DXBY])

    @pl.when(which == 1)
    def _():
        dpack = dpack_ref[...]
        for c in range(block):
            y = y_ref[:, c].reshape(nodes, elements)
            slopes = dot(dpack, pack_field(y))
            moved = coef_ref[BXR] * slopes[:nodes] + coef_ref[BYS] * slopes[nodes:]
            o_ref[0, c] = part_ref[0, c] + y + TIME_STEP * (y * coef_ref[DYBY] - moved)


def finish(y, coef, dpack, partial):
    groups, coefs, part, elements = y.shape
    nodes = groups * part
    block = coef_block(coefs)
    comp = pl.BlockSpec((1, block, nodes, elements), lambda i, j: (j, i, 0, 0))
    size = coefs * nodes * elements
    return pl.pallas_call(
        functools.partial(finish_kernel, block),
        out_shape=jax.ShapeDtypeStruct(partial.shape, F32),
        grid=(coefs // block, 2),
        in_specs=[
            pl.BlockSpec((groups, block, part, elements), lambda i, j: (0, i, 0, 0)),
            whole(coef.shape), whole(dpack.shape), comp,
        ],
        out_specs=comp,
        input_output_aliases={3: 0},
        compiler_params=params(),
        cost_estimate=cost(12 * nodes * size, 20 * size),
        name="finish",
    )(y, coef, dpack, partial)


def to_all(blocks):
    return lax.all_to_all(blocks, "four", split_axis=0, concat_axis=0, tiled=True)


def swap_faces(up, lo):
    peers = lax.axis_size("dom")
    up_way = [(i, (i + 1) % peers) for i in range(peers)]
    down_way = [(j, i) for i, j in up_way]
    return lax.ppermute(lo, "dom", down_way), lax.ppermute(up, "dom", up_way)


def per_device(
    adjoint, base_bank, snapshot, geometry, diff_r, diff_s, stiffness, upper_list, lower_list
):
    _, per, nodes, elements = adjoint.shape
    peers = lax.axis_size("four")
    share = nodes // peers
    table = jnp.asarray(coef_table(PLANES))
    position = lax.axis_index("four").astype(jnp.int32).reshape(1)

    def columns(comp):
        blocks = adjoint[comp].reshape(per, peers, share, elements)
        return to_all(jnp.swapaxes(blocks, 0, 1))

    def coefficients(cols):
        got = to_all(transform(cols, table))
        if share % 8:
            got = jnp.swapaxes(got, 0, 1).reshape(1, per, nodes, elements)
        return got

    z_cols = columns(2)
    x_cols = columns(0)
    coef, dpack, spack, gather, scatter, mask = prepare(
        base_bank, snapshot, geometry, diff_r, diff_s, stiffness, upper_list, lower_list
    )
    z = coefficients(z_cols)
    x = coefficients(x_cols)
    y_cols = columns(1)
    source, inverse, local, up, lo = start_solve(
        position, z, x, geometry, coef, dpack, spack, gather, mask
    )
    got = swap_faces(up, lo)
    inv = got
    partial = partial_update(z, x, coef, dpack)
    local, up, lo = two_sweeps(
        2, local, source, inverse, (up, lo), got, inv, spack, gather, scatter, mask
    )
    got = swap_faces(up, lo)
    local, up, lo = two_sweeps(
        1, local, source, inverse, (up, lo), got, inv, spack, gather, scatter, mask
    )
    got = swap_faces(up, lo)
    partial = add_force(position, local, inverse, got, geometry, dpack, scatter, mask, partial)
    y = coefficients(y_cols)
    return finish(y, coef, dpack, partial)


def solution(mesh):
    in_specs = (
        P(None, "four", None, "dom"),
        P(None, None, None, "dom"),
        P("dom"),
        P(None, "dom"),
        P(),
        P(),
        P(),
        P("dom", None),
        P("dom", None),
    )
    out_specs = P(None, "four", None, "dom")
    return jax.shard_map(
        per_device, mesh=mesh, in_specs=in_specs, out_specs=out_specs, check_vma=False
    )
```

time: 698 us -> 241 us (0.35); the launches traced: 686 us -> 239 us
  waiting for transfers between devices: 284 us -> 128 us
  local copies, waits for them, and re-layouts: 174 us -> 27.6 us
  other arithmetic: 109 us -> 0 us
  matrix products: 84.7 us -> 0 us
  Pallas kernels: 0 us -> 50.6 us
    all_to_all x2 -> x6, waiting for transfers between devices: 269 us -> 112 us  [to_all(): lax.all_to_all(blocks, 'four', split_axis=0, concat_axis=0, tiled=True)]
    scatter-add x12 -> x0, other arithmetic: 84.9 us -> none  [the longest x5 48.3 us: face_penalty(): penalty = penalty.at[:, lower_idx].add(PENALTY * (lower_vals - extended[0]))]
    dot_general x12 -> x0, matrix products: 84.7 us -> none  [the longest x11 57.7 us: along_nodes(): return jnp.einsum('mn,...ne->...me', matrix, field, precision=HIGHEST)]
    reshape x10 -> x0, local copies, waits for them, and re-layouts: 64.8 us -> none  [the longest x5 33.3 us: face_penalty(): return penalty.reshape(field.shape)]
    pallas_call x0 -> x10, Pallas kernels: none -> 50.6 us  [the longest x2 13.8 us: two_sweeps(): pl.pallas_call(functools.partial(sweeps_kernel, block, keep), out_shape=[...]
    gather x11 -> x0, local copies, waits for them, and re-layouts: 44.9 us -> none  [the longest x5 22.1 us: face_penalty(): upper_vals = flat_field[:, upper_idx]]
    all_to_all x2 -> x0, local copies, waits for them, and re-layouts: 32 us -> none  [the longest x1 21.7 us: per_device(): lax.all_to_all(jnp.concatenate([adjoint, rates], 0), 'four', split_axis=2...]
    ppermute x10 -> x6, starting transfers between devices: 22 us -> 7.73 us  [swap_faces(): return (lax.ppermute(lo, 'dom', down_way), lax.ppermute(up, 'dom', up_way))]
  transfers between devices with their start and end apart: 12 -> 12, of which waited for: 8 -> 9; matrix products, arithmetic and copies ran while one was open for 7% -> 3% of each run, Pallas kernels for 0% -> 18%
where the time goes in v1:
time: 241 us; the launch traced here: 239 us
  waiting for transfers between devices  128 us (53%)
  Pallas kernels  50.6 us (21%)
  starting transfers between devices  32.7 us (14%)
  local copies, waits for them, and re-layouts  27.6 us (11%)
    all_to_all x6, waiting for transfers between devices, to_all(): lax.all_to_all(blocks, 'four', split_axis=0, concat_axis=0, tiled=True)  112 us
    all_to_all x6, starting transfers between devices, to_all(): lax.all_to_all(blocks, 'four', split_axis=0, concat_axis=0, tiled=True)  25 us
    ppermute x6, waiting for transfers between devices, swap_faces(): return (lax.ppermute(lo, 'dom', down_way), lax.ppermute(up, 'dom', up_way))  16.4 us
    unnamed x42, local copies, waits for them, and re-layouts  14.1 us
    pallas_call x2, Pallas kernels, two_sweeps(): pl.pallas_call(functools.partial(sweeps_kernel, block, keep), out_shape=[...  13.8 us
    another operation x4, local copies, waits for them, and re-layouts, columns(): blocks = adjoint[comp].reshape(per, peers, share, elements)  13.6 us
    pallas_call x3, Pallas kernels, transform(): pl.pallas_call(functools.partial(transform_kernel, nodes), out_shape=jax....  8.96 us
    pallas_call x1, Pallas kernels, add_force(): pl.pallas_call(functools.partial(force_kernel, block), out_shape=jax.Shap...  7.8 us
  transfers between devices with their start and end apart: 12, of which 9 were waited for; matrix products, arithmetic and copies ran while one was open for 3% of the time, Pallas kernels for 18%

profile of v1, /device:TPU:0, one launch (start us, length us, event | category | flops | bytes accessed | tf_op | source)
XLA Modules:
  0.0 239.5 jit_solution(710364434824606495)
XLA Ops:
  0.0 5.7 %slice_bitcast_fusion = (f32[32,8,8,256]{3,2,1,0:T(8,128)}, f32[32,8,8,256]{3,2,1,0:T(8,128)S(1)}, f32[32,8,8,256]{3,2,1,0:T(8,128)}) fusion(f32[3,32,64,256]{3,2,1,0:T(8,128)} %param.10), kind=kLoop, calls=%fused_computation.3 | loop fusion | bytes 12582912 | tf_op jit(solution)/shard_map/reshape;squeeze | solution.py:491
  5.7 1.6 copy.21
  7.3 5.2 %all-to-all-start = ((f32[8,32,8,256]{3,2,1,0:T(8,128)}), f32[8,32,8,256]{3,2,1,0:T(8,128)S(1)}, u32[]{:S(2)}, u32[]{:S(2)}) async-start(f32[8,32,8,256]{3,2,1,0:T(8,128)} %bitcast.30), calls=%async_computation | async-start | bytes 4194304 | tf_op jit(solution)/shard_map/all_to_all | solution.py:471
  12.4 3.1 %copy.20 = f32[32,8,8,256]{3,2,0,1:T(8,128)} copy(f32[32,8,8,256]{3,2,1,0:T(8,128)} %get-tuple-element.41) | data formatting | bytes 4194304 | tf_op jit(solution)/shard_map/reshape;squeeze | solution.py:491
  15.6 23.5 %all-to-all-done = f32[8,32,8,256]{3,2,1,0:T(8,128)S(1)} async-done(((f32[8,32,8,256]{3,2,1,0:T(8,128)}), f32[8,32,8,256]{3,2,1,0:T(8,128)S(1)}, u32[]{:S(2)}, u32[]{:S(2)}) %all-to-all-start) | async-done | bytes 2097184 | tf_op jit(solution)/shard_map/all_to_all | solution.py:471
  39.1 1.4 copy-done.4
  40.5 4.4 %all-to-all-start.2 = ((f32[8,32,8,256]{3,2,1,0:T(8,128)}), f32[8,32,8,256]{3,2,1,0:T(8,128)}, u32[]{:S(2)}, u32[]{:S(2)}) async-start(f32[8,32,8,256]{3,2,1,0:T(8,128)} %bitcast.28), calls=%async_computation.2 | async-start | bytes 4194304 | tf_op jit(solution)/shard_map/all_to_all | solution.py:471
  44.8 3.2 %copy.19 = f32[32,8,8,256]{3,2,0,1:T(8,128)} copy(f32[32,8,8,256]{3,2,1,0:T(8,128)} %get-tuple-element.39) | data formatting | bytes 4194304 | tf_op jit(solution)/shard_map/reshape;squeeze | solution.py:491
  48.0 23.5 %all-to-all-done.2 = f32[8,32,8,256]{3,2,1,0:T(8,128)} async-done(((f32[8,32,8,256]{3,2,1,0:T(8,128)}), f32[8,32,8,256]{3,2,1,0:T(8,128)}, u32[]{:S(2)}, u32[]{:S(2)}) %all-to-all-start.2) | async-done | bytes 2097184 | tf_op jit(solution)/shard_map/all_to_all | solution.py:471
  71.5 3.7 %all-to-all-start.4 = ((f32[8,32,8,256]{3,2,1,0:T(8,128)}), f32[8,32,8,256]{3,2,1,0:T(8,128)S(1)}, u32[]{:S(2)}, u32[]{:S(2)}) async-start(f32[8,32,8,256]{3,2,1,0:T(8,128)} %bitcast.29), calls=%async_computation.4 | async-start | bytes 4194304 | tf_op jit(solution)/shard_map/all_to_all | solution.py:471
  75.2 3.4 %transform.4 = f32[2048,256]{1,0:T(8,128)S(1)} custom-call(bf16[512,256]{1,0:T(8,128)(2,1)S(1)} %copy-done.11, f32[2048,256]{1,0:T(8,128)} %bitcast.8.x_ref), custom_call_target="tpu_custom_call" | custom-call | flops 805306368 | bytes 4194304 | tf_op jit(solution)/shard_map/transform/pallas_call | solution.py:81
  78.6 0.0 copy-start.9
  78.7 1.3 copy-done.9
  80.0 21.8 %all-to-all-done.4 = f32[8,32,8,256]{3,2,1,0:T(8,128)S(1)} async-done(((f32[8,32,8,256]{3,2,1,0:T(8,128)}), f32[8,32,8,256]{3,2,1,0:T(8,128)S(1)}, u32[]{:S(2)}, u32[]{:S(2)}) %all-to-all-start.4) | async-done | bytes 2097184 | tf_op jit(solution)/shard_map/all_to_all | solution.py:471
  101.8 1.3 copy-done.6
  103.1 3.6 %all-to-all-start.3 = ((f32[8,32,8,256]{3,2,1,0:T(8,128)}), f32[8,32,8,256]{3,2,1,0:T(8,128)S(1)}, u32[]{:S(2)}, u32[]{:S(2)}) async-start(f32[8,32,8,256]{3,2,1,0:T(8,128)} %bitcast.26), calls=%async_computation.3 | async-start | bytes 4194304 | tf_op jit(solution)/shard_map/all_to_all | solution.py:471
  106.7 1.6 copy-done.7
  108.3 2.3 transform.5
  110.7 1.4 copy-done.8
  112.0 21.3 %all-to-all-done.3.z_ref = f32[8,32,8,256]{3,2,1,0:T(8,128)S(1)} async-done(((f32[8,32,8,256]{3,2,1,0:T(8,128)}), f32[8,32,8,256]{3,2,1,0:T(8,128)S(1)}, u32[]{:S(2)}, u32[]{:S(2)}) %all-to-all-start.3) | async-done | bytes 2097184 | tf_op jit(solution)/shard_map/all_to_all | solution.py:471
  133.3 1.3 copy-done
  134.6 4.4 %all-to-all-start.5 = ((f32[8,32,8,256]{3,2,1,0:T(8,128)}), f32[8,32,8,256]{3,2,1,0:T(8,128)}, u32[]{:S(2)}, u32[]{:S(2)}) async-start(f32[8,32,8,256]{3,2,1,0:T(8,128)} %bitcast.25), calls=%async_computation.5 | async-start | bytes 4194304 | tf_op jit(solution)/shard_map/all_to_all | solution.py:471
  139.0 1.6 copy-done.5
  140.6 3.2 %transform.3 = f32[2048,256]{1,0:T(8,128)} custom-call(bf16[512,256]{1,0:T(8,128)(2,1)S(1)} %copy-done.11, f32[2048,256]{1,0:T(8,128)S(1)} %bitcast.23), custom_call_target="tpu_custom_call" | custom-call | flops 805306368 | bytes 4194304 | tf_op jit(solution)/shard_map/transform/pallas_call | solution.py:81
  143.8 21.8 %all-to-all-done.5.x_ref = f32[8,32,8,256]{3,2,1,0:T(8,128)} async-done(((f32[8,32,8,256]{3,2,1,0:T(8,128)}), f32[8,32,8,256]{3,2,1,0:T(8,128)}, u32[]{:S(2)}, u32[]{:S(2)}) %all-to-all-start.5) | async-done | bytes 2097184 | tf_op jit(solution)/shard_map/all_to_all | solution.py:471
  165.6 0.0 copy-start.17
  165.7 0.0 copy-start.19
  165.7 0.0 copy-start.20
  165.7 3.7 %all-to-all-start.1 = ((f32[8,32,8,256]{3,2,1,0:T(8,128)}), f32[8,32,8,256]{3,2,1,0:T(8,128)S(1)}, u32[]{:S(2)}, u32[]{:S(2)}) async-start(f32[8,32,8,256]{3,2,1,0:T(8,128)} %bitcast.3), calls=%async_computation.1 | async-start | bytes 4194304 | tf_op jit(solution)/shard_map/all_to_all | solution.py:471
  169.5 0.5 prepare.1
  170.0 6.0 %start_solve.1 = (f32[2048,256]{1,0:T(8,128)S(1)}, f32[2048,256]{1,0:T(8,128)S(1)}, f32[2048,256]{1,0:T(8,128)}, f32[3,32,512]{2,1,0:T(8,128)S(1)}, f32[3,32,512]{2,1,0:T(8,128)S(1)}) custom-call(s32[1]{0:T(128)} %bitcast.5.pos_ref, f32[8,32,8,256]{3,2,1,0:T(8,128)} %copy-done, f32[8,32,8,256]{3,2,1,0:T(8,128)} %all-to-all-done.5.x_ref, ...), custom_call_target="tpu_custom_call" | custom-call | flops 402653184 | bytes 10485760 | tf_op jit(solution)/shard_map/start_solve/pallas_call | solution.py:254
  176.0 1.4 copy-done.2
  177.4 1.4 copy-done.10
  178.8 3.6 %collective-permute-start = (f32[3,32,512]{2,1,0:T(8,128)S(1)}, f32[3,32,512]{2,1,0:T(8,128)S(1)}, u32[]{:S(2)}, u32[]{:S(2)}) collective-permute-start(f32[3,32,512]{2,1,0:T(8,128)S(1)} %get-tuple-element.31.own_lo_ref), channel_id=1, source_target_pairs={{8,0},{16,8},{24,16},{0,24},{9,1},{17,9},{25,17},{1,25},{10,2},{18... | collective-permute-start | bytes 589832 | tf_op jit(solution)/shard_map/ppermute | solution.py:478
  182.4 5.3 %collective-permute-done.got_up_ref.inv_up_ref = f32[3,32,512]{2,1,0:T(8,128)S(1)} collective-permute-done((f32[3,32,512]{2,1,0:T(8,128)S(1)}, f32[3,32,512]{2,1,0:T(8,128)S(1)}, u32[]{:S(2)}, u32[]{:S(2)}) %collective-permute-start) | collective-permute-done | bytes 196640 | tf_op jit(solution)/shard_map/ppermute | solution.py:478
  187.7 4.5 %collective-permute-done.1.got_lo_ref.inv_lo_ref = f32[3,32,512]{2,1,0:T(8,128)S(1)} collective-permute-done((f32[3,32,512]{2,1,0:T(8,128)S(1)}, f32[3,32,512]{2,1,0:T(8,128)S(1)}, u32[]{:S(2)}, u32[]{:S(2)}) %collective-permute-start.1) | collective-permute-done | bytes 196640 | tf_op jit(solution)/shard_map/ppermute | solution.py:478
  192.2 6.6 %two_sweeps.2 = (f32[2048,256]{1,0:T(8,128)S(1)}, f32[2,32,512]{2,1,0:T(8,128)S(1)}, f32[2,32,512]{2,1,0:T(8,128)S(1)}) custom-call(f32[2048,256]{1,0:T(8,128)} %get-tuple-element.27.local_ref, f32[2048,256]{1,0:T(8,128)} %copy-done.10, f32[2048,256]{1,0:T(8,128)} %copy-done.2, f32[3,32,512]{2,1,0:T(8,128)S(1)} %get-tuple-element.30.own_up_ref, ...), custom_call_target="tpu_custom_call" | custom-call | flops 402653184 | bytes 8388608 | tf_op jit(solution)/shard_map/two_sweeps/pallas_call | solution.py:322
  198.9 1.4 copy-done.12
  200.3 1.7 collective-permute-start.2
  202.0 0.3 collective-permute-start.3
  202.3 3.3 %collective-permute-done.2.got_up_ref = f32[2,32,512]{2,1,0:T(8,128)S(1)} collective-permute-done((f32[2,32,512]{2,1,0:T(8,128)S(1)}, f32[2,32,512]{2,1,0:T(8,128)S(1)}, u32[]{:S(2)}, u32[]{:S(2)}) %collective-permute-start.2) | collective-permute-done | bytes 131104 | tf_op jit(solution)/shard_map/ppermute | solution.py:478
  205.6 3.3 %collective-permute-done.3.got_lo_ref = f32[2,32,512]{2,1,0:T(8,128)S(1)} collective-permute-done((f32[2,32,512]{2,1,0:T(8,128)S(1)}, f32[2,32,512]{2,1,0:T(8,128)S(1)}, u32[]{:S(2)}, u32[]{:S(2)}) %collective-permute-start.3) | collective-permute-done | bytes 131104 | tf_op jit(solution)/shard_map/ppermute | solution.py:478
  208.9 7.2 %two_sweeps.3 = (f32[2048,256]{1,0:T(8,128)S(1)}, f32[1,32,512]{2,1,0:T(8,128)S(1)}, f32[1,32,512]{2,1,0:T(8,128)S(1)}) custom-call(f32[2048,256]{1,0:T(8,128)} %copy-done.12, f32[2048,256]{1,0:T(8,128)} %copy-done.10, f32[2048,256]{1,0:T(8,128)} %copy-done.2, f32[2,32,512]{2,1,0:T(8,128)S(1)} %get-tuple-element.34.own_up_ref, ...), custom_call_target="tpu_custom_call" | custom-call | flops 402653184 | bytes 8388608 | tf_op jit(solution)/shard_map/two_sweeps/pallas_call | solution.py:322
  216.1 1.7 collective-permute-start.4
  217.8 0.3 collective-permute-start.5
  218.1 6.0 %partial_update.1.part_ref = f32[3,32,64,256]{3,2,1,0:T(8,128)} custom-call(f32[8,32,8,256]{3,2,1,0:T(8,128)S(1)} %copy-done.1, f32[8,32,8,256]{3,2,1,0:T(8,128)} %all-to-all-done.5.x_ref, f32[7,64,256]{2,1,0:T(8,128)S(1)} %get-tuple-element.22.diag_ref.coef_ref, bf16[128,192]{1,0:T(8,128)(2,1)S(1)} %get-tuple-element.23.dpack_ref), custom_call_target="tpu_custom_call" | custom-call | flops 805306368 | bytes 10485760 | tf_op jit(solution)/shard_map/partial_update/pallas_call | solution.py:360
  224.2 7.8 %add_force.1.part_ref = f32[3,32,64,256]{3,2,1,0:T(8,128)} custom-call(s32[1]{0:T(128)} %bitcast.5.pos_ref, f32[2048,256]{1,0:T(8,128)S(1)} %get-tuple-element.36.local_ref, f32[2048,256]{1,0:T(8,128)S(1)} %copy-done.3, f32[1,32,512]{2,1,0:T(8,128)S(1)} %collective-permute-done.4.got_up_ref, ...), custom_call_target="tpu_custom_call", output_to_operand_aliasing={{}: (9, {})} | custom-call | flops 201326592 | bytes 12582912 | tf_op jit(solution)/shard_map/add_force/pallas_call | solution.py:411
  232.0 7.5 %finish.1 = f32[3,32,64,256]{3,2,1,0:T(8,128)} custom-call(f32[8,32,8,256]{3,2,1,0:T(8,128)S(1)} %all-to-all-done.1.y_ref, f32[7,64,256]{2,1,0:T(8,128)S(1)} %get-tuple-element.22.diag_ref.coef_ref, bf16[128,192]{1,0:T(8,128)(2,1)S(1)} %get-tuple-element.23.dpack_ref, f32[3,32,64,256]{3,2,1,0:T(8,128)} %add_force.1.part_ref), custom_call_target="tpu_custom_call", output_to_operand_aliasing={{}: (3, {})} | custom-call | flops 402653184 | bytes 10485760 | tf_op jit(solution)/shard_map/finish/pallas_call | solution.py:454
  (32 shorter events, 0.1 us)
Async XLA Ops:
  7.3 31.8 %all-to-all-start = ((f32[8,32,8,256]{3,2,1,0:T(8,128)}), f32[8,32,8,256]{3,2,1,0:T(8,128)S(1)}, u32[]{:S(2)}, u32[]{:S(2)}) async-start(f32[8,32,8,256]{3,2,1,0:T(8,128)} %bitcast.30), calls=%async_computation | async-start | bytes 4194304 | tf_op jit(solution)/shard_map/all_to_all | solution.py:471
  39.1 1.4 copy-start.4
  40.5 31.0 %all-to-all-start.2 = ((f32[8,32,8,256]{3,2,1,0:T(8,128)}), f32[8,32,8,256]{3,2,1,0:T(8,128)}, u32[]{:S(2)}, u32[]{:S(2)}) async-start(f32[8,32,8,256]{3,2,1,0:T(8,128)} %bitcast.28), calls=%async_computation.2 | async-start | bytes 4194304 | tf_op jit(solution)/shard_map/all_to_all | solution.py:471
  71.5 3.7 %copy-start.11 = (bf16[512,256]{1,0:T(8,128)(2,1)S(1)}, bf16[512,256]{1,0:T(8,128)(2,1)}, u32[]{:S(2)}) copy-start(bf16[512,256]{1,0:T(8,128)(2,1)} %constant.6.clone.table_ref) | copy-start | bytes 786436
  71.5 30.3 %all-to-all-start.4 = ((f32[8,32,8,256]{3,2,1,0:T(8,128)}), f32[8,32,8,256]{3,2,1,0:T(8,128)S(1)}, u32[]{:S(2)}, u32[]{:S(2)}) async-start(f32[8,32,8,256]{3,2,1,0:T(8,128)} %bitcast.29), calls=%async_computation.4 | async-start | bytes 4194304 | tf_op jit(solution)/shard_map/all_to_all | solution.py:471
  78.6 1.3 copy-start.9
  101.8 1.3 copy-start.6
  103.1 30.2 %all-to-all-start.3 = ((f32[8,32,8,256]{3,2,1,0:T(8,128)}), f32[8,32,8,256]{3,2,1,0:T(8,128)S(1)}, u32[]{:S(2)}, u32[]{:S(2)}) async-start(f32[8,32,8,256]{3,2,1,0:T(8,128)} %bitcast.26), calls=%async_computation.3 | async-start | bytes 4194304 | tf_op jit(solution)/shard_map/all_to_all | solution.py:471
  106.7 1.6 copy-start.7
  110.7 1.4 copy-start.8
  133.3 1.3 copy-start
  134.6 31.0 %all-to-all-start.5 = ((f32[8,32,8,256]{3,2,1,0:T(8,128)}), f32[8,32,8,256]{3,2,1,0:T(8,128)}, u32[]{:S(2)}, u32[]{:S(2)}) async-start(f32[8,32,8,256]{3,2,1,0:T(8,128)} %bitcast.25), calls=%async_computation.5 | async-start | bytes 4194304 | tf_op jit(solution)/shard_map/all_to_all | solution.py:471
  139.0 1.6 copy-start.5
  165.6 3.8 %copy-start.13 = (f32[4,2,64,256]{3,2,1,0:T(8,128)S(1)}, f32[4,2,64,256]{3,2,1,0:T(8,128)}, u32[]{:S(2)}) copy-start(f32[4,2,64,256]{3,2,1,0:T(8,128)} %bank_ref.1) | copy-start | bytes 1572868
  165.6 3.8 %copy-start.14 = (f32[64,64]{1,0:T(8,128)S(1)}, f32[64,64]{1,0:T(8,128)}, u32[]{:S(2)}) copy-start(f32[64,64]{1,0:T(8,128)} %dr_ref.1) | copy-start | bytes 49156
  165.6 3.8 %copy-start.15 = (f32[64,64]{1,0:T(8,128)S(1)}, f32[64,64]{1,0:T(8,128)}, u32[]{:S(2)}) copy-start(f32[64,64]{1,0:T(8,128)} %ds_ref.1) | copy-start | bytes 49156
  165.6 3.8 %copy-start.16 = (f32[64,64]{1,0:T(8,128)S(1)}, f32[64,64]{1,0:T(8,128)}, u32[]{:S(2)}) copy-start(f32[64,64]{1,0:T(8,128)} %st_ref.1) | copy-start | bytes 49156
  165.6 3.8 %copy-start.17 = (f32[2,256]{1,0:T(2,128)S(1)}, f32[2,256]{1,0:T(2,128)}, u32[]{:S(2)}) copy-start(f32[2,256]{1,0:T(2,128)} %geo_ref.5) | copy-start | bytes 6148
  165.7 3.8 %copy-start.18 = (s32[1,512]{1,0:T(1,128)S(1)}, s32[1,512]{1,0:T(1,128)}, u32[]{:S(2)}) copy-start(s32[1,512]{1,0:T(1,128)} %up_ref.1) | copy-start | bytes 6148
  165.7 3.8 %copy-start.19 = (s32[1,512]{1,0:T(1,128)S(1)}, s32[1,512]{1,0:T(1,128)}, u32[]{:S(2)}) copy-start(s32[1,512]{1,0:T(1,128)} %lo_ref.1) | copy-start | bytes 6148
  165.7 3.8 %copy-start.20 = (s32[256]{0:T(256)S(1)}, s32[256]{0:T(256)}, u32[]{:S(2)}) copy-start(s32[256]{0:T(256)} %param.12) | copy-start | bytes 3076
  165.7 66.3 %all-to-all-start.1 = ((f32[8,32,8,256]{3,2,1,0:T(8,128)}), f32[8,32,8,256]{3,2,1,0:T(8,128)S(1)}, u32[]{:S(2)}, u32[]{:S(2)}) async-start(f32[8,32,8,256]{3,2,1,0:T(8,128)} %bitcast.3), calls=%async_computation.1 | async-start | bytes 4194304 | tf_op jit(solution)/shard_map/all_to_all | solution.py:471
  176.0 1.4 copy-start.2
  177.4 1.4 copy-start.10
  178.8 8.9 %collective-permute-start = (f32[3,32,512]{2,1,0:T(8,128)S(1)}, f32[3,32,512]{2,1,0:T(8,128)S(1)}, u32[]{:S(2)}, u32[]{:S(2)}) collective-permute-start(f32[3,32,512]{2,1,0:T(8,128)S(1)} %get-tuple-element.31.own_lo_ref), channel_id=1, source_target_pairs={{8,0},{16,8},{24,16},{0,24},{9,1},{17,9},{25,17},{1,25},{10,2},{18... | collective-permute-start | bytes 589832 | tf_op jit(solution)/shard_map/ppermute | solution.py:478
  182.4 9.8 %collective-permute-start.1 = (f32[3,32,512]{2,1,0:T(8,128)S(1)}, f32[3,32,512]{2,1,0:T(8,128)S(1)}, u32[]{:S(2)}, u32[]{:S(2)}) collective-permute-start(f32[3,32,512]{2,1,0:T(8,128)S(1)} %get-tuple-element.30.own_up_ref), channel_id=1, source_target_pairs={{0,8},{8,16},{16,24},{24,0},{1,9},{9,17},{17,25},{25,1},{2,10},{10... | collective-permute-start | bytes 589832 | tf_op jit(solution)/shard_map/ppermute | solution.py:478
  198.9 1.4 copy-start.12
  200.3 5.3 %collective-permute-start.2 = (f32[2,32,512]{2,1,0:T(8,128)S(1)}, f32[2,32,512]{2,1,0:T(8,128)S(1)}, u32[]{:S(2)}, u32[]{:S(2)}) collective-permute-start(f32[2,32,512]{2,1,0:T(8,128)S(1)} %get-tuple-element.35.own_lo_ref), channel_id=1, source_target_pairs={{8,0},{16,8},{24,16},{0,24},{9,1},{17,9},{25,17},{1,25},{10,2},{18... | collective-permute-start | bytes 393224 | tf_op jit(solution)/shard_map/ppermute | solution.py:478
  202.0 6.9 %collective-permute-start.3 = (f32[2,32,512]{2,1,0:T(8,128)S(1)}, f32[2,32,512]{2,1,0:T(8,128)S(1)}, u32[]{:S(2)}, u32[]{:S(2)}) collective-permute-start(f32[2,32,512]{2,1,0:T(8,128)S(1)} %get-tuple-element.34.own_up_ref), channel_id=1, source_target_pairs={{0,8},{8,16},{16,24},{24,0},{1,9},{9,17},{17,25},{25,1},{2,10},{10... | collective-permute-start | bytes 393224 | tf_op jit(solution)/shard_map/ppermute | solution.py:478
  208.9 9.3 %copy-start.1 = (f32[8,32,8,256]{3,2,1,0:T(8,128)S(1)}, f32[8,32,8,256]{3,2,1,0:T(8,128)}, u32[]{:S(2)}) copy-start(f32[8,32,8,256]{3,2,1,0:T(8,128)} %copy-done) | copy-start | bytes 6291460
  216.1 8.1 %collective-permute-start.4 = (f32[1,32,512]{2,1,0:T(8,128)S(1)}, f32[1,32,512]{2,1,0:T(8,128)S(1)}, u32[]{:S(2)}, u32[]{:S(2)}) collective-permute-start(f32[1,32,512]{2,1,0:T(8,128)S(1)} %get-tuple-element.37), channel_id=1, source_target_pairs={{8,0},{16,8},{24,16},{0,24},{9,1},{17,9},{25,17},{1,25},{10,2},{18... | collective-permute-start | bytes 196616 | tf_op jit(solution)/shard_map/ppermute | solution.py:478
  217.8 6.4 %copy-start.3 = (f32[2048,256]{1,0:T(8,128)S(1)}, f32[2048,256]{1,0:T(8,128)}, u32[]{:S(2)}) copy-start(f32[2048,256]{1,0:T(8,128)} %copy-done.2) | copy-start | bytes 6291460
  217.8 6.4 %collective-permute-start.5 = (f32[1,32,512]{2,1,0:T(8,128)S(1)}, f32[1,32,512]{2,1,0:T(8,128)S(1)}, u32[]{:S(2)}, u32[]{:S(2)}) collective-permute-start(f32[1,32,512]{2,1,0:T(8,128)S(1)} %get-tuple-element.38), channel_id=1, source_target_pairs={{0,8},{8,16},{16,24},{24,0},{1,9},{9,17},{17,25},{25,1},{2,10},{10... | collective-permute-start | bytes 196616 | tf_op jit(solution)/shard_map/ppermute | solution.py:478

commit v2 on v1

--- a/solution.py
+++ b/solution.py
@@ -19,7 +19,7 @@
 
 F32 = jnp.float32
 BF16 = jnp.bfloat16
-VMEM_LIMIT = 48 * 1024 * 1024
+VMEM_LIMIT = 60 * 1024 * 1024
 
 
 def params():
@@ -66,32 +66,59 @@
     planes = table_ref.shape[1]
     both = table_ref[...]
     high_table = both[:planes]
+    width = x_ref.shape[-1]
+    x_flat = x_ref.reshape(planes * nodes, width)
+    o_flat = o_ref.reshape(planes * nodes, width)
     for n in range(nodes):
         rows = pl.ds(n, planes, stride=nodes) if nodes > 1 else pl.ds(0, planes)
-        high, low = split(x_ref[rows, :])
+        high, low = split(x_flat[rows, :])
         wide = dot(both, high)
-        o_ref[rows, :] = wide[:planes] + (wide[planes:] + dot(high_table, low))
+        o_flat[rows, :] = wide[:planes] + (wide[planes:] + dot(high_table, low))
 
 
 def transform(columns, table):
-    peers, per, nodes, elements = columns.shape
-    rows = peers * per * nodes
+    peers, comps, per, nodes, elements = columns.shape
     width = 128
-    flat = columns.reshape(rows, elements)
-    out = pl.pallas_call(
+    block = pl.BlockSpec((peers, 1, per, nodes, width), lambda k, i: (0, k, 0, 0, i))
+    size = columns.size
+    return pl.pallas_call(
         functools.partial(transform_kernel, nodes),
-        out_shape=jax.ShapeDtypeStruct((rows, elements), F32),
-        grid=(elements // width,),
-        in_specs=[
-            pl.BlockSpec(table.shape, lambda i: (0, 0)),
-            pl.BlockSpec((rows, width), lambda i: (0, i)),
-        ],
-        out_specs=pl.BlockSpec((rows, width), lambda i: (0, i)),
-        compiler_params=params(),
-        cost_estimate=cost(6 * PLANES * rows * elements, 8 * rows * elements),
+        out_shape=jax.ShapeDtypeStruct(columns.shape, F32),
+        grid=(comps, elements // width),
+        in_specs=[pl.BlockSpec(table.shape, lambda k, i: (0, 0)), block],
+        out_specs=block,
+        compiler_params=params(),
+        cost_estimate=cost(6 * PLANES * size, 8 * size),
         name="transform",
-    )(table, flat)
-    return out.reshape(columns.shape)
+    )(table, columns)
+
+
+def pack_kernel(x_ref, o_ref):
+    part = o_ref.shape[3]
+    for d in range(o_ref.shape[0]):
+        o_ref[d, 0] = x_ref[0, :, d * part : (d + 1) * part, :]
+
+
+def pack(adjoint, comps, peers):
+    _, per, nodes, elements = adjoint.shape
+    part = nodes // peers
+    if part % 8:
+        picked = jnp.stack([adjoint[k] for k in comps])
+        return jnp.moveaxis(picked.reshape(len(comps), per, peers, part, elements), 2, 0)
+    block = per // 4
+    first = comps[0]
+    step = comps[1] - first if len(comps) > 1 else 0
+    size = len(comps) * per * nodes * elements
+    return pl.pallas_call(
+        pack_kernel,
+        out_shape=jax.ShapeDtypeStruct((peers, len(comps), per, part, elements), F32),
+        grid=(len(comps), per // block),
+        in_specs=[pl.BlockSpec((1, block, nodes, elements), lambda k, q: (first + step * k, q, 0, 0))],
+        out_specs=pl.BlockSpec((peers, 1, block, part, elements), lambda k, q: (0, k, q, 0, 0)),
+        compiler_params=params(),
+        cost_estimate=cost(0, 8 * size),
+        name="pack",
+    )(adjoint)
 
 
 BXR, BYS, DXBX, DXBY, DYBX, DYBY, DIAG = range(7)
@@ -217,8 +244,8 @@
         wave = beta * (index // 2).astype(F32)
         shift = beta * jnp.where(index == 1, PLANES // 2, index // 2).astype(F32)
         shift = shift * shift
-        z = z_ref[:, c].reshape(nodes, elements)
-        other = x_ref[:, c + 1 if c % 2 == 0 else c - 1].reshape(nodes, elements)
+        z = z_ref[:, 0, c].reshape(nodes, elements)
+        other = x_ref[:, 0, c + 1 if c % 2 == 0 else c - 1].reshape(nodes, elements)
         turned = (wave if c % 2 == 0 else -wave) * other
         source = turned - rx * dot(drpack, pack_field(z))
         inverse = RELAXATION / (diag + shift * mass)
@@ -242,12 +269,14 @@
 SMEM_SPEC = pl.BlockSpec(memory_space=pltpu.SMEM)
 
 
-def start_solve(position, z, x, geometry, coef, dpack, spack, gather, mask):
-    groups, coefs, part, elements = z.shape
+def start_solve(position, zx, geometry, coef, dpack, spack, gather, mask):
+    groups, _, coefs, part, elements = zx.shape
     nodes = groups * part
     shared = gather.shape[2]
     block = coef_block(coefs)
-    field = pl.BlockSpec((groups, block, part, elements), lambda i: (0, i, 0, 0))
+    z_spec, x_spec = (
+        pl.BlockSpec((groups, 1, block, part, elements), lambda i, k=k: (0, k, i, 0, 0)) for k in range(2)
+    )
     flat = pl.BlockSpec((block * nodes, elements), lambda i: (i, 0))
     face = pl.BlockSpec((3, block, shared), lambda i: (0, i, 0))
     size = coefs * nodes * elements
@@ -257,7 +286,7 @@
         + [jax.ShapeDtypeStruct((3, coefs, shared), F32)] * 2,
         grid=(coefs // block,),
         in_specs=[
-            SMEM_SPEC, field, field, whole(geometry.shape),
+            SMEM_SPEC, z_spec, x_spec, whole(geometry.shape),
             pl.BlockSpec((1, nodes, elements), lambda i: (DIAG, 0, 0)),
             whole(dpack.shape), whole(spack.shape), whole(gather.shape), whole(mask.shape),
         ],
@@ -266,7 +295,7 @@
         compiler_params=params(),
         cost_estimate=cost(12 * nodes * size, 20 * size),
         name="start_solve",
-    )(position, z, x, geometry, coef, dpack, spack, gather, mask)
+    )(position, zx, zx, geometry, coef, dpack, spack, gather, mask)
 
 
 def sweeps_kernel(
@@ -340,33 +369,35 @@
     nodes, elements = coef_ref.shape[1:]
     dpack = dpack_ref[...]
     for c in range(block):
-        z = z_ref[:, c].reshape(nodes, elements)
+        z = z_ref[:, 0, c].reshape(nodes, elements)
         slopes = dot(dpack, pack_field(z))
         moved = coef_ref[BXR] * slopes[:nodes] + coef_ref[BYS] * slopes[nodes:]
         o_ref[2, c] = z - TIME_STEP * (moved + INTERACTION * z)
-        x = x_ref[:, c].reshape(nodes, elements)
+        x = x_ref[:, 0, c].reshape(nodes, elements)
         slopes = dot(dpack, pack_field(x))
         moved = coef_ref[BXR] * slopes[:nodes] + coef_ref[BYS] * slopes[nodes:]
         o_ref[0, c] = x + TIME_STEP * (x * coef_ref[DXBX] - moved - INTERACTION * x)
         o_ref[1, c] = TIME_STEP * (x * coef_ref[DYBX])
 
 
-def partial_update(z, x, coef, dpack):
-    groups, coefs, part, elements = z.shape
+def partial_update(zx, coef, dpack):
+    groups, _, coefs, part, elements = zx.shape
     nodes = groups * part
     block = coef_block(coefs)
-    field = pl.BlockSpec((groups, block, part, elements), lambda i: (0, i, 0, 0))
+    z_spec, x_spec = (
+        pl.BlockSpec((groups, 1, block, part, elements), lambda i, k=k: (0, k, i, 0, 0)) for k in range(2)
+    )
     size = coefs * nodes * elements
     return pl.pallas_call(
         functools.partial(partial_kernel, block),
         out_shape=jax.ShapeDtypeStruct((3, coefs, nodes, elements), F32),
         grid=(coefs // block,),
-        in_specs=[field, field, whole(coef.shape), whole(dpack.shape)],
+        in_specs=[z_spec, x_spec, whole(coef.shape), whole(dpack.shape)],
         out_specs=pl.BlockSpec((3, block, nodes, elements), lambda i: (0, i, 0, 0)),
         compiler_params=params(),
         cost_estimate=cost(24 * nodes * size, 20 * size),
         name="partial_update",
-    )(z, x, coef, dpack)
+    )(zx, zx, coef, dpack)
 
 
 def force_kernel(
@@ -432,21 +463,21 @@
     @pl.when(which == 0)
     def _():
         for c in range(block):
-            y = y_ref[:, c].reshape(nodes, elements)
+            y = y_ref[:, 0, c].reshape(nodes, elements)
             o_ref[0, c] = part_ref[0, c] + TIME_STEP * (y * coef_ref[DXBY])
 
     @pl.when(which == 1)
     def _():
         dpack = dpack_ref[...]
         for c in range(block):
-            y = y_ref[:, c].reshape(nodes, elements)
+            y = y_ref[:, 0, c].reshape(nodes, elements)
             slopes = dot(dpack, pack_field(y))
             moved = coef_ref[BXR] * slopes[:nodes] + coef_ref[BYS] * slopes[nodes:]
             o_ref[0, c] = part_ref[0, c] + y + TIME_STEP * (y * coef_ref[DYBY] - moved)
 
 
 def finish(y, coef, dpack, partial):
-    groups, coefs, part, elements = y.shape
+    groups, _, coefs, part, elements = y.shape
     nodes = groups * part
     block = coef_block(coefs)
     comp = pl.BlockSpec((1, block, nodes, elements), lambda i, j: (j, i, 0, 0))
@@ -456,7 +487,7 @@
         out_shape=jax.ShapeDtypeStruct(partial.shape, F32),
         grid=(coefs // block, 2),
         in_specs=[
-            pl.BlockSpec((groups, block, part, elements), lambda i, j: (0, i, 0, 0)),
+            pl.BlockSpec((groups, 1, block, part, elements), lambda i, j: (0, 0, i, 0, 0)),
             whole(coef.shape), whole(dpack.shape), comp,
         ],
         out_specs=comp,
@@ -487,30 +518,28 @@
     table = jnp.asarray(coef_table(PLANES))
     position = lax.axis_index("four").astype(jnp.int32).reshape(1)
 
-    def columns(comp):
-        blocks = adjoint[comp].reshape(per, peers, share, elements)
-        return to_all(jnp.swapaxes(blocks, 0, 1))
-
-    def coefficients(cols):
-        got = to_all(transform(cols, table))
+    def coefficients(columns):
+        got = to_all(transform(columns, table))
         if share % 8:
-            got = jnp.swapaxes(got, 0, 1).reshape(1, per, nodes, elements)
+            comps = got.shape[1]
+            got = jnp.moveaxis(got, 0, 2).reshape(1, comps, per, nodes, elements)
         return got
 
-    z_cols = columns(2)
-    x_cols = columns(0)
+    zx_sent = pack(adjoint, (2, 0), peers)
+    zx_columns = to_all(zx_sent)
     coef, dpack, spack, gather, scatter, mask = prepare(
         base_bank, snapshot, geometry, diff_r, diff_s, stiffness, upper_list, lower_list
     )
-    z = coefficients(z_cols)
-    x = coefficients(x_cols)
-    y_cols = columns(1)
+    y_sent = pack(adjoint, (1,), peers)
+    zx = coefficients(zx_columns)
+    zx, y_sent = lax.optimization_barrier((zx, y_sent))
+    y_columns = to_all(y_sent)
     source, inverse, local, up, lo = start_solve(
-        position, z, x, geometry, coef, dpack, spack, gather, mask
+        position, zx, geometry, coef, dpack, spack, gather, mask
     )
     got = swap_faces(up, lo)
     inv = got
-    partial = partial_update(z, x, coef, dpack)
+    partial = partial_update(zx, coef, dpack)
     local, up, lo = two_sweeps(
         2, local, source, inverse, (up, lo), got, inv, spack, gather, scatter, mask
     )
@@ -520,7 +549,7 @@
     )
     got = swap_faces(up, lo)
     partial = add_force(position, local, inverse, got, geometry, dpack, scatter, mask, partial)
-    y = coefficients(y_cols)
+    y = coefficients(y_columns)
     return finish(y, coef, dpack, partial)
 
 

time: 241 us -> 240 us (level)
  blocking collectives: 0 us -> 85.3 us
  waiting for transfers between devices: 128 us -> 62.1 us
  local copies, waits for them, and re-layouts: 27.6 us -> 3.28 us
  Pallas kernels: 50.6 us -> 71.5 us
  starting transfers between devices: 32.7 us -> 16.6 us
    all_to_all x0 -> x2, blocking collectives: none -> 85.3 us  [to_all(): lax.all_to_all(blocks, 'four', split_axis=0, concat_axis=0, tiled=True)]
    all_to_all x6 -> x2, waiting for transfers between devices: 112 us -> 45.3 us  [to_all(): lax.all_to_all(blocks, 'four', split_axis=0, concat_axis=0, tiled=True)]
    all_to_all x6 -> x2, starting transfers between devices: 25 us -> 8.15 us  [to_all(): lax.all_to_all(blocks, 'four', split_axis=0, concat_axis=0, tiled=True)]
    another operation x4 -> x0, local copies, waits for them, and re-layouts: 13.6 us -> none  [columns(): blocks = adjoint[comp].reshape(per, peers, share, elements)]
    unnamed x42 -> x14, local copies, waits for them, and re-layouts: 14.1 us -> 3.28 us
    pallas_call x0 -> x2, Pallas kernels: none -> 10.5 us  [pack(): pl.pallas_call(pack_kernel, out_shape=jax.ShapeDtypeStruct((peers, len(co...]
    pallas_call x2, Pallas kernels: 13.8 us -> 16.4 us  [two_sweeps(): pl.pallas_call(functools.partial(sweeps_kernel, block, keep), out_shape=[...]
    pallas_call x3 -> x2, Pallas kernels: 8.96 us -> 11.3 us  [transform(): pl.pallas_call(functools.partial(transform_kernel, nodes), out_shape=jax....]
  transfers between devices with their start and end apart: 12 -> 8, of which waited for: 9 -> 5; matrix products, arithmetic and copies ran while one was open for 3% -> 0% of each run, Pallas kernels for 18% -> 19%
where the time goes in v2:
time: 240 us; the launch traced here: 239 us
  blocking collectives  85.3 us (36%)
  Pallas kernels  71.5 us (30%)
  waiting for transfers between devices  62.1 us (26%)
  starting transfers between devices  16.6 us (7%)
  local copies, waits for them, and re-layouts  3.28 us (1%)
    all_to_all x2, blocking collectives, to_all(): lax.all_to_all(blocks, 'four', split_axis=0, concat_axis=0, tiled=True)  85.3 us
    all_to_all x2, waiting for transfers between devices, to_all(): lax.all_to_all(blocks, 'four', split_axis=0, concat_axis=0, tiled=True)  45.3 us
    ppermute x6, waiting for transfers between devices, swap_faces(): return (lax.ppermute(lo, 'dom', down_way), lax.ppermute(up, 'dom', up_way))  16.8 us
    pallas_call x2, Pallas kernels, two_sweeps(): pl.pallas_call(functools.partial(sweeps_kernel, block, keep), out_shape=[...  16.4 us
    pallas_call x2, Pallas kernels, transform(): pl.pallas_call(functools.partial(transform_kernel, nodes), out_shape=jax....  11.3 us
    pallas_call x2, Pallas kernels, pack(): pl.pallas_call(pack_kernel, out_shape=jax.ShapeDtypeStruct((peers, len(co...  10.5 us
    pallas_call x1, Pallas kernels, add_force(): pl.pallas_call(functools.partial(force_kernel, block), out_shape=jax.Shap...  9.66 us
    ppermute x6, starting transfers between devices, swap_faces(): return (lax.ppermute(lo, 'dom', down_way), lax.ppermute(up, 'dom', up_way))  8.49 us
  transfers between devices with their start and end apart: 8, of which 5 were waited for; matrix products, arithmetic and copies ran while one was open for 0% of the time, Pallas kernels for 19%

profile of v2, /device:TPU:0, one launch (start us, length us, event | category | flops | bytes accessed | tf_op | source)
XLA Modules:
  0.0 238.9 jit_solution(10688560901470805)
XLA Ops:
  0.0 6.6 %pack.2 = f32[8,2,32,8,256]{4,3,2,1,0:T(8,128)} custom-call(f32[3,32,64,256]{3,2,1,0:T(8,128)} %x_ref.3), custom_call_target="tpu_custom_call" | custom-call | bytes 8388608 | tf_op jit(solution)/shard_map/pack/pallas_call | solution.py:112
  6.6 54.3 %all_to_all.20.x_ref = f32[8,2,32,8,256]{4,3,2,1,0:T(8,128)} all-to-all(f32[8,2,32,8,256]{4,3,2,1,0:T(8,128)} %pack.2), channel_id=1, replica_groups=mesh['dom'=4,'four'=8] {'four'}, dimensions={0} | all-to-all | bytes 8388608 | tf_op jit(solution)/shard_map/all_to_all | solution.py:502
  60.9 7.0 %transform.2 = f32[8,2,32,8,256]{4,3,2,1,0:T(8,128)} custom-call(bf16[512,256]{1,0:T(8,128)(2,1)} %constant.6.clone.table_ref, f32[8,2,32,8,256]{4,3,2,1,0:T(8,128)} %all_to_all.20.x_ref), custom_call_target="tpu_custom_call" | custom-call | flops 1610612736 | bytes 8388608 | tf_op jit(solution)/shard_map/transform/pallas_call | solution.py:84
  68.0 4.5 %all-to-all-start.1 = ((f32[8,2,32,8,256]{4,3,2,1,0:T(8,128)}), f32[8,2,32,8,256]{4,3,2,1,0:T(8,128)}, u32[]{:S(2)}, u32[]{:S(2)}) async-start(f32[8,2,32,8,256]{4,3,2,1,0:T(8,128)} %transform.2), calls=%async_computation.1 | async-start | bytes 8388608 | tf_op jit(solution)/shard_map/all_to_all | solution.py:502
  72.5 3.9 %pack.3 = f32[8,1,32,8,256]{4,3,2,1,0:T(8,128)} custom-call(f32[3,32,64,256]{3,2,1,0:T(8,128)} %x_ref.3), custom_call_target="tpu_custom_call" | custom-call | bytes 4194304 | tf_op jit(solution)/shard_map/pack/pallas_call | solution.py:112
  76.4 45.3 %all-to-all-done.1.z_ref.x_ref = f32[8,2,32,8,256]{4,3,2,1,0:T(8,128)} async-done(((f32[8,2,32,8,256]{4,3,2,1,0:T(8,128)}), f32[8,2,32,8,256]{4,3,2,1,0:T(8,128)}, u32[]{:S(2)}, u32[]{:S(2)}) %all-to-all-start.1) | async-done | bytes 4194336 | tf_op jit(solution)/shard_map/all_to_all | solution.py:502
  121.6 30.9 %all_to_all.21.x_ref = f32[8,1,32,8,256]{4,3,2,1,0:T(8,128)} all-to-all(f32[8,1,32,8,256]{4,3,2,1,0:T(8,128)} %pack.3), channel_id=1, replica_groups=mesh['dom'=4,'four'=8] {'four'}, dimensions={0} | all-to-all | bytes 4194304 | tf_op jit(solution)/shard_map/all_to_all | solution.py:502
  152.6 4.3 %transform.3 = f32[8,1,32,8,256]{4,3,2,1,0:T(8,128)} custom-call(bf16[512,256]{1,0:T(8,128)(2,1)} %constant.6.clone.table_ref, f32[8,1,32,8,256]{4,3,2,1,0:T(8,128)} %all_to_all.21.x_ref), custom_call_target="tpu_custom_call" | custom-call | flops 805306368 | bytes 4194304 | tf_op jit(solution)/shard_map/transform/pallas_call | solution.py:84
  156.9 3.6 %all-to-all-start.3 = ((f32[8,1,32,8,256]{4,3,2,1,0:T(8,128)}), f32[8,1,32,8,256]{4,3,2,1,0:T(8,128)S(1)}, u32[]{:S(2)}, u32[]{:S(2)}) async-start(f32[8,1,32,8,256]{4,3,2,1,0:T(8,128)} %transform.3), calls=%async_computation.3 | async-start | bytes 4194304 | tf_op jit(solution)/shard_map/all_to_all | solution.py:502
  160.5 2.6 %prepare.1 = (f32[7,64,256]{2,1,0:T(8,128)}, bf16[128,192]{1,0:T(8,128)(2,1)}, bf16[64,192]{1,0:T(8,128)(2,1)}, bf16[2,256,512]{2,1,0:T(8,128)(2,1)}, bf16[2,512...) custom-call(f32[4,2,64,256]{3,2,1,0:T(8,128)} %bank_ref.1, s32[1,256]{1,0:T(1,128)} %bitcast.2, f32[2,256]{1,0:T(2,128)} %geo_ref.5, ...), custom_call_target="tpu_custom_call" | custom-call | flops 10000000 | bytes 4000000 | tf_op jit(solution)/shard_map/prepare/pallas_call | solution.py:180
  163.1 6.9 %start_solve.1 = (f32[2048,256]{1,0:T(8,128)}, f32[2048,256]{1,0:T(8,128)}, f32[2048,256]{1,0:T(8,128)}, f32[3,32,512]{2,1,0:T(8,128)}, f32[3,32,512]{2,1,0:T(8,128)}) custom-call(s32[1]{0:T(128)} %bitcast.1.pos_ref, f32[8,2,32,8,256]{4,3,2,1,0:T(8,128)} %all-to-all-done.1.z_ref.x_ref, f32[8,2,32,8,256]{4,3,2,1,0:T(8,128)} %all-to-all-done.1.z_ref.x_ref, ...), custom_call_target="tpu_custom_call" | custom-call | flops 402653184 | bytes 10485760 | tf_op jit(solution)/shard_map/start_solve/pallas_call | solution.py:283
  170.0 4.3 %collective-permute-start = (f32[3,32,512]{2,1,0:T(8,128)}, f32[3,32,512]{2,1,0:T(8,128)S(1)}, u32[]{:S(2)}, u32[]{:S(2)}) collective-permute-start(f32[3,32,512]{2,1,0:T(8,128)} %get-tuple-element.35.own_lo_ref), channel_id=1, source_target_pairs={{8,0},{16,8},{24,16},{0,24},{9,1},{17,9},{25,17},{1,25},{10,2},{18... | collective-permute-start | bytes 589832 | tf_op jit(solution)/shard_map/ppermute | solution.py:509
  174.3 0.0 collective-permute-start.1
  174.3 5.6 %collective-permute-done.got_up_ref.inv_up_ref = f32[3,32,512]{2,1,0:T(8,128)S(1)} collective-permute-done((f32[3,32,512]{2,1,0:T(8,128)}, f32[3,32,512]{2,1,0:T(8,128)S(1)}, u32[]{:S(2)}, u32[]{:S(2)}) %collective-permute-start) | collective-permute-done | bytes 196640 | tf_op jit(solution)/shard_map/ppermute | solution.py:509
  179.9 0.0 copy-start.1
  179.9 4.4 %collective-permute-done.1.got_lo_ref.inv_lo_ref = f32[3,32,512]{2,1,0:T(8,128)S(1)} collective-permute-done((f32[3,32,512]{2,1,0:T(8,128)}, f32[3,32,512]{2,1,0:T(8,128)S(1)}, u32[]{:S(2)}, u32[]{:S(2)}) %collective-permute-start.1) | collective-permute-done | bytes 196640 | tf_op jit(solution)/shard_map/ppermute | solution.py:509
  184.4 0.0 copy-start.2
  184.4 0.0 copy-done.1
  184.4 0.7 copy-done.2
  185.0 7.9 %two_sweeps.2 = (f32[2048,256]{1,0:T(8,128)}, f32[2,32,512]{2,1,0:T(8,128)}, f32[2,32,512]{2,1,0:T(8,128)}) custom-call(f32[2048,256]{1,0:T(8,128)} %get-tuple-element.31.local_ref, f32[2048,256]{1,0:T(8,128)} %get-tuple-element.32.source_ref, f32[2048,256]{1,0:T(8,128)} %get-tuple-element.33.inverse_ref, f32[3,32,512]{2,1,0:T(8,128)} %get-tuple-element.34.own_up_ref, ...), custom_call_target="tpu_custom_call" | custom-call | flops 402653184 | bytes 8388608 | tf_op jit(solution)/shard_map/two_sweeps/pallas_call | solution.py:351
  193.0 1.8 collective-permute-start.2
  194.8 0.3 collective-permute-start.3
  195.0 3.6 %collective-permute-done.2.got_up_ref = f32[2,32,512]{2,1,0:T(8,128)S(1)} collective-permute-done((f32[2,32,512]{2,1,0:T(8,128)}, f32[2,32,512]{2,1,0:T(8,128)S(1)}, u32[]{:S(2)}, u32[]{:S(2)}) %collective-permute-start.2) | collective-permute-done | bytes 131104 | tf_op jit(solution)/shard_map/ppermute | solution.py:509
  198.6 0.0 copy-start.3
  198.7 3.2 %collective-permute-done.3.got_lo_ref = f32[2,32,512]{2,1,0:T(8,128)S(1)} collective-permute-done((f32[2,32,512]{2,1,0:T(8,128)}, f32[2,32,512]{2,1,0:T(8,128)S(1)}, u32[]{:S(2)}, u32[]{:S(2)}) %collective-permute-start.3) | collective-permute-done | bytes 131104 | tf_op jit(solution)/shard_map/ppermute | solution.py:509
  201.8 0.0 copy-start.4
  201.9 0.0 copy-done.3
  201.9 0.7 copy-done.4
  202.5 8.5 %two_sweeps.3 = (f32[2048,256]{1,0:T(8,128)}, f32[1,32,512]{2,1,0:T(8,128)}, f32[1,32,512]{2,1,0:T(8,128)}) custom-call(f32[2048,256]{1,0:T(8,128)} %get-tuple-element.37.local_ref, f32[2048,256]{1,0:T(8,128)} %get-tuple-element.32.source_ref, f32[2048,256]{1,0:T(8,128)} %get-tuple-element.33.inverse_ref, f32[2,32,512]{2,1,0:T(8,128)} %get-tuple-element.38.own_up_ref, ...), custom_call_target="tpu_custom_call" | custom-call | flops 402653184 | bytes 8388608 | tf_op jit(solution)/shard_map/two_sweeps/pallas_call | solution.py:351
  211.0 1.7 collective-permute-start.4
  212.7 0.4 collective-permute-start.5
  213.1 6.4 %partial_update.1.part_ref = f32[3,32,64,256]{3,2,1,0:T(8,128)} custom-call(f32[8,2,32,8,256]{4,3,2,1,0:T(8,128)} %all-to-all-done.1.z_ref.x_ref, f32[8,2,32,8,256]{4,3,2,1,0:T(8,128)} %all-to-all-done.1.z_ref.x_ref, f32[7,64,256]{2,1,0:T(8,128)} %get-tuple-element.25.diag_ref.coef_ref, bf16[128,192]{1,0:T(8,128)(2,1)} %get-tuple-element.26.dpack_ref), custom_call_target="tpu_custom_call" | custom-call | flops 805306368 | bytes 10485760 | tf_op jit(solution)/shard_map/partial_update/pallas_call | solution.py:391
  219.4 0.0 collective-permute-done.4.got_up_ref
  219.4 0.0 copy-start.5
  219.4 0.0 collective-permute-done.5.got_lo_ref
  219.5 0.0 copy-start.6
  219.5 0.6 copy-done.5
  220.1 0.0 copy-done.6
  220.1 9.7 %add_force.1.part_ref = f32[3,32,64,256]{3,2,1,0:T(8,128)} custom-call(s32[1]{0:T(128)} %bitcast.1.pos_ref, f32[2048,256]{1,0:T(8,128)} %get-tuple-element.40.local_ref, f32[2048,256]{1,0:T(8,128)} %get-tuple-element.33.inverse_ref, f32[1,32,512]{2,1,0:T(8,128)} %copy-done.5, f32[1,32,512]{2,1,0:T(8,128)} %copy-done.6, ...), custom_call_target="tpu_custom_call", output_to_operand_aliasing={{}: (9, {})} | custom-call | flops 201326592 | bytes 12582912 | tf_op jit(solution)/shard_map/add_force/pallas_call | solution.py:442
  229.7 0.0 all-to-all-done.3.y_ref
  229.8 0.0 copy-start
  229.8 1.3 copy-done
  231.1 7.8 %finish.1 = f32[3,32,64,256]{3,2,1,0:T(8,128)} custom-call(f32[8,1,32,8,256]{4,3,2,1,0:T(8,128)} %copy-done, f32[7,64,256]{2,1,0:T(8,128)} %get-tuple-element.25.diag_ref.coef_ref, bf16[128,192]{1,0:T(8,128)(2,1)} %get-tuple-element.26.dpack_ref, f32[3,32,64,256]{3,2,1,0:T(8,128)} %add_force.1.part_ref), custom_call_target="tpu_custom_call", output_to_operand_aliasing={{}: (3, {})} | custom-call | flops 402653184 | bytes 10485760 | tf_op jit(solution)/shard_map/finish/pallas_call | solution.py:485
Async XLA Ops:
  68.0 53.7 %all-to-all-start.1 = ((f32[8,2,32,8,256]{4,3,2,1,0:T(8,128)}), f32[8,2,32,8,256]{4,3,2,1,0:T(8,128)}, u32[]{:S(2)}, u32[]{:S(2)}) async-start(f32[8,2,32,8,256]{4,3,2,1,0:T(8,128)} %transform.2), calls=%async_computation.1 | async-start | bytes 8388608 | tf_op jit(solution)/shard_map/all_to_all | solution.py:502
  156.9 72.9 %all-to-all-start.3 = ((f32[8,1,32,8,256]{4,3,2,1,0:T(8,128)}), f32[8,1,32,8,256]{4,3,2,1,0:T(8,128)S(1)}, u32[]{:S(2)}, u32[]{:S(2)}) async-start(f32[8,1,32,8,256]{4,3,2,1,0:T(8,128)} %transform.3), calls=%async_computation.3 | async-start | bytes 4194304 | tf_op jit(solution)/shard_map/all_to_all | solution.py:502
  170.0 9.9 %collective-permute-start = (f32[3,32,512]{2,1,0:T(8,128)}, f32[3,32,512]{2,1,0:T(8,128)S(1)}, u32[]{:S(2)}, u32[]{:S(2)}) collective-permute-start(f32[3,32,512]{2,1,0:T(8,128)} %get-tuple-element.35.own_lo_ref), channel_id=1, source_target_pairs={{8,0},{16,8},{24,16},{0,24},{9,1},{17,9},{25,17},{1,25},{10,2},{18... | collective-permute-start | bytes 589832 | tf_op jit(solution)/shard_map/ppermute | solution.py:509
  174.3 10.0 %collective-permute-start.1 = (f32[3,32,512]{2,1,0:T(8,128)}, f32[3,32,512]{2,1,0:T(8,128)S(1)}, u32[]{:S(2)}, u32[]{:S(2)}) collective-permute-start(f32[3,32,512]{2,1,0:T(8,128)} %get-tuple-element.34.own_up_ref), channel_id=1, source_target_pairs={{0,8},{8,16},{16,24},{24,0},{1,9},{9,17},{17,25},{25,1},{2,10},{10... | collective-permute-start | bytes 589832 | tf_op jit(solution)/shard_map/ppermute | solution.py:509
  179.9 4.4 %copy-start.1 = (f32[3,32,512]{2,1,0:T(8,128)}, f32[3,32,512]{2,1,0:T(8,128)S(1)}, u32[]{:S(2)}) copy-start(f32[3,32,512]{2,1,0:T(8,128)S(1)} %collective-permute-done.got_up_ref.inv_up_ref) | copy-start | bytes 589828
  184.4 0.7 copy-start.2
  193.0 5.7 %collective-permute-start.2 = (f32[2,32,512]{2,1,0:T(8,128)}, f32[2,32,512]{2,1,0:T(8,128)S(1)}, u32[]{:S(2)}, u32[]{:S(2)}) collective-permute-start(f32[2,32,512]{2,1,0:T(8,128)} %get-tuple-element.39.own_lo_ref), channel_id=1, source_target_pairs={{8,0},{16,8},{24,16},{0,24},{9,1},{17,9},{25,17},{1,25},{10,2},{18... | collective-permute-start | bytes 393224 | tf_op jit(solution)/shard_map/ppermute | solution.py:509
  194.8 7.1 %collective-permute-start.3 = (f32[2,32,512]{2,1,0:T(8,128)}, f32[2,32,512]{2,1,0:T(8,128)S(1)}, u32[]{:S(2)}, u32[]{:S(2)}) collective-permute-start(f32[2,32,512]{2,1,0:T(8,128)} %get-tuple-element.38.own_up_ref), channel_id=1, source_target_pairs={{0,8},{8,16},{16,24},{24,0},{1,9},{9,17},{17,25},{25,1},{2,10},{10... | collective-permute-start | bytes 393224 | tf_op jit(solution)/shard_map/ppermute | solution.py:509
  198.6 3.2 %copy-start.3 = (f32[2,32,512]{2,1,0:T(8,128)}, f32[2,32,512]{2,1,0:T(8,128)S(1)}, u32[]{:S(2)}) copy-start(f32[2,32,512]{2,1,0:T(8,128)S(1)} %collective-permute-done.2.got_up_ref) | copy-start | bytes 393220
  201.8 0.7 copy-start.4
  211.0 8.4 %collective-permute-start.4 = (f32[1,32,512]{2,1,0:T(8,128)}, f32[1,32,512]{2,1,0:T(8,128)S(1)}, u32[]{:S(2)}, u32[]{:S(2)}) collective-permute-start(f32[1,32,512]{2,1,0:T(8,128)} %get-tuple-element.41), channel_id=1, source_target_pairs={{8,0},{16,8},{24,16},{0,24},{9,1},{17,9},{25,17},{1,25},{10,2},{18... | collective-permute-start | bytes 196616 | tf_op jit(solution)/shard_map/ppermute | solution.py:509
  212.7 6.7 %collective-permute-start.5 = (f32[1,32,512]{2,1,0:T(8,128)}, f32[1,32,512]{2,1,0:T(8,128)S(1)}, u32[]{:S(2)}, u32[]{:S(2)}) collective-permute-start(f32[1,32,512]{2,1,0:T(8,128)} %get-tuple-element.42), channel_id=1, source_target_pairs={{0,8},{8,16},{16,24},{24,0},{1,9},{9,17},{17,25},{25,1},{2,10},{10... | collective-permute-start | bytes 196616 | tf_op jit(solution)/shard_map/ppermute | solution.py:509
  219.4 0.6 copy-start.5
  219.5 0.6 copy-start.6
  229.8 1.3 copy-start

commit v3 on v1

--- a/solution.py
+++ b/solution.py
@@ -20,6 +20,7 @@
 F32 = jnp.float32
 BF16 = jnp.bfloat16
 VMEM_LIMIT = 48 * 1024 * 1024
+SMEM_SPEC = pl.BlockSpec(memory_space=pltpu.SMEM)
 
 
 def params():
@@ -43,6 +44,10 @@
 def pack_matrix(m):
     high, low = split(m)
     return jnp.concatenate([high, low, high], axis=1)
+
+
+def slab(refs, c):
+    return jnp.concatenate([ref[c] for ref in refs], axis=0)
 
 
 def pack_field(v):
@@ -62,55 +67,131 @@
     return np.concatenate([high, low], axis=0)
 
 
-def transform_kernel(nodes, table_ref, x_ref, o_ref):
+def permute_kernel(peers, pos_ref, table_ref, o_ref):
+    planes = table_ref.shape[1]
+    per = planes // peers
+    me = pos_ref[1]
+    row = lax.broadcasted_iota(jnp.int32, (planes, planes), 0)
+    col = lax.broadcasted_iota(jnp.int32, (planes, planes), 1)
+    swap = jnp.where(row == ((col // per) ^ me) * per + col % per, 1.0, 0.0).astype(BF16)
+    for half in range(2):
+        rows = pl.ds(half * planes, planes)
+        turned = dot(swap, table_ref[rows, :]).astype(BF16)
+        o_ref[rows, :] = dot(turned, swap).astype(BF16)
+
+
+def permuted_table(position, table, peers):
+    return pl.pallas_call(
+        functools.partial(permute_kernel, peers),
+        out_shape=jax.ShapeDtypeStruct(table.shape, BF16),
+        in_specs=[SMEM_SPEC, pl.BlockSpec(memory_space=pltpu.VMEM)],
+        compiler_params=params(),
+        cost_estimate=cost(1e8, 4e6),
+        name="permuted_table",
+    )(position, table)
+
+
+def transform_kernel(count, table_ref, *refs):
     planes = table_ref.shape[1]
     both = table_ref[...]
     high_table = both[:planes]
+    per, nodes, width = refs[0].shape
+    flat = [ref.reshape(per * nodes, width) for ref in refs]
     for n in range(nodes):
-        rows = pl.ds(n, planes, stride=nodes) if nodes > 1 else pl.ds(0, planes)
-        high, low = split(x_ref[rows, :])
+        rows = pl.ds(n, per, stride=nodes) if nodes > 1 else pl.ds(0, per)
+        high, low = split(jnp.concatenate([ref[rows, :] for ref in flat[:count]], axis=0))
         wide = dot(both, high)
-        o_ref[rows, :] = wide[:planes] + (wide[planes:] + dot(high_table, low))
-
-
-def transform(columns, table):
-    peers, per, nodes, elements = columns.shape
-    rows = peers * per * nodes
+        result = wide[:planes] + (wide[planes:] + dot(high_table, low))
+        for d, ref in enumerate(flat[count:]):
+            ref[rows, :] = result[d * per : (d + 1) * per]
+
+
+def transform(blocks, table):
+    per, nodes, elements = blocks[0].shape
     width = 128
-    flat = columns.reshape(rows, elements)
-    out = pl.pallas_call(
-        functools.partial(transform_kernel, nodes),
-        out_shape=jax.ShapeDtypeStruct((rows, elements), F32),
+    block = pl.BlockSpec((per, nodes, width), lambda i: (0, 0, i))
+    size = len(blocks) * blocks[0].size
+    return pl.pallas_call(
+        functools.partial(transform_kernel, len(blocks)),
+        out_shape=[jax.ShapeDtypeStruct(v.shape, F32) for v in blocks],
         grid=(elements // width,),
-        in_specs=[
-            pl.BlockSpec(table.shape, lambda i: (0, 0)),
-            pl.BlockSpec((rows, width), lambda i: (0, i)),
-        ],
-        out_specs=pl.BlockSpec((rows, width), lambda i: (0, i)),
-        compiler_params=params(),
-        cost_estimate=cost(6 * PLANES * rows * elements, 8 * rows * elements),
+        in_specs=[pl.BlockSpec(table.shape, lambda i: (0, 0))] + [block] * len(blocks),
+        out_specs=[block] * len(blocks),
+        compiler_params=params(),
+        cost_estimate=cost(6 * PLANES * size, 20 * size),
         name="transform",
-    )(table, flat)
-    return out.reshape(columns.shape)
+    )(table, *blocks)
+
+
+def pack_kernel(pos_ref, *refs):
+    count = len(refs) // 2
+    for source, target in zip(refs[:count], refs[count:]):
+        target[...] = source[0]
+
+
+def pack(position, adjoint, comp, peers):
+    _, per, nodes, elements = adjoint.shape
+    part = nodes // peers
+    block = per // 2
+
+    def source(d):
+        return pl.BlockSpec((1, block, part, elements), lambda i, pos: (comp, i, pos[1] ^ d, 0))
+
+    size = per * nodes * elements
+    return pl.pallas_call(
+        pack_kernel,
+        out_shape=[jax.ShapeDtypeStruct((per, part, elements), F32)] * peers,
+        grid_spec=pltpu.PrefetchScalarGridSpec(
+            num_scalar_prefetch=1,
+            grid=(per // block,),
+            in_specs=[source(d) for d in range(peers)],
+            out_specs=[pl.BlockSpec((block, part, elements), lambda i, pos: (i, 0, 0))] * peers,
+        ),
+        compiler_params=params(),
+        cost_estimate=cost(0, 16 * size),
+        name="pack",
+    )(position, *[adjoint] * peers)
 
 
 BXR, BYS, DXBX, DXBY, DYBX, DYBY, DIAG = range(7)
 
 
+def line_of(me, d):
+    return pl.ds(pl.multiple_of((me ^ d) * LINE, LINE), LINE)
+
+
+def own_order(ref, me, *lead):
+    lines = ref.shape[-2] // LINE
+    return jnp.concatenate([ref[(*lead, line_of(me, d), slice(None))] for d in range(lines)], axis=0)
+
+
 def prep_kernel(
-    bank_ref, snap_ref, geo_ref, dr_ref, ds_ref, st_ref, up_ref, lo_ref,
+    pos_ref, bank_ref, snap_ref, geo_ref, dr_ref, ds_ref, st_ref, up_ref, lo_ref,
     coef_ref, dpack_ref, spack_ref, gather_ref, scatter_ref, mask_ref,
 ):
     elements = geo_ref.shape[1]
     nodes = dr_ref.shape[0]
+    lines = nodes // LINE
+    me = pos_ref[1]
+    row = lax.broadcasted_iota(jnp.int32, (nodes, nodes), 0)
+    col = lax.broadcasted_iota(jnp.int32, (nodes, nodes), 1)
+    swap = jnp.where(row == ((col // LINE) ^ me) * LINE + col % LINE, 1.0, 0.0).astype(BF16)
+
+    def permuted(ref):
+        high, low = split(own_order(ref, me))
+        return dot(high, swap) + dot(low, swap)
+
     snap = snap_ref[...]
     base = [
-        sum(jnp.where(snap == k, bank_ref[k, i], 0.0) for k in range(bank_ref.shape[0]))
+        sum(
+            jnp.where(snap == k, own_order(bank_ref, me, k, i), 0.0)
+            for k in range(bank_ref.shape[0])
+        )
         for i in range(2)
     ]
     rx = geo_ref[0:1, :]
     sy = geo_ref[1:2, :]
-    dpack = pack_matrix(jnp.concatenate([dr_ref[...], ds_ref[...]], axis=0))
+    dpack = pack_matrix(jnp.concatenate([permuted(dr_ref), permuted(ds_ref)], axis=0))
     dpack_ref[...] = dpack
     bx = dot(dpack, pack_field(base[0]))
     by = dot(dpack, pack_field(base[1]))
@@ -120,14 +201,12 @@
     coef_ref[DXBY] = rx * by[:nodes]
     coef_ref[DYBX] = sy * bx[nodes:]
     coef_ref[DYBY] = sy * by[nodes:]
-    row = lax.broadcasted_iota(jnp.int32, (nodes, nodes), 0)
-    col = lax.broadcasted_iota(jnp.int32, (nodes, nodes), 1)
-    stiff = st_ref[...]
-    spack_ref[...] = pack_matrix(jnp.where(row == col, 0.0, stiff))
-    diag = jnp.sum(jnp.where(row == col, stiff, 0.0), axis=1, keepdims=True)
+    diag = jnp.sum(jnp.where(row == col, st_ref[...], 0.0), axis=0, keepdims=True)
+    own = ((row // LINE) ^ me) * LINE + row % LINE == col
+    diag = jnp.sum(jnp.where(own, diag, 0.0), axis=1, keepdims=True)
+    spack_ref[...] = pack_matrix(jnp.where(row == col, 0.0, permuted(st_ref)))
     coef_ref[DIAG] = jnp.broadcast_to(diag, (nodes, elements))
     shared = up_ref.shape[1]
-    lines = nodes // LINE
     for side, (ref, first) in enumerate(((up_ref, LINE - 1), (lo_ref, 0))):
         index = ref[...]
         node = index // elements
@@ -137,7 +216,7 @@
         gather_ref[side] = hot.astype(BF16)
         back = hot.T.astype(BF16)
         scatter_ref[side] = back
-        mask = lax.broadcasted_iota(jnp.int32, (lines, shared), 0) == node // LINE
+        mask = (lax.broadcasted_iota(jnp.int32, (lines, shared), 0) ^ me) == node // LINE
         mask = jnp.where(mask, 1.0, 0.0)
         mask_ref[side] = mask
         count = dot(mask.astype(BF16), back)
@@ -146,7 +225,7 @@
             coef_ref[DIAG, n : n + 1, :] = coef_ref[DIAG, n : n + 1, :] + PENALTY * count[s : s + 1]
 
 
-def prepare(base_bank, snapshot, geometry, diff_r, diff_s, stiffness, upper, lower):
+def prepare(position, base_bank, snapshot, geometry, diff_r, diff_s, stiffness, upper, lower):
     nodes = diff_r.shape[0]
     elements = geometry.shape[1]
     shared = upper.shape[1]
@@ -160,10 +239,11 @@
             jax.ShapeDtypeStruct((2, shared, elements), BF16),
             jax.ShapeDtypeStruct((2, nodes // LINE, shared), F32),
         ],
-        compiler_params=params(),
-        cost_estimate=cost(1e7, 4e6),
+        in_specs=[SMEM_SPEC] + [pl.BlockSpec(memory_space=pltpu.VMEM)] * 8,
+        compiler_params=params(),
+        cost_estimate=cost(1e7, 8e6),
         name="prepare",
-    )(base_bank, snapshot.reshape(1, elements), geometry, diff_r, diff_s, stiffness, upper, lower)
+    )(position, base_bank, snapshot.reshape(1, elements), geometry, diff_r, diff_s, stiffness, upper, lower)
 
 
 def face_of(ref, side):
@@ -201,9 +281,10 @@
 
 
 def start_kernel(
-    block, pos_ref, z_ref, x_ref, geo_ref, diag_ref, dpack_ref, spack_ref, gather_ref, mask_ref,
-    source_ref, inverse_ref, local_ref, up_ref, lo_ref, pot_ref,
+    block, count, pos_ref, geo_ref, diag_ref, dpack_ref, spack_ref, gather_ref, mask_ref, *refs
 ):
+    z_refs, x_refs = refs[:count], refs[count : 2 * count]
+    source_ref, inverse_ref, local_ref, up_ref, lo_ref, pot_ref = refs[2 * count :]
     nodes, elements = diag_ref.shape[1:]
     beta = 4.0 / PLANES
     first = pos_ref[0] * (block * pl.num_programs(0)) + pl.program_id(0) * block
@@ -217,8 +298,8 @@
         wave = beta * (index // 2).astype(F32)
         shift = beta * jnp.where(index == 1, PLANES // 2, index // 2).astype(F32)
         shift = shift * shift
-        z = z_ref[:, c].reshape(nodes, elements)
-        other = x_ref[:, c + 1 if c % 2 == 0 else c - 1].reshape(nodes, elements)
+        z = slab(z_refs, c)
+        other = slab(x_refs, c + 1 if c % 2 == 0 else c - 1)
         turned = (wave if c % 2 == 0 else -wave) * other
         source = turned - rx * dot(drpack, pack_field(z))
         inverse = RELAXATION / (diag + shift * mass)
@@ -239,34 +320,32 @@
     return pl.BlockSpec(shape, lambda *i: (0,) * len(shape))
 
 
-SMEM_SPEC = pl.BlockSpec(memory_space=pltpu.SMEM)
-
-
 def start_solve(position, z, x, geometry, coef, dpack, spack, gather, mask):
-    groups, coefs, part, elements = z.shape
-    nodes = groups * part
+    coefs, part, elements = z[0].shape
+    nodes = len(z) * part
     shared = gather.shape[2]
     block = coef_block(coefs)
-    field = pl.BlockSpec((groups, block, part, elements), lambda i: (0, i, 0, 0))
+    field = [pl.BlockSpec((block, part, elements), lambda i: (i, 0, 0))] * len(z)
     flat = pl.BlockSpec((block * nodes, elements), lambda i: (i, 0))
     face = pl.BlockSpec((3, block, shared), lambda i: (0, i, 0))
     size = coefs * nodes * elements
     return pl.pallas_call(
-        functools.partial(start_kernel, block),
+        functools.partial(start_kernel, block, len(z)),
         out_shape=[jax.ShapeDtypeStruct((coefs * nodes, elements), F32)] * 3
         + [jax.ShapeDtypeStruct((3, coefs, shared), F32)] * 2,
         grid=(coefs // block,),
         in_specs=[
-            SMEM_SPEC, field, field, whole(geometry.shape),
+            SMEM_SPEC, whole(geometry.shape),
             pl.BlockSpec((1, nodes, elements), lambda i: (DIAG, 0, 0)),
             whole(dpack.shape), whole(spack.shape), whole(gather.shape), whole(mask.shape),
+            *field, *field,
         ],
         out_specs=[flat, flat, flat, face, face],
         scratch_shapes=[pltpu.VMEM((block * nodes, elements), F32)],
         compiler_params=params(),
         cost_estimate=cost(12 * nodes * size, 20 * size),
         name="start_solve",
-    )(position, z, x, geometry, coef, dpack, spack, gather, mask)
+    )(position, geometry, coef, dpack, spack, gather, mask, *z, *x)
 
 
 def sweeps_kernel(
@@ -336,37 +415,44 @@
     )(local, source, inverse, *own, *got, *inv, spack, gather, scatter, mask)
 
 
-def partial_kernel(block, z_ref, x_ref, coef_ref, dpack_ref, o_ref):
-    nodes, elements = coef_ref.shape[1:]
+def store_own(ref, me, value, *lead):
+    for d in range(value.shape[0] // LINE):
+        ref[(*lead, line_of(me, d), slice(None))] = value[d * LINE : (d + 1) * LINE]
+
+
+def partial_kernel(block, count, pos_ref, coef_ref, dpack_ref, *refs):
+    z_refs, x_refs, o_ref = refs[:count], refs[count : 2 * count], refs[2 * count]
+    nodes = coef_ref.shape[1]
     dpack = dpack_ref[...]
+    me = pos_ref[1]
     for c in range(block):
-        z = z_ref[:, c].reshape(nodes, elements)
+        z = slab(z_refs, c)
         slopes = dot(dpack, pack_field(z))
         moved = coef_ref[BXR] * slopes[:nodes] + coef_ref[BYS] * slopes[nodes:]
-        o_ref[2, c] = z - TIME_STEP * (moved + INTERACTION * z)
-        x = x_ref[:, c].reshape(nodes, elements)
+        store_own(o_ref, me, z - TIME_STEP * (moved + INTERACTION * z), 2, c)
+        x = slab(x_refs, c)
         slopes = dot(dpack, pack_field(x))
         moved = coef_ref[BXR] * slopes[:nodes] + coef_ref[BYS] * slopes[nodes:]
-        o_ref[0, c] = x + TIME_STEP * (x * coef_ref[DXBX] - moved - INTERACTION * x)
-        o_ref[1, c] = TIME_STEP * (x * coef_ref[DYBX])
-
-
-def partial_update(z, x, coef, dpack):
-    groups, coefs, part, elements = z.shape
-    nodes = groups * part
+        store_own(o_ref, me, x + TIME_STEP * (x * coef_ref[DXBX] - moved - INTERACTION * x), 0, c)
+        store_own(o_ref, me, TIME_STEP * (x * coef_ref[DYBX]), 1, c)
+
+
+def partial_update(position, z, x, coef, dpack):
+    coefs, part, elements = z[0].shape
+    nodes = len(z) * part
     block = coef_block(coefs)
-    field = pl.BlockSpec((groups, block, part, elements), lambda i: (0, i, 0, 0))
+    field = [pl.BlockSpec((block, part, elements), lambda i: (i, 0, 0))] * len(z)
     size = coefs * nodes * elements
     return pl.pallas_call(
-        functools.partial(partial_kernel, block),
+        functools.partial(partial_kernel, block, len(z)),
         out_shape=jax.ShapeDtypeStruct((3, coefs, nodes, elements), F32),
         grid=(coefs // block,),
-        in_specs=[field, field, whole(coef.shape), whole(dpack.shape)],
+        in_specs=[SMEM_SPEC, whole(coef.shape), whole(dpack.shape), *field, *field],
         out_specs=pl.BlockSpec((3, block, nodes, elements), lambda i: (0, i, 0, 0)),
         compiler_params=params(),
-        cost_estimate=cost(24 * nodes * size, 20 * size),
+        cost_estimate=cost(24 * nodes * size, 45 * size),
         name="partial_update",
-    )(z, x, coef, dpack)
+    )(position, coef, dpack, *z, *x)
 
 
 def force_kernel(
@@ -376,6 +462,7 @@
     nodes = dpack_ref.shape[0] // 2
     scale = TIME_STEP * INTERACTION
     which = pl.program_id(1)
+    me = pos_ref[1]
 
     @pl.when(which == 0)
     def _():
@@ -389,7 +476,8 @@
             wave = (4.0 / PLANES) * ((first + c) // 2).astype(F32)
             factor = scale * (wave if c % 2 == 0 else -wave)
             other = c + 1 if c % 2 == 0 else c - 1
-            o_ref[0, c] = part_ref[0, c] + factor * pot_ref[pl.ds(other * nodes, nodes), :]
+            turned = factor * pot_ref[pl.ds(other * nodes, nodes), :]
+            store_own(o_ref, me, own_order(part_ref, me, 0, c) + turned, 0, c)
 
     @pl.when(which == 1)
     def _():
@@ -397,7 +485,7 @@
         factor = scale * geo_ref[0:1, :]
         for c in range(block):
             slope = dot(drpack, pack_field(pot_ref[pl.ds(c * nodes, nodes), :]))
-            o_ref[0, c] = part_ref[0, c] - factor * slope
+            store_own(o_ref, me, own_order(part_ref, me, 0, c) - factor * slope, 0, c)
 
 
 def add_force(position, local, inverse, got, geometry, dpack, scatter, mask, partial):
@@ -425,46 +513,47 @@
     )(position, local, inverse, *got, geometry, dpack, scatter, mask, partial)
 
 
-def finish_kernel(block, y_ref, coef_ref, dpack_ref, part_ref, o_ref):
-    nodes, elements = coef_ref.shape[1:]
+def finish_kernel(block, count, pos_ref, coef_ref, dpack_ref, part_ref, *refs):
+    y_refs, o_ref = refs[:count], refs[count]
+    nodes = coef_ref.shape[1]
     which = pl.program_id(1)
+    me = pos_ref[1]
 
     @pl.when(which == 0)
     def _():
         for c in range(block):
-            y = y_ref[:, c].reshape(nodes, elements)
-            o_ref[0, c] = part_ref[0, c] + TIME_STEP * (y * coef_ref[DXBY])
+            y = slab(y_refs, c)
+            store_own(o_ref, me, own_order(part_ref, me, 0, c) + TIME_STEP * (y * coef_ref[DXBY]), 0, c)
 
     @pl.when(which == 1)
     def _():
         dpack = dpack_ref[...]
         for c in range(block):
-            y = y_ref[:, c].reshape(nodes, elements)
+            y = slab(y_refs, c)
             slopes = dot(dpack, pack_field(y))
             moved = coef_ref[BXR] * slopes[:nodes] + coef_ref[BYS] * slopes[nodes:]
-            o_ref[0, c] = part_ref[0, c] + y + TIME_STEP * (y * coef_ref[DYBY] - moved)
-
-
-def finish(y, coef, dpack, partial):
-    groups, coefs, part, elements = y.shape
-    nodes = groups * part
+            change = y + TIME_STEP * (y * coef_ref[DYBY] - moved)
+            store_own(o_ref, me, own_order(part_ref, me, 0, c) + change, 0, c)
+
+
+def finish(position, y, coef, dpack, partial):
+    coefs, part, elements = y[0].shape
+    nodes = len(y) * part
     block = coef_block(coefs)
     comp = pl.BlockSpec((1, block, nodes, elements), lambda i, j: (j, i, 0, 0))
     size = coefs * nodes * elements
     return pl.pallas_call(
-        functools.partial(finish_kernel, block),
+        functools.partial(finish_kernel, block, len(y)),
         out_shape=jax.ShapeDtypeStruct(partial.shape, F32),
         grid=(coefs // block, 2),
-        in_specs=[
-            pl.BlockSpec((groups, block, part, elements), lambda i, j: (0, i, 0, 0)),
-            whole(coef.shape), whole(dpack.shape), comp,
-        ],
+        in_specs=[SMEM_SPEC, whole(coef.shape), whole(dpack.shape), comp]
+        + [pl.BlockSpec((block, part, elements), lambda i, j: (i, 0, 0))] * len(y),
         out_specs=comp,
         input_output_aliases={3: 0},
         compiler_params=params(),
-        cost_estimate=cost(12 * nodes * size, 20 * size),
+        cost_estimate=cost(12 * nodes * size, 50 * size),
         name="finish",
-    )(y, coef, dpack, partial)
+    )(position, coef, dpack, partial, *y)
 
 
 def to_all(blocks):
@@ -483,45 +572,66 @@
 ):
     _, per, nodes, elements = adjoint.shape
     peers = lax.axis_size("four")
-    share = nodes // peers
-    table = jnp.asarray(coef_table(PLANES))
-    position = lax.axis_index("four").astype(jnp.int32).reshape(1)
+    lines = nodes // LINE
+    direct = peers == lines
+    place = lax.axis_index("four").astype(jnp.int32)
+    position = jnp.stack([place, place if direct else jnp.zeros_like(place)])
+    table = permuted_table(position, jnp.asarray(coef_table(PLANES)), lines)
+
+    def exchange(blocks):
+        return [blocks[0]] + [
+            lax.ppermute(blocks[d], "four", [(i, i ^ d) for i in range(peers)]) for d in range(1, peers)
+        ]
 
     def columns(comp):
-        blocks = adjoint[comp].reshape(per, peers, share, elements)
-        return to_all(jnp.swapaxes(blocks, 0, 1))
-
-    def coefficients(cols):
-        got = to_all(transform(cols, table))
-        if share % 8:
-            got = jnp.swapaxes(got, 0, 1).reshape(1, per, nodes, elements)
-        return got
-
-    z_cols = columns(2)
-    x_cols = columns(0)
+        if direct:
+            return pack(position, adjoint, comp, peers)
+        return [jnp.moveaxis(adjoint[comp].reshape(per, peers, nodes // peers, elements), 1, 0)]
+
+    def spread(blocks):
+        if direct:
+            return exchange(blocks)
+        return [to_all(blocks[0]).reshape(per * peers, nodes // peers, elements)]
+
+    def collect(blocks):
+        if direct:
+            return exchange(blocks)
+        got = to_all(blocks[0].reshape(peers, per, nodes // peers, elements))
+        got = jnp.moveaxis(got, 0, 1).reshape(per, lines, LINE, elements)
+        return [got[:, d] for d in range(lines)]
+
+    z_blocks = columns(2)
+    x_blocks = columns(0)
+    y_blocks = columns(1)
+    z_blocks, x_blocks = lax.optimization_barrier((z_blocks, x_blocks))
+    z_columns = spread(z_blocks)
+    x_columns = spread(x_blocks)
     coef, dpack, spack, gather, scatter, mask = prepare(
-        base_bank, snapshot, geometry, diff_r, diff_s, stiffness, upper_list, lower_list
+        position, base_bank, snapshot, geometry, diff_r, diff_s, stiffness, upper_list, lower_list
     )
-    z = coefficients(z_cols)
-    x = coefficients(x_cols)
-    y_cols = columns(1)
+    z_coefs = transform(z_columns, table)
+    z = collect(z_coefs)
+    x_coefs = transform(x_columns, table)
+    x_coefs, y_blocks = lax.optimization_barrier((x_coefs, y_blocks))
+    x = collect(x_coefs)
+    y_columns = spread(y_blocks)
     source, inverse, local, up, lo = start_solve(
         position, z, x, geometry, coef, dpack, spack, gather, mask
     )
     got = swap_faces(up, lo)
     inv = got
-    partial = partial_update(z, x, coef, dpack)
+    partial = partial_update(position, z, x, coef, dpack)
     local, up, lo = two_sweeps(
         2, local, source, inverse, (up, lo), got, inv, spack, gather, scatter, mask
     )
     got = swap_faces(up, lo)
+    y = collect(transform(y_columns, table))
     local, up, lo = two_sweeps(
         1, local, source, inverse, (up, lo), got, inv, spack, gather, scatter, mask
     )
     got = swap_faces(up, lo)
     partial = add_force(position, local, inverse, got, geometry, dpack, scatter, mask, partial)
-    y = coefficients(y_cols)
-    return finish(y, coef, dpack, partial)
+    return finish(position, y, coef, dpack, partial)
 
 
 def solution(mesh):

time: 241 us -> 201 us (0.83)
  waiting for transfers between devices: 128 us -> 83.5 us
  local copies, waits for them, and re-layouts: 27.6 us -> 1.4 us
  starting transfers between devices: 32.7 us -> 58.6 us
  Pallas kernels: 50.6 us -> 56.6 us
    all_to_all x6 -> x0, waiting for transfers between devices: 112 us -> none  [to_all(): lax.all_to_all(blocks, 'four', split_axis=0, concat_axis=0, tiled=True)]
    ppermute x0 -> x42, waiting for transfers between devices: none -> 75.4 us  [exchange(): lax.ppermute(blocks[d], 'four', [(i, i ^ d) for i in range(peers)])]
    ppermute x0 -> x42, starting transfers between devices: none -> 47.5 us  [exchange(): lax.ppermute(blocks[d], 'four', [(i, i ^ d) for i in range(peers)])]
    all_to_all x6 -> x0, starting transfers between devices: 25 us -> none  [to_all(): lax.all_to_all(blocks, 'four', split_axis=0, concat_axis=0, tiled=True)]
    another operation x4 -> x0, local copies, waits for them, and re-layouts: 13.6 us -> none  [columns(): blocks = adjoint[comp].reshape(per, peers, share, elements)]
    unnamed x42 -> x22, local copies, waits for them, and re-layouts: 14.1 us -> 1.4 us
    ppermute x6, waiting for transfers between devices: 16.4 us -> 8.13 us  [swap_faces(): return (lax.ppermute(lo, 'dom', down_way), lax.ppermute(up, 'dom', up_way))]
    pallas_call x6 -> x10, Pallas kernels: 28.5 us -> 33.8 us  [the longest x1 7.79 us: finish(): pl.pallas_call(functools.partial(finish_kernel, block, len(y)), out_shape...]
  transfers between devices with their start and end apart: 12 -> 48, of which waited for: 9 -> 19; matrix products, arithmetic and copies ran while one was open for 3% -> 0% of each run, Pallas kernels for 18% -> 22%
where the time goes in v3:
time: 201 us; the launch traced here: 200 us
  waiting for transfers between devices  83.5 us (42%)
  starting transfers between devices  58.6 us (29%)
  Pallas kernels  56.6 us (28%)
    ppermute x42, waiting for transfers between devices, exchange(): lax.ppermute(blocks[d], 'four', [(i, i ^ d) for i in range(peers)])  75.4 us
    ppermute x42, starting transfers between devices, exchange(): lax.ppermute(blocks[d], 'four', [(i, i ^ d) for i in range(peers)])  47.5 us
    pallas_call x2, Pallas kernels, two_sweeps(): pl.pallas_call(functools.partial(sweeps_kernel, block, keep), out_shape=[...  13.7 us
    ppermute x6, starting transfers between devices, swap_faces(): return (lax.ppermute(lo, 'dom', down_way), lax.ppermute(up, 'dom', up_way))  11 us
    ppermute x6, waiting for transfers between devices, swap_faces(): return (lax.ppermute(lo, 'dom', down_way), lax.ppermute(up, 'dom', up_way))  8.13 us
    pallas_call x1, Pallas kernels, add_force(): pl.pallas_call(functools.partial(force_kernel, block), out_shape=jax.Shap...  7.92 us
    pallas_call x1, Pallas kernels, finish(): pl.pallas_call(functools.partial(finish_kernel, block, len(y)), out_shape...  7.79 us
    pallas_call x3, Pallas kernels, transform(): pl.pallas_call(functools.partial(transform_kernel, len(blocks)), out_shap...  7.4 us
  transfers between devices with their start and end apart: 48, of which 19 were waited for; matrix products, arithmetic and copies ran while one was open for 0% of the time, Pallas kernels for 22%

profile of v3, /device:TPU:0, one launch (start us, length us, event | category | flops | bytes accessed | tf_op | source)
XLA Modules:
  0.0 200.4 jit_solution(5254409167657102046)
XLA Ops:
  0.1 2.4 %pack.3 = (f32[32,8,256]{2,1,0:T(8,128)S(1)}, f32[32,8,256]{2,1,0:T(8,128)S(1)}, f32[32,8,256]{2,1,0:T(8,128)S(1)}, f32[32,8,256]{2,1,0:T(8,128)S(1)}, f32[32,8,...) custom-call(s32[2]{0:T(128)S(1)} %pad_add_fusion.pos_ref, ...), custom_call_target="tpu_custom_call" | custom-call | bytes 8388608 | tf_op jit(solution)/shard_map/pack/pallas_call | solution.py:141
  2.5 2.4 %pack.4 = (f32[32,8,256]{2,1,0:T(8,128)S(1)}, f32[32,8,256]{2,1,0:T(8,128)S(1)}, f32[32,8,256]{2,1,0:T(8,128)S(1)}, f32[32,8,256]{2,1,0:T(8,128)S(1)}, f32[32,8,...) custom-call(s32[2]{0:T(128)S(1)} %pad_add_fusion.pos_ref, ...), custom_call_target="tpu_custom_call" | custom-call | bytes 8388608 | tf_op jit(solution)/shard_map/pack/pallas_call | solution.py:141
  5.4 2.6 %collective-permute-start.1 = (f32[32,8,256]{2,1,0:T(8,128)S(1)}, f32[32,8,256]{2,1,0:T(8,128)S(1)}, u32[]{:S(2)}, u32[]{:S(2)}) collective-permute-start(f32[32,8,256]{2,1,0:T(8,128)S(1)} %get-tuple-element.125), channel_id=1, source_target_pairs={{0,2},{1,3},{2,0},{3,1},{4,6},{5,7},{6,4},{7,5},{8,10},{9,11},{10,... | collective-permute-start | bytes 786440 | tf_op jit(solution)/shard_map/ppermute | solution.py:583
  8.0 1.8 collective-permute-start.3
  9.8 2.6 %collective-permute-start.5 = (f32[32,8,256]{2,1,0:T(8,128)S(1)}, f32[32,8,256]{2,1,0:T(8,128)S(1)}, u32[]{:S(2)}, u32[]{:S(2)}) collective-permute-start(f32[32,8,256]{2,1,0:T(8,128)S(1)} %get-tuple-element.129), channel_id=1, source_target_pairs={{0,6},{1,7},{2,4},{3,5},{4,2},{5,3},{6,0},{7,1},{8,14},{9,15},{10,... | collective-permute-start | bytes 786440 | tf_op jit(solution)/shard_map/ppermute | solution.py:583
  12.4 2.7 %collective-permute-done.1.refs_2_ = f32[32,8,256]{2,1,0:T(8,128)S(1)} collective-permute-done((f32[32,8,256]{2,1,0:T(8,128)S(1)}, f32[32,8,256]{2,1,0:T(8,128)S(1)}, u32[]{:S(2)}, u32[]{:S(2)}) %collective-permute-start.1) | collective-permute-done | bytes 262176 | tf_op jit(solution)/shard_map/ppermute | solution.py:583
  15.1 1.7 collective-permute-start.6
  16.8 3.4 %collective-permute-done.2.refs_3_ = f32[32,8,256]{2,1,0:T(8,128)S(1)} collective-permute-done((f32[32,8,256]{2,1,0:T(8,128)S(1)}, f32[32,8,256]{2,1,0:T(8,128)S(1)}, u32[]{:S(2)}, u32[]{:S(2)}) %collective-permute-start.2) | collective-permute-done | bytes 262176 | tf_op jit(solution)/shard_map/ppermute | solution.py:583
  20.8 1.9 collective-permute-start.15
  22.8 9.9 %collective-permute-done.4.refs_5_ = f32[32,8,256]{2,1,0:T(8,128)S(1)} collective-permute-done((f32[32,8,256]{2,1,0:T(8,128)S(1)}, f32[32,8,256]{2,1,0:T(8,128)S(1)}, u32[]{:S(2)}, u32[]{:S(2)}) %collective-permute-start.4) | collective-permute-done | bytes 262176 | tf_op jit(solution)/shard_map/ppermute | solution.py:583
  32.7 2.2 %collective-permute-start.16 = (f32[32,8,256]{2,1,0:T(8,128)S(1)}, f32[32,8,256]{2,1,0:T(8,128)S(1)}, u32[]{:S(2)}, u32[]{:S(2)}) collective-permute-start(f32[32,8,256]{2,1,0:T(8,128)S(1)} %get-tuple-element.142), channel_id=1, source_target_pairs={{0,3},{1,2},{2,1},{3,0},{4,7},{5,6},{6,5},{7,4},{8,11},{9,10},{10,... | collective-permute-start | bytes 786440 | tf_op jit(solution)/shard_map/ppermute | solution.py:583
  34.9 1.5 collective-permute-start.17
  37.3 2.5 %transform.3 = (f32[32,8,256]{2,1,0:T(8,128)S(1)}, f32[32,8,256]{2,1,0:T(8,128)S(1)}, f32[32,8,256]{2,1,0:T(8,128)S(1)}, f32[32,8,256]{2,1,0:T(8,128)S(1)}, f32[...) custom-call(bf16[512,256]{1,0:T(8,128)(2,1)S(1)} %permuted_table.1.tab, ...), custom_call_target="tpu_custom_call" | custom-call | flops 805306368 | bytes 10485760 | tf_op jit(solution)/shard_map/transform/pallas_call | solution.py:114
  41.1 1.7 collective-permute-start.20
  44.9 13.9 %collective-permute-done.18.refs_5_ = f32[32,8,256]{2,1,0:T(8,128)S(1)} collective-permute-done((f32[32,8,256]{2,1,0:T(8,128)S(1)}, f32[32,8,256]{2,1,0:T(8,128)S(1)}, u32[]{:S(2)}, u32[]{:S(2)}) %collective-permute-start.18) | collective-permute-done | bytes 262176 | tf_op jit(solution)/shard_map/ppermute | solution.py:583
  60.0 1.5 collective-permute-start.10
  61.6 1.5 collective-permute-start.12
  63.0 2.4 %pack.5 = (f32[32,8,256]{2,1,0:T(8,128)S(1)}, f32[32,8,256]{2,1,0:T(8,128)S(1)}, f32[32,8,256]{2,1,0:T(8,128)S(1)}, f32[32,8,256]{2,1,0:T(8,128)S(1)}, f32[32,8,...) custom-call(s32[2]{0:T(128)S(1)} %pad_add_fusion.pos_ref, ...), custom_call_target="tpu_custom_call" | custom-call | bytes 8388608 | tf_op jit(solution)/shard_map/pack/pallas_call | solution.py:141
  65.5 2.5 %transform.4 = (f32[32,8,256]{2,1,0:T(8,128)S(1)}, f32[32,8,256]{2,1,0:T(8,128)S(1)}, f32[32,8,256]{2,1,0:T(8,128)S(1)}, f32[32,8,256]{2,1,0:T(8,128)S(1)}, f32[...) custom-call(bf16[512,256]{1,0:T(8,128)(2,1)S(1)} %permuted_table.1.tab, ...), custom_call_target="tpu_custom_call" | custom-call | flops 805306368 | bytes 10485760 | tf_op jit(solution)/shard_map/transform/pallas_call | solution.py:114
  68.0 1.5 collective-permute-start.13
  69.7 10.4 %collective-permute-done.10.refs_4_ = f32[32,8,256]{2,1,0:T(8,128)S(1)} collective-permute-done((f32[32,8,256]{2,1,0:T(8,128)S(1)}, f32[32,8,256]{2,1,0:T(8,128)S(1)}, u32[]{:S(2)}, u32[]{:S(2)}) %collective-permute-start.10) | collective-permute-done | bytes 262176 | tf_op jit(solution)/shard_map/ppermute | solution.py:583
  80.1 1.7 collective-permute-start.22
  81.7 2.2 %collective-permute-done.11.refs_5_ = f32[32,8,256]{2,1,0:T(8,128)S(1)} collective-permute-done((f32[32,8,256]{2,1,0:T(8,128)S(1)}, f32[32,8,256]{2,1,0:T(8,128)S(1)}, u32[]{:S(2)}, u32[]{:S(2)}) %collective-permute-start.11) | collective-permute-done | bytes 262176 | tf_op jit(solution)/shard_map/ppermute | solution.py:583
  84.0 1.7 collective-permute-start.23
  88.2 1.9 collective-permute-start.27
  90.1 2.3 %collective-permute-done.23.refs_11_ = f32[32,8,256]{2,1,0:T(8,128)S(1)} collective-permute-done((f32[32,8,256]{2,1,0:T(8,128)S(1)}, f32[32,8,256]{2,1,0:T(8,128)S(1)}, u32[]{:S(2)}, u32[]{:S(2)}) %collective-permute-start.23) | collective-permute-done | bytes 262176 | tf_op jit(solution)/shard_map/ppermute | solution.py:583
  93.7 12.5 %collective-permute-done.24.refs_12_ = f32[32,8,256]{2,1,0:T(8,128)S(1)} collective-permute-done((f32[32,8,256]{2,1,0:T(8,128)S(1)}, f32[32,8,256]{2,1,0:T(8,128)S(1)}, u32[]{:S(2)}, u32[]{:S(2)}) %collective-permute-start.24) | collective-permute-done | bytes 262176 | tf_op jit(solution)/shard_map/ppermute | solution.py:583
  106.9 2.3 %collective-permute-done.25.refs_13_ = f32[32,8,256]{2,1,0:T(8,128)S(1)} collective-permute-done((f32[32,8,256]{2,1,0:T(8,128)S(1)}, f32[32,8,256]{2,1,0:T(8,128)S(1)}, u32[]{:S(2)}, u32[]{:S(2)}) %collective-permute-start.25) | collective-permute-done | bytes 262176 | tf_op jit(solution)/shard_map/ppermute | solution.py:583
  109.2 1.7 collective-permute-start.36
  113.4 1.9 collective-permute-start.40
  116.6 5.6 %start_solve.1 = (f32[2048,256]{1,0:T(8,128)}, f32[2048,256]{1,0:T(8,128)}, f32[2048,256]{1,0:T(8,128)}, f32[3,32,512]{2,1,0:T(8,128)S(1)}, f32[3,32,512]{2,1,0:T(8,128)S(1)}) custom-call(s32[2]{0:T(128)S(1)} %pad_add_fusion.pos_ref, f32[2,256]{1,0:T(2,128)S(1)} %copy-done.7, f32[7,64,256]{2,1,0:T(8,128)S(1)} %get-tuple-element.102.diag_ref.coef_ref, ...), custom_call_target="tpu_custom_call" | custom-call | flops 402653184 | bytes 10485760 | tf_op jit(solution)/shard_map/start_solve/pallas_call | solution.py:332
  122.1 3.6 %collective-permute-start.28 = (f32[3,32,512]{2,1,0:T(8,128)S(1)}, f32[3,32,512]{2,1,0:T(8,128)S(1)}, u32[]{:S(2)}, u32[]{:S(2)}) collective-permute-start(f32[3,32,512]{2,1,0:T(8,128)S(1)} %get-tuple-element.175.own_lo_ref), channel_id=1, source_target_pairs={{8,0},{16,8},{24,16},{0,24},{9,1},{17,9},{25,17},{1,25},{10,2},{18... | collective-permute-start | bytes 589832 | tf_op jit(solution)/shard_map/ppermute | solution.py:567
  125.7 5.7 %collective-permute-done.37.refs_4_ = f32[32,8,256]{2,1,0:T(8,128)S(1)} collective-permute-done((f32[32,8,256]{2,1,0:T(8,128)S(1)}, f32[32,8,256]{2,1,0:T(8,128)S(1)}, u32[]{:S(2)}, u32[]{:S(2)}) %collective-permute-start.37) | collective-permute-done | bytes 262176 | tf_op jit(solution)/shard_map/ppermute | solution.py:583
  131.4 1.6 collective-permute-start.29
  133.0 1.4 collective-permute-done.38.refs_5_
  134.3 2.4 %transform.5 = (f32[32,8,256]{2,1,0:T(8,128)S(1)}, f32[32,8,256]{2,1,0:T(8,128)S(1)}, f32[32,8,256]{2,1,0:T(8,128)S(1)}, f32[32,8,256]{2,1,0:T(8,128)S(1)}, f32[...) custom-call(bf16[512,256]{1,0:T(8,128)(2,1)S(1)} %permuted_table.1.tab, ...), custom_call_target="tpu_custom_call" | custom-call | flops 805306368 | bytes 10485760 | tf_op jit(solution)/shard_map/transform/pallas_call | solution.py:114
  138.8 6.7 %two_sweeps.2 = (f32[2048,256]{1,0:T(8,128)S(1)}, f32[2,32,512]{2,1,0:T(8,128)S(1)}, f32[2,32,512]{2,1,0:T(8,128)S(1)}) custom-call(f32[2048,256]{1,0:T(8,128)} %get-tuple-element.171.local_ref, f32[2048,256]{1,0:T(8,128)} %get-tuple-element.172.source_ref, f32[2048,256]{1,0:T(8,128)} %get-tuple-element.173.inverse_ref, ...), custom_call_target="tpu_custom_call" | custom-call | flops 402653184 | bytes 8388608 | tf_op jit(solution)/shard_map/two_sweeps/pallas_call | solution.py:401
  145.5 1.3 copy-done.1
  146.9 3.8 %collective-permute-start.30 = (f32[2,32,512]{2,1,0:T(8,128)S(1)}, f32[2,32,512]{2,1,0:T(8,128)S(1)}, u32[]{:S(2)}, u32[]{:S(2)}) collective-permute-start(f32[2,32,512]{2,1,0:T(8,128)S(1)} %get-tuple-element.179.own_lo_ref), channel_id=1, source_target_pairs={{8,0},{16,8},{24,16},{0,24},{9,1},{17,9},{25,17},{1,25},{10,2},{18... | collective-permute-start | bytes 393224 | tf_op jit(solution)/shard_map/ppermute | solution.py:567
  150.7 3.9 %collective-permute-done.30.got_up_ref = f32[2,32,512]{2,1,0:T(8,128)S(1)} collective-permute-done((f32[2,32,512]{2,1,0:T(8,128)S(1)}, f32[2,32,512]{2,1,0:T(8,128)S(1)}, u32[]{:S(2)}, u32[]{:S(2)}) %collective-permute-start.30) | collective-permute-done | bytes 131104 | tf_op jit(solution)/shard_map/ppermute | solution.py:567
  154.6 2.9 %collective-permute-done.31.got_lo_ref = f32[2,32,512]{2,1,0:T(8,128)S(1)} collective-permute-done((f32[2,32,512]{2,1,0:T(8,128)S(1)}, f32[2,32,512]{2,1,0:T(8,128)S(1)}, u32[]{:S(2)}, u32[]{:S(2)}) %collective-permute-start.31) | collective-permute-done | bytes 131104 | tf_op jit(solution)/shard_map/ppermute | solution.py:567
  157.4 7.1 %two_sweeps.3 = (f32[2048,256]{1,0:T(8,128)S(1)}, f32[1,32,512]{2,1,0:T(8,128)S(1)}, f32[1,32,512]{2,1,0:T(8,128)S(1)}) custom-call(f32[2048,256]{1,0:T(8,128)} %copy-done.1, f32[2048,256]{1,0:T(8,128)} %get-tuple-element.172.source_ref, f32[2048,256]{1,0:T(8,128)} %get-tuple-element.173.inverse_ref, f32[2,32,512]{2,1,0:T(8,128)S(1)} %get-tuple-element.178.own_up_ref, ...), custom_call_target="tpu_custom_call" | custom-call | flops 402653184 | bytes 8388608 | tf_op jit(solution)/shard_map/two_sweeps/pallas_call | solution.py:401
  164.5 1.5 collective-permute-start.32
  169.4 1.9 collective-permute-start.46
  172.1 5.0 %partial_update.1.part_ref = f32[3,32,64,256]{3,2,1,0:T(8,128)} custom-call(s32[2]{0:T(128)S(1)} %pad_add_fusion.pos_ref, f32[7,64,256]{2,1,0:T(8,128)S(1)} %get-tuple-element.102.diag_ref.coef_ref, bf16[128,192]{1,0:T(8,128)(2,1)S(1)} %get-tuple-element.103.dpack_ref, f32[32,8,256]{2,1,0:T(8,128)S(1)} %get-tuple-element.131.refs_0_, ...), custom_call_target="tpu_custom_call" | custom-call | flops 805306368 | bytes 23592960 | tf_op jit(solution)/shard_map/partial_update/pallas_call | solution.py:446
  177.0 7.9 %add_force.1.part_ref = f32[3,32,64,256]{3,2,1,0:T(8,128)} custom-call(s32[2]{0:T(128)S(1)} %pad_add_fusion.pos_ref, f32[2048,256]{1,0:T(8,128)S(1)} %get-tuple-element.180.local_ref, f32[2048,256]{1,0:T(8,128)S(1)} %copy-done, f32[1,32,512]{2,1,0:T(8,128)S(1)} %collective-permute-done.32.got_up_ref, ...), custom_call_target="tpu_custom_call", output_to_operand_aliasing={{}: (9, {})} | custom-call | flops 201326592 | bytes 12582912 | tf_op jit(solution)/shard_map/add_force/pallas_call | solution.py:499
  185.4 7.2 %collective-permute-done.45.refs_5_ = f32[32,8,256]{2,1,0:T(8,128)S(1)} collective-permute-done((f32[32,8,256]{2,1,0:T(8,128)S(1)}, f32[32,8,256]{2,1,0:T(8,128)S(1)}, u32[]{:S(2)}, u32[]{:S(2)}) %collective-permute-start.45) | collective-permute-done | bytes 262176 | tf_op jit(solution)/shard_map/ppermute | solution.py:583
  192.6 7.8 %finish.1 = f32[3,32,64,256]{3,2,1,0:T(8,128)} custom-call(s32[2]{0:T(128)S(1)} %pad_add_fusion.pos_ref, f32[7,64,256]{2,1,0:T(8,128)S(1)} %get-tuple-element.102.diag_ref.coef_ref, bf16[128,192]{1,0:T(8,128)(2,1)S(1)} %get-tuple-element.103.dpack_ref, f32[3,32,64,256]{3,2,1,0:T(8,128)} %add_force.1.part_ref, ...), custom_call_target="tpu_custom_call", output_to_operand_aliasing={{}: (3, {})} | custom-call | flops 402653184 | bytes 26214400 | tf_op jit(solution)/shard_map/finish/pallas_call | solution.py:545
  (85 shorter events, 22.0 us)
Async XLA Ops:
  4.8 4.9 %collective-permute-start = (f32[32,8,256]{2,1,0:T(8,128)S(1)}, f32[32,8,256]{2,1,0:T(8,128)S(1)}, u32[]{:S(2)}, u32[]{:S(2)}) collective-permute-start(f32[32,8,256]{2,1,0:T(8,128)S(1)} %get-tuple-element.124), channel_id=1, source_target_pairs={{0,1},{1,0},{2,3},{3,2},{4,5},{5,4},{6,7},{7,6},{8,9},{9,8},{10,11... | collective-permute-start | bytes 786440 | tf_op jit(solution)/shard_map/ppermute | solution.py:583
  5.4 9.7 %collective-permute-start.1 = (f32[32,8,256]{2,1,0:T(8,128)S(1)}, f32[32,8,256]{2,1,0:T(8,128)S(1)}, u32[]{:S(2)}, u32[]{:S(2)}) collective-permute-start(f32[32,8,256]{2,1,0:T(8,128)S(1)} %get-tuple-element.125), channel_id=1, source_target_pairs={{0,2},{1,3},{2,0},{3,1},{4,6},{5,7},{6,4},{7,5},{8,10},{9,11},{10,... | collective-permute-start | bytes 786440 | tf_op jit(solution)/shard_map/ppermute | solution.py:583
  7.9 12.3 %collective-permute-start.2 = (f32[32,8,256]{2,1,0:T(8,128)S(1)}, f32[32,8,256]{2,1,0:T(8,128)S(1)}, u32[]{:S(2)}, u32[]{:S(2)}) collective-permute-start(f32[32,8,256]{2,1,0:T(8,128)S(1)} %get-tuple-element.126), channel_id=1, source_target_pairs={{0,3},{1,2},{2,1},{3,0},{4,7},{5,6},{6,5},{7,4},{8,11},{9,10},{10,... | collective-permute-start | bytes 786440 | tf_op jit(solution)/shard_map/ppermute | solution.py:583
  8.0 12.8 %collective-permute-start.3 = (f32[32,8,256]{2,1,0:T(8,128)S(1)}, f32[32,8,256]{2,1,0:T(8,128)S(1)}, u32[]{:S(2)}, u32[]{:S(2)}) collective-permute-start(f32[32,8,256]{2,1,0:T(8,128)S(1)} %get-tuple-element.127), channel_id=1, source_target_pairs={{0,4},{1,5},{2,6},{3,7},{4,0},{5,1},{6,2},{7,3},{8,12},{9,13},{10,... | collective-permute-start | bytes 786440 | tf_op jit(solution)/shard_map/ppermute | solution.py:583
  9.8 22.9 %collective-permute-start.4 = (f32[32,8,256]{2,1,0:T(8,128)S(1)}, f32[32,8,256]{2,1,0:T(8,128)S(1)}, u32[]{:S(2)}, u32[]{:S(2)}) collective-permute-start(f32[32,8,256]{2,1,0:T(8,128)S(1)} %get-tuple-element.128), channel_id=1, source_target_pairs={{0,5},{1,4},{2,7},{3,6},{4,1},{5,0},{6,3},{7,2},{8,13},{9,12},{10,... | collective-permute-start | bytes 786440 | tf_op jit(solution)/shard_map/ppermute | solution.py:583
  9.8 25.1 %collective-permute-start.5 = (f32[32,8,256]{2,1,0:T(8,128)S(1)}, f32[32,8,256]{2,1,0:T(8,128)S(1)}, u32[]{:S(2)}, u32[]{:S(2)}) collective-permute-start(f32[32,8,256]{2,1,0:T(8,128)S(1)} %get-tuple-element.129), channel_id=1, source_target_pairs={{0,6},{1,7},{2,4},{3,5},{4,2},{5,3},{6,0},{7,1},{8,14},{9,15},{10,... | collective-permute-start | bytes 786440 | tf_op jit(solution)/shard_map/ppermute | solution.py:583
  15.1 21.3 %collective-permute-start.6 = (f32[32,8,256]{2,1,0:T(8,128)S(1)}, f32[32,8,256]{2,1,0:T(8,128)S(1)}, u32[]{:S(2)}, u32[]{:S(2)}) collective-permute-start(f32[32,8,256]{2,1,0:T(8,128)S(1)} %get-tuple-element.130), channel_id=1, source_target_pairs={{0,7},{1,6},{2,5},{3,4},{4,3},{5,2},{6,1},{7,0},{8,15},{9,14},{10,... | collective-permute-start | bytes 786440 | tf_op jit(solution)/shard_map/ppermute | solution.py:583
  20.2 19.6 %collective-permute-start.14 = (f32[32,8,256]{2,1,0:T(8,128)S(1)}, f32[32,8,256]{2,1,0:T(8,128)S(1)}, u32[]{:S(2)}, u32[]{:S(2)}) collective-permute-start(f32[32,8,256]{2,1,0:T(8,128)S(1)} %get-tuple-element.140), channel_id=1, source_target_pairs={{0,1},{1,0},{2,3},{3,2},{4,5},{5,4},{6,7},{7,6},{8,9},{9,8},{10,11... | collective-permute-start | bytes 786440 | tf_op jit(solution)/shard_map/ppermute | solution.py:583
  20.8 20.3 %collective-permute-start.15 = (f32[32,8,256]{2,1,0:T(8,128)S(1)}, f32[32,8,256]{2,1,0:T(8,128)S(1)}, u32[]{:S(2)}, u32[]{:S(2)}) collective-permute-start(f32[32,8,256]{2,1,0:T(8,128)S(1)} %get-tuple-element.141), channel_id=1, source_target_pairs={{0,2},{1,3},{2,0},{3,1},{4,6},{5,7},{6,4},{7,5},{8,10},{9,11},{10,... | collective-permute-start | bytes 786440 | tf_op jit(solution)/shard_map/ppermute | solution.py:583
  32.7 10.1 %collective-permute-start.16 = (f32[32,8,256]{2,1,0:T(8,128)S(1)}, f32[32,8,256]{2,1,0:T(8,128)S(1)}, u32[]{:S(2)}, u32[]{:S(2)}) collective-permute-start(f32[32,8,256]{2,1,0:T(8,128)S(1)} %get-tuple-element.142), channel_id=1, source_target_pairs={{0,3},{1,2},{2,1},{3,0},{4,7},{5,6},{6,5},{7,4},{8,11},{9,10},{10,... | collective-permute-start | bytes 786440 | tf_op jit(solution)/shard_map/ppermute | solution.py:583
  34.9 9.2 %collective-permute-start.17 = (f32[32,8,256]{2,1,0:T(8,128)S(1)}, f32[32,8,256]{2,1,0:T(8,128)S(1)}, u32[]{:S(2)}, u32[]{:S(2)}) collective-permute-start(f32[32,8,256]{2,1,0:T(8,128)S(1)} %get-tuple-element.143), channel_id=1, source_target_pairs={{0,4},{1,5},{2,6},{3,7},{4,0},{5,1},{6,2},{7,3},{8,12},{9,13},{10,... | collective-permute-start | bytes 786440 | tf_op jit(solution)/shard_map/ppermute | solution.py:583
  36.4 22.4 %collective-permute-start.18 = (f32[32,8,256]{2,1,0:T(8,128)S(1)}, f32[32,8,256]{2,1,0:T(8,128)S(1)}, u32[]{:S(2)}, u32[]{:S(2)}) collective-permute-start(f32[32,8,256]{2,1,0:T(8,128)S(1)} %get-tuple-element.144), channel_id=1, source_target_pairs={{0,5},{1,4},{2,7},{3,6},{4,1},{5,0},{6,3},{7,2},{8,13},{9,12},{10,... | collective-permute-start | bytes 786440 | tf_op jit(solution)/shard_map/ppermute | solution.py:583
  39.8 20.2 %collective-permute-start.19 = (f32[32,8,256]{2,1,0:T(8,128)S(1)}, f32[32,8,256]{2,1,0:T(8,128)S(1)}, u32[]{:S(2)}, u32[]{:S(2)}) collective-permute-start(f32[32,8,256]{2,1,0:T(8,128)S(1)} %get-tuple-element.145), channel_id=1, source_target_pairs={{0,6},{1,7},{2,4},{3,5},{4,2},{5,3},{6,0},{7,1},{8,14},{9,15},{10,... | collective-permute-start | bytes 786440 | tf_op jit(solution)/shard_map/ppermute | solution.py:583
  41.1 20.5 %collective-permute-start.20 = (f32[32,8,256]{2,1,0:T(8,128)S(1)}, f32[32,8,256]{2,1,0:T(8,128)S(1)}, u32[]{:S(2)}, u32[]{:S(2)}) collective-permute-start(f32[32,8,256]{2,1,0:T(8,128)S(1)} %get-tuple-element.146), channel_id=1, source_target_pairs={{0,7},{1,6},{2,5},{3,4},{4,3},{5,2},{6,1},{7,0},{8,15},{9,14},{10,... | collective-permute-start | bytes 786440 | tf_op jit(solution)/shard_map/ppermute | solution.py:583
  42.8 18.8 %collective-permute-start.7 = (f32[32,8,256]{2,1,0:T(8,128)S(1)}, f32[32,8,256]{2,1,0:T(8,128)S(1)}, u32[]{:S(2)}, u32[]{:S(2)}) collective-permute-start(f32[32,8,256]{2,1,0:T(8,128)S(1)} %get-tuple-element.132), channel_id=1, source_target_pairs={{0,1},{1,0},{2,3},{3,2},{4,5},{5,4},{6,7},{7,6},{8,9},{9,8},{10,11... | collective-permute-start | bytes 786440 | tf_op jit(solution)/shard_map/ppermute | solution.py:583
  44.1 23.9 %collective-permute-start.8 = (f32[32,8,256]{2,1,0:T(8,128)S(1)}, f32[32,8,256]{2,1,0:T(8,128)S(1)}, u32[]{:S(2)}, u32[]{:S(2)}) collective-permute-start(f32[32,8,256]{2,1,0:T(8,128)S(1)} %get-tuple-element.133), channel_id=1, source_target_pairs={{0,2},{1,3},{2,0},{3,1},{4,6},{5,7},{6,4},{7,5},{8,10},{9,11},{10,... | collective-permute-start | bytes 786440 | tf_op jit(solution)/shard_map/ppermute | solution.py:583
  58.8 10.7 %collective-permute-start.9 = (f32[32,8,256]{2,1,0:T(8,128)S(1)}, f32[32,8,256]{2,1,0:T(8,128)S(1)}, u32[]{:S(2)}, u32[]{:S(2)}) collective-permute-start(f32[32,8,256]{2,1,0:T(8,128)S(1)} %get-tuple-element.134), channel_id=1, source_target_pairs={{0,3},{1,2},{2,1},{3,0},{4,7},{5,6},{6,5},{7,4},{8,11},{9,10},{10,... | collective-permute-start | bytes 786440 | tf_op jit(solution)/shard_map/ppermute | solution.py:583
  60.0 20.0 %collective-permute-start.10 = (f32[32,8,256]{2,1,0:T(8,128)S(1)}, f32[32,8,256]{2,1,0:T(8,128)S(1)}, u32[]{:S(2)}, u32[]{:S(2)}) collective-permute-start(f32[32,8,256]{2,1,0:T(8,128)S(1)} %get-tuple-element.135), channel_id=1, source_target_pairs={{0,4},{1,5},{2,6},{3,7},{4,0},{5,1},{6,2},{7,3},{8,12},{9,13},{10,... | collective-permute-start | bytes 786440 | tf_op jit(solution)/shard_map/ppermute | solution.py:583
  61.6 22.4 %collective-permute-start.11 = (f32[32,8,256]{2,1,0:T(8,128)S(1)}, f32[32,8,256]{2,1,0:T(8,128)S(1)}, u32[]{:S(2)}, u32[]{:S(2)}) collective-permute-start(f32[32,8,256]{2,1,0:T(8,128)S(1)} %get-tuple-element.136), channel_id=1, source_target_pairs={{0,5},{1,4},{2,7},{3,6},{4,1},{5,0},{6,3},{7,2},{8,13},{9,12},{10,... | collective-permute-start | bytes 786440 | tf_op jit(solution)/shard_map/ppermute | solution.py:583
  61.6 24.1 %collective-permute-start.12 = (f32[32,8,256]{2,1,0:T(8,128)S(1)}, f32[32,8,256]{2,1,0:T(8,128)S(1)}, u32[]{:S(2)}, u32[]{:S(2)}) collective-permute-start(f32[32,8,256]{2,1,0:T(8,128)S(1)} %get-tuple-element.137), channel_id=1, source_target_pairs={{0,6},{1,7},{2,4},{3,5},{4,2},{5,3},{6,0},{7,1},{8,14},{9,15},{10,... | collective-permute-start | bytes 786440 | tf_op jit(solution)/shard_map/ppermute | solution.py:583
  68.0 19.0 %collective-permute-start.13 = (f32[32,8,256]{2,1,0:T(8,128)S(1)}, f32[32,8,256]{2,1,0:T(8,128)S(1)}, u32[]{:S(2)}, u32[]{:S(2)}) collective-permute-start(f32[32,8,256]{2,1,0:T(8,128)S(1)} %get-tuple-element.138), channel_id=1, source_target_pairs={{0,7},{1,6},{2,5},{3,4},{4,3},{5,2},{6,1},{7,0},{8,15},{9,14},{10,... | collective-permute-start | bytes 786440 | tf_op jit(solution)/shard_map/ppermute | solution.py:583
  69.5 17.6 %collective-permute-start.21 = (f32[32,8,256]{2,1,0:T(8,128)S(1)}, f32[32,8,256]{2,1,0:T(8,128)S(1)}, u32[]{:S(2)}, u32[]{:S(2)}) collective-permute-start(f32[32,8,256]{2,1,0:T(8,128)S(1)} %get-tuple-element.164), channel_id=1, source_target_pairs={{0,1},{1,0},{2,3},{3,2},{4,5},{5,4},{6,7},{7,6},{8,9},{9,8},{10,11... | collective-permute-start | bytes 786440 | tf_op jit(solution)/shard_map/ppermute | solution.py:583
  80.1 8.2 %collective-permute-start.22 = (f32[32,8,256]{2,1,0:T(8,128)S(1)}, f32[32,8,256]{2,1,0:T(8,128)S(1)}, u32[]{:S(2)}, u32[]{:S(2)}) collective-permute-start(f32[32,8,256]{2,1,0:T(8,128)S(1)} %get-tuple-element.165), channel_id=1, source_target_pairs={{0,2},{1,3},{2,0},{3,1},{4,6},{5,7},{6,4},{7,5},{8,10},{9,11},{10,... | collective-permute-start | bytes 786440 | tf_op jit(solution)/shard_map/ppermute | solution.py:583
  84.0 8.5 %collective-permute-start.23 = (f32[32,8,256]{2,1,0:T(8,128)S(1)}, f32[32,8,256]{2,1,0:T(8,128)S(1)}, u32[]{:S(2)}, u32[]{:S(2)}) collective-permute-start(f32[32,8,256]{2,1,0:T(8,128)S(1)} %get-tuple-element.166), channel_id=1, source_target_pairs={{0,3},{1,2},{2,1},{3,0},{4,7},{5,6},{6,5},{7,4},{8,11},{9,10},{10,... | collective-permute-start | bytes 786440 | tf_op jit(solution)/shard_map/ppermute | solution.py:583
  85.7 20.5 %collective-permute-start.24 = (f32[32,8,256]{2,1,0:T(8,128)S(1)}, f32[32,8,256]{2,1,0:T(8,128)S(1)}, u32[]{:S(2)}, u32[]{:S(2)}) collective-permute-start(f32[32,8,256]{2,1,0:T(8,128)S(1)} %get-tuple-element.167), channel_id=1, source_target_pairs={{0,4},{1,5},{2,6},{3,7},{4,0},{5,1},{6,2},{7,3},{8,12},{9,13},{10,... | collective-permute-start | bytes 786440 | tf_op jit(solution)/shard_map/ppermute | solution.py:583
  87.0 22.1 %collective-permute-start.25 = (f32[32,8,256]{2,1,0:T(8,128)S(1)}, f32[32,8,256]{2,1,0:T(8,128)S(1)}, u32[]{:S(2)}, u32[]{:S(2)}) collective-permute-start(f32[32,8,256]{2,1,0:T(8,128)S(1)} %get-tuple-element.168), channel_id=1, source_target_pairs={{0,5},{1,4},{2,7},{3,6},{4,1},{5,0},{6,3},{7,2},{8,13},{9,12},{10,... | collective-permute-start | bytes 786440 | tf_op jit(solution)/shard_map/ppermute | solution.py:583
  87.0 23.9 %collective-permute-start.26 = (f32[32,8,256]{2,1,0:T(8,128)S(1)}, f32[32,8,256]{2,1,0:T(8,128)S(1)}, u32[]{:S(2)}, u32[]{:S(2)}) collective-permute-start(f32[32,8,256]{2,1,0:T(8,128)S(1)} %get-tuple-element.169), channel_id=1, source_target_pairs={{0,6},{1,7},{2,4},{3,5},{4,2},{5,3},{6,0},{7,1},{8,14},{9,15},{10,... | collective-permute-start | bytes 786440 | tf_op jit(solution)/shard_map/ppermute | solution.py:583
  88.2 24.0 %collective-permute-start.27 = (f32[32,8,256]{2,1,0:T(8,128)S(1)}, f32[32,8,256]{2,1,0:T(8,128)S(1)}, u32[]{:S(2)}, u32[]{:S(2)}) collective-permute-start(f32[32,8,256]{2,1,0:T(8,128)S(1)} %get-tuple-element.170), channel_id=1, source_target_pairs={{0,7},{1,6},{2,5},{3,4},{4,3},{5,2},{6,1},{7,0},{8,15},{9,14},{10,... | collective-permute-start | bytes 786440 | tf_op jit(solution)/shard_map/ppermute | solution.py:583
  92.5 19.8 %collective-permute-start.34 = (f32[32,8,256]{2,1,0:T(8,128)S(1)}, f32[32,8,256]{2,1,0:T(8,128)S(1)}, u32[]{:S(2)}, u32[]{:S(2)}) collective-permute-start(f32[32,8,256]{2,1,0:T(8,128)S(1)} %get-tuple-element.184), channel_id=1, source_target_pairs={{0,1},{1,0},{2,3},{3,2},{4,5},{5,4},{6,7},{7,6},{8,9},{9,8},{10,11... | collective-permute-start | bytes 786440 | tf_op jit(solution)/shard_map/ppermute | solution.py:583
  106.2 7.2 %collective-permute-start.35 = (f32[32,8,256]{2,1,0:T(8,128)S(1)}, f32[32,8,256]{2,1,0:T(8,128)S(1)}, u32[]{:S(2)}, u32[]{:S(2)}) collective-permute-start(f32[32,8,256]{2,1,0:T(8,128)S(1)} %get-tuple-element.185), channel_id=1, source_target_pairs={{0,2},{1,3},{2,0},{3,1},{4,6},{5,7},{6,4},{7,5},{8,10},{9,11},{10,... | collective-permute-start | bytes 786440 | tf_op jit(solution)/shard_map/ppermute | solution.py:583
  109.2 13.0 %collective-permute-start.36 = (f32[32,8,256]{2,1,0:T(8,128)S(1)}, f32[32,8,256]{2,1,0:T(8,128)S(1)}, u32[]{:S(2)}, u32[]{:S(2)}) collective-permute-start(f32[32,8,256]{2,1,0:T(8,128)S(1)} %get-tuple-element.186), channel_id=1, source_target_pairs={{0,3},{1,2},{2,1},{3,0},{4,7},{5,6},{6,5},{7,4},{8,11},{9,10},{10,... | collective-permute-start | bytes 786440 | tf_op jit(solution)/shard_map/ppermute | solution.py:583
  110.9 20.5 %collective-permute-start.37 = (f32[32,8,256]{2,1,0:T(8,128)S(1)}, f32[32,8,256]{2,1,0:T(8,128)S(1)}, u32[]{:S(2)}, u32[]{:S(2)}) collective-permute-start(f32[32,8,256]{2,1,0:T(8,128)S(1)} %get-tuple-element.187), channel_id=1, source_target_pairs={{0,4},{1,5},{2,6},{3,7},{4,0},{5,1},{6,2},{7,3},{8,12},{9,13},{10,... | collective-permute-start | bytes 786440 | tf_op jit(solution)/shard_map/ppermute | solution.py:583
  112.2 22.1 %collective-permute-start.38 = (f32[32,8,256]{2,1,0:T(8,128)S(1)}, f32[32,8,256]{2,1,0:T(8,128)S(1)}, u32[]{:S(2)}, u32[]{:S(2)}) collective-permute-start(f32[32,8,256]{2,1,0:T(8,128)S(1)} %get-tuple-element.188), channel_id=1, source_target_pairs={{0,5},{1,4},{2,7},{3,6},{4,1},{5,0},{6,3},{7,2},{8,13},{9,12},{10,... | collective-permute-start | bytes 786440 | tf_op jit(solution)/shard_map/ppermute | solution.py:583
  112.2 22.1 %collective-permute-start.39 = (f32[32,8,256]{2,1,0:T(8,128)S(1)}, f32[32,8,256]{2,1,0:T(8,128)S(1)}, u32[]{:S(2)}, u32[]{:S(2)}) collective-permute-start(f32[32,8,256]{2,1,0:T(8,128)S(1)} %get-tuple-element.189), channel_id=1, source_target_pairs={{0,6},{1,7},{2,4},{3,5},{4,2},{5,3},{6,0},{7,1},{8,14},{9,15},{10,... | collective-permute-start | bytes 786440 | tf_op jit(solution)/shard_map/ppermute | solution.py:583
  113.4 20.9 %collective-permute-start.40 = (f32[32,8,256]{2,1,0:T(8,128)S(1)}, f32[32,8,256]{2,1,0:T(8,128)S(1)}, u32[]{:S(2)}, u32[]{:S(2)}) collective-permute-start(f32[32,8,256]{2,1,0:T(8,128)S(1)} %get-tuple-element.190), channel_id=1, source_target_pairs={{0,7},{1,6},{2,5},{3,4},{4,3},{5,2},{6,1},{7,0},{8,15},{9,14},{10,... | collective-permute-start | bytes 786440 | tf_op jit(solution)/shard_map/ppermute | solution.py:583
  122.1 16.6 %collective-permute-start.28 = (f32[3,32,512]{2,1,0:T(8,128)S(1)}, f32[3,32,512]{2,1,0:T(8,128)S(1)}, u32[]{:S(2)}, u32[]{:S(2)}) collective-permute-start(f32[3,32,512]{2,1,0:T(8,128)S(1)} %get-tuple-element.175.own_lo_ref), channel_id=1, source_target_pairs={{8,0},{16,8},{24,16},{0,24},{9,1},{17,9},{25,17},{1,25},{10,2},{18... | collective-permute-start | bytes 589832 | tf_op jit(solution)/shard_map/ppermute | solution.py:567
  131.4 7.5 %collective-permute-start.29 = (f32[3,32,512]{2,1,0:T(8,128)S(1)}, f32[3,32,512]{2,1,0:T(8,128)S(1)}, u32[]{:S(2)}, u32[]{:S(2)}) collective-permute-start(f32[3,32,512]{2,1,0:T(8,128)S(1)} %get-tuple-element.174.own_up_ref), channel_id=1, source_target_pairs={{0,8},{8,16},{16,24},{24,0},{1,9},{9,17},{17,25},{25,1},{2,10},{10... | collective-permute-start | bytes 589832 | tf_op jit(solution)/shard_map/ppermute | solution.py:567
  136.8 29.8 %collective-permute-start.41 = (f32[32,8,256]{2,1,0:T(8,128)S(1)}, f32[32,8,256]{2,1,0:T(8,128)S(1)}, u32[]{:S(2)}, u32[]{:S(2)}) collective-permute-start(f32[32,8,256]{2,1,0:T(8,128)S(1)} %get-tuple-element.192), channel_id=1, source_target_pairs={{0,1},{1,0},{2,3},{3,2},{4,5},{5,4},{6,7},{7,6},{8,9},{9,8},{10,11... | collective-permute-start | bytes 786440 | tf_op jit(solution)/shard_map/ppermute | solution.py:583
  137.5 30.3 %collective-permute-start.42 = (f32[32,8,256]{2,1,0:T(8,128)S(1)}, f32[32,8,256]{2,1,0:T(8,128)S(1)}, u32[]{:S(2)}, u32[]{:S(2)}) collective-permute-start(f32[32,8,256]{2,1,0:T(8,128)S(1)} %get-tuple-element.193), channel_id=1, source_target_pairs={{0,2},{1,3},{2,0},{3,1},{4,6},{5,7},{6,4},{7,5},{8,10},{9,11},{10,... | collective-permute-start | bytes 786440 | tf_op jit(solution)/shard_map/ppermute | solution.py:583
  146.9 7.7 %collective-permute-start.30 = (f32[2,32,512]{2,1,0:T(8,128)S(1)}, f32[2,32,512]{2,1,0:T(8,128)S(1)}, u32[]{:S(2)}, u32[]{:S(2)}) collective-permute-start(f32[2,32,512]{2,1,0:T(8,128)S(1)} %get-tuple-element.179.own_lo_ref), channel_id=1, source_target_pairs={{8,0},{16,8},{24,16},{0,24},{9,1},{17,9},{25,17},{1,25},{10,2},{18... | collective-permute-start | bytes 393224 | tf_op jit(solution)/shard_map/ppermute | solution.py:567
  150.7 6.8 %collective-permute-start.31 = (f32[2,32,512]{2,1,0:T(8,128)S(1)}, f32[2,32,512]{2,1,0:T(8,128)S(1)}, u32[]{:S(2)}, u32[]{:S(2)}) collective-permute-start(f32[2,32,512]{2,1,0:T(8,128)S(1)} %get-tuple-element.178.own_up_ref), channel_id=1, source_target_pairs={{0,8},{8,16},{16,24},{24,0},{1,9},{9,17},{17,25},{25,1},{2,10},{10... | collective-permute-start | bytes 393224 | tf_op jit(solution)/shard_map/ppermute | solution.py:567
  164.5 4.9 %collective-permute-start.32 = (f32[1,32,512]{2,1,0:T(8,128)S(1)}, f32[1,32,512]{2,1,0:T(8,128)S(1)}, u32[]{:S(2)}, u32[]{:S(2)}) collective-permute-start(f32[1,32,512]{2,1,0:T(8,128)S(1)} %get-tuple-element.181), channel_id=1, source_target_pairs={{8,0},{16,8},{24,16},{0,24},{9,1},{17,9},{25,17},{1,25},{10,2},{18... | collective-permute-start | bytes 196616 | tf_op jit(solution)/shard_map/ppermute | solution.py:567
  166.0 6.1 %collective-permute-start.33 = (f32[1,32,512]{2,1,0:T(8,128)S(1)}, f32[1,32,512]{2,1,0:T(8,128)S(1)}, u32[]{:S(2)}, u32[]{:S(2)}) collective-permute-start(f32[1,32,512]{2,1,0:T(8,128)S(1)} %get-tuple-element.182), channel_id=1, source_target_pairs={{0,8},{8,16},{16,24},{24,0},{1,9},{9,17},{17,25},{25,1},{2,10},{10... | collective-permute-start | bytes 196616 | tf_op jit(solution)/shard_map/ppermute | solution.py:567
  166.6 18.4 %collective-permute-start.43 = (f32[32,8,256]{2,1,0:T(8,128)S(1)}, f32[32,8,256]{2,1,0:T(8,128)S(1)}, u32[]{:S(2)}, u32[]{:S(2)}) collective-permute-start(f32[32,8,256]{2,1,0:T(8,128)S(1)} %get-tuple-element.194), channel_id=1, source_target_pairs={{0,3},{1,2},{2,1},{3,0},{4,7},{5,6},{6,5},{7,4},{8,11},{9,10},{10,... | collective-permute-start | bytes 786440 | tf_op jit(solution)/shard_map/ppermute | solution.py:583
  166.6 18.8 %collective-permute-start.44 = (f32[32,8,256]{2,1,0:T(8,128)S(1)}, f32[32,8,256]{2,1,0:T(8,128)S(1)}, u32[]{:S(2)}, u32[]{:S(2)}) collective-permute-start(f32[32,8,256]{2,1,0:T(8,128)S(1)} %get-tuple-element.195), channel_id=1, source_target_pairs={{0,4},{1,5},{2,6},{3,7},{4,0},{5,1},{6,2},{7,3},{8,12},{9,13},{10,... | collective-permute-start | bytes 786440 | tf_op jit(solution)/shard_map/ppermute | solution.py:583
  167.9 24.7 %collective-permute-start.45 = (f32[32,8,256]{2,1,0:T(8,128)S(1)}, f32[32,8,256]{2,1,0:T(8,128)S(1)}, u32[]{:S(2)}, u32[]{:S(2)}) collective-permute-start(f32[32,8,256]{2,1,0:T(8,128)S(1)} %get-tuple-element.196), channel_id=1, source_target_pairs={{0,5},{1,4},{2,7},{3,6},{4,1},{5,0},{6,3},{7,2},{8,13},{9,12},{10,... | collective-permute-start | bytes 786440 | tf_op jit(solution)/shard_map/ppermute | solution.py:583
  169.4 23.2 %collective-permute-start.46 = (f32[32,8,256]{2,1,0:T(8,128)S(1)}, f32[32,8,256]{2,1,0:T(8,128)S(1)}, u32[]{:S(2)}, u32[]{:S(2)}) collective-permute-start(f32[32,8,256]{2,1,0:T(8,128)S(1)} %get-tuple-element.197), channel_id=1, source_target_pairs={{0,6},{1,7},{2,4},{3,5},{4,2},{5,3},{6,0},{7,1},{8,14},{9,15},{10,... | collective-permute-start | bytes 786440 | tf_op jit(solution)/shard_map/ppermute | solution.py:583
  172.1 20.5 %collective-permute-start.47 = (f32[32,8,256]{2,1,0:T(8,128)S(1)}, f32[32,8,256]{2,1,0:T(8,128)S(1)}, u32[]{:S(2)}, u32[]{:S(2)}) collective-permute-start(f32[32,8,256]{2,1,0:T(8,128)S(1)} %get-tuple-element.198), channel_id=1, source_target_pairs={{0,7},{1,6},{2,5},{3,4},{4,3},{5,2},{6,1},{7,0},{8,15},{9,14},{10,... | collective-permute-start | bytes 786440 | tf_op jit(solution)/shard_map/ppermute | solution.py:583
  (11 other events, 439.3 us)

commit v4 on v3

--- a/solution.py
+++ b/solution.py
@@ -16,6 +16,7 @@
 TIME_STEP = 0.2
 INTERACTION = 2.0
 LINE = 8
+IN_FLIGHT = 5
 
 F32 = jnp.float32
 BF16 = jnp.bfloat16
@@ -95,7 +96,9 @@
     planes = table_ref.shape[1]
     both = table_ref[...]
     high_table = both[:planes]
-    per, nodes, width = refs[0].shape
+    width = refs[0].shape[-1]
+    nodes = refs[0].shape[-2]
+    per = planes // count
     flat = [ref.reshape(per * nodes, width) for ref in refs]
     for n in range(nodes):
         rows = pl.ds(n, per, stride=nodes) if nodes > 1 else pl.ds(0, per)
@@ -107,9 +110,10 @@
 
 
 def transform(blocks, table):
-    per, nodes, elements = blocks[0].shape
+    *lead, nodes, elements = blocks[0].shape
+    zeros = (0,) * (len(lead) + 1)
     width = 128
-    block = pl.BlockSpec((per, nodes, width), lambda i: (0, 0, i))
+    block = pl.BlockSpec((*lead, nodes, width), lambda i: (*zeros, i))
     size = len(blocks) * blocks[0].size
     return pl.pallas_call(
         functools.partial(transform_kernel, len(blocks)),
@@ -118,7 +122,7 @@
         in_specs=[pl.BlockSpec(table.shape, lambda i: (0, 0))] + [block] * len(blocks),
         out_specs=[block] * len(blocks),
         compiler_params=params(),
-        cost_estimate=cost(6 * PLANES * size, 20 * size),
+        cost_estimate=cost(6 * PLANES * size, 8 * size),
         name="transform",
     )(table, *blocks)
 
@@ -151,6 +155,31 @@
         cost_estimate=cost(0, 16 * size),
         name="pack",
     )(position, *[adjoint] * peers)
+
+
+def pack_joined_kernel(x_ref, o_ref):
+    part = o_ref.shape[2]
+    for d in range(o_ref.shape[0]):
+        o_ref[d] = x_ref[0, :, d * part : (d + 1) * part, :]
+
+
+def pack_joined(adjoint, comp, peers):
+    _, per, nodes, elements = adjoint.shape
+    part = nodes // peers
+    if part % 8:
+        return jnp.moveaxis(adjoint[comp].reshape(per, peers, part, elements), 1, 0)
+    block = per // 4
+    size = per * nodes * elements
+    return pl.pallas_call(
+        pack_joined_kernel,
+        out_shape=jax.ShapeDtypeStruct((peers, per, part, elements), F32),
+        grid=(per // block,),
+        in_specs=[pl.BlockSpec((1, block, nodes, elements), lambda q: (comp, q, 0, 0))],
+        out_specs=pl.BlockSpec((peers, block, part, elements), lambda q: (0, q, 0, 0)),
+        compiler_params=params(),
+        cost_estimate=cost(0, 8 * size),
+        name="pack_joined",
+    )(adjoint)
 
 
 BXR, BYS, DXBX, DXBY, DYBX, DYBY, DIAG = range(7)
@@ -450,7 +479,7 @@
         in_specs=[SMEM_SPEC, whole(coef.shape), whole(dpack.shape), *field, *field],
         out_specs=pl.BlockSpec((3, block, nodes, elements), lambda i: (0, i, 0, 0)),
         compiler_params=params(),
-        cost_estimate=cost(24 * nodes * size, 45 * size),
+        cost_estimate=cost(24 * nodes * size, 20 * size),
         name="partial_update",
     )(position, coef, dpack, *z, *x)
 
@@ -522,14 +551,14 @@
     @pl.when(which == 0)
     def _():
         for c in range(block):
-            y = slab(y_refs, c)
+            y = slab([ref.at[0] for ref in y_refs], c)
             store_own(o_ref, me, own_order(part_ref, me, 0, c) + TIME_STEP * (y * coef_ref[DXBY]), 0, c)
 
     @pl.when(which == 1)
     def _():
         dpack = dpack_ref[...]
         for c in range(block):
-            y = slab(y_refs, c)
+            y = slab([ref.at[0] for ref in y_refs], c)
             slopes = dot(dpack, pack_field(y))
             moved = coef_ref[BXR] * slopes[:nodes] + coef_ref[BYS] * slopes[nodes:]
             change = y + TIME_STEP * (y * coef_ref[DYBY] - moved)
@@ -537,23 +566,29 @@
 
 
 def finish(position, y, coef, dpack, partial):
-    coefs, part, elements = y[0].shape
-    nodes = len(y) * part
+    lines, coefs, part, elements = y.shape
+    nodes = lines * part
     block = coef_block(coefs)
-    comp = pl.BlockSpec((1, block, nodes, elements), lambda i, j: (j, i, 0, 0))
+
+    def source(d):
+        return pl.BlockSpec((1, block, part, elements), lambda i, j, pos: (pos[1] ^ d, i, 0, 0))
+
+    comp = pl.BlockSpec((1, block, nodes, elements), lambda i, j, pos: (j, i, 0, 0))
     size = coefs * nodes * elements
     return pl.pallas_call(
-        functools.partial(finish_kernel, block, len(y)),
+        functools.partial(finish_kernel, block, lines),
         out_shape=jax.ShapeDtypeStruct(partial.shape, F32),
-        grid=(coefs // block, 2),
-        in_specs=[SMEM_SPEC, whole(coef.shape), whole(dpack.shape), comp]
-        + [pl.BlockSpec((block, part, elements), lambda i, j: (i, 0, 0))] * len(y),
-        out_specs=comp,
+        grid_spec=pltpu.PrefetchScalarGridSpec(
+            num_scalar_prefetch=1,
+            grid=(coefs // block, 2),
+            in_specs=[whole(coef.shape), whole(dpack.shape), comp] + [source(d) for d in range(lines)],
+            out_specs=comp,
+        ),
         input_output_aliases={3: 0},
         compiler_params=params(),
-        cost_estimate=cost(12 * nodes * size, 50 * size),
+        cost_estimate=cost(12 * nodes * size, 20 * size),
         name="finish",
-    )(position, coef, dpack, partial, *y)
+    )(position, coef, dpack, partial, *[y] * lines)
 
 
 def to_all(blocks):
@@ -576,45 +611,66 @@
     direct = peers == lines
     place = lax.axis_index("four").astype(jnp.int32)
     position = jnp.stack([place, place if direct else jnp.zeros_like(place)])
-    table = permuted_table(position, jnp.asarray(coef_table(PLANES)), lines)
+    natural = jnp.asarray(coef_table(PLANES))
+    table = permuted_table(position, natural, lines)
+    flight = []
 
     def exchange(blocks):
-        return [blocks[0]] + [
-            lax.ppermute(blocks[d], "four", [(i, i ^ d) for i in range(peers)]) for d in range(1, peers)
-        ]
+        first = len(flight)
+        order = sorted(range(1, peers), key=lambda d: (d < 2, d % 2, d))
+        for d in order:
+            block = blocks[d]
+            if len(flight) >= IN_FLIGHT:
+                block, flight[-IN_FLIGHT] = lax.optimization_barrier((block, flight[-IN_FLIGHT]))
+            flight.append(lax.ppermute(block, "four", [(i, i ^ d) for i in range(peers)]))
+
+        def received():
+            got = {d: flight[first + k] for k, d in enumerate(order)}
+            return [blocks[0]] + [got[d] for d in range(1, peers)]
+
+        return received
 
     def columns(comp):
         if direct:
             return pack(position, adjoint, comp, peers)
-        return [jnp.moveaxis(adjoint[comp].reshape(per, peers, nodes // peers, elements), 1, 0)]
+        return [pack_joined(adjoint, comp, peers)]
 
     def spread(blocks):
         if direct:
             return exchange(blocks)
-        return [to_all(blocks[0]).reshape(per * peers, nodes // peers, elements)]
+        got = [to_all(blocks[0])]
+        return lambda: got
 
     def collect(blocks):
         if direct:
             return exchange(blocks)
-        got = to_all(blocks[0].reshape(peers, per, nodes // peers, elements))
+        got = by_line(to_all(blocks[0]))
+        return lambda: [got[d] for d in range(lines)]
+
+    def by_line(got):
+        if peers == lines:
+            return got
         got = jnp.moveaxis(got, 0, 1).reshape(per, lines, LINE, elements)
-        return [got[:, d] for d in range(lines)]
+        return jnp.moveaxis(got, 1, 0)
 
     z_blocks = columns(2)
+    z_columns = spread(z_blocks)
     x_blocks = columns(0)
-    y_blocks = columns(1)
-    z_blocks, x_blocks = lax.optimization_barrier((z_blocks, x_blocks))
-    z_columns = spread(z_blocks)
     x_columns = spread(x_blocks)
-    coef, dpack, spack, gather, scatter, mask = prepare(
+    constants = prepare(
         position, base_bank, snapshot, geometry, diff_r, diff_s, stiffness, upper_list, lower_list
     )
-    z_coefs = transform(z_columns, table)
-    z = collect(z_coefs)
-    x_coefs = transform(x_columns, table)
-    x_coefs, y_blocks = lax.optimization_barrier((x_coefs, y_blocks))
-    x = collect(x_coefs)
-    y_columns = spread(y_blocks)
+    y_sent = pack_joined(adjoint, 1, peers)
+    z_got, constants, y_sent, table = lax.optimization_barrier((z_columns(), constants, y_sent, table))
+    coef, dpack, spack, gather, scatter, mask = constants
+    z_coefs = transform(z_got, table)
+    z_later = collect(z_coefs)
+    x_coefs = transform(x_columns(), table)
+    x_later = collect(x_coefs)
+    z = z_later()
+    x = x_later()
+    x[2], y_sent = lax.optimization_barrier((x[2], y_sent))
+    y_columns = to_all(y_sent)
     source, inverse, local, up, lo = start_solve(
         position, z, x, geometry, coef, dpack, spack, gather, mask
     )
@@ -624,8 +680,9 @@
     local, up, lo = two_sweeps(
         2, local, source, inverse, (up, lo), got, inv, spack, gather, scatter, mask
     )
+    y_columns, local = lax.optimization_barrier((y_columns, local))
     got = swap_faces(up, lo)
-    y = collect(transform(y_columns, table))
+    y = by_line(to_all(transform([y_columns], natural)[0]))
     local, up, lo = two_sweeps(
         1, local, source, inverse, (up, lo), got, inv, spack, gather, scatter, mask
     )

time: 201 us -> 236 us (1.17)
  local copies, waits for them, and re-layouts: 1.4 us -> 26.5 us
  waiting for transfers between devices: 83.5 us -> 102 us
  starting transfers between devices: 58.6 us -> 48.4 us
    unnamed x22 -> x156, local copies, waits for them, and re-layouts: 1.4 us -> 26.5 us
    ppermute x42 -> x28, starting transfers between devices: 47.5 us -> 33.1 us  [exchange(): lax.ppermute(block, 'four', [(i, i ^ d) for i in range(peers)])]
    ppermute x6, waiting for transfers between devices: 8.13 us -> 17.9 us  [swap_faces(): return (lax.ppermute(lo, 'dom', down_way), lax.ppermute(up, 'dom', up_way))]
    ppermute x42 -> x28, waiting for transfers between devices: 75.4 us -> 84.3 us  [exchange(): lax.ppermute(block, 'four', [(i, i ^ d) for i in range(peers)])]
    all_to_all x0 -> x2, starting transfers between devices: none -> 7.2 us  [to_all(): lax.all_to_all(blocks, 'four', split_axis=0, concat_axis=0, tiled=True)]
    pallas_call x1 -> x2, Pallas kernels: 7.79 us -> 10.8 us  [the longest x1 8.15 us: finish(): pl.pallas_call(functools.partial(finish_kernel, block, lines), out_shape=...]
    ppermute x6, starting transfers between devices: 11 us -> 8.07 us  [swap_faces(): return (lax.ppermute(lo, 'dom', down_way), lax.ppermute(up, 'dom', up_way))]
    pallas_call x3 -> x2, Pallas kernels: 7.09 us -> 4.72 us  [pack(): pl.pallas_call(pack_kernel, out_shape=[jax.ShapeDtypeStruct((per, part, e...]
  transfers between devices with their start and end apart: 48 -> 36, of which waited for: 19 -> 19; matrix products, arithmetic and copies ran while one was open for 0% -> 0% of each run, Pallas kernels for 22% -> 19%
where the time goes in v4:
time: 236 us; the launch traced here: 234 us
  waiting for transfers between devices  102 us (43%)
  Pallas kernels  56.6 us (24%)
  starting transfers between devices  48.4 us (21%)
  local copies, waits for them, and re-layouts  26.5 us (11%)
    ppermute x28, waiting for transfers between devices, exchange(): lax.ppermute(block, 'four', [(i, i ^ d) for i in range(peers)])  84.3 us
    ppermute x28, starting transfers between devices, exchange(): lax.ppermute(block, 'four', [(i, i ^ d) for i in range(peers)])  33.1 us
    unnamed x156, local copies, waits for them, and re-layouts  26.5 us
    ppermute x6, waiting for transfers between devices, swap_faces(): return (lax.ppermute(lo, 'dom', down_way), lax.ppermute(up, 'dom', up_way))  17.9 us
    pallas_call x2, Pallas kernels, two_sweeps(): pl.pallas_call(functools.partial(sweeps_kernel, block, keep), out_shape=[...  13.7 us
    pallas_call x1, Pallas kernels, finish(): pl.pallas_call(functools.partial(finish_kernel, block, lines), out_shape=...  8.15 us
    ppermute x6, starting transfers between devices, swap_faces(): return (lax.ppermute(lo, 'dom', down_way), lax.ppermute(up, 'dom', up_way))  8.07 us
    pallas_call x1, Pallas kernels, add_force(): pl.pallas_call(functools.partial(force_kernel, block), out_shape=jax.Shap...  7.95 us
  transfers between devices with their start and end apart: 36, of which 19 were waited for; matrix products, arithmetic and copies ran while one was open for 0% of the time, Pallas kernels for 19%

profile of v4, /device:TPU:0, one launch (start us, length us, event | category | flops | bytes accessed | tf_op | source)
XLA Modules:
  0.0 234.5 jit_solution(12994521649023172706)
XLA Ops:
  0.1 2.4 %pack.2 = (f32[32,8,256]{2,1,0:T(8,128)S(1)}, f32[32,8,256]{2,1,0:T(8,128)S(1)}, f32[32,8,256]{2,1,0:T(8,128)S(1)}, f32[32,8,256]{2,1,0:T(8,128)S(1)}, f32[32,8,...) custom-call(s32[2]{0:T(128)S(1)} %pad_add_fusion.pos_ref, ...), custom_call_target="tpu_custom_call" | custom-call | bytes 8388608 | tf_op jit(solution)/shard_map/pack/pallas_call | solution.py:145
  2.4 3.0 %collective-permute-start = (f32[32,8,256]{2,1,0:T(8,128)S(1)}, f32[32,8,256]{2,1,0:T(8,128)S(1)}, u32[]{:S(2)}, u32[]{:S(2)}) collective-permute-start(f32[32,8,256]{2,1,0:T(8,128)S(1)} %get-tuple-element.123), channel_id=1, source_target_pairs={{0,4},{1,5},{2,6},{3,7},{4,0},{5,1},{6,2},{7,3},{8,12},{9,13},{10,... | collective-permute-start | bytes 786440 | tf_op jit(solution)/shard_map/ppermute | solution.py:625
  5.5 1.5 collective-permute-start.2
  7.8 4.0 %collective-permute-done.refs_4_ = f32[32,8,256]{2,1,0:T(8,128)S(1)} collective-permute-done((f32[32,8,256]{2,1,0:T(8,128)S(1)}, f32[32,8,256]{2,1,0:T(8,128)S(1)}, u32[]{:S(2)}, u32[]{:S(2)}) %collective-permute-start) | collective-permute-done | bytes 262176 | tf_op jit(solution)/shard_map/ppermute | solution.py:625
  11.8 1.9 collective-permute-start.4
  14.7 2.4 %pack.3 = (f32[32,8,256]{2,1,0:T(8,128)S(1)}, f32[32,8,256]{2,1,0:T(8,128)S(1)}, f32[32,8,256]{2,1,0:T(8,128)S(1)}, f32[32,8,256]{2,1,0:T(8,128)S(1)}, f32[32,8,...) custom-call(s32[2]{0:T(128)S(1)} %pad_add_fusion.pos_ref, ...), custom_call_target="tpu_custom_call" | custom-call | bytes 8388608 | tf_op jit(solution)/shard_map/pack/pallas_call | solution.py:145
  17.1 2.3 collective-permute-done.3.refs_3_
  19.8 5.7 %collective-permute-done.5.refs_6_ = f32[32,8,256]{2,1,0:T(8,128)S(1)} collective-permute-done((f32[32,8,256]{2,1,0:T(8,128)S(1)}, f32[32,8,256]{2,1,0:T(8,128)S(1)}, u32[]{:S(2)}, u32[]{:S(2)}) %collective-permute-start.5) | collective-permute-done | bytes 262176 | tf_op jit(solution)/shard_map/ppermute | solution.py:625
  25.5 2.0 collective-permute-start.9
  27.6 2.6 %pack_joined.1 = f32[8,32,8,256]{3,2,1,0:T(8,128)S(1)} custom-call(f32[3,32,64,256]{3,2,1,0:T(8,128)} %x_ref.1), custom_call_target="tpu_custom_call" | custom-call | bytes 4194304 | tf_op jit(solution)/shard_map/pack_joined/pallas_call | solution.py:173
  30.3 1.3 copy-done.2
  34.6 1.6 collective-permute-start.12
  36.2 1.7 collective-permute-done.7.refs_4_
  37.9 7.5 %collective-permute-start.10 = (f32[32,8,256]{2,1,0:T(8,128)S(1)}, f32[32,8,256]{2,1,0:T(8,128)S(1)}, u32[]{:S(2)}, u32[]{:S(2)}) collective-permute-start(f32[32,8,256]{2,1,0:T(8,128)S(1)} %get-tuple-element.169), channel_id=1, source_target_pairs={{0,3},{1,2},{2,1},{3,0},{4,7},{5,6},{6,5},{7,4},{8,11},{9,10},{10,... | collective-permute-start | bytes 786440 | tf_op jit(solution)/shard_map/ppermute | solution.py:625
  46.3 2.4 %transform.3 = (f32[32,8,256]{2,1,0:T(8,128)S(1)}, f32[32,8,256]{2,1,0:T(8,128)S(1)}, f32[32,8,256]{2,1,0:T(8,128)S(1)}, f32[32,8,256]{2,1,0:T(8,128)S(1)}, f32[...) custom-call(bf16[512,256]{1,0:T(8,128)(2,1)S(1)} %permuted_table.1.tab, ...), custom_call_target="tpu_custom_call" | custom-call | flops 805306368 | bytes 4194304 | tf_op jit(solution)/shard_map/transform/pallas_call | solution.py:118
  53.0 1.6 collective-permute-start.14
  54.6 4.0 %collective-permute-done.13.refs_7_ = f32[32,8,256]{2,1,0:T(8,128)S(1)} collective-permute-done((f32[32,8,256]{2,1,0:T(8,128)S(1)}, f32[32,8,256]{2,1,0:T(8,128)S(1)}, u32[]{:S(2)}, u32[]{:S(2)}) %collective-permute-start.13) | collective-permute-done | bytes 262176 | tf_op jit(solution)/shard_map/ppermute | solution.py:625
  58.6 2.4 %transform.4 = (f32[32,8,256]{2,1,0:T(8,128)S(1)}, f32[32,8,256]{2,1,0:T(8,128)S(1)}, f32[32,8,256]{2,1,0:T(8,128)S(1)}, f32[32,8,256]{2,1,0:T(8,128)S(1)}, f32[...) custom-call(bf16[512,256]{1,0:T(8,128)(2,1)S(1)} %permuted_table.1.tab, ...), custom_call_target="tpu_custom_call" | custom-call | flops 805306368 | bytes 4194304 | tf_op jit(solution)/shard_map/transform/pallas_call | solution.py:118
  67.8 7.6 %collective-permute-done.15.refs_10_ = f32[32,8,256]{2,1,0:T(8,128)S(1)} collective-permute-done((f32[32,8,256]{2,1,0:T(8,128)S(1)}, f32[32,8,256]{2,1,0:T(8,128)S(1)}, u32[]{:S(2)}, u32[]{:S(2)}) %collective-permute-start.15) | collective-permute-done | bytes 262176 | tf_op jit(solution)/shard_map/ppermute | solution.py:625
  76.1 3.6 %all-to-all-start = ((f32[8,32,8,256]{3,2,1,0:T(8,128)}), f32[8,32,8,256]{3,2,1,0:T(8,128)S(1)}, u32[]{:S(2)}, u32[]{:S(2)}) async-start(f32[8,32,8,256]{3,2,1,0:T(8,128)} %copy-done.2), calls=%async_computation | async-start | bytes 4194304 | tf_op jit(solution)/shard_map/all_to_all | solution.py:595
  79.7 1.9 collective-permute-start.18
  81.7 1.5 collective-permute-start.16
  83.6 27.9 %collective-permute-done.18.refs_2_ = f32[32,8,256]{2,1,0:T(8,128)S(1)} collective-permute-done((f32[32,8,256]{2,1,0:T(8,128)}, f32[32,8,256]{2,1,0:T(8,128)S(1)}, u32[]{:S(2)}, u32[]{:S(2)}) %collective-permute-start.18) | collective-permute-done | bytes 262176 | tf_op jit(solution)/shard_map/ppermute | solution.py:625
  111.8 1.3 collective-permute-start.17
  113.1 3.1 %collective-permute-done.19.refs_3_ = f32[32,8,256]{2,1,0:T(8,128)S(1)} collective-permute-done((f32[32,8,256]{2,1,0:T(8,128)}, f32[32,8,256]{2,1,0:T(8,128)S(1)}, u32[]{:S(2)}, u32[]{:S(2)}) %collective-permute-start.19) | collective-permute-done | bytes 262176 | tf_op jit(solution)/shard_map/ppermute | solution.py:625
  116.2 1.5 collective-permute-start.22
  117.7 5.1 %collective-permute-done.21.refs_7_ = f32[32,8,256]{2,1,0:T(8,128)S(1)} collective-permute-done((f32[32,8,256]{2,1,0:T(8,128)}, f32[32,8,256]{2,1,0:T(8,128)S(1)}, u32[]{:S(2)}, u32[]{:S(2)}) %collective-permute-start.21) | collective-permute-done | bytes 262176 | tf_op jit(solution)/shard_map/ppermute | solution.py:625
  123.3 1.5 collective-permute-start.26
  124.7 4.1 %collective-permute-done.22.refs_12_ = f32[32,8,256]{2,1,0:T(8,128)S(1)} collective-permute-done((f32[32,8,256]{2,1,0:T(8,128)}, f32[32,8,256]{2,1,0:T(8,128)S(1)}, u32[]{:S(2)}, u32[]{:S(2)}) %collective-permute-start.22) | collective-permute-done | bytes 262176 | tf_op jit(solution)/shard_map/ppermute | solution.py:625
  131.2 6.5 %collective-permute-done.26.refs_14_ = f32[32,8,256]{2,1,0:T(8,128)S(1)} collective-permute-done((f32[32,8,256]{2,1,0:T(8,128)}, f32[32,8,256]{2,1,0:T(8,128)S(1)}, u32[]{:S(2)}, u32[]{:S(2)}) %collective-permute-start.26) | collective-permute-done | bytes 262176 | tf_op jit(solution)/shard_map/ppermute | solution.py:625
  137.7 10.7 %collective-permute-done.25.refs_13_ = f32[32,8,256]{2,1,0:T(8,128)S(1)} collective-permute-done((f32[32,8,256]{2,1,0:T(8,128)}, f32[32,8,256]{2,1,0:T(8,128)S(1)}, u32[]{:S(2)}, u32[]{:S(2)}) %collective-permute-start.25) | collective-permute-done | bytes 262176 | tf_op jit(solution)/shard_map/ppermute | solution.py:625
  152.5 5.3 %start_solve.1 = (f32[2048,256]{1,0:T(8,128)}, f32[2048,256]{1,0:T(8,128)}, f32[2048,256]{1,0:T(8,128)}, f32[3,32,512]{2,1,0:T(8,128)S(1)}, f32[3,32,512]{2,1,0:T(8,128)S(1)}) custom-call(s32[2]{0:T(128)S(1)} %pad_add_fusion.pos_ref, f32[2,256]{1,0:T(2,128)S(1)} %copy-done.62, f32[7,64,256]{2,1,0:T(8,128)S(1)} %copy-done.4, ...), custom_call_target="tpu_custom_call" | custom-call | flops 402653184 | bytes 10485760 | tf_op jit(solution)/shard_map/start_solve/pallas_call | solution.py:361
  158.0 3.7 %collective-permute-start.28 = (f32[3,32,512]{2,1,0:T(8,128)S(1)}, f32[3,32,512]{2,1,0:T(8,128)S(1)}, u32[]{:S(2)}, u32[]{:S(2)}) collective-permute-start(f32[3,32,512]{2,1,0:T(8,128)S(1)} %get-tuple-element.225.own_lo_ref), channel_id=1, source_target_pairs={{8,0},{16,8},{24,16},{0,24},{9,1},{17,9},{25,17},{1,25},{10,2},{18... | collective-permute-start | bytes 589832 | tf_op jit(solution)/shard_map/ppermute | solution.py:602
  161.6 5.3 %collective-permute-done.28.got_up_ref.inv_up_ref = f32[3,32,512]{2,1,0:T(8,128)S(1)} collective-permute-done((f32[3,32,512]{2,1,0:T(8,128)S(1)}, f32[3,32,512]{2,1,0:T(8,128)S(1)}, u32[]{:S(2)}, u32[]{:S(2)}) %collective-permute-start.28) | collective-permute-done | bytes 196640 | tf_op jit(solution)/shard_map/ppermute | solution.py:602
  167.0 4.2 %collective-permute-done.29.got_lo_ref.inv_lo_ref = f32[3,32,512]{2,1,0:T(8,128)S(1)} collective-permute-done((f32[3,32,512]{2,1,0:T(8,128)S(1)}, f32[3,32,512]{2,1,0:T(8,128)S(1)}, u32[]{:S(2)}, u32[]{:S(2)}) %collective-permute-start.29) | collective-permute-done | bytes 196640 | tf_op jit(solution)/shard_map/ppermute | solution.py:602
  172.7 6.6 %two_sweeps.2 = (f32[2048,256]{1,0:T(8,128)S(1)}, f32[2,32,512]{2,1,0:T(8,128)S(1)}, f32[2,32,512]{2,1,0:T(8,128)S(1)}) custom-call(f32[2048,256]{1,0:T(8,128)} %get-tuple-element.221.local_ref, f32[2048,256]{1,0:T(8,128)} %get-tuple-element.222.source_ref, f32[2048,256]{1,0:T(8,128)} %get-tuple-element.223.inverse_ref, ...), custom_call_target="tpu_custom_call" | custom-call | flops 402653184 | bytes 8388608 | tf_op jit(solution)/shard_map/two_sweeps/pallas_call | solution.py:430
  179.3 1.3 copy-done.7
  182.9 2.3 transform.5
  185.3 1.3 copy-done.1
  186.6 3.6 %all-to-all-start.1 = ((f32[8,32,8,256]{3,2,1,0:T(8,128)}), f32[8,32,8,256]{3,2,1,0:T(8,128)S(1)}, u32[]{:S(2)}, u32[]{:S(2)}) async-start(f32[8,32,8,256]{3,2,1,0:T(8,128)} %copy-done.1), calls=%async_computation.1 | async-start | bytes 4194304 | tf_op jit(solution)/shard_map/all_to_all | solution.py:595
  190.2 1.8 collective-permute-start.30
  192.6 3.6 %collective-permute-done.30.got_up_ref = f32[2,32,512]{2,1,0:T(8,128)S(1)} collective-permute-done((f32[2,32,512]{2,1,0:T(8,128)}, f32[2,32,512]{2,1,0:T(8,128)S(1)}, u32[]{:S(2)}, u32[]{:S(2)}) %collective-permute-start.30) | collective-permute-done | bytes 131104 | tf_op jit(solution)/shard_map/ppermute | solution.py:602
  196.2 3.8 %collective-permute-done.31.got_lo_ref = f32[2,32,512]{2,1,0:T(8,128)S(1)} collective-permute-done((f32[2,32,512]{2,1,0:T(8,128)}, f32[2,32,512]{2,1,0:T(8,128)S(1)}, u32[]{:S(2)}, u32[]{:S(2)}) %collective-permute-start.31) | collective-permute-done | bytes 131104 | tf_op jit(solution)/shard_map/ppermute | solution.py:602
  203.3 7.0 %two_sweeps.3 = (f32[2048,256]{1,0:T(8,128)S(1)}, f32[1,32,512]{2,1,0:T(8,128)S(1)}, f32[1,32,512]{2,1,0:T(8,128)S(1)}) custom-call(f32[2048,256]{1,0:T(8,128)} %copy-done.7, f32[2048,256]{1,0:T(8,128)} %get-tuple-element.222.source_ref, f32[2048,256]{1,0:T(8,128)} %get-tuple-element.223.inverse_ref, f32[2,32,512]{2,1,0:T(8,128)S(1)} %copy-done.56, ...), custom_call_target="tpu_custom_call" | custom-call | flops 402653184 | bytes 8388608 | tf_op jit(solution)/shard_map/two_sweeps/pallas_call | solution.py:430
  210.3 2.0 collective-permute-start.32
  212.5 4.8 %partial_update.1.part_ref = f32[3,32,64,256]{3,2,1,0:T(8,128)} custom-call(s32[2]{0:T(128)S(1)} %pad_add_fusion.pos_ref, f32[7,64,256]{2,1,0:T(8,128)S(1)} %copy-done.5, bf16[128,192]{1,0:T(8,128)(2,1)S(1)} %copy-done.9, f32[32,8,256]{2,1,0:T(8,128)S(1)} %copy-done.12, f32[32,8,256]{2,1,0:T(8,128)S(1)} %copy-done.33, f32[32,8,256]{2,1,0:T(8,128)S(1)} %copy-done.23, ...), custom_call_target="tpu_custom_call" | custom-call | flops 805306368 | bytes 10485760 | tf_op jit(solution)/shard_map/partial_update/pallas_call | solution.py:475
  218.4 7.9 %add_force.1.part_ref = f32[3,32,64,256]{3,2,1,0:T(8,128)} custom-call(s32[2]{0:T(128)S(1)} %pad_add_fusion.pos_ref, f32[2048,256]{1,0:T(8,128)S(1)} %get-tuple-element.231.local_ref, f32[2048,256]{1,0:T(8,128)S(1)} %copy-done, f32[1,32,512]{2,1,0:T(8,128)S(1)} %collective-permute-done.32.got_up_ref, ...), custom_call_target="tpu_custom_call", output_to_operand_aliasing={{}: (9, {})} | custom-call | flops 201326592 | bytes 12582912 | tf_op jit(solution)/shard_map/add_force/pallas_call | solution.py:528
  226.4 8.1 %finish.1 = f32[3,32,64,256]{3,2,1,0:T(8,128)} custom-call(s32[2]{0:T(128)S(1)} %pad_add_fusion.pos_ref, f32[7,64,256]{2,1,0:T(8,128)S(1)} %copy-done.6, bf16[128,192]{1,0:T(8,128)(2,1)S(1)} %copy-done.10, f32[3,32,64,256]{3,2,1,0:T(8,128)} %add_force.1.part_ref, ...), custom_call_target="tpu_custom_call", output_to_operand_aliasing={{}: (3, {})} | custom-call | flops 402653184 | bytes 10485760 | tf_op jit(solution)/shard_map/finish/pallas_call | solution.py:578
  (195 shorter events, 34.7 us)
Async XLA Ops:
  2.4 9.3 %collective-permute-start = (f32[32,8,256]{2,1,0:T(8,128)S(1)}, f32[32,8,256]{2,1,0:T(8,128)S(1)}, u32[]{:S(2)}, u32[]{:S(2)}) collective-permute-start(f32[32,8,256]{2,1,0:T(8,128)S(1)} %get-tuple-element.123), channel_id=1, source_target_pairs={{0,4},{1,5},{2,6},{3,7},{4,0},{5,1},{6,2},{7,3},{8,12},{9,13},{10,... | collective-permute-start | bytes 786440 | tf_op jit(solution)/shard_map/ppermute | solution.py:625
  5.5 9.2 %collective-permute-start.2 = (f32[32,8,256]{2,1,0:T(8,128)S(1)}, f32[32,8,256]{2,1,0:T(8,128)S(1)}, u32[]{:S(2)}, u32[]{:S(2)}) collective-permute-start(f32[32,8,256]{2,1,0:T(8,128)S(1)} %get-tuple-element.127), channel_id=1, source_target_pairs={{0,2},{1,3},{2,0},{3,1},{4,6},{5,7},{6,4},{7,5},{8,10},{9,11},{10,... | collective-permute-start | bytes 786440 | tf_op jit(solution)/shard_map/ppermute | solution.py:625
  7.0 12.4 %collective-permute-start.3 = (f32[32,8,256]{2,1,0:T(8,128)S(1)}, f32[32,8,256]{2,1,0:T(8,128)S(1)}, u32[]{:S(2)}, u32[]{:S(2)}) collective-permute-start(f32[32,8,256]{2,1,0:T(8,128)S(1)} %get-tuple-element.130), channel_id=1, source_target_pairs={{0,3},{1,2},{2,1},{3,0},{4,7},{5,6},{6,5},{7,4},{8,11},{9,10},{10,... | collective-permute-start | bytes 786440 | tf_op jit(solution)/shard_map/ppermute | solution.py:625
  7.0 18.5 %collective-permute-start.5 = (f32[32,8,256]{2,1,0:T(8,128)S(1)}, f32[32,8,256]{2,1,0:T(8,128)S(1)}, u32[]{:S(2)}, u32[]{:S(2)}) collective-permute-start(f32[32,8,256]{2,1,0:T(8,128)S(1)} %get-tuple-element.137), channel_id=1, source_target_pairs={{0,6},{1,7},{2,4},{3,5},{4,2},{5,3},{6,0},{7,1},{8,14},{9,15},{10,... | collective-permute-start | bytes 786440 | tf_op jit(solution)/shard_map/ppermute | solution.py:625
  11.8 15.7 %collective-permute-start.1 = (f32[32,8,256]{2,1,0:T(8,128)S(1)}, f32[32,8,256]{2,1,0:T(8,128)S(1)}, u32[]{:S(2)}, u32[]{:S(2)}) collective-permute-start(f32[32,8,256]{2,1,0:T(8,128)S(1)} %get-tuple-element.124), channel_id=1, source_target_pairs={{0,1},{1,0},{2,3},{3,2},{4,5},{5,4},{6,7},{7,6},{8,9},{9,8},{10,11... | collective-permute-start | bytes 786440 | tf_op jit(solution)/shard_map/ppermute | solution.py:625
  11.8 22.8 %collective-permute-start.4 = (f32[32,8,256]{2,1,0:T(8,128)S(1)}, f32[32,8,256]{2,1,0:T(8,128)S(1)}, u32[]{:S(2)}, u32[]{:S(2)}) collective-permute-start(f32[32,8,256]{2,1,0:T(8,128)S(1)} %get-tuple-element.134), channel_id=1, source_target_pairs={{0,5},{1,4},{2,7},{3,6},{4,1},{5,0},{6,3},{7,2},{8,13},{9,12},{10,... | collective-permute-start | bytes 786440 | tf_op jit(solution)/shard_map/ppermute | solution.py:625
  14.7 21.5 %collective-permute-start.6 = (f32[32,8,256]{2,1,0:T(8,128)S(1)}, f32[32,8,256]{2,1,0:T(8,128)S(1)}, u32[]{:S(2)}, u32[]{:S(2)}) collective-permute-start(f32[32,8,256]{2,1,0:T(8,128)S(1)} %get-tuple-element.140), channel_id=1, source_target_pairs={{0,7},{1,6},{2,5},{3,4},{4,3},{5,2},{6,1},{7,0},{8,15},{9,14},{10,... | collective-permute-start | bytes 786440 | tf_op jit(solution)/shard_map/ppermute | solution.py:625
  19.3 18.5 %collective-permute-start.7 = (f32[32,8,256]{2,1,0:T(8,128)S(1)}, f32[32,8,256]{2,1,0:T(8,128)S(1)}, u32[]{:S(2)}, u32[]{:S(2)}) collective-permute-start(f32[32,8,256]{2,1,0:T(8,128)S(1)} %get-tuple-element.162), channel_id=1, source_target_pairs={{0,4},{1,5},{2,6},{3,7},{4,0},{5,1},{6,2},{7,3},{8,12},{9,13},{10,... | collective-permute-start | bytes 786440 | tf_op jit(solution)/shard_map/ppermute | solution.py:625
  25.5 12.4 %collective-permute-start.9 = (f32[32,8,256]{2,1,0:T(8,128)S(1)}, f32[32,8,256]{2,1,0:T(8,128)S(1)}, u32[]{:S(2)}, u32[]{:S(2)}) collective-permute-start(f32[32,8,256]{2,1,0:T(8,128)S(1)} %get-tuple-element.166), channel_id=1, source_target_pairs={{0,2},{1,3},{2,0},{3,1},{4,6},{5,7},{6,4},{7,5},{8,10},{9,11},{10,... | collective-permute-start | bytes 786440 | tf_op jit(solution)/shard_map/ppermute | solution.py:625
  27.6 25.4 %collective-permute-start.11 = (f32[32,8,256]{2,1,0:T(8,128)S(1)}, f32[32,8,256]{2,1,0:T(8,128)S(1)}, u32[]{:S(2)}, u32[]{:S(2)}) collective-permute-start(f32[32,8,256]{2,1,0:T(8,128)S(1)} %get-tuple-element.173), channel_id=1, source_target_pairs={{0,5},{1,4},{2,7},{3,6},{4,1},{5,0},{6,3},{7,2},{8,13},{9,12},{10,... | collective-permute-start | bytes 786440 | tf_op jit(solution)/shard_map/ppermute | solution.py:625
  33.6 114.8 %copy-start.8 = (bf16[128,192]{1,0:T(8,128)(2,1)}, bf16[128,192]{1,0:T(8,128)(2,1)S(1)}, u32[]{:S(2)}) copy-start(bf16[128,192]{1,0:T(8,128)(2,1)S(1)} %get-tuple-element.149.dpack_ref) | copy-start | bytes 147460
  33.6 114.8 %copy-start.48 = (f32[2,8,512]{2,1,0:T(8,128)}, f32[2,8,512]{2,1,0:T(8,128)S(1)}, u32[]{:S(2)}) copy-start(f32[2,8,512]{2,1,0:T(8,128)S(1)} %get-tuple-element.190.mask_ref) | copy-start | bytes 98308
  33.6 114.8 %copy-start.52 = (bf16[64,192]{1,0:T(8,128)(2,1)}, bf16[64,192]{1,0:T(8,128)(2,1)S(1)}, u32[]{:S(2)}) copy-start(bf16[64,192]{1,0:T(8,128)(2,1)S(1)} %get-tuple-element.188.spack_ref) | copy-start | bytes 73732
  34.6 20.0 %collective-permute-start.12 = (f32[32,8,256]{2,1,0:T(8,128)S(1)}, f32[32,8,256]{2,1,0:T(8,128)S(1)}, u32[]{:S(2)}, u32[]{:S(2)}) collective-permute-start(f32[32,8,256]{2,1,0:T(8,128)S(1)} %get-tuple-element.176), channel_id=1, source_target_pairs={{0,6},{1,7},{2,4},{3,5},{4,2},{5,3},{6,0},{7,1},{8,14},{9,15},{10,... | collective-permute-start | bytes 786440 | tf_op jit(solution)/shard_map/ppermute | solution.py:625
  37.9 16.7 %collective-permute-start.8 = (f32[32,8,256]{2,1,0:T(8,128)S(1)}, f32[32,8,256]{2,1,0:T(8,128)S(1)}, u32[]{:S(2)}, u32[]{:S(2)}) collective-permute-start(f32[32,8,256]{2,1,0:T(8,128)S(1)} %get-tuple-element.163), channel_id=1, source_target_pairs={{0,1},{1,0},{2,3},{3,2},{4,5},{5,4},{6,7},{7,6},{8,9},{9,8},{10,11... | collective-permute-start | bytes 786440 | tf_op jit(solution)/shard_map/ppermute | solution.py:625
  37.9 16.7 %collective-permute-start.10 = (f32[32,8,256]{2,1,0:T(8,128)S(1)}, f32[32,8,256]{2,1,0:T(8,128)S(1)}, u32[]{:S(2)}, u32[]{:S(2)}) collective-permute-start(f32[32,8,256]{2,1,0:T(8,128)S(1)} %get-tuple-element.169), channel_id=1, source_target_pairs={{0,3},{1,2},{2,1},{3,0},{4,7},{5,6},{6,5},{7,4},{8,11},{9,10},{10,... | collective-permute-start | bytes 786440 | tf_op jit(solution)/shard_map/ppermute | solution.py:625
  45.3 13.2 %collective-permute-start.13 = (f32[32,8,256]{2,1,0:T(8,128)S(1)}, f32[32,8,256]{2,1,0:T(8,128)S(1)}, u32[]{:S(2)}, u32[]{:S(2)}) collective-permute-start(f32[32,8,256]{2,1,0:T(8,128)S(1)} %get-tuple-element.179), channel_id=1, source_target_pairs={{0,7},{1,6},{2,5},{3,4},{4,3},{5,2},{6,1},{7,0},{8,15},{9,14},{10,... | collective-permute-start | bytes 786440 | tf_op jit(solution)/shard_map/ppermute | solution.py:625
  53.0 95.5 %copy-start.11 = (f32[32,8,256]{2,1,0:T(8,128)}, f32[32,8,256]{2,1,0:T(8,128)S(1)}, u32[]{:S(2)}) copy-start(f32[32,8,256]{2,1,0:T(8,128)S(1)} %get-tuple-element.191.refs_0_) | copy-start | bytes 786436
  53.0 13.0 %collective-permute-start.14 = (f32[32,8,256]{2,1,0:T(8,128)S(1)}, f32[32,8,256]{2,1,0:T(8,128)S(1)}, u32[]{:S(2)}, u32[]{:S(2)}) collective-permute-start(f32[32,8,256]{2,1,0:T(8,128)S(1)} %get-tuple-element.183), channel_id=1, source_target_pairs={{0,6},{1,7},{2,4},{3,5},{4,2},{5,3},{6,0},{7,1},{8,14},{9,15},{10,... | collective-permute-start | bytes 786440 | tf_op jit(solution)/shard_map/ppermute | solution.py:625
  66.6 8.7 %collective-permute-start.15 = (f32[32,8,256]{2,1,0:T(8,128)S(1)}, f32[32,8,256]{2,1,0:T(8,128)S(1)}, u32[]{:S(2)}, u32[]{:S(2)}) collective-permute-start(f32[32,8,256]{2,1,0:T(8,128)S(1)} %get-tuple-element.184), channel_id=1, source_target_pairs={{0,2},{1,3},{2,0},{3,1},{4,6},{5,7},{6,4},{7,5},{8,10},{9,11},{10,... | collective-permute-start | bytes 786440 | tf_op jit(solution)/shard_map/ppermute | solution.py:625
  76.1 105.9 %all-to-all-start = ((f32[8,32,8,256]{3,2,1,0:T(8,128)}), f32[8,32,8,256]{3,2,1,0:T(8,128)S(1)}, u32[]{:S(2)}, u32[]{:S(2)}) async-start(f32[8,32,8,256]{3,2,1,0:T(8,128)} %copy-done.2), calls=%async_computation | async-start | bytes 4194304 | tf_op jit(solution)/shard_map/all_to_all | solution.py:595
  79.7 31.8 %collective-permute-start.18 = (f32[32,8,256]{2,1,0:T(8,128)}, f32[32,8,256]{2,1,0:T(8,128)S(1)}, u32[]{:S(2)}, u32[]{:S(2)}) collective-permute-start(f32[32,8,256]{2,1,0:T(8,128)} %copy-done.77), channel_id=1, source_target_pairs={{0,2},{1,3},{2,0},{3,1},{4,6},{5,7},{6,4},{7,5},{8,10},{9,11},{10,... | collective-permute-start | bytes 786440 | tf_op jit(solution)/shard_map/ppermute | solution.py:625
  81.7 30.1 %collective-permute-start.16 = (f32[32,8,256]{2,1,0:T(8,128)}, f32[32,8,256]{2,1,0:T(8,128)S(1)}, u32[]{:S(2)}, u32[]{:S(2)}) collective-permute-start(f32[32,8,256]{2,1,0:T(8,128)} %copy-done.75), channel_id=1, source_target_pairs={{0,4},{1,5},{2,6},{3,7},{4,0},{5,1},{6,2},{7,3},{8,12},{9,13},{10,... | collective-permute-start | bytes 786440 | tf_op jit(solution)/shard_map/ppermute | solution.py:625
  83.1 33.0 %collective-permute-start.19 = (f32[32,8,256]{2,1,0:T(8,128)}, f32[32,8,256]{2,1,0:T(8,128)S(1)}, u32[]{:S(2)}, u32[]{:S(2)}) collective-permute-start(f32[32,8,256]{2,1,0:T(8,128)} %copy-done.74), channel_id=1, source_target_pairs={{0,3},{1,2},{2,1},{3,0},{4,7},{5,6},{6,5},{7,4},{8,11},{9,10},{10,... | collective-permute-start | bytes 786440 | tf_op jit(solution)/shard_map/ppermute | solution.py:625
  83.2 34.5 %collective-permute-start.20 = (f32[32,8,256]{2,1,0:T(8,128)}, f32[32,8,256]{2,1,0:T(8,128)S(1)}, u32[]{:S(2)}, u32[]{:S(2)}) collective-permute-start(f32[32,8,256]{2,1,0:T(8,128)} %copy-done.71), channel_id=1, source_target_pairs={{0,5},{1,4},{2,7},{3,6},{4,1},{5,0},{6,3},{7,2},{8,13},{9,12},{10,... | collective-permute-start | bytes 786440 | tf_op jit(solution)/shard_map/ppermute | solution.py:625
  111.5 46.3 %copy-start.22 = (f32[32,8,256]{2,1,0:T(8,128)}, f32[32,8,256]{2,1,0:T(8,128)S(1)}, u32[]{:S(2)}) copy-start(f32[32,8,256]{2,1,0:T(8,128)S(1)} %collective-permute-done.18.refs_2_) | copy-start | bytes 786436
  111.5 11.3 %collective-permute-start.21 = (f32[32,8,256]{2,1,0:T(8,128)}, f32[32,8,256]{2,1,0:T(8,128)S(1)}, u32[]{:S(2)}, u32[]{:S(2)}) collective-permute-start(f32[32,8,256]{2,1,0:T(8,128)} %copy-done.69), channel_id=1, source_target_pairs={{0,7},{1,6},{2,5},{3,4},{4,3},{5,2},{6,1},{7,0},{8,15},{9,14},{10,... | collective-permute-start | bytes 786440 | tf_op jit(solution)/shard_map/ppermute | solution.py:625
  111.8 46.1 %copy-start.24 = (f32[32,8,256]{2,1,0:T(8,128)}, f32[32,8,256]{2,1,0:T(8,128)S(1)}, u32[]{:S(2)}) copy-start(f32[32,8,256]{2,1,0:T(8,128)S(1)} %collective-permute-done.16.refs_4_) | copy-start | bytes 786436
  111.8 13.0 %collective-permute-start.17 = (f32[32,8,256]{2,1,0:T(8,128)}, f32[32,8,256]{2,1,0:T(8,128)S(1)}, u32[]{:S(2)}, u32[]{:S(2)}) collective-permute-start(f32[32,8,256]{2,1,0:T(8,128)} %copy-done.66), channel_id=1, source_target_pairs={{0,1},{1,0},{2,3},{3,2},{4,5},{5,4},{6,7},{7,6},{8,9},{9,8},{10,11... | collective-permute-start | bytes 786440 | tf_op jit(solution)/shard_map/ppermute | solution.py:625
  116.2 41.7 %copy-start.26 = (f32[32,8,256]{2,1,0:T(8,128)}, f32[32,8,256]{2,1,0:T(8,128)S(1)}, u32[]{:S(2)}) copy-start(f32[32,8,256]{2,1,0:T(8,128)S(1)} %collective-permute-done.19.refs_3_) | copy-start | bytes 786436
  116.2 12.6 %collective-permute-start.22 = (f32[32,8,256]{2,1,0:T(8,128)}, f32[32,8,256]{2,1,0:T(8,128)S(1)}, u32[]{:S(2)}, u32[]{:S(2)}) collective-permute-start(f32[32,8,256]{2,1,0:T(8,128)} %copy-done.76), channel_id=1, source_target_pairs={{0,4},{1,5},{2,6},{3,7},{4,0},{5,1},{6,2},{7,3},{8,12},{9,13},{10,... | collective-permute-start | bytes 786440 | tf_op jit(solution)/shard_map/ppermute | solution.py:625
  117.7 40.2 %copy-start.28 = (f32[32,8,256]{2,1,0:T(8,128)}, f32[32,8,256]{2,1,0:T(8,128)S(1)}, u32[]{:S(2)}) copy-start(f32[32,8,256]{2,1,0:T(8,128)S(1)} %collective-permute-done.20.refs_5_) | copy-start | bytes 786436
  122.8 35.0 %copy-start.30 = (f32[32,8,256]{2,1,0:T(8,128)}, f32[32,8,256]{2,1,0:T(8,128)S(1)}, u32[]{:S(2)}) copy-start(f32[32,8,256]{2,1,0:T(8,128)S(1)} %collective-permute-done.21.refs_7_) | copy-start | bytes 786436
  122.8 8.4 %collective-permute-start.24 = (f32[32,8,256]{2,1,0:T(8,128)}, f32[32,8,256]{2,1,0:T(8,128)S(1)}, u32[]{:S(2)}, u32[]{:S(2)}) collective-permute-start(f32[32,8,256]{2,1,0:T(8,128)} %copy-done.73), channel_id=1, source_target_pairs={{0,3},{1,2},{2,1},{3,0},{4,7},{5,6},{6,5},{7,4},{8,11},{9,10},{10,... | collective-permute-start | bytes 786440 | tf_op jit(solution)/shard_map/ppermute | solution.py:625
  123.3 14.5 %collective-permute-start.26 = (f32[32,8,256]{2,1,0:T(8,128)}, f32[32,8,256]{2,1,0:T(8,128)S(1)}, u32[]{:S(2)}, u32[]{:S(2)}) collective-permute-start(f32[32,8,256]{2,1,0:T(8,128)} %copy-done.72), channel_id=1, source_target_pairs={{0,6},{1,7},{2,4},{3,5},{4,2},{5,3},{6,0},{7,1},{8,14},{9,15},{10,... | collective-permute-start | bytes 786440 | tf_op jit(solution)/shard_map/ppermute | solution.py:625
  124.7 33.1 %copy-start.32 = (f32[32,8,256]{2,1,0:T(8,128)}, f32[32,8,256]{2,1,0:T(8,128)S(1)}, u32[]{:S(2)}) copy-start(f32[32,8,256]{2,1,0:T(8,128)S(1)} %collective-permute-done.17.refs_1_) | copy-start | bytes 786436
  128.8 29.1 %copy-start.34 = (f32[32,8,256]{2,1,0:T(8,128)}, f32[32,8,256]{2,1,0:T(8,128)S(1)}, u32[]{:S(2)}) copy-start(f32[32,8,256]{2,1,0:T(8,128)S(1)} %collective-permute-done.22.refs_12_) | copy-start | bytes 786436
  128.8 8.9 %collective-permute-start.23 = (f32[32,8,256]{2,1,0:T(8,128)}, f32[32,8,256]{2,1,0:T(8,128)S(1)}, u32[]{:S(2)}, u32[]{:S(2)}) collective-permute-start(f32[32,8,256]{2,1,0:T(8,128)} %copy-done.70), channel_id=1, source_target_pairs={{0,1},{1,0},{2,3},{3,2},{4,5},{5,4},{6,7},{7,6},{8,9},{9,8},{10,11... | collective-permute-start | bytes 786440 | tf_op jit(solution)/shard_map/ppermute | solution.py:625
  128.9 19.5 %collective-permute-start.25 = (f32[32,8,256]{2,1,0:T(8,128)}, f32[32,8,256]{2,1,0:T(8,128)S(1)}, u32[]{:S(2)}, u32[]{:S(2)}) collective-permute-start(f32[32,8,256]{2,1,0:T(8,128)} %copy-done.68), channel_id=1, source_target_pairs={{0,5},{1,4},{2,7},{3,6},{4,1},{5,0},{6,3},{7,2},{8,13},{9,12},{10,... | collective-permute-start | bytes 786440 | tf_op jit(solution)/shard_map/ppermute | solution.py:625
  129.5 19.0 %collective-permute-start.27 = (f32[32,8,256]{2,1,0:T(8,128)}, f32[32,8,256]{2,1,0:T(8,128)S(1)}, u32[]{:S(2)}, u32[]{:S(2)}) collective-permute-start(f32[32,8,256]{2,1,0:T(8,128)} %copy-done.67), channel_id=1, source_target_pairs={{0,7},{1,6},{2,5},{3,4},{4,3},{5,2},{6,1},{7,0},{8,15},{9,14},{10,... | collective-permute-start | bytes 786440 | tf_op jit(solution)/shard_map/ppermute | solution.py:625
  131.2 26.7 %copy-start.36 = (f32[32,8,256]{2,1,0:T(8,128)}, f32[32,8,256]{2,1,0:T(8,128)S(1)}, u32[]{:S(2)}) copy-start(f32[32,8,256]{2,1,0:T(8,128)S(1)} %collective-permute-done.24.refs_11_) | copy-start | bytes 786436
  158.0 9.0 %collective-permute-start.28 = (f32[3,32,512]{2,1,0:T(8,128)S(1)}, f32[3,32,512]{2,1,0:T(8,128)S(1)}, u32[]{:S(2)}, u32[]{:S(2)}) collective-permute-start(f32[3,32,512]{2,1,0:T(8,128)S(1)} %get-tuple-element.225.own_lo_ref), channel_id=1, source_target_pairs={{8,0},{16,8},{24,16},{0,24},{9,1},{17,9},{25,17},{1,25},{10,2},{18... | collective-permute-start | bytes 589832 | tf_op jit(solution)/shard_map/ppermute | solution.py:602
  161.6 9.5 %collective-permute-start.29 = (f32[3,32,512]{2,1,0:T(8,128)S(1)}, f32[3,32,512]{2,1,0:T(8,128)S(1)}, u32[]{:S(2)}, u32[]{:S(2)}) collective-permute-start(f32[3,32,512]{2,1,0:T(8,128)S(1)} %get-tuple-element.224.own_up_ref), channel_id=1, source_target_pairs={{0,8},{8,16},{16,24},{24,0},{1,9},{9,17},{17,25},{25,1},{2,10},{10... | collective-permute-start | bytes 589832 | tf_op jit(solution)/shard_map/ppermute | solution.py:602
  186.6 39.8 %all-to-all-start.1 = ((f32[8,32,8,256]{3,2,1,0:T(8,128)}), f32[8,32,8,256]{3,2,1,0:T(8,128)S(1)}, u32[]{:S(2)}, u32[]{:S(2)}) async-start(f32[8,32,8,256]{3,2,1,0:T(8,128)} %copy-done.1), calls=%async_computation.1 | async-start | bytes 4194304 | tf_op jit(solution)/shard_map/all_to_all | solution.py:595
  190.2 6.0 %collective-permute-start.30 = (f32[2,32,512]{2,1,0:T(8,128)}, f32[2,32,512]{2,1,0:T(8,128)S(1)}, u32[]{:S(2)}, u32[]{:S(2)}) collective-permute-start(f32[2,32,512]{2,1,0:T(8,128)} %copy-done.57), channel_id=1, source_target_pairs={{8,0},{16,8},{24,16},{0,24},{9,1},{17,9},{25,17},{1,25},{10,2},{18... | collective-permute-start | bytes 393224 | tf_op jit(solution)/shard_map/ppermute | solution.py:602
  192.1 7.8 %collective-permute-start.31 = (f32[2,32,512]{2,1,0:T(8,128)}, f32[2,32,512]{2,1,0:T(8,128)S(1)}, u32[]{:S(2)}, u32[]{:S(2)}) collective-permute-start(f32[2,32,512]{2,1,0:T(8,128)} %copy-done.55), channel_id=1, source_target_pairs={{0,8},{8,16},{16,24},{24,0},{1,9},{9,17},{17,25},{25,1},{2,10},{10... | collective-permute-start | bytes 393224 | tf_op jit(solution)/shard_map/ppermute | solution.py:602
  210.3 7.1 %collective-permute-start.32 = (f32[1,32,512]{2,1,0:T(8,128)S(1)}, f32[1,32,512]{2,1,0:T(8,128)S(1)}, u32[]{:S(2)}, u32[]{:S(2)}) collective-permute-start(f32[1,32,512]{2,1,0:T(8,128)S(1)} %get-tuple-element.232), channel_id=1, source_target_pairs={{8,0},{16,8},{24,16},{0,24},{9,1},{17,9},{25,17},{1,25},{10,2},{18... | collective-permute-start | bytes 196616 | tf_op jit(solution)/shard_map/ppermute | solution.py:602
  212.3 6.1 %collective-permute-start.33 = (f32[1,32,512]{2,1,0:T(8,128)S(1)}, f32[1,32,512]{2,1,0:T(8,128)S(1)}, u32[]{:S(2)}, u32[]{:S(2)}) collective-permute-start(f32[1,32,512]{2,1,0:T(8,128)S(1)} %get-tuple-element.233), channel_id=1, source_target_pairs={{0,8},{8,16},{16,24},{24,0},{1,9},{9,17},{17,25},{25,1},{2,10},{10... | collective-permute-start | bytes 196616 | tf_op jit(solution)/shard_map/ppermute | solution.py:602
  (66 other events, 513.8 us)

commit v5 on v4

--- a/solution.py
+++ b/solution.py
@@ -20,7 +20,7 @@
 
 F32 = jnp.float32
 BF16 = jnp.bfloat16
-VMEM_LIMIT = 48 * 1024 * 1024
+VMEM_LIMIT = 24 * 1024 * 1024
 SMEM_SPEC = pl.BlockSpec(memory_space=pltpu.SMEM)
 
 
@@ -92,39 +92,48 @@
     )(position, table)
 
 
-def transform_kernel(count, table_ref, *refs):
+def transform_kernel(count, pos_ref, table_ref, *refs):
     planes = table_ref.shape[1]
     both = table_ref[...]
     high_table = both[:planes]
     width = refs[0].shape[-1]
     nodes = refs[0].shape[-2]
     per = planes // count
-    flat = [ref.reshape(per * nodes, width) for ref in refs]
+    outs = refs[count:]
+    if len(outs) < count:
+        outs = [outs[0].at[pos_ref[1] ^ d] for d in range(count)]
+    flat = [ref.reshape(per * nodes, width) for ref in refs[:count]]
+    outs = [ref.reshape(per * nodes, width) for ref in outs]
     for n in range(nodes):
         rows = pl.ds(n, per, stride=nodes) if nodes > 1 else pl.ds(0, per)
-        high, low = split(jnp.concatenate([ref[rows, :] for ref in flat[:count]], axis=0))
+        high, low = split(jnp.concatenate([ref[rows, :] for ref in flat], axis=0))
         wide = dot(both, high)
         result = wide[:planes] + (wide[planes:] + dot(high_table, low))
-        for d, ref in enumerate(flat[count:]):
+        for d, ref in enumerate(outs):
             ref[rows, :] = result[d * per : (d + 1) * per]
 
 
-def transform(blocks, table):
-    *lead, nodes, elements = blocks[0].shape
-    zeros = (0,) * (len(lead) + 1)
+def transform(position, blocks, table, join=False):
+    per, nodes, elements = blocks[0].shape
+    count = len(blocks)
     width = 128
-    block = pl.BlockSpec((*lead, nodes, width), lambda i: (*zeros, i))
-    size = len(blocks) * blocks[0].size
-    return pl.pallas_call(
-        functools.partial(transform_kernel, len(blocks)),
-        out_shape=[jax.ShapeDtypeStruct(v.shape, F32) for v in blocks],
+    block = pl.BlockSpec((per, nodes, width), lambda i: (0, 0, i))
+    out_shape = [jax.ShapeDtypeStruct(v.shape, F32) for v in blocks]
+    out_specs = [block] * count
+    if join:
+        out_shape = jax.ShapeDtypeStruct((count, per, nodes, elements), F32)
+        out_specs = pl.BlockSpec((count, per, nodes, width), lambda i: (0, 0, 0, i))
+    size = count * blocks[0].size
+    return pl.pallas_call(
+        functools.partial(transform_kernel, count),
+        out_shape=out_shape,
         grid=(elements // width,),
-        in_specs=[pl.BlockSpec(table.shape, lambda i: (0, 0))] + [block] * len(blocks),
-        out_specs=[block] * len(blocks),
+        in_specs=[SMEM_SPEC, pl.BlockSpec(table.shape, lambda i: (0, 0))] + [block] * count,
+        out_specs=out_specs,
         compiler_params=params(),
         cost_estimate=cost(6 * PLANES * size, 8 * size),
         name="transform",
-    )(table, *blocks)
+    )(position, table, *blocks)
 
 
 def pack_kernel(pos_ref, *refs):
@@ -155,31 +164,6 @@
         cost_estimate=cost(0, 16 * size),
         name="pack",
     )(position, *[adjoint] * peers)
-
-
-def pack_joined_kernel(x_ref, o_ref):
-    part = o_ref.shape[2]
-    for d in range(o_ref.shape[0]):
-        o_ref[d] = x_ref[0, :, d * part : (d + 1) * part, :]
-
-
-def pack_joined(adjoint, comp, peers):
-    _, per, nodes, elements = adjoint.shape
-    part = nodes // peers
-    if part % 8:
-        return jnp.moveaxis(adjoint[comp].reshape(per, peers, part, elements), 1, 0)
-    block = per // 4
-    size = per * nodes * elements
-    return pl.pallas_call(
-        pack_joined_kernel,
-        out_shape=jax.ShapeDtypeStruct((peers, per, part, elements), F32),
-        grid=(per // block,),
-        in_specs=[pl.BlockSpec((1, block, nodes, elements), lambda q: (comp, q, 0, 0))],
-        out_specs=pl.BlockSpec((peers, block, part, elements), lambda q: (0, q, 0, 0)),
-        compiler_params=params(),
-        cost_estimate=cost(0, 8 * size),
-        name="pack_joined",
-    )(adjoint)
 
 
 BXR, BYS, DXBX, DXBY, DYBX, DYBY, DIAG = range(7)
@@ -379,22 +363,22 @@
 
 def sweeps_kernel(
     block, keep, local_ref, source_ref, inverse_ref, own_up_ref, own_lo_ref,
-    got_up_ref, got_lo_ref, inv_up_ref, inv_lo_ref, spack_ref, gather_ref, scatter_ref, mask_ref,
+    own_inv_up_ref, own_inv_lo_ref, got_up_ref, got_lo_ref, inv_up_ref, inv_lo_ref, spack_ref, gather_ref, scatter_ref, mask_ref,
     next_ref, up_ref, lo_ref, pot_ref,
 ):
     nodes = spack_ref.shape[0]
     spack = spack_ref[...]
     lines = block * (nodes // LINE)
     partners = []
-    for side, own, got, inv in (
-        (0, own_up_ref, got_up_ref, inv_up_ref),
-        (1, own_lo_ref, got_lo_ref, inv_lo_ref),
+    for side, own, own_inv, got, inv in (
+        (0, own_up_ref, own_inv_up_ref, got_up_ref, inv_up_ref),
+        (1, own_lo_ref, own_inv_lo_ref, got_lo_ref, inv_lo_ref),
     ):
-        now = got[0]
-        later = got[1] + PENALTY * inv[0] * own[0]
+        scale = PENALTY * own_inv[0]
+        now = scale * got[0]
+        later = scale * (got[1] + PENALTY * inv[0] * own[0])
         both = scatter_faces(side, jnp.concatenate([now, later], axis=0), scatter_ref, mask_ref)
-        scale = PENALTY * face_of(inverse_ref, side)[...]
-        partners.append((scale * both[:lines], scale * both[lines:]))
+        partners.append((both[:lines], both[lines:]))
     pot_ref[...] = local_ref[...]
     for side in range(2):
         face = face_of(pot_ref, side)
@@ -415,7 +399,7 @@
             out[k] = picked[k * block : (k + 1) * block]
 
 
-def two_sweeps(keep, local, source, inverse, own, got, inv, spack, gather, scatter, mask):
+def two_sweeps(keep, local, source, inverse, own, own_inv, got, inv, spack, gather, scatter, mask):
     nodes = spack.shape[0]
     elements = local.shape[1]
     coefs = local.shape[0] // nodes
@@ -433,7 +417,7 @@
         + [jax.ShapeDtypeStruct((keep, coefs, shared), F32)] * 2,
         grid=(coefs // block,),
         in_specs=[
-            flat, flat, flat, one, one, two, two, third, third,
+            flat, flat, flat, one, one, third, third, two, two, third, third,
             whole(spack.shape), whole(gather.shape), whole(scatter.shape), whole(mask.shape),
         ],
         out_specs=[flat, face, face],
@@ -441,7 +425,7 @@
         compiler_params=params(),
         cost_estimate=cost(12 * nodes * size, 16 * size),
         name="two_sweeps",
-    )(local, source, inverse, *own, *got, *inv, spack, gather, scatter, mask)
+    )(local, source, inverse, *own, *own_inv, *got, *inv, spack, gather, scatter, mask)
 
 
 def store_own(ref, me, value, *lead):
@@ -485,8 +469,8 @@
 
 
 def force_kernel(
-    block, pos_ref, local_ref, inverse_ref, got_up_ref, got_lo_ref, geo_ref, dpack_ref, scatter_ref,
-    mask_ref, part_ref, o_ref, pot_ref,
+    block, pos_ref, local_ref, inv_up_ref, inv_lo_ref, got_up_ref, got_lo_ref, geo_ref, dpack_ref,
+    scatter_ref, mask_ref, part_ref, o_ref, pot_ref,
 ):
     nodes = dpack_ref.shape[0] // 2
     scale = TIME_STEP * INTERACTION
@@ -496,10 +480,10 @@
     @pl.when(which == 0)
     def _():
         pot_ref[...] = local_ref[...]
-        for side, got in ((0, got_up_ref), (1, got_lo_ref)):
+        for side, inv, got in ((0, inv_up_ref, got_up_ref), (1, inv_lo_ref, got_lo_ref)):
             face = face_of(pot_ref, side)
-            partner = scatter_faces(side, got[0], scatter_ref, mask_ref)
-            face[...] = face[...] + PENALTY * face_of(inverse_ref, side)[...] * partner
+            partner = PENALTY * inv[0] * got[0]
+            face[...] = face[...] + scatter_faces(side, partner, scatter_ref, mask_ref)
         first = pos_ref[0] * (block * pl.num_programs(0)) + pl.program_id(0) * block
         for c in range(block):
             wave = (4.0 / PLANES) * ((first + c) // 2).astype(F32)
@@ -517,12 +501,13 @@
             store_own(o_ref, me, own_order(part_ref, me, 0, c) - factor * slope, 0, c)
 
 
-def add_force(position, local, inverse, got, geometry, dpack, scatter, mask, partial):
+def add_force(position, local, own_inv, got, geometry, dpack, scatter, mask, partial):
     _, coefs, nodes, elements = partial.shape
     shared = scatter.shape[1]
     block = coef_block(coefs)
     flat = pl.BlockSpec((block * nodes, elements), lambda i, j: (i, 0))
     one = pl.BlockSpec((1, block, shared), lambda i, j: (0, i, 0))
+    third = pl.BlockSpec((1, block, shared), lambda i, j: (2, i, 0))
     comp = pl.BlockSpec((1, block, nodes, elements), lambda i, j: (2 * j, i, 0, 0))
     size = coefs * nodes * elements
     return pl.pallas_call(
@@ -530,39 +515,31 @@
         out_shape=jax.ShapeDtypeStruct(partial.shape, F32),
         grid=(coefs // block, 2),
         in_specs=[
-            SMEM_SPEC, flat, flat, one, one, whole(geometry.shape), whole(dpack.shape),
+            SMEM_SPEC, flat, third, third, one, one, whole(geometry.shape), whole(dpack.shape),
             whole(scatter.shape), whole(mask.shape), comp,
         ],
         out_specs=comp,
         scratch_shapes=[pltpu.VMEM((block * nodes, elements), F32)],
-        input_output_aliases={9: 0},
+        input_output_aliases={10: 0},
         compiler_params=params(),
         cost_estimate=cost(6 * nodes * size, 24 * size),
         name="add_force",
-    )(position, local, inverse, *got, geometry, dpack, scatter, mask, partial)
+    )(position, local, *own_inv, *got, geometry, dpack, scatter, mask, partial)
 
 
 def finish_kernel(block, count, pos_ref, coef_ref, dpack_ref, part_ref, *refs):
-    y_refs, o_ref = refs[:count], refs[count]
+    y_refs, o_ref = [ref.at[0] for ref in refs[:count]], refs[count]
     nodes = coef_ref.shape[1]
-    which = pl.program_id(1)
     me = pos_ref[1]
-
-    @pl.when(which == 0)
-    def _():
-        for c in range(block):
-            y = slab([ref.at[0] for ref in y_refs], c)
-            store_own(o_ref, me, own_order(part_ref, me, 0, c) + TIME_STEP * (y * coef_ref[DXBY]), 0, c)
-
-    @pl.when(which == 1)
-    def _():
-        dpack = dpack_ref[...]
-        for c in range(block):
-            y = slab([ref.at[0] for ref in y_refs], c)
-            slopes = dot(dpack, pack_field(y))
-            moved = coef_ref[BXR] * slopes[:nodes] + coef_ref[BYS] * slopes[nodes:]
-            change = y + TIME_STEP * (y * coef_ref[DYBY] - moved)
-            store_own(o_ref, me, own_order(part_ref, me, 0, c) + change, 0, c)
+    dpack = dpack_ref[...]
+    for c in range(block):
+        y = slab(y_refs, c)
+        slopes = dot(dpack, pack_field(y))
+        moved = coef_ref[BXR] * slopes[:nodes] + coef_ref[BYS] * slopes[nodes:]
+        change = y + TIME_STEP * (y * coef_ref[DYBY] - moved)
+        store_own(o_ref, me, own_order(part_ref, me, 1, c) + change, 1, c)
+        change = TIME_STEP * (y * coef_ref[DXBY])
+        store_own(o_ref, me, own_order(part_ref, me, 0, c) + change, 0, c)
 
 
 def finish(position, y, coef, dpack, partial):
@@ -571,16 +548,16 @@
     block = coef_block(coefs)
 
     def source(d):
-        return pl.BlockSpec((1, block, part, elements), lambda i, j, pos: (pos[1] ^ d, i, 0, 0))
-
-    comp = pl.BlockSpec((1, block, nodes, elements), lambda i, j, pos: (j, i, 0, 0))
+        return pl.BlockSpec((1, block, part, elements), lambda i, pos: (pos[1] ^ d, i, 0, 0))
+
+    comp = pl.BlockSpec((2, block, nodes, elements), lambda i, pos: (0, i, 0, 0))
     size = coefs * nodes * elements
     return pl.pallas_call(
         functools.partial(finish_kernel, block, lines),
         out_shape=jax.ShapeDtypeStruct(partial.shape, F32),
         grid_spec=pltpu.PrefetchScalarGridSpec(
             num_scalar_prefetch=1,
-            grid=(coefs // block, 2),
+            grid=(coefs // block,),
             in_specs=[whole(coef.shape), whole(dpack.shape), comp] + [source(d) for d in range(lines)],
             out_specs=comp,
         ),
@@ -600,6 +577,13 @@
     up_way = [(i, (i + 1) % peers) for i in range(peers)]
     down_way = [(j, i) for i, j in up_way]
     return lax.ppermute(lo, "dom", down_way), lax.ppermute(up, "dom", up_way)
+
+
+def tie(blocks, value):
+    blocks = list(blocks)
+    first = min(2, len(blocks) - 1)
+    blocks[first], value = lax.optimization_barrier((blocks[first], value))
+    return blocks, value
 
 
 def per_device(
@@ -633,61 +617,65 @@
     def columns(comp):
         if direct:
             return pack(position, adjoint, comp, peers)
-        return [pack_joined(adjoint, comp, peers)]
+        return [jnp.moveaxis(adjoint[comp].reshape(per, peers, nodes // peers, elements), 1, 0)]
 
     def spread(blocks):
         if direct:
             return exchange(blocks)
-        got = [to_all(blocks[0])]
+        got = [to_all(blocks[0]).reshape(PLANES, nodes // peers, elements)]
         return lambda: got
+
+    def by_line(joined):
+        if direct:
+            return to_all(joined)
+        got = to_all(joined.reshape(peers, per, nodes // peers, elements))
+        got = jnp.moveaxis(got, 0, 1).reshape(per, lines, LINE, elements)
+        return jnp.moveaxis(got, 1, 0)
 
     def collect(blocks):
         if direct:
             return exchange(blocks)
-        got = by_line(to_all(blocks[0]))
+        got = by_line(blocks[0])
         return lambda: [got[d] for d in range(lines)]
-
-    def by_line(got):
-        if peers == lines:
-            return got
-        got = jnp.moveaxis(got, 0, 1).reshape(per, lines, LINE, elements)
-        return jnp.moveaxis(got, 1, 0)
 
     z_blocks = columns(2)
     z_columns = spread(z_blocks)
     x_blocks = columns(0)
+    x_blocks, table = tie(x_blocks, table)
     x_columns = spread(x_blocks)
     constants = prepare(
         position, base_bank, snapshot, geometry, diff_r, diff_s, stiffness, upper_list, lower_list
     )
-    y_sent = pack_joined(adjoint, 1, peers)
-    z_got, constants, y_sent, table = lax.optimization_barrier((z_columns(), constants, y_sent, table))
+    z_coefs = transform(position, z_columns(), table)
+    z_coefs, constants = tie(z_coefs, constants)
     coef, dpack, spack, gather, scatter, mask = constants
-    z_coefs = transform(z_got, table)
     z_later = collect(z_coefs)
-    x_coefs = transform(x_columns(), table)
+    y_blocks = columns(1)
+    x_coefs = transform(position, x_columns(), table)
+    x_coefs, y_blocks = tie(x_coefs, y_blocks)
     x_later = collect(x_coefs)
+    y_columns = spread(y_blocks)
     z = z_later()
     x = x_later()
-    x[2], y_sent = lax.optimization_barrier((x[2], y_sent))
-    y_columns = to_all(y_sent)
     source, inverse, local, up, lo = start_solve(
         position, z, x, geometry, coef, dpack, spack, gather, mask
     )
+    own_inv = (up, lo)
     got = swap_faces(up, lo)
     inv = got
     partial = partial_update(position, z, x, coef, dpack)
     local, up, lo = two_sweeps(
-        2, local, source, inverse, (up, lo), got, inv, spack, gather, scatter, mask
+        2, local, source, inverse, (up, lo), own_inv, got, inv, spack, gather, scatter, mask
     )
-    y_columns, local = lax.optimization_barrier((y_columns, local))
+    y_got = y_columns()
+    y_got[0], local = lax.optimization_barrier((y_got[0], local))
     got = swap_faces(up, lo)
-    y = by_line(to_all(transform([y_columns], natural)[0]))
+    y = by_line(transform(position, y_got, table, join=True))
     local, up, lo = two_sweeps(
-        1, local, source, inverse, (up, lo), got, inv, spack, gather, scatter, mask
+        1, local, source, inverse, (up, lo), own_inv, got, inv, spack, gather, scatter, mask
     )
     got = swap_faces(up, lo)
-    partial = add_force(position, local, inverse, got, geometry, dpack, scatter, mask, partial)
+    partial = add_force(position, local, own_inv, got, geometry, dpack, scatter, mask, partial)
     return finish(position, y, coef, dpack, partial)
 
 

time: 236 us -> 190 us (0.81)
  waiting for transfers between devices: 102 us -> 71.1 us
  local copies, waits for them, and re-layouts: 26.5 us -> 15.6 us
  Pallas kernels: 56.6 us -> 48 us
  starting transfers between devices: 48.4 us -> 54.1 us
    ppermute x28 -> x35, waiting for transfers between devices: 84.3 us -> 56.9 us  [exchange(): lax.ppermute(block, 'four', [(i, i ^ d) for i in range(peers)])]
    unnamed x156 -> x138, local copies, waits for them, and re-layouts: 26.5 us -> 15.6 us
    ppermute x28 -> x35, starting transfers between devices: 33.1 us -> 40.8 us  [exchange(): lax.ppermute(block, 'four', [(i, i ^ d) for i in range(peers)])]
    ppermute x6, waiting for transfers between devices: 17.9 us -> 14.2 us  [swap_faces(): return (lax.ppermute(lo, 'dom', down_way), lax.ppermute(up, 'dom', up_way))]
    all_to_all x2 -> x1, starting transfers between devices: 7.2 us -> 3.6 us  [to_all(): lax.all_to_all(blocks, 'four', split_axis=0, concat_axis=0, tiled=True)]
    pallas_call x2, Pallas kernels: 13.7 us -> 10.7 us  [two_sweeps(): pl.pallas_call(functools.partial(sweeps_kernel, block, keep), out_shape=[...]
    pallas_call x4 -> x3, Pallas kernels: 9.83 us -> 8.67 us  [transform(): pl.pallas_call(functools.partial(transform_kernel, count), out_shape=out_...]
  transfers between devices with their start and end apart: 36 -> 42, of which waited for: 19 -> 23; matrix products, arithmetic and copies ran while one was open for 0% -> 0% of each run, Pallas kernels for 19% -> 20%
where the time goes in v5:
time: 190 us
  waiting for transfers between devices  71.1 us (37%)
  starting transfers between devices  54.1 us (28%)
  Pallas kernels  48 us (25%)
  local copies, waits for them, and re-layouts  15.6 us (8%)
    ppermute x35, waiting for transfers between devices, exchange(): lax.ppermute(block, 'four', [(i, i ^ d) for i in range(peers)])  56.9 us
    ppermute x35, starting transfers between devices, exchange(): lax.ppermute(block, 'four', [(i, i ^ d) for i in range(peers)])  40.8 us
    unnamed x138, local copies, waits for them, and re-layouts  15.6 us
    ppermute x6, waiting for transfers between devices, swap_faces(): return (lax.ppermute(lo, 'dom', down_way), lax.ppermute(up, 'dom', up_way))  14.2 us
    pallas_call x2, Pallas kernels, two_sweeps(): pl.pallas_call(functools.partial(sweeps_kernel, block, keep), out_shape=[...  10.7 us
    ppermute x6, starting transfers between devices, swap_faces(): return (lax.ppermute(lo, 'dom', down_way), lax.ppermute(up, 'dom', up_way))  9.63 us
    pallas_call x3, Pallas kernels, transform(): pl.pallas_call(functools.partial(transform_kernel, count), out_shape=out_...  8.67 us
    pallas_call x1, Pallas kernels, add_force(): pl.pallas_call(functools.partial(force_kernel, block), out_shape=jax.Shap...  7.81 us
  transfers between devices with their start and end apart: 42, of which 23 were waited for; matrix products, arithmetic and copies ran while one was open for 0% of the time, Pallas kernels for 20%

profile of v5, /device:TPU:0, one launch (start us, length us, event | category | flops | bytes accessed | tf_op | source)
XLA Modules:
  0.0 189.6 jit_solution(17877826569834303277)
XLA Ops:
  0.1 2.8 %copy-done = f32[3,32,64,256]{3,2,1,0:T(8,128)S(1)} copy-done((f32[3,32,64,256]{3,2,1,0:T(8,128)S(1)}, f32[3,32,64,256]{3,2,1,0:T(8,128)}, u32[]{:S(2)}) %copy-start) | copy-done | bytes 6291480
  3.9 3.0 %collective-permute-start.2 = (f32[32,8,256]{2,1,0:T(8,128)S(1)}, f32[32,8,256]{2,1,0:T(8,128)S(1)}, u32[]{:S(2)}, u32[]{:S(2)}) collective-permute-start(f32[32,8,256]{2,1,0:T(8,128)S(1)} %get-tuple-element.151), channel_id=1, source_target_pairs={{0,2},{1,3},{2,0},{3,1},{4,6},{5,7},{6,4},{7,5},{8,10},{9,11},{10,... | collective-permute-start | bytes 786440 | tf_op jit(solution)/shard_map/ppermute | solution.py:609
  6.9 1.5 collective-permute-start.5
  9.1 2.7 %collective-permute-start.4 = (f32[32,8,256]{2,1,0:T(8,128)S(1)}, f32[32,8,256]{2,1,0:T(8,128)S(1)}, u32[]{:S(2)}, u32[]{:S(2)}) collective-permute-start(f32[32,8,256]{2,1,0:T(8,128)S(1)} %get-tuple-element.158), channel_id=1, source_target_pairs={{0,5},{1,4},{2,7},{3,6},{4,1},{5,0},{6,3},{7,2},{8,13},{9,12},{10,... | collective-permute-start | bytes 786440 | tf_op jit(solution)/shard_map/ppermute | solution.py:609
  14.5 6.8 %collective-permute-done.5.refs_6_ = f32[32,8,256]{2,1,0:T(8,128)S(1)} collective-permute-done((f32[32,8,256]{2,1,0:T(8,128)S(1)}, f32[32,8,256]{2,1,0:T(8,128)S(1)}, u32[]{:S(2)}, u32[]{:S(2)}) %collective-permute-start.5) | collective-permute-done | bytes 262176 | tf_op jit(solution)/shard_map/ppermute | solution.py:609
  21.3 1.5 collective-permute-start.9
  23.3 1.6 collective-permute-done.3.refs_3_
  24.9 1.5 collective-permute-start.7
  26.4 5.5 %collective-permute-done.4.refs_5_ = f32[32,8,256]{2,1,0:T(8,128)S(1)} collective-permute-done((f32[32,8,256]{2,1,0:T(8,128)S(1)}, f32[32,8,256]{2,1,0:T(8,128)S(1)}, u32[]{:S(2)}, u32[]{:S(2)}) %collective-permute-start.4) | collective-permute-done | bytes 262176 | tf_op jit(solution)/shard_map/ppermute | solution.py:609
  31.9 2.6 %collective-permute-start.12 = (f32[32,8,256]{2,1,0:T(8,128)S(1)}, f32[32,8,256]{2,1,0:T(8,128)S(1)}, u32[]{:S(2)}, u32[]{:S(2)}) collective-permute-start(f32[32,8,256]{2,1,0:T(8,128)S(1)} %get-tuple-element.192), channel_id=1, source_target_pairs={{0,6},{1,7},{2,4},{3,5},{4,2},{5,3},{6,0},{7,1},{8,14},{9,15},{10,... | collective-permute-start | bytes 786440 | tf_op jit(solution)/shard_map/ppermute | solution.py:609
  37.1 1.7 collective-permute-start.11
  40.0 2.9 %transform.3 = (f32[32,8,256]{2,1,0:T(8,128)S(1)}, f32[32,8,256]{2,1,0:T(8,128)S(1)}, f32[32,8,256]{2,1,0:T(8,128)S(1)}, f32[32,8,256]{2,1,0:T(8,128)S(1)}, f32[...) custom-call(s32[2]{0:T(128)S(1)} %pad_add_fusion.pos_ref, ...), custom_call_target="tpu_custom_call" | custom-call | flops 805306368 | bytes 4194304 | tf_op jit(solution)/shard_map/transform/pallas_call | solution.py:127
  42.9 2.3 %collective-permute-done.7.refs_4_ = f32[32,8,256]{2,1,0:T(8,128)S(1)} collective-permute-done((f32[32,8,256]{2,1,0:T(8,128)S(1)}, f32[32,8,256]{2,1,0:T(8,128)S(1)}, u32[]{:S(2)}, u32[]{:S(2)}) %collective-permute-start.7) | collective-permute-done | bytes 262176 | tf_op jit(solution)/shard_map/ppermute | solution.py:609
  45.3 1.5 collective-permute-start.16
  47.8 1.7 collective-permute-start.14
  49.5 5.1 %collective-permute-done.13.refs_7_ = f32[32,8,256]{2,1,0:T(8,128)S(1)} collective-permute-done((f32[32,8,256]{2,1,0:T(8,128)S(1)}, f32[32,8,256]{2,1,0:T(8,128)S(1)}, u32[]{:S(2)}, u32[]{:S(2)}) %collective-permute-start.13) | collective-permute-done | bytes 262176 | tf_op jit(solution)/shard_map/ppermute | solution.py:609
  54.6 2.2 %collective-permute-start.19 = (f32[32,8,256]{2,1,0:T(8,128)S(1)}, f32[32,8,256]{2,1,0:T(8,128)S(1)}, u32[]{:S(2)}, u32[]{:S(2)}) collective-permute-start(f32[32,8,256]{2,1,0:T(8,128)S(1)} %get-tuple-element.227), channel_id=1, source_target_pairs={{0,6},{1,7},{2,4},{3,5},{4,2},{5,3},{6,0},{7,1},{8,14},{9,15},{10,... | collective-permute-start | bytes 786440 | tf_op jit(solution)/shard_map/ppermute | solution.py:609
  59.1 1.4 collective-permute-start.18
  61.7 2.9 %transform.4 = (f32[32,8,256]{2,1,0:T(8,128)S(1)}, f32[32,8,256]{2,1,0:T(8,128)S(1)}, f32[32,8,256]{2,1,0:T(8,128)S(1)}, f32[32,8,256]{2,1,0:T(8,128)S(1)}, f32[...) custom-call(s32[2]{0:T(128)S(1)} %pad_add_fusion.pos_ref, ...), custom_call_target="tpu_custom_call" | custom-call | flops 805306368 | bytes 4194304 | tf_op jit(solution)/shard_map/transform/pallas_call | solution.py:127
  65.0 1.6 collective-permute-start.21
  66.6 3.6 %collective-permute-done.19.refs_6_ = f32[32,8,256]{2,1,0:T(8,128)S(1)} collective-permute-done((f32[32,8,256]{2,1,0:T(8,128)S(1)}, f32[32,8,256]{2,1,0:T(8,128)S(1)}, u32[]{:S(2)}, u32[]{:S(2)}) %collective-permute-start.19) | collective-permute-done | bytes 262176 | tf_op jit(solution)/shard_map/ppermute | solution.py:609
  70.2 1.5 collective-permute-start.23
  71.7 5.4 %collective-permute-done.20.refs_7_ = f32[32,8,256]{2,1,0:T(8,128)S(1)} collective-permute-done((f32[32,8,256]{2,1,0:T(8,128)S(1)}, f32[32,8,256]{2,1,0:T(8,128)S(1)}, u32[]{:S(2)}, u32[]{:S(2)}) %collective-permute-start.20) | collective-permute-done | bytes 262176 | tf_op jit(solution)/shard_map/ppermute | solution.py:609
  77.2 1.5 collective-permute-done.18.refs_5_
  79.8 4.8 %collective-permute-done.21.refs_12_ = f32[32,8,256]{2,1,0:T(8,128)S(1)} collective-permute-done((f32[32,8,256]{2,1,0:T(8,128)S(1)}, f32[32,8,256]{2,1,0:T(8,128)S(1)}, u32[]{:S(2)}, u32[]{:S(2)}) %collective-permute-start.21) | collective-permute-done | bytes 262176 | tf_op jit(solution)/shard_map/ppermute | solution.py:609
  85.0 2.1 %collective-permute-start.27 = (f32[32,8,256]{2,1,0:T(8,128)S(1)}, f32[32,8,256]{2,1,0:T(8,128)S(1)}, u32[]{:S(2)}, u32[]{:S(2)}) collective-permute-start(f32[32,8,256]{2,1,0:T(8,128)S(1)} %get-tuple-element.252), channel_id=1, source_target_pairs={{0,7},{1,6},{2,5},{3,4},{4,3},{5,2},{6,1},{7,0},{8,15},{9,14},{10,... | collective-permute-start | bytes 786440 | tf_op jit(solution)/shard_map/ppermute | solution.py:609
  87.3 1.7 collective-permute-start.34
  88.9 3.8 %collective-permute-done.26.refs_14_ = f32[32,8,256]{2,1,0:T(8,128)S(1)} collective-permute-done((f32[32,8,256]{2,1,0:T(8,128)S(1)}, f32[32,8,256]{2,1,0:T(8,128)S(1)}, u32[]{:S(2)}, u32[]{:S(2)}) %collective-permute-start.26) | collective-permute-done | bytes 262176 | tf_op jit(solution)/shard_map/ppermute | solution.py:609
  92.7 1.5 collective-permute-start.36
  94.2 9.6 %collective-permute-done.25.refs_13_ = f32[32,8,256]{2,1,0:T(8,128)S(1)} collective-permute-done((f32[32,8,256]{2,1,0:T(8,128)S(1)}, f32[32,8,256]{2,1,0:T(8,128)S(1)}, u32[]{:S(2)}, u32[]{:S(2)}) %collective-permute-start.25) | collective-permute-done | bytes 262176 | tf_op jit(solution)/shard_map/ppermute | solution.py:609
  103.8 4.5 %start_solve.1 = (f32[2048,256]{1,0:T(8,128)S(1)}, f32[2048,256]{1,0:T(8,128)S(1)}, f32[2048,256]{1,0:T(8,128)S(1)}, f32[3,32,512]{2,1,0:T(8,128)S(1)}, f32[3,32,512]{2,1,0:T(8,128)S(1)}) custom-call(s32[2]{0:T(128)S(1)} %pad_add_fusion.pos_ref, f32[2,256]{1,0:T(2,128)S(1)} %copy-done.63, f32[7,64,256]{2,1,0:T(8,128)S(1)} %get-tuple-element.173.diag_ref.coef_ref, ...), custom_call_target="tpu_custom_call" | custom-call | flops 402653184 | bytes 10485760 | tf_op jit(solution)/shard_map/start_solve/pallas_call | solution.py:345
  108.6 3.6 %collective-permute-start.28 = (f32[3,32,512]{2,1,0:T(8,128)S(1)}, f32[3,32,512]{2,1,0:T(8,128)S(1)}, u32[]{:S(2)}, u32[]{:S(2)}) collective-permute-start(f32[3,32,512]{2,1,0:T(8,128)S(1)} %get-tuple-element.258.own_lo_ref.own_inv_lo_ref.inv_lo_ref), channel_id=1, source_target_pairs={{8,0},{16,8},{24,16},{0,24},{9,1},{17,9},{25,17},{1,25},{10,2},{18... | collective-permute-start | bytes 589832 | tf_op jit(solution)/shard_map/ppermute | solution.py:579
  114.6 2.8 %collective-permute-done.28.got_up_ref.inv_up_ref = f32[3,32,512]{2,1,0:T(8,128)S(1)} collective-permute-done((f32[3,32,512]{2,1,0:T(8,128)S(1)}, f32[3,32,512]{2,1,0:T(8,128)S(1)}, u32[]{:S(2)}, u32[]{:S(2)}) %collective-permute-start.28) | collective-permute-done | bytes 196640 | tf_op jit(solution)/shard_map/ppermute | solution.py:579
  118.6 3.5 %collective-permute-done.29.got_lo_ref.inv_lo_ref = f32[3,32,512]{2,1,0:T(8,128)S(1)} collective-permute-done((f32[3,32,512]{2,1,0:T(8,128)S(1)}, f32[3,32,512]{2,1,0:T(8,128)S(1)}, u32[]{:S(2)}, u32[]{:S(2)}) %collective-permute-start.29) | collective-permute-done | bytes 196640 | tf_op jit(solution)/shard_map/ppermute | solution.py:579
  123.5 5.1 %two_sweeps.2 = (f32[2048,256]{1,0:T(8,128)S(1)}, f32[2,32,512]{2,1,0:T(8,128)S(1)}, f32[2,32,512]{2,1,0:T(8,128)S(1)}) custom-call(f32[2048,256]{1,0:T(8,128)S(1)} %get-tuple-element.254.local_ref, f32[2048,256]{1,0:T(8,128)S(1)} %get-tuple-element.255.source_ref, f32[2048,256]{1,0:T(8,128)S(1)} %get-tuple-element.256.inverse_ref, ...), custom_call_target="tpu_custom_call" | custom-call | flops 402653184 | bytes 8388608 | tf_op jit(solution)/shard_map/two_sweeps/pallas_call | solution.py:414
  130.0 3.3 %collective-permute-done.38.refs_5_ = f32[32,8,256]{2,1,0:T(8,128)S(1)} collective-permute-done((f32[32,8,256]{2,1,0:T(8,128)S(1)}, f32[32,8,256]{2,1,0:T(8,128)S(1)}, u32[]{:S(2)}, u32[]{:S(2)}) %collective-permute-start.38) | collective-permute-done | bytes 262176 | tf_op jit(solution)/shard_map/ppermute | solution.py:609
  133.3 2.9 %transform.5 = f32[8,32,8,256]{3,2,1,0:T(8,128)S(1)} custom-call(s32[2]{0:T(128)S(1)} %pad_add_fusion.pos_ref, bf16[512,256]{1,0:T(8,128)(2,1)S(1)} %permuted_table.1.table_ref, f32[32,8,256]{2,1,0:T(8,128)S(1)} %get-tuple-element.267.refs_0_, f32[32,8,256]{2,1,0:T(8,128)S(1)} %collective-permute-done.35.refs_1_, ...), custom_call_target="tpu_custom_call" | custom-call | flops 805306368 | bytes 4194304 | tf_op jit(solution)/shard_map/transform/pallas_call | solution.py:127
  137.5 3.6 %all-to-all-start = ((f32[8,32,8,256]{3,2,1,0:T(8,128)}), f32[8,32,8,256]{3,2,1,0:T(8,128)S(1)}, u32[]{:S(2)}, u32[]{:S(2)}) async-start(f32[8,32,8,256]{3,2,1,0:T(8,128)} %copy-done.5), calls=%async_computation | async-start | bytes 4194304 | tf_op jit(solution)/shard_map/all_to_all | solution.py:572
  141.1 3.9 %collective-permute-start.30 = (f32[2,32,512]{2,1,0:T(8,128)}, f32[2,32,512]{2,1,0:T(8,128)S(1)}, u32[]{:S(2)}, u32[]{:S(2)}) collective-permute-start(f32[2,32,512]{2,1,0:T(8,128)} %copy-done.58), channel_id=1, source_target_pairs={{8,0},{16,8},{24,16},{0,24},{9,1},{17,9},{25,17},{1,25},{10,2},{18... | collective-permute-start | bytes 393224 | tf_op jit(solution)/shard_map/ppermute | solution.py:579
  145.1 4.1 %collective-permute-done.30.got_up_ref = f32[2,32,512]{2,1,0:T(8,128)S(1)} collective-permute-done((f32[2,32,512]{2,1,0:T(8,128)}, f32[2,32,512]{2,1,0:T(8,128)S(1)}, u32[]{:S(2)}, u32[]{:S(2)}) %collective-permute-start.30) | collective-permute-done | bytes 131104 | tf_op jit(solution)/shard_map/ppermute | solution.py:579
  149.2 3.3 %collective-permute-done.31.got_lo_ref = f32[2,32,512]{2,1,0:T(8,128)S(1)} collective-permute-done((f32[2,32,512]{2,1,0:T(8,128)}, f32[2,32,512]{2,1,0:T(8,128)S(1)}, u32[]{:S(2)}, u32[]{:S(2)}) %collective-permute-start.31) | collective-permute-done | bytes 131104 | tf_op jit(solution)/shard_map/ppermute | solution.py:579
  152.6 1.6 copy-done.2
  154.1 1.6 copy-done.4
  155.7 1.6 copy-done.10
  162.7 5.6 %two_sweeps.3 = (f32[2048,256]{1,0:T(8,128)S(1)}, f32[1,32,512]{2,1,0:T(8,128)S(1)}, f32[1,32,512]{2,1,0:T(8,128)S(1)}) custom-call(f32[2048,256]{1,0:T(8,128)S(1)} %copy-done.10, f32[2048,256]{1,0:T(8,128)S(1)} %copy-done.2, f32[2048,256]{1,0:T(8,128)S(1)} %copy-done.4, f32[2,32,512]{2,1,0:T(8,128)S(1)} %copy-done.57, f32[2,32,512]{2,1,0:T(8,128)S(1)} %copy-done.59, ...), custom_call_target="tpu_custom_call" | custom-call | flops 402653184 | bytes 8388608 | tf_op jit(solution)/shard_map/two_sweeps/pallas_call | solution.py:414
  170.5 4.8 %partial_update.1.part_ref = f32[3,32,64,256]{3,2,1,0:T(8,128)} custom-call(s32[2]{0:T(128)S(1)} %pad_add_fusion.pos_ref, f32[7,64,256]{2,1,0:T(8,128)S(1)} %copy-done.7, bf16[128,192]{1,0:T(8,128)(2,1)S(1)} %copy-done.16, f32[32,8,256]{2,1,0:T(8,128)S(1)} %copy-done.19, f32[32,8,256]{2,1,0:T(8,128)S(1)} %copy-done.35, f32[32,8,256]{2,1,0:T(8,128)S(1)} %copy-done.21, ...), custom_call_target="tpu_custom_call" | custom-call | flops 805306368 | bytes 10485760 | tf_op jit(solution)/shard_map/partial_update/pallas_call | solution.py:459
  175.7 7.8 %add_force.1.part_ref = f32[3,32,64,256]{3,2,1,0:T(8,128)} custom-call(s32[2]{0:T(128)S(1)} %pad_add_fusion.pos_ref, f32[2048,256]{1,0:T(8,128)S(1)} %get-tuple-element.264.local_ref, f32[3,32,512]{2,1,0:T(8,128)S(1)} %get-tuple-element.257.own_up_ref.own_inv_up_ref.inv_up_ref, ...), custom_call_target="tpu_custom_call", output_to_operand_aliasing={{}: (10, {})} | custom-call | flops 201326592 | bytes 12582912 | tf_op jit(solution)/shard_map/add_force/pallas_call | solution.py:513
  183.5 6.1 %finish.1 = f32[3,32,64,256]{3,2,1,0:T(8,128)} custom-call(s32[2]{0:T(128)S(1)} %pad_add_fusion.pos_ref, f32[7,64,256]{2,1,0:T(8,128)S(1)} %copy-done.8, bf16[128,192]{1,0:T(8,128)(2,1)S(1)} %copy-done.17, f32[3,32,64,256]{3,2,1,0:T(8,128)} %add_force.1.part_ref, ...), custom_call_target="tpu_custom_call", output_to_operand_aliasing={{}: (3, {})} | custom-call | flops 402653184 | bytes 10485760 | tf_op jit(solution)/shard_map/finish/pallas_call | solution.py:555
  (190 shorter events, 30.7 us)
Async XLA Ops:
  3.9 10.1 %collective-permute-start.2 = (f32[32,8,256]{2,1,0:T(8,128)S(1)}, f32[32,8,256]{2,1,0:T(8,128)S(1)}, u32[]{:S(2)}, u32[]{:S(2)}) collective-permute-start(f32[32,8,256]{2,1,0:T(8,128)S(1)} %get-tuple-element.151), channel_id=1, source_target_pairs={{0,2},{1,3},{2,0},{3,1},{4,6},{5,7},{6,4},{7,5},{8,10},{9,11},{10,... | collective-permute-start | bytes 786440 | tf_op jit(solution)/shard_map/ppermute | solution.py:609
  6.9 14.3 %collective-permute-start.5 = (f32[32,8,256]{2,1,0:T(8,128)S(1)}, f32[32,8,256]{2,1,0:T(8,128)S(1)}, u32[]{:S(2)}, u32[]{:S(2)}) collective-permute-start(f32[32,8,256]{2,1,0:T(8,128)S(1)} %get-tuple-element.161), channel_id=1, source_target_pairs={{0,6},{1,7},{2,4},{3,5},{4,2},{5,3},{6,0},{7,1},{8,14},{9,15},{10,... | collective-permute-start | bytes 786440 | tf_op jit(solution)/shard_map/ppermute | solution.py:609
  8.4 14.9 %collective-permute-start = (f32[32,8,256]{2,1,0:T(8,128)S(1)}, f32[32,8,256]{2,1,0:T(8,128)S(1)}, u32[]{:S(2)}, u32[]{:S(2)}) collective-permute-start(f32[32,8,256]{2,1,0:T(8,128)S(1)} %get-tuple-element.147), channel_id=1, source_target_pairs={{0,4},{1,5},{2,6},{3,7},{4,0},{5,1},{6,2},{7,3},{8,12},{9,13},{10,... | collective-permute-start | bytes 786440 | tf_op jit(solution)/shard_map/ppermute | solution.py:609
  8.5 16.4 %collective-permute-start.3 = (f32[32,8,256]{2,1,0:T(8,128)S(1)}, f32[32,8,256]{2,1,0:T(8,128)S(1)}, u32[]{:S(2)}, u32[]{:S(2)}) collective-permute-start(f32[32,8,256]{2,1,0:T(8,128)S(1)} %get-tuple-element.154), channel_id=1, source_target_pairs={{0,3},{1,2},{2,1},{3,0},{4,7},{5,6},{6,5},{7,4},{8,11},{9,10},{10,... | collective-permute-start | bytes 786440 | tf_op jit(solution)/shard_map/ppermute | solution.py:609
  9.1 22.8 %collective-permute-start.4 = (f32[32,8,256]{2,1,0:T(8,128)S(1)}, f32[32,8,256]{2,1,0:T(8,128)S(1)}, u32[]{:S(2)}, u32[]{:S(2)}) collective-permute-start(f32[32,8,256]{2,1,0:T(8,128)S(1)} %get-tuple-element.158), channel_id=1, source_target_pairs={{0,5},{1,4},{2,7},{3,6},{4,1},{5,0},{6,3},{7,2},{8,13},{9,12},{10,... | collective-permute-start | bytes 786440 | tf_op jit(solution)/shard_map/ppermute | solution.py:609
  14.1 20.4 %collective-permute-start.6 = (f32[32,8,256]{2,1,0:T(8,128)S(1)}, f32[32,8,256]{2,1,0:T(8,128)S(1)}, u32[]{:S(2)}, u32[]{:S(2)}) collective-permute-start(f32[32,8,256]{2,1,0:T(8,128)S(1)} %get-tuple-element.164), channel_id=1, source_target_pairs={{0,7},{1,6},{2,5},{3,4},{4,3},{5,2},{6,1},{7,0},{8,15},{9,14},{10,... | collective-permute-start | bytes 786440 | tf_op jit(solution)/shard_map/ppermute | solution.py:609
  21.3 14.5 %collective-permute-start.9 = (f32[32,8,256]{2,1,0:T(8,128)S(1)}, f32[32,8,256]{2,1,0:T(8,128)S(1)}, u32[]{:S(2)}, u32[]{:S(2)}) collective-permute-start(f32[32,8,256]{2,1,0:T(8,128)S(1)} %get-tuple-element.182), channel_id=1, source_target_pairs={{0,2},{1,3},{2,0},{3,1},{4,6},{5,7},{6,4},{7,5},{8,10},{9,11},{10,... | collective-permute-start | bytes 786440 | tf_op jit(solution)/shard_map/ppermute | solution.py:609
  23.3 13.8 %collective-permute-start.1 = (f32[32,8,256]{2,1,0:T(8,128)S(1)}, f32[32,8,256]{2,1,0:T(8,128)S(1)}, u32[]{:S(2)}, u32[]{:S(2)}) collective-permute-start(f32[32,8,256]{2,1,0:T(8,128)S(1)} %get-tuple-element.148), channel_id=1, source_target_pairs={{0,1},{1,0},{2,3},{3,2},{4,5},{5,4},{6,7},{7,6},{8,9},{9,8},{10,11... | collective-permute-start | bytes 786440 | tf_op jit(solution)/shard_map/ppermute | solution.py:609
  24.9 20.3 %collective-permute-start.7 = (f32[32,8,256]{2,1,0:T(8,128)S(1)}, f32[32,8,256]{2,1,0:T(8,128)S(1)}, u32[]{:S(2)}, u32[]{:S(2)}) collective-permute-start(f32[32,8,256]{2,1,0:T(8,128)S(1)} %get-tuple-element.178), channel_id=1, source_target_pairs={{0,4},{1,5},{2,6},{3,7},{4,0},{5,1},{6,2},{7,3},{8,12},{9,13},{10,... | collective-permute-start | bytes 786440 | tf_op jit(solution)/shard_map/ppermute | solution.py:609
  31.9 13.3 %collective-permute-start.12 = (f32[32,8,256]{2,1,0:T(8,128)S(1)}, f32[32,8,256]{2,1,0:T(8,128)S(1)}, u32[]{:S(2)}, u32[]{:S(2)}) collective-permute-start(f32[32,8,256]{2,1,0:T(8,128)S(1)} %get-tuple-element.192), channel_id=1, source_target_pairs={{0,6},{1,7},{2,4},{3,5},{4,2},{5,3},{6,0},{7,1},{8,14},{9,15},{10,... | collective-permute-start | bytes 786440 | tf_op jit(solution)/shard_map/ppermute | solution.py:609
  34.5 13.4 %collective-permute-start.10 = (f32[32,8,256]{2,1,0:T(8,128)S(1)}, f32[32,8,256]{2,1,0:T(8,128)S(1)}, u32[]{:S(2)}, u32[]{:S(2)}) collective-permute-start(f32[32,8,256]{2,1,0:T(8,128)S(1)} %get-tuple-element.185), channel_id=1, source_target_pairs={{0,3},{1,2},{2,1},{3,0},{4,7},{5,6},{6,5},{7,4},{8,11},{9,10},{10,... | collective-permute-start | bytes 786440 | tf_op jit(solution)/shard_map/ppermute | solution.py:609
  35.8 18.8 %collective-permute-start.13 = (f32[32,8,256]{2,1,0:T(8,128)S(1)}, f32[32,8,256]{2,1,0:T(8,128)S(1)}, u32[]{:S(2)}, u32[]{:S(2)}) collective-permute-start(f32[32,8,256]{2,1,0:T(8,128)S(1)} %get-tuple-element.195), channel_id=1, source_target_pairs={{0,7},{1,6},{2,5},{3,4},{4,3},{5,2},{6,1},{7,0},{8,15},{9,14},{10,... | collective-permute-start | bytes 786440 | tf_op jit(solution)/shard_map/ppermute | solution.py:609
  37.1 17.6 %collective-permute-start.11 = (f32[32,8,256]{2,1,0:T(8,128)S(1)}, f32[32,8,256]{2,1,0:T(8,128)S(1)}, u32[]{:S(2)}, u32[]{:S(2)}) collective-permute-start(f32[32,8,256]{2,1,0:T(8,128)S(1)} %get-tuple-element.189), channel_id=1, source_target_pairs={{0,5},{1,4},{2,7},{3,6},{4,1},{5,0},{6,3},{7,2},{8,13},{9,12},{10,... | collective-permute-start | bytes 786440 | tf_op jit(solution)/shard_map/ppermute | solution.py:609
  40.0 63.8 %copy-start.6 = (f32[7,64,256]{2,1,0:T(8,128)}, f32[7,64,256]{2,1,0:T(8,128)S(1)}, u32[]{:S(2)}) copy-start(f32[7,64,256]{2,1,0:T(8,128)S(1)} %get-tuple-element.173.diag_ref.coef_ref) | copy-start | bytes 1376260
  40.0 63.8 %copy-start.15 = (bf16[128,192]{1,0:T(8,128)(2,1)}, bf16[128,192]{1,0:T(8,128)(2,1)S(1)}, u32[]{:S(2)}) copy-start(bf16[128,192]{1,0:T(8,128)(2,1)S(1)} %get-tuple-element.174.dpack_ref) | copy-start | bytes 147460
  40.0 83.5 %copy-start.50 = (f32[2,8,512]{2,1,0:T(8,128)}, f32[2,8,512]{2,1,0:T(8,128)S(1)}, u32[]{:S(2)}) copy-start(f32[2,8,512]{2,1,0:T(8,128)S(1)} %get-tuple-element.209.mask_ref) | copy-start | bytes 98308
  40.0 83.5 %copy-start.53 = (bf16[64,192]{1,0:T(8,128)(2,1)}, bf16[64,192]{1,0:T(8,128)(2,1)S(1)}, u32[]{:S(2)}) copy-start(bf16[64,192]{1,0:T(8,128)(2,1)S(1)} %get-tuple-element.207.spack_ref) | copy-start | bytes 73732
  42.9 60.9 %copy-start.18 = (f32[32,8,256]{2,1,0:T(8,128)}, f32[32,8,256]{2,1,0:T(8,128)S(1)}, u32[]{:S(2)}) copy-start(f32[32,8,256]{2,1,0:T(8,128)S(1)} %get-tuple-element.210.refs_0_) | copy-start | bytes 786436
  45.3 12.7 %collective-permute-start.8 = (f32[32,8,256]{2,1,0:T(8,128)S(1)}, f32[32,8,256]{2,1,0:T(8,128)S(1)}, u32[]{:S(2)}, u32[]{:S(2)}) collective-permute-start(f32[32,8,256]{2,1,0:T(8,128)S(1)} %get-tuple-element.179), channel_id=1, source_target_pairs={{0,1},{1,0},{2,3},{3,2},{4,5},{5,4},{6,7},{7,6},{8,9},{9,8},{10,11... | collective-permute-start | bytes 786440 | tf_op jit(solution)/shard_map/ppermute | solution.py:609
  45.3 13.9 %collective-permute-start.16 = (f32[32,8,256]{2,1,0:T(8,128)S(1)}, f32[32,8,256]{2,1,0:T(8,128)S(1)}, u32[]{:S(2)}, u32[]{:S(2)}) collective-permute-start(f32[32,8,256]{2,1,0:T(8,128)S(1)} %get-tuple-element.217), channel_id=1, source_target_pairs={{0,2},{1,3},{2,0},{3,1},{4,6},{5,7},{6,4},{7,5},{8,10},{9,11},{10,... | collective-permute-start | bytes 786440 | tf_op jit(solution)/shard_map/ppermute | solution.py:609
  47.8 16.7 %collective-permute-start.14 = (f32[32,8,256]{2,1,0:T(8,128)S(1)}, f32[32,8,256]{2,1,0:T(8,128)S(1)}, u32[]{:S(2)}, u32[]{:S(2)}) collective-permute-start(f32[32,8,256]{2,1,0:T(8,128)S(1)} %get-tuple-element.213), channel_id=1, source_target_pairs={{0,4},{1,5},{2,6},{3,7},{4,0},{5,1},{6,2},{7,3},{8,12},{9,13},{10,... | collective-permute-start | bytes 786440 | tf_op jit(solution)/shard_map/ppermute | solution.py:609
  54.6 10.4 %collective-permute-start.17 = (f32[32,8,256]{2,1,0:T(8,128)S(1)}, f32[32,8,256]{2,1,0:T(8,128)S(1)}, u32[]{:S(2)}, u32[]{:S(2)}) collective-permute-start(f32[32,8,256]{2,1,0:T(8,128)S(1)} %get-tuple-element.220), channel_id=1, source_target_pairs={{0,3},{1,2},{2,1},{3,0},{4,7},{5,6},{6,5},{7,4},{8,11},{9,10},{10,... | collective-permute-start | bytes 786440 | tf_op jit(solution)/shard_map/ppermute | solution.py:609
  54.6 15.6 %collective-permute-start.19 = (f32[32,8,256]{2,1,0:T(8,128)S(1)}, f32[32,8,256]{2,1,0:T(8,128)S(1)}, u32[]{:S(2)}, u32[]{:S(2)}) collective-permute-start(f32[32,8,256]{2,1,0:T(8,128)S(1)} %get-tuple-element.227), channel_id=1, source_target_pairs={{0,6},{1,7},{2,4},{3,5},{4,2},{5,3},{6,0},{7,1},{8,14},{9,15},{10,... | collective-permute-start | bytes 786440 | tf_op jit(solution)/shard_map/ppermute | solution.py:609
  59.1 49.3 %copy-start.20 = (f32[32,8,256]{2,1,0:T(8,128)}, f32[32,8,256]{2,1,0:T(8,128)S(1)}, u32[]{:S(2)}) copy-start(f32[32,8,256]{2,1,0:T(8,128)S(1)} %collective-permute-done.16.refs_2_) | copy-start | bytes 786436
  59.1 19.5 %collective-permute-start.18 = (f32[32,8,256]{2,1,0:T(8,128)S(1)}, f32[32,8,256]{2,1,0:T(8,128)S(1)}, u32[]{:S(2)}, u32[]{:S(2)}) collective-permute-start(f32[32,8,256]{2,1,0:T(8,128)S(1)} %get-tuple-element.224), channel_id=1, source_target_pairs={{0,5},{1,4},{2,7},{3,6},{4,1},{5,0},{6,3},{7,2},{8,13},{9,12},{10,... | collective-permute-start | bytes 786440 | tf_op jit(solution)/shard_map/ppermute | solution.py:609
  60.5 16.6 %collective-permute-start.20 = (f32[32,8,256]{2,1,0:T(8,128)S(1)}, f32[32,8,256]{2,1,0:T(8,128)S(1)}, u32[]{:S(2)}, u32[]{:S(2)}) collective-permute-start(f32[32,8,256]{2,1,0:T(8,128)S(1)} %get-tuple-element.230), channel_id=1, source_target_pairs={{0,7},{1,6},{2,5},{3,4},{4,3},{5,2},{6,1},{7,0},{8,15},{9,14},{10,... | collective-permute-start | bytes 786440 | tf_op jit(solution)/shard_map/ppermute | solution.py:609
  64.6 15.2 %collective-permute-start.15 = (f32[32,8,256]{2,1,0:T(8,128)S(1)}, f32[32,8,256]{2,1,0:T(8,128)S(1)}, u32[]{:S(2)}, u32[]{:S(2)}) collective-permute-start(f32[32,8,256]{2,1,0:T(8,128)S(1)} %get-tuple-element.214), channel_id=1, source_target_pairs={{0,1},{1,0},{2,3},{3,2},{4,5},{5,4},{6,7},{7,6},{8,9},{9,8},{10,11... | collective-permute-start | bytes 786440 | tf_op jit(solution)/shard_map/ppermute | solution.py:609
  65.0 19.6 %collective-permute-start.21 = (f32[32,8,256]{2,1,0:T(8,128)S(1)}, f32[32,8,256]{2,1,0:T(8,128)S(1)}, u32[]{:S(2)}, u32[]{:S(2)}) collective-permute-start(f32[32,8,256]{2,1,0:T(8,128)S(1)} %get-tuple-element.235), channel_id=1, source_target_pairs={{0,4},{1,5},{2,6},{3,7},{4,0},{5,1},{6,2},{7,3},{8,12},{9,13},{10,... | collective-permute-start | bytes 786440 | tf_op jit(solution)/shard_map/ppermute | solution.py:609
  70.2 14.8 %collective-permute-start.23 = (f32[32,8,256]{2,1,0:T(8,128)S(1)}, f32[32,8,256]{2,1,0:T(8,128)S(1)}, u32[]{:S(2)}, u32[]{:S(2)}) collective-permute-start(f32[32,8,256]{2,1,0:T(8,128)S(1)} %get-tuple-element.239), channel_id=1, source_target_pairs={{0,2},{1,3},{2,0},{3,1},{4,6},{5,7},{6,4},{7,5},{8,10},{9,11},{10,... | collective-permute-start | bytes 786440 | tf_op jit(solution)/shard_map/ppermute | solution.py:609
  77.1 10.1 %collective-permute-start.24 = (f32[32,8,256]{2,1,0:T(8,128)S(1)}, f32[32,8,256]{2,1,0:T(8,128)S(1)}, u32[]{:S(2)}, u32[]{:S(2)}) collective-permute-start(f32[32,8,256]{2,1,0:T(8,128)S(1)} %get-tuple-element.242), channel_id=1, source_target_pairs={{0,3},{1,2},{2,1},{3,0},{4,7},{5,6},{6,5},{7,4},{8,11},{9,10},{10,... | collective-permute-start | bytes 786440 | tf_op jit(solution)/shard_map/ppermute | solution.py:609
  78.7 14.1 %collective-permute-start.26 = (f32[32,8,256]{2,1,0:T(8,128)S(1)}, f32[32,8,256]{2,1,0:T(8,128)S(1)}, u32[]{:S(2)}, u32[]{:S(2)}) collective-permute-start(f32[32,8,256]{2,1,0:T(8,128)S(1)} %get-tuple-element.249), channel_id=1, source_target_pairs={{0,6},{1,7},{2,4},{3,5},{4,2},{5,3},{6,0},{7,1},{8,14},{9,15},{10,... | collective-permute-start | bytes 786440 | tf_op jit(solution)/shard_map/ppermute | solution.py:609
  84.6 9.6 %collective-permute-start.22 = (f32[32,8,256]{2,1,0:T(8,128)S(1)}, f32[32,8,256]{2,1,0:T(8,128)S(1)}, u32[]{:S(2)}, u32[]{:S(2)}) collective-permute-start(f32[32,8,256]{2,1,0:T(8,128)S(1)} %get-tuple-element.236), channel_id=1, source_target_pairs={{0,1},{1,0},{2,3},{3,2},{4,5},{5,4},{6,7},{7,6},{8,9},{9,8},{10,11... | collective-permute-start | bytes 786440 | tf_op jit(solution)/shard_map/ppermute | solution.py:609
  84.6 19.2 %collective-permute-start.25 = (f32[32,8,256]{2,1,0:T(8,128)S(1)}, f32[32,8,256]{2,1,0:T(8,128)S(1)}, u32[]{:S(2)}, u32[]{:S(2)}) collective-permute-start(f32[32,8,256]{2,1,0:T(8,128)S(1)} %get-tuple-element.246), channel_id=1, source_target_pairs={{0,5},{1,4},{2,7},{3,6},{4,1},{5,0},{6,3},{7,2},{8,13},{9,12},{10,... | collective-permute-start | bytes 786440 | tf_op jit(solution)/shard_map/ppermute | solution.py:609
  85.0 18.8 %collective-permute-start.27 = (f32[32,8,256]{2,1,0:T(8,128)S(1)}, f32[32,8,256]{2,1,0:T(8,128)S(1)}, u32[]{:S(2)}, u32[]{:S(2)}) collective-permute-start(f32[32,8,256]{2,1,0:T(8,128)S(1)} %get-tuple-element.252), channel_id=1, source_target_pairs={{0,7},{1,6},{2,5},{3,4},{4,3},{5,2},{6,1},{7,0},{8,15},{9,14},{10,... | collective-permute-start | bytes 786440 | tf_op jit(solution)/shard_map/ppermute | solution.py:609
  87.3 24.9 %collective-permute-start.34 = (f32[32,8,256]{2,1,0:T(8,128)S(1)}, f32[32,8,256]{2,1,0:T(8,128)S(1)}, u32[]{:S(2)}, u32[]{:S(2)}) collective-permute-start(f32[32,8,256]{2,1,0:T(8,128)S(1)} %get-tuple-element.269), channel_id=1, source_target_pairs={{0,4},{1,5},{2,6},{3,7},{4,0},{5,1},{6,2},{7,3},{8,12},{9,13},{10,... | collective-permute-start | bytes 786440 | tf_op jit(solution)/shard_map/ppermute | solution.py:609
  92.7 19.7 %collective-permute-start.36 = (f32[32,8,256]{2,1,0:T(8,128)S(1)}, f32[32,8,256]{2,1,0:T(8,128)S(1)}, u32[]{:S(2)}, u32[]{:S(2)}) collective-permute-start(f32[32,8,256]{2,1,0:T(8,128)S(1)} %get-tuple-element.272), channel_id=1, source_target_pairs={{0,2},{1,3},{2,0},{3,1},{4,6},{5,7},{6,4},{7,5},{8,10},{9,11},{10,... | collective-permute-start | bytes 786440 | tf_op jit(solution)/shard_map/ppermute | solution.py:609
  108.6 8.9 %collective-permute-start.28 = (f32[3,32,512]{2,1,0:T(8,128)S(1)}, f32[3,32,512]{2,1,0:T(8,128)S(1)}, u32[]{:S(2)}, u32[]{:S(2)}) collective-permute-start(f32[3,32,512]{2,1,0:T(8,128)S(1)} %get-tuple-element.258.own_lo_ref.own_inv_lo_ref.inv_lo_ref), channel_id=1, source_target_pairs={{8,0},{16,8},{24,16},{0,24},{9,1},{17,9},{25,17},{1,25},{10,2},{18... | collective-permute-start | bytes 589832 | tf_op jit(solution)/shard_map/ppermute | solution.py:579
  112.2 9.9 %collective-permute-start.29 = (f32[3,32,512]{2,1,0:T(8,128)S(1)}, f32[3,32,512]{2,1,0:T(8,128)S(1)}, u32[]{:S(2)}, u32[]{:S(2)}) collective-permute-start(f32[3,32,512]{2,1,0:T(8,128)S(1)} %get-tuple-element.257.own_up_ref.own_inv_up_ref.inv_up_ref), channel_id=1, source_target_pairs={{0,8},{8,16},{16,24},{24,0},{1,9},{9,17},{17,25},{25,1},{2,10},{10... | collective-permute-start | bytes 589832 | tf_op jit(solution)/shard_map/ppermute | solution.py:579
  112.2 17.8 %collective-permute-start.35 = (f32[32,8,256]{2,1,0:T(8,128)S(1)}, f32[32,8,256]{2,1,0:T(8,128)S(1)}, u32[]{:S(2)}, u32[]{:S(2)}) collective-permute-start(f32[32,8,256]{2,1,0:T(8,128)S(1)} %get-tuple-element.270), channel_id=1, source_target_pairs={{0,1},{1,0},{2,3},{3,2},{4,5},{5,4},{6,7},{7,6},{8,9},{9,8},{10,11... | collective-permute-start | bytes 786440 | tf_op jit(solution)/shard_map/ppermute | solution.py:609
  112.4 17.6 %collective-permute-start.37 = (f32[32,8,256]{2,1,0:T(8,128)S(1)}, f32[32,8,256]{2,1,0:T(8,128)S(1)}, u32[]{:S(2)}, u32[]{:S(2)}) collective-permute-start(f32[32,8,256]{2,1,0:T(8,128)S(1)} %get-tuple-element.274), channel_id=1, source_target_pairs={{0,3},{1,2},{2,1},{3,0},{4,7},{5,6},{6,5},{7,4},{8,11},{9,10},{10,... | collective-permute-start | bytes 786440 | tf_op jit(solution)/shard_map/ppermute | solution.py:609
  113.8 19.5 %collective-permute-start.38 = (f32[32,8,256]{2,1,0:T(8,128)S(1)}, f32[32,8,256]{2,1,0:T(8,128)S(1)}, u32[]{:S(2)}, u32[]{:S(2)}) collective-permute-start(f32[32,8,256]{2,1,0:T(8,128)S(1)} %get-tuple-element.276), channel_id=1, source_target_pairs={{0,5},{1,4},{2,7},{3,6},{4,1},{5,0},{6,3},{7,2},{8,13},{9,12},{10,... | collective-permute-start | bytes 786440 | tf_op jit(solution)/shard_map/ppermute | solution.py:609
  117.4 15.9 %collective-permute-start.39 = (f32[32,8,256]{2,1,0:T(8,128)S(1)}, f32[32,8,256]{2,1,0:T(8,128)S(1)}, u32[]{:S(2)}, u32[]{:S(2)}) collective-permute-start(f32[32,8,256]{2,1,0:T(8,128)S(1)} %get-tuple-element.277), channel_id=1, source_target_pairs={{0,6},{1,7},{2,4},{3,5},{4,2},{5,3},{6,0},{7,1},{8,14},{9,15},{10,... | collective-permute-start | bytes 786440 | tf_op jit(solution)/shard_map/ppermute | solution.py:609
  122.1 11.2 %collective-permute-start.40 = (f32[32,8,256]{2,1,0:T(8,128)S(1)}, f32[32,8,256]{2,1,0:T(8,128)S(1)}, u32[]{:S(2)}, u32[]{:S(2)}) collective-permute-start(f32[32,8,256]{2,1,0:T(8,128)S(1)} %get-tuple-element.278), channel_id=1, source_target_pairs={{0,7},{1,6},{2,5},{3,4},{4,3},{5,2},{6,1},{7,0},{8,15},{9,14},{10,... | collective-permute-start | bytes 786440 | tf_op jit(solution)/shard_map/ppermute | solution.py:609
  137.5 46.0 %all-to-all-start = ((f32[8,32,8,256]{3,2,1,0:T(8,128)}), f32[8,32,8,256]{3,2,1,0:T(8,128)S(1)}, u32[]{:S(2)}, u32[]{:S(2)}) async-start(f32[8,32,8,256]{3,2,1,0:T(8,128)} %copy-done.5), calls=%async_computation | async-start | bytes 4194304 | tf_op jit(solution)/shard_map/all_to_all | solution.py:572
  141.1 8.1 %collective-permute-start.30 = (f32[2,32,512]{2,1,0:T(8,128)}, f32[2,32,512]{2,1,0:T(8,128)S(1)}, u32[]{:S(2)}, u32[]{:S(2)}) collective-permute-start(f32[2,32,512]{2,1,0:T(8,128)} %copy-done.58), channel_id=1, source_target_pairs={{8,0},{16,8},{24,16},{0,24},{9,1},{17,9},{25,17},{1,25},{10,2},{18... | collective-permute-start | bytes 393224 | tf_op jit(solution)/shard_map/ppermute | solution.py:579
  145.1 7.5 %collective-permute-start.31 = (f32[2,32,512]{2,1,0:T(8,128)}, f32[2,32,512]{2,1,0:T(8,128)S(1)}, u32[]{:S(2)}, u32[]{:S(2)}) collective-permute-start(f32[2,32,512]{2,1,0:T(8,128)} %copy-done.56), channel_id=1, source_target_pairs={{0,8},{8,16},{16,24},{24,0},{1,9},{9,17},{17,25},{25,1},{2,10},{10... | collective-permute-start | bytes 393224 | tf_op jit(solution)/shard_map/ppermute | solution.py:579
  168.3 7.0 %collective-permute-start.32 = (f32[1,32,512]{2,1,0:T(8,128)S(1)}, f32[1,32,512]{2,1,0:T(8,128)S(1)}, u32[]{:S(2)}, u32[]{:S(2)}) collective-permute-start(f32[1,32,512]{2,1,0:T(8,128)S(1)} %get-tuple-element.265), channel_id=1, source_target_pairs={{8,0},{16,8},{24,16},{0,24},{9,1},{17,9},{25,17},{1,25},{10,2},{18... | collective-permute-start | bytes 196616 | tf_op jit(solution)/shard_map/ppermute | solution.py:579
  169.6 6.1 %collective-permute-start.33 = (f32[1,32,512]{2,1,0:T(8,128)S(1)}, f32[1,32,512]{2,1,0:T(8,128)S(1)}, u32[]{:S(2)}, u32[]{:S(2)}) collective-permute-start(f32[1,32,512]{2,1,0:T(8,128)S(1)} %get-tuple-element.266), channel_id=1, source_target_pairs={{0,8},{8,16},{16,24},{24,0},{1,9},{9,17},{17,25},{25,1},{2,10},{10... | collective-permute-start | bytes 196616 | tf_op jit(solution)/shard_map/ppermute | solution.py:579
  (63 other events, 941.1 us)

commit v6 on v5

--- a/solution.py
+++ b/solution.py
@@ -20,12 +20,16 @@
 
 F32 = jnp.float32
 BF16 = jnp.bfloat16
-VMEM_LIMIT = 24 * 1024 * 1024
+VMEM_LIMIT = 20 * 1024 * 1024
+LARGE_LIMIT = 56 * 1024 * 1024
 SMEM_SPEC = pl.BlockSpec(memory_space=pltpu.SMEM)
 
 
-def params():
-    return pltpu.CompilerParams(vmem_limit_bytes=VMEM_LIMIT)
+def params(limit=VMEM_LIMIT):
+    return pltpu.CompilerParams(vmem_limit_bytes=limit)
+
+
+SHORT = pl.CostEstimate(flops=10**6, bytes_accessed=10**5, transcendentals=0)
 
 
 def cost(flops, moved):
@@ -92,78 +96,67 @@
     )(position, table)
 
 
-def transform_kernel(count, pos_ref, table_ref, *refs):
+def transform_kernel(count, table_ref, *refs):
     planes = table_ref.shape[1]
     both = table_ref[...]
     high_table = both[:planes]
     width = refs[0].shape[-1]
     nodes = refs[0].shape[-2]
     per = planes // count
-    outs = refs[count:]
-    if len(outs) < count:
-        outs = [outs[0].at[pos_ref[1] ^ d] for d in range(count)]
-    flat = [ref.reshape(per * nodes, width) for ref in refs[:count]]
-    outs = [ref.reshape(per * nodes, width) for ref in outs]
+    flat = [ref.reshape(per * nodes, width) for ref in refs]
     for n in range(nodes):
         rows = pl.ds(n, per, stride=nodes) if nodes > 1 else pl.ds(0, per)
-        high, low = split(jnp.concatenate([ref[rows, :] for ref in flat], axis=0))
+        high, low = split(jnp.concatenate([ref[rows, :] for ref in flat[:count]], axis=0))
         wide = dot(both, high)
         result = wide[:planes] + (wide[planes:] + dot(high_table, low))
-        for d, ref in enumerate(outs):
+        for d, ref in enumerate(flat[count:]):
             ref[rows, :] = result[d * per : (d + 1) * per]
 
 
-def transform(position, blocks, table, join=False):
+def transform(blocks, table):
     per, nodes, elements = blocks[0].shape
     count = len(blocks)
     width = 128
     block = pl.BlockSpec((per, nodes, width), lambda i: (0, 0, i))
-    out_shape = [jax.ShapeDtypeStruct(v.shape, F32) for v in blocks]
-    out_specs = [block] * count
-    if join:
-        out_shape = jax.ShapeDtypeStruct((count, per, nodes, elements), F32)
-        out_specs = pl.BlockSpec((count, per, nodes, width), lambda i: (0, 0, 0, i))
     size = count * blocks[0].size
     return pl.pallas_call(
         functools.partial(transform_kernel, count),
-        out_shape=out_shape,
+        out_shape=[jax.ShapeDtypeStruct(v.shape, F32) for v in blocks],
         grid=(elements // width,),
-        in_specs=[SMEM_SPEC, pl.BlockSpec(table.shape, lambda i: (0, 0))] + [block] * count,
-        out_specs=out_specs,
+        in_specs=[pl.BlockSpec(table.shape, lambda i: (0, 0))] + [block] * count,
+        out_specs=[block] * count,
         compiler_params=params(),
         cost_estimate=cost(6 * PLANES * size, 8 * size),
         name="transform",
-    )(position, table, *blocks)
-
-
-def pack_kernel(pos_ref, *refs):
-    count = len(refs) // 2
-    for source, target in zip(refs[:count], refs[count:]):
-        target[...] = source[0]
-
-
-def pack(position, adjoint, comp, peers):
+    )(table, *blocks)
+
+
+def pack_kernel(comp, pos_ref, x_ref, *refs):
+    outs, sems = refs[:-1], refs[-1]
+    copies = [
+        pltpu.make_async_copy(x_ref.at[comp, :, line_of(pos_ref[1], d), :], out, sems.at[d])
+        for d, out in enumerate(outs)
+    ]
+    for copy in copies:
+        copy.start()
+    for copy in copies:
+        copy.wait()
+
+
+def pack(position, adjoint, comp, limit):
     _, per, nodes, elements = adjoint.shape
-    part = nodes // peers
-    block = per // 2
-
-    def source(d):
-        return pl.BlockSpec((1, block, part, elements), lambda i, pos: (comp, i, pos[1] ^ d, 0))
-
+    lines = nodes // LINE
     size = per * nodes * elements
     return pl.pallas_call(
-        pack_kernel,
-        out_shape=[jax.ShapeDtypeStruct((per, part, elements), F32)] * peers,
-        grid_spec=pltpu.PrefetchScalarGridSpec(
-            num_scalar_prefetch=1,
-            grid=(per // block,),
-            in_specs=[source(d) for d in range(peers)],
-            out_specs=[pl.BlockSpec((block, part, elements), lambda i, pos: (i, 0, 0))] * peers,
-        ),
-        compiler_params=params(),
-        cost_estimate=cost(0, 16 * size),
+        functools.partial(pack_kernel, comp),
+        out_shape=[jax.ShapeDtypeStruct((per, LINE, elements), F32)] * lines,
+        in_specs=[SMEM_SPEC, pl.BlockSpec(memory_space=pltpu.HBM)],
+        out_specs=[pl.BlockSpec(memory_space=pl.ANY)] * lines,
+        scratch_shapes=[pltpu.SemaphoreType.DMA((lines,))],
+        compiler_params=params(limit),
+        cost_estimate=cost(0, 8 * size),
         name="pack",
-    )(position, *[adjoint] * peers)
+    )(position, adjoint)
 
 
 BXR, BYS, DXBX, DXBY, DYBX, DYBY, DIAG = range(7)
@@ -356,7 +349,7 @@
         out_specs=[flat, flat, flat, face, face],
         scratch_shapes=[pltpu.VMEM((block * nodes, elements), F32)],
         compiler_params=params(),
-        cost_estimate=cost(12 * nodes * size, 20 * size),
+        cost_estimate=SHORT,
         name="start_solve",
     )(position, geometry, coef, dpack, spack, gather, mask, *z, *x)
 
@@ -423,7 +416,7 @@
         out_specs=[flat, face, face],
         scratch_shapes=[pltpu.VMEM((block * nodes, elements), F32)],
         compiler_params=params(),
-        cost_estimate=cost(12 * nodes * size, 16 * size),
+        cost_estimate=SHORT,
         name="two_sweeps",
     )(local, source, inverse, *own, *own_inv, *got, *inv, spack, gather, scatter, mask)
 
@@ -433,102 +426,96 @@
         ref[(*lead, line_of(me, d), slice(None))] = value[d * LINE : (d + 1) * LINE]
 
 
-def partial_kernel(block, count, pos_ref, coef_ref, dpack_ref, *refs):
-    z_refs, x_refs, o_ref = refs[:count], refs[count : 2 * count], refs[2 * count]
+def partial_kernel(block, count, coef_ref, dpack_ref, *refs):
+    z_refs, x_refs = refs[:count], refs[count : 2 * count]
+    px_ref, py_ref, pz_ref = refs[2 * count :]
     nodes = coef_ref.shape[1]
     dpack = dpack_ref[...]
-    me = pos_ref[1]
     for c in range(block):
         z = slab(z_refs, c)
         slopes = dot(dpack, pack_field(z))
         moved = coef_ref[BXR] * slopes[:nodes] + coef_ref[BYS] * slopes[nodes:]
-        store_own(o_ref, me, z - TIME_STEP * (moved + INTERACTION * z), 2, c)
+        pz_ref[c] = z - TIME_STEP * (moved + INTERACTION * z)
         x = slab(x_refs, c)
         slopes = dot(dpack, pack_field(x))
         moved = coef_ref[BXR] * slopes[:nodes] + coef_ref[BYS] * slopes[nodes:]
-        store_own(o_ref, me, x + TIME_STEP * (x * coef_ref[DXBX] - moved - INTERACTION * x), 0, c)
-        store_own(o_ref, me, TIME_STEP * (x * coef_ref[DYBX]), 1, c)
-
-
-def partial_update(position, z, x, coef, dpack):
+        px_ref[c] = x + TIME_STEP * (x * coef_ref[DXBX] - moved - INTERACTION * x)
+        py_ref[c] = TIME_STEP * (x * coef_ref[DYBX])
+
+
+def partial_update(z, x, coef, dpack):
     coefs, part, elements = z[0].shape
     nodes = len(z) * part
     block = coef_block(coefs)
     field = [pl.BlockSpec((block, part, elements), lambda i: (i, 0, 0))] * len(z)
-    size = coefs * nodes * elements
+    out = pl.BlockSpec((block, nodes, elements), lambda i: (i, 0, 0))
     return pl.pallas_call(
         functools.partial(partial_kernel, block, len(z)),
-        out_shape=jax.ShapeDtypeStruct((3, coefs, nodes, elements), F32),
+        out_shape=[jax.ShapeDtypeStruct((coefs, nodes, elements), F32)] * 3,
         grid=(coefs // block,),
-        in_specs=[SMEM_SPEC, whole(coef.shape), whole(dpack.shape), *field, *field],
-        out_specs=pl.BlockSpec((3, block, nodes, elements), lambda i: (0, i, 0, 0)),
-        compiler_params=params(),
-        cost_estimate=cost(24 * nodes * size, 20 * size),
+        in_specs=[whole(coef.shape), whole(dpack.shape), *field, *field],
+        out_specs=[out] * 3,
+        compiler_params=params(),
+        cost_estimate=SHORT,
         name="partial_update",
-    )(position, coef, dpack, *z, *x)
+    )(coef, dpack, *z, *x)
 
 
 def force_kernel(
     block, pos_ref, local_ref, inv_up_ref, inv_lo_ref, got_up_ref, got_lo_ref, geo_ref, dpack_ref,
-    scatter_ref, mask_ref, part_ref, o_ref, pot_ref,
+    scatter_ref, mask_ref, px_ref, pz_ref, o_ref, x_ref, pot_ref,
 ):
     nodes = dpack_ref.shape[0] // 2
     scale = TIME_STEP * INTERACTION
-    which = pl.program_id(1)
     me = pos_ref[1]
-
-    @pl.when(which == 0)
-    def _():
-        pot_ref[...] = local_ref[...]
-        for side, inv, got in ((0, inv_up_ref, got_up_ref), (1, inv_lo_ref, got_lo_ref)):
-            face = face_of(pot_ref, side)
-            partner = PENALTY * inv[0] * got[0]
-            face[...] = face[...] + scatter_faces(side, partner, scatter_ref, mask_ref)
-        first = pos_ref[0] * (block * pl.num_programs(0)) + pl.program_id(0) * block
-        for c in range(block):
-            wave = (4.0 / PLANES) * ((first + c) // 2).astype(F32)
-            factor = scale * (wave if c % 2 == 0 else -wave)
-            other = c + 1 if c % 2 == 0 else c - 1
-            turned = factor * pot_ref[pl.ds(other * nodes, nodes), :]
-            store_own(o_ref, me, own_order(part_ref, me, 0, c) + turned, 0, c)
-
-    @pl.when(which == 1)
-    def _():
-        drpack = dpack_ref[:nodes]
-        factor = scale * geo_ref[0:1, :]
-        for c in range(block):
-            slope = dot(drpack, pack_field(pot_ref[pl.ds(c * nodes, nodes), :]))
-            store_own(o_ref, me, own_order(part_ref, me, 0, c) - factor * slope, 0, c)
-
-
-def add_force(position, local, own_inv, got, geometry, dpack, scatter, mask, partial):
-    _, coefs, nodes, elements = partial.shape
+    pot_ref[...] = local_ref[...]
+    for side, inv, got in ((0, inv_up_ref, got_up_ref), (1, inv_lo_ref, got_lo_ref)):
+        face = face_of(pot_ref, side)
+        partner = PENALTY * inv[0] * got[0]
+        face[...] = face[...] + scatter_faces(side, partner, scatter_ref, mask_ref)
+    first = pos_ref[0] * (block * pl.num_programs(0)) + pl.program_id(0) * block
+    drpack = dpack_ref[:nodes]
+    slope_scale = scale * geo_ref[0:1, :]
+    for c in range(block):
+        pot = pot_ref[pl.ds(c * nodes, nodes), :]
+        slope = dot(drpack, pack_field(pot))
+        store_own(o_ref, me, pz_ref[c] - slope_scale * slope, 0, c)
+        wave = (4.0 / PLANES) * ((first + c) // 2).astype(F32)
+        factor = scale * (wave if c % 2 else -wave)
+        other = c - 1 if c % 2 else c + 1
+        x_ref[other] = px_ref[other] + factor * pot
+
+
+def add_force(position, local, own_inv, got, geometry, dpack, scatter, mask, px, pz):
+    coefs, nodes, elements = px.shape
     shared = scatter.shape[1]
     block = coef_block(coefs)
-    flat = pl.BlockSpec((block * nodes, elements), lambda i, j: (i, 0))
-    one = pl.BlockSpec((1, block, shared), lambda i, j: (0, i, 0))
-    third = pl.BlockSpec((1, block, shared), lambda i, j: (2, i, 0))
-    comp = pl.BlockSpec((1, block, nodes, elements), lambda i, j: (2 * j, i, 0, 0))
-    size = coefs * nodes * elements
+    flat = pl.BlockSpec((block * nodes, elements), lambda i: (i, 0))
+    one = pl.BlockSpec((1, block, shared), lambda i: (0, i, 0))
+    third = pl.BlockSpec((1, block, shared), lambda i: (2, i, 0))
+    part = pl.BlockSpec((block, nodes, elements), lambda i: (i, 0, 0))
     return pl.pallas_call(
         functools.partial(force_kernel, block),
-        out_shape=jax.ShapeDtypeStruct(partial.shape, F32),
-        grid=(coefs // block, 2),
+        out_shape=[
+            jax.ShapeDtypeStruct((3, coefs, nodes, elements), F32),
+            jax.ShapeDtypeStruct(px.shape, F32),
+        ],
+        grid=(coefs // block,),
         in_specs=[
             SMEM_SPEC, flat, third, third, one, one, whole(geometry.shape), whole(dpack.shape),
-            whole(scatter.shape), whole(mask.shape), comp,
+            whole(scatter.shape), whole(mask.shape), part, part,
         ],
-        out_specs=comp,
+        out_specs=[pl.BlockSpec((1, block, nodes, elements), lambda i: (2, i, 0, 0)), part],
         scratch_shapes=[pltpu.VMEM((block * nodes, elements), F32)],
-        input_output_aliases={10: 0},
-        compiler_params=params(),
-        cost_estimate=cost(6 * nodes * size, 24 * size),
+        compiler_params=params(),
+        cost_estimate=SHORT,
         name="add_force",
-    )(position, local, *own_inv, *got, geometry, dpack, scatter, mask, partial)
-
-
-def finish_kernel(block, count, pos_ref, coef_ref, dpack_ref, part_ref, *refs):
-    y_refs, o_ref = [ref.at[0] for ref in refs[:count]], refs[count]
+    )(position, local, *own_inv, *got, geometry, dpack, scatter, mask, px, pz)
+
+
+def finish_kernel(block, count, pos_ref, coef_ref, dpack_ref, px_ref, py_ref, filled_ref, *refs):
+    del filled_ref
+    y_refs, o_ref = refs[:count], refs[count]
     nodes = coef_ref.shape[1]
     me = pos_ref[1]
     dpack = dpack_ref[...]
@@ -537,35 +524,30 @@
         slopes = dot(dpack, pack_field(y))
         moved = coef_ref[BXR] * slopes[:nodes] + coef_ref[BYS] * slopes[nodes:]
         change = y + TIME_STEP * (y * coef_ref[DYBY] - moved)
-        store_own(o_ref, me, own_order(part_ref, me, 1, c) + change, 1, c)
-        change = TIME_STEP * (y * coef_ref[DXBY])
-        store_own(o_ref, me, own_order(part_ref, me, 0, c) + change, 0, c)
-
-
-def finish(position, y, coef, dpack, partial):
-    lines, coefs, part, elements = y.shape
-    nodes = lines * part
+        store_own(o_ref, me, py_ref[c] + change, 1, c)
+        store_own(o_ref, me, px_ref[c] + TIME_STEP * (y * coef_ref[DXBY]), 0, c)
+
+
+def finish(position, y, coef, dpack, px, py, filled):
+    coefs, part, elements = y[0].shape
+    nodes = len(y) * part
     block = coef_block(coefs)
-
-    def source(d):
-        return pl.BlockSpec((1, block, part, elements), lambda i, pos: (pos[1] ^ d, i, 0, 0))
-
-    comp = pl.BlockSpec((2, block, nodes, elements), lambda i, pos: (0, i, 0, 0))
-    size = coefs * nodes * elements
-    return pl.pallas_call(
-        functools.partial(finish_kernel, block, lines),
-        out_shape=jax.ShapeDtypeStruct(partial.shape, F32),
-        grid_spec=pltpu.PrefetchScalarGridSpec(
-            num_scalar_prefetch=1,
-            grid=(coefs // block,),
-            in_specs=[whole(coef.shape), whole(dpack.shape), comp] + [source(d) for d in range(lines)],
-            out_specs=comp,
-        ),
-        input_output_aliases={3: 0},
-        compiler_params=params(),
-        cost_estimate=cost(12 * nodes * size, 20 * size),
+    field = pl.BlockSpec((block, part, elements), lambda i: (i, 0, 0))
+    own = pl.BlockSpec((block, nodes, elements), lambda i: (i, 0, 0))
+    return pl.pallas_call(
+        functools.partial(finish_kernel, block, len(y)),
+        out_shape=jax.ShapeDtypeStruct(filled.shape, F32),
+        grid=(coefs // block,),
+        in_specs=[
+            SMEM_SPEC, whole(coef.shape), whole(dpack.shape), own, own,
+            pl.BlockSpec(memory_space=pl.ANY), *[field] * len(y),
+        ],
+        out_specs=pl.BlockSpec((2, block, nodes, elements), lambda i: (0, i, 0, 0)),
+        input_output_aliases={5: 0},
+        compiler_params=params(),
+        cost_estimate=SHORT,
         name="finish",
-    )(position, coef, dpack, partial, *[y] * lines)
+    )(position, coef, dpack, px, py, filled, *y)
 
 
 def to_all(blocks):
@@ -616,7 +598,7 @@
 
     def columns(comp):
         if direct:
-            return pack(position, adjoint, comp, peers)
+            return pack(position, adjoint, comp, LARGE_LIMIT if comp == 2 else VMEM_LIMIT)
         return [jnp.moveaxis(adjoint[comp].reshape(per, peers, nodes // peers, elements), 1, 0)]
 
     def spread(blocks):
@@ -625,18 +607,12 @@
         got = [to_all(blocks[0]).reshape(PLANES, nodes // peers, elements)]
         return lambda: got
 
-    def by_line(joined):
-        if direct:
-            return to_all(joined)
-        got = to_all(joined.reshape(peers, per, nodes // peers, elements))
-        got = jnp.moveaxis(got, 0, 1).reshape(per, lines, LINE, elements)
-        return jnp.moveaxis(got, 1, 0)
-
     def collect(blocks):
         if direct:
             return exchange(blocks)
-        got = by_line(blocks[0])
-        return lambda: [got[d] for d in range(lines)]
+        got = to_all(blocks[0].reshape(peers, per, nodes // peers, elements))
+        got = jnp.moveaxis(got, 0, 1).reshape(per, lines, LINE, elements)
+        return lambda: [got[:, d] for d in range(lines)]
 
     z_blocks = columns(2)
     z_columns = spread(z_blocks)
@@ -646,12 +622,12 @@
     constants = prepare(
         position, base_bank, snapshot, geometry, diff_r, diff_s, stiffness, upper_list, lower_list
     )
-    z_coefs = transform(position, z_columns(), table)
+    z_coefs = transform(z_columns(), table)
     z_coefs, constants = tie(z_coefs, constants)
     coef, dpack, spack, gather, scatter, mask = constants
     z_later = collect(z_coefs)
     y_blocks = columns(1)
-    x_coefs = transform(position, x_columns(), table)
+    x_coefs = transform(x_columns(), table)
     x_coefs, y_blocks = tie(x_coefs, y_blocks)
     x_later = collect(x_coefs)
     y_columns = spread(y_blocks)
@@ -663,20 +639,20 @@
     own_inv = (up, lo)
     got = swap_faces(up, lo)
     inv = got
-    partial = partial_update(position, z, x, coef, dpack)
+    px, py, pz = partial_update(z, x, coef, dpack)
     local, up, lo = two_sweeps(
         2, local, source, inverse, (up, lo), own_inv, got, inv, spack, gather, scatter, mask
     )
     y_got = y_columns()
     y_got[0], local = lax.optimization_barrier((y_got[0], local))
     got = swap_faces(up, lo)
-    y = by_line(transform(position, y_got, table, join=True))
+    y_later = collect(transform(y_got, table))
     local, up, lo = two_sweeps(
         1, local, source, inverse, (up, lo), own_inv, got, inv, spack, gather, scatter, mask
     )
     got = swap_faces(up, lo)
-    partial = add_force(position, local, own_inv, got, geometry, dpack, scatter, mask, partial)
-    return finish(position, y, coef, dpack, partial)
+    filled, px = add_force(position, local, own_inv, got, geometry, dpack, scatter, mask, px, pz)
+    return finish(position, y_later(), coef, dpack, px, py, filled)
 
 
 def solution(mesh):

time: 190 us -> 243 us (1.28)
  Pallas kernels: 48 us -> 103 us
  local copies, waits for them, and re-layouts: 15.6 us -> 0.07 us
  waiting for transfers between devices: 71.1 us -> 83.6 us
    pallas_call x8, Pallas kernels: 25.7 us -> 82.3 us  [the longest x3 67.1 us: pack(): pl.pallas_call(functools.partial(pack_kernel, comp), out_shape=[jax.Shape...]
    unnamed x138 -> x28, local copies, waits for them, and re-layouts: 15.6 us -> 0.07 us
    ppermute x35 -> x42, waiting for transfers between devices: 56.9 us -> 68.5 us  [exchange(): lax.ppermute(block, 'four', [(i, i ^ d) for i in range(peers)])]
    ppermute x35 -> x42, starting transfers between devices: 40.8 us -> 46.1 us  [exchange(): lax.ppermute(block, 'four', [(i, i ^ d) for i in range(peers)])]
    all_to_all x1 -> x0, starting transfers between devices: 3.6 us -> none  [to_all(): lax.all_to_all(blocks, 'four', split_axis=0, concat_axis=0, tiled=True)]
  transfers between devices with their start and end apart: 42 -> 48, of which waited for: 23 -> 25; matrix products, arithmetic and copies ran while one was open for 0% -> 0% of each run, Pallas kernels for 20% -> 13%
where the time goes in v6:
time: 243 us
  Pallas kernels  103 us (42%)
  waiting for transfers between devices  83.6 us (34%)
  starting transfers between devices  55 us (23%)
    ppermute x42, waiting for transfers between devices, exchange(): lax.ppermute(block, 'four', [(i, i ^ d) for i in range(peers)])  68.5 us
    pallas_call x3, Pallas kernels, pack(): pl.pallas_call(functools.partial(pack_kernel, comp), out_shape=[jax.Shape...  67.1 us
    ppermute x42, starting transfers between devices, exchange(): lax.ppermute(block, 'four', [(i, i ^ d) for i in range(peers)])  46.1 us
    ppermute x6, waiting for transfers between devices, swap_faces(): return (lax.ppermute(lo, 'dom', down_way), lax.ppermute(up, 'dom', up_way))  15.1 us
    pallas_call x2, Pallas kernels, two_sweeps(): pl.pallas_call(functools.partial(sweeps_kernel, block, keep), out_shape=[...  11.2 us
    ppermute x6, starting transfers between devices, swap_faces(): return (lax.ppermute(lo, 'dom', down_way), lax.ppermute(up, 'dom', up_way))  8.88 us
    pallas_call x3, Pallas kernels, transform(): pl.pallas_call(functools.partial(transform_kernel, count), out_shape=[jax...  7.37 us
  transfers between devices with their start and end apart: 48, of which 25 were waited for; matrix products, arithmetic and copies ran while one was open for 0% of the time, Pallas kernels for 13%

profile of v6, /device:TPU:0, one launch (start us, length us, event | category | flops | bytes accessed | tf_op | source)
XLA Modules:
  0.0 242.5 jit_solution(16789771178902225302)
XLA Ops:
  0.6 65.5 %pack.4 = (f32[32,8,256]{2,1,0:T(8,128)}, f32[32,8,256]{2,1,0:T(8,128)}, f32[32,8,256]{2,1,0:T(8,128)}, f32[32,8,256]{2,1,0:T(8,128)}, f32[32,8,256]{2,1,0:T(8,1...) custom-call(s32[2]{0:T(128)} %pad_add_fusion.pos_ref, f32[3,32,64,256]{3,2,1,0:T(8,128)} %x_ref.5), custom_call_target="tpu_custom_call" | custom-call | bytes 4194304 | tf_op jit(solution)/shard_map/pack/pallas_call | solution.py:150
  66.1 3.0 %collective-permute-start.2 = (f32[32,8,256]{2,1,0:T(8,128)}, f32[32,8,256]{2,1,0:T(8,128)S(1)}, u32[]{:S(2)}, u32[]{:S(2)}) collective-permute-start(f32[32,8,256]{2,1,0:T(8,128)} %get-tuple-element.173), channel_id=1, source_target_pairs={{0,2},{1,3},{2,0},{3,1},{4,6},{5,7},{6,4},{7,5},{8,10},{9,11},{10,... | collective-permute-start | bytes 786440 | tf_op jit(solution)/shard_map/ppermute | solution.py:591
  71.3 2.7 %collective-permute-start.4 = (f32[32,8,256]{2,1,0:T(8,128)}, f32[32,8,256]{2,1,0:T(8,128)S(1)}, u32[]{:S(2)}, u32[]{:S(2)}) collective-permute-start(f32[32,8,256]{2,1,0:T(8,128)} %get-tuple-element.180), channel_id=1, source_target_pairs={{0,5},{1,4},{2,7},{3,6},{4,1},{5,0},{6,3},{7,2},{8,13},{9,12},{10,... | collective-permute-start | bytes 786440 | tf_op jit(solution)/shard_map/ppermute | solution.py:591
  76.9 6.7 %collective-permute-done.5.refs_6_ = f32[32,8,256]{2,1,0:T(8,128)S(1)} collective-permute-done((f32[32,8,256]{2,1,0:T(8,128)}, f32[32,8,256]{2,1,0:T(8,128)S(1)}, u32[]{:S(2)}, u32[]{:S(2)}) %collective-permute-start.5) | collective-permute-done | bytes 262176 | tf_op jit(solution)/shard_map/ppermute | solution.py:591
  83.6 1.5 collective-permute-start.9
  85.7 1.7 collective-permute-done.3.refs_3_
  87.4 1.5 collective-permute-start.7
  88.9 5.5 %collective-permute-done.4.refs_5_ = f32[32,8,256]{2,1,0:T(8,128)S(1)} collective-permute-done((f32[32,8,256]{2,1,0:T(8,128)}, f32[32,8,256]{2,1,0:T(8,128)S(1)}, u32[]{:S(2)}, u32[]{:S(2)}) %collective-permute-start.4) | collective-permute-done | bytes 262176 | tf_op jit(solution)/shard_map/ppermute | solution.py:591
  94.4 2.6 %collective-permute-start.12 = (f32[32,8,256]{2,1,0:T(8,128)S(1)}, f32[32,8,256]{2,1,0:T(8,128)S(1)}, u32[]{:S(2)}, u32[]{:S(2)}) collective-permute-start(f32[32,8,256]{2,1,0:T(8,128)S(1)} %get-tuple-element.214), channel_id=1, source_target_pairs={{0,6},{1,7},{2,4},{3,5},{4,2},{5,3},{6,0},{7,1},{8,14},{9,15},{10,... | collective-permute-start | bytes 786440 | tf_op jit(solution)/shard_map/ppermute | solution.py:591
  99.4 1.7 collective-permute-start.11
  102.4 2.5 %transform.3 = (f32[32,8,256]{2,1,0:T(8,128)S(1)}, f32[32,8,256]{2,1,0:T(8,128)S(1)}, f32[32,8,256]{2,1,0:T(8,128)S(1)}, f32[32,8,256]{2,1,0:T(8,128)S(1)}, f32[...) custom-call(bf16[512,256]{1,0:T(8,128)(2,1)S(1)} %permuted_table.1.tab, ...), custom_call_target="tpu_custom_call" | custom-call | flops 805306368 | bytes 4194304 | tf_op jit(solution)/shard_map/transform/pallas_call | solution.py:122
  104.8 2.8 %collective-permute-done.7.refs_4_ = f32[32,8,256]{2,1,0:T(8,128)S(1)} collective-permute-done((f32[32,8,256]{2,1,0:T(8,128)S(1)}, f32[32,8,256]{2,1,0:T(8,128)S(1)}, u32[]{:S(2)}, u32[]{:S(2)}) %collective-permute-start.7) | collective-permute-done | bytes 262176 | tf_op jit(solution)/shard_map/ppermute | solution.py:591
  107.6 1.5 collective-permute-start.16
  110.1 1.8 collective-permute-start.14
  111.9 5.1 %collective-permute-done.13.refs_7_ = f32[32,8,256]{2,1,0:T(8,128)S(1)} collective-permute-done((f32[32,8,256]{2,1,0:T(8,128)S(1)}, f32[32,8,256]{2,1,0:T(8,128)S(1)}, u32[]{:S(2)}, u32[]{:S(2)}) %collective-permute-start.13) | collective-permute-done | bytes 262176 | tf_op jit(solution)/shard_map/ppermute | solution.py:591
  117.0 2.2 collective-permute-start.19
  120.1 1.5 collective-permute-done.16.refs_2_
  124.3 2.4 %transform.4 = (f32[32,8,256]{2,1,0:T(8,128)S(1)}, f32[32,8,256]{2,1,0:T(8,128)S(1)}, f32[32,8,256]{2,1,0:T(8,128)S(1)}, f32[32,8,256]{2,1,0:T(8,128)S(1)}, f32[...) custom-call(bf16[512,256]{1,0:T(8,128)(2,1)S(1)} %permuted_table.1.tab, ...), custom_call_target="tpu_custom_call" | custom-call | flops 805306368 | bytes 4194304 | tf_op jit(solution)/shard_map/transform/pallas_call | solution.py:122
  127.0 1.8 collective-permute-start.21
  128.8 3.8 %collective-permute-done.19.refs_6_ = f32[32,8,256]{2,1,0:T(8,128)S(1)} collective-permute-done((f32[32,8,256]{2,1,0:T(8,128)S(1)}, f32[32,8,256]{2,1,0:T(8,128)S(1)}, u32[]{:S(2)}, u32[]{:S(2)}) %collective-permute-start.19) | collective-permute-done | bytes 262176 | tf_op jit(solution)/shard_map/ppermute | solution.py:591
  132.6 1.5 collective-permute-start.23
  134.1 5.4 %collective-permute-done.20.refs_7_ = f32[32,8,256]{2,1,0:T(8,128)S(1)} collective-permute-done((f32[32,8,256]{2,1,0:T(8,128)S(1)}, f32[32,8,256]{2,1,0:T(8,128)S(1)}, u32[]{:S(2)}, u32[]{:S(2)}) %collective-permute-start.20) | collective-permute-done | bytes 262176 | tf_op jit(solution)/shard_map/ppermute | solution.py:591
  139.5 1.8 collective-permute-done.18.refs_5_
  142.2 4.8 %collective-permute-done.21.refs_12_ = f32[32,8,256]{2,1,0:T(8,128)S(1)} collective-permute-done((f32[32,8,256]{2,1,0:T(8,128)S(1)}, f32[32,8,256]{2,1,0:T(8,128)S(1)}, u32[]{:S(2)}, u32[]{:S(2)}) %collective-permute-start.21) | collective-permute-done | bytes 262176 | tf_op jit(solution)/shard_map/ppermute | solution.py:591
  147.4 2.4 collective-permute-start.27
  149.7 1.6 collective-permute-start.34
  151.3 3.8 %collective-permute-done.26.refs_14_ = f32[32,8,256]{2,1,0:T(8,128)S(1)} collective-permute-done((f32[32,8,256]{2,1,0:T(8,128)S(1)}, f32[32,8,256]{2,1,0:T(8,128)S(1)}, u32[]{:S(2)}, u32[]{:S(2)}) %collective-permute-start.26) | collective-permute-done | bytes 262176 | tf_op jit(solution)/shard_map/ppermute | solution.py:591
  155.1 1.5 collective-permute-start.36
  156.6 9.6 %collective-permute-done.25.refs_13_ = f32[32,8,256]{2,1,0:T(8,128)S(1)} collective-permute-done((f32[32,8,256]{2,1,0:T(8,128)S(1)}, f32[32,8,256]{2,1,0:T(8,128)S(1)}, u32[]{:S(2)}, u32[]{:S(2)}) %collective-permute-start.25) | collective-permute-done | bytes 262176 | tf_op jit(solution)/shard_map/ppermute | solution.py:591
  166.2 4.7 %start_solve.1 = (f32[2048,256]{1,0:T(8,128)S(1)}, f32[2048,256]{1,0:T(8,128)S(1)}, f32[2048,256]{1,0:T(8,128)S(1)}, f32[3,32,512]{2,1,0:T(8,128)S(1)}, f32[3,32,512]{2,1,0:T(8,128)S(1)}) custom-call(s32[2]{0:T(128)S(1)} %copy-done.6, f32[2,256]{1,0:T(2,128)S(1)} %copy-done.7, f32[7,64,256]{2,1,0:T(8,128)S(1)} %get-tuple-element.195.diag_ref.coef_ref, ...), custom_call_target="tpu_custom_call" | custom-call | flops 1000000 | bytes 100000 | tf_op jit(solution)/shard_map/start_solve/pallas_call | solution.py:338
  171.0 3.6 %collective-permute-start.28 = (f32[3,32,512]{2,1,0:T(8,128)S(1)}, f32[3,32,512]{2,1,0:T(8,128)S(1)}, u32[]{:S(2)}, u32[]{:S(2)}) collective-permute-start(f32[3,32,512]{2,1,0:T(8,128)S(1)} %get-tuple-element.280.own_lo_ref.own_inv_lo_ref.inv_lo_ref), channel_id=1, source_target_pairs={{8,0},{16,8},{24,16},{0,24},{9,1},{17,9},{25,17},{1,25},{10,2},{18... | collective-permute-start | bytes 589832 | tf_op jit(solution)/shard_map/ppermute | solution.py:561
  176.9 2.9 %collective-permute-done.28.got_up_ref.inv_up_ref = f32[3,32,512]{2,1,0:T(8,128)S(1)} collective-permute-done((f32[3,32,512]{2,1,0:T(8,128)S(1)}, f32[3,32,512]{2,1,0:T(8,128)S(1)}, u32[]{:S(2)}, u32[]{:S(2)}) %collective-permute-start.28) | collective-permute-done | bytes 196640 | tf_op jit(solution)/shard_map/ppermute | solution.py:561
  179.8 1.7 collective-permute-start.39
  181.5 3.1 %collective-permute-done.29.got_lo_ref.inv_lo_ref = f32[3,32,512]{2,1,0:T(8,128)S(1)} collective-permute-done((f32[3,32,512]{2,1,0:T(8,128)S(1)}, f32[3,32,512]{2,1,0:T(8,128)S(1)}, u32[]{:S(2)}, u32[]{:S(2)}) %collective-permute-start.29) | collective-permute-done | bytes 196640 | tf_op jit(solution)/shard_map/ppermute | solution.py:561
  185.7 5.3 %two_sweeps.2 = (f32[2048,256]{1,0:T(8,128)S(1)}, f32[2,32,512]{2,1,0:T(8,128)S(1)}, f32[2,32,512]{2,1,0:T(8,128)S(1)}) custom-call(f32[2048,256]{1,0:T(8,128)S(1)} %get-tuple-element.276.local_ref, f32[2048,256]{1,0:T(8,128)S(1)} %get-tuple-element.277.source_ref, f32[2048,256]{1,0:T(8,128)S(1)} %get-tuple-element.278.inverse_ref, ...), custom_call_target="tpu_custom_call" | custom-call | flops 1000000 | bytes 100000 | tf_op jit(solution)/shard_map/two_sweeps/pallas_call | solution.py:407
  191.1 4.6 %collective-permute-done.38.refs_5_ = f32[32,8,256]{2,1,0:T(8,128)S(1)} collective-permute-done((f32[32,8,256]{2,1,0:T(8,128)S(1)}, f32[32,8,256]{2,1,0:T(8,128)S(1)}, u32[]{:S(2)}, u32[]{:S(2)}) %collective-permute-start.38) | collective-permute-done | bytes 262176 | tf_op jit(solution)/shard_map/ppermute | solution.py:591
  195.7 2.4 %transform.5 = (f32[32,8,256]{2,1,0:T(8,128)S(1)}, f32[32,8,256]{2,1,0:T(8,128)S(1)}, f32[32,8,256]{2,1,0:T(8,128)S(1)}, f32[32,8,256]{2,1,0:T(8,128)S(1)}, f32[...) custom-call(bf16[512,256]{1,0:T(8,128)(2,1)S(1)} %permuted_table.1.tab, ...), custom_call_target="tpu_custom_call" | custom-call | flops 805306368 | bytes 4194304 | tf_op jit(solution)/shard_map/transform/pallas_call | solution.py:122
  199.8 3.2 %collective-permute-start.30 = (f32[2,32,512]{2,1,0:T(8,128)S(1)}, f32[2,32,512]{2,1,0:T(8,128)S(1)}, u32[]{:S(2)}, u32[]{:S(2)}) collective-permute-start(f32[2,32,512]{2,1,0:T(8,128)S(1)} %get-tuple-element.285.own_lo_ref), channel_id=1, source_target_pairs={{8,0},{16,8},{24,16},{0,24},{9,1},{17,9},{25,17},{1,25},{10,2},{18... | collective-permute-start | bytes 393224 | tf_op jit(solution)/shard_map/ppermute | solution.py:561
  203.0 3.9 %collective-permute-done.30.got_up_ref = f32[2,32,512]{2,1,0:T(8,128)S(1)} collective-permute-done((f32[2,32,512]{2,1,0:T(8,128)S(1)}, f32[2,32,512]{2,1,0:T(8,128)S(1)}, u32[]{:S(2)}, u32[]{:S(2)}) %collective-permute-start.30) | collective-permute-done | bytes 131104 | tf_op jit(solution)/shard_map/ppermute | solution.py:561
  206.9 3.1 %collective-permute-done.31.got_lo_ref = f32[2,32,512]{2,1,0:T(8,128)S(1)} collective-permute-done((f32[2,32,512]{2,1,0:T(8,128)S(1)}, f32[2,32,512]{2,1,0:T(8,128)S(1)}, u32[]{:S(2)}, u32[]{:S(2)}) %collective-permute-start.31) | collective-permute-done | bytes 131104 | tf_op jit(solution)/shard_map/ppermute | solution.py:561
  210.0 5.8 %two_sweeps.3 = (f32[2048,256]{1,0:T(8,128)S(1)}, f32[1,32,512]{2,1,0:T(8,128)S(1)}, f32[1,32,512]{2,1,0:T(8,128)S(1)}) custom-call(f32[2048,256]{1,0:T(8,128)S(1)} %get-tuple-element.283.local_ref, f32[2048,256]{1,0:T(8,128)S(1)} %get-tuple-element.277.source_ref, f32[2048,256]{1,0:T(8,128)S(1)} %get-tuple-element.278.inverse_ref, ...), custom_call_target="tpu_custom_call" | custom-call | flops 1000000 | bytes 100000 | tf_op jit(solution)/shard_map/two_sweeps/pallas_call | solution.py:407
  217.9 2.7 %collective-permute-start.45 = (f32[32,8,256]{2,1,0:T(8,128)S(1)}, f32[32,8,256]{2,1,0:T(8,128)S(1)}, u32[]{:S(2)}, u32[]{:S(2)}) collective-permute-start(f32[32,8,256]{2,1,0:T(8,128)S(1)} %get-tuple-element.319), channel_id=1, source_target_pairs={{0,5},{1,4},{2,7},{3,6},{4,1},{5,0},{6,3},{7,2},{8,13},{9,12},{10,... | collective-permute-start | bytes 786440 | tf_op jit(solution)/shard_map/ppermute | solution.py:591
  221.1 2.1 collective-permute-done.33.got_lo_ref
  223.6 2.7 %partial_update.1 = (f32[32,64,256]{2,1,0:T(8,128)S(1)}, f32[32,64,256]{2,1,0:T(8,128)S(1)}, f32[32,64,256]{2,1,0:T(8,128)S(1)}) custom-call(f32[7,64,256]{2,1,0:T(8,128)S(1)} %get-tuple-element.195.diag_ref.coef_ref, bf16[128,192]{1,0:T(8,128)(2,1)S(1)} %get-tuple-element.196.dpack_ref, f32[32,8,256]{2,1,0:T(8,128)S(1)} %get-tuple-element.232.refs_0_, ...), custom_call_target="tpu_custom_call" | custom-call | flops 1000000 | bytes 100000 | tf_op jit(solution)/shard_map/partial_update/pallas_call | solution.py:452
  226.3 3.9 %add_force.1 = (f32[3,32,64,256]{3,2,1,0:T(8,128)}, f32[32,64,256]{2,1,0:T(8,128)S(1)}) custom-call(s32[2]{0:T(128)S(1)} %copy-done.6, f32[2048,256]{1,0:T(8,128)S(1)} %get-tuple-element.286.local_ref, f32[3,32,512]{2,1,0:T(8,128)S(1)} %get-tuple-element.279.own_up_ref.own_inv_up_ref.inv_up_ref, ...), custom_call_target="tpu_custom_call" | custom-call | flops 1000000 | bytes 100000 | tf_op jit(solution)/shard_map/add_force/pallas_call | solution.py:497
  230.2 2.8 %collective-permute-done.46.refs_6_ = f32[32,8,256]{2,1,0:T(8,128)S(1)} collective-permute-done((f32[32,8,256]{2,1,0:T(8,128)S(1)}, f32[32,8,256]{2,1,0:T(8,128)S(1)}, u32[]{:S(2)}, u32[]{:S(2)}) %collective-permute-start.46) | collective-permute-done | bytes 262176 | tf_op jit(solution)/shard_map/ppermute | solution.py:591
  233.1 5.5 %collective-permute-done.47.refs_7_ = f32[32,8,256]{2,1,0:T(8,128)S(1)} collective-permute-done((f32[32,8,256]{2,1,0:T(8,128)S(1)}, f32[32,8,256]{2,1,0:T(8,128)S(1)}, u32[]{:S(2)}, u32[]{:S(2)}) %collective-permute-start.47) | collective-permute-done | bytes 262176 | tf_op jit(solution)/shard_map/ppermute | solution.py:591
  238.6 3.9 %finish.1 = f32[3,32,64,256]{3,2,1,0:T(8,128)} custom-call(s32[2]{0:T(128)S(1)} %copy-done.6, f32[7,64,256]{2,1,0:T(8,128)S(1)} %get-tuple-element.195.diag_ref.coef_ref, bf16[128,192]{1,0:T(8,128)(2,1)S(1)} %get-tuple-element.196.dpack_ref, f32[32,64,256]{2,1,0:T(8,128)S(1)} %get-tuple-element.291.px_ref, ...), custom_call_target="tpu_custom_call", output_to_operand_aliasing={{}: (5, {})} | custom-call | flops 1000000 | bytes 100000 | tf_op jit(solution)/shard_map/finish/pallas_call | solution.py:537
  (91 shorter events, 23.9 us)
Async XLA Ops:
  66.1 10.3 %collective-permute-start.2 = (f32[32,8,256]{2,1,0:T(8,128)}, f32[32,8,256]{2,1,0:T(8,128)S(1)}, u32[]{:S(2)}, u32[]{:S(2)}) collective-permute-start(f32[32,8,256]{2,1,0:T(8,128)} %get-tuple-element.173), channel_id=1, source_target_pairs={{0,2},{1,3},{2,0},{3,1},{4,6},{5,7},{6,4},{7,5},{8,10},{9,11},{10,... | collective-permute-start | bytes 786440 | tf_op jit(solution)/shard_map/ppermute | solution.py:591
  69.1 14.5 %collective-permute-start.5 = (f32[32,8,256]{2,1,0:T(8,128)}, f32[32,8,256]{2,1,0:T(8,128)S(1)}, u32[]{:S(2)}, u32[]{:S(2)}) collective-permute-start(f32[32,8,256]{2,1,0:T(8,128)} %get-tuple-element.183), channel_id=1, source_target_pairs={{0,6},{1,7},{2,4},{3,5},{4,2},{5,3},{6,0},{7,1},{8,14},{9,15},{10,... | collective-permute-start | bytes 786440 | tf_op jit(solution)/shard_map/ppermute | solution.py:591
  70.6 15.1 %collective-permute-start = (f32[32,8,256]{2,1,0:T(8,128)}, f32[32,8,256]{2,1,0:T(8,128)S(1)}, u32[]{:S(2)}, u32[]{:S(2)}) collective-permute-start(f32[32,8,256]{2,1,0:T(8,128)} %get-tuple-element.169), channel_id=1, source_target_pairs={{0,4},{1,5},{2,6},{3,7},{4,0},{5,1},{6,2},{7,3},{8,12},{9,13},{10,... | collective-permute-start | bytes 786440 | tf_op jit(solution)/shard_map/ppermute | solution.py:591
  70.6 16.8 %collective-permute-start.3 = (f32[32,8,256]{2,1,0:T(8,128)}, f32[32,8,256]{2,1,0:T(8,128)S(1)}, u32[]{:S(2)}, u32[]{:S(2)}) collective-permute-start(f32[32,8,256]{2,1,0:T(8,128)} %get-tuple-element.176), channel_id=1, source_target_pairs={{0,3},{1,2},{2,1},{3,0},{4,7},{5,6},{6,5},{7,4},{8,11},{9,10},{10,... | collective-permute-start | bytes 786440 | tf_op jit(solution)/shard_map/ppermute | solution.py:591
  71.3 23.1 %collective-permute-start.4 = (f32[32,8,256]{2,1,0:T(8,128)}, f32[32,8,256]{2,1,0:T(8,128)S(1)}, u32[]{:S(2)}, u32[]{:S(2)}) collective-permute-start(f32[32,8,256]{2,1,0:T(8,128)} %get-tuple-element.180), channel_id=1, source_target_pairs={{0,5},{1,4},{2,7},{3,6},{4,1},{5,0},{6,3},{7,2},{8,13},{9,12},{10,... | collective-permute-start | bytes 786440 | tf_op jit(solution)/shard_map/ppermute | solution.py:591
  76.4 20.5 %collective-permute-start.6 = (f32[32,8,256]{2,1,0:T(8,128)S(1)}, f32[32,8,256]{2,1,0:T(8,128)S(1)}, u32[]{:S(2)}, u32[]{:S(2)}) collective-permute-start(f32[32,8,256]{2,1,0:T(8,128)S(1)} %copy-done.13), channel_id=1, source_target_pairs={{0,7},{1,6},{2,5},{3,4},{4,3},{5,2},{6,1},{7,0},{8,15},{9,14},{10,... | collective-permute-start | bytes 786440 | tf_op jit(solution)/shard_map/ppermute | solution.py:591
  83.6 14.5 %collective-permute-start.9 = (f32[32,8,256]{2,1,0:T(8,128)S(1)}, f32[32,8,256]{2,1,0:T(8,128)S(1)}, u32[]{:S(2)}, u32[]{:S(2)}) collective-permute-start(f32[32,8,256]{2,1,0:T(8,128)S(1)} %get-tuple-element.204), channel_id=1, source_target_pairs={{0,2},{1,3},{2,0},{3,1},{4,6},{5,7},{6,4},{7,5},{8,10},{9,11},{10,... | collective-permute-start | bytes 786440 | tf_op jit(solution)/shard_map/ppermute | solution.py:591
  85.7 13.8 %collective-permute-start.1 = (f32[32,8,256]{2,1,0:T(8,128)S(1)}, f32[32,8,256]{2,1,0:T(8,128)S(1)}, u32[]{:S(2)}, u32[]{:S(2)}) collective-permute-start(f32[32,8,256]{2,1,0:T(8,128)S(1)} %copy-done.12), channel_id=1, source_target_pairs={{0,1},{1,0},{2,3},{3,2},{4,5},{5,4},{6,7},{7,6},{8,9},{9,8},{10,11... | collective-permute-start | bytes 786440 | tf_op jit(solution)/shard_map/ppermute | solution.py:591
  87.4 20.2 %collective-permute-start.7 = (f32[32,8,256]{2,1,0:T(8,128)S(1)}, f32[32,8,256]{2,1,0:T(8,128)S(1)}, u32[]{:S(2)}, u32[]{:S(2)}) collective-permute-start(f32[32,8,256]{2,1,0:T(8,128)S(1)} %get-tuple-element.200), channel_id=1, source_target_pairs={{0,4},{1,5},{2,6},{3,7},{4,0},{5,1},{6,2},{7,3},{8,12},{9,13},{10,... | collective-permute-start | bytes 786440 | tf_op jit(solution)/shard_map/ppermute | solution.py:591
  94.4 13.2 %collective-permute-start.12 = (f32[32,8,256]{2,1,0:T(8,128)S(1)}, f32[32,8,256]{2,1,0:T(8,128)S(1)}, u32[]{:S(2)}, u32[]{:S(2)}) collective-permute-start(f32[32,8,256]{2,1,0:T(8,128)S(1)} %get-tuple-element.214), channel_id=1, source_target_pairs={{0,6},{1,7},{2,4},{3,5},{4,2},{5,3},{6,0},{7,1},{8,14},{9,15},{10,... | collective-permute-start | bytes 786440 | tf_op jit(solution)/shard_map/ppermute | solution.py:591
  97.0 13.1 %collective-permute-start.10 = (f32[32,8,256]{2,1,0:T(8,128)S(1)}, f32[32,8,256]{2,1,0:T(8,128)S(1)}, u32[]{:S(2)}, u32[]{:S(2)}) collective-permute-start(f32[32,8,256]{2,1,0:T(8,128)S(1)} %get-tuple-element.207), channel_id=1, source_target_pairs={{0,3},{1,2},{2,1},{3,0},{4,7},{5,6},{6,5},{7,4},{8,11},{9,10},{10,... | collective-permute-start | bytes 786440 | tf_op jit(solution)/shard_map/ppermute | solution.py:591
  98.2 18.8 %collective-permute-start.13 = (f32[32,8,256]{2,1,0:T(8,128)S(1)}, f32[32,8,256]{2,1,0:T(8,128)S(1)}, u32[]{:S(2)}, u32[]{:S(2)}) collective-permute-start(f32[32,8,256]{2,1,0:T(8,128)S(1)} %get-tuple-element.217), channel_id=1, source_target_pairs={{0,7},{1,6},{2,5},{3,4},{4,3},{5,2},{6,1},{7,0},{8,15},{9,14},{10,... | collective-permute-start | bytes 786440 | tf_op jit(solution)/shard_map/ppermute | solution.py:591
  99.4 17.6 %collective-permute-start.11 = (f32[32,8,256]{2,1,0:T(8,128)S(1)}, f32[32,8,256]{2,1,0:T(8,128)S(1)}, u32[]{:S(2)}, u32[]{:S(2)}) collective-permute-start(f32[32,8,256]{2,1,0:T(8,128)S(1)} %get-tuple-element.211), channel_id=1, source_target_pairs={{0,5},{1,4},{2,7},{3,6},{4,1},{5,0},{6,3},{7,2},{8,13},{9,12},{10,... | collective-permute-start | bytes 786440 | tf_op jit(solution)/shard_map/ppermute | solution.py:591
  107.6 12.4 %collective-permute-start.8 = (f32[32,8,256]{2,1,0:T(8,128)S(1)}, f32[32,8,256]{2,1,0:T(8,128)S(1)}, u32[]{:S(2)}, u32[]{:S(2)}) collective-permute-start(f32[32,8,256]{2,1,0:T(8,128)S(1)} %get-tuple-element.201), channel_id=1, source_target_pairs={{0,1},{1,0},{2,3},{3,2},{4,5},{5,4},{6,7},{7,6},{8,9},{9,8},{10,11... | collective-permute-start | bytes 786440 | tf_op jit(solution)/shard_map/ppermute | solution.py:591
  107.6 14.0 %collective-permute-start.16 = (f32[32,8,256]{2,1,0:T(8,128)S(1)}, f32[32,8,256]{2,1,0:T(8,128)S(1)}, u32[]{:S(2)}, u32[]{:S(2)}) collective-permute-start(f32[32,8,256]{2,1,0:T(8,128)S(1)} %get-tuple-element.239), channel_id=1, source_target_pairs={{0,2},{1,3},{2,0},{3,1},{4,6},{5,7},{6,4},{7,5},{8,10},{9,11},{10,... | collective-permute-start | bytes 786440 | tf_op jit(solution)/shard_map/ppermute | solution.py:591
  110.1 16.6 %collective-permute-start.14 = (f32[32,8,256]{2,1,0:T(8,128)S(1)}, f32[32,8,256]{2,1,0:T(8,128)S(1)}, u32[]{:S(2)}, u32[]{:S(2)}) collective-permute-start(f32[32,8,256]{2,1,0:T(8,128)S(1)} %get-tuple-element.235), channel_id=1, source_target_pairs={{0,4},{1,5},{2,6},{3,7},{4,0},{5,1},{6,2},{7,3},{8,12},{9,13},{10,... | collective-permute-start | bytes 786440 | tf_op jit(solution)/shard_map/ppermute | solution.py:591
  117.0 10.0 %collective-permute-start.17 = (f32[32,8,256]{2,1,0:T(8,128)S(1)}, f32[32,8,256]{2,1,0:T(8,128)S(1)}, u32[]{:S(2)}, u32[]{:S(2)}) collective-permute-start(f32[32,8,256]{2,1,0:T(8,128)S(1)} %get-tuple-element.242), channel_id=1, source_target_pairs={{0,3},{1,2},{2,1},{3,0},{4,7},{5,6},{6,5},{7,4},{8,11},{9,10},{10,... | collective-permute-start | bytes 786440 | tf_op jit(solution)/shard_map/ppermute | solution.py:591
  117.0 15.6 %collective-permute-start.19 = (f32[32,8,256]{2,1,0:T(8,128)S(1)}, f32[32,8,256]{2,1,0:T(8,128)S(1)}, u32[]{:S(2)}, u32[]{:S(2)}) collective-permute-start(f32[32,8,256]{2,1,0:T(8,128)S(1)} %get-tuple-element.249), channel_id=1, source_target_pairs={{0,6},{1,7},{2,4},{3,5},{4,2},{5,3},{6,0},{7,1},{8,14},{9,15},{10,... | collective-permute-start | bytes 786440 | tf_op jit(solution)/shard_map/ppermute | solution.py:591
  121.6 19.7 %collective-permute-start.18 = (f32[32,8,256]{2,1,0:T(8,128)S(1)}, f32[32,8,256]{2,1,0:T(8,128)S(1)}, u32[]{:S(2)}, u32[]{:S(2)}) collective-permute-start(f32[32,8,256]{2,1,0:T(8,128)S(1)} %get-tuple-element.246), channel_id=1, source_target_pairs={{0,5},{1,4},{2,7},{3,6},{4,1},{5,0},{6,3},{7,2},{8,13},{9,12},{10,... | collective-permute-start | bytes 786440 | tf_op jit(solution)/shard_map/ppermute | solution.py:591
  122.9 16.6 %collective-permute-start.20 = (f32[32,8,256]{2,1,0:T(8,128)S(1)}, f32[32,8,256]{2,1,0:T(8,128)S(1)}, u32[]{:S(2)}, u32[]{:S(2)}) collective-permute-start(f32[32,8,256]{2,1,0:T(8,128)S(1)} %get-tuple-element.252), channel_id=1, source_target_pairs={{0,7},{1,6},{2,5},{3,4},{4,3},{5,2},{6,1},{7,0},{8,15},{9,14},{10,... | collective-permute-start | bytes 786440 | tf_op jit(solution)/shard_map/ppermute | solution.py:591
  126.7 15.5 %collective-permute-start.15 = (f32[32,8,256]{2,1,0:T(8,128)S(1)}, f32[32,8,256]{2,1,0:T(8,128)S(1)}, u32[]{:S(2)}, u32[]{:S(2)}) collective-permute-start(f32[32,8,256]{2,1,0:T(8,128)S(1)} %get-tuple-element.236), channel_id=1, source_target_pairs={{0,1},{1,0},{2,3},{3,2},{4,5},{5,4},{6,7},{7,6},{8,9},{9,8},{10,11... | collective-permute-start | bytes 786440 | tf_op jit(solution)/shard_map/ppermute | solution.py:591
  127.0 20.0 %collective-permute-start.21 = (f32[32,8,256]{2,1,0:T(8,128)S(1)}, f32[32,8,256]{2,1,0:T(8,128)S(1)}, u32[]{:S(2)}, u32[]{:S(2)}) collective-permute-start(f32[32,8,256]{2,1,0:T(8,128)S(1)} %get-tuple-element.257), channel_id=1, source_target_pairs={{0,4},{1,5},{2,6},{3,7},{4,0},{5,1},{6,2},{7,3},{8,12},{9,13},{10,... | collective-permute-start | bytes 786440 | tf_op jit(solution)/shard_map/ppermute | solution.py:591
  132.6 14.8 %collective-permute-start.23 = (f32[32,8,256]{2,1,0:T(8,128)S(1)}, f32[32,8,256]{2,1,0:T(8,128)S(1)}, u32[]{:S(2)}, u32[]{:S(2)}) collective-permute-start(f32[32,8,256]{2,1,0:T(8,128)S(1)} %get-tuple-element.261), channel_id=1, source_target_pairs={{0,2},{1,3},{2,0},{3,1},{4,6},{5,7},{6,4},{7,5},{8,10},{9,11},{10,... | collective-permute-start | bytes 786440 | tf_op jit(solution)/shard_map/ppermute | solution.py:591
  139.5 10.2 %collective-permute-start.24 = (f32[32,8,256]{2,1,0:T(8,128)S(1)}, f32[32,8,256]{2,1,0:T(8,128)S(1)}, u32[]{:S(2)}, u32[]{:S(2)}) collective-permute-start(f32[32,8,256]{2,1,0:T(8,128)S(1)} %get-tuple-element.264), channel_id=1, source_target_pairs={{0,3},{1,2},{2,1},{3,0},{4,7},{5,6},{6,5},{7,4},{8,11},{9,10},{10,... | collective-permute-start | bytes 786440 | tf_op jit(solution)/shard_map/ppermute | solution.py:591
  141.3 13.7 %collective-permute-start.26 = (f32[32,8,256]{2,1,0:T(8,128)S(1)}, f32[32,8,256]{2,1,0:T(8,128)S(1)}, u32[]{:S(2)}, u32[]{:S(2)}) collective-permute-start(f32[32,8,256]{2,1,0:T(8,128)S(1)} %get-tuple-element.271), channel_id=1, source_target_pairs={{0,6},{1,7},{2,4},{3,5},{4,2},{5,3},{6,0},{7,1},{8,14},{9,15},{10,... | collective-permute-start | bytes 786440 | tf_op jit(solution)/shard_map/ppermute | solution.py:591
  147.1 9.5 %collective-permute-start.22 = (f32[32,8,256]{2,1,0:T(8,128)S(1)}, f32[32,8,256]{2,1,0:T(8,128)S(1)}, u32[]{:S(2)}, u32[]{:S(2)}) collective-permute-start(f32[32,8,256]{2,1,0:T(8,128)S(1)} %get-tuple-element.258), channel_id=1, source_target_pairs={{0,1},{1,0},{2,3},{3,2},{4,5},{5,4},{6,7},{7,6},{8,9},{9,8},{10,11... | collective-permute-start | bytes 786440 | tf_op jit(solution)/shard_map/ppermute | solution.py:591
  147.1 19.2 %collective-permute-start.25 = (f32[32,8,256]{2,1,0:T(8,128)S(1)}, f32[32,8,256]{2,1,0:T(8,128)S(1)}, u32[]{:S(2)}, u32[]{:S(2)}) collective-permute-start(f32[32,8,256]{2,1,0:T(8,128)S(1)} %get-tuple-element.268), channel_id=1, source_target_pairs={{0,5},{1,4},{2,7},{3,6},{4,1},{5,0},{6,3},{7,2},{8,13},{9,12},{10,... | collective-permute-start | bytes 786440 | tf_op jit(solution)/shard_map/ppermute | solution.py:591
  147.4 18.9 %collective-permute-start.27 = (f32[32,8,256]{2,1,0:T(8,128)S(1)}, f32[32,8,256]{2,1,0:T(8,128)S(1)}, u32[]{:S(2)}, u32[]{:S(2)}) collective-permute-start(f32[32,8,256]{2,1,0:T(8,128)S(1)} %get-tuple-element.274), channel_id=1, source_target_pairs={{0,7},{1,6},{2,5},{3,4},{4,3},{5,2},{6,1},{7,0},{8,15},{9,14},{10,... | collective-permute-start | bytes 786440 | tf_op jit(solution)/shard_map/ppermute | solution.py:591
  149.7 24.8 %collective-permute-start.34 = (f32[32,8,256]{2,1,0:T(8,128)S(1)}, f32[32,8,256]{2,1,0:T(8,128)S(1)}, u32[]{:S(2)}, u32[]{:S(2)}) collective-permute-start(f32[32,8,256]{2,1,0:T(8,128)S(1)} %get-tuple-element.296), channel_id=1, source_target_pairs={{0,4},{1,5},{2,6},{3,7},{4,0},{5,1},{6,2},{7,3},{8,12},{9,13},{10,... | collective-permute-start | bytes 786440 | tf_op jit(solution)/shard_map/ppermute | solution.py:591
  155.1 19.8 %collective-permute-start.36 = (f32[32,8,256]{2,1,0:T(8,128)S(1)}, f32[32,8,256]{2,1,0:T(8,128)S(1)}, u32[]{:S(2)}, u32[]{:S(2)}) collective-permute-start(f32[32,8,256]{2,1,0:T(8,128)S(1)} %get-tuple-element.299), channel_id=1, source_target_pairs={{0,2},{1,3},{2,0},{3,1},{4,6},{5,7},{6,4},{7,5},{8,10},{9,11},{10,... | collective-permute-start | bytes 786440 | tf_op jit(solution)/shard_map/ppermute | solution.py:591
  171.0 8.9 %collective-permute-start.28 = (f32[3,32,512]{2,1,0:T(8,128)S(1)}, f32[3,32,512]{2,1,0:T(8,128)S(1)}, u32[]{:S(2)}, u32[]{:S(2)}) collective-permute-start(f32[3,32,512]{2,1,0:T(8,128)S(1)} %get-tuple-element.280.own_lo_ref.own_inv_lo_ref.inv_lo_ref), channel_id=1, source_target_pairs={{8,0},{16,8},{24,16},{0,24},{9,1},{17,9},{25,17},{1,25},{10,2},{18... | collective-permute-start | bytes 589832 | tf_op jit(solution)/shard_map/ppermute | solution.py:561
  174.6 10.0 %collective-permute-start.29 = (f32[3,32,512]{2,1,0:T(8,128)S(1)}, f32[3,32,512]{2,1,0:T(8,128)S(1)}, u32[]{:S(2)}, u32[]{:S(2)}) collective-permute-start(f32[3,32,512]{2,1,0:T(8,128)S(1)} %get-tuple-element.279.own_up_ref.own_inv_up_ref.inv_up_ref), channel_id=1, source_target_pairs={{0,8},{8,16},{16,24},{24,0},{1,9},{9,17},{17,25},{25,1},{2,10},{10... | collective-permute-start | bytes 589832 | tf_op jit(solution)/shard_map/ppermute | solution.py:561
  174.6 16.5 %collective-permute-start.35 = (f32[32,8,256]{2,1,0:T(8,128)S(1)}, f32[32,8,256]{2,1,0:T(8,128)S(1)}, u32[]{:S(2)}, u32[]{:S(2)}) collective-permute-start(f32[32,8,256]{2,1,0:T(8,128)S(1)} %get-tuple-element.297), channel_id=1, source_target_pairs={{0,1},{1,0},{2,3},{3,2},{4,5},{5,4},{6,7},{7,6},{8,9},{9,8},{10,11... | collective-permute-start | bytes 786440 | tf_op jit(solution)/shard_map/ppermute | solution.py:591
  174.9 16.2 %collective-permute-start.37 = (f32[32,8,256]{2,1,0:T(8,128)S(1)}, f32[32,8,256]{2,1,0:T(8,128)S(1)}, u32[]{:S(2)}, u32[]{:S(2)}) collective-permute-start(f32[32,8,256]{2,1,0:T(8,128)S(1)} %get-tuple-element.301), channel_id=1, source_target_pairs={{0,3},{1,2},{2,1},{3,0},{4,7},{5,6},{6,5},{7,4},{8,11},{9,10},{10,... | collective-permute-start | bytes 786440 | tf_op jit(solution)/shard_map/ppermute | solution.py:591
  176.2 19.5 %collective-permute-start.38 = (f32[32,8,256]{2,1,0:T(8,128)S(1)}, f32[32,8,256]{2,1,0:T(8,128)S(1)}, u32[]{:S(2)}, u32[]{:S(2)}) collective-permute-start(f32[32,8,256]{2,1,0:T(8,128)S(1)} %get-tuple-element.303), channel_id=1, source_target_pairs={{0,5},{1,4},{2,7},{3,6},{4,1},{5,0},{6,3},{7,2},{8,13},{9,12},{10,... | collective-permute-start | bytes 786440 | tf_op jit(solution)/shard_map/ppermute | solution.py:591
  179.8 15.9 %collective-permute-start.39 = (f32[32,8,256]{2,1,0:T(8,128)S(1)}, f32[32,8,256]{2,1,0:T(8,128)S(1)}, u32[]{:S(2)}, u32[]{:S(2)}) collective-permute-start(f32[32,8,256]{2,1,0:T(8,128)S(1)} %get-tuple-element.304), channel_id=1, source_target_pairs={{0,6},{1,7},{2,4},{3,5},{4,2},{5,3},{6,0},{7,1},{8,14},{9,15},{10,... | collective-permute-start | bytes 786440 | tf_op jit(solution)/shard_map/ppermute | solution.py:591
  184.5 11.1 %collective-permute-start.40 = (f32[32,8,256]{2,1,0:T(8,128)S(1)}, f32[32,8,256]{2,1,0:T(8,128)S(1)}, u32[]{:S(2)}, u32[]{:S(2)}) collective-permute-start(f32[32,8,256]{2,1,0:T(8,128)S(1)} %get-tuple-element.305), channel_id=1, source_target_pairs={{0,7},{1,6},{2,5},{3,4},{4,3},{5,2},{6,1},{7,0},{8,15},{9,14},{10,... | collective-permute-start | bytes 786440 | tf_op jit(solution)/shard_map/ppermute | solution.py:591
  198.1 19.7 %collective-permute-start.41 = (f32[32,8,256]{2,1,0:T(8,128)S(1)}, f32[32,8,256]{2,1,0:T(8,128)S(1)}, u32[]{:S(2)}, u32[]{:S(2)}) collective-permute-start(f32[32,8,256]{2,1,0:T(8,128)S(1)} %get-tuple-element.309), channel_id=1, source_target_pairs={{0,4},{1,5},{2,6},{3,7},{4,0},{5,1},{6,2},{7,3},{8,12},{9,13},{10,... | collective-permute-start | bytes 786440 | tf_op jit(solution)/shard_map/ppermute | solution.py:591
  198.4 22.1 %collective-permute-start.43 = (f32[32,8,256]{2,1,0:T(8,128)S(1)}, f32[32,8,256]{2,1,0:T(8,128)S(1)}, u32[]{:S(2)}, u32[]{:S(2)}) collective-permute-start(f32[32,8,256]{2,1,0:T(8,128)S(1)} %get-tuple-element.313), channel_id=1, source_target_pairs={{0,2},{1,3},{2,0},{3,1},{4,6},{5,7},{6,4},{7,5},{8,10},{9,11},{10,... | collective-permute-start | bytes 786440 | tf_op jit(solution)/shard_map/ppermute | solution.py:591
  199.8 7.1 %collective-permute-start.30 = (f32[2,32,512]{2,1,0:T(8,128)S(1)}, f32[2,32,512]{2,1,0:T(8,128)S(1)}, u32[]{:S(2)}, u32[]{:S(2)}) collective-permute-start(f32[2,32,512]{2,1,0:T(8,128)S(1)} %get-tuple-element.285.own_lo_ref), channel_id=1, source_target_pairs={{8,0},{16,8},{24,16},{0,24},{9,1},{17,9},{25,17},{1,25},{10,2},{18... | collective-permute-start | bytes 393224 | tf_op jit(solution)/shard_map/ppermute | solution.py:561
  203.0 7.0 %collective-permute-start.31 = (f32[2,32,512]{2,1,0:T(8,128)S(1)}, f32[2,32,512]{2,1,0:T(8,128)S(1)}, u32[]{:S(2)}, u32[]{:S(2)}) collective-permute-start(f32[2,32,512]{2,1,0:T(8,128)S(1)} %get-tuple-element.284.own_up_ref), channel_id=1, source_target_pairs={{0,8},{8,16},{16,24},{24,0},{1,9},{9,17},{17,25},{25,1},{2,10},{10... | collective-permute-start | bytes 393224 | tf_op jit(solution)/shard_map/ppermute | solution.py:561
  215.8 5.3 %collective-permute-start.32 = (f32[1,32,512]{2,1,0:T(8,128)S(1)}, f32[1,32,512]{2,1,0:T(8,128)S(1)}, u32[]{:S(2)}, u32[]{:S(2)}) collective-permute-start(f32[1,32,512]{2,1,0:T(8,128)S(1)} %get-tuple-element.287), channel_id=1, source_target_pairs={{8,0},{16,8},{24,16},{0,24},{9,1},{17,9},{25,17},{1,25},{10,2},{18... | collective-permute-start | bytes 196616 | tf_op jit(solution)/shard_map/ppermute | solution.py:561
  217.1 6.1 %collective-permute-start.33 = (f32[1,32,512]{2,1,0:T(8,128)S(1)}, f32[1,32,512]{2,1,0:T(8,128)S(1)}, u32[]{:S(2)}, u32[]{:S(2)}) collective-permute-start(f32[1,32,512]{2,1,0:T(8,128)S(1)} %get-tuple-element.288), channel_id=1, source_target_pairs={{0,8},{8,16},{16,24},{24,0},{1,9},{9,17},{17,25},{25,1},{2,10},{10... | collective-permute-start | bytes 196616 | tf_op jit(solution)/shard_map/ppermute | solution.py:561
  217.9 12.4 %collective-permute-start.44 = (f32[32,8,256]{2,1,0:T(8,128)S(1)}, f32[32,8,256]{2,1,0:T(8,128)S(1)}, u32[]{:S(2)}, u32[]{:S(2)}) collective-permute-start(f32[32,8,256]{2,1,0:T(8,128)S(1)} %get-tuple-element.316), channel_id=1, source_target_pairs={{0,3},{1,2},{2,1},{3,0},{4,7},{5,6},{6,5},{7,4},{8,11},{9,10},{10,... | collective-permute-start | bytes 786440 | tf_op jit(solution)/shard_map/ppermute | solution.py:591
  217.9 12.4 %collective-permute-start.45 = (f32[32,8,256]{2,1,0:T(8,128)S(1)}, f32[32,8,256]{2,1,0:T(8,128)S(1)}, u32[]{:S(2)}, u32[]{:S(2)}) collective-permute-start(f32[32,8,256]{2,1,0:T(8,128)S(1)} %get-tuple-element.319), channel_id=1, source_target_pairs={{0,5},{1,4},{2,7},{3,6},{4,1},{5,0},{6,3},{7,2},{8,13},{9,12},{10,... | collective-permute-start | bytes 786440 | tf_op jit(solution)/shard_map/ppermute | solution.py:591
  220.6 12.5 %collective-permute-start.46 = (f32[32,8,256]{2,1,0:T(8,128)S(1)}, f32[32,8,256]{2,1,0:T(8,128)S(1)}, u32[]{:S(2)}, u32[]{:S(2)}) collective-permute-start(f32[32,8,256]{2,1,0:T(8,128)S(1)} %get-tuple-element.321), channel_id=1, source_target_pairs={{0,6},{1,7},{2,4},{3,5},{4,2},{5,3},{6,0},{7,1},{8,14},{9,15},{10,... | collective-permute-start | bytes 786440 | tf_op jit(solution)/shard_map/ppermute | solution.py:591
  221.1 12.0 %collective-permute-start.42 = (f32[32,8,256]{2,1,0:T(8,128)S(1)}, f32[32,8,256]{2,1,0:T(8,128)S(1)}, u32[]{:S(2)}, u32[]{:S(2)}) collective-permute-start(f32[32,8,256]{2,1,0:T(8,128)S(1)} %get-tuple-element.310), channel_id=1, source_target_pairs={{0,1},{1,0},{2,3},{3,2},{4,5},{5,4},{6,7},{7,6},{8,9},{9,8},{10,11... | collective-permute-start | bytes 786440 | tf_op jit(solution)/shard_map/ppermute | solution.py:591
  223.2 15.4 %collective-permute-start.47 = (f32[32,8,256]{2,1,0:T(8,128)S(1)}, f32[32,8,256]{2,1,0:T(8,128)S(1)}, u32[]{:S(2)}, u32[]{:S(2)}) collective-permute-start(f32[32,8,256]{2,1,0:T(8,128)S(1)} %get-tuple-element.322), channel_id=1, source_target_pairs={{0,7},{1,6},{2,5},{3,4},{4,3},{5,2},{6,1},{7,0},{8,15},{9,14},{10,... | collective-permute-start | bytes 786440 | tf_op jit(solution)/shard_map/ppermute | solution.py:591
  (14 other events, 440.4 us)

commit v7 on v6

--- a/solution.py
+++ b/solution.py
@@ -21,7 +21,7 @@
 F32 = jnp.float32
 BF16 = jnp.bfloat16
 VMEM_LIMIT = 20 * 1024 * 1024
-LARGE_LIMIT = 56 * 1024 * 1024
+LARGE_LIMIT = 55 * 1024 * 1024
 SMEM_SPEC = pl.BlockSpec(memory_space=pltpu.SMEM)
 
 
@@ -131,32 +131,34 @@
     )(table, *blocks)
 
 
-def pack_kernel(comp, pos_ref, x_ref, *refs):
-    outs, sems = refs[:-1], refs[-1]
-    copies = [
-        pltpu.make_async_copy(x_ref.at[comp, :, line_of(pos_ref[1], d), :], out, sems.at[d])
-        for d, out in enumerate(outs)
-    ]
-    for copy in copies:
-        copy.start()
-    for copy in copies:
-        copy.wait()
+def pack_kernel(pos_ref, *refs):
+    count = len(refs) // 2
+    for source, target in zip(refs[:count], refs[count:]):
+        target[...] = source[0]
 
 
 def pack(position, adjoint, comp, limit):
     _, per, nodes, elements = adjoint.shape
     lines = nodes // LINE
+    block = per // 2
+
+    def source(d):
+        return pl.BlockSpec((1, block, LINE, elements), lambda i, pos: (comp, i, pos[1] ^ d, 0))
+
     size = per * nodes * elements
     return pl.pallas_call(
-        functools.partial(pack_kernel, comp),
+        pack_kernel,
         out_shape=[jax.ShapeDtypeStruct((per, LINE, elements), F32)] * lines,
-        in_specs=[SMEM_SPEC, pl.BlockSpec(memory_space=pltpu.HBM)],
-        out_specs=[pl.BlockSpec(memory_space=pl.ANY)] * lines,
-        scratch_shapes=[pltpu.SemaphoreType.DMA((lines,))],
+        grid_spec=pltpu.PrefetchScalarGridSpec(
+            num_scalar_prefetch=1,
+            grid=(per // block,),
+            in_specs=[source(d) for d in range(lines)],
+            out_specs=[pl.BlockSpec((block, LINE, elements), lambda i, pos: (i, 0, 0))] * lines,
+        ),
         compiler_params=params(limit),
         cost_estimate=cost(0, 8 * size),
         name="pack",
-    )(position, adjoint)
+    )(position, *[adjoint] * lines)
 
 
 BXR, BYS, DXBX, DXBY, DYBX, DYBY, DIAG = range(7)
@@ -173,7 +175,7 @@
 
 def prep_kernel(
     pos_ref, bank_ref, snap_ref, geo_ref, dr_ref, ds_ref, st_ref, up_ref, lo_ref,
-    coef_ref, dpack_ref, spack_ref, gather_ref, scatter_ref, mask_ref,
+    coef_ref, dpack_ref, spack_ref, gather_ref, scatter_ref, mask_ref, face_ref,
 ):
     elements = geo_ref.shape[1]
     nodes = dr_ref.shape[0]
@@ -213,6 +215,7 @@
     spack_ref[...] = pack_matrix(jnp.where(row == col, 0.0, permuted(st_ref)))
     coef_ref[DIAG] = jnp.broadcast_to(diag, (nodes, elements))
     shared = up_ref.shape[1]
+    mass = jnp.broadcast_to(1.0 / (rx * sy), (16, elements))
     for side, (ref, first) in enumerate(((up_ref, LINE - 1), (lo_ref, 0))):
         index = ref[...]
         node = index // elements
@@ -225,6 +228,12 @@
         mask = (lax.broadcasted_iota(jnp.int32, (lines, shared), 0) ^ me) == node // LINE
         mask = jnp.where(mask, 1.0, 0.0)
         mask_ref[side] = mask
+        high, low = split(mass)
+        rest = (mass - high.astype(F32) - low.astype(F32)).astype(BF16)
+        at_face = sum(dot(part, gather_ref[side])[:1] for part in (high, low, rest))
+        face_ref[side, 0:1, :] = at_face
+        lead = jnp.concatenate([diag[s * LINE + first : s * LINE + first + 1] for s in range(lines)], axis=0)
+        face_ref[side, 1:2, :] = PENALTY + jnp.sum(mask * lead, axis=0, keepdims=True)
         count = dot(mask.astype(BF16), back)
         for s in range(lines):
             n = s * LINE + first
@@ -244,6 +253,7 @@
             jax.ShapeDtypeStruct((2, elements, shared), BF16),
             jax.ShapeDtypeStruct((2, shared, elements), BF16),
             jax.ShapeDtypeStruct((2, nodes // LINE, shared), F32),
+            jax.ShapeDtypeStruct((2, 2, shared), F32),
         ],
         in_specs=[SMEM_SPEC] + [pl.BlockSpec(memory_space=pltpu.VMEM)] * 8,
         compiler_params=params(),
@@ -316,9 +326,9 @@
         pot_ref[rows, :] = pot
         local_ref[rows, :] = local_sweep(pot, source, inverse, spack)
     for side, out in ((0, up_ref), (1, lo_ref)):
-        fields = [face_of(ref, side)[...] for ref in (pot_ref, local_ref, inverse_ref)]
+        fields = [face_of(ref, side)[...] for ref in (pot_ref, local_ref)]
         picked = gather_faces(side, fields, gather_ref, mask_ref)
-        for k in range(3):
+        for k in range(2):
             out[k] = picked[k * block : (k + 1) * block]
 
 
@@ -333,12 +343,12 @@
     block = coef_block(coefs)
     field = [pl.BlockSpec((block, part, elements), lambda i: (i, 0, 0))] * len(z)
     flat = pl.BlockSpec((block * nodes, elements), lambda i: (i, 0))
-    face = pl.BlockSpec((3, block, shared), lambda i: (0, i, 0))
+    face = pl.BlockSpec((2, block, shared), lambda i: (0, i, 0))
     size = coefs * nodes * elements
     return pl.pallas_call(
         functools.partial(start_kernel, block, len(z)),
         out_shape=[jax.ShapeDtypeStruct((coefs * nodes, elements), F32)] * 3
-        + [jax.ShapeDtypeStruct((3, coefs, shared), F32)] * 2,
+        + [jax.ShapeDtypeStruct((2, coefs, shared), F32)] * 2,
         grid=(coefs // block,),
         in_specs=[
             SMEM_SPEC, whole(geometry.shape),
@@ -354,22 +364,28 @@
     )(position, geometry, coef, dpack, spack, gather, mask, *z, *x)
 
 
+def face_inverse(face, first, coefs):
+    index = first + lax.broadcasted_iota(jnp.int32, (coefs, 1), 0)
+    wave = jnp.where(index == 1, PLANES // 2, index // 2).astype(F32)
+    shift = (4.0 / PLANES) * wave
+    shift = shift * shift
+    return RELAXATION / (face[1:2] + shift * face[0:1])
+
+
 def sweeps_kernel(
-    block, keep, local_ref, source_ref, inverse_ref, own_up_ref, own_lo_ref,
-    own_inv_up_ref, own_inv_lo_ref, got_up_ref, got_lo_ref, inv_up_ref, inv_lo_ref, spack_ref, gather_ref, scatter_ref, mask_ref,
-    next_ref, up_ref, lo_ref, pot_ref,
+    block, keep, pos_ref, local_ref, source_ref, inverse_ref, own_up_ref, own_lo_ref,
+    got_up_ref, got_lo_ref, face_ref, far_up_ref, far_lo_ref, spack_ref, gather_ref, scatter_ref,
+    mask_ref, next_ref, up_ref, lo_ref, pot_ref,
 ):
     nodes = spack_ref.shape[0]
     spack = spack_ref[...]
     lines = block * (nodes // LINE)
+    first = pos_ref[0] * (block * pl.num_programs(0)) + pl.program_id(0) * block
     partners = []
-    for side, own, own_inv, got, inv in (
-        (0, own_up_ref, own_inv_up_ref, got_up_ref, inv_up_ref),
-        (1, own_lo_ref, own_inv_lo_ref, got_lo_ref, inv_lo_ref),
-    ):
-        scale = PENALTY * own_inv[0]
+    for side, own, got, far in ((0, own_up_ref, got_up_ref, far_up_ref), (1, own_lo_ref, got_lo_ref, far_lo_ref)):
+        scale = PENALTY * face_inverse(face_ref[side], first, block)
         now = scale * got[0]
-        later = scale * (got[1] + PENALTY * inv[0] * own[0])
+        later = scale * (got[1] + PENALTY * face_inverse(far[...], first, block) * own[0])
         both = scatter_faces(side, jnp.concatenate([now, later], axis=0), scatter_ref, mask_ref)
         partners.append((both[:lines], both[lines:]))
     pot_ref[...] = local_ref[...]
@@ -392,7 +408,7 @@
             out[k] = picked[k * block : (k + 1) * block]
 
 
-def two_sweeps(keep, local, source, inverse, own, own_inv, got, inv, spack, gather, scatter, mask):
+def two_sweeps(keep, position, local, source, inverse, own, got, face, far, spack, gather, scatter, mask):
     nodes = spack.shape[0]
     elements = local.shape[1]
     coefs = local.shape[0] // nodes
@@ -401,8 +417,7 @@
     flat = pl.BlockSpec((block * nodes, elements), lambda i: (i, 0))
     one = pl.BlockSpec((1, block, shared), lambda i: (0, i, 0))
     two = pl.BlockSpec((2, block, shared), lambda i: (0, i, 0))
-    third = pl.BlockSpec((1, block, shared), lambda i: (2, i, 0))
-    face = pl.BlockSpec((keep, block, shared), lambda i: (0, i, 0))
+    kept = pl.BlockSpec((keep, block, shared), lambda i: (0, i, 0))
     size = coefs * nodes * elements
     return pl.pallas_call(
         functools.partial(sweeps_kernel, block, keep),
@@ -410,15 +425,16 @@
         + [jax.ShapeDtypeStruct((keep, coefs, shared), F32)] * 2,
         grid=(coefs // block,),
         in_specs=[
-            flat, flat, flat, one, one, third, third, two, two, third, third,
+            SMEM_SPEC, flat, flat, flat, one, one, two, two,
+            whole(face.shape), whole(far[0].shape), whole(far[1].shape),
             whole(spack.shape), whole(gather.shape), whole(scatter.shape), whole(mask.shape),
         ],
-        out_specs=[flat, face, face],
+        out_specs=[flat, kept, kept],
         scratch_shapes=[pltpu.VMEM((block * nodes, elements), F32)],
         compiler_params=params(),
         cost_estimate=SHORT,
         name="two_sweeps",
-    )(local, source, inverse, *own, *own_inv, *got, *inv, spack, gather, scatter, mask)
+    )(position, local, source, inverse, *own, *got, face, *far, spack, gather, scatter, mask)
 
 
 def store_own(ref, me, value, *lead):
@@ -462,18 +478,18 @@
 
 
 def force_kernel(
-    block, pos_ref, local_ref, inv_up_ref, inv_lo_ref, got_up_ref, got_lo_ref, geo_ref, dpack_ref,
+    block, pos_ref, local_ref, got_up_ref, got_lo_ref, face_ref, geo_ref, dpack_ref,
     scatter_ref, mask_ref, px_ref, pz_ref, o_ref, x_ref, pot_ref,
 ):
     nodes = dpack_ref.shape[0] // 2
     scale = TIME_STEP * INTERACTION
     me = pos_ref[1]
     pot_ref[...] = local_ref[...]
-    for side, inv, got in ((0, inv_up_ref, got_up_ref), (1, inv_lo_ref, got_lo_ref)):
+    first = pos_ref[0] * (block * pl.num_programs(0)) + pl.program_id(0) * block
+    for side, got in ((0, got_up_ref), (1, got_lo_ref)):
         face = face_of(pot_ref, side)
-        partner = PENALTY * inv[0] * got[0]
+        partner = PENALTY * face_inverse(face_ref[side], first, block) * got[0]
         face[...] = face[...] + scatter_faces(side, partner, scatter_ref, mask_ref)
-    first = pos_ref[0] * (block * pl.num_programs(0)) + pl.program_id(0) * block
     drpack = dpack_ref[:nodes]
     slope_scale = scale * geo_ref[0:1, :]
     for c in range(block):
@@ -486,13 +502,12 @@
         x_ref[other] = px_ref[other] + factor * pot
 
 
-def add_force(position, local, own_inv, got, geometry, dpack, scatter, mask, px, pz):
+def add_force(position, local, got, face, geometry, dpack, scatter, mask, px, pz):
     coefs, nodes, elements = px.shape
     shared = scatter.shape[1]
     block = coef_block(coefs)
     flat = pl.BlockSpec((block * nodes, elements), lambda i: (i, 0))
     one = pl.BlockSpec((1, block, shared), lambda i: (0, i, 0))
-    third = pl.BlockSpec((1, block, shared), lambda i: (2, i, 0))
     part = pl.BlockSpec((block, nodes, elements), lambda i: (i, 0, 0))
     return pl.pallas_call(
         functools.partial(force_kernel, block),
@@ -502,7 +517,7 @@
         ],
         grid=(coefs // block,),
         in_specs=[
-            SMEM_SPEC, flat, third, third, one, one, whole(geometry.shape), whole(dpack.shape),
+            SMEM_SPEC, flat, one, one, whole(face.shape), whole(geometry.shape), whole(dpack.shape),
             whole(scatter.shape), whole(mask.shape), part, part,
         ],
         out_specs=[pl.BlockSpec((1, block, nodes, elements), lambda i: (2, i, 0, 0)), part],
@@ -510,7 +525,7 @@
         compiler_params=params(),
         cost_estimate=SHORT,
         name="add_force",
-    )(position, local, *own_inv, *got, geometry, dpack, scatter, mask, px, pz)
+    )(position, local, *got, face, geometry, dpack, scatter, mask, px, pz)
 
 
 def finish_kernel(block, count, pos_ref, coef_ref, dpack_ref, px_ref, py_ref, filled_ref, *refs):
@@ -624,11 +639,12 @@
     )
     z_coefs = transform(z_columns(), table)
     z_coefs, constants = tie(z_coefs, constants)
-    coef, dpack, spack, gather, scatter, mask = constants
+    coef, dpack, spack, gather, scatter, mask, face = constants
+    far = swap_faces(face[0], face[1])
     z_later = collect(z_coefs)
     y_blocks = columns(1)
     x_coefs = transform(x_columns(), table)
-    x_coefs, y_blocks = tie(x_coefs, y_blocks)
+    x_coefs, (y_blocks, far) = tie(x_coefs, (y_blocks, far))
     x_later = collect(x_coefs)
     y_columns = spread(y_blocks)
     z = z_later()
@@ -636,22 +652,31 @@
     source, inverse, local, up, lo = start_solve(
         position, z, x, geometry, coef, dpack, spack, gather, mask
     )
-    own_inv = (up, lo)
     got = swap_faces(up, lo)
-    inv = got
-    px, py, pz = partial_update(z, x, coef, dpack)
+    parts = partial_update(z, x, coef, dpack)
+    local, (px, py, pz) = lax.optimization_barrier((local, parts))
     local, up, lo = two_sweeps(
-        2, local, source, inverse, (up, lo), own_inv, got, inv, spack, gather, scatter, mask
+        2, position, local, source, inverse, (up, lo), got, face, far, spack, gather, scatter, mask
     )
     y_got = y_columns()
     y_got[0], local = lax.optimization_barrier((y_got[0], local))
     got = swap_faces(up, lo)
+    begun = len(flight)
     y_later = collect(transform(y_got, table))
+
+    def after(value, first, last):
+        here = slice(begun + first, begun + last)
+        value, flight[here] = lax.optimization_barrier((value, flight[here]))
+        return value
+
+    local = after(local, 0, 2)
     local, up, lo = two_sweeps(
-        1, local, source, inverse, (up, lo), own_inv, got, inv, spack, gather, scatter, mask
+        1, position, local, source, inverse, (up, lo), got, face, far, spack, gather, scatter, mask
     )
+    up, lo = after((up, lo), 2, 4)
     got = swap_faces(up, lo)
-    filled, px = add_force(position, local, own_inv, got, geometry, dpack, scatter, mask, px, pz)
+    local = after(local, 4, 5)
+    filled, px = add_force(position, local, got, face, geometry, dpack, scatter, mask, px, pz)
     return finish(position, y_later(), coef, dpack, px, py, filled)
 
 

time: 243 us -> 178 us (0.73)
  Pallas kernels: 103 us -> 42.9 us
  waiting for transfers between devices: 83.6 us -> 76.6 us
  starting transfers between devices: 55 us -> 57.7 us
    pallas_call x3, Pallas kernels: 67.1 us -> 6.1 us  [pack(): pl.pallas_call(pack_kernel, out_shape=[jax.ShapeDtypeStruct((per, LINE, e...]
    ppermute x6 -> x8, waiting for transfers between devices: 15.1 us -> 6.29 us  [swap_faces(): return (lax.ppermute(lo, 'dom', down_way), lax.ppermute(up, 'dom', up_way))]
    ppermute x6 -> x8, starting transfers between devices: 8.88 us -> 15.3 us  [swap_faces(): return (lax.ppermute(lo, 'dom', down_way), lax.ppermute(up, 'dom', up_way))]
    ppermute x42, starting transfers between devices: 46.1 us -> 42.4 us  [exchange(): lax.ppermute(block, 'four', [(i, i ^ d) for i in range(peers)])]
  transfers between devices with their start and end apart: 48 -> 50, of which waited for: 25 -> 28; matrix products, arithmetic and copies ran while one was open for 0% -> 0% of each run, Pallas kernels for 13% -> 18%
where the time goes in v7:
time: 178 us
  waiting for transfers between devices  76.6 us (43%)
  starting transfers between devices  57.7 us (32%)
  Pallas kernels  42.9 us (24%)
    ppermute x42, waiting for transfers between devices, exchange(): lax.ppermute(block, 'four', [(i, i ^ d) for i in range(peers)])  70.4 us
    ppermute x42, starting transfers between devices, exchange(): lax.ppermute(block, 'four', [(i, i ^ d) for i in range(peers)])  42.4 us
    ppermute x8, starting transfers between devices, swap_faces(): return (lax.ppermute(lo, 'dom', down_way), lax.ppermute(up, 'dom', up_way))  15.3 us
    pallas_call x2, Pallas kernels, two_sweeps(): pl.pallas_call(functools.partial(sweeps_kernel, block, keep), out_shape=[...  12.3 us
    pallas_call x3, Pallas kernels, transform(): pl.pallas_call(functools.partial(transform_kernel, count), out_shape=[jax...  7.35 us
    ppermute x8, waiting for transfers between devices, swap_faces(): return (lax.ppermute(lo, 'dom', down_way), lax.ppermute(up, 'dom', up_way))  6.29 us
    pallas_call x3, Pallas kernels, pack(): pl.pallas_call(pack_kernel, out_shape=[jax.ShapeDtypeStruct((per, LINE, e...  6.1 us
    pallas_call x1, Pallas kernels, start_solve(): pl.pallas_call(functools.partial(start_kernel, block, len(z)), out_shape=...  4.25 us
  transfers between devices with their start and end apart: 50, of which 28 were waited for; matrix products, arithmetic and copies ran while one was open for 0% of the time, Pallas kernels for 18%

profile of v7, /device:TPU:0, one launch (start us, length us, event | category | flops | bytes accessed | tf_op | source)
XLA Modules:
  0.0 178.2 jit_solution(15951269843473719285)
XLA Ops:
  0.6 4.0 %pack.4 = (f32[32,8,256]{2,1,0:T(8,128)}, f32[32,8,256]{2,1,0:T(8,128)}, f32[32,8,256]{2,1,0:T(8,128)}, f32[32,8,256]{2,1,0:T(8,128)}, f32[32,8,256]{2,1,0:T(8,1...) custom-call(s32[2]{0:T(128)} %pad_add_fusion.pos_ref, f32[3,32,64,256]{3,2,1,0:T(8,128)} %refs_7_.5, ...), custom_call_target="tpu_custom_call" | custom-call | bytes 4194304 | tf_op jit(solution)/shard_map/pack/pallas_call | solution.py:149
  4.5 3.0 %collective-permute-start = (f32[32,8,256]{2,1,0:T(8,128)}, f32[32,8,256]{2,1,0:T(8,128)S(1)}, u32[]{:S(2)}, u32[]{:S(2)}) collective-permute-start(f32[32,8,256]{2,1,0:T(8,128)} %get-tuple-element.186), channel_id=1, source_target_pairs={{0,4},{1,5},{2,6},{3,7},{4,0},{5,1},{6,2},{7,3},{8,12},{9,13},{10,... | collective-permute-start | bytes 786440 | tf_op jit(solution)/shard_map/ppermute | solution.py:606
  10.0 2.1 %collective-permute-start.4 = (f32[32,8,256]{2,1,0:T(8,128)}, f32[32,8,256]{2,1,0:T(8,128)S(1)}, u32[]{:S(2)}, u32[]{:S(2)}) collective-permute-start(f32[32,8,256]{2,1,0:T(8,128)} %get-tuple-element.197), channel_id=1, source_target_pairs={{0,5},{1,4},{2,7},{3,6},{4,1},{5,0},{6,3},{7,2},{8,13},{9,12},{10,... | collective-permute-start | bytes 786440 | tf_op jit(solution)/shard_map/ppermute | solution.py:606
  14.5 2.5 %collective-permute-done.2.refs_2_ = f32[32,8,256]{2,1,0:T(8,128)S(1)} collective-permute-done((f32[32,8,256]{2,1,0:T(8,128)}, f32[32,8,256]{2,1,0:T(8,128)S(1)}, u32[]{:S(2)}, u32[]{:S(2)}) %collective-permute-start.2) | collective-permute-done | bytes 262176 | tf_op jit(solution)/shard_map/ppermute | solution.py:606
  18.0 3.7 %collective-permute-done.3.refs_3_ = f32[32,8,256]{2,1,0:T(8,128)S(1)} collective-permute-done((f32[32,8,256]{2,1,0:T(8,128)}, f32[32,8,256]{2,1,0:T(8,128)S(1)}, u32[]{:S(2)}, u32[]{:S(2)}) %collective-permute-start.3) | collective-permute-done | bytes 262176 | tf_op jit(solution)/shard_map/ppermute | solution.py:606
  22.2 5.6 %collective-permute-done.5.refs_6_ = f32[32,8,256]{2,1,0:T(8,128)S(1)} collective-permute-done((f32[32,8,256]{2,1,0:T(8,128)}, f32[32,8,256]{2,1,0:T(8,128)S(1)}, u32[]{:S(2)}, u32[]{:S(2)}) %collective-permute-start.5) | collective-permute-done | bytes 262176 | tf_op jit(solution)/shard_map/ppermute | solution.py:606
  27.8 2.0 %collective-permute-start.9 = (f32[32,8,256]{2,1,0:T(8,128)S(1)}, f32[32,8,256]{2,1,0:T(8,128)S(1)}, u32[]{:S(2)}, u32[]{:S(2)}) collective-permute-start(f32[32,8,256]{2,1,0:T(8,128)S(1)} %get-tuple-element.222), channel_id=1, source_target_pairs={{0,2},{1,3},{2,0},{3,1},{4,6},{5,7},{6,4},{7,5},{8,10},{9,11},{10,... | collective-permute-start | bytes 786440 | tf_op jit(solution)/shard_map/ppermute | solution.py:606
  32.9 1.9 %collective-permute-start.10 = (f32[32,8,256]{2,1,0:T(8,128)S(1)}, f32[32,8,256]{2,1,0:T(8,128)S(1)}, u32[]{:S(2)}, u32[]{:S(2)}) collective-permute-start(f32[32,8,256]{2,1,0:T(8,128)S(1)} %get-tuple-element.225), channel_id=1, source_target_pairs={{0,3},{1,2},{2,1},{3,0},{4,7},{5,6},{6,5},{7,4},{8,11},{9,10},{10,... | collective-permute-start | bytes 786440 | tf_op jit(solution)/shard_map/ppermute | solution.py:606
  34.8 4.1 %collective-permute-done.7.refs_4_ = f32[32,8,256]{2,1,0:T(8,128)S(1)} collective-permute-done((f32[32,8,256]{2,1,0:T(8,128)S(1)}, f32[32,8,256]{2,1,0:T(8,128)S(1)}, u32[]{:S(2)}, u32[]{:S(2)}) %collective-permute-start.7) | collective-permute-done | bytes 262176 | tf_op jit(solution)/shard_map/ppermute | solution.py:606
  39.5 2.2 %collective-permute-start.13 = (f32[32,8,256]{2,1,0:T(8,128)S(1)}, f32[32,8,256]{2,1,0:T(8,128)S(1)}, u32[]{:S(2)}, u32[]{:S(2)}) collective-permute-start(f32[32,8,256]{2,1,0:T(8,128)S(1)} %get-tuple-element.235), channel_id=1, source_target_pairs={{0,7},{1,6},{2,5},{3,4},{4,3},{5,2},{6,1},{7,0},{8,15},{9,14},{10,... | collective-permute-start | bytes 786440 | tf_op jit(solution)/shard_map/ppermute | solution.py:606
  41.7 2.4 %transform.3 = (f32[32,8,256]{2,1,0:T(8,128)S(1)}, f32[32,8,256]{2,1,0:T(8,128)S(1)}, f32[32,8,256]{2,1,0:T(8,128)S(1)}, f32[32,8,256]{2,1,0:T(8,128)S(1)}, f32[...) custom-call(bf16[512,256]{1,0:T(8,128)(2,1)S(1)} %permuted_table.1.tab, ...), custom_call_target="tpu_custom_call" | custom-call | flops 805306368 | bytes 4194304 | tf_op jit(solution)/shard_map/transform/pallas_call | solution.py:122
  44.7 2.0 %collective-permute-start.18 = (f32[32,8,256]{2,1,0:T(8,128)S(1)}, f32[32,8,256]{2,1,0:T(8,128)S(1)}, u32[]{:S(2)}, u32[]{:S(2)}) collective-permute-start(f32[32,8,256]{2,1,0:T(8,128)S(1)} %get-tuple-element.258), channel_id=1, source_target_pairs={{0,2},{1,3},{2,0},{3,1},{4,6},{5,7},{6,4},{7,5},{8,10},{9,11},{10,... | collective-permute-start | bytes 786440 | tf_op jit(solution)/shard_map/ppermute | solution.py:606
  46.6 3.2 %collective-permute-done.10.refs_3_ = f32[32,8,256]{2,1,0:T(8,128)S(1)} collective-permute-done((f32[32,8,256]{2,1,0:T(8,128)S(1)}, f32[32,8,256]{2,1,0:T(8,128)S(1)}, u32[]{:S(2)}, u32[]{:S(2)}) %collective-permute-start.10) | collective-permute-done | bytes 262176 | tf_op jit(solution)/shard_map/ppermute | solution.py:606
  49.8 1.6 collective-permute-start.15
  52.1 3.4 %collective-permute-done.13.refs_7_ = f32[32,8,256]{2,1,0:T(8,128)S(1)} collective-permute-done((f32[32,8,256]{2,1,0:T(8,128)S(1)}, f32[32,8,256]{2,1,0:T(8,128)S(1)}, u32[]{:S(2)}, u32[]{:S(2)}) %collective-permute-start.13) | collective-permute-done | bytes 262176 | tf_op jit(solution)/shard_map/ppermute | solution.py:606
  55.9 2.6 %collective-permute-start.19 = (f32[32,8,256]{2,1,0:T(8,128)S(1)}, f32[32,8,256]{2,1,0:T(8,128)S(1)}, u32[]{:S(2)}, u32[]{:S(2)}) collective-permute-start(f32[32,8,256]{2,1,0:T(8,128)S(1)} %get-tuple-element.261), channel_id=1, source_target_pairs={{0,3},{1,2},{2,1},{3,0},{4,7},{5,6},{6,5},{7,4},{8,11},{9,10},{10,... | collective-permute-start | bytes 786440 | tf_op jit(solution)/shard_map/ppermute | solution.py:606
  58.5 2.8 %collective-permute-done.18.refs_2_ = f32[32,8,256]{2,1,0:T(8,128)S(1)} collective-permute-done((f32[32,8,256]{2,1,0:T(8,128)S(1)}, f32[32,8,256]{2,1,0:T(8,128)S(1)}, u32[]{:S(2)}, u32[]{:S(2)}) %collective-permute-start.18) | collective-permute-done | bytes 262176 | tf_op jit(solution)/shard_map/ppermute | solution.py:606
  61.3 3.6 %collective-permute-start.14 = (f32[2,512]{1,0:T(2,128)S(1)}, f32[2,512]{1,0:T(2,128)S(1)}, u32[]{:S(2)}, u32[]{:S(2)}) collective-permute-start(f32[2,512]{1,0:T(2,128)S(1)} %get-tuple-element.358), channel_id=1, source_target_pairs={{8,0},{16,8},{24,16},{0,24},{9,1},{17,9},{25,17},{1,25},{10,2},{18... | collective-permute-start | bytes 12296 | tf_op jit(solution)/shard_map/ppermute | solution.py:576
  68.7 2.5 %transform.4 = (f32[32,8,256]{2,1,0:T(8,128)S(1)}, f32[32,8,256]{2,1,0:T(8,128)S(1)}, f32[32,8,256]{2,1,0:T(8,128)S(1)}, f32[32,8,256]{2,1,0:T(8,128)S(1)}, f32[...) custom-call(bf16[512,256]{1,0:T(8,128)(2,1)S(1)} %permuted_table.1.tab, ...), custom_call_target="tpu_custom_call" | custom-call | flops 805306368 | bytes 4194304 | tf_op jit(solution)/shard_map/transform/pallas_call | solution.py:122
  72.0 1.5 collective-permute-start.23
  73.5 3.8 %collective-permute-done.22.refs_7_ = f32[32,8,256]{2,1,0:T(8,128)S(1)} collective-permute-done((f32[32,8,256]{2,1,0:T(8,128)S(1)}, f32[32,8,256]{2,1,0:T(8,128)S(1)}, u32[]{:S(2)}, u32[]{:S(2)}) %collective-permute-start.22) | collective-permute-done | bytes 262176 | tf_op jit(solution)/shard_map/ppermute | solution.py:606
  77.3 1.8 %collective-permute-start.26 = (f32[32,8,256]{2,1,0:T(8,128)S(1)}, f32[32,8,256]{2,1,0:T(8,128)S(1)}, u32[]{:S(2)}, u32[]{:S(2)}) collective-permute-start(f32[32,8,256]{2,1,0:T(8,128)S(1)} %get-tuple-element.283), channel_id=1, source_target_pairs={{0,3},{1,2},{2,1},{3,0},{4,7},{5,6},{6,5},{7,4},{8,11},{9,10},{10,... | collective-permute-start | bytes 786440 | tf_op jit(solution)/shard_map/ppermute | solution.py:606
  81.5 2.4 %collective-permute-done.25.refs_10_ = f32[32,8,256]{2,1,0:T(8,128)S(1)} collective-permute-done((f32[32,8,256]{2,1,0:T(8,128)S(1)}, f32[32,8,256]{2,1,0:T(8,128)S(1)}, u32[]{:S(2)}, u32[]{:S(2)}) %collective-permute-start.25) | collective-permute-done | bytes 262176 | tf_op jit(solution)/shard_map/ppermute | solution.py:606
  83.9 2.7 %collective-permute-start.27 = (f32[32,8,256]{2,1,0:T(8,128)S(1)}, f32[32,8,256]{2,1,0:T(8,128)S(1)}, u32[]{:S(2)}, u32[]{:S(2)}) collective-permute-start(f32[32,8,256]{2,1,0:T(8,128)S(1)} %get-tuple-element.287), channel_id=1, source_target_pairs={{0,5},{1,4},{2,7},{3,6},{4,1},{5,0},{6,3},{7,2},{8,13},{9,12},{10,... | collective-permute-start | bytes 786440 | tf_op jit(solution)/shard_map/ppermute | solution.py:606
  86.6 1.9 %collective-permute-done.26.refs_11_ = f32[32,8,256]{2,1,0:T(8,128)S(1)} collective-permute-done((f32[32,8,256]{2,1,0:T(8,128)S(1)}, f32[32,8,256]{2,1,0:T(8,128)S(1)}, u32[]{:S(2)}, u32[]{:S(2)}) %collective-permute-start.26) | collective-permute-done | bytes 262176 | tf_op jit(solution)/shard_map/ppermute | solution.py:606
  89.0 6.0 %collective-permute-done.28.refs_14_ = f32[32,8,256]{2,1,0:T(8,128)S(1)} collective-permute-done((f32[32,8,256]{2,1,0:T(8,128)S(1)}, f32[32,8,256]{2,1,0:T(8,128)S(1)}, u32[]{:S(2)}, u32[]{:S(2)}) %collective-permute-start.28) | collective-permute-done | bytes 262176 | tf_op jit(solution)/shard_map/ppermute | solution.py:606
  95.1 1.6 collective-permute-start.34
  96.7 3.1 %collective-permute-done.29.refs_15_ = f32[32,8,256]{2,1,0:T(8,128)S(1)} collective-permute-done((f32[32,8,256]{2,1,0:T(8,128)S(1)}, f32[32,8,256]{2,1,0:T(8,128)S(1)}, u32[]{:S(2)}, u32[]{:S(2)}) %collective-permute-start.29) | collective-permute-done | bytes 262176 | tf_op jit(solution)/shard_map/ppermute | solution.py:606
  99.8 4.4 %collective-permute-done.27.refs_13_ = f32[32,8,256]{2,1,0:T(8,128)S(1)} collective-permute-done((f32[32,8,256]{2,1,0:T(8,128)S(1)}, f32[32,8,256]{2,1,0:T(8,128)S(1)}, u32[]{:S(2)}, u32[]{:S(2)}) %collective-permute-start.27) | collective-permute-done | bytes 262176 | tf_op jit(solution)/shard_map/ppermute | solution.py:606
  104.3 4.3 %start_solve.1 = (f32[2048,256]{1,0:T(8,128)S(1)}, f32[2048,256]{1,0:T(8,128)S(1)}, f32[2048,256]{1,0:T(8,128)S(1)}, f32[2,32,512]{2,1,0:T(8,128)S(1)}, f32[2,32,512]{2,1,0:T(8,128)S(1)}) custom-call(s32[2]{0:T(128)S(1)} %copy-done.2, f32[2,256]{1,0:T(2,128)S(1)} %copy-done.6, f32[7,64,256]{2,1,0:T(8,128)S(1)} %get-tuple-element.213.diag_ref.coef_ref, ...), custom_call_target="tpu_custom_call" | custom-call | flops 1000000 | bytes 100000 | tf_op jit(solution)/shard_map/start_solve/pallas_call | solution.py:348
  108.5 1.6 collective-permute-start.31
  110.1 2.3 %collective-permute-start.30 = (f32[2,32,512]{2,1,0:T(8,128)S(1)}, f32[2,32,512]{2,1,0:T(8,128)S(1)}, u32[]{:S(2)}, u32[]{:S(2)}) collective-permute-start(f32[2,32,512]{2,1,0:T(8,128)S(1)} %get-tuple-element.303.own_lo_ref), channel_id=1, source_target_pairs={{8,0},{16,8},{24,16},{0,24},{9,1},{17,9},{25,17},{1,25},{10,2},{18... | collective-permute-start | bytes 393224 | tf_op jit(solution)/shard_map/ppermute | solution.py:576
  113.4 2.0 %collective-permute-start.38 = (f32[32,8,256]{2,1,0:T(8,128)S(1)}, f32[32,8,256]{2,1,0:T(8,128)S(1)}, u32[]{:S(2)}, u32[]{:S(2)}) collective-permute-start(f32[32,8,256]{2,1,0:T(8,128)S(1)} %get-tuple-element.320), channel_id=1, source_target_pairs={{0,7},{1,6},{2,5},{3,4},{4,3},{5,2},{6,1},{7,0},{8,15},{9,14},{10,... | collective-permute-start | bytes 786440 | tf_op jit(solution)/shard_map/ppermute | solution.py:606
  115.4 1.5 collective-permute-done.31.got_lo_ref
  116.9 2.1 %collective-permute-done.30.got_up_ref = f32[2,32,512]{2,1,0:T(8,128)S(1)} collective-permute-done((f32[2,32,512]{2,1,0:T(8,128)S(1)}, f32[2,32,512]{2,1,0:T(8,128)S(1)}, u32[]{:S(2)}, u32[]{:S(2)}) %collective-permute-start.30) | collective-permute-done | bytes 131104 | tf_op jit(solution)/shard_map/ppermute | solution.py:576
  119.4 2.8 %partial_update.1 = (f32[32,64,256]{2,1,0:T(8,128)S(1)}, f32[32,64,256]{2,1,0:T(8,128)S(1)}, f32[32,64,256]{2,1,0:T(8,128)S(1)}) custom-call(f32[7,64,256]{2,1,0:T(8,128)S(1)} %get-tuple-element.213.diag_ref.coef_ref, bf16[128,192]{1,0:T(8,128)(2,1)S(1)} %get-tuple-element.214.dpack_ref, f32[32,8,256]{2,1,0:T(8,128)S(1)} %get-tuple-element.251.refs_0_, ...), custom_call_target="tpu_custom_call" | custom-call | flops 1000000 | bytes 100000 | tf_op jit(solution)/shard_map/partial_update/pallas_call | solution.py:468
  122.2 5.9 %two_sweeps.2 = (f32[2048,256]{1,0:T(8,128)S(1)}, f32[2,32,512]{2,1,0:T(8,128)S(1)}, f32[2,32,512]{2,1,0:T(8,128)S(1)}) custom-call(s32[2]{0:T(128)S(1)} %copy-done.2, f32[2048,256]{1,0:T(8,128)S(1)} %get-tuple-element.299.local_ref, f32[2048,256]{1,0:T(8,128)S(1)} %get-tuple-element.300.source_ref, f32[2048,256]{1,0:T(8,128)S(1)} %get-tuple-element.301.inverse_ref, ...), custom_call_target="tpu_custom_call" | custom-call | flops 1000000 | bytes 100000 | tf_op jit(solution)/shard_map/two_sweeps/pallas_call | solution.py:422
  128.2 4.4 %collective-permute-done.37.refs_6_ = f32[32,8,256]{2,1,0:T(8,128)S(1)} collective-permute-done((f32[32,8,256]{2,1,0:T(8,128)S(1)}, f32[32,8,256]{2,1,0:T(8,128)S(1)}, u32[]{:S(2)}, u32[]{:S(2)}) %collective-permute-start.37) | collective-permute-done | bytes 262176 | tf_op jit(solution)/shard_map/ppermute | solution.py:606
  132.6 5.3 %collective-permute-done.36.refs_5_ = f32[32,8,256]{2,1,0:T(8,128)S(1)} collective-permute-done((f32[32,8,256]{2,1,0:T(8,128)S(1)}, f32[32,8,256]{2,1,0:T(8,128)S(1)}, u32[]{:S(2)}, u32[]{:S(2)}) %collective-permute-start.36) | collective-permute-done | bytes 262176 | tf_op jit(solution)/shard_map/ppermute | solution.py:606
  137.9 2.4 %transform.5 = (f32[32,8,256]{2,1,0:T(8,128)S(1)}, f32[32,8,256]{2,1,0:T(8,128)S(1)}, f32[32,8,256]{2,1,0:T(8,128)S(1)}, f32[32,8,256]{2,1,0:T(8,128)S(1)}, f32[...) custom-call(bf16[512,256]{1,0:T(8,128)(2,1)S(1)} %permuted_table.1.tab, ...), custom_call_target="tpu_custom_call" | custom-call | flops 805306368 | bytes 4194304 | tf_op jit(solution)/shard_map/transform/pallas_call | solution.py:122
  142.4 3.6 %collective-permute-start.41 = (f32[2,32,512]{2,1,0:T(8,128)S(1)}, f32[2,32,512]{2,1,0:T(8,128)S(1)}, u32[]{:S(2)}, u32[]{:S(2)}) collective-permute-start(f32[2,32,512]{2,1,0:T(8,128)S(1)} %get-tuple-element.331.own_lo_ref), channel_id=1, source_target_pairs={{8,0},{16,8},{24,16},{0,24},{9,1},{17,9},{25,17},{1,25},{10,2},{18... | collective-permute-start | bytes 393224 | tf_op jit(solution)/shard_map/ppermute | solution.py:576
  146.0 2.8 %collective-permute-done.40.refs_4_ = f32[32,8,256]{2,1,0:T(8,128)S(1)} collective-permute-done((f32[32,8,256]{2,1,0:T(8,128)S(1)}, f32[32,8,256]{2,1,0:T(8,128)S(1)}, u32[]{:S(2)}, u32[]{:S(2)}) %collective-permute-start.40) | collective-permute-done | bytes 262176 | tf_op jit(solution)/shard_map/ppermute | solution.py:606
  152.4 6.4 %two_sweeps.3 = (f32[2048,256]{1,0:T(8,128)S(1)}, f32[1,32,512]{2,1,0:T(8,128)S(1)}, f32[1,32,512]{2,1,0:T(8,128)S(1)}) custom-call(s32[2]{0:T(128)S(1)} %copy-done.2, f32[2048,256]{1,0:T(8,128)S(1)} %get-tuple-element.329.local_ref, f32[2048,256]{1,0:T(8,128)S(1)} %get-tuple-element.300.source_ref, f32[2048,256]{1,0:T(8,128)S(1)} %get-tuple-element.301.inverse_ref, ...), custom_call_target="tpu_custom_call" | custom-call | flops 1000000 | bytes 100000 | tf_op jit(solution)/shard_map/two_sweeps/pallas_call | solution.py:422
  158.8 3.1 %collective-permute-done.44.refs_6_ = f32[32,8,256]{2,1,0:T(8,128)S(1)} collective-permute-done((f32[32,8,256]{2,1,0:T(8,128)S(1)}, f32[32,8,256]{2,1,0:T(8,128)S(1)}, u32[]{:S(2)}, u32[]{:S(2)}) %collective-permute-start.44) | collective-permute-done | bytes 262176 | tf_op jit(solution)/shard_map/ppermute | solution.py:606
  161.8 2.4 %collective-permute-start.46 = (f32[1,32,512]{2,1,0:T(8,128)S(1)}, f32[1,32,512]{2,1,0:T(8,128)S(1)}, u32[]{:S(2)}, u32[]{:S(2)}) collective-permute-start(f32[1,32,512]{2,1,0:T(8,128)S(1)} %get-tuple-element.342), channel_id=1, source_target_pairs={{8,0},{16,8},{24,16},{0,24},{9,1},{17,9},{25,17},{1,25},{10,2},{18... | collective-permute-start | bytes 196616 | tf_op jit(solution)/shard_map/ppermute | solution.py:576
  164.3 5.2 %collective-permute-done.43.refs_5_ = f32[32,8,256]{2,1,0:T(8,128)S(1)} collective-permute-done((f32[32,8,256]{2,1,0:T(8,128)S(1)}, f32[32,8,256]{2,1,0:T(8,128)S(1)}, u32[]{:S(2)}, u32[]{:S(2)}) %collective-permute-start.43) | collective-permute-done | bytes 262176 | tf_op jit(solution)/shard_map/ppermute | solution.py:606
  170.3 3.9 %add_force.1 = (f32[3,32,64,256]{3,2,1,0:T(8,128)}, f32[32,64,256]{2,1,0:T(8,128)S(1)}) custom-call(s32[2]{0:T(128)S(1)} %copy-done.2, f32[2048,256]{1,0:T(8,128)S(1)} %get-tuple-element.335.local_ref, f32[1,32,512]{2,1,0:T(8,128)S(1)} %collective-permute-done.46.got_up_ref, f32[1,32,512]{2,1,0:T(8,128)S(1)} %collective-permute-done.47.got_lo_ref, ...), custom_call_target="tpu_custom_call" | custom-call | flops 1000000 | bytes 100000 | tf_op jit(solution)/shard_map/add_force/pallas_call | solution.py:512
  174.2 4.0 %finish.1 = f32[3,32,64,256]{3,2,1,0:T(8,128)} custom-call(s32[2]{0:T(128)S(1)} %copy-done.2, f32[7,64,256]{2,1,0:T(8,128)S(1)} %get-tuple-element.213.diag_ref.coef_ref, bf16[128,192]{1,0:T(8,128)(2,1)S(1)} %get-tuple-element.214.dpack_ref, f32[32,64,256]{2,1,0:T(8,128)S(1)} %get-tuple-element.346.px_ref, ...), custom_call_target="tpu_custom_call", output_to_operand_aliasing={{}: (5, {})} | custom-call | flops 1000000 | bytes 100000 | tf_op jit(solution)/shard_map/finish/pallas_call | solution.py:552
  (99 shorter events, 27.4 us)
Async XLA Ops:
  4.5 9.9 %collective-permute-start = (f32[32,8,256]{2,1,0:T(8,128)}, f32[32,8,256]{2,1,0:T(8,128)S(1)}, u32[]{:S(2)}, u32[]{:S(2)}) collective-permute-start(f32[32,8,256]{2,1,0:T(8,128)} %get-tuple-element.186), channel_id=1, source_target_pairs={{0,4},{1,5},{2,6},{3,7},{4,0},{5,1},{6,2},{7,3},{8,12},{9,13},{10,... | collective-permute-start | bytes 786440 | tf_op jit(solution)/shard_map/ppermute | solution.py:606
  7.6 9.4 %collective-permute-start.2 = (f32[32,8,256]{2,1,0:T(8,128)}, f32[32,8,256]{2,1,0:T(8,128)S(1)}, u32[]{:S(2)}, u32[]{:S(2)}) collective-permute-start(f32[32,8,256]{2,1,0:T(8,128)} %get-tuple-element.190), channel_id=1, source_target_pairs={{0,2},{1,3},{2,0},{3,1},{4,6},{5,7},{6,4},{7,5},{8,10},{9,11},{10,... | collective-permute-start | bytes 786440 | tf_op jit(solution)/shard_map/ppermute | solution.py:606
  9.1 12.7 %collective-permute-start.3 = (f32[32,8,256]{2,1,0:T(8,128)}, f32[32,8,256]{2,1,0:T(8,128)S(1)}, u32[]{:S(2)}, u32[]{:S(2)}) collective-permute-start(f32[32,8,256]{2,1,0:T(8,128)} %get-tuple-element.193), channel_id=1, source_target_pairs={{0,3},{1,2},{2,1},{3,0},{4,7},{5,6},{6,5},{7,4},{8,11},{9,10},{10,... | collective-permute-start | bytes 786440 | tf_op jit(solution)/shard_map/ppermute | solution.py:606
  9.1 18.8 %collective-permute-start.5 = (f32[32,8,256]{2,1,0:T(8,128)}, f32[32,8,256]{2,1,0:T(8,128)S(1)}, u32[]{:S(2)}, u32[]{:S(2)}) collective-permute-start(f32[32,8,256]{2,1,0:T(8,128)} %get-tuple-element.200), channel_id=1, source_target_pairs={{0,6},{1,7},{2,4},{3,5},{4,2},{5,3},{6,0},{7,1},{8,14},{9,15},{10,... | collective-permute-start | bytes 786440 | tf_op jit(solution)/shard_map/ppermute | solution.py:606
  10.0 19.8 %collective-permute-start.4 = (f32[32,8,256]{2,1,0:T(8,128)}, f32[32,8,256]{2,1,0:T(8,128)S(1)}, u32[]{:S(2)}, u32[]{:S(2)}) collective-permute-start(f32[32,8,256]{2,1,0:T(8,128)} %get-tuple-element.197), channel_id=1, source_target_pairs={{0,5},{1,4},{2,7},{3,6},{4,1},{5,0},{6,3},{7,2},{8,13},{9,12},{10,... | collective-permute-start | bytes 786440 | tf_op jit(solution)/shard_map/ppermute | solution.py:606
  14.5 18.1 %collective-permute-start.1 = (f32[32,8,256]{2,1,0:T(8,128)S(1)}, f32[32,8,256]{2,1,0:T(8,128)S(1)}, u32[]{:S(2)}, u32[]{:S(2)}) collective-permute-start(f32[32,8,256]{2,1,0:T(8,128)S(1)} %copy-done.12), channel_id=1, source_target_pairs={{0,1},{1,0},{2,3},{3,2},{4,5},{5,4},{6,7},{7,6},{8,9},{9,8},{10,11... | collective-permute-start | bytes 786440 | tf_op jit(solution)/shard_map/ppermute | solution.py:606
  17.0 15.9 %collective-permute-start.6 = (f32[32,8,256]{2,1,0:T(8,128)S(1)}, f32[32,8,256]{2,1,0:T(8,128)S(1)}, u32[]{:S(2)}, u32[]{:S(2)}) collective-permute-start(f32[32,8,256]{2,1,0:T(8,128)S(1)} %copy-done.11), channel_id=1, source_target_pairs={{0,7},{1,6},{2,5},{3,4},{4,3},{5,2},{6,1},{7,0},{8,15},{9,14},{10,... | collective-permute-start | bytes 786440 | tf_op jit(solution)/shard_map/ppermute | solution.py:606
  21.7 17.2 %collective-permute-start.7 = (f32[32,8,256]{2,1,0:T(8,128)S(1)}, f32[32,8,256]{2,1,0:T(8,128)S(1)}, u32[]{:S(2)}, u32[]{:S(2)}) collective-permute-start(f32[32,8,256]{2,1,0:T(8,128)S(1)} %get-tuple-element.218), channel_id=1, source_target_pairs={{0,4},{1,5},{2,6},{3,7},{4,0},{5,1},{6,2},{7,3},{8,12},{9,13},{10,... | collective-permute-start | bytes 786440 | tf_op jit(solution)/shard_map/ppermute | solution.py:606
  27.8 11.7 %collective-permute-start.9 = (f32[32,8,256]{2,1,0:T(8,128)S(1)}, f32[32,8,256]{2,1,0:T(8,128)S(1)}, u32[]{:S(2)}, u32[]{:S(2)}) collective-permute-start(f32[32,8,256]{2,1,0:T(8,128)S(1)} %get-tuple-element.222), channel_id=1, source_target_pairs={{0,2},{1,3},{2,0},{3,1},{4,6},{5,7},{6,4},{7,5},{8,10},{9,11},{10,... | collective-permute-start | bytes 786440 | tf_op jit(solution)/shard_map/ppermute | solution.py:606
  29.8 14.9 %collective-permute-start.12 = (f32[32,8,256]{2,1,0:T(8,128)S(1)}, f32[32,8,256]{2,1,0:T(8,128)S(1)}, u32[]{:S(2)}, u32[]{:S(2)}) collective-permute-start(f32[32,8,256]{2,1,0:T(8,128)S(1)} %get-tuple-element.232), channel_id=1, source_target_pairs={{0,6},{1,7},{2,4},{3,5},{4,2},{5,3},{6,0},{7,1},{8,14},{9,15},{10,... | collective-permute-start | bytes 786440 | tf_op jit(solution)/shard_map/ppermute | solution.py:606
  32.6 18.8 %collective-permute-start.11 = (f32[32,8,256]{2,1,0:T(8,128)S(1)}, f32[32,8,256]{2,1,0:T(8,128)S(1)}, u32[]{:S(2)}, u32[]{:S(2)}) collective-permute-start(f32[32,8,256]{2,1,0:T(8,128)S(1)} %get-tuple-element.229), channel_id=1, source_target_pairs={{0,5},{1,4},{2,7},{3,6},{4,1},{5,0},{6,3},{7,2},{8,13},{9,12},{10,... | collective-permute-start | bytes 786440 | tf_op jit(solution)/shard_map/ppermute | solution.py:606
  32.9 16.9 %collective-permute-start.10 = (f32[32,8,256]{2,1,0:T(8,128)S(1)}, f32[32,8,256]{2,1,0:T(8,128)S(1)}, u32[]{:S(2)}, u32[]{:S(2)}) collective-permute-start(f32[32,8,256]{2,1,0:T(8,128)S(1)} %get-tuple-element.225), channel_id=1, source_target_pairs={{0,3},{1,2},{2,1},{3,0},{4,7},{5,6},{6,5},{7,4},{8,11},{9,10},{10,... | collective-permute-start | bytes 786440 | tf_op jit(solution)/shard_map/ppermute | solution.py:606
  38.9 26.1 %collective-permute-start.8 = (f32[32,8,256]{2,1,0:T(8,128)S(1)}, f32[32,8,256]{2,1,0:T(8,128)S(1)}, u32[]{:S(2)}, u32[]{:S(2)}) collective-permute-start(f32[32,8,256]{2,1,0:T(8,128)S(1)} %get-tuple-element.219), channel_id=1, source_target_pairs={{0,1},{1,0},{2,3},{3,2},{4,5},{5,4},{6,7},{7,6},{8,9},{9,8},{10,11... | collective-permute-start | bytes 786440 | tf_op jit(solution)/shard_map/ppermute | solution.py:606
  39.5 15.9 %collective-permute-start.13 = (f32[32,8,256]{2,1,0:T(8,128)S(1)}, f32[32,8,256]{2,1,0:T(8,128)S(1)}, u32[]{:S(2)}, u32[]{:S(2)}) collective-permute-start(f32[32,8,256]{2,1,0:T(8,128)S(1)} %get-tuple-element.235), channel_id=1, source_target_pairs={{0,7},{1,6},{2,5},{3,4},{4,3},{5,2},{6,1},{7,0},{8,15},{9,14},{10,... | collective-permute-start | bytes 786440 | tf_op jit(solution)/shard_map/ppermute | solution.py:606
  44.7 16.7 %collective-permute-start.18 = (f32[32,8,256]{2,1,0:T(8,128)S(1)}, f32[32,8,256]{2,1,0:T(8,128)S(1)}, u32[]{:S(2)}, u32[]{:S(2)}) collective-permute-start(f32[32,8,256]{2,1,0:T(8,128)S(1)} %get-tuple-element.258), channel_id=1, source_target_pairs={{0,2},{1,3},{2,0},{3,1},{4,6},{5,7},{6,4},{7,5},{8,10},{9,11},{10,... | collective-permute-start | bytes 786440 | tf_op jit(solution)/shard_map/ppermute | solution.py:606
  49.8 6.1 %collective-permute-start.15 = (f32[2,512]{1,0:T(2,128)S(1)}, f32[2,512]{1,0:T(2,128)S(1)}, u32[]{:S(2)}, u32[]{:S(2)}) collective-permute-start(f32[2,512]{1,0:T(2,128)S(1)} %get-tuple-element.357), channel_id=1, source_target_pairs={{0,8},{8,16},{16,24},{24,0},{1,9},{9,17},{17,25},{25,1},{2,10},{10... | collective-permute-start | bytes 12296 | tf_op jit(solution)/shard_map/ppermute | solution.py:576
  51.4 19.8 %collective-permute-start.16 = (f32[32,8,256]{2,1,0:T(8,128)S(1)}, f32[32,8,256]{2,1,0:T(8,128)S(1)}, u32[]{:S(2)}, u32[]{:S(2)}) collective-permute-start(f32[32,8,256]{2,1,0:T(8,128)S(1)} %get-tuple-element.254), channel_id=1, source_target_pairs={{0,4},{1,5},{2,6},{3,7},{4,0},{5,1},{6,2},{7,3},{8,12},{9,13},{10,... | collective-permute-start | bytes 786440 | tf_op jit(solution)/shard_map/ppermute | solution.py:606
  55.4 15.8 %collective-permute-start.21 = (f32[32,8,256]{2,1,0:T(8,128)S(1)}, f32[32,8,256]{2,1,0:T(8,128)S(1)}, u32[]{:S(2)}, u32[]{:S(2)}) collective-permute-start(f32[32,8,256]{2,1,0:T(8,128)S(1)} %get-tuple-element.268), channel_id=1, source_target_pairs={{0,6},{1,7},{2,4},{3,5},{4,2},{5,3},{6,0},{7,1},{8,14},{9,15},{10,... | collective-permute-start | bytes 786440 | tf_op jit(solution)/shard_map/ppermute | solution.py:606
  55.9 16.1 %collective-permute-start.19 = (f32[32,8,256]{2,1,0:T(8,128)S(1)}, f32[32,8,256]{2,1,0:T(8,128)S(1)}, u32[]{:S(2)}, u32[]{:S(2)}) collective-permute-start(f32[32,8,256]{2,1,0:T(8,128)S(1)} %get-tuple-element.261), channel_id=1, source_target_pairs={{0,3},{1,2},{2,1},{3,0},{4,7},{5,6},{6,5},{7,4},{8,11},{9,10},{10,... | collective-permute-start | bytes 786440 | tf_op jit(solution)/shard_map/ppermute | solution.py:606
  64.9 12.3 %collective-permute-start.22 = (f32[32,8,256]{2,1,0:T(8,128)S(1)}, f32[32,8,256]{2,1,0:T(8,128)S(1)}, u32[]{:S(2)}, u32[]{:S(2)}) collective-permute-start(f32[32,8,256]{2,1,0:T(8,128)S(1)} %get-tuple-element.271), channel_id=1, source_target_pairs={{0,7},{1,6},{2,5},{3,4},{4,3},{5,2},{6,1},{7,0},{8,15},{9,14},{10,... | collective-permute-start | bytes 786440 | tf_op jit(solution)/shard_map/ppermute | solution.py:606
  66.3 13.9 %collective-permute-start.20 = (f32[32,8,256]{2,1,0:T(8,128)S(1)}, f32[32,8,256]{2,1,0:T(8,128)S(1)}, u32[]{:S(2)}, u32[]{:S(2)}) collective-permute-start(f32[32,8,256]{2,1,0:T(8,128)S(1)} %get-tuple-element.265), channel_id=1, source_target_pairs={{0,5},{1,4},{2,7},{3,6},{4,1},{5,0},{6,3},{7,2},{8,13},{9,12},{10,... | collective-permute-start | bytes 786440 | tf_op jit(solution)/shard_map/ppermute | solution.py:606
  71.2 10.4 %collective-permute-start.17 = (f32[32,8,256]{2,1,0:T(8,128)S(1)}, f32[32,8,256]{2,1,0:T(8,128)S(1)}, u32[]{:S(2)}, u32[]{:S(2)}) collective-permute-start(f32[32,8,256]{2,1,0:T(8,128)S(1)} %get-tuple-element.255), channel_id=1, source_target_pairs={{0,1},{1,0},{2,3},{3,2},{4,5},{5,4},{6,7},{7,6},{8,9},{9,8},{10,11... | collective-permute-start | bytes 786440 | tf_op jit(solution)/shard_map/ppermute | solution.py:606
  71.3 12.6 %collective-permute-start.25 = (f32[32,8,256]{2,1,0:T(8,128)S(1)}, f32[32,8,256]{2,1,0:T(8,128)S(1)}, u32[]{:S(2)}, u32[]{:S(2)}) collective-permute-start(f32[32,8,256]{2,1,0:T(8,128)S(1)} %get-tuple-element.280), channel_id=1, source_target_pairs={{0,2},{1,3},{2,0},{3,1},{4,6},{5,7},{6,4},{7,5},{8,10},{9,11},{10,... | collective-permute-start | bytes 786440 | tf_op jit(solution)/shard_map/ppermute | solution.py:606
  72.0 14.6 %collective-permute-start.23 = (f32[32,8,256]{2,1,0:T(8,128)S(1)}, f32[32,8,256]{2,1,0:T(8,128)S(1)}, u32[]{:S(2)}, u32[]{:S(2)}) collective-permute-start(f32[32,8,256]{2,1,0:T(8,128)S(1)} %get-tuple-element.276), channel_id=1, source_target_pairs={{0,4},{1,5},{2,6},{3,7},{4,0},{5,1},{6,2},{7,3},{8,12},{9,13},{10,... | collective-permute-start | bytes 786440 | tf_op jit(solution)/shard_map/ppermute | solution.py:606
  77.3 11.2 %collective-permute-start.26 = (f32[32,8,256]{2,1,0:T(8,128)S(1)}, f32[32,8,256]{2,1,0:T(8,128)S(1)}, u32[]{:S(2)}, u32[]{:S(2)}) collective-permute-start(f32[32,8,256]{2,1,0:T(8,128)S(1)} %get-tuple-element.283), channel_id=1, source_target_pairs={{0,3},{1,2},{2,1},{3,0},{4,7},{5,6},{6,5},{7,4},{8,11},{9,10},{10,... | collective-permute-start | bytes 786440 | tf_op jit(solution)/shard_map/ppermute | solution.py:606
  80.2 14.9 %collective-permute-start.28 = (f32[32,8,256]{2,1,0:T(8,128)S(1)}, f32[32,8,256]{2,1,0:T(8,128)S(1)}, u32[]{:S(2)}, u32[]{:S(2)}) collective-permute-start(f32[32,8,256]{2,1,0:T(8,128)S(1)} %get-tuple-element.290), channel_id=1, source_target_pairs={{0,6},{1,7},{2,4},{3,5},{4,2},{5,3},{6,0},{7,1},{8,14},{9,15},{10,... | collective-permute-start | bytes 786440 | tf_op jit(solution)/shard_map/ppermute | solution.py:606
  83.9 15.9 %collective-permute-start.29 = (f32[32,8,256]{2,1,0:T(8,128)S(1)}, f32[32,8,256]{2,1,0:T(8,128)S(1)}, u32[]{:S(2)}, u32[]{:S(2)}) collective-permute-start(f32[32,8,256]{2,1,0:T(8,128)S(1)} %get-tuple-element.293), channel_id=1, source_target_pairs={{0,7},{1,6},{2,5},{3,4},{4,3},{5,2},{6,1},{7,0},{8,15},{9,14},{10,... | collective-permute-start | bytes 786440 | tf_op jit(solution)/shard_map/ppermute | solution.py:606
  83.9 20.4 %collective-permute-start.27 = (f32[32,8,256]{2,1,0:T(8,128)S(1)}, f32[32,8,256]{2,1,0:T(8,128)S(1)}, u32[]{:S(2)}, u32[]{:S(2)}) collective-permute-start(f32[32,8,256]{2,1,0:T(8,128)S(1)} %get-tuple-element.287), channel_id=1, source_target_pairs={{0,5},{1,4},{2,7},{3,6},{4,1},{5,0},{6,3},{7,2},{8,13},{9,12},{10,... | collective-permute-start | bytes 786440 | tf_op jit(solution)/shard_map/ppermute | solution.py:606
  86.6 17.7 %collective-permute-start.24 = (f32[32,8,256]{2,1,0:T(8,128)S(1)}, f32[32,8,256]{2,1,0:T(8,128)S(1)}, u32[]{:S(2)}, u32[]{:S(2)}) collective-permute-start(f32[32,8,256]{2,1,0:T(8,128)S(1)} %get-tuple-element.277), channel_id=1, source_target_pairs={{0,1},{1,0},{2,3},{3,2},{4,5},{5,4},{6,7},{7,6},{8,9},{9,8},{10,11... | collective-permute-start | bytes 786440 | tf_op jit(solution)/shard_map/ppermute | solution.py:606
  88.5 24.8 %collective-permute-start.32 = (f32[32,8,256]{2,1,0:T(8,128)S(1)}, f32[32,8,256]{2,1,0:T(8,128)S(1)}, u32[]{:S(2)}, u32[]{:S(2)}) collective-permute-start(f32[32,8,256]{2,1,0:T(8,128)S(1)} %get-tuple-element.311), channel_id=1, source_target_pairs={{0,4},{1,5},{2,6},{3,7},{4,0},{5,1},{6,2},{7,3},{8,12},{9,13},{10,... | collective-permute-start | bytes 786440 | tf_op jit(solution)/shard_map/ppermute | solution.py:606
  95.1 18.3 %collective-permute-start.34 = (f32[32,8,256]{2,1,0:T(8,128)S(1)}, f32[32,8,256]{2,1,0:T(8,128)S(1)}, u32[]{:S(2)}, u32[]{:S(2)}) collective-permute-start(f32[32,8,256]{2,1,0:T(8,128)S(1)} %get-tuple-element.314), channel_id=1, source_target_pairs={{0,2},{1,3},{2,0},{3,1},{4,6},{5,7},{6,4},{7,5},{8,10},{9,11},{10,... | collective-permute-start | bytes 786440 | tf_op jit(solution)/shard_map/ppermute | solution.py:606
  108.5 8.4 %collective-permute-start.31 = (f32[2,32,512]{2,1,0:T(8,128)S(1)}, f32[2,32,512]{2,1,0:T(8,128)S(1)}, u32[]{:S(2)}, u32[]{:S(2)}) collective-permute-start(f32[2,32,512]{2,1,0:T(8,128)S(1)} %get-tuple-element.302.own_up_ref), channel_id=1, source_target_pairs={{0,8},{8,16},{16,24},{24,0},{1,9},{9,17},{17,25},{25,1},{2,10},{10... | collective-permute-start | bytes 393224 | tf_op jit(solution)/shard_map/ppermute | solution.py:576
  110.1 8.9 %collective-permute-start.30 = (f32[2,32,512]{2,1,0:T(8,128)S(1)}, f32[2,32,512]{2,1,0:T(8,128)S(1)}, u32[]{:S(2)}, u32[]{:S(2)}) collective-permute-start(f32[2,32,512]{2,1,0:T(8,128)S(1)} %get-tuple-element.303.own_lo_ref), channel_id=1, source_target_pairs={{8,0},{16,8},{24,16},{0,24},{9,1},{17,9},{25,17},{1,25},{10,2},{18... | collective-permute-start | bytes 393224 | tf_op jit(solution)/shard_map/ppermute | solution.py:576
  112.4 15.8 %collective-permute-start.35 = (f32[32,8,256]{2,1,0:T(8,128)S(1)}, f32[32,8,256]{2,1,0:T(8,128)S(1)}, u32[]{:S(2)}, u32[]{:S(2)}) collective-permute-start(f32[32,8,256]{2,1,0:T(8,128)S(1)} %get-tuple-element.316), channel_id=1, source_target_pairs={{0,3},{1,2},{2,1},{3,0},{4,7},{5,6},{6,5},{7,4},{8,11},{9,10},{10,... | collective-permute-start | bytes 786440 | tf_op jit(solution)/shard_map/ppermute | solution.py:606
  113.4 14.8 %collective-permute-start.33 = (f32[32,8,256]{2,1,0:T(8,128)S(1)}, f32[32,8,256]{2,1,0:T(8,128)S(1)}, u32[]{:S(2)}, u32[]{:S(2)}) collective-permute-start(f32[32,8,256]{2,1,0:T(8,128)S(1)} %get-tuple-element.312), channel_id=1, source_target_pairs={{0,1},{1,0},{2,3},{3,2},{4,5},{5,4},{6,7},{7,6},{8,9},{9,8},{10,11... | collective-permute-start | bytes 786440 | tf_op jit(solution)/shard_map/ppermute | solution.py:606
  113.4 14.8 %collective-permute-start.38 = (f32[32,8,256]{2,1,0:T(8,128)S(1)}, f32[32,8,256]{2,1,0:T(8,128)S(1)}, u32[]{:S(2)}, u32[]{:S(2)}) collective-permute-start(f32[32,8,256]{2,1,0:T(8,128)S(1)} %get-tuple-element.320), channel_id=1, source_target_pairs={{0,7},{1,6},{2,5},{3,4},{4,3},{5,2},{6,1},{7,0},{8,15},{9,14},{10,... | collective-permute-start | bytes 786440 | tf_op jit(solution)/shard_map/ppermute | solution.py:606
  116.9 15.7 %collective-permute-start.37 = (f32[32,8,256]{2,1,0:T(8,128)S(1)}, f32[32,8,256]{2,1,0:T(8,128)S(1)}, u32[]{:S(2)}, u32[]{:S(2)}) collective-permute-start(f32[32,8,256]{2,1,0:T(8,128)S(1)} %get-tuple-element.319), channel_id=1, source_target_pairs={{0,6},{1,7},{2,4},{3,5},{4,2},{5,3},{6,0},{7,1},{8,14},{9,15},{10,... | collective-permute-start | bytes 786440 | tf_op jit(solution)/shard_map/ppermute | solution.py:606
  119.0 18.9 %collective-permute-start.36 = (f32[32,8,256]{2,1,0:T(8,128)S(1)}, f32[32,8,256]{2,1,0:T(8,128)S(1)}, u32[]{:S(2)}, u32[]{:S(2)}) collective-permute-start(f32[32,8,256]{2,1,0:T(8,128)S(1)} %get-tuple-element.318), channel_id=1, source_target_pairs={{0,5},{1,4},{2,7},{3,6},{4,1},{5,0},{6,3},{7,2},{8,13},{9,12},{10,... | collective-permute-start | bytes 786440 | tf_op jit(solution)/shard_map/ppermute | solution.py:606
  140.4 8.4 %collective-permute-start.40 = (f32[32,8,256]{2,1,0:T(8,128)S(1)}, f32[32,8,256]{2,1,0:T(8,128)S(1)}, u32[]{:S(2)}, u32[]{:S(2)}) collective-permute-start(f32[32,8,256]{2,1,0:T(8,128)S(1)} %get-tuple-element.327), channel_id=1, source_target_pairs={{0,4},{1,5},{2,6},{3,7},{4,0},{5,1},{6,2},{7,3},{8,12},{9,13},{10,... | collective-permute-start | bytes 786440 | tf_op jit(solution)/shard_map/ppermute | solution.py:606
  141.3 8.6 %collective-permute-start.39 = (f32[32,8,256]{2,1,0:T(8,128)S(1)}, f32[32,8,256]{2,1,0:T(8,128)S(1)}, u32[]{:S(2)}, u32[]{:S(2)}) collective-permute-start(f32[32,8,256]{2,1,0:T(8,128)S(1)} %get-tuple-element.323), channel_id=1, source_target_pairs={{0,2},{1,3},{2,0},{3,1},{4,6},{5,7},{6,4},{7,5},{8,10},{9,11},{10,... | collective-permute-start | bytes 786440 | tf_op jit(solution)/shard_map/ppermute | solution.py:606
  142.2 8.2 %collective-permute-start.42 = (f32[2,32,512]{2,1,0:T(8,128)S(1)}, f32[2,32,512]{2,1,0:T(8,128)S(1)}, u32[]{:S(2)}, u32[]{:S(2)}) collective-permute-start(f32[2,32,512]{2,1,0:T(8,128)S(1)} %get-tuple-element.330.own_up_ref), channel_id=1, source_target_pairs={{0,8},{8,16},{16,24},{24,0},{1,9},{9,17},{17,25},{25,1},{2,10},{10... | collective-permute-start | bytes 393224 | tf_op jit(solution)/shard_map/ppermute | solution.py:576
  142.4 8.8 %collective-permute-start.41 = (f32[2,32,512]{2,1,0:T(8,128)S(1)}, f32[2,32,512]{2,1,0:T(8,128)S(1)}, u32[]{:S(2)}, u32[]{:S(2)}) collective-permute-start(f32[2,32,512]{2,1,0:T(8,128)S(1)} %get-tuple-element.331.own_lo_ref), channel_id=1, source_target_pairs={{8,0},{16,8},{24,16},{0,24},{9,1},{17,9},{25,17},{1,25},{10,2},{18... | collective-permute-start | bytes 393224 | tf_op jit(solution)/shard_map/ppermute | solution.py:576
  146.0 12.8 %collective-permute-start.45 = (f32[32,8,256]{2,1,0:T(8,128)S(1)}, f32[32,8,256]{2,1,0:T(8,128)S(1)}, u32[]{:S(2)}, u32[]{:S(2)}) collective-permute-start(f32[32,8,256]{2,1,0:T(8,128)S(1)} %get-tuple-element.341), channel_id=1, source_target_pairs={{0,3},{1,2},{2,1},{3,0},{4,7},{5,6},{6,5},{7,4},{8,11},{9,10},{10,... | collective-permute-start | bytes 786440 | tf_op jit(solution)/shard_map/ppermute | solution.py:606
  148.8 13.1 %collective-permute-start.44 = (f32[32,8,256]{2,1,0:T(8,128)S(1)}, f32[32,8,256]{2,1,0:T(8,128)S(1)}, u32[]{:S(2)}, u32[]{:S(2)}) collective-permute-start(f32[32,8,256]{2,1,0:T(8,128)S(1)} %get-tuple-element.339), channel_id=1, source_target_pairs={{0,6},{1,7},{2,4},{3,5},{4,2},{5,3},{6,0},{7,1},{8,14},{9,15},{10,... | collective-permute-start | bytes 786440 | tf_op jit(solution)/shard_map/ppermute | solution.py:606
  149.9 19.5 %collective-permute-start.43 = (f32[32,8,256]{2,1,0:T(8,128)S(1)}, f32[32,8,256]{2,1,0:T(8,128)S(1)}, u32[]{:S(2)}, u32[]{:S(2)}) collective-permute-start(f32[32,8,256]{2,1,0:T(8,128)S(1)} %get-tuple-element.334), channel_id=1, source_target_pairs={{0,5},{1,4},{2,7},{3,6},{4,1},{5,0},{6,3},{7,2},{8,13},{9,12},{10,... | collective-permute-start | bytes 786440 | tf_op jit(solution)/shard_map/ppermute | solution.py:606
  150.4 23.9 %collective-permute-start.48 = (f32[32,8,256]{2,1,0:T(8,128)S(1)}, f32[32,8,256]{2,1,0:T(8,128)S(1)}, u32[]{:S(2)}, u32[]{:S(2)}) collective-permute-start(f32[32,8,256]{2,1,0:T(8,128)S(1)} %get-tuple-element.350), channel_id=1, source_target_pairs={{0,1},{1,0},{2,3},{3,2},{4,5},{5,4},{6,7},{7,6},{8,9},{9,8},{10,11... | collective-permute-start | bytes 786440 | tf_op jit(solution)/shard_map/ppermute | solution.py:606
  151.2 23.1 %collective-permute-start.49 = (f32[32,8,256]{2,1,0:T(8,128)S(1)}, f32[32,8,256]{2,1,0:T(8,128)S(1)}, u32[]{:S(2)}, u32[]{:S(2)}) collective-permute-start(f32[32,8,256]{2,1,0:T(8,128)S(1)} %get-tuple-element.356), channel_id=1, source_target_pairs={{0,7},{1,6},{2,5},{3,4},{4,3},{5,2},{6,1},{7,0},{8,15},{9,14},{10,... | collective-permute-start | bytes 786440 | tf_op jit(solution)/shard_map/ppermute | solution.py:606
  161.8 7.6 %collective-permute-start.46 = (f32[1,32,512]{2,1,0:T(8,128)S(1)}, f32[1,32,512]{2,1,0:T(8,128)S(1)}, u32[]{:S(2)}, u32[]{:S(2)}) collective-permute-start(f32[1,32,512]{2,1,0:T(8,128)S(1)} %get-tuple-element.342), channel_id=1, source_target_pairs={{8,0},{16,8},{24,16},{0,24},{9,1},{17,9},{25,17},{1,25},{10,2},{18... | collective-permute-start | bytes 196616 | tf_op jit(solution)/shard_map/ppermute | solution.py:576
  (17 other events, 263.9 us)

commit v8 on v7

--- a/solution.py
+++ b/solution.py
@@ -21,7 +21,7 @@
 F32 = jnp.float32
 BF16 = jnp.bfloat16
 VMEM_LIMIT = 20 * 1024 * 1024
-LARGE_LIMIT = 55 * 1024 * 1024
+LARGE_LIMIT = 48 * 1024 * 1024
 SMEM_SPEC = pl.BlockSpec(memory_space=pltpu.SMEM)
 
 
@@ -576,11 +576,45 @@
     return lax.ppermute(lo, "dom", down_way), lax.ppermute(up, "dom", up_way)
 
 
-def tie(blocks, value):
-    blocks = list(blocks)
-    first = min(2, len(blocks) - 1)
-    blocks[first], value = lax.optimization_barrier((blocks[first], value))
-    return blocks, value
+class Exchange:
+    def __init__(self, blocks, flight):
+        self.blocks = list(blocks)
+        self.flight = flight
+        self.places = {}
+        self.order = sorted(range(1, len(self.blocks)), key=lambda d: (-bin(d >> 1).count("1"), d % 2, d))
+
+    def hold(self, value):
+        if len(self.places) < len(self.order):
+            d = self.order[len(self.places)]
+            self.blocks[d], value = lax.optimization_barrier((self.blocks[d], value))
+        return value
+
+    def send(self, count):
+        for d in self.order[len(self.places) :][:count]:
+            block = self.blocks[d]
+            if len(self.flight) >= IN_FLIGHT:
+                block, self.flight[-IN_FLIGHT] = lax.optimization_barrier((block, self.flight[-IN_FLIGHT]))
+            pairs = [(i, i ^ d) for i in range(len(self.blocks))]
+            self.places[d] = len(self.flight)
+            self.flight.append(lax.ppermute(block, "four", pairs))
+
+    def after(self, value, first, last):
+        for d in self.order[first:last]:
+            place = self.places[d]
+            value, self.flight[place] = lax.optimization_barrier((value, self.flight[place]))
+        return value
+
+    def got(self):
+        return [self.blocks[0]] + [self.flight[self.places[d]] for d in range(1, len(self.blocks))]
+
+
+class Whole(Exchange):
+    def __init__(self, blocks, exchange):
+        super().__init__(blocks[:1], [])
+        self.exchange = exchange
+
+    def got(self):
+        return self.exchange(self.blocks[0])
 
 
 def per_device(
@@ -595,89 +629,75 @@
     natural = jnp.asarray(coef_table(PLANES))
     table = permuted_table(position, natural, lines)
     flight = []
-
-    def exchange(blocks):
-        first = len(flight)
-        order = sorted(range(1, peers), key=lambda d: (d < 2, d % 2, d))
-        for d in order:
-            block = blocks[d]
-            if len(flight) >= IN_FLIGHT:
-                block, flight[-IN_FLIGHT] = lax.optimization_barrier((block, flight[-IN_FLIGHT]))
-            flight.append(lax.ppermute(block, "four", [(i, i ^ d) for i in range(peers)]))
-
-        def received():
-            got = {d: flight[first + k] for k, d in enumerate(order)}
-            return [blocks[0]] + [got[d] for d in range(1, peers)]
-
-        return received
+    share = nodes // peers
 
     def columns(comp):
         if direct:
             return pack(position, adjoint, comp, LARGE_LIMIT if comp == 2 else VMEM_LIMIT)
-        return [jnp.moveaxis(adjoint[comp].reshape(per, peers, nodes // peers, elements), 1, 0)]
+        return [jnp.moveaxis(adjoint[comp].reshape(per, peers, share, elements), 1, 0)]
+
+    def gather_planes(block):
+        return [to_all(block).reshape(PLANES, share, elements)]
+
+    def gather_lines(block):
+        got = jnp.moveaxis(to_all(block.reshape(peers, per, share, elements)), 0, 1)
+        got = got.reshape(per, lines, LINE, elements)
+        return [got[:, d] for d in range(lines)]
 
     def spread(blocks):
-        if direct:
-            return exchange(blocks)
-        got = [to_all(blocks[0]).reshape(PLANES, nodes // peers, elements)]
-        return lambda: got
+        return Exchange(blocks, flight) if direct else Whole(blocks, gather_planes)
 
     def collect(blocks):
-        if direct:
-            return exchange(blocks)
-        got = to_all(blocks[0].reshape(peers, per, nodes // peers, elements))
-        got = jnp.moveaxis(got, 0, 1).reshape(per, lines, LINE, elements)
-        return lambda: [got[:, d] for d in range(lines)]
-
-    z_blocks = columns(2)
-    z_columns = spread(z_blocks)
-    x_blocks = columns(0)
-    x_blocks, table = tie(x_blocks, table)
-    x_columns = spread(x_blocks)
-    constants = prepare(
+        return Exchange(blocks, flight) if direct else Whole(blocks, gather_lines)
+
+    z_out = spread(columns(2))
+    z_out.send(3)
+    *constants, face = prepare(
         position, base_bank, snapshot, geometry, diff_r, diff_s, stiffness, upper_list, lower_list
     )
-    z_coefs = transform(z_columns(), table)
-    z_coefs, constants = tie(z_coefs, constants)
-    coef, dpack, spack, gather, scatter, mask, face = constants
-    far = swap_faces(face[0], face[1])
-    z_later = collect(z_coefs)
+    coef, dpack, spack, gather, scatter, mask = constants
+    far = z_out.hold(swap_faces(face[0], face[1]))
+    z_out.send(4)
+    x_out = spread(columns(0))
+    table = x_out.hold(table)
+    x_out.send(5)
+    z_coefs = x_out.hold(transform(z_out.got(), table))
+    x_out.send(2)
     y_blocks = columns(1)
-    x_coefs = transform(x_columns(), table)
-    x_coefs, (y_blocks, far) = tie(x_coefs, (y_blocks, far))
-    x_later = collect(x_coefs)
-    y_columns = spread(y_blocks)
-    z = z_later()
-    x = x_later()
+    z_back = collect(z_coefs)
+    z_back.send(5)
+    x_coefs, y_blocks = z_back.hold((transform(x_out.got(), table), y_blocks))
+    z_back.send(2)
+    x_back = collect(x_coefs)
+    x_back.send(7)
+    y_out = spread(y_blocks)
+    y_out.send(7)
+    z = z_back.got()
+    x = x_back.got()
     source, inverse, local, up, lo = start_solve(
         position, z, x, geometry, coef, dpack, spack, gather, mask
     )
     got = swap_faces(up, lo)
     parts = partial_update(z, x, coef, dpack)
     local, (px, py, pz) = lax.optimization_barrier((local, parts))
+    local = y_out.after(local, 2, 3)
     local, up, lo = two_sweeps(
         2, position, local, source, inverse, (up, lo), got, face, far, spack, gather, scatter, mask
     )
-    y_got = y_columns()
+    y_got = list(y_out.got())
     y_got[0], local = lax.optimization_barrier((y_got[0], local))
     got = swap_faces(up, lo)
-    begun = len(flight)
-    y_later = collect(transform(y_got, table))
-
-    def after(value, first, last):
-        here = slice(begun + first, begun + last)
-        value, flight[here] = lax.optimization_barrier((value, flight[here]))
-        return value
-
-    local = after(local, 0, 2)
+    y_back = collect(transform(y_got, table))
+    y_back.send(7)
+    local = y_back.after(local, 0, 1)
     local, up, lo = two_sweeps(
         1, position, local, source, inverse, (up, lo), got, face, far, spack, gather, scatter, mask
     )
-    up, lo = after((up, lo), 2, 4)
+    up, lo = y_back.after((up, lo), 1, 3)
     got = swap_faces(up, lo)
-    local = after(local, 4, 5)
+    local = y_back.after(local, 3, 5)
     filled, px = add_force(position, local, got, face, geometry, dpack, scatter, mask, px, pz)
-    return finish(position, y_later(), coef, dpack, px, py, filled)
+    return finish(position, y_back.got(), coef, dpack, px, py, filled)
 
 
 def solution(mesh):

time: 178 us -> 184 us (1.034)
  waiting for transfers between devices: 76.6 us -> 82.4 us
    ppermute x42, waiting for transfers between devices: 70.4 us -> 74.7 us  [send(): self.flight.append(lax.ppermute(block, 'four', pairs))]
  transfers between devices with their start and end apart: 50 -> 50, of which waited for: 28 -> 18; matrix products, arithmetic and copies ran while one was open for 0% -> 0% of each run, Pallas kernels for 18% -> 18%
where the time goes in v8:
time: 184 us
  waiting for transfers between devices  82.4 us (45%)
  starting transfers between devices  59.5 us (32%)
  Pallas kernels  41.7 us (23%)
    ppermute x42, waiting for transfers between devices, send(): self.flight.append(lax.ppermute(block, 'four', pairs))  74.7 us
    ppermute x42, starting transfers between devices, send(): self.flight.append(lax.ppermute(block, 'four', pairs))  42.5 us
    ppermute x8, starting transfers between devices, swap_faces(): return (lax.ppermute(lo, 'dom', down_way), lax.ppermute(up, 'dom', up_way))  17 us
    pallas_call x2, Pallas kernels, two_sweeps(): pl.pallas_call(functools.partial(sweeps_kernel, block, keep), out_shape=[...  12.3 us
    ppermute x8, waiting for transfers between devices, swap_faces(): return (lax.ppermute(lo, 'dom', down_way), lax.ppermute(up, 'dom', up_way))  7.65 us
    pallas_call x3, Pallas kernels, transform(): pl.pallas_call(functools.partial(transform_kernel, count), out_shape=[jax...  7.37 us
    pallas_call x3, Pallas kernels, pack(): pl.pallas_call(pack_kernel, out_shape=[jax.ShapeDtypeStruct((per, LINE, e...  4.88 us
    pallas_call x1, Pallas kernels, start_solve(): pl.pallas_call(functools.partial(start_kernel, block, len(z)), out_shape=...  4.24 us
  transfers between devices with their start and end apart: 50, of which 18 were waited for; matrix products, arithmetic and copies ran while one was open for 0% of the time, Pallas kernels for 18%

profile of v8, /device:TPU:0, one launch (start us, length us, event | category | flops | bytes accessed | tf_op | source)
XLA Modules:
  0.0 184.1 jit_solution(11814258140488331331)
XLA Ops:
  0.2 2.8 %pack.4 = (f32[32,8,256]{2,1,0:T(8,128)S(1)}, f32[32,8,256]{2,1,0:T(8,128)S(1)}, f32[32,8,256]{2,1,0:T(8,128)S(1)}, f32[32,8,256]{2,1,0:T(8,128)S(1)}, f32[32,8,...) custom-call(s32[2]{0:T(128)S(1)} %pad_add_fusion.pos_ref, ...), custom_call_target="tpu_custom_call" | custom-call | bytes 4194304 | tf_op jit(solution)/shard_map/pack/pallas_call | solution.py:149
  2.9 3.4 %collective-permute-start = (f32[32,8,256]{2,1,0:T(8,128)S(1)}, f32[32,8,256]{2,1,0:T(8,128)S(1)}, u32[]{:S(2)}, u32[]{:S(2)}) collective-permute-start(f32[32,8,256]{2,1,0:T(8,128)S(1)} %get-tuple-element.204), channel_id=1, source_target_pairs={{0,7},{1,6},{2,5},{3,4},{4,3},{5,2},{6,1},{7,0},{8,15},{9,14},{10,... | collective-permute-start | bytes 786440 | tf_op jit(solution)/shard_map/ppermute | solution.py:599
  6.9 1.4 collective-permute-start.7
  9.6 1.6 collective-permute-start.5
  11.3 2.2 %collective-permute-start.4 = (f32[2,512]{1,0:T(2,128)S(1)}, f32[2,512]{1,0:T(2,128)S(1)}, u32[]{:S(2)}, u32[]{:S(2)}) collective-permute-start(f32[2,512]{1,0:T(2,128)S(1)} %get-tuple-element.388), channel_id=1, source_target_pairs={{8,0},{16,8},{24,16},{0,24},{9,1},{17,9},{25,17},{1,25},{10,2},{18... | collective-permute-start | bytes 12296 | tf_op jit(solution)/shard_map/ppermute | solution.py:576
  13.5 1.6 collective-permute-done.5.far_lo_ref
  15.1 1.5 collective-permute-start.6
  17.3 8.0 %collective-permute-done.7.refs_6_ = f32[32,8,256]{2,1,0:T(8,128)S(1)} collective-permute-done((f32[32,8,256]{2,1,0:T(8,128)S(1)}, f32[32,8,256]{2,1,0:T(8,128)S(1)}, u32[]{:S(2)}, u32[]{:S(2)}) %collective-permute-start.7) | collective-permute-done | bytes 262176 | tf_op jit(solution)/shard_map/ppermute | solution.py:599
  28.5 1.5 collective-permute-start.14
  30.0 1.3 collective-permute-start.9
  31.3 1.5 collective-permute-start.11
  32.8 12.3 %collective-permute-done.8.refs_5_ = f32[32,8,256]{2,1,0:T(8,128)S(1)} collective-permute-done((f32[32,8,256]{2,1,0:T(8,128)S(1)}, f32[32,8,256]{2,1,0:T(8,128)S(1)}, u32[]{:S(2)}, u32[]{:S(2)}) %collective-permute-start.8) | collective-permute-done | bytes 262176 | tf_op jit(solution)/shard_map/ppermute | solution.py:599
  45.1 2.4 %transform.3 = (f32[32,8,256]{2,1,0:T(8,128)S(1)}, f32[32,8,256]{2,1,0:T(8,128)S(1)}, f32[32,8,256]{2,1,0:T(8,128)S(1)}, f32[32,8,256]{2,1,0:T(8,128)S(1)}, f32[...) custom-call(bf16[512,256]{1,0:T(8,128)(2,1)S(1)} %permuted_table.1.tab, ...), custom_call_target="tpu_custom_call" | custom-call | flops 805306368 | bytes 4194304 | tf_op jit(solution)/shard_map/transform/pallas_call | solution.py:122
  47.5 1.4 collective-permute-start.15
  50.7 1.5 collective-permute-start.21
  52.2 3.7 %collective-permute-done.15.refs_5_ = f32[32,8,256]{2,1,0:T(8,128)S(1)} collective-permute-done((f32[32,8,256]{2,1,0:T(8,128)S(1)}, f32[32,8,256]{2,1,0:T(8,128)S(1)}, u32[]{:S(2)}, u32[]{:S(2)}) %collective-permute-start.15) | collective-permute-done | bytes 262176 | tf_op jit(solution)/shard_map/ppermute | solution.py:599
  57.2 1.5 collective-permute-start.18
  58.7 9.0 %collective-permute-done.13.refs_4_ = f32[32,8,256]{2,1,0:T(8,128)S(1)} collective-permute-done((f32[32,8,256]{2,1,0:T(8,128)S(1)}, f32[32,8,256]{2,1,0:T(8,128)S(1)}, u32[]{:S(2)}, u32[]{:S(2)}) %collective-permute-start.13) | collective-permute-done | bytes 262176 | tf_op jit(solution)/shard_map/ppermute | solution.py:599
  67.7 1.3 collective-permute-start.16
  70.1 2.5 %transform.4 = (f32[32,8,256]{2,1,0:T(8,128)S(1)}, f32[32,8,256]{2,1,0:T(8,128)S(1)}, f32[32,8,256]{2,1,0:T(8,128)S(1)}, f32[32,8,256]{2,1,0:T(8,128)S(1)}, f32[...) custom-call(bf16[512,256]{1,0:T(8,128)(2,1)S(1)} %permuted_table.1.tab, ...), custom_call_target="tpu_custom_call" | custom-call | flops 805306368 | bytes 4194304 | tf_op jit(solution)/shard_map/transform/pallas_call | solution.py:122
  72.6 1.5 collective-permute-start.22
  74.1 4.8 %collective-permute-done.20.refs_4_ = f32[32,8,256]{2,1,0:T(8,128)S(1)} collective-permute-done((f32[32,8,256]{2,1,0:T(8,128)S(1)}, f32[32,8,256]{2,1,0:T(8,128)S(1)}, u32[]{:S(2)}, u32[]{:S(2)}) %collective-permute-start.20) | collective-permute-done | bytes 262176 | tf_op jit(solution)/shard_map/ppermute | solution.py:599
  81.7 13.6 %collective-permute-done.22.refs_5_ = f32[32,8,256]{2,1,0:T(8,128)S(1)} collective-permute-done((f32[32,8,256]{2,1,0:T(8,128)S(1)}, f32[32,8,256]{2,1,0:T(8,128)S(1)}, u32[]{:S(2)}, u32[]{:S(2)}) %collective-permute-start.22) | collective-permute-done | bytes 262176 | tf_op jit(solution)/shard_map/ppermute | solution.py:599
  96.4 1.5 collective-permute-start.25
  99.1 5.3 %collective-permute-done.27.refs_12_ = f32[32,8,256]{2,1,0:T(8,128)S(1)} collective-permute-done((f32[32,8,256]{2,1,0:T(8,128)S(1)}, f32[32,8,256]{2,1,0:T(8,128)S(1)}, u32[]{:S(2)}, u32[]{:S(2)}) %collective-permute-start.27) | collective-permute-done | bytes 262176 | tf_op jit(solution)/shard_map/ppermute | solution.py:599
  105.6 1.4 collective-permute-start.37
  107.1 1.3 collective-permute-done.29.refs_13_
  108.4 1.9 %collective-permute-done.26.refs_11_ = f32[32,8,256]{2,1,0:T(8,128)S(1)} collective-permute-done((f32[32,8,256]{2,1,0:T(8,128)S(1)}, f32[32,8,256]{2,1,0:T(8,128)S(1)}, u32[]{:S(2)}, u32[]{:S(2)}) %collective-permute-start.26) | collective-permute-done | bytes 262176 | tf_op jit(solution)/shard_map/ppermute | solution.py:599
  110.8 4.2 %start_solve.1 = (f32[2048,256]{1,0:T(8,128)S(1)}, f32[2048,256]{1,0:T(8,128)S(1)}, f32[2048,256]{1,0:T(8,128)S(1)}, f32[2,32,512]{2,1,0:T(8,128)S(1)}, f32[2,32,512]{2,1,0:T(8,128)S(1)}) custom-call(s32[2]{0:T(128)S(1)} %pad_add_fusion.pos_ref, f32[2,256]{1,0:T(2,128)S(1)} %copy-done.5, f32[7,64,256]{2,1,0:T(8,128)S(1)} %get-tuple-element.196.diag_ref.coef_ref, ...), custom_call_target="tpu_custom_call" | custom-call | flops 1000000 | bytes 100000 | tf_op jit(solution)/shard_map/start_solve/pallas_call | solution.py:348
  115.0 1.6 collective-permute-start.32
  116.7 1.7 collective-permute-start.35
  119.2 3.6 %collective-permute-done.37.refs_6_ = f32[32,8,256]{2,1,0:T(8,128)S(1)} collective-permute-done((f32[32,8,256]{2,1,0:T(8,128)S(1)}, f32[32,8,256]{2,1,0:T(8,128)S(1)}, u32[]{:S(2)}, u32[]{:S(2)}) %collective-permute-start.37) | collective-permute-done | bytes 262176 | tf_op jit(solution)/shard_map/ppermute | solution.py:599
  124.0 4.0 %collective-permute-done.30.refs_2_ = f32[32,8,256]{2,1,0:T(8,128)S(1)} collective-permute-done((f32[32,8,256]{2,1,0:T(8,128)S(1)}, f32[32,8,256]{2,1,0:T(8,128)S(1)}, u32[]{:S(2)}, u32[]{:S(2)}) %collective-permute-start.30) | collective-permute-done | bytes 262176 | tf_op jit(solution)/shard_map/ppermute | solution.py:599
  128.1 3.6 %collective-permute-start.31 = (f32[2,32,512]{2,1,0:T(8,128)S(1)}, f32[2,32,512]{2,1,0:T(8,128)S(1)}, u32[]{:S(2)}, u32[]{:S(2)}) collective-permute-start(f32[2,32,512]{2,1,0:T(8,128)S(1)} %get-tuple-element.330.own_lo_ref), channel_id=1, source_target_pairs={{8,0},{16,8},{24,16},{0,24},{9,1},{17,9},{25,17},{1,25},{10,2},{18... | collective-permute-start | bytes 393224 | tf_op jit(solution)/shard_map/ppermute | solution.py:576
  131.7 2.8 %partial_update.1 = (f32[32,64,256]{2,1,0:T(8,128)S(1)}, f32[32,64,256]{2,1,0:T(8,128)S(1)}, f32[32,64,256]{2,1,0:T(8,128)S(1)}) custom-call(f32[7,64,256]{2,1,0:T(8,128)S(1)} %get-tuple-element.196.diag_ref.coef_ref, bf16[128,192]{1,0:T(8,128)(2,1)S(1)} %get-tuple-element.197.dpack_ref, f32[32,8,256]{2,1,0:T(8,128)S(1)} %get-tuple-element.276.refs_0_, ...), custom_call_target="tpu_custom_call" | custom-call | flops 1000000 | bytes 100000 | tf_op jit(solution)/shard_map/partial_update/pallas_call | solution.py:468
  134.5 6.0 %two_sweeps.2 = (f32[2048,256]{1,0:T(8,128)S(1)}, f32[2,32,512]{2,1,0:T(8,128)S(1)}, f32[2,32,512]{2,1,0:T(8,128)S(1)}) custom-call(s32[2]{0:T(128)S(1)} %pad_add_fusion.pos_ref, f32[2048,256]{1,0:T(8,128)S(1)} %get-tuple-element.326.local_ref, f32[2048,256]{1,0:T(8,128)S(1)} %get-tuple-element.327.source_ref, ...), custom_call_target="tpu_custom_call" | custom-call | flops 1000000 | bytes 100000 | tf_op jit(solution)/shard_map/two_sweeps/pallas_call | solution.py:422
  140.5 2.5 %transform.5 = (f32[32,8,256]{2,1,0:T(8,128)S(1)}, f32[32,8,256]{2,1,0:T(8,128)S(1)}, f32[32,8,256]{2,1,0:T(8,128)S(1)}, f32[32,8,256]{2,1,0:T(8,128)S(1)}, f32[...) custom-call(bf16[512,256]{1,0:T(8,128)(2,1)S(1)} %permuted_table.1.tab, ...), custom_call_target="tpu_custom_call" | custom-call | flops 805306368 | bytes 4194304 | tf_op jit(solution)/shard_map/transform/pallas_call | solution.py:122
  143.1 1.5 collective-permute-start.39
  144.7 3.8 %collective-permute-start.40 = (f32[2,32,512]{2,1,0:T(8,128)S(1)}, f32[2,32,512]{2,1,0:T(8,128)S(1)}, u32[]{:S(2)}, u32[]{:S(2)}) collective-permute-start(f32[2,32,512]{2,1,0:T(8,128)S(1)} %get-tuple-element.354.own_lo_ref), channel_id=1, source_target_pairs={{8,0},{16,8},{24,16},{0,24},{9,1},{17,9},{25,17},{1,25},{10,2},{18... | collective-permute-start | bytes 393224 | tf_op jit(solution)/shard_map/ppermute | solution.py:576
  149.3 3.2 %collective-permute-done.44.refs_7_ = f32[32,8,256]{2,1,0:T(8,128)S(1)} collective-permute-done((f32[32,8,256]{2,1,0:T(8,128)S(1)}, f32[32,8,256]{2,1,0:T(8,128)S(1)}, u32[]{:S(2)}, u32[]{:S(2)}) %collective-permute-start.44) | collective-permute-done | bytes 262176 | tf_op jit(solution)/shard_map/ppermute | solution.py:599
  153.4 3.1 %collective-permute-done.39.refs_6_ = f32[32,8,256]{2,1,0:T(8,128)S(1)} collective-permute-done((f32[32,8,256]{2,1,0:T(8,128)S(1)}, f32[32,8,256]{2,1,0:T(8,128)S(1)}, u32[]{:S(2)}, u32[]{:S(2)}) %collective-permute-start.39) | collective-permute-done | bytes 262176 | tf_op jit(solution)/shard_map/ppermute | solution.py:599
  156.5 2.7 %collective-permute-start.43 = (f32[32,8,256]{2,1,0:T(8,128)S(1)}, f32[32,8,256]{2,1,0:T(8,128)S(1)}, u32[]{:S(2)}, u32[]{:S(2)}) collective-permute-start(f32[32,8,256]{2,1,0:T(8,128)S(1)} %get-tuple-element.360), channel_id=1, source_target_pairs={{0,3},{1,2},{2,1},{3,0},{4,7},{5,6},{6,5},{7,4},{8,11},{9,10},{10,... | collective-permute-start | bytes 786440 | tf_op jit(solution)/shard_map/ppermute | solution.py:599
  159.7 6.4 %two_sweeps.3 = (f32[2048,256]{1,0:T(8,128)S(1)}, f32[1,32,512]{2,1,0:T(8,128)S(1)}, f32[1,32,512]{2,1,0:T(8,128)S(1)}) custom-call(s32[2]{0:T(128)S(1)} %pad_add_fusion.pos_ref, f32[2048,256]{1,0:T(8,128)S(1)} %get-tuple-element.352.local_ref, f32[2048,256]{1,0:T(8,128)S(1)} %get-tuple-element.327.source_ref, ...), custom_call_target="tpu_custom_call" | custom-call | flops 1000000 | bytes 100000 | tf_op jit(solution)/shard_map/two_sweeps/pallas_call | solution.py:422
  166.1 4.0 %collective-permute-start.46 = (f32[1,32,512]{2,1,0:T(8,128)S(1)}, f32[1,32,512]{2,1,0:T(8,128)S(1)}, u32[]{:S(2)}, u32[]{:S(2)}) collective-permute-start(f32[1,32,512]{2,1,0:T(8,128)S(1)} %get-tuple-element.372), channel_id=1, source_target_pairs={{8,0},{16,8},{24,16},{0,24},{9,1},{17,9},{25,17},{1,25},{10,2},{18... | collective-permute-start | bytes 196616 | tf_op jit(solution)/shard_map/ppermute | solution.py:576
  170.1 2.3 %collective-permute-done.46.got_up_ref = f32[1,32,512]{2,1,0:T(8,128)S(1)} collective-permute-done((f32[1,32,512]{2,1,0:T(8,128)S(1)}, f32[1,32,512]{2,1,0:T(8,128)S(1)}, u32[]{:S(2)}, u32[]{:S(2)}) %collective-permute-start.46) | collective-permute-done | bytes 65568 | tf_op jit(solution)/shard_map/ppermute | solution.py:576
  172.4 3.8 %collective-permute-done.47.got_lo_ref = f32[1,32,512]{2,1,0:T(8,128)S(1)} collective-permute-done((f32[1,32,512]{2,1,0:T(8,128)S(1)}, f32[1,32,512]{2,1,0:T(8,128)S(1)}, u32[]{:S(2)}, u32[]{:S(2)}) %collective-permute-start.47) | collective-permute-done | bytes 65568 | tf_op jit(solution)/shard_map/ppermute | solution.py:576
  176.2 3.9 %add_force.1 = (f32[3,32,64,256]{3,2,1,0:T(8,128)}, f32[32,64,256]{2,1,0:T(8,128)S(1)}) custom-call(s32[2]{0:T(128)S(1)} %pad_add_fusion.pos_ref, f32[2048,256]{1,0:T(8,128)S(1)} %get-tuple-element.361.local_ref, f32[1,32,512]{2,1,0:T(8,128)S(1)} %collective-permute-done.46.got_up_ref, f32[1,32,512]{2,1,0:T(8,128)S(1)} %collective-permute-done.47.got_lo_ref, ...), custom_call_target="tpu_custom_call" | custom-call | flops 1000000 | bytes 100000 | tf_op jit(solution)/shard_map/add_force/pallas_call | solution.py:512
  180.1 4.0 %finish.1 = f32[3,32,64,256]{3,2,1,0:T(8,128)} custom-call(s32[2]{0:T(128)S(1)} %pad_add_fusion.pos_ref, f32[7,64,256]{2,1,0:T(8,128)S(1)} %get-tuple-element.196.diag_ref.coef_ref, bf16[128,192]{1,0:T(8,128)(2,1)S(1)} %get-tuple-element.197.dpack_ref, f32[32,64,256]{2,1,0:T(8,128)S(1)} %get-tuple-element.376.px_ref, ...), custom_call_target="tpu_custom_call", output_to_operand_aliasing={{}: (5, {})} | custom-call | flops 1000000 | bytes 100000 | tf_op jit(solution)/shard_map/finish/pallas_call | solution.py:552
  (91 shorter events, 21.4 us)
Async XLA Ops:
  2.9 13.7 %collective-permute-start = (f32[32,8,256]{2,1,0:T(8,128)S(1)}, f32[32,8,256]{2,1,0:T(8,128)S(1)}, u32[]{:S(2)}, u32[]{:S(2)}) collective-permute-start(f32[32,8,256]{2,1,0:T(8,128)S(1)} %get-tuple-element.204), channel_id=1, source_target_pairs={{0,7},{1,6},{2,5},{3,4},{4,3},{5,2},{6,1},{7,0},{8,15},{9,14},{10,... | collective-permute-start | bytes 786440 | tf_op jit(solution)/shard_map/ppermute | solution.py:599
  6.3 22.2 %collective-permute-start.2 = (f32[32,8,256]{2,1,0:T(8,128)S(1)}, f32[32,8,256]{2,1,0:T(8,128)S(1)}, u32[]{:S(2)}, u32[]{:S(2)}) collective-permute-start(f32[32,8,256]{2,1,0:T(8,128)S(1)} %get-tuple-element.208), channel_id=1, source_target_pairs={{0,2},{1,3},{2,0},{3,1},{4,6},{5,7},{6,4},{7,5},{8,10},{9,11},{10,... | collective-permute-start | bytes 786440 | tf_op jit(solution)/shard_map/ppermute | solution.py:599
  6.9 18.4 %collective-permute-start.7 = (f32[32,8,256]{2,1,0:T(8,128)S(1)}, f32[32,8,256]{2,1,0:T(8,128)S(1)}, u32[]{:S(2)}, u32[]{:S(2)}) collective-permute-start(f32[32,8,256]{2,1,0:T(8,128)S(1)} %get-tuple-element.220), channel_id=1, source_target_pairs={{0,6},{1,7},{2,4},{3,5},{4,2},{5,3},{6,0},{7,1},{8,14},{9,15},{10,... | collective-permute-start | bytes 786440 | tf_op jit(solution)/shard_map/ppermute | solution.py:599
  15.1 14.9 %collective-permute-start.6 = (f32[32,8,256]{2,1,0:T(8,128)S(1)}, f32[32,8,256]{2,1,0:T(8,128)S(1)}, u32[]{:S(2)}, u32[]{:S(2)}) collective-permute-start(f32[32,8,256]{2,1,0:T(8,128)S(1)} %get-tuple-element.216), channel_id=1, source_target_pairs={{0,4},{1,5},{2,6},{3,7},{4,0},{5,1},{6,2},{7,3},{8,12},{9,13},{10,... | collective-permute-start | bytes 786440 | tf_op jit(solution)/shard_map/ppermute | solution.py:599
  16.6 14.7 %collective-permute-start.3 = (f32[32,8,256]{2,1,0:T(8,128)S(1)}, f32[32,8,256]{2,1,0:T(8,128)S(1)}, u32[]{:S(2)}, u32[]{:S(2)}) collective-permute-start(f32[32,8,256]{2,1,0:T(8,128)S(1)} %get-tuple-element.211), channel_id=1, source_target_pairs={{0,3},{1,2},{2,1},{3,0},{4,7},{5,6},{6,5},{7,4},{8,11},{9,10},{10,... | collective-permute-start | bytes 786440 | tf_op jit(solution)/shard_map/ppermute | solution.py:599
  16.6 16.2 %collective-permute-start.1 = (f32[32,8,256]{2,1,0:T(8,128)S(1)}, f32[32,8,256]{2,1,0:T(8,128)S(1)}, u32[]{:S(2)}, u32[]{:S(2)}) collective-permute-start(f32[32,8,256]{2,1,0:T(8,128)S(1)} %get-tuple-element.205), channel_id=1, source_target_pairs={{0,1},{1,0},{2,3},{3,2},{4,5},{5,4},{6,7},{7,6},{8,9},{9,8},{10,11... | collective-permute-start | bytes 786440 | tf_op jit(solution)/shard_map/ppermute | solution.py:599
  25.3 19.8 %collective-permute-start.8 = (f32[32,8,256]{2,1,0:T(8,128)S(1)}, f32[32,8,256]{2,1,0:T(8,128)S(1)}, u32[]{:S(2)}, u32[]{:S(2)}) collective-permute-start(f32[32,8,256]{2,1,0:T(8,128)S(1)} %get-tuple-element.221), channel_id=1, source_target_pairs={{0,5},{1,4},{2,7},{3,6},{4,1},{5,0},{6,3},{7,2},{8,13},{9,12},{10,... | collective-permute-start | bytes 786440 | tf_op jit(solution)/shard_map/ppermute | solution.py:599
  28.5 19.0 %collective-permute-start.14 = (f32[32,8,256]{2,1,0:T(8,128)S(1)}, f32[32,8,256]{2,1,0:T(8,128)S(1)}, u32[]{:S(2)}, u32[]{:S(2)}) collective-permute-start(f32[32,8,256]{2,1,0:T(8,128)S(1)} %get-tuple-element.251), channel_id=1, source_target_pairs={{0,6},{1,7},{2,4},{3,5},{4,2},{5,3},{6,0},{7,1},{8,14},{9,15},{10,... | collective-permute-start | bytes 786440 | tf_op jit(solution)/shard_map/ppermute | solution.py:599
  30.0 20.7 %collective-permute-start.9 = (f32[32,8,256]{2,1,0:T(8,128)S(1)}, f32[32,8,256]{2,1,0:T(8,128)S(1)}, u32[]{:S(2)}, u32[]{:S(2)}) collective-permute-start(f32[32,8,256]{2,1,0:T(8,128)S(1)} %get-tuple-element.237), channel_id=1, source_target_pairs={{0,7},{1,6},{2,5},{3,4},{4,3},{5,2},{6,1},{7,0},{8,15},{9,14},{10,... | collective-permute-start | bytes 786440 | tf_op jit(solution)/shard_map/ppermute | solution.py:599
  31.3 19.4 %collective-permute-start.11 = (f32[32,8,256]{2,1,0:T(8,128)S(1)}, f32[32,8,256]{2,1,0:T(8,128)S(1)}, u32[]{:S(2)}, u32[]{:S(2)}) collective-permute-start(f32[32,8,256]{2,1,0:T(8,128)S(1)} %get-tuple-element.241), channel_id=1, source_target_pairs={{0,2},{1,3},{2,0},{3,1},{4,6},{5,7},{6,4},{7,5},{8,10},{9,11},{10,... | collective-permute-start | bytes 786440 | tf_op jit(solution)/shard_map/ppermute | solution.py:599
  47.5 8.4 %collective-permute-start.15 = (f32[32,8,256]{2,1,0:T(8,128)S(1)}, f32[32,8,256]{2,1,0:T(8,128)S(1)}, u32[]{:S(2)}, u32[]{:S(2)}) collective-permute-start(f32[32,8,256]{2,1,0:T(8,128)S(1)} %get-tuple-element.252), channel_id=1, source_target_pairs={{0,5},{1,4},{2,7},{3,6},{4,1},{5,0},{6,3},{7,2},{8,13},{9,12},{10,... | collective-permute-start | bytes 786440 | tf_op jit(solution)/shard_map/ppermute | solution.py:599
  48.9 8.3 %collective-permute-start.12 = (f32[32,8,256]{2,1,0:T(8,128)S(1)}, f32[32,8,256]{2,1,0:T(8,128)S(1)}, u32[]{:S(2)}, u32[]{:S(2)}) collective-permute-start(f32[32,8,256]{2,1,0:T(8,128)S(1)} %get-tuple-element.244), channel_id=1, source_target_pairs={{0,3},{1,2},{2,1},{3,0},{4,7},{5,6},{6,5},{7,4},{8,11},{9,10},{10,... | collective-permute-start | bytes 786440 | tf_op jit(solution)/shard_map/ppermute | solution.py:599
  50.2 17.5 %collective-permute-start.13 = (f32[32,8,256]{2,1,0:T(8,128)S(1)}, f32[32,8,256]{2,1,0:T(8,128)S(1)}, u32[]{:S(2)}, u32[]{:S(2)}) collective-permute-start(f32[32,8,256]{2,1,0:T(8,128)S(1)} %get-tuple-element.247), channel_id=1, source_target_pairs={{0,4},{1,5},{2,6},{3,7},{4,0},{5,1},{6,2},{7,3},{8,12},{9,13},{10,... | collective-permute-start | bytes 786440 | tf_op jit(solution)/shard_map/ppermute | solution.py:599
  50.7 19.4 %collective-permute-start.10 = (f32[32,8,256]{2,1,0:T(8,128)S(1)}, f32[32,8,256]{2,1,0:T(8,128)S(1)}, u32[]{:S(2)}, u32[]{:S(2)}) collective-permute-start(f32[32,8,256]{2,1,0:T(8,128)S(1)} %get-tuple-element.238), channel_id=1, source_target_pairs={{0,1},{1,0},{2,3},{3,2},{4,5},{5,4},{6,7},{7,6},{8,9},{9,8},{10,11... | collective-permute-start | bytes 786440 | tf_op jit(solution)/shard_map/ppermute | solution.py:599
  50.7 21.8 %collective-permute-start.21 = (f32[32,8,256]{2,1,0:T(8,128)S(1)}, f32[32,8,256]{2,1,0:T(8,128)S(1)}, u32[]{:S(2)}, u32[]{:S(2)}) collective-permute-start(f32[32,8,256]{2,1,0:T(8,128)S(1)} %get-tuple-element.293), channel_id=1, source_target_pairs={{0,6},{1,7},{2,4},{3,5},{4,2},{5,3},{6,0},{7,1},{8,14},{9,15},{10,... | collective-permute-start | bytes 786440 | tf_op jit(solution)/shard_map/ppermute | solution.py:599
  56.0 23.0 %collective-permute-start.20 = (f32[32,8,256]{2,1,0:T(8,128)S(1)}, f32[32,8,256]{2,1,0:T(8,128)S(1)}, u32[]{:S(2)}, u32[]{:S(2)}) collective-permute-start(f32[32,8,256]{2,1,0:T(8,128)S(1)} %get-tuple-element.289), channel_id=1, source_target_pairs={{0,4},{1,5},{2,6},{3,7},{4,0},{5,1},{6,2},{7,3},{8,12},{9,13},{10,... | collective-permute-start | bytes 786440 | tf_op jit(solution)/shard_map/ppermute | solution.py:599
  57.2 23.0 %collective-permute-start.18 = (f32[32,8,256]{2,1,0:T(8,128)S(1)}, f32[32,8,256]{2,1,0:T(8,128)S(1)}, u32[]{:S(2)}, u32[]{:S(2)}) collective-permute-start(f32[32,8,256]{2,1,0:T(8,128)S(1)} %get-tuple-element.283), channel_id=1, source_target_pairs={{0,2},{1,3},{2,0},{3,1},{4,6},{5,7},{6,4},{7,5},{8,10},{9,11},{10,... | collective-permute-start | bytes 786440 | tf_op jit(solution)/shard_map/ppermute | solution.py:599
  67.7 13.7 %collective-permute-start.16 = (f32[32,8,256]{2,1,0:T(8,128)S(1)}, f32[32,8,256]{2,1,0:T(8,128)S(1)}, u32[]{:S(2)}, u32[]{:S(2)}) collective-permute-start(f32[32,8,256]{2,1,0:T(8,128)S(1)} %get-tuple-element.279), channel_id=1, source_target_pairs={{0,7},{1,6},{2,5},{3,4},{4,3},{5,2},{6,1},{7,0},{8,15},{9,14},{10,... | collective-permute-start | bytes 786440 | tf_op jit(solution)/shard_map/ppermute | solution.py:599
  72.6 22.7 %collective-permute-start.22 = (f32[32,8,256]{2,1,0:T(8,128)S(1)}, f32[32,8,256]{2,1,0:T(8,128)S(1)}, u32[]{:S(2)}, u32[]{:S(2)}) collective-permute-start(f32[32,8,256]{2,1,0:T(8,128)S(1)} %get-tuple-element.294), channel_id=1, source_target_pairs={{0,5},{1,4},{2,7},{3,6},{4,1},{5,0},{6,3},{7,2},{8,13},{9,12},{10,... | collective-permute-start | bytes 786440 | tf_op jit(solution)/shard_map/ppermute | solution.py:599
  74.0 22.4 %collective-permute-start.19 = (f32[32,8,256]{2,1,0:T(8,128)S(1)}, f32[32,8,256]{2,1,0:T(8,128)S(1)}, u32[]{:S(2)}, u32[]{:S(2)}) collective-permute-start(f32[32,8,256]{2,1,0:T(8,128)S(1)} %get-tuple-element.286), channel_id=1, source_target_pairs={{0,3},{1,2},{2,1},{3,0},{4,7},{5,6},{6,5},{7,4},{8,11},{9,10},{10,... | collective-permute-start | bytes 786440 | tf_op jit(solution)/shard_map/ppermute | solution.py:599
  78.9 19.0 %collective-permute-start.23 = (f32[32,8,256]{2,1,0:T(8,128)S(1)}, f32[32,8,256]{2,1,0:T(8,128)S(1)}, u32[]{:S(2)}, u32[]{:S(2)}) collective-permute-start(f32[32,8,256]{2,1,0:T(8,128)S(1)} %get-tuple-element.301), channel_id=1, source_target_pairs={{0,7},{1,6},{2,5},{3,4},{4,3},{5,2},{6,1},{7,0},{8,15},{9,14},{10,... | collective-permute-start | bytes 786440 | tf_op jit(solution)/shard_map/ppermute | solution.py:599
  80.2 17.7 %collective-permute-start.28 = (f32[32,8,256]{2,1,0:T(8,128)S(1)}, f32[32,8,256]{2,1,0:T(8,128)S(1)}, u32[]{:S(2)}, u32[]{:S(2)}) collective-permute-start(f32[32,8,256]{2,1,0:T(8,128)S(1)} %get-tuple-element.315), channel_id=1, source_target_pairs={{0,6},{1,7},{2,4},{3,5},{4,2},{5,3},{6,0},{7,1},{8,14},{9,15},{10,... | collective-permute-start | bytes 786440 | tf_op jit(solution)/shard_map/ppermute | solution.py:599
  81.4 17.1 %collective-permute-start.17 = (f32[32,8,256]{2,1,0:T(8,128)S(1)}, f32[32,8,256]{2,1,0:T(8,128)S(1)}, u32[]{:S(2)}, u32[]{:S(2)}) collective-permute-start(f32[32,8,256]{2,1,0:T(8,128)S(1)} %get-tuple-element.280), channel_id=1, source_target_pairs={{0,1},{1,0},{2,3},{3,2},{4,5},{5,4},{6,7},{7,6},{8,9},{9,8},{10,11... | collective-permute-start | bytes 786440 | tf_op jit(solution)/shard_map/ppermute | solution.py:599
  95.3 9.2 %collective-permute-start.27 = (f32[32,8,256]{2,1,0:T(8,128)S(1)}, f32[32,8,256]{2,1,0:T(8,128)S(1)}, u32[]{:S(2)}, u32[]{:S(2)}) collective-permute-start(f32[32,8,256]{2,1,0:T(8,128)S(1)} %get-tuple-element.311), channel_id=1, source_target_pairs={{0,4},{1,5},{2,6},{3,7},{4,0},{5,1},{6,2},{7,3},{8,12},{9,13},{10,... | collective-permute-start | bytes 786440 | tf_op jit(solution)/shard_map/ppermute | solution.py:599
  96.4 9.2 %collective-permute-start.25 = (f32[32,8,256]{2,1,0:T(8,128)S(1)}, f32[32,8,256]{2,1,0:T(8,128)S(1)}, u32[]{:S(2)}, u32[]{:S(2)}) collective-permute-start(f32[32,8,256]{2,1,0:T(8,128)S(1)} %get-tuple-element.305), channel_id=1, source_target_pairs={{0,2},{1,3},{2,0},{3,1},{4,6},{5,7},{6,4},{7,5},{8,10},{9,11},{10,... | collective-permute-start | bytes 786440 | tf_op jit(solution)/shard_map/ppermute | solution.py:599
  97.9 9.1 %collective-permute-start.24 = (f32[32,8,256]{2,1,0:T(8,128)S(1)}, f32[32,8,256]{2,1,0:T(8,128)S(1)}, u32[]{:S(2)}, u32[]{:S(2)}) collective-permute-start(f32[32,8,256]{2,1,0:T(8,128)S(1)} %get-tuple-element.302), channel_id=1, source_target_pairs={{0,1},{1,0},{2,3},{3,2},{4,5},{5,4},{6,7},{7,6},{8,9},{9,8},{10,11... | collective-permute-start | bytes 786440 | tf_op jit(solution)/shard_map/ppermute | solution.py:599
  97.9 10.4 %collective-permute-start.29 = (f32[32,8,256]{2,1,0:T(8,128)S(1)}, f32[32,8,256]{2,1,0:T(8,128)S(1)}, u32[]{:S(2)}, u32[]{:S(2)}) collective-permute-start(f32[32,8,256]{2,1,0:T(8,128)S(1)} %get-tuple-element.316), channel_id=1, source_target_pairs={{0,5},{1,4},{2,7},{3,6},{4,1},{5,0},{6,3},{7,2},{8,13},{9,12},{10,... | collective-permute-start | bytes 786440 | tf_op jit(solution)/shard_map/ppermute | solution.py:599
  98.6 11.7 %collective-permute-start.26 = (f32[32,8,256]{2,1,0:T(8,128)S(1)}, f32[32,8,256]{2,1,0:T(8,128)S(1)}, u32[]{:S(2)}, u32[]{:S(2)}) collective-permute-start(f32[32,8,256]{2,1,0:T(8,128)S(1)} %get-tuple-element.308), channel_id=1, source_target_pairs={{0,3},{1,2},{2,1},{3,0},{4,7},{5,6},{6,5},{7,4},{8,11},{9,10},{10,... | collective-permute-start | bytes 786440 | tf_op jit(solution)/shard_map/ppermute | solution.py:599
  104.4 13.9 %collective-permute-start.33 = (f32[32,8,256]{2,1,0:T(8,128)S(1)}, f32[32,8,256]{2,1,0:T(8,128)S(1)}, u32[]{:S(2)}, u32[]{:S(2)}) collective-permute-start(f32[32,8,256]{2,1,0:T(8,128)S(1)} %get-tuple-element.338), channel_id=1, source_target_pairs={{0,7},{1,6},{2,5},{3,4},{4,3},{5,2},{6,1},{7,0},{8,15},{9,14},{10,... | collective-permute-start | bytes 786440 | tf_op jit(solution)/shard_map/ppermute | solution.py:599
  105.6 17.2 %collective-permute-start.37 = (f32[32,8,256]{2,1,0:T(8,128)S(1)}, f32[32,8,256]{2,1,0:T(8,128)S(1)}, u32[]{:S(2)}, u32[]{:S(2)}) collective-permute-start(f32[32,8,256]{2,1,0:T(8,128)S(1)} %get-tuple-element.344), channel_id=1, source_target_pairs={{0,6},{1,7},{2,4},{3,5},{4,2},{5,3},{6,0},{7,1},{8,14},{9,15},{10,... | collective-permute-start | bytes 786440 | tf_op jit(solution)/shard_map/ppermute | solution.py:599
  110.2 17.8 %collective-permute-start.30 = (f32[32,8,256]{2,1,0:T(8,128)S(1)}, f32[32,8,256]{2,1,0:T(8,128)S(1)}, u32[]{:S(2)}, u32[]{:S(2)}) collective-permute-start(f32[32,8,256]{2,1,0:T(8,128)S(1)} %get-tuple-element.325), channel_id=1, source_target_pairs={{0,2},{1,3},{2,0},{3,1},{4,6},{5,7},{6,4},{7,5},{8,10},{9,11},{10,... | collective-permute-start | bytes 786440 | tf_op jit(solution)/shard_map/ppermute | solution.py:599
  115.0 7.8 %collective-permute-start.32 = (f32[2,32,512]{2,1,0:T(8,128)S(1)}, f32[2,32,512]{2,1,0:T(8,128)S(1)}, u32[]{:S(2)}, u32[]{:S(2)}) collective-permute-start(f32[2,32,512]{2,1,0:T(8,128)S(1)} %get-tuple-element.329.own_up_ref), channel_id=1, source_target_pairs={{0,8},{8,16},{16,24},{24,0},{1,9},{9,17},{17,25},{25,1},{2,10},{10... | collective-permute-start | bytes 393224 | tf_op jit(solution)/shard_map/ppermute | solution.py:576
  116.7 23.8 %collective-permute-start.35 = (f32[32,8,256]{2,1,0:T(8,128)S(1)}, f32[32,8,256]{2,1,0:T(8,128)S(1)}, u32[]{:S(2)}, u32[]{:S(2)}) collective-permute-start(f32[32,8,256]{2,1,0:T(8,128)S(1)} %get-tuple-element.341), channel_id=1, source_target_pairs={{0,3},{1,2},{2,1},{3,0},{4,7},{5,6},{6,5},{7,4},{8,11},{9,10},{10,... | collective-permute-start | bytes 786440 | tf_op jit(solution)/shard_map/ppermute | solution.py:599
  118.4 22.1 %collective-permute-start.36 = (f32[32,8,256]{2,1,0:T(8,128)S(1)}, f32[32,8,256]{2,1,0:T(8,128)S(1)}, u32[]{:S(2)}, u32[]{:S(2)}) collective-permute-start(f32[32,8,256]{2,1,0:T(8,128)S(1)} %get-tuple-element.342), channel_id=1, source_target_pairs={{0,4},{1,5},{2,6},{3,7},{4,0},{5,1},{6,2},{7,3},{8,12},{9,13},{10,... | collective-permute-start | bytes 786440 | tf_op jit(solution)/shard_map/ppermute | solution.py:599
  122.8 17.7 %collective-permute-start.34 = (f32[32,8,256]{2,1,0:T(8,128)S(1)}, f32[32,8,256]{2,1,0:T(8,128)S(1)}, u32[]{:S(2)}, u32[]{:S(2)}) collective-permute-start(f32[32,8,256]{2,1,0:T(8,128)S(1)} %get-tuple-element.339), channel_id=1, source_target_pairs={{0,1},{1,0},{2,3},{3,2},{4,5},{5,4},{6,7},{7,6},{8,9},{9,8},{10,11... | collective-permute-start | bytes 786440 | tf_op jit(solution)/shard_map/ppermute | solution.py:599
  122.8 17.7 %collective-permute-start.38 = (f32[32,8,256]{2,1,0:T(8,128)S(1)}, f32[32,8,256]{2,1,0:T(8,128)S(1)}, u32[]{:S(2)}, u32[]{:S(2)}) collective-permute-start(f32[32,8,256]{2,1,0:T(8,128)S(1)} %get-tuple-element.345), channel_id=1, source_target_pairs={{0,5},{1,4},{2,7},{3,6},{4,1},{5,0},{6,3},{7,2},{8,13},{9,12},{10,... | collective-permute-start | bytes 786440 | tf_op jit(solution)/shard_map/ppermute | solution.py:599
  128.1 6.4 %collective-permute-start.31 = (f32[2,32,512]{2,1,0:T(8,128)S(1)}, f32[2,32,512]{2,1,0:T(8,128)S(1)}, u32[]{:S(2)}, u32[]{:S(2)}) collective-permute-start(f32[2,32,512]{2,1,0:T(8,128)S(1)} %get-tuple-element.330.own_lo_ref), channel_id=1, source_target_pairs={{8,0},{16,8},{24,16},{0,24},{9,1},{17,9},{25,17},{1,25},{10,2},{18... | collective-permute-start | bytes 393224 | tf_op jit(solution)/shard_map/ppermute | solution.py:576
  143.0 9.6 %collective-permute-start.44 = (f32[32,8,256]{2,1,0:T(8,128)S(1)}, f32[32,8,256]{2,1,0:T(8,128)S(1)}, u32[]{:S(2)}, u32[]{:S(2)}) collective-permute-start(f32[32,8,256]{2,1,0:T(8,128)S(1)} %get-tuple-element.366), channel_id=1, source_target_pairs={{0,7},{1,6},{2,5},{3,4},{4,3},{5,2},{6,1},{7,0},{8,15},{9,14},{10,... | collective-permute-start | bytes 786440 | tf_op jit(solution)/shard_map/ppermute | solution.py:599
  143.1 13.4 %collective-permute-start.39 = (f32[32,8,256]{2,1,0:T(8,128)S(1)}, f32[32,8,256]{2,1,0:T(8,128)S(1)}, u32[]{:S(2)}, u32[]{:S(2)}) collective-permute-start(f32[32,8,256]{2,1,0:T(8,128)S(1)} %get-tuple-element.350), channel_id=1, source_target_pairs={{0,6},{1,7},{2,4},{3,5},{4,2},{5,3},{6,0},{7,1},{8,14},{9,15},{10,... | collective-permute-start | bytes 786440 | tf_op jit(solution)/shard_map/ppermute | solution.py:599
  144.6 14.6 %collective-permute-start.41 = (f32[2,32,512]{2,1,0:T(8,128)S(1)}, f32[2,32,512]{2,1,0:T(8,128)S(1)}, u32[]{:S(2)}, u32[]{:S(2)}) collective-permute-start(f32[2,32,512]{2,1,0:T(8,128)S(1)} %get-tuple-element.353.own_up_ref), channel_id=1, source_target_pairs={{0,8},{8,16},{16,24},{24,0},{1,9},{9,17},{17,25},{25,1},{2,10},{10... | collective-permute-start | bytes 393224 | tf_op jit(solution)/shard_map/ppermute | solution.py:576
  144.7 14.5 %collective-permute-start.40 = (f32[2,32,512]{2,1,0:T(8,128)S(1)}, f32[2,32,512]{2,1,0:T(8,128)S(1)}, u32[]{:S(2)}, u32[]{:S(2)}) collective-permute-start(f32[2,32,512]{2,1,0:T(8,128)S(1)} %get-tuple-element.354.own_lo_ref), channel_id=1, source_target_pairs={{8,0},{16,8},{24,16},{0,24},{9,1},{17,9},{25,17},{1,25},{10,2},{18... | collective-permute-start | bytes 393224 | tf_op jit(solution)/shard_map/ppermute | solution.py:576
  148.5 17.6 %collective-permute-start.45 = (f32[32,8,256]{2,1,0:T(8,128)S(1)}, f32[32,8,256]{2,1,0:T(8,128)S(1)}, u32[]{:S(2)}, u32[]{:S(2)}) collective-permute-start(f32[32,8,256]{2,1,0:T(8,128)S(1)} %get-tuple-element.371), channel_id=1, source_target_pairs={{0,2},{1,3},{2,0},{3,1},{4,6},{5,7},{6,4},{7,5},{8,10},{9,11},{10,... | collective-permute-start | bytes 786440 | tf_op jit(solution)/shard_map/ppermute | solution.py:599
  152.5 17.6 %collective-permute-start.42 = (f32[32,8,256]{2,1,0:T(8,128)S(1)}, f32[32,8,256]{2,1,0:T(8,128)S(1)}, u32[]{:S(2)}, u32[]{:S(2)}) collective-permute-start(f32[32,8,256]{2,1,0:T(8,128)S(1)} %get-tuple-element.357), channel_id=1, source_target_pairs={{0,4},{1,5},{2,6},{3,7},{4,0},{5,1},{6,2},{7,3},{8,12},{9,13},{10,... | collective-permute-start | bytes 786440 | tf_op jit(solution)/shard_map/ppermute | solution.py:599
  156.5 13.6 %collective-permute-start.43 = (f32[32,8,256]{2,1,0:T(8,128)S(1)}, f32[32,8,256]{2,1,0:T(8,128)S(1)}, u32[]{:S(2)}, u32[]{:S(2)}) collective-permute-start(f32[32,8,256]{2,1,0:T(8,128)S(1)} %get-tuple-element.360), channel_id=1, source_target_pairs={{0,3},{1,2},{2,1},{3,0},{4,7},{5,6},{6,5},{7,4},{8,11},{9,10},{10,... | collective-permute-start | bytes 786440 | tf_op jit(solution)/shard_map/ppermute | solution.py:599
  159.2 20.9 %collective-permute-start.48 = (f32[32,8,256]{2,1,0:T(8,128)S(1)}, f32[32,8,256]{2,1,0:T(8,128)S(1)}, u32[]{:S(2)}, u32[]{:S(2)}) collective-permute-start(f32[32,8,256]{2,1,0:T(8,128)S(1)} %get-tuple-element.380), channel_id=1, source_target_pairs={{0,1},{1,0},{2,3},{3,2},{4,5},{5,4},{6,7},{7,6},{8,9},{9,8},{10,11... | collective-permute-start | bytes 786440 | tf_op jit(solution)/shard_map/ppermute | solution.py:599
  159.2 20.9 %collective-permute-start.49 = (f32[32,8,256]{2,1,0:T(8,128)S(1)}, f32[32,8,256]{2,1,0:T(8,128)S(1)}, u32[]{:S(2)}, u32[]{:S(2)}) collective-permute-start(f32[32,8,256]{2,1,0:T(8,128)S(1)} %get-tuple-element.384), channel_id=1, source_target_pairs={{0,5},{1,4},{2,7},{3,6},{4,1},{5,0},{6,3},{7,2},{8,13},{9,12},{10,... | collective-permute-start | bytes 786440 | tf_op jit(solution)/shard_map/ppermute | solution.py:599
  166.1 6.3 %collective-permute-start.46 = (f32[1,32,512]{2,1,0:T(8,128)S(1)}, f32[1,32,512]{2,1,0:T(8,128)S(1)}, u32[]{:S(2)}, u32[]{:S(2)}) collective-permute-start(f32[1,32,512]{2,1,0:T(8,128)S(1)} %get-tuple-element.372), channel_id=1, source_target_pairs={{8,0},{16,8},{24,16},{0,24},{9,1},{17,9},{25,17},{1,25},{10,2},{18... | collective-permute-start | bytes 196616 | tf_op jit(solution)/shard_map/ppermute | solution.py:576
  170.1 6.1 %collective-permute-start.47 = (f32[1,32,512]{2,1,0:T(8,128)S(1)}, f32[1,32,512]{2,1,0:T(8,128)S(1)}, u32[]{:S(2)}, u32[]{:S(2)}) collective-permute-start(f32[1,32,512]{2,1,0:T(8,128)S(1)} %get-tuple-element.373), channel_id=1, source_target_pairs={{0,8},{8,16},{16,24},{24,0},{1,9},{9,17},{17,25},{25,1},{2,10},{10... | collective-permute-start | bytes 196616 | tf_op jit(solution)/shard_map/ppermute | solution.py:576
  (13 other events, 130.0 us)

commit v9 on v8

--- a/solution.py
+++ b/solution.py
@@ -581,7 +581,7 @@
         self.blocks = list(blocks)
         self.flight = flight
         self.places = {}
-        self.order = sorted(range(1, len(self.blocks)), key=lambda d: (-bin(d >> 1).count("1"), d % 2, d))
+        self.order = sorted(range(1, len(self.blocks)), key=lambda d: (d < 2, d % 2, d))
 
     def hold(self, value):
         if len(self.places) < len(self.order):
@@ -689,13 +689,13 @@
     got = swap_faces(up, lo)
     y_back = collect(transform(y_got, table))
     y_back.send(7)
-    local = y_back.after(local, 0, 1)
+    local = y_back.after(local, 0, 2)
     local, up, lo = two_sweeps(
         1, position, local, source, inverse, (up, lo), got, face, far, spack, gather, scatter, mask
     )
-    up, lo = y_back.after((up, lo), 1, 3)
+    up, lo = y_back.after((up, lo), 2, 4)
     got = swap_faces(up, lo)
-    local = y_back.after(local, 3, 5)
+    local = y_back.after(local, 4, 5)
     filled, px = add_force(position, local, got, face, geometry, dpack, scatter, mask, px, pz)
     return finish(position, y_back.got(), coef, dpack, px, py, filled)
 

time: 184 us -> 165 us (0.90)
  waiting for transfers between devices: 82.4 us -> 64.6 us
    ppermute x42, waiting for transfers between devices: 74.7 us -> 56.1 us  [send(): self.flight.append(lax.ppermute(block, 'four', pairs))]
  transfers between devices with their start and end apart: 50 -> 50, of which waited for: 18 -> 25; matrix products, arithmetic and copies ran while one was open for 0% -> 0% of each run, Pallas kernels for 18% -> 20%
where the time goes in v9:
time: 165 us
  waiting for transfers between devices  64.6 us (39%)
  starting transfers between devices  57.9 us (35%)
  Pallas kernels  41.7 us (25%)
    ppermute x42, waiting for transfers between devices, send(): self.flight.append(lax.ppermute(block, 'four', pairs))  56.1 us
    ppermute x42, starting transfers between devices, send(): self.flight.append(lax.ppermute(block, 'four', pairs))  42 us
    ppermute x8, starting transfers between devices, swap_faces(): return (lax.ppermute(lo, 'dom', down_way), lax.ppermute(up, 'dom', up_way))  15.9 us
    pallas_call x2, Pallas kernels, two_sweeps(): pl.pallas_call(functools.partial(sweeps_kernel, block, keep), out_shape=[...  12.3 us
    ppermute x8, waiting for transfers between devices, swap_faces(): return (lax.ppermute(lo, 'dom', down_way), lax.ppermute(up, 'dom', up_way))  8.42 us
    pallas_call x3, Pallas kernels, transform(): pl.pallas_call(functools.partial(transform_kernel, count), out_shape=[jax...  7.35 us
    pallas_call x3, Pallas kernels, pack(): pl.pallas_call(pack_kernel, out_shape=[jax.ShapeDtypeStruct((per, LINE, e...  4.88 us
    pallas_call x1, Pallas kernels, start_solve(): pl.pallas_call(functools.partial(start_kernel, block, len(z)), out_shape=...  4.31 us
  transfers between devices with their start and end apart: 50, of which 25 were waited for; matrix products, arithmetic and copies ran while one was open for 0% of the time, Pallas kernels for 20%

profile of v9, /device:TPU:0, one launch (start us, length us, event | category | flops | bytes accessed | tf_op | source)
XLA Modules:
  0.0 164.6 jit_solution(543998005810681009)
XLA Ops:
  0.2 2.8 %pack.4 = (f32[32,8,256]{2,1,0:T(8,128)S(1)}, f32[32,8,256]{2,1,0:T(8,128)S(1)}, f32[32,8,256]{2,1,0:T(8,128)S(1)}, f32[32,8,256]{2,1,0:T(8,128)S(1)}, f32[32,8,...) custom-call(s32[2]{0:T(128)S(1)} %pad_add_fusion.pos_ref, ...), custom_call_target="tpu_custom_call" | custom-call | bytes 4194304 | tf_op jit(solution)/shard_map/pack/pallas_call | solution.py:149
  2.9 3.0 %collective-permute-start = (f32[32,8,256]{2,1,0:T(8,128)S(1)}, f32[32,8,256]{2,1,0:T(8,128)S(1)}, u32[]{:S(2)}, u32[]{:S(2)}) collective-permute-start(f32[32,8,256]{2,1,0:T(8,128)S(1)} %get-tuple-element.204), channel_id=1, source_target_pairs={{0,4},{1,5},{2,6},{3,7},{4,0},{5,1},{6,2},{7,3},{8,12},{9,13},{10,... | collective-permute-start | bytes 786440 | tf_op jit(solution)/shard_map/ppermute | solution.py:599
  6.0 1.5 collective-permute-start.2
  8.8 2.1 %collective-permute-start.4 = (f32[2,512]{1,0:T(2,128)S(1)}, f32[2,512]{1,0:T(2,128)S(1)}, u32[]{:S(2)}, u32[]{:S(2)}) collective-permute-start(f32[2,512]{1,0:T(2,128)S(1)} %get-tuple-element.387), channel_id=1, source_target_pairs={{0,8},{8,16},{16,24},{24,0},{1,9},{9,17},{17,25},{25,1},{2,10},{10... | collective-permute-start | bytes 12296 | tf_op jit(solution)/shard_map/ppermute | solution.py:576
  10.9 2.1 %collective-permute-start.3 = (f32[2,512]{1,0:T(2,128)S(1)}, f32[2,512]{1,0:T(2,128)S(1)}, u32[]{:S(2)}, u32[]{:S(2)}) collective-permute-start(f32[2,512]{1,0:T(2,128)S(1)} %get-tuple-element.388), channel_id=1, source_target_pairs={{8,0},{16,8},{24,16},{0,24},{9,1},{17,9},{25,17},{1,25},{10,2},{18... | collective-permute-start | bytes 12296 | tf_op jit(solution)/shard_map/ppermute | solution.py:576
  13.0 1.6 collective-permute-done.4.far_lo_ref
  14.6 2.9 %collective-permute-start.6 = (f32[32,8,256]{2,1,0:T(8,128)S(1)}, f32[32,8,256]{2,1,0:T(8,128)S(1)}, u32[]{:S(2)}, u32[]{:S(2)}) collective-permute-start(f32[32,8,256]{2,1,0:T(8,128)S(1)} %get-tuple-element.217), channel_id=1, source_target_pairs={{0,5},{1,4},{2,7},{3,6},{4,1},{5,0},{6,3},{7,2},{8,13},{9,12},{10,... | collective-permute-start | bytes 786440 | tf_op jit(solution)/shard_map/ppermute | solution.py:599
  19.9 1.7 %collective-permute-start.11 = (f32[32,8,256]{2,1,0:T(8,128)S(1)}, f32[32,8,256]{2,1,0:T(8,128)S(1)}, u32[]{:S(2)}, u32[]{:S(2)}) collective-permute-start(f32[32,8,256]{2,1,0:T(8,128)S(1)} %get-tuple-element.241), channel_id=1, source_target_pairs={{0,2},{1,3},{2,0},{3,1},{4,6},{5,7},{6,4},{7,5},{8,10},{9,11},{10,... | collective-permute-start | bytes 786440 | tf_op jit(solution)/shard_map/ppermute | solution.py:599
  21.7 3.8 %collective-permute-done.5.refs_3_ = f32[32,8,256]{2,1,0:T(8,128)S(1)} collective-permute-done((f32[32,8,256]{2,1,0:T(8,128)S(1)}, f32[32,8,256]{2,1,0:T(8,128)S(1)}, u32[]{:S(2)}, u32[]{:S(2)}) %collective-permute-start.5) | collective-permute-done | bytes 262176 | tf_op jit(solution)/shard_map/ppermute | solution.py:599
  25.4 2.7 %collective-permute-start.14 = (f32[32,8,256]{2,1,0:T(8,128)S(1)}, f32[32,8,256]{2,1,0:T(8,128)S(1)}, u32[]{:S(2)}, u32[]{:S(2)}) collective-permute-start(f32[32,8,256]{2,1,0:T(8,128)S(1)} %get-tuple-element.251), channel_id=1, source_target_pairs={{0,6},{1,7},{2,4},{3,5},{4,2},{5,3},{6,0},{7,1},{8,14},{9,15},{10,... | collective-permute-start | bytes 786440 | tf_op jit(solution)/shard_map/ppermute | solution.py:599
  28.8 2.3 %collective-permute-done.8.refs_7_ = f32[32,8,256]{2,1,0:T(8,128)S(1)} collective-permute-done((f32[32,8,256]{2,1,0:T(8,128)S(1)}, f32[32,8,256]{2,1,0:T(8,128)S(1)}, u32[]{:S(2)}, u32[]{:S(2)}) %collective-permute-start.8) | collective-permute-done | bytes 262176 | tf_op jit(solution)/shard_map/ppermute | solution.py:599
  32.0 2.4 %transform.3 = (f32[32,8,256]{2,1,0:T(8,128)S(1)}, f32[32,8,256]{2,1,0:T(8,128)S(1)}, f32[32,8,256]{2,1,0:T(8,128)S(1)}, f32[32,8,256]{2,1,0:T(8,128)S(1)}, f32[...) custom-call(bf16[512,256]{1,0:T(8,128)(2,1)S(1)} %permuted_table.1.tab, ...), custom_call_target="tpu_custom_call" | custom-call | flops 805306368 | bytes 4194304 | tf_op jit(solution)/shard_map/transform/pallas_call | solution.py:122
  34.5 3.2 %collective-permute-done.11.refs_2_ = f32[32,8,256]{2,1,0:T(8,128)S(1)} collective-permute-done((f32[32,8,256]{2,1,0:T(8,128)S(1)}, f32[32,8,256]{2,1,0:T(8,128)S(1)}, u32[]{:S(2)}, u32[]{:S(2)}) %collective-permute-start.11) | collective-permute-done | bytes 262176 | tf_op jit(solution)/shard_map/ppermute | solution.py:599
  38.3 4.0 %collective-permute-done.14.refs_6_ = f32[32,8,256]{2,1,0:T(8,128)S(1)} collective-permute-done((f32[32,8,256]{2,1,0:T(8,128)S(1)}, f32[32,8,256]{2,1,0:T(8,128)S(1)}, u32[]{:S(2)}, u32[]{:S(2)}) %collective-permute-start.14) | collective-permute-done | bytes 262176 | tf_op jit(solution)/shard_map/ppermute | solution.py:599
  42.4 1.5 collective-permute-start.18
  43.9 3.7 %collective-permute-done.13.refs_5_ = f32[32,8,256]{2,1,0:T(8,128)S(1)} collective-permute-done((f32[32,8,256]{2,1,0:T(8,128)S(1)}, f32[32,8,256]{2,1,0:T(8,128)S(1)}, u32[]{:S(2)}, u32[]{:S(2)}) %collective-permute-start.13) | collective-permute-done | bytes 262176 | tf_op jit(solution)/shard_map/ppermute | solution.py:599
  47.6 3.6 %collective-permute-start.21 = (f32[32,8,256]{2,1,0:T(8,128)S(1)}, f32[32,8,256]{2,1,0:T(8,128)S(1)}, u32[]{:S(2)}, u32[]{:S(2)}) collective-permute-start(f32[32,8,256]{2,1,0:T(8,128)S(1)} %get-tuple-element.293), channel_id=1, source_target_pairs={{0,6},{1,7},{2,4},{3,5},{4,2},{5,3},{6,0},{7,1},{8,14},{9,15},{10,... | collective-permute-start | bytes 786440 | tf_op jit(solution)/shard_map/ppermute | solution.py:599
  51.2 2.4 %collective-permute-done.15.refs_7_ = f32[32,8,256]{2,1,0:T(8,128)S(1)} collective-permute-done((f32[32,8,256]{2,1,0:T(8,128)S(1)}, f32[32,8,256]{2,1,0:T(8,128)S(1)}, u32[]{:S(2)}, u32[]{:S(2)}) %collective-permute-start.15) | collective-permute-done | bytes 262176 | tf_op jit(solution)/shard_map/ppermute | solution.py:599
  56.6 2.4 %transform.4 = (f32[32,8,256]{2,1,0:T(8,128)S(1)}, f32[32,8,256]{2,1,0:T(8,128)S(1)}, f32[32,8,256]{2,1,0:T(8,128)S(1)}, f32[32,8,256]{2,1,0:T(8,128)S(1)}, f32[...) custom-call(bf16[512,256]{1,0:T(8,128)(2,1)S(1)} %permuted_table.1.tab, ...), custom_call_target="tpu_custom_call" | custom-call | flops 805306368 | bytes 4194304 | tf_op jit(solution)/shard_map/transform/pallas_call | solution.py:122
  60.2 4.7 %collective-permute-done.21.refs_6_ = f32[32,8,256]{2,1,0:T(8,128)S(1)} collective-permute-done((f32[32,8,256]{2,1,0:T(8,128)S(1)}, f32[32,8,256]{2,1,0:T(8,128)S(1)}, u32[]{:S(2)}, u32[]{:S(2)}) %collective-permute-start.21) | collective-permute-done | bytes 262176 | tf_op jit(solution)/shard_map/ppermute | solution.py:599
  64.9 1.5 collective-permute-start.25
  66.4 4.1 %collective-permute-done.19.refs_3_ = f32[32,8,256]{2,1,0:T(8,128)S(1)} collective-permute-done((f32[32,8,256]{2,1,0:T(8,128)S(1)}, f32[32,8,256]{2,1,0:T(8,128)S(1)}, u32[]{:S(2)}, u32[]{:S(2)}) %collective-permute-start.19) | collective-permute-done | bytes 262176 | tf_op jit(solution)/shard_map/ppermute | solution.py:599
  70.8 2.3 %collective-permute-start.28 = (f32[32,8,256]{2,1,0:T(8,128)S(1)}, f32[32,8,256]{2,1,0:T(8,128)S(1)}, u32[]{:S(2)}, u32[]{:S(2)}) collective-permute-start(f32[32,8,256]{2,1,0:T(8,128)S(1)} %get-tuple-element.315), channel_id=1, source_target_pairs={{0,6},{1,7},{2,4},{3,5},{4,2},{5,3},{6,0},{7,1},{8,14},{9,15},{10,... | collective-permute-start | bytes 786440 | tf_op jit(solution)/shard_map/ppermute | solution.py:599
  73.1 3.1 %collective-permute-done.22.refs_7_ = f32[32,8,256]{2,1,0:T(8,128)S(1)} collective-permute-done((f32[32,8,256]{2,1,0:T(8,128)S(1)}, f32[32,8,256]{2,1,0:T(8,128)S(1)}, u32[]{:S(2)}, u32[]{:S(2)}) %collective-permute-start.22) | collective-permute-done | bytes 262176 | tf_op jit(solution)/shard_map/ppermute | solution.py:599
  77.1 5.7 %collective-permute-done.25.refs_10_ = f32[32,8,256]{2,1,0:T(8,128)S(1)} collective-permute-done((f32[32,8,256]{2,1,0:T(8,128)S(1)}, f32[32,8,256]{2,1,0:T(8,128)S(1)}, u32[]{:S(2)}, u32[]{:S(2)}) %collective-permute-start.25) | collective-permute-done | bytes 262176 | tf_op jit(solution)/shard_map/ppermute | solution.py:599
  82.7 2.7 %collective-permute-start.27 = (f32[32,8,256]{2,1,0:T(8,128)S(1)}, f32[32,8,256]{2,1,0:T(8,128)S(1)}, u32[]{:S(2)}, u32[]{:S(2)}) collective-permute-start(f32[32,8,256]{2,1,0:T(8,128)S(1)} %get-tuple-element.312), channel_id=1, source_target_pairs={{0,5},{1,4},{2,7},{3,6},{4,1},{5,0},{6,3},{7,2},{8,13},{9,12},{10,... | collective-permute-start | bytes 786440 | tf_op jit(solution)/shard_map/ppermute | solution.py:599
  85.4 1.9 %collective-permute-done.23.refs_12_ = f32[32,8,256]{2,1,0:T(8,128)S(1)} collective-permute-done((f32[32,8,256]{2,1,0:T(8,128)S(1)}, f32[32,8,256]{2,1,0:T(8,128)S(1)}, u32[]{:S(2)}, u32[]{:S(2)}) %collective-permute-start.23) | collective-permute-done | bytes 262176 | tf_op jit(solution)/shard_map/ppermute | solution.py:599
  87.4 1.5 collective-permute-start.35
  88.9 4.1 %collective-permute-done.26.refs_11_ = f32[32,8,256]{2,1,0:T(8,128)S(1)} collective-permute-done((f32[32,8,256]{2,1,0:T(8,128)S(1)}, f32[32,8,256]{2,1,0:T(8,128)S(1)}, u32[]{:S(2)}, u32[]{:S(2)}) %collective-permute-start.26) | collective-permute-done | bytes 262176 | tf_op jit(solution)/shard_map/ppermute | solution.py:599
  93.0 5.7 %collective-permute-done.29.refs_15_ = f32[32,8,256]{2,1,0:T(8,128)S(1)} collective-permute-done((f32[32,8,256]{2,1,0:T(8,128)S(1)}, f32[32,8,256]{2,1,0:T(8,128)S(1)}, u32[]{:S(2)}, u32[]{:S(2)}) %collective-permute-start.29) | collective-permute-done | bytes 262176 | tf_op jit(solution)/shard_map/ppermute | solution.py:599
  99.2 4.3 %start_solve.1 = (f32[2048,256]{1,0:T(8,128)S(1)}, f32[2048,256]{1,0:T(8,128)S(1)}, f32[2048,256]{1,0:T(8,128)S(1)}, f32[2,32,512]{2,1,0:T(8,128)S(1)}, f32[2,32,512]{2,1,0:T(8,128)S(1)}) custom-call(s32[2]{0:T(128)S(1)} %pad_add_fusion.pos_ref, f32[2,256]{1,0:T(2,128)S(1)} %copy-done.5, f32[7,64,256]{2,1,0:T(8,128)S(1)} %get-tuple-element.196.diag_ref.coef_ref, ...), custom_call_target="tpu_custom_call" | custom-call | flops 1000000 | bytes 100000 | tf_op jit(solution)/shard_map/start_solve/pallas_call | solution.py:348
  103.5 1.6 collective-permute-start.32
  105.1 2.3 %collective-permute-start.36 = (f32[32,8,256]{2,1,0:T(8,128)S(1)}, f32[32,8,256]{2,1,0:T(8,128)S(1)}, u32[]{:S(2)}, u32[]{:S(2)}) collective-permute-start(f32[32,8,256]{2,1,0:T(8,128)S(1)} %get-tuple-element.343), channel_id=1, source_target_pairs={{0,3},{1,2},{2,1},{3,0},{4,7},{5,6},{6,5},{7,4},{8,11},{9,10},{10,... | collective-permute-start | bytes 786440 | tf_op jit(solution)/shard_map/ppermute | solution.py:599
  107.8 1.8 %collective-permute-done.33.refs_4_ = f32[32,8,256]{2,1,0:T(8,128)S(1)} collective-permute-done((f32[32,8,256]{2,1,0:T(8,128)S(1)}, f32[32,8,256]{2,1,0:T(8,128)S(1)}, u32[]{:S(2)}, u32[]{:S(2)}) %collective-permute-start.33) | collective-permute-done | bytes 262176 | tf_op jit(solution)/shard_map/ppermute | solution.py:599
  111.6 2.2 %collective-permute-start.31 = (f32[2,32,512]{2,1,0:T(8,128)S(1)}, f32[2,32,512]{2,1,0:T(8,128)S(1)}, u32[]{:S(2)}, u32[]{:S(2)}) collective-permute-start(f32[2,32,512]{2,1,0:T(8,128)S(1)} %get-tuple-element.330.own_lo_ref), channel_id=1, source_target_pairs={{8,0},{16,8},{24,16},{0,24},{9,1},{17,9},{25,17},{1,25},{10,2},{18... | collective-permute-start | bytes 393224 | tf_op jit(solution)/shard_map/ppermute | solution.py:576
  113.8 2.8 %partial_update.1 = (f32[32,64,256]{2,1,0:T(8,128)S(1)}, f32[32,64,256]{2,1,0:T(8,128)S(1)}, f32[32,64,256]{2,1,0:T(8,128)S(1)}) custom-call(f32[7,64,256]{2,1,0:T(8,128)S(1)} %get-tuple-element.196.diag_ref.coef_ref, bf16[128,192]{1,0:T(8,128)(2,1)S(1)} %get-tuple-element.197.dpack_ref, f32[32,8,256]{2,1,0:T(8,128)S(1)} %get-tuple-element.276.refs_0_, ...), custom_call_target="tpu_custom_call" | custom-call | flops 1000000 | bytes 100000 | tf_op jit(solution)/shard_map/partial_update/pallas_call | solution.py:468
  117.0 5.9 %two_sweeps.2 = (f32[2048,256]{1,0:T(8,128)S(1)}, f32[2,32,512]{2,1,0:T(8,128)S(1)}, f32[2,32,512]{2,1,0:T(8,128)S(1)}) custom-call(s32[2]{0:T(128)S(1)} %pad_add_fusion.pos_ref, f32[2048,256]{1,0:T(8,128)S(1)} %get-tuple-element.326.local_ref, f32[2048,256]{1,0:T(8,128)S(1)} %get-tuple-element.327.source_ref, ...), custom_call_target="tpu_custom_call" | custom-call | flops 1000000 | bytes 100000 | tf_op jit(solution)/shard_map/two_sweeps/pallas_call | solution.py:422
  123.0 2.5 %transform.5 = (f32[32,8,256]{2,1,0:T(8,128)S(1)}, f32[32,8,256]{2,1,0:T(8,128)S(1)}, f32[32,8,256]{2,1,0:T(8,128)S(1)}, f32[32,8,256]{2,1,0:T(8,128)S(1)}, f32[...) custom-call(bf16[512,256]{1,0:T(8,128)(2,1)S(1)} %permuted_table.1.tab, ...), custom_call_target="tpu_custom_call" | custom-call | flops 805306368 | bytes 4194304 | tf_op jit(solution)/shard_map/transform/pallas_call | solution.py:122
  125.4 1.7 %collective-permute-start.40 = (f32[32,8,256]{2,1,0:T(8,128)S(1)}, f32[32,8,256]{2,1,0:T(8,128)S(1)}, u32[]{:S(2)}, u32[]{:S(2)}) collective-permute-start(f32[32,8,256]{2,1,0:T(8,128)S(1)} %get-tuple-element.355), channel_id=1, source_target_pairs={{0,4},{1,5},{2,6},{3,7},{4,0},{5,1},{6,2},{7,3},{8,12},{9,13},{10,... | collective-permute-start | bytes 786440 | tf_op jit(solution)/shard_map/ppermute | solution.py:599
  129.0 3.5 %collective-permute-start.41 = (f32[2,32,512]{2,1,0:T(8,128)S(1)}, f32[2,32,512]{2,1,0:T(8,128)S(1)}, u32[]{:S(2)}, u32[]{:S(2)}) collective-permute-start(f32[2,32,512]{2,1,0:T(8,128)S(1)} %get-tuple-element.359.own_lo_ref), channel_id=1, source_target_pairs={{8,0},{16,8},{24,16},{0,24},{9,1},{17,9},{25,17},{1,25},{10,2},{18... | collective-permute-start | bytes 393224 | tf_op jit(solution)/shard_map/ppermute | solution.py:576
  133.4 2.8 %collective-permute-done.39.refs_2_ = f32[32,8,256]{2,1,0:T(8,128)S(1)} collective-permute-done((f32[32,8,256]{2,1,0:T(8,128)S(1)}, f32[32,8,256]{2,1,0:T(8,128)S(1)}, u32[]{:S(2)}, u32[]{:S(2)}) %collective-permute-start.39) | collective-permute-done | bytes 262176 | tf_op jit(solution)/shard_map/ppermute | solution.py:599
  136.6 2.4 %collective-permute-start.49 = (f32[32,8,256]{2,1,0:T(8,128)S(1)}, f32[32,8,256]{2,1,0:T(8,128)S(1)}, u32[]{:S(2)}, u32[]{:S(2)}) collective-permute-start(f32[32,8,256]{2,1,0:T(8,128)S(1)} %get-tuple-element.386), channel_id=1, source_target_pairs={{0,7},{1,6},{2,5},{3,4},{4,3},{5,2},{6,1},{7,0},{8,15},{9,14},{10,... | collective-permute-start | bytes 786440 | tf_op jit(solution)/shard_map/ppermute | solution.py:599
  139.0 6.4 %two_sweeps.3 = (f32[2048,256]{1,0:T(8,128)S(1)}, f32[1,32,512]{2,1,0:T(8,128)S(1)}, f32[1,32,512]{2,1,0:T(8,128)S(1)}) custom-call(s32[2]{0:T(128)S(1)} %pad_add_fusion.pos_ref, f32[2048,256]{1,0:T(8,128)S(1)} %get-tuple-element.357.local_ref, f32[2048,256]{1,0:T(8,128)S(1)} %get-tuple-element.327.source_ref, ...), custom_call_target="tpu_custom_call" | custom-call | flops 1000000 | bytes 100000 | tf_op jit(solution)/shard_map/two_sweeps/pallas_call | solution.py:422
  146.5 4.0 %collective-permute-start.46 = (f32[1,32,512]{2,1,0:T(8,128)S(1)}, f32[1,32,512]{2,1,0:T(8,128)S(1)}, u32[]{:S(2)}, u32[]{:S(2)}) collective-permute-start(f32[1,32,512]{2,1,0:T(8,128)S(1)} %get-tuple-element.372), channel_id=1, source_target_pairs={{8,0},{16,8},{24,16},{0,24},{9,1},{17,9},{25,17},{1,25},{10,2},{18... | collective-permute-start | bytes 196616 | tf_op jit(solution)/shard_map/ppermute | solution.py:576
  150.5 2.5 %collective-permute-done.46.got_up_ref = f32[1,32,512]{2,1,0:T(8,128)S(1)} collective-permute-done((f32[1,32,512]{2,1,0:T(8,128)S(1)}, f32[1,32,512]{2,1,0:T(8,128)S(1)}, u32[]{:S(2)}, u32[]{:S(2)}) %collective-permute-start.46) | collective-permute-done | bytes 65568 | tf_op jit(solution)/shard_map/ppermute | solution.py:576
  152.9 3.8 %collective-permute-done.47.got_lo_ref = f32[1,32,512]{2,1,0:T(8,128)S(1)} collective-permute-done((f32[1,32,512]{2,1,0:T(8,128)S(1)}, f32[1,32,512]{2,1,0:T(8,128)S(1)}, u32[]{:S(2)}, u32[]{:S(2)}) %collective-permute-start.47) | collective-permute-done | bytes 65568 | tf_op jit(solution)/shard_map/ppermute | solution.py:576
  156.7 3.9 %add_force.1 = (f32[3,32,64,256]{3,2,1,0:T(8,128)}, f32[32,64,256]{2,1,0:T(8,128)S(1)}) custom-call(s32[2]{0:T(128)S(1)} %pad_add_fusion.pos_ref, f32[2048,256]{1,0:T(8,128)S(1)} %get-tuple-element.363.local_ref, f32[1,32,512]{2,1,0:T(8,128)S(1)} %collective-permute-done.46.got_up_ref, f32[1,32,512]{2,1,0:T(8,128)S(1)} %collective-permute-done.47.got_lo_ref, ...), custom_call_target="tpu_custom_call" | custom-call | flops 1000000 | bytes 100000 | tf_op jit(solution)/shard_map/add_force/pallas_call | solution.py:512
  160.6 4.0 %finish.1 = f32[3,32,64,256]{3,2,1,0:T(8,128)} custom-call(s32[2]{0:T(128)S(1)} %pad_add_fusion.pos_ref, f32[7,64,256]{2,1,0:T(8,128)S(1)} %get-tuple-element.196.diag_ref.coef_ref, bf16[128,192]{1,0:T(8,128)(2,1)S(1)} %get-tuple-element.197.dpack_ref, f32[32,64,256]{2,1,0:T(8,128)S(1)} %get-tuple-element.376.px_ref, ...), custom_call_target="tpu_custom_call", output_to_operand_aliasing={{}: (5, {})} | custom-call | flops 1000000 | bytes 100000 | tf_op jit(solution)/shard_map/finish/pallas_call | solution.py:552
  (91 shorter events, 19.0 us)
Async XLA Ops:
  2.9 14.5 %collective-permute-start = (f32[32,8,256]{2,1,0:T(8,128)S(1)}, f32[32,8,256]{2,1,0:T(8,128)S(1)}, u32[]{:S(2)}, u32[]{:S(2)}) collective-permute-start(f32[32,8,256]{2,1,0:T(8,128)S(1)} %get-tuple-element.204), channel_id=1, source_target_pairs={{0,4},{1,5},{2,6},{3,7},{4,0},{5,1},{6,2},{7,3},{8,12},{9,13},{10,... | collective-permute-start | bytes 786440 | tf_op jit(solution)/shard_map/ppermute | solution.py:599
  6.0 11.5 %collective-permute-start.2 = (f32[32,8,256]{2,1,0:T(8,128)S(1)}, f32[32,8,256]{2,1,0:T(8,128)S(1)}, u32[]{:S(2)}, u32[]{:S(2)}) collective-permute-start(f32[32,8,256]{2,1,0:T(8,128)S(1)} %get-tuple-element.208), channel_id=1, source_target_pairs={{0,2},{1,3},{2,0},{3,1},{4,6},{5,7},{6,4},{7,5},{8,10},{9,11},{10,... | collective-permute-start | bytes 786440 | tf_op jit(solution)/shard_map/ppermute | solution.py:599
  7.4 12.5 %collective-permute-start.7 = (f32[32,8,256]{2,1,0:T(8,128)S(1)}, f32[32,8,256]{2,1,0:T(8,128)S(1)}, u32[]{:S(2)}, u32[]{:S(2)}) collective-permute-start(f32[32,8,256]{2,1,0:T(8,128)S(1)} %get-tuple-element.220), channel_id=1, source_target_pairs={{0,6},{1,7},{2,4},{3,5},{4,2},{5,3},{6,0},{7,1},{8,14},{9,15},{10,... | collective-permute-start | bytes 786440 | tf_op jit(solution)/shard_map/ppermute | solution.py:599
  8.8 5.7 %collective-permute-start.4 = (f32[2,512]{1,0:T(2,128)S(1)}, f32[2,512]{1,0:T(2,128)S(1)}, u32[]{:S(2)}, u32[]{:S(2)}) collective-permute-start(f32[2,512]{1,0:T(2,128)S(1)} %get-tuple-element.387), channel_id=1, source_target_pairs={{0,8},{8,16},{16,24},{24,0},{1,9},{9,17},{17,25},{25,1},{2,10},{10... | collective-permute-start | bytes 12296 | tf_op jit(solution)/shard_map/ppermute | solution.py:576
  14.5 10.9 %collective-permute-start.5 = (f32[32,8,256]{2,1,0:T(8,128)S(1)}, f32[32,8,256]{2,1,0:T(8,128)S(1)}, u32[]{:S(2)}, u32[]{:S(2)}) collective-permute-start(f32[32,8,256]{2,1,0:T(8,128)S(1)} %get-tuple-element.213), channel_id=1, source_target_pairs={{0,3},{1,2},{2,1},{3,0},{4,7},{5,6},{6,5},{7,4},{8,11},{9,10},{10,... | collective-permute-start | bytes 786440 | tf_op jit(solution)/shard_map/ppermute | solution.py:599
  14.6 10.9 %collective-permute-start.6 = (f32[32,8,256]{2,1,0:T(8,128)S(1)}, f32[32,8,256]{2,1,0:T(8,128)S(1)}, u32[]{:S(2)}, u32[]{:S(2)}) collective-permute-start(f32[32,8,256]{2,1,0:T(8,128)S(1)} %get-tuple-element.217), channel_id=1, source_target_pairs={{0,5},{1,4},{2,7},{3,6},{4,1},{5,0},{6,3},{7,2},{8,13},{9,12},{10,... | collective-permute-start | bytes 786440 | tf_op jit(solution)/shard_map/ppermute | solution.py:599
  17.5 10.7 %collective-permute-start.1 = (f32[32,8,256]{2,1,0:T(8,128)S(1)}, f32[32,8,256]{2,1,0:T(8,128)S(1)}, u32[]{:S(2)}, u32[]{:S(2)}) collective-permute-start(f32[32,8,256]{2,1,0:T(8,128)S(1)} %get-tuple-element.205), channel_id=1, source_target_pairs={{0,1},{1,0},{2,3},{3,2},{4,5},{5,4},{6,7},{7,6},{8,9},{9,8},{10,11... | collective-permute-start | bytes 786440 | tf_op jit(solution)/shard_map/ppermute | solution.py:599
  17.5 13.6 %collective-permute-start.8 = (f32[32,8,256]{2,1,0:T(8,128)S(1)}, f32[32,8,256]{2,1,0:T(8,128)S(1)}, u32[]{:S(2)}, u32[]{:S(2)}) collective-permute-start(f32[32,8,256]{2,1,0:T(8,128)S(1)} %get-tuple-element.223), channel_id=1, source_target_pairs={{0,7},{1,6},{2,5},{3,4},{4,3},{5,2},{6,1},{7,0},{8,15},{9,14},{10,... | collective-permute-start | bytes 786440 | tf_op jit(solution)/shard_map/ppermute | solution.py:599
  19.9 17.7 %collective-permute-start.11 = (f32[32,8,256]{2,1,0:T(8,128)S(1)}, f32[32,8,256]{2,1,0:T(8,128)S(1)}, u32[]{:S(2)}, u32[]{:S(2)}) collective-permute-start(f32[32,8,256]{2,1,0:T(8,128)S(1)} %get-tuple-element.241), channel_id=1, source_target_pairs={{0,2},{1,3},{2,0},{3,1},{4,6},{5,7},{6,4},{7,5},{8,10},{9,11},{10,... | collective-permute-start | bytes 786440 | tf_op jit(solution)/shard_map/ppermute | solution.py:599
  25.4 12.2 %collective-permute-start.9 = (f32[32,8,256]{2,1,0:T(8,128)S(1)}, f32[32,8,256]{2,1,0:T(8,128)S(1)}, u32[]{:S(2)}, u32[]{:S(2)}) collective-permute-start(f32[32,8,256]{2,1,0:T(8,128)S(1)} %get-tuple-element.237), channel_id=1, source_target_pairs={{0,4},{1,5},{2,6},{3,7},{4,0},{5,1},{6,2},{7,3},{8,12},{9,13},{10,... | collective-permute-start | bytes 786440 | tf_op jit(solution)/shard_map/ppermute | solution.py:599
  25.4 16.9 %collective-permute-start.14 = (f32[32,8,256]{2,1,0:T(8,128)S(1)}, f32[32,8,256]{2,1,0:T(8,128)S(1)}, u32[]{:S(2)}, u32[]{:S(2)}) collective-permute-start(f32[32,8,256]{2,1,0:T(8,128)S(1)} %get-tuple-element.251), channel_id=1, source_target_pairs={{0,6},{1,7},{2,4},{3,5},{4,2},{5,3},{6,0},{7,1},{8,14},{9,15},{10,... | collective-permute-start | bytes 786440 | tf_op jit(solution)/shard_map/ppermute | solution.py:599
  28.1 19.4 %collective-permute-start.13 = (f32[32,8,256]{2,1,0:T(8,128)S(1)}, f32[32,8,256]{2,1,0:T(8,128)S(1)}, u32[]{:S(2)}, u32[]{:S(2)}) collective-permute-start(f32[32,8,256]{2,1,0:T(8,128)S(1)} %get-tuple-element.248), channel_id=1, source_target_pairs={{0,5},{1,4},{2,7},{3,6},{4,1},{5,0},{6,3},{7,2},{8,13},{9,12},{10,... | collective-permute-start | bytes 786440 | tf_op jit(solution)/shard_map/ppermute | solution.py:599
  31.1 20.1 %collective-permute-start.12 = (f32[32,8,256]{2,1,0:T(8,128)S(1)}, f32[32,8,256]{2,1,0:T(8,128)S(1)}, u32[]{:S(2)}, u32[]{:S(2)}) collective-permute-start(f32[32,8,256]{2,1,0:T(8,128)S(1)} %get-tuple-element.244), channel_id=1, source_target_pairs={{0,3},{1,2},{2,1},{3,0},{4,7},{5,6},{6,5},{7,4},{8,11},{9,10},{10,... | collective-permute-start | bytes 786440 | tf_op jit(solution)/shard_map/ppermute | solution.py:599
  37.7 15.9 %collective-permute-start.15 = (f32[32,8,256]{2,1,0:T(8,128)S(1)}, f32[32,8,256]{2,1,0:T(8,128)S(1)}, u32[]{:S(2)}, u32[]{:S(2)}) collective-permute-start(f32[32,8,256]{2,1,0:T(8,128)S(1)} %get-tuple-element.254), channel_id=1, source_target_pairs={{0,7},{1,6},{2,5},{3,4},{4,3},{5,2},{6,1},{7,0},{8,15},{9,14},{10,... | collective-permute-start | bytes 786440 | tf_op jit(solution)/shard_map/ppermute | solution.py:599
  37.7 17.9 %collective-permute-start.10 = (f32[32,8,256]{2,1,0:T(8,128)S(1)}, f32[32,8,256]{2,1,0:T(8,128)S(1)}, u32[]{:S(2)}, u32[]{:S(2)}) collective-permute-start(f32[32,8,256]{2,1,0:T(8,128)S(1)} %get-tuple-element.238), channel_id=1, source_target_pairs={{0,1},{1,0},{2,3},{3,2},{4,5},{5,4},{6,7},{7,6},{8,9},{9,8},{10,11... | collective-permute-start | bytes 786440 | tf_op jit(solution)/shard_map/ppermute | solution.py:599
  42.4 17.8 %collective-permute-start.18 = (f32[32,8,256]{2,1,0:T(8,128)S(1)}, f32[32,8,256]{2,1,0:T(8,128)S(1)}, u32[]{:S(2)}, u32[]{:S(2)}) collective-permute-start(f32[32,8,256]{2,1,0:T(8,128)S(1)} %get-tuple-element.283), channel_id=1, source_target_pairs={{0,2},{1,3},{2,0},{3,1},{4,6},{5,7},{6,4},{7,5},{8,10},{9,11},{10,... | collective-permute-start | bytes 786440 | tf_op jit(solution)/shard_map/ppermute | solution.py:599
  47.6 17.3 %collective-permute-start.21 = (f32[32,8,256]{2,1,0:T(8,128)S(1)}, f32[32,8,256]{2,1,0:T(8,128)S(1)}, u32[]{:S(2)}, u32[]{:S(2)}) collective-permute-start(f32[32,8,256]{2,1,0:T(8,128)S(1)} %get-tuple-element.293), channel_id=1, source_target_pairs={{0,6},{1,7},{2,4},{3,5},{4,2},{5,3},{6,0},{7,1},{8,14},{9,15},{10,... | collective-permute-start | bytes 786440 | tf_op jit(solution)/shard_map/ppermute | solution.py:599
  51.2 15.2 %collective-permute-start.16 = (f32[32,8,256]{2,1,0:T(8,128)S(1)}, f32[32,8,256]{2,1,0:T(8,128)S(1)}, u32[]{:S(2)}, u32[]{:S(2)}) collective-permute-start(f32[32,8,256]{2,1,0:T(8,128)S(1)} %get-tuple-element.279), channel_id=1, source_target_pairs={{0,4},{1,5},{2,6},{3,7},{4,0},{5,1},{6,2},{7,3},{8,12},{9,13},{10,... | collective-permute-start | bytes 786440 | tf_op jit(solution)/shard_map/ppermute | solution.py:599
  53.6 16.9 %collective-permute-start.19 = (f32[32,8,256]{2,1,0:T(8,128)S(1)}, f32[32,8,256]{2,1,0:T(8,128)S(1)}, u32[]{:S(2)}, u32[]{:S(2)}) collective-permute-start(f32[32,8,256]{2,1,0:T(8,128)S(1)} %get-tuple-element.286), channel_id=1, source_target_pairs={{0,3},{1,2},{2,1},{3,0},{4,7},{5,6},{6,5},{7,4},{8,11},{9,10},{10,... | collective-permute-start | bytes 786440 | tf_op jit(solution)/shard_map/ppermute | solution.py:599
  55.6 15.2 %collective-permute-start.20 = (f32[32,8,256]{2,1,0:T(8,128)S(1)}, f32[32,8,256]{2,1,0:T(8,128)S(1)}, u32[]{:S(2)}, u32[]{:S(2)}) collective-permute-start(f32[32,8,256]{2,1,0:T(8,128)S(1)} %get-tuple-element.290), channel_id=1, source_target_pairs={{0,5},{1,4},{2,7},{3,6},{4,1},{5,0},{6,3},{7,2},{8,13},{9,12},{10,... | collective-permute-start | bytes 786440 | tf_op jit(solution)/shard_map/ppermute | solution.py:599
  60.2 16.0 %collective-permute-start.22 = (f32[32,8,256]{2,1,0:T(8,128)S(1)}, f32[32,8,256]{2,1,0:T(8,128)S(1)}, u32[]{:S(2)}, u32[]{:S(2)}) collective-permute-start(f32[32,8,256]{2,1,0:T(8,128)S(1)} %get-tuple-element.296), channel_id=1, source_target_pairs={{0,7},{1,6},{2,5},{3,4},{4,3},{5,2},{6,1},{7,0},{8,15},{9,14},{10,... | collective-permute-start | bytes 786440 | tf_op jit(solution)/shard_map/ppermute | solution.py:599
  64.9 17.9 %collective-permute-start.25 = (f32[32,8,256]{2,1,0:T(8,128)S(1)}, f32[32,8,256]{2,1,0:T(8,128)S(1)}, u32[]{:S(2)}, u32[]{:S(2)}) collective-permute-start(f32[32,8,256]{2,1,0:T(8,128)S(1)} %get-tuple-element.305), channel_id=1, source_target_pairs={{0,2},{1,3},{2,0},{3,1},{4,6},{5,7},{6,4},{7,5},{8,10},{9,11},{10,... | collective-permute-start | bytes 786440 | tf_op jit(solution)/shard_map/ppermute | solution.py:599
  66.4 16.4 %collective-permute-start.17 = (f32[32,8,256]{2,1,0:T(8,128)S(1)}, f32[32,8,256]{2,1,0:T(8,128)S(1)}, u32[]{:S(2)}, u32[]{:S(2)}) collective-permute-start(f32[32,8,256]{2,1,0:T(8,128)S(1)} %get-tuple-element.280), channel_id=1, source_target_pairs={{0,1},{1,0},{2,3},{3,2},{4,5},{5,4},{6,7},{7,6},{8,9},{9,8},{10,11... | collective-permute-start | bytes 786440 | tf_op jit(solution)/shard_map/ppermute | solution.py:599
  70.5 16.8 %collective-permute-start.23 = (f32[32,8,256]{2,1,0:T(8,128)S(1)}, f32[32,8,256]{2,1,0:T(8,128)S(1)}, u32[]{:S(2)}, u32[]{:S(2)}) collective-permute-start(f32[32,8,256]{2,1,0:T(8,128)S(1)} %get-tuple-element.301), channel_id=1, source_target_pairs={{0,4},{1,5},{2,6},{3,7},{4,0},{5,1},{6,2},{7,3},{8,12},{9,13},{10,... | collective-permute-start | bytes 786440 | tf_op jit(solution)/shard_map/ppermute | solution.py:599
  70.8 16.6 %collective-permute-start.28 = (f32[32,8,256]{2,1,0:T(8,128)S(1)}, f32[32,8,256]{2,1,0:T(8,128)S(1)}, u32[]{:S(2)}, u32[]{:S(2)}) collective-permute-start(f32[32,8,256]{2,1,0:T(8,128)S(1)} %get-tuple-element.315), channel_id=1, source_target_pairs={{0,6},{1,7},{2,4},{3,5},{4,2},{5,3},{6,0},{7,1},{8,14},{9,15},{10,... | collective-permute-start | bytes 786440 | tf_op jit(solution)/shard_map/ppermute | solution.py:599
  76.2 16.9 %collective-permute-start.26 = (f32[32,8,256]{2,1,0:T(8,128)S(1)}, f32[32,8,256]{2,1,0:T(8,128)S(1)}, u32[]{:S(2)}, u32[]{:S(2)}) collective-permute-start(f32[32,8,256]{2,1,0:T(8,128)S(1)} %get-tuple-element.308), channel_id=1, source_target_pairs={{0,3},{1,2},{2,1},{3,0},{4,7},{5,6},{6,5},{7,4},{8,11},{9,10},{10,... | collective-permute-start | bytes 786440 | tf_op jit(solution)/shard_map/ppermute | solution.py:599
  82.7 15.9 %collective-permute-start.29 = (f32[32,8,256]{2,1,0:T(8,128)S(1)}, f32[32,8,256]{2,1,0:T(8,128)S(1)}, u32[]{:S(2)}, u32[]{:S(2)}) collective-permute-start(f32[32,8,256]{2,1,0:T(8,128)S(1)} %get-tuple-element.318), channel_id=1, source_target_pairs={{0,7},{1,6},{2,5},{3,4},{4,3},{5,2},{6,1},{7,0},{8,15},{9,14},{10,... | collective-permute-start | bytes 786440 | tf_op jit(solution)/shard_map/ppermute | solution.py:599
  82.7 15.9 %collective-permute-start.27 = (f32[32,8,256]{2,1,0:T(8,128)S(1)}, f32[32,8,256]{2,1,0:T(8,128)S(1)}, u32[]{:S(2)}, u32[]{:S(2)}) collective-permute-start(f32[32,8,256]{2,1,0:T(8,128)S(1)} %get-tuple-element.312), channel_id=1, source_target_pairs={{0,5},{1,4},{2,7},{3,6},{4,1},{5,0},{6,3},{7,2},{8,13},{9,12},{10,... | collective-permute-start | bytes 786440 | tf_op jit(solution)/shard_map/ppermute | solution.py:599
  87.3 11.9 %collective-permute-start.24 = (f32[32,8,256]{2,1,0:T(8,128)S(1)}, f32[32,8,256]{2,1,0:T(8,128)S(1)}, u32[]{:S(2)}, u32[]{:S(2)}) collective-permute-start(f32[32,8,256]{2,1,0:T(8,128)S(1)} %get-tuple-element.302), channel_id=1, source_target_pairs={{0,1},{1,0},{2,3},{3,2},{4,5},{5,4},{6,7},{7,6},{8,9},{9,8},{10,11... | collective-permute-start | bytes 786440 | tf_op jit(solution)/shard_map/ppermute | solution.py:599
  87.4 20.0 %collective-permute-start.35 = (f32[32,8,256]{2,1,0:T(8,128)S(1)}, f32[32,8,256]{2,1,0:T(8,128)S(1)}, u32[]{:S(2)}, u32[]{:S(2)}) collective-permute-start(f32[32,8,256]{2,1,0:T(8,128)S(1)} %get-tuple-element.341), channel_id=1, source_target_pairs={{0,2},{1,3},{2,0},{3,1},{4,6},{5,7},{6,4},{7,5},{8,10},{9,11},{10,... | collective-permute-start | bytes 786440 | tf_op jit(solution)/shard_map/ppermute | solution.py:599
  93.0 16.6 %collective-permute-start.33 = (f32[32,8,256]{2,1,0:T(8,128)S(1)}, f32[32,8,256]{2,1,0:T(8,128)S(1)}, u32[]{:S(2)}, u32[]{:S(2)}) collective-permute-start(f32[32,8,256]{2,1,0:T(8,128)S(1)} %get-tuple-element.338), channel_id=1, source_target_pairs={{0,4},{1,5},{2,6},{3,7},{4,0},{5,1},{6,2},{7,3},{8,12},{9,13},{10,... | collective-permute-start | bytes 786440 | tf_op jit(solution)/shard_map/ppermute | solution.py:599
  98.7 12.9 %collective-permute-start.30 = (f32[32,8,256]{2,1,0:T(8,128)S(1)}, f32[32,8,256]{2,1,0:T(8,128)S(1)}, u32[]{:S(2)}, u32[]{:S(2)}) collective-permute-start(f32[32,8,256]{2,1,0:T(8,128)S(1)} %get-tuple-element.325), channel_id=1, source_target_pairs={{0,6},{1,7},{2,4},{3,5},{4,2},{5,3},{6,0},{7,1},{8,14},{9,15},{10,... | collective-permute-start | bytes 786440 | tf_op jit(solution)/shard_map/ppermute | solution.py:599
  103.5 6.8 %collective-permute-start.32 = (f32[2,32,512]{2,1,0:T(8,128)S(1)}, f32[2,32,512]{2,1,0:T(8,128)S(1)}, u32[]{:S(2)}, u32[]{:S(2)}) collective-permute-start(f32[2,32,512]{2,1,0:T(8,128)S(1)} %get-tuple-element.329.own_up_ref), channel_id=1, source_target_pairs={{0,8},{8,16},{16,24},{24,0},{1,9},{9,17},{17,25},{25,1},{2,10},{10... | collective-permute-start | bytes 393224 | tf_op jit(solution)/shard_map/ppermute | solution.py:576
  105.1 17.8 %collective-permute-start.36 = (f32[32,8,256]{2,1,0:T(8,128)S(1)}, f32[32,8,256]{2,1,0:T(8,128)S(1)}, u32[]{:S(2)}, u32[]{:S(2)}) collective-permute-start(f32[32,8,256]{2,1,0:T(8,128)S(1)} %get-tuple-element.343), channel_id=1, source_target_pairs={{0,3},{1,2},{2,1},{3,0},{4,7},{5,6},{6,5},{7,4},{8,11},{9,10},{10,... | collective-permute-start | bytes 786440 | tf_op jit(solution)/shard_map/ppermute | solution.py:599
  107.4 15.5 %collective-permute-start.37 = (f32[32,8,256]{2,1,0:T(8,128)S(1)}, f32[32,8,256]{2,1,0:T(8,128)S(1)}, u32[]{:S(2)}, u32[]{:S(2)}) collective-permute-start(f32[32,8,256]{2,1,0:T(8,128)S(1)} %get-tuple-element.345), channel_id=1, source_target_pairs={{0,5},{1,4},{2,7},{3,6},{4,1},{5,0},{6,3},{7,2},{8,13},{9,12},{10,... | collective-permute-start | bytes 786440 | tf_op jit(solution)/shard_map/ppermute | solution.py:599
  109.6 13.3 %collective-permute-start.38 = (f32[32,8,256]{2,1,0:T(8,128)S(1)}, f32[32,8,256]{2,1,0:T(8,128)S(1)}, u32[]{:S(2)}, u32[]{:S(2)}) collective-permute-start(f32[32,8,256]{2,1,0:T(8,128)S(1)} %get-tuple-element.347), channel_id=1, source_target_pairs={{0,7},{1,6},{2,5},{3,4},{4,3},{5,2},{6,1},{7,0},{8,15},{9,14},{10,... | collective-permute-start | bytes 786440 | tf_op jit(solution)/shard_map/ppermute | solution.py:599
  110.3 12.6 %collective-permute-start.34 = (f32[32,8,256]{2,1,0:T(8,128)S(1)}, f32[32,8,256]{2,1,0:T(8,128)S(1)}, u32[]{:S(2)}, u32[]{:S(2)}) collective-permute-start(f32[32,8,256]{2,1,0:T(8,128)S(1)} %get-tuple-element.339), channel_id=1, source_target_pairs={{0,1},{1,0},{2,3},{3,2},{4,5},{5,4},{6,7},{7,6},{8,9},{9,8},{10,11... | collective-permute-start | bytes 786440 | tf_op jit(solution)/shard_map/ppermute | solution.py:599
  125.4 7.9 %collective-permute-start.40 = (f32[32,8,256]{2,1,0:T(8,128)S(1)}, f32[32,8,256]{2,1,0:T(8,128)S(1)}, u32[]{:S(2)}, u32[]{:S(2)}) collective-permute-start(f32[32,8,256]{2,1,0:T(8,128)S(1)} %get-tuple-element.355), channel_id=1, source_target_pairs={{0,4},{1,5},{2,6},{3,7},{4,0},{5,1},{6,2},{7,3},{8,12},{9,13},{10,... | collective-permute-start | bytes 786440 | tf_op jit(solution)/shard_map/ppermute | solution.py:599
  127.2 9.1 %collective-permute-start.39 = (f32[32,8,256]{2,1,0:T(8,128)S(1)}, f32[32,8,256]{2,1,0:T(8,128)S(1)}, u32[]{:S(2)}, u32[]{:S(2)}) collective-permute-start(f32[32,8,256]{2,1,0:T(8,128)S(1)} %get-tuple-element.350), channel_id=1, source_target_pairs={{0,2},{1,3},{2,0},{3,1},{4,6},{5,7},{6,4},{7,5},{8,10},{9,11},{10,... | collective-permute-start | bytes 786440 | tf_op jit(solution)/shard_map/ppermute | solution.py:599
  128.5 8.1 %collective-permute-start.42 = (f32[2,32,512]{2,1,0:T(8,128)S(1)}, f32[2,32,512]{2,1,0:T(8,128)S(1)}, u32[]{:S(2)}, u32[]{:S(2)}) collective-permute-start(f32[2,32,512]{2,1,0:T(8,128)S(1)} %get-tuple-element.358.own_up_ref), channel_id=1, source_target_pairs={{0,8},{8,16},{16,24},{24,0},{1,9},{9,17},{17,25},{25,1},{2,10},{10... | collective-permute-start | bytes 393224 | tf_op jit(solution)/shard_map/ppermute | solution.py:576
  129.0 7.6 %collective-permute-start.41 = (f32[2,32,512]{2,1,0:T(8,128)S(1)}, f32[2,32,512]{2,1,0:T(8,128)S(1)}, u32[]{:S(2)}, u32[]{:S(2)}) collective-permute-start(f32[2,32,512]{2,1,0:T(8,128)S(1)} %get-tuple-element.359.own_lo_ref), channel_id=1, source_target_pairs={{8,0},{16,8},{24,16},{0,24},{9,1},{17,9},{25,17},{1,25},{10,2},{18... | collective-permute-start | bytes 393224 | tf_op jit(solution)/shard_map/ppermute | solution.py:576
  132.5 12.9 %collective-permute-start.44 = (f32[32,8,256]{2,1,0:T(8,128)S(1)}, f32[32,8,256]{2,1,0:T(8,128)S(1)}, u32[]{:S(2)}, u32[]{:S(2)}) collective-permute-start(f32[32,8,256]{2,1,0:T(8,128)S(1)} %get-tuple-element.367), channel_id=1, source_target_pairs={{0,6},{1,7},{2,4},{3,5},{4,2},{5,3},{6,0},{7,1},{8,14},{9,15},{10,... | collective-permute-start | bytes 786440 | tf_op jit(solution)/shard_map/ppermute | solution.py:599
  133.4 13.1 %collective-permute-start.45 = (f32[32,8,256]{2,1,0:T(8,128)S(1)}, f32[32,8,256]{2,1,0:T(8,128)S(1)}, u32[]{:S(2)}, u32[]{:S(2)}) collective-permute-start(f32[32,8,256]{2,1,0:T(8,128)S(1)} %get-tuple-element.371), channel_id=1, source_target_pairs={{0,3},{1,2},{2,1},{3,0},{4,7},{5,6},{6,5},{7,4},{8,11},{9,10},{10,... | collective-permute-start | bytes 786440 | tf_op jit(solution)/shard_map/ppermute | solution.py:599
  136.3 14.2 %collective-permute-start.43 = (f32[32,8,256]{2,1,0:T(8,128)S(1)}, f32[32,8,256]{2,1,0:T(8,128)S(1)}, u32[]{:S(2)}, u32[]{:S(2)}) collective-permute-start(f32[32,8,256]{2,1,0:T(8,128)S(1)} %get-tuple-element.362), channel_id=1, source_target_pairs={{0,5},{1,4},{2,7},{3,6},{4,1},{5,0},{6,3},{7,2},{8,13},{9,12},{10,... | collective-permute-start | bytes 786440 | tf_op jit(solution)/shard_map/ppermute | solution.py:599
  136.6 24.1 %collective-permute-start.48 = (f32[32,8,256]{2,1,0:T(8,128)S(1)}, f32[32,8,256]{2,1,0:T(8,128)S(1)}, u32[]{:S(2)}, u32[]{:S(2)}) collective-permute-start(f32[32,8,256]{2,1,0:T(8,128)S(1)} %get-tuple-element.380), channel_id=1, source_target_pairs={{0,1},{1,0},{2,3},{3,2},{4,5},{5,4},{6,7},{7,6},{8,9},{9,8},{10,11... | collective-permute-start | bytes 786440 | tf_op jit(solution)/shard_map/ppermute | solution.py:599
  136.6 24.0 %collective-permute-start.49 = (f32[32,8,256]{2,1,0:T(8,128)S(1)}, f32[32,8,256]{2,1,0:T(8,128)S(1)}, u32[]{:S(2)}, u32[]{:S(2)}) collective-permute-start(f32[32,8,256]{2,1,0:T(8,128)S(1)} %get-tuple-element.386), channel_id=1, source_target_pairs={{0,7},{1,6},{2,5},{3,4},{4,3},{5,2},{6,1},{7,0},{8,15},{9,14},{10,... | collective-permute-start | bytes 786440 | tf_op jit(solution)/shard_map/ppermute | solution.py:599
  146.5 6.4 %collective-permute-start.46 = (f32[1,32,512]{2,1,0:T(8,128)S(1)}, f32[1,32,512]{2,1,0:T(8,128)S(1)}, u32[]{:S(2)}, u32[]{:S(2)}) collective-permute-start(f32[1,32,512]{2,1,0:T(8,128)S(1)} %get-tuple-element.372), channel_id=1, source_target_pairs={{8,0},{16,8},{24,16},{0,24},{9,1},{17,9},{25,17},{1,25},{10,2},{18... | collective-permute-start | bytes 196616 | tf_op jit(solution)/shard_map/ppermute | solution.py:576
  150.5 6.2 %collective-permute-start.47 = (f32[1,32,512]{2,1,0:T(8,128)S(1)}, f32[1,32,512]{2,1,0:T(8,128)S(1)}, u32[]{:S(2)}, u32[]{:S(2)}) collective-permute-start(f32[1,32,512]{2,1,0:T(8,128)S(1)} %get-tuple-element.373), channel_id=1, source_target_pairs={{0,8},{8,16},{16,24},{24,0},{1,9},{9,17},{17,25},{25,1},{2,10},{10... | collective-permute-start | bytes 196616 | tf_op jit(solution)/shard_map/ppermute | solution.py:576
  (13 other events, 105.6 us)

commit v10 on v9

--- a/solution.py
+++ b/solution.py
@@ -292,8 +292,8 @@
     return (1.0 - RELAXATION) * pot + inverse * (source - applied)
 
 
-def coef_block(coefs):
-    return 8 if coefs % 8 == 0 else coefs
+def coef_block(coefs, block=8):
+    return block if coefs % block == 0 else coefs
 
 
 def start_kernel(
@@ -413,7 +413,7 @@
     elements = local.shape[1]
     coefs = local.shape[0] // nodes
     shared = gather.shape[2]
-    block = coef_block(coefs)
+    block = coef_block(coefs, 16)
     flat = pl.BlockSpec((block * nodes, elements), lambda i: (i, 0))
     one = pl.BlockSpec((1, block, shared), lambda i: (0, i, 0))
     two = pl.BlockSpec((2, block, shared), lambda i: (0, i, 0))
@@ -546,7 +546,7 @@
 def finish(position, y, coef, dpack, px, py, filled):
     coefs, part, elements = y[0].shape
     nodes = len(y) * part
-    block = coef_block(coefs)
+    block = coef_block(coefs, 4)
     field = pl.BlockSpec((block, part, elements), lambda i: (i, 0, 0))
     own = pl.BlockSpec((block, nodes, elements), lambda i: (i, 0, 0))
     return pl.pallas_call(
@@ -688,14 +688,16 @@
     y_got[0], local = lax.optimization_barrier((y_got[0], local))
     got = swap_faces(up, lo)
     y_back = collect(transform(y_got, table))
-    y_back.send(7)
+    y_back.send(6)
     local = y_back.after(local, 0, 2)
     local, up, lo = two_sweeps(
         1, position, local, source, inverse, (up, lo), got, face, far, spack, gather, scatter, mask
     )
-    up, lo = y_back.after((up, lo), 2, 4)
+    up = y_back.hold(up)
+    y_back.send(1)
+    up, lo = y_back.after((up, lo), 2, 3)
     got = swap_faces(up, lo)
-    local = y_back.after(local, 4, 5)
+    local = y_back.after(local, 4, 6)
     filled, px = add_force(position, local, got, face, geometry, dpack, scatter, mask, px, pz)
     return finish(position, y_back.got(), coef, dpack, px, py, filled)
 

time: 165 us -> 169 us (1.024)
  waiting for transfers between devices: 64.6 us -> 67.2 us
    ppermute x42, waiting for transfers between devices: 56.1 us -> 61 us  [send(): self.flight.append(lax.ppermute(block, 'four', pairs))]
    ppermute x8, waiting for transfers between devices: 8.42 us -> 6.24 us  [swap_faces(): return (lax.ppermute(lo, 'dom', down_way), lax.ppermute(up, 'dom', up_way))]
  transfers between devices with their start and end apart: 50 -> 50, of which waited for: 25 -> 25; matrix products, arithmetic and copies ran while one was open for 0% -> 0% of each run, Pallas kernels for 20% -> 19%
where the time goes in v10:
time: 169 us
  waiting for transfers between devices  67.2 us (40%)
  starting transfers between devices  58.8 us (35%)
  Pallas kernels  42.3 us (25%)
    ppermute x42, waiting for transfers between devices, send(): self.flight.append(lax.ppermute(block, 'four', pairs))  61 us
    ppermute x42, starting transfers between devices, send(): self.flight.append(lax.ppermute(block, 'four', pairs))  43.1 us
    ppermute x8, starting transfers between devices, swap_faces(): return (lax.ppermute(lo, 'dom', down_way), lax.ppermute(up, 'dom', up_way))  15.6 us
    pallas_call x2, Pallas kernels, two_sweeps(): pl.pallas_call(functools.partial(sweeps_kernel, block, keep), out_shape=[...  11.6 us
    pallas_call x3, Pallas kernels, transform(): pl.pallas_call(functools.partial(transform_kernel, count), out_shape=[jax...  7.35 us
    ppermute x8, waiting for transfers between devices, swap_faces(): return (lax.ppermute(lo, 'dom', down_way), lax.ppermute(up, 'dom', up_way))  6.24 us
    pallas_call x1, Pallas kernels, finish(): pl.pallas_call(functools.partial(finish_kernel, block, len(y)), out_shape...  5.26 us
    pallas_call x3, Pallas kernels, pack(): pl.pallas_call(pack_kernel, out_shape=[jax.ShapeDtypeStruct((per, LINE, e...  4.88 us
  transfers between devices with their start and end apart: 50, of which 25 were waited for; matrix products, arithmetic and copies ran while one was open for 0% of the time, Pallas kernels for 19%

profile of v10, /device:TPU:0, one launch (start us, length us, event | category | flops | bytes accessed | tf_op | source)
XLA Modules:
  0.0 168.8 jit_solution(11118803564781539387)
XLA Ops:
  0.2 2.8 %pack.4 = (f32[32,8,256]{2,1,0:T(8,128)S(1)}, f32[32,8,256]{2,1,0:T(8,128)S(1)}, f32[32,8,256]{2,1,0:T(8,128)S(1)}, f32[32,8,256]{2,1,0:T(8,128)S(1)}, f32[32,8,...) custom-call(s32[2]{0:T(128)S(1)} %pad_add_fusion.pos_ref, ...), custom_call_target="tpu_custom_call" | custom-call | bytes 4194304 | tf_op jit(solution)/shard_map/pack/pallas_call | solution.py:149
  2.9 3.0 %collective-permute-start = (f32[32,8,256]{2,1,0:T(8,128)S(1)}, f32[32,8,256]{2,1,0:T(8,128)S(1)}, u32[]{:S(2)}, u32[]{:S(2)}) collective-permute-start(f32[32,8,256]{2,1,0:T(8,128)S(1)} %get-tuple-element.205), channel_id=1, source_target_pairs={{0,4},{1,5},{2,6},{3,7},{4,0},{5,1},{6,2},{7,3},{8,12},{9,13},{10,... | collective-permute-start | bytes 786440 | tf_op jit(solution)/shard_map/ppermute | solution.py:599
  6.0 1.5 collective-permute-start.2
  8.8 2.1 %collective-permute-start.4 = (f32[2,512]{1,0:T(2,128)S(1)}, f32[2,512]{1,0:T(2,128)S(1)}, u32[]{:S(2)}, u32[]{:S(2)}) collective-permute-start(f32[2,512]{1,0:T(2,128)S(1)} %get-tuple-element.389), channel_id=1, source_target_pairs={{0,8},{8,16},{16,24},{24,0},{1,9},{9,17},{17,25},{25,1},{2,10},{10... | collective-permute-start | bytes 12296 | tf_op jit(solution)/shard_map/ppermute | solution.py:576
  10.9 2.1 %collective-permute-start.3 = (f32[2,512]{1,0:T(2,128)S(1)}, f32[2,512]{1,0:T(2,128)S(1)}, u32[]{:S(2)}, u32[]{:S(2)}) collective-permute-start(f32[2,512]{1,0:T(2,128)S(1)} %get-tuple-element.390), channel_id=1, source_target_pairs={{8,0},{16,8},{24,16},{0,24},{9,1},{17,9},{25,17},{1,25},{10,2},{18... | collective-permute-start | bytes 12296 | tf_op jit(solution)/shard_map/ppermute | solution.py:576
  13.0 1.6 collective-permute-done.4.far_lo_ref
  14.6 2.9 %collective-permute-start.6 = (f32[32,8,256]{2,1,0:T(8,128)S(1)}, f32[32,8,256]{2,1,0:T(8,128)S(1)}, u32[]{:S(2)}, u32[]{:S(2)}) collective-permute-start(f32[32,8,256]{2,1,0:T(8,128)S(1)} %get-tuple-element.218), channel_id=1, source_target_pairs={{0,5},{1,4},{2,7},{3,6},{4,1},{5,0},{6,3},{7,2},{8,13},{9,12},{10,... | collective-permute-start | bytes 786440 | tf_op jit(solution)/shard_map/ppermute | solution.py:599
  19.9 1.7 %collective-permute-start.11 = (f32[32,8,256]{2,1,0:T(8,128)S(1)}, f32[32,8,256]{2,1,0:T(8,128)S(1)}, u32[]{:S(2)}, u32[]{:S(2)}) collective-permute-start(f32[32,8,256]{2,1,0:T(8,128)S(1)} %get-tuple-element.242), channel_id=1, source_target_pairs={{0,2},{1,3},{2,0},{3,1},{4,6},{5,7},{6,4},{7,5},{8,10},{9,11},{10,... | collective-permute-start | bytes 786440 | tf_op jit(solution)/shard_map/ppermute | solution.py:599
  21.7 3.8 %collective-permute-done.5.refs_3_ = f32[32,8,256]{2,1,0:T(8,128)S(1)} collective-permute-done((f32[32,8,256]{2,1,0:T(8,128)S(1)}, f32[32,8,256]{2,1,0:T(8,128)S(1)}, u32[]{:S(2)}, u32[]{:S(2)}) %collective-permute-start.5) | collective-permute-done | bytes 262176 | tf_op jit(solution)/shard_map/ppermute | solution.py:599
  25.4 2.7 %collective-permute-start.14 = (f32[32,8,256]{2,1,0:T(8,128)S(1)}, f32[32,8,256]{2,1,0:T(8,128)S(1)}, u32[]{:S(2)}, u32[]{:S(2)}) collective-permute-start(f32[32,8,256]{2,1,0:T(8,128)S(1)} %get-tuple-element.252), channel_id=1, source_target_pairs={{0,6},{1,7},{2,4},{3,5},{4,2},{5,3},{6,0},{7,1},{8,14},{9,15},{10,... | collective-permute-start | bytes 786440 | tf_op jit(solution)/shard_map/ppermute | solution.py:599
  28.8 2.3 %collective-permute-done.8.refs_7_ = f32[32,8,256]{2,1,0:T(8,128)S(1)} collective-permute-done((f32[32,8,256]{2,1,0:T(8,128)S(1)}, f32[32,8,256]{2,1,0:T(8,128)S(1)}, u32[]{:S(2)}, u32[]{:S(2)}) %collective-permute-start.8) | collective-permute-done | bytes 262176 | tf_op jit(solution)/shard_map/ppermute | solution.py:599
  32.0 2.4 %transform.3 = (f32[32,8,256]{2,1,0:T(8,128)S(1)}, f32[32,8,256]{2,1,0:T(8,128)S(1)}, f32[32,8,256]{2,1,0:T(8,128)S(1)}, f32[32,8,256]{2,1,0:T(8,128)S(1)}, f32[...) custom-call(bf16[512,256]{1,0:T(8,128)(2,1)S(1)} %permuted_table.1.tab, ...), custom_call_target="tpu_custom_call" | custom-call | flops 805306368 | bytes 4194304 | tf_op jit(solution)/shard_map/transform/pallas_call | solution.py:122
  34.5 3.2 %collective-permute-done.11.refs_2_ = f32[32,8,256]{2,1,0:T(8,128)S(1)} collective-permute-done((f32[32,8,256]{2,1,0:T(8,128)S(1)}, f32[32,8,256]{2,1,0:T(8,128)S(1)}, u32[]{:S(2)}, u32[]{:S(2)}) %collective-permute-start.11) | collective-permute-done | bytes 262176 | tf_op jit(solution)/shard_map/ppermute | solution.py:599
  38.3 4.0 %collective-permute-done.14.refs_6_ = f32[32,8,256]{2,1,0:T(8,128)S(1)} collective-permute-done((f32[32,8,256]{2,1,0:T(8,128)S(1)}, f32[32,8,256]{2,1,0:T(8,128)S(1)}, u32[]{:S(2)}, u32[]{:S(2)}) %collective-permute-start.14) | collective-permute-done | bytes 262176 | tf_op jit(solution)/shard_map/ppermute | solution.py:599
  42.4 1.5 collective-permute-start.18
  43.9 3.7 %collective-permute-done.13.refs_5_ = f32[32,8,256]{2,1,0:T(8,128)S(1)} collective-permute-done((f32[32,8,256]{2,1,0:T(8,128)S(1)}, f32[32,8,256]{2,1,0:T(8,128)S(1)}, u32[]{:S(2)}, u32[]{:S(2)}) %collective-permute-start.13) | collective-permute-done | bytes 262176 | tf_op jit(solution)/shard_map/ppermute | solution.py:599
  47.6 3.6 %collective-permute-start.21 = (f32[32,8,256]{2,1,0:T(8,128)S(1)}, f32[32,8,256]{2,1,0:T(8,128)S(1)}, u32[]{:S(2)}, u32[]{:S(2)}) collective-permute-start(f32[32,8,256]{2,1,0:T(8,128)S(1)} %get-tuple-element.294), channel_id=1, source_target_pairs={{0,6},{1,7},{2,4},{3,5},{4,2},{5,3},{6,0},{7,1},{8,14},{9,15},{10,... | collective-permute-start | bytes 786440 | tf_op jit(solution)/shard_map/ppermute | solution.py:599
  51.2 2.4 %collective-permute-done.15.refs_7_ = f32[32,8,256]{2,1,0:T(8,128)S(1)} collective-permute-done((f32[32,8,256]{2,1,0:T(8,128)S(1)}, f32[32,8,256]{2,1,0:T(8,128)S(1)}, u32[]{:S(2)}, u32[]{:S(2)}) %collective-permute-start.15) | collective-permute-done | bytes 262176 | tf_op jit(solution)/shard_map/ppermute | solution.py:599
  56.6 2.4 %transform.4 = (f32[32,8,256]{2,1,0:T(8,128)S(1)}, f32[32,8,256]{2,1,0:T(8,128)S(1)}, f32[32,8,256]{2,1,0:T(8,128)S(1)}, f32[32,8,256]{2,1,0:T(8,128)S(1)}, f32[...) custom-call(bf16[512,256]{1,0:T(8,128)(2,1)S(1)} %permuted_table.1.tab, ...), custom_call_target="tpu_custom_call" | custom-call | flops 805306368 | bytes 4194304 | tf_op jit(solution)/shard_map/transform/pallas_call | solution.py:122
  60.2 4.7 %collective-permute-done.21.refs_6_ = f32[32,8,256]{2,1,0:T(8,128)S(1)} collective-permute-done((f32[32,8,256]{2,1,0:T(8,128)S(1)}, f32[32,8,256]{2,1,0:T(8,128)S(1)}, u32[]{:S(2)}, u32[]{:S(2)}) %collective-permute-start.21) | collective-permute-done | bytes 262176 | tf_op jit(solution)/shard_map/ppermute | solution.py:599
  64.9 1.5 collective-permute-start.25
  66.4 4.1 %collective-permute-done.19.refs_3_ = f32[32,8,256]{2,1,0:T(8,128)S(1)} collective-permute-done((f32[32,8,256]{2,1,0:T(8,128)S(1)}, f32[32,8,256]{2,1,0:T(8,128)S(1)}, u32[]{:S(2)}, u32[]{:S(2)}) %collective-permute-start.19) | collective-permute-done | bytes 262176 | tf_op jit(solution)/shard_map/ppermute | solution.py:599
  70.8 2.3 %collective-permute-start.28 = (f32[32,8,256]{2,1,0:T(8,128)S(1)}, f32[32,8,256]{2,1,0:T(8,128)S(1)}, u32[]{:S(2)}, u32[]{:S(2)}) collective-permute-start(f32[32,8,256]{2,1,0:T(8,128)S(1)} %get-tuple-element.316), channel_id=1, source_target_pairs={{0,6},{1,7},{2,4},{3,5},{4,2},{5,3},{6,0},{7,1},{8,14},{9,15},{10,... | collective-permute-start | bytes 786440 | tf_op jit(solution)/shard_map/ppermute | solution.py:599
  73.1 3.1 %collective-permute-done.22.refs_7_ = f32[32,8,256]{2,1,0:T(8,128)S(1)} collective-permute-done((f32[32,8,256]{2,1,0:T(8,128)S(1)}, f32[32,8,256]{2,1,0:T(8,128)S(1)}, u32[]{:S(2)}, u32[]{:S(2)}) %collective-permute-start.22) | collective-permute-done | bytes 262176 | tf_op jit(solution)/shard_map/ppermute | solution.py:599
  77.1 5.7 %collective-permute-done.25.refs_10_ = f32[32,8,256]{2,1,0:T(8,128)S(1)} collective-permute-done((f32[32,8,256]{2,1,0:T(8,128)S(1)}, f32[32,8,256]{2,1,0:T(8,128)S(1)}, u32[]{:S(2)}, u32[]{:S(2)}) %collective-permute-start.25) | collective-permute-done | bytes 262176 | tf_op jit(solution)/shard_map/ppermute | solution.py:599
  82.7 2.7 %collective-permute-start.27 = (f32[32,8,256]{2,1,0:T(8,128)S(1)}, f32[32,8,256]{2,1,0:T(8,128)S(1)}, u32[]{:S(2)}, u32[]{:S(2)}) collective-permute-start(f32[32,8,256]{2,1,0:T(8,128)S(1)} %get-tuple-element.313), channel_id=1, source_target_pairs={{0,5},{1,4},{2,7},{3,6},{4,1},{5,0},{6,3},{7,2},{8,13},{9,12},{10,... | collective-permute-start | bytes 786440 | tf_op jit(solution)/shard_map/ppermute | solution.py:599
  85.4 1.9 %collective-permute-done.23.refs_12_ = f32[32,8,256]{2,1,0:T(8,128)S(1)} collective-permute-done((f32[32,8,256]{2,1,0:T(8,128)S(1)}, f32[32,8,256]{2,1,0:T(8,128)S(1)}, u32[]{:S(2)}, u32[]{:S(2)}) %collective-permute-start.23) | collective-permute-done | bytes 262176 | tf_op jit(solution)/shard_map/ppermute | solution.py:599
  87.4 1.5 collective-permute-start.35
  88.9 4.1 %collective-permute-done.26.refs_11_ = f32[32,8,256]{2,1,0:T(8,128)S(1)} collective-permute-done((f32[32,8,256]{2,1,0:T(8,128)S(1)}, f32[32,8,256]{2,1,0:T(8,128)S(1)}, u32[]{:S(2)}, u32[]{:S(2)}) %collective-permute-start.26) | collective-permute-done | bytes 262176 | tf_op jit(solution)/shard_map/ppermute | solution.py:599
  93.0 5.7 %collective-permute-done.29.refs_15_ = f32[32,8,256]{2,1,0:T(8,128)S(1)} collective-permute-done((f32[32,8,256]{2,1,0:T(8,128)S(1)}, f32[32,8,256]{2,1,0:T(8,128)S(1)}, u32[]{:S(2)}, u32[]{:S(2)}) %collective-permute-start.29) | collective-permute-done | bytes 262176 | tf_op jit(solution)/shard_map/ppermute | solution.py:599
  99.2 4.3 %start_solve.1 = (f32[2048,256]{1,0:T(8,128)S(1)}, f32[2048,256]{1,0:T(8,128)S(1)}, f32[2048,256]{1,0:T(8,128)S(1)}, f32[2,32,512]{2,1,0:T(8,128)S(1)}, f32[2,32,512]{2,1,0:T(8,128)S(1)}) custom-call(s32[2]{0:T(128)S(1)} %pad_add_fusion.pos_ref, f32[2,256]{1,0:T(2,128)S(1)} %copy-done.5, f32[7,64,256]{2,1,0:T(8,128)S(1)} %get-tuple-element.197.diag_ref.coef_ref, ...), custom_call_target="tpu_custom_call" | custom-call | flops 1000000 | bytes 100000 | tf_op jit(solution)/shard_map/start_solve/pallas_call | solution.py:348
  103.5 1.6 collective-permute-start.32
  105.1 2.3 %collective-permute-start.36 = (f32[32,8,256]{2,1,0:T(8,128)S(1)}, f32[32,8,256]{2,1,0:T(8,128)S(1)}, u32[]{:S(2)}, u32[]{:S(2)}) collective-permute-start(f32[32,8,256]{2,1,0:T(8,128)S(1)} %get-tuple-element.344), channel_id=1, source_target_pairs={{0,3},{1,2},{2,1},{3,0},{4,7},{5,6},{6,5},{7,4},{8,11},{9,10},{10,... | collective-permute-start | bytes 786440 | tf_op jit(solution)/shard_map/ppermute | solution.py:599
  107.8 1.8 %collective-permute-done.33.refs_4_ = f32[32,8,256]{2,1,0:T(8,128)S(1)} collective-permute-done((f32[32,8,256]{2,1,0:T(8,128)S(1)}, f32[32,8,256]{2,1,0:T(8,128)S(1)}, u32[]{:S(2)}, u32[]{:S(2)}) %collective-permute-start.33) | collective-permute-done | bytes 262176 | tf_op jit(solution)/shard_map/ppermute | solution.py:599
  111.6 2.2 %collective-permute-start.31 = (f32[2,32,512]{2,1,0:T(8,128)S(1)}, f32[2,32,512]{2,1,0:T(8,128)S(1)}, u32[]{:S(2)}, u32[]{:S(2)}) collective-permute-start(f32[2,32,512]{2,1,0:T(8,128)S(1)} %get-tuple-element.331.own_lo_ref), channel_id=1, source_target_pairs={{8,0},{16,8},{24,16},{0,24},{9,1},{17,9},{25,17},{1,25},{10,2},{18... | collective-permute-start | bytes 393224 | tf_op jit(solution)/shard_map/ppermute | solution.py:576
  113.8 2.8 %partial_update.1 = (f32[32,64,256]{2,1,0:T(8,128)S(1)}, f32[32,64,256]{2,1,0:T(8,128)S(1)}, f32[32,64,256]{2,1,0:T(8,128)S(1)}) custom-call(f32[7,64,256]{2,1,0:T(8,128)S(1)} %get-tuple-element.197.diag_ref.coef_ref, bf16[128,192]{1,0:T(8,128)(2,1)S(1)} %get-tuple-element.198.dpack_ref, f32[32,8,256]{2,1,0:T(8,128)S(1)} %get-tuple-element.277.refs_0_, ...), custom_call_target="tpu_custom_call" | custom-call | flops 1000000 | bytes 100000 | tf_op jit(solution)/shard_map/partial_update/pallas_call | solution.py:468
  117.0 5.5 %two_sweeps.2 = (f32[2048,256]{1,0:T(8,128)S(1)}, f32[2,32,512]{2,1,0:T(8,128)S(1)}, f32[2,32,512]{2,1,0:T(8,128)S(1)}) custom-call(s32[2]{0:T(128)S(1)} %pad_add_fusion.pos_ref, f32[2048,256]{1,0:T(8,128)S(1)} %get-tuple-element.327.local_ref, f32[2048,256]{1,0:T(8,128)S(1)} %get-tuple-element.328.source_ref, ...), custom_call_target="tpu_custom_call" | custom-call | flops 1000000 | bytes 100000 | tf_op jit(solution)/shard_map/two_sweeps/pallas_call | solution.py:422
  122.5 2.5 %transform.5 = (f32[32,8,256]{2,1,0:T(8,128)S(1)}, f32[32,8,256]{2,1,0:T(8,128)S(1)}, f32[32,8,256]{2,1,0:T(8,128)S(1)}, f32[32,8,256]{2,1,0:T(8,128)S(1)}, f32[...) custom-call(bf16[512,256]{1,0:T(8,128)(2,1)S(1)} %permuted_table.1.tab, ...), custom_call_target="tpu_custom_call" | custom-call | flops 805306368 | bytes 4194304 | tf_op jit(solution)/shard_map/transform/pallas_call | solution.py:122
  125.8 2.3 %collective-permute-start.40 = (f32[32,8,256]{2,1,0:T(8,128)S(1)}, f32[32,8,256]{2,1,0:T(8,128)S(1)}, u32[]{:S(2)}, u32[]{:S(2)}) collective-permute-start(f32[32,8,256]{2,1,0:T(8,128)S(1)} %get-tuple-element.355), channel_id=1, source_target_pairs={{0,4},{1,5},{2,6},{3,7},{4,0},{5,1},{6,2},{7,3},{8,12},{9,13},{10,... | collective-permute-start | bytes 786440 | tf_op jit(solution)/shard_map/ppermute | solution.py:599
  128.7 3.5 %collective-permute-start.41 = (f32[2,32,512]{2,1,0:T(8,128)S(1)}, f32[2,32,512]{2,1,0:T(8,128)S(1)}, u32[]{:S(2)}, u32[]{:S(2)}) collective-permute-start(f32[2,32,512]{2,1,0:T(8,128)S(1)} %get-tuple-element.358.own_lo_ref), channel_id=1, source_target_pairs={{8,0},{16,8},{24,16},{0,24},{9,1},{17,9},{25,17},{1,25},{10,2},{18... | collective-permute-start | bytes 393224 | tf_op jit(solution)/shard_map/ppermute | solution.py:576
  133.1 7.0 %collective-permute-done.40.refs_4_ = f32[32,8,256]{2,1,0:T(8,128)S(1)} collective-permute-done((f32[32,8,256]{2,1,0:T(8,128)S(1)}, f32[32,8,256]{2,1,0:T(8,128)S(1)}, u32[]{:S(2)}, u32[]{:S(2)}) %collective-permute-start.40) | collective-permute-done | bytes 262176 | tf_op jit(solution)/shard_map/ppermute | solution.py:599
  140.1 3.7 %collective-permute-start.44 = (f32[32,8,256]{2,1,0:T(8,128)S(1)}, f32[32,8,256]{2,1,0:T(8,128)S(1)}, u32[]{:S(2)}, u32[]{:S(2)}) collective-permute-start(f32[32,8,256]{2,1,0:T(8,128)S(1)} %get-tuple-element.363), channel_id=1, source_target_pairs={{0,7},{1,6},{2,5},{3,4},{4,3},{5,2},{6,1},{7,0},{8,15},{9,14},{10,... | collective-permute-start | bytes 786440 | tf_op jit(solution)/shard_map/ppermute | solution.py:599
  143.8 6.1 %two_sweeps.3 = (f32[2048,256]{1,0:T(8,128)S(1)}, f32[1,32,512]{2,1,0:T(8,128)S(1)}, f32[1,32,512]{2,1,0:T(8,128)S(1)}) custom-call(s32[2]{0:T(128)S(1)} %pad_add_fusion.pos_ref, f32[2048,256]{1,0:T(8,128)S(1)} %get-tuple-element.356.local_ref, f32[2048,256]{1,0:T(8,128)S(1)} %get-tuple-element.328.source_ref, ...), custom_call_target="tpu_custom_call" | custom-call | flops 1000000 | bytes 100000 | tf_op jit(solution)/shard_map/two_sweeps/pallas_call | solution.py:422
  150.0 3.5 %collective-permute-start.46 = (f32[1,32,512]{2,1,0:T(8,128)S(1)}, f32[1,32,512]{2,1,0:T(8,128)S(1)}, u32[]{:S(2)}, u32[]{:S(2)}) collective-permute-start(f32[1,32,512]{2,1,0:T(8,128)S(1)} %get-tuple-element.371), channel_id=1, source_target_pairs={{8,0},{16,8},{24,16},{0,24},{9,1},{17,9},{25,17},{1,25},{10,2},{18... | collective-permute-start | bytes 196616 | tf_op jit(solution)/shard_map/ppermute | solution.py:576
  153.5 2.0 %collective-permute-done.44.refs_7_ = f32[32,8,256]{2,1,0:T(8,128)S(1)} collective-permute-done((f32[32,8,256]{2,1,0:T(8,128)S(1)}, f32[32,8,256]{2,1,0:T(8,128)S(1)}, u32[]{:S(2)}, u32[]{:S(2)}) %collective-permute-start.44) | collective-permute-done | bytes 262176 | tf_op jit(solution)/shard_map/ppermute | solution.py:599
  156.0 3.6 %collective-permute-done.47.got_lo_ref = f32[1,32,512]{2,1,0:T(8,128)S(1)} collective-permute-done((f32[1,32,512]{2,1,0:T(8,128)S(1)}, f32[1,32,512]{2,1,0:T(8,128)S(1)}, u32[]{:S(2)}, u32[]{:S(2)}) %collective-permute-start.47) | collective-permute-done | bytes 65568 | tf_op jit(solution)/shard_map/ppermute | solution.py:576
  159.6 3.9 %add_force.1 = (f32[3,32,64,256]{3,2,1,0:T(8,128)}, f32[32,64,256]{2,1,0:T(8,128)S(1)}) custom-call(s32[2]{0:T(128)S(1)} %pad_add_fusion.pos_ref, f32[2048,256]{1,0:T(8,128)S(1)} %get-tuple-element.364.local_ref, f32[1,32,512]{2,1,0:T(8,128)S(1)} %collective-permute-done.46.got_up_ref, f32[1,32,512]{2,1,0:T(8,128)S(1)} %collective-permute-done.47.got_lo_ref, ...), custom_call_target="tpu_custom_call" | custom-call | flops 1000000 | bytes 100000 | tf_op jit(solution)/shard_map/add_force/pallas_call | solution.py:512
  163.5 5.3 %finish.1 = f32[3,32,64,256]{3,2,1,0:T(8,128)} custom-call(s32[2]{0:T(128)S(1)} %pad_add_fusion.pos_ref, f32[7,64,256]{2,1,0:T(8,128)S(1)} %get-tuple-element.197.diag_ref.coef_ref, bf16[128,192]{1,0:T(8,128)(2,1)S(1)} %get-tuple-element.198.dpack_ref, f32[32,64,256]{2,1,0:T(8,128)S(1)} %get-tuple-element.375.px_ref, ...), custom_call_target="tpu_custom_call", output_to_operand_aliasing={{}: (5, {})} | custom-call | flops 1000000 | bytes 100000 | tf_op jit(solution)/shard_map/finish/pallas_call | solution.py:552
  (91 shorter events, 17.6 us)
Async XLA Ops:
  2.9 14.5 %collective-permute-start = (f32[32,8,256]{2,1,0:T(8,128)S(1)}, f32[32,8,256]{2,1,0:T(8,128)S(1)}, u32[]{:S(2)}, u32[]{:S(2)}) collective-permute-start(f32[32,8,256]{2,1,0:T(8,128)S(1)} %get-tuple-element.205), channel_id=1, source_target_pairs={{0,4},{1,5},{2,6},{3,7},{4,0},{5,1},{6,2},{7,3},{8,12},{9,13},{10,... | collective-permute-start | bytes 786440 | tf_op jit(solution)/shard_map/ppermute | solution.py:599
  6.0 11.5 %collective-permute-start.2 = (f32[32,8,256]{2,1,0:T(8,128)S(1)}, f32[32,8,256]{2,1,0:T(8,128)S(1)}, u32[]{:S(2)}, u32[]{:S(2)}) collective-permute-start(f32[32,8,256]{2,1,0:T(8,128)S(1)} %get-tuple-element.209), channel_id=1, source_target_pairs={{0,2},{1,3},{2,0},{3,1},{4,6},{5,7},{6,4},{7,5},{8,10},{9,11},{10,... | collective-permute-start | bytes 786440 | tf_op jit(solution)/shard_map/ppermute | solution.py:599
  7.4 12.5 %collective-permute-start.7 = (f32[32,8,256]{2,1,0:T(8,128)S(1)}, f32[32,8,256]{2,1,0:T(8,128)S(1)}, u32[]{:S(2)}, u32[]{:S(2)}) collective-permute-start(f32[32,8,256]{2,1,0:T(8,128)S(1)} %get-tuple-element.221), channel_id=1, source_target_pairs={{0,6},{1,7},{2,4},{3,5},{4,2},{5,3},{6,0},{7,1},{8,14},{9,15},{10,... | collective-permute-start | bytes 786440 | tf_op jit(solution)/shard_map/ppermute | solution.py:599
  8.8 5.7 %collective-permute-start.4 = (f32[2,512]{1,0:T(2,128)S(1)}, f32[2,512]{1,0:T(2,128)S(1)}, u32[]{:S(2)}, u32[]{:S(2)}) collective-permute-start(f32[2,512]{1,0:T(2,128)S(1)} %get-tuple-element.389), channel_id=1, source_target_pairs={{0,8},{8,16},{16,24},{24,0},{1,9},{9,17},{17,25},{25,1},{2,10},{10... | collective-permute-start | bytes 12296 | tf_op jit(solution)/shard_map/ppermute | solution.py:576
  14.5 10.9 %collective-permute-start.5 = (f32[32,8,256]{2,1,0:T(8,128)S(1)}, f32[32,8,256]{2,1,0:T(8,128)S(1)}, u32[]{:S(2)}, u32[]{:S(2)}) collective-permute-start(f32[32,8,256]{2,1,0:T(8,128)S(1)} %get-tuple-element.214), channel_id=1, source_target_pairs={{0,3},{1,2},{2,1},{3,0},{4,7},{5,6},{6,5},{7,4},{8,11},{9,10},{10,... | collective-permute-start | bytes 786440 | tf_op jit(solution)/shard_map/ppermute | solution.py:599
  14.6 10.9 %collective-permute-start.6 = (f32[32,8,256]{2,1,0:T(8,128)S(1)}, f32[32,8,256]{2,1,0:T(8,128)S(1)}, u32[]{:S(2)}, u32[]{:S(2)}) collective-permute-start(f32[32,8,256]{2,1,0:T(8,128)S(1)} %get-tuple-element.218), channel_id=1, source_target_pairs={{0,5},{1,4},{2,7},{3,6},{4,1},{5,0},{6,3},{7,2},{8,13},{9,12},{10,... | collective-permute-start | bytes 786440 | tf_op jit(solution)/shard_map/ppermute | solution.py:599
  17.5 10.7 %collective-permute-start.1 = (f32[32,8,256]{2,1,0:T(8,128)S(1)}, f32[32,8,256]{2,1,0:T(8,128)S(1)}, u32[]{:S(2)}, u32[]{:S(2)}) collective-permute-start(f32[32,8,256]{2,1,0:T(8,128)S(1)} %get-tuple-element.206), channel_id=1, source_target_pairs={{0,1},{1,0},{2,3},{3,2},{4,5},{5,4},{6,7},{7,6},{8,9},{9,8},{10,11... | collective-permute-start | bytes 786440 | tf_op jit(solution)/shard_map/ppermute | solution.py:599
  17.5 13.6 %collective-permute-start.8 = (f32[32,8,256]{2,1,0:T(8,128)S(1)}, f32[32,8,256]{2,1,0:T(8,128)S(1)}, u32[]{:S(2)}, u32[]{:S(2)}) collective-permute-start(f32[32,8,256]{2,1,0:T(8,128)S(1)} %get-tuple-element.224), channel_id=1, source_target_pairs={{0,7},{1,6},{2,5},{3,4},{4,3},{5,2},{6,1},{7,0},{8,15},{9,14},{10,... | collective-permute-start | bytes 786440 | tf_op jit(solution)/shard_map/ppermute | solution.py:599
  19.9 17.7 %collective-permute-start.11 = (f32[32,8,256]{2,1,0:T(8,128)S(1)}, f32[32,8,256]{2,1,0:T(8,128)S(1)}, u32[]{:S(2)}, u32[]{:S(2)}) collective-permute-start(f32[32,8,256]{2,1,0:T(8,128)S(1)} %get-tuple-element.242), channel_id=1, source_target_pairs={{0,2},{1,3},{2,0},{3,1},{4,6},{5,7},{6,4},{7,5},{8,10},{9,11},{10,... | collective-permute-start | bytes 786440 | tf_op jit(solution)/shard_map/ppermute | solution.py:599
  25.4 12.2 %collective-permute-start.9 = (f32[32,8,256]{2,1,0:T(8,128)S(1)}, f32[32,8,256]{2,1,0:T(8,128)S(1)}, u32[]{:S(2)}, u32[]{:S(2)}) collective-permute-start(f32[32,8,256]{2,1,0:T(8,128)S(1)} %get-tuple-element.238), channel_id=1, source_target_pairs={{0,4},{1,5},{2,6},{3,7},{4,0},{5,1},{6,2},{7,3},{8,12},{9,13},{10,... | collective-permute-start | bytes 786440 | tf_op jit(solution)/shard_map/ppermute | solution.py:599
  25.4 16.9 %collective-permute-start.14 = (f32[32,8,256]{2,1,0:T(8,128)S(1)}, f32[32,8,256]{2,1,0:T(8,128)S(1)}, u32[]{:S(2)}, u32[]{:S(2)}) collective-permute-start(f32[32,8,256]{2,1,0:T(8,128)S(1)} %get-tuple-element.252), channel_id=1, source_target_pairs={{0,6},{1,7},{2,4},{3,5},{4,2},{5,3},{6,0},{7,1},{8,14},{9,15},{10,... | collective-permute-start | bytes 786440 | tf_op jit(solution)/shard_map/ppermute | solution.py:599
  28.1 19.4 %collective-permute-start.13 = (f32[32,8,256]{2,1,0:T(8,128)S(1)}, f32[32,8,256]{2,1,0:T(8,128)S(1)}, u32[]{:S(2)}, u32[]{:S(2)}) collective-permute-start(f32[32,8,256]{2,1,0:T(8,128)S(1)} %get-tuple-element.249), channel_id=1, source_target_pairs={{0,5},{1,4},{2,7},{3,6},{4,1},{5,0},{6,3},{7,2},{8,13},{9,12},{10,... | collective-permute-start | bytes 786440 | tf_op jit(solution)/shard_map/ppermute | solution.py:599
  31.1 20.1 %collective-permute-start.12 = (f32[32,8,256]{2,1,0:T(8,128)S(1)}, f32[32,8,256]{2,1,0:T(8,128)S(1)}, u32[]{:S(2)}, u32[]{:S(2)}) collective-permute-start(f32[32,8,256]{2,1,0:T(8,128)S(1)} %get-tuple-element.245), channel_id=1, source_target_pairs={{0,3},{1,2},{2,1},{3,0},{4,7},{5,6},{6,5},{7,4},{8,11},{9,10},{10,... | collective-permute-start | bytes 786440 | tf_op jit(solution)/shard_map/ppermute | solution.py:599
  37.7 15.9 %collective-permute-start.15 = (f32[32,8,256]{2,1,0:T(8,128)S(1)}, f32[32,8,256]{2,1,0:T(8,128)S(1)}, u32[]{:S(2)}, u32[]{:S(2)}) collective-permute-start(f32[32,8,256]{2,1,0:T(8,128)S(1)} %get-tuple-element.255), channel_id=1, source_target_pairs={{0,7},{1,6},{2,5},{3,4},{4,3},{5,2},{6,1},{7,0},{8,15},{9,14},{10,... | collective-permute-start | bytes 786440 | tf_op jit(solution)/shard_map/ppermute | solution.py:599
  37.7 17.9 %collective-permute-start.10 = (f32[32,8,256]{2,1,0:T(8,128)S(1)}, f32[32,8,256]{2,1,0:T(8,128)S(1)}, u32[]{:S(2)}, u32[]{:S(2)}) collective-permute-start(f32[32,8,256]{2,1,0:T(8,128)S(1)} %get-tuple-element.239), channel_id=1, source_target_pairs={{0,1},{1,0},{2,3},{3,2},{4,5},{5,4},{6,7},{7,6},{8,9},{9,8},{10,11... | collective-permute-start | bytes 786440 | tf_op jit(solution)/shard_map/ppermute | solution.py:599
  42.4 17.8 %collective-permute-start.18 = (f32[32,8,256]{2,1,0:T(8,128)S(1)}, f32[32,8,256]{2,1,0:T(8,128)S(1)}, u32[]{:S(2)}, u32[]{:S(2)}) collective-permute-start(f32[32,8,256]{2,1,0:T(8,128)S(1)} %get-tuple-element.284), channel_id=1, source_target_pairs={{0,2},{1,3},{2,0},{3,1},{4,6},{5,7},{6,4},{7,5},{8,10},{9,11},{10,... | collective-permute-start | bytes 786440 | tf_op jit(solution)/shard_map/ppermute | solution.py:599
  47.6 17.3 %collective-permute-start.21 = (f32[32,8,256]{2,1,0:T(8,128)S(1)}, f32[32,8,256]{2,1,0:T(8,128)S(1)}, u32[]{:S(2)}, u32[]{:S(2)}) collective-permute-start(f32[32,8,256]{2,1,0:T(8,128)S(1)} %get-tuple-element.294), channel_id=1, source_target_pairs={{0,6},{1,7},{2,4},{3,5},{4,2},{5,3},{6,0},{7,1},{8,14},{9,15},{10,... | collective-permute-start | bytes 786440 | tf_op jit(solution)/shard_map/ppermute | solution.py:599
  51.2 15.2 %collective-permute-start.16 = (f32[32,8,256]{2,1,0:T(8,128)S(1)}, f32[32,8,256]{2,1,0:T(8,128)S(1)}, u32[]{:S(2)}, u32[]{:S(2)}) collective-permute-start(f32[32,8,256]{2,1,0:T(8,128)S(1)} %get-tuple-element.280), channel_id=1, source_target_pairs={{0,4},{1,5},{2,6},{3,7},{4,0},{5,1},{6,2},{7,3},{8,12},{9,13},{10,... | collective-permute-start | bytes 786440 | tf_op jit(solution)/shard_map/ppermute | solution.py:599
  53.6 16.9 %collective-permute-start.19 = (f32[32,8,256]{2,1,0:T(8,128)S(1)}, f32[32,8,256]{2,1,0:T(8,128)S(1)}, u32[]{:S(2)}, u32[]{:S(2)}) collective-permute-start(f32[32,8,256]{2,1,0:T(8,128)S(1)} %get-tuple-element.287), channel_id=1, source_target_pairs={{0,3},{1,2},{2,1},{3,0},{4,7},{5,6},{6,5},{7,4},{8,11},{9,10},{10,... | collective-permute-start | bytes 786440 | tf_op jit(solution)/shard_map/ppermute | solution.py:599
  55.6 15.2 %collective-permute-start.20 = (f32[32,8,256]{2,1,0:T(8,128)S(1)}, f32[32,8,256]{2,1,0:T(8,128)S(1)}, u32[]{:S(2)}, u32[]{:S(2)}) collective-permute-start(f32[32,8,256]{2,1,0:T(8,128)S(1)} %get-tuple-element.291), channel_id=1, source_target_pairs={{0,5},{1,4},{2,7},{3,6},{4,1},{5,0},{6,3},{7,2},{8,13},{9,12},{10,... | collective-permute-start | bytes 786440 | tf_op jit(solution)/shard_map/ppermute | solution.py:599
  60.2 16.0 %collective-permute-start.22 = (f32[32,8,256]{2,1,0:T(8,128)S(1)}, f32[32,8,256]{2,1,0:T(8,128)S(1)}, u32[]{:S(2)}, u32[]{:S(2)}) collective-permute-start(f32[32,8,256]{2,1,0:T(8,128)S(1)} %get-tuple-element.297), channel_id=1, source_target_pairs={{0,7},{1,6},{2,5},{3,4},{4,3},{5,2},{6,1},{7,0},{8,15},{9,14},{10,... | collective-permute-start | bytes 786440 | tf_op jit(solution)/shard_map/ppermute | solution.py:599
  64.9 17.9 %collective-permute-start.25 = (f32[32,8,256]{2,1,0:T(8,128)S(1)}, f32[32,8,256]{2,1,0:T(8,128)S(1)}, u32[]{:S(2)}, u32[]{:S(2)}) collective-permute-start(f32[32,8,256]{2,1,0:T(8,128)S(1)} %get-tuple-element.306), channel_id=1, source_target_pairs={{0,2},{1,3},{2,0},{3,1},{4,6},{5,7},{6,4},{7,5},{8,10},{9,11},{10,... | collective-permute-start | bytes 786440 | tf_op jit(solution)/shard_map/ppermute | solution.py:599
  66.4 16.4 %collective-permute-start.17 = (f32[32,8,256]{2,1,0:T(8,128)S(1)}, f32[32,8,256]{2,1,0:T(8,128)S(1)}, u32[]{:S(2)}, u32[]{:S(2)}) collective-permute-start(f32[32,8,256]{2,1,0:T(8,128)S(1)} %get-tuple-element.281), channel_id=1, source_target_pairs={{0,1},{1,0},{2,3},{3,2},{4,5},{5,4},{6,7},{7,6},{8,9},{9,8},{10,11... | collective-permute-start | bytes 786440 | tf_op jit(solution)/shard_map/ppermute | solution.py:599
  70.5 16.8 %collective-permute-start.23 = (f32[32,8,256]{2,1,0:T(8,128)S(1)}, f32[32,8,256]{2,1,0:T(8,128)S(1)}, u32[]{:S(2)}, u32[]{:S(2)}) collective-permute-start(f32[32,8,256]{2,1,0:T(8,128)S(1)} %get-tuple-element.302), channel_id=1, source_target_pairs={{0,4},{1,5},{2,6},{3,7},{4,0},{5,1},{6,2},{7,3},{8,12},{9,13},{10,... | collective-permute-start | bytes 786440 | tf_op jit(solution)/shard_map/ppermute | solution.py:599
  70.8 16.6 %collective-permute-start.28 = (f32[32,8,256]{2,1,0:T(8,128)S(1)}, f32[32,8,256]{2,1,0:T(8,128)S(1)}, u32[]{:S(2)}, u32[]{:S(2)}) collective-permute-start(f32[32,8,256]{2,1,0:T(8,128)S(1)} %get-tuple-element.316), channel_id=1, source_target_pairs={{0,6},{1,7},{2,4},{3,5},{4,2},{5,3},{6,0},{7,1},{8,14},{9,15},{10,... | collective-permute-start | bytes 786440 | tf_op jit(solution)/shard_map/ppermute | solution.py:599
  76.2 16.9 %collective-permute-start.26 = (f32[32,8,256]{2,1,0:T(8,128)S(1)}, f32[32,8,256]{2,1,0:T(8,128)S(1)}, u32[]{:S(2)}, u32[]{:S(2)}) collective-permute-start(f32[32,8,256]{2,1,0:T(8,128)S(1)} %get-tuple-element.309), channel_id=1, source_target_pairs={{0,3},{1,2},{2,1},{3,0},{4,7},{5,6},{6,5},{7,4},{8,11},{9,10},{10,... | collective-permute-start | bytes 786440 | tf_op jit(solution)/shard_map/ppermute | solution.py:599
  82.7 15.9 %collective-permute-start.29 = (f32[32,8,256]{2,1,0:T(8,128)S(1)}, f32[32,8,256]{2,1,0:T(8,128)S(1)}, u32[]{:S(2)}, u32[]{:S(2)}) collective-permute-start(f32[32,8,256]{2,1,0:T(8,128)S(1)} %get-tuple-element.319), channel_id=1, source_target_pairs={{0,7},{1,6},{2,5},{3,4},{4,3},{5,2},{6,1},{7,0},{8,15},{9,14},{10,... | collective-permute-start | bytes 786440 | tf_op jit(solution)/shard_map/ppermute | solution.py:599
  82.7 15.9 %collective-permute-start.27 = (f32[32,8,256]{2,1,0:T(8,128)S(1)}, f32[32,8,256]{2,1,0:T(8,128)S(1)}, u32[]{:S(2)}, u32[]{:S(2)}) collective-permute-start(f32[32,8,256]{2,1,0:T(8,128)S(1)} %get-tuple-element.313), channel_id=1, source_target_pairs={{0,5},{1,4},{2,7},{3,6},{4,1},{5,0},{6,3},{7,2},{8,13},{9,12},{10,... | collective-permute-start | bytes 786440 | tf_op jit(solution)/shard_map/ppermute | solution.py:599
  87.3 11.9 %collective-permute-start.24 = (f32[32,8,256]{2,1,0:T(8,128)S(1)}, f32[32,8,256]{2,1,0:T(8,128)S(1)}, u32[]{:S(2)}, u32[]{:S(2)}) collective-permute-start(f32[32,8,256]{2,1,0:T(8,128)S(1)} %get-tuple-element.303), channel_id=1, source_target_pairs={{0,1},{1,0},{2,3},{3,2},{4,5},{5,4},{6,7},{7,6},{8,9},{9,8},{10,11... | collective-permute-start | bytes 786440 | tf_op jit(solution)/shard_map/ppermute | solution.py:599
  87.4 20.0 %collective-permute-start.35 = (f32[32,8,256]{2,1,0:T(8,128)S(1)}, f32[32,8,256]{2,1,0:T(8,128)S(1)}, u32[]{:S(2)}, u32[]{:S(2)}) collective-permute-start(f32[32,8,256]{2,1,0:T(8,128)S(1)} %get-tuple-element.342), channel_id=1, source_target_pairs={{0,2},{1,3},{2,0},{3,1},{4,6},{5,7},{6,4},{7,5},{8,10},{9,11},{10,... | collective-permute-start | bytes 786440 | tf_op jit(solution)/shard_map/ppermute | solution.py:599
  93.0 16.6 %collective-permute-start.33 = (f32[32,8,256]{2,1,0:T(8,128)S(1)}, f32[32,8,256]{2,1,0:T(8,128)S(1)}, u32[]{:S(2)}, u32[]{:S(2)}) collective-permute-start(f32[32,8,256]{2,1,0:T(8,128)S(1)} %get-tuple-element.339), channel_id=1, source_target_pairs={{0,4},{1,5},{2,6},{3,7},{4,0},{5,1},{6,2},{7,3},{8,12},{9,13},{10,... | collective-permute-start | bytes 786440 | tf_op jit(solution)/shard_map/ppermute | solution.py:599
  98.7 12.9 %collective-permute-start.30 = (f32[32,8,256]{2,1,0:T(8,128)S(1)}, f32[32,8,256]{2,1,0:T(8,128)S(1)}, u32[]{:S(2)}, u32[]{:S(2)}) collective-permute-start(f32[32,8,256]{2,1,0:T(8,128)S(1)} %get-tuple-element.326), channel_id=1, source_target_pairs={{0,6},{1,7},{2,4},{3,5},{4,2},{5,3},{6,0},{7,1},{8,14},{9,15},{10,... | collective-permute-start | bytes 786440 | tf_op jit(solution)/shard_map/ppermute | solution.py:599
  103.5 6.8 %collective-permute-start.32 = (f32[2,32,512]{2,1,0:T(8,128)S(1)}, f32[2,32,512]{2,1,0:T(8,128)S(1)}, u32[]{:S(2)}, u32[]{:S(2)}) collective-permute-start(f32[2,32,512]{2,1,0:T(8,128)S(1)} %get-tuple-element.330.own_up_ref), channel_id=1, source_target_pairs={{0,8},{8,16},{16,24},{24,0},{1,9},{9,17},{17,25},{25,1},{2,10},{10... | collective-permute-start | bytes 393224 | tf_op jit(solution)/shard_map/ppermute | solution.py:576
  105.1 17.4 %collective-permute-start.36 = (f32[32,8,256]{2,1,0:T(8,128)S(1)}, f32[32,8,256]{2,1,0:T(8,128)S(1)}, u32[]{:S(2)}, u32[]{:S(2)}) collective-permute-start(f32[32,8,256]{2,1,0:T(8,128)S(1)} %get-tuple-element.344), channel_id=1, source_target_pairs={{0,3},{1,2},{2,1},{3,0},{4,7},{5,6},{6,5},{7,4},{8,11},{9,10},{10,... | collective-permute-start | bytes 786440 | tf_op jit(solution)/shard_map/ppermute | solution.py:599
  107.4 15.1 %collective-permute-start.37 = (f32[32,8,256]{2,1,0:T(8,128)S(1)}, f32[32,8,256]{2,1,0:T(8,128)S(1)}, u32[]{:S(2)}, u32[]{:S(2)}) collective-permute-start(f32[32,8,256]{2,1,0:T(8,128)S(1)} %get-tuple-element.346), channel_id=1, source_target_pairs={{0,5},{1,4},{2,7},{3,6},{4,1},{5,0},{6,3},{7,2},{8,13},{9,12},{10,... | collective-permute-start | bytes 786440 | tf_op jit(solution)/shard_map/ppermute | solution.py:599
  109.6 12.9 %collective-permute-start.38 = (f32[32,8,256]{2,1,0:T(8,128)S(1)}, f32[32,8,256]{2,1,0:T(8,128)S(1)}, u32[]{:S(2)}, u32[]{:S(2)}) collective-permute-start(f32[32,8,256]{2,1,0:T(8,128)S(1)} %get-tuple-element.348), channel_id=1, source_target_pairs={{0,7},{1,6},{2,5},{3,4},{4,3},{5,2},{6,1},{7,0},{8,15},{9,14},{10,... | collective-permute-start | bytes 786440 | tf_op jit(solution)/shard_map/ppermute | solution.py:599
  110.3 12.2 %collective-permute-start.34 = (f32[32,8,256]{2,1,0:T(8,128)S(1)}, f32[32,8,256]{2,1,0:T(8,128)S(1)}, u32[]{:S(2)}, u32[]{:S(2)}) collective-permute-start(f32[32,8,256]{2,1,0:T(8,128)S(1)} %get-tuple-element.340), channel_id=1, source_target_pairs={{0,1},{1,0},{2,3},{3,2},{4,5},{5,4},{6,7},{7,6},{8,9},{9,8},{10,11... | collective-permute-start | bytes 786440 | tf_op jit(solution)/shard_map/ppermute | solution.py:599
  125.0 7.7 %collective-permute-start.39 = (f32[32,8,256]{2,1,0:T(8,128)S(1)}, f32[32,8,256]{2,1,0:T(8,128)S(1)}, u32[]{:S(2)}, u32[]{:S(2)}) collective-permute-start(f32[32,8,256]{2,1,0:T(8,128)S(1)} %get-tuple-element.351), channel_id=1, source_target_pairs={{0,2},{1,3},{2,0},{3,1},{4,6},{5,7},{6,4},{7,5},{8,10},{9,11},{10,... | collective-permute-start | bytes 786440 | tf_op jit(solution)/shard_map/ppermute | solution.py:599
  125.8 14.3 %collective-permute-start.40 = (f32[32,8,256]{2,1,0:T(8,128)S(1)}, f32[32,8,256]{2,1,0:T(8,128)S(1)}, u32[]{:S(2)}, u32[]{:S(2)}) collective-permute-start(f32[32,8,256]{2,1,0:T(8,128)S(1)} %get-tuple-element.355), channel_id=1, source_target_pairs={{0,4},{1,5},{2,6},{3,7},{4,0},{5,1},{6,2},{7,3},{8,12},{9,13},{10,... | collective-permute-start | bytes 786440 | tf_op jit(solution)/shard_map/ppermute | solution.py:599
  128.1 12.1 %collective-permute-start.42 = (f32[2,32,512]{2,1,0:T(8,128)S(1)}, f32[2,32,512]{2,1,0:T(8,128)S(1)}, u32[]{:S(2)}, u32[]{:S(2)}) collective-permute-start(f32[2,32,512]{2,1,0:T(8,128)S(1)} %get-tuple-element.357.own_up_ref), channel_id=1, source_target_pairs={{0,8},{8,16},{16,24},{24,0},{1,9},{9,17},{17,25},{25,1},{2,10},{10... | collective-permute-start | bytes 393224 | tf_op jit(solution)/shard_map/ppermute | solution.py:576
  128.7 15.1 %collective-permute-start.41 = (f32[2,32,512]{2,1,0:T(8,128)S(1)}, f32[2,32,512]{2,1,0:T(8,128)S(1)}, u32[]{:S(2)}, u32[]{:S(2)}) collective-permute-start(f32[2,32,512]{2,1,0:T(8,128)S(1)} %get-tuple-element.358.own_lo_ref), channel_id=1, source_target_pairs={{8,0},{16,8},{24,16},{0,24},{9,1},{17,9},{25,17},{1,25},{10,2},{18... | collective-permute-start | bytes 393224 | tf_op jit(solution)/shard_map/ppermute | solution.py:576
  132.2 17.8 %collective-permute-start.45 = (f32[32,8,256]{2,1,0:T(8,128)S(1)}, f32[32,8,256]{2,1,0:T(8,128)S(1)}, u32[]{:S(2)}, u32[]{:S(2)}) collective-permute-start(f32[32,8,256]{2,1,0:T(8,128)S(1)} %get-tuple-element.370), channel_id=1, source_target_pairs={{0,6},{1,7},{2,4},{3,5},{4,2},{5,3},{6,0},{7,1},{8,14},{9,15},{10,... | collective-permute-start | bytes 786440 | tf_op jit(solution)/shard_map/ppermute | solution.py:599
  132.7 20.8 %collective-permute-start.43 = (f32[32,8,256]{2,1,0:T(8,128)S(1)}, f32[32,8,256]{2,1,0:T(8,128)S(1)}, u32[]{:S(2)}, u32[]{:S(2)}) collective-permute-start(f32[32,8,256]{2,1,0:T(8,128)S(1)} %get-tuple-element.361), channel_id=1, source_target_pairs={{0,5},{1,4},{2,7},{3,6},{4,1},{5,0},{6,3},{7,2},{8,13},{9,12},{10,... | collective-permute-start | bytes 786440 | tf_op jit(solution)/shard_map/ppermute | solution.py:599
  140.1 23.4 %collective-permute-start.49 = (f32[32,8,256]{2,1,0:T(8,128)S(1)}, f32[32,8,256]{2,1,0:T(8,128)S(1)}, u32[]{:S(2)}, u32[]{:S(2)}) collective-permute-start(f32[32,8,256]{2,1,0:T(8,128)S(1)} %get-tuple-element.384), channel_id=1, source_target_pairs={{0,3},{1,2},{2,1},{3,0},{4,7},{5,6},{6,5},{7,4},{8,11},{9,10},{10,... | collective-permute-start | bytes 786440 | tf_op jit(solution)/shard_map/ppermute | solution.py:599
  140.1 15.4 %collective-permute-start.44 = (f32[32,8,256]{2,1,0:T(8,128)S(1)}, f32[32,8,256]{2,1,0:T(8,128)S(1)}, u32[]{:S(2)}, u32[]{:S(2)}) collective-permute-start(f32[32,8,256]{2,1,0:T(8,128)S(1)} %get-tuple-element.363), channel_id=1, source_target_pairs={{0,7},{1,6},{2,5},{3,4},{4,3},{5,2},{6,1},{7,0},{8,15},{9,14},{10,... | collective-permute-start | bytes 786440 | tf_op jit(solution)/shard_map/ppermute | solution.py:599
  149.9 13.6 %collective-permute-start.48 = (f32[32,8,256]{2,1,0:T(8,128)S(1)}, f32[32,8,256]{2,1,0:T(8,128)S(1)}, u32[]{:S(2)}, u32[]{:S(2)}) collective-permute-start(f32[32,8,256]{2,1,0:T(8,128)S(1)} %get-tuple-element.381), channel_id=1, source_target_pairs={{0,1},{1,0},{2,3},{3,2},{4,5},{5,4},{6,7},{7,6},{8,9},{9,8},{10,11... | collective-permute-start | bytes 786440 | tf_op jit(solution)/shard_map/ppermute | solution.py:599
  150.0 5.9 %collective-permute-start.46 = (f32[1,32,512]{2,1,0:T(8,128)S(1)}, f32[1,32,512]{2,1,0:T(8,128)S(1)}, u32[]{:S(2)}, u32[]{:S(2)}) collective-permute-start(f32[1,32,512]{2,1,0:T(8,128)S(1)} %get-tuple-element.371), channel_id=1, source_target_pairs={{8,0},{16,8},{24,16},{0,24},{9,1},{17,9},{25,17},{1,25},{10,2},{18... | collective-permute-start | bytes 196616 | tf_op jit(solution)/shard_map/ppermute | solution.py:576
  153.5 6.1 %collective-permute-start.47 = (f32[1,32,512]{2,1,0:T(8,128)S(1)}, f32[1,32,512]{2,1,0:T(8,128)S(1)}, u32[]{:S(2)}, u32[]{:S(2)}) collective-permute-start(f32[1,32,512]{2,1,0:T(8,128)S(1)} %get-tuple-element.372), channel_id=1, source_target_pairs={{0,8},{8,16},{16,24},{24,0},{1,9},{9,17},{17,25},{25,1},{2,10},{10... | collective-permute-start | bytes 196616 | tf_op jit(solution)/shard_map/ppermute | solution.py:576
  (13 other events, 105.6 us)

commit v11 on v9

--- a/solution.py
+++ b/solution.py
@@ -137,22 +137,22 @@
         target[...] = source[0]
 
 
-def pack(position, adjoint, comp, limit):
+def pack(position, adjoint, comp, limit, distances):
     _, per, nodes, elements = adjoint.shape
-    lines = nodes // LINE
+    lines = len(distances)
     block = per // 2
 
     def source(d):
         return pl.BlockSpec((1, block, LINE, elements), lambda i, pos: (comp, i, pos[1] ^ d, 0))
 
-    size = per * nodes * elements
+    size = per * lines * LINE * elements
     return pl.pallas_call(
         pack_kernel,
         out_shape=[jax.ShapeDtypeStruct((per, LINE, elements), F32)] * lines,
         grid_spec=pltpu.PrefetchScalarGridSpec(
             num_scalar_prefetch=1,
             grid=(per // block,),
-            in_specs=[source(d) for d in range(lines)],
+            in_specs=[source(d) for d in distances],
             out_specs=[pl.BlockSpec((block, LINE, elements), lambda i, pos: (i, 0, 0))] * lines,
         ),
         compiler_params=params(limit),
@@ -292,8 +292,8 @@
     return (1.0 - RELAXATION) * pot + inverse * (source - applied)
 
 
-def coef_block(coefs):
-    return 8 if coefs % 8 == 0 else coefs
+def coef_block(coefs, block=8):
+    return block if coefs % block == 0 else coefs
 
 
 def start_kernel(
@@ -340,7 +340,7 @@
     coefs, part, elements = z[0].shape
     nodes = len(z) * part
     shared = gather.shape[2]
-    block = coef_block(coefs)
+    block = coef_block(coefs, 16)
     field = [pl.BlockSpec((block, part, elements), lambda i: (i, 0, 0))] * len(z)
     flat = pl.BlockSpec((block * nodes, elements), lambda i: (i, 0))
     face = pl.BlockSpec((2, block, shared), lambda i: (0, i, 0))
@@ -413,7 +413,7 @@
     elements = local.shape[1]
     coefs = local.shape[0] // nodes
     shared = gather.shape[2]
-    block = coef_block(coefs)
+    block = coef_block(coefs, 16)
     flat = pl.BlockSpec((block * nodes, elements), lambda i: (i, 0))
     one = pl.BlockSpec((1, block, shared), lambda i: (0, i, 0))
     two = pl.BlockSpec((2, block, shared), lambda i: (0, i, 0))
@@ -505,7 +505,7 @@
 def add_force(position, local, got, face, geometry, dpack, scatter, mask, px, pz):
     coefs, nodes, elements = px.shape
     shared = scatter.shape[1]
-    block = coef_block(coefs)
+    block = coef_block(coefs, 16)
     flat = pl.BlockSpec((block * nodes, elements), lambda i: (i, 0))
     one = pl.BlockSpec((1, block, shared), lambda i: (0, i, 0))
     part = pl.BlockSpec((block, nodes, elements), lambda i: (i, 0, 0))
@@ -633,7 +633,13 @@
 
     def columns(comp):
         if direct:
-            return pack(position, adjoint, comp, LARGE_LIMIT if comp == 2 else VMEM_LIMIT)
+            if comp != 2:
+                return pack(position, adjoint, comp, VMEM_LIMIT, range(lines))
+            early = (2, 4, 6)
+            late = [d for d in range(lines) if d not in early]
+            got = dict(zip(early, pack(position, adjoint, comp, LARGE_LIMIT, early)))
+            got.update(zip(late, pack(position, adjoint, comp, LARGE_LIMIT, late)))
+            return [got[d] for d in range(lines)]
         return [jnp.moveaxis(adjoint[comp].reshape(per, peers, share, elements), 1, 0)]
 
     def gather_planes(block):

time: 165 us -> 172 us (1.042)
  waiting for transfers between devices: 64.6 us -> 69.5 us
  starting transfers between devices: 57.9 us -> 60.2 us
    ppermute x42, waiting for transfers between devices: 56.1 us -> 62.2 us  [send(): self.flight.append(lax.ppermute(block, 'four', pairs))]
    pallas_call x3 -> x4, Pallas kernels: 4.88 us -> 6 us  [pack(): pl.pallas_call(pack_kernel, out_shape=[jax.ShapeDtypeStruct((per, LINE, e...]
  transfers between devices with their start and end apart: 50 -> 50, of which waited for: 25 -> 19; matrix products, arithmetic and copies ran while one was open for 0% -> 0% of each run, Pallas kernels for 20% -> 19%
where the time goes in v11:
time: 172 us; the launch traced here: 171 us
  waiting for transfers between devices  69.5 us (40%)
  starting transfers between devices  60.2 us (35%)
  Pallas kernels  41.3 us (24%)
    ppermute x42, waiting for transfers between devices, send(): self.flight.append(lax.ppermute(block, 'four', pairs))  62.2 us
    ppermute x42, starting transfers between devices, send(): self.flight.append(lax.ppermute(block, 'four', pairs))  42.6 us
    ppermute x8, starting transfers between devices, swap_faces(): return (lax.ppermute(lo, 'dom', down_way), lax.ppermute(up, 'dom', up_way))  17.6 us
    pallas_call x2, Pallas kernels, two_sweeps(): pl.pallas_call(functools.partial(sweeps_kernel, block, keep), out_shape=[...  11.7 us
    pallas_call x3, Pallas kernels, transform(): pl.pallas_call(functools.partial(transform_kernel, count), out_shape=[jax...  7.34 us
    ppermute x8, waiting for transfers between devices, swap_faces(): return (lax.ppermute(lo, 'dom', down_way), lax.ppermute(up, 'dom', up_way))  7.32 us
    pallas_call x4, Pallas kernels, pack(): pl.pallas_call(pack_kernel, out_shape=[jax.ShapeDtypeStruct((per, LINE, e...  6 us
    pallas_call x1, Pallas kernels, finish(): pl.pallas_call(functools.partial(finish_kernel, block, len(y)), out_shape...  4 us
  transfers between devices with their start and end apart: 50, of which 19 were waited for; matrix products, arithmetic and copies ran while one was open for 0% of the time, Pallas kernels for 19%

profile of v11, /device:TPU:0, one launch (start us, length us, event | category | flops | bytes accessed | tf_op | source)
XLA Modules:
  0.0 171.5 jit_solution(2769010061844181700)
XLA Ops:
  0.1 1.8 %pack.6 = (f32[32,8,256]{2,1,0:T(8,128)S(1)}, f32[32,8,256]{2,1,0:T(8,128)S(1)}, f32[32,8,256]{2,1,0:T(8,128)S(1)}) custom-call(s32[2]{0:T(128)S(1)} %pad_add_fusion.pos_ref, f32[3,32,64,256]{3,2,1,0:T(8,128)} %refs_7_.3, f32[3,32,64,256]{3,2,1,0:T(8,128)} %refs_7_.3, f32[3,32,64,256]{3,2,1,0:T(8,128)} %refs_7_.3), custom_call_target="tpu_custom_call" | custom-call | bytes 1572864 | tf_op jit(solution)/shard_map/pack/pallas_call | solution.py:149
  2.0 3.0 %collective-permute-start = (f32[32,8,256]{2,1,0:T(8,128)S(1)}, f32[32,8,256]{2,1,0:T(8,128)S(1)}, u32[]{:S(2)}, u32[]{:S(2)}) collective-permute-start(f32[32,8,256]{2,1,0:T(8,128)S(1)} %get-tuple-element.204), channel_id=1, source_target_pairs={{0,4},{1,5},{2,6},{3,7},{4,0},{5,1},{6,2},{7,3},{8,12},{9,13},{10,... | collective-permute-start | bytes 786440 | tf_op jit(solution)/shard_map/ppermute | solution.py:599
  5.0 1.5 collective-permute-start.2
  7.9 2.1 %collective-permute-start.4 = (f32[2,512]{1,0:T(2,128)S(1)}, f32[2,512]{1,0:T(2,128)S(1)}, u32[]{:S(2)}, u32[]{:S(2)}) collective-permute-start(f32[2,512]{1,0:T(2,128)S(1)} %get-tuple-element.387), channel_id=1, source_target_pairs={{0,8},{8,16},{16,24},{24,0},{1,9},{9,17},{17,25},{25,1},{2,10},{10... | collective-permute-start | bytes 12296 | tf_op jit(solution)/shard_map/ppermute | solution.py:576
  10.0 2.1 %collective-permute-start.3 = (f32[2,512]{1,0:T(2,128)S(1)}, f32[2,512]{1,0:T(2,128)S(1)}, u32[]{:S(2)}, u32[]{:S(2)}) collective-permute-start(f32[2,512]{1,0:T(2,128)S(1)} %get-tuple-element.388), channel_id=1, source_target_pairs={{8,0},{16,8},{24,16},{0,24},{9,1},{17,9},{25,17},{1,25},{10,2},{18... | collective-permute-start | bytes 12296 | tf_op jit(solution)/shard_map/ppermute | solution.py:576
  12.1 2.0 %pack.5 = (f32[32,8,256]{2,1,0:T(8,128)S(1)}, f32[32,8,256]{2,1,0:T(8,128)S(1)}, f32[32,8,256]{2,1,0:T(8,128)S(1)}, f32[32,8,256]{2,1,0:T(8,128)S(1)}, f32[32,8,256]{2,1,0:T(8,128)S(1)}) custom-call(s32[2]{0:T(128)S(1)} %pad_add_fusion.pos_ref, f32[3,32,64,256]{3,2,1,0:T(8,128)} %refs_7_.3, f32[3,32,64,256]{3,2,1,0:T(8,128)} %refs_7_.3, ...), custom_call_target="tpu_custom_call" | custom-call | bytes 2621440 | tf_op jit(solution)/shard_map/pack/pallas_call | solution.py:149
  14.2 2.9 %collective-permute-start.6 = (f32[32,8,256]{2,1,0:T(8,128)S(1)}, f32[32,8,256]{2,1,0:T(8,128)S(1)}, u32[]{:S(2)}, u32[]{:S(2)}) collective-permute-start(f32[32,8,256]{2,1,0:T(8,128)S(1)} %get-tuple-element.217), channel_id=1, source_target_pairs={{0,5},{1,4},{2,7},{3,6},{4,1},{5,0},{6,3},{7,2},{8,13},{9,12},{10,... | collective-permute-start | bytes 786440 | tf_op jit(solution)/shard_map/ppermute | solution.py:599
  19.6 1.7 collective-permute-start.11
  21.3 2.7 %collective-permute-done.5.refs_3_ = f32[32,8,256]{2,1,0:T(8,128)S(1)} collective-permute-done((f32[32,8,256]{2,1,0:T(8,128)S(1)}, f32[32,8,256]{2,1,0:T(8,128)S(1)}, u32[]{:S(2)}, u32[]{:S(2)}) %collective-permute-start.5) | collective-permute-done | bytes 262176 | tf_op jit(solution)/shard_map/ppermute | solution.py:599
  24.4 2.4 %collective-permute-start.14 = (f32[32,8,256]{2,1,0:T(8,128)S(1)}, f32[32,8,256]{2,1,0:T(8,128)S(1)}, u32[]{:S(2)}, u32[]{:S(2)}) collective-permute-start(f32[32,8,256]{2,1,0:T(8,128)S(1)} %get-tuple-element.251), channel_id=1, source_target_pairs={{0,6},{1,7},{2,4},{3,5},{4,2},{5,3},{6,0},{7,1},{8,14},{9,15},{10,... | collective-permute-start | bytes 786440 | tf_op jit(solution)/shard_map/ppermute | solution.py:599
  26.8 2.9 %collective-permute-done.8.refs_7_ = f32[32,8,256]{2,1,0:T(8,128)S(1)} collective-permute-done((f32[32,8,256]{2,1,0:T(8,128)S(1)}, f32[32,8,256]{2,1,0:T(8,128)S(1)}, u32[]{:S(2)}, u32[]{:S(2)}) %collective-permute-start.8) | collective-permute-done | bytes 262176 | tf_op jit(solution)/shard_map/ppermute | solution.py:599
  29.7 2.4 %transform.3 = (f32[32,8,256]{2,1,0:T(8,128)S(1)}, f32[32,8,256]{2,1,0:T(8,128)S(1)}, f32[32,8,256]{2,1,0:T(8,128)S(1)}, f32[32,8,256]{2,1,0:T(8,128)S(1)}, f32[...) custom-call(bf16[512,256]{1,0:T(8,128)(2,1)S(1)} %permuted_table.1.tab, ...), custom_call_target="tpu_custom_call" | custom-call | flops 805306368 | bytes 4194304 | tf_op jit(solution)/shard_map/transform/pallas_call | solution.py:122
  32.1 2.1 %collective-permute-start.13 = (f32[32,8,256]{2,1,0:T(8,128)S(1)}, f32[32,8,256]{2,1,0:T(8,128)S(1)}, u32[]{:S(2)}, u32[]{:S(2)}) collective-permute-start(f32[32,8,256]{2,1,0:T(8,128)S(1)} %get-tuple-element.248), channel_id=1, source_target_pairs={{0,5},{1,4},{2,7},{3,6},{4,1},{5,0},{6,3},{7,2},{8,13},{9,12},{10,... | collective-permute-start | bytes 786440 | tf_op jit(solution)/shard_map/ppermute | solution.py:599
  34.2 2.2 %collective-permute-done.11.refs_2_ = f32[32,8,256]{2,1,0:T(8,128)S(1)} collective-permute-done((f32[32,8,256]{2,1,0:T(8,128)S(1)}, f32[32,8,256]{2,1,0:T(8,128)S(1)}, u32[]{:S(2)}, u32[]{:S(2)}) %collective-permute-start.11) | collective-permute-done | bytes 262176 | tf_op jit(solution)/shard_map/ppermute | solution.py:599
  37.9 3.1 %collective-permute-done.14.refs_6_ = f32[32,8,256]{2,1,0:T(8,128)S(1)} collective-permute-done((f32[32,8,256]{2,1,0:T(8,128)S(1)}, f32[32,8,256]{2,1,0:T(8,128)S(1)}, u32[]{:S(2)}, u32[]{:S(2)}) %collective-permute-start.14) | collective-permute-done | bytes 262176 | tf_op jit(solution)/shard_map/ppermute | solution.py:599
  41.0 1.5 collective-permute-start.18
  42.4 9.6 %collective-permute-done.13.refs_5_ = f32[32,8,256]{2,1,0:T(8,128)S(1)} collective-permute-done((f32[32,8,256]{2,1,0:T(8,128)S(1)}, f32[32,8,256]{2,1,0:T(8,128)S(1)}, u32[]{:S(2)}, u32[]{:S(2)}) %collective-permute-start.13) | collective-permute-done | bytes 262176 | tf_op jit(solution)/shard_map/ppermute | solution.py:599
  52.0 2.5 %collective-permute-start.21 = (f32[32,8,256]{2,1,0:T(8,128)S(1)}, f32[32,8,256]{2,1,0:T(8,128)S(1)}, u32[]{:S(2)}, u32[]{:S(2)}) collective-permute-start(f32[32,8,256]{2,1,0:T(8,128)S(1)} %get-tuple-element.293), channel_id=1, source_target_pairs={{0,6},{1,7},{2,4},{3,5},{4,2},{5,3},{6,0},{7,1},{8,14},{9,15},{10,... | collective-permute-start | bytes 786440 | tf_op jit(solution)/shard_map/ppermute | solution.py:599
  56.2 1.6 collective-permute-start.20
  57.8 2.4 %transform.4 = (f32[32,8,256]{2,1,0:T(8,128)S(1)}, f32[32,8,256]{2,1,0:T(8,128)S(1)}, f32[32,8,256]{2,1,0:T(8,128)S(1)}, f32[32,8,256]{2,1,0:T(8,128)S(1)}, f32[...) custom-call(bf16[512,256]{1,0:T(8,128)(2,1)S(1)} %permuted_table.1.tab, ...), custom_call_target="tpu_custom_call" | custom-call | flops 805306368 | bytes 4194304 | tf_op jit(solution)/shard_map/transform/pallas_call | solution.py:122
  61.4 2.1 %collective-permute-done.21.refs_6_ = f32[32,8,256]{2,1,0:T(8,128)S(1)} collective-permute-done((f32[32,8,256]{2,1,0:T(8,128)S(1)}, f32[32,8,256]{2,1,0:T(8,128)S(1)}, u32[]{:S(2)}, u32[]{:S(2)}) %collective-permute-start.21) | collective-permute-done | bytes 262176 | tf_op jit(solution)/shard_map/ppermute | solution.py:599
  63.5 1.5 collective-permute-start.25
  64.9 4.2 %collective-permute-done.19.refs_3_ = f32[32,8,256]{2,1,0:T(8,128)S(1)} collective-permute-done((f32[32,8,256]{2,1,0:T(8,128)S(1)}, f32[32,8,256]{2,1,0:T(8,128)S(1)}, u32[]{:S(2)}, u32[]{:S(2)}) %collective-permute-start.19) | collective-permute-done | bytes 262176 | tf_op jit(solution)/shard_map/ppermute | solution.py:599
  70.4 9.8 %collective-permute-done.20.refs_5_ = f32[32,8,256]{2,1,0:T(8,128)S(1)} collective-permute-done((f32[32,8,256]{2,1,0:T(8,128)S(1)}, f32[32,8,256]{2,1,0:T(8,128)S(1)}, u32[]{:S(2)}, u32[]{:S(2)}) %collective-permute-start.20) | collective-permute-done | bytes 262176 | tf_op jit(solution)/shard_map/ppermute | solution.py:599
  81.7 2.6 %collective-permute-start.29 = (f32[32,8,256]{2,1,0:T(8,128)S(1)}, f32[32,8,256]{2,1,0:T(8,128)S(1)}, u32[]{:S(2)}, u32[]{:S(2)}) collective-permute-start(f32[32,8,256]{2,1,0:T(8,128)S(1)} %get-tuple-element.318), channel_id=1, source_target_pairs={{0,7},{1,6},{2,5},{3,4},{4,3},{5,2},{6,1},{7,0},{8,15},{9,14},{10,... | collective-permute-start | bytes 786440 | tf_op jit(solution)/shard_map/ppermute | solution.py:599
  84.3 7.1 %collective-permute-done.23.refs_12_ = f32[32,8,256]{2,1,0:T(8,128)S(1)} collective-permute-done((f32[32,8,256]{2,1,0:T(8,128)S(1)}, f32[32,8,256]{2,1,0:T(8,128)S(1)}, u32[]{:S(2)}, u32[]{:S(2)}) %collective-permute-start.23) | collective-permute-done | bytes 262176 | tf_op jit(solution)/shard_map/ppermute | solution.py:599
  92.0 1.6 collective-permute-start.35
  93.9 1.6 collective-permute-start.33
  95.5 4.5 %collective-permute-done.29.refs_15_ = f32[32,8,256]{2,1,0:T(8,128)S(1)} collective-permute-done((f32[32,8,256]{2,1,0:T(8,128)S(1)}, f32[32,8,256]{2,1,0:T(8,128)S(1)}, u32[]{:S(2)}, u32[]{:S(2)}) %collective-permute-start.29) | collective-permute-done | bytes 262176 | tf_op jit(solution)/shard_map/ppermute | solution.py:599
  100.0 5.3 %collective-permute-done.27.refs_13_ = f32[32,8,256]{2,1,0:T(8,128)S(1)} collective-permute-done((f32[32,8,256]{2,1,0:T(8,128)S(1)}, f32[32,8,256]{2,1,0:T(8,128)S(1)}, u32[]{:S(2)}, u32[]{:S(2)}) %collective-permute-start.27) | collective-permute-done | bytes 262176 | tf_op jit(solution)/shard_map/ppermute | solution.py:599
  105.3 1.4 collective-permute-start.30
  106.8 4.0 %start_solve.1 = (f32[2048,256]{1,0:T(8,128)S(1)}, f32[2048,256]{1,0:T(8,128)S(1)}, f32[2048,256]{1,0:T(8,128)S(1)}, f32[2,32,512]{2,1,0:T(8,128)S(1)}, f32[2,32,512]{2,1,0:T(8,128)S(1)}) custom-call(s32[2]{0:T(128)S(1)} %pad_add_fusion.pos_ref, f32[2,256]{1,0:T(2,128)S(1)} %copy-done.5, f32[7,64,256]{2,1,0:T(8,128)S(1)} %get-tuple-element.196.diag_ref.coef_ref, ...), custom_call_target="tpu_custom_call" | custom-call | flops 1000000 | bytes 100000 | tf_op jit(solution)/shard_map/start_solve/pallas_call | solution.py:348
  110.7 1.5 collective-permute-start.32
  113.9 3.3 %collective-permute-done.33.refs_4_ = f32[32,8,256]{2,1,0:T(8,128)S(1)} collective-permute-done((f32[32,8,256]{2,1,0:T(8,128)S(1)}, f32[32,8,256]{2,1,0:T(8,128)S(1)}, u32[]{:S(2)}, u32[]{:S(2)}) %collective-permute-start.33) | collective-permute-done | bytes 262176 | tf_op jit(solution)/shard_map/ppermute | solution.py:599
  118.9 3.4 %collective-permute-start.31 = (f32[2,32,512]{2,1,0:T(8,128)S(1)}, f32[2,32,512]{2,1,0:T(8,128)S(1)}, u32[]{:S(2)}, u32[]{:S(2)}) collective-permute-start(f32[2,32,512]{2,1,0:T(8,128)S(1)} %get-tuple-element.330.own_lo_ref), channel_id=1, source_target_pairs={{8,0},{16,8},{24,16},{0,24},{9,1},{17,9},{25,17},{1,25},{10,2},{18... | collective-permute-start | bytes 393224 | tf_op jit(solution)/shard_map/ppermute | solution.py:576
  122.3 2.7 %partial_update.1 = (f32[32,64,256]{2,1,0:T(8,128)S(1)}, f32[32,64,256]{2,1,0:T(8,128)S(1)}, f32[32,64,256]{2,1,0:T(8,128)S(1)}) custom-call(f32[7,64,256]{2,1,0:T(8,128)S(1)} %get-tuple-element.196.diag_ref.coef_ref, bf16[128,192]{1,0:T(8,128)(2,1)S(1)} %get-tuple-element.197.dpack_ref, f32[32,8,256]{2,1,0:T(8,128)S(1)} %get-tuple-element.276.refs_0_, ...), custom_call_target="tpu_custom_call" | custom-call | flops 1000000 | bytes 100000 | tf_op jit(solution)/shard_map/partial_update/pallas_call | solution.py:468
  125.4 5.5 %two_sweeps.2 = (f32[2048,256]{1,0:T(8,128)S(1)}, f32[2,32,512]{2,1,0:T(8,128)S(1)}, f32[2,32,512]{2,1,0:T(8,128)S(1)}) custom-call(s32[2]{0:T(128)S(1)} %pad_add_fusion.pos_ref, f32[2048,256]{1,0:T(8,128)S(1)} %get-tuple-element.326.local_ref, f32[2048,256]{1,0:T(8,128)S(1)} %get-tuple-element.327.source_ref, ...), custom_call_target="tpu_custom_call" | custom-call | flops 1000000 | bytes 100000 | tf_op jit(solution)/shard_map/two_sweeps/pallas_call | solution.py:422
  131.0 2.5 %transform.5 = (f32[32,8,256]{2,1,0:T(8,128)S(1)}, f32[32,8,256]{2,1,0:T(8,128)S(1)}, f32[32,8,256]{2,1,0:T(8,128)S(1)}, f32[32,8,256]{2,1,0:T(8,128)S(1)}, f32[...) custom-call(bf16[512,256]{1,0:T(8,128)(2,1)S(1)} %permuted_table.1.tab, ...), custom_call_target="tpu_custom_call" | custom-call | flops 805306368 | bytes 4194304 | tf_op jit(solution)/shard_map/transform/pallas_call | solution.py:122
  133.5 1.7 %collective-permute-start.40 = (f32[32,8,256]{2,1,0:T(8,128)S(1)}, f32[32,8,256]{2,1,0:T(8,128)S(1)}, u32[]{:S(2)}, u32[]{:S(2)}) collective-permute-start(f32[32,8,256]{2,1,0:T(8,128)S(1)} %get-tuple-element.355), channel_id=1, source_target_pairs={{0,4},{1,5},{2,6},{3,7},{4,0},{5,1},{6,2},{7,3},{8,12},{9,13},{10,... | collective-permute-start | bytes 786440 | tf_op jit(solution)/shard_map/ppermute | solution.py:599
  136.2 3.8 %collective-permute-start.41 = (f32[2,32,512]{2,1,0:T(8,128)S(1)}, f32[2,32,512]{2,1,0:T(8,128)S(1)}, u32[]{:S(2)}, u32[]{:S(2)}) collective-permute-start(f32[2,32,512]{2,1,0:T(8,128)S(1)} %get-tuple-element.359.own_lo_ref), channel_id=1, source_target_pairs={{8,0},{16,8},{24,16},{0,24},{9,1},{17,9},{25,17},{1,25},{10,2},{18... | collective-permute-start | bytes 393224 | tf_op jit(solution)/shard_map/ppermute | solution.py:576
  141.3 2.9 %collective-permute-done.39.refs_2_ = f32[32,8,256]{2,1,0:T(8,128)S(1)} collective-permute-done((f32[32,8,256]{2,1,0:T(8,128)S(1)}, f32[32,8,256]{2,1,0:T(8,128)S(1)}, u32[]{:S(2)}, u32[]{:S(2)}) %collective-permute-start.39) | collective-permute-done | bytes 262176 | tf_op jit(solution)/shard_map/ppermute | solution.py:599
  145.4 6.1 %two_sweeps.3 = (f32[2048,256]{1,0:T(8,128)S(1)}, f32[1,32,512]{2,1,0:T(8,128)S(1)}, f32[1,32,512]{2,1,0:T(8,128)S(1)}) custom-call(s32[2]{0:T(128)S(1)} %pad_add_fusion.pos_ref, f32[2048,256]{1,0:T(8,128)S(1)} %get-tuple-element.357.local_ref, f32[2048,256]{1,0:T(8,128)S(1)} %get-tuple-element.327.source_ref, ...), custom_call_target="tpu_custom_call" | custom-call | flops 1000000 | bytes 100000 | tf_op jit(solution)/shard_map/two_sweeps/pallas_call | solution.py:422
  151.6 2.2 %collective-permute-done.45.refs_3_ = f32[32,8,256]{2,1,0:T(8,128)S(1)} collective-permute-done((f32[32,8,256]{2,1,0:T(8,128)S(1)}, f32[32,8,256]{2,1,0:T(8,128)S(1)}, u32[]{:S(2)}, u32[]{:S(2)}) %collective-permute-start.45) | collective-permute-done | bytes 262176 | tf_op jit(solution)/shard_map/ppermute | solution.py:599
  153.7 4.3 %collective-permute-start.46 = (f32[1,32,512]{2,1,0:T(8,128)S(1)}, f32[1,32,512]{2,1,0:T(8,128)S(1)}, u32[]{:S(2)}, u32[]{:S(2)}) collective-permute-start(f32[1,32,512]{2,1,0:T(8,128)S(1)} %get-tuple-element.372), channel_id=1, source_target_pairs={{8,0},{16,8},{24,16},{0,24},{9,1},{17,9},{25,17},{1,25},{10,2},{18... | collective-permute-start | bytes 196616 | tf_op jit(solution)/shard_map/ppermute | solution.py:576
  158.0 1.9 %collective-permute-done.46.got_up_ref = f32[1,32,512]{2,1,0:T(8,128)S(1)} collective-permute-done((f32[1,32,512]{2,1,0:T(8,128)S(1)}, f32[1,32,512]{2,1,0:T(8,128)S(1)}, u32[]{:S(2)}, u32[]{:S(2)}) %collective-permute-start.46) | collective-permute-done | bytes 65568 | tf_op jit(solution)/shard_map/ppermute | solution.py:576
  159.9 4.2 %collective-permute-done.47.got_lo_ref = f32[1,32,512]{2,1,0:T(8,128)S(1)} collective-permute-done((f32[1,32,512]{2,1,0:T(8,128)S(1)}, f32[1,32,512]{2,1,0:T(8,128)S(1)}, u32[]{:S(2)}, u32[]{:S(2)}) %collective-permute-start.47) | collective-permute-done | bytes 65568 | tf_op jit(solution)/shard_map/ppermute | solution.py:576
  164.1 3.4 %add_force.1 = (f32[3,32,64,256]{3,2,1,0:T(8,128)}, f32[32,64,256]{2,1,0:T(8,128)S(1)}) custom-call(s32[2]{0:T(128)S(1)} %pad_add_fusion.pos_ref, f32[2048,256]{1,0:T(8,128)S(1)} %get-tuple-element.363.local_ref, f32[1,32,512]{2,1,0:T(8,128)S(1)} %collective-permute-done.46.got_up_ref, f32[1,32,512]{2,1,0:T(8,128)S(1)} %collective-permute-done.47.got_lo_ref, ...), custom_call_target="tpu_custom_call" | custom-call | flops 1000000 | bytes 100000 | tf_op jit(solution)/shard_map/add_force/pallas_call | solution.py:512
  167.5 4.0 %finish.1 = f32[3,32,64,256]{3,2,1,0:T(8,128)} custom-call(s32[2]{0:T(128)S(1)} %pad_add_fusion.pos_ref, f32[7,64,256]{2,1,0:T(8,128)S(1)} %get-tuple-element.196.diag_ref.coef_ref, bf16[128,192]{1,0:T(8,128)(2,1)S(1)} %get-tuple-element.197.dpack_ref, f32[32,64,256]{2,1,0:T(8,128)S(1)} %get-tuple-element.376.px_ref, ...), custom_call_target="tpu_custom_call", output_to_operand_aliasing={{}: (5, {})} | custom-call | flops 1000000 | bytes 100000 | tf_op jit(solution)/shard_map/finish/pallas_call | solution.py:552
  (92 shorter events, 19.8 us)
Async XLA Ops:
  2.0 15.1 %collective-permute-start = (f32[32,8,256]{2,1,0:T(8,128)S(1)}, f32[32,8,256]{2,1,0:T(8,128)S(1)}, u32[]{:S(2)}, u32[]{:S(2)}) collective-permute-start(f32[32,8,256]{2,1,0:T(8,128)S(1)} %get-tuple-element.204), channel_id=1, source_target_pairs={{0,4},{1,5},{2,6},{3,7},{4,0},{5,1},{6,2},{7,3},{8,12},{9,13},{10,... | collective-permute-start | bytes 786440 | tf_op jit(solution)/shard_map/ppermute | solution.py:599
  5.0 12.1 %collective-permute-start.2 = (f32[32,8,256]{2,1,0:T(8,128)S(1)}, f32[32,8,256]{2,1,0:T(8,128)S(1)}, u32[]{:S(2)}, u32[]{:S(2)}) collective-permute-start(f32[32,8,256]{2,1,0:T(8,128)S(1)} %get-tuple-element.208), channel_id=1, source_target_pairs={{0,2},{1,3},{2,0},{3,1},{4,6},{5,7},{6,4},{7,5},{8,10},{9,11},{10,... | collective-permute-start | bytes 786440 | tf_op jit(solution)/shard_map/ppermute | solution.py:599
  6.5 13.1 %collective-permute-start.7 = (f32[32,8,256]{2,1,0:T(8,128)S(1)}, f32[32,8,256]{2,1,0:T(8,128)S(1)}, u32[]{:S(2)}, u32[]{:S(2)}) collective-permute-start(f32[32,8,256]{2,1,0:T(8,128)S(1)} %get-tuple-element.220), channel_id=1, source_target_pairs={{0,6},{1,7},{2,4},{3,5},{4,2},{5,3},{6,0},{7,1},{8,14},{9,15},{10,... | collective-permute-start | bytes 786440 | tf_op jit(solution)/shard_map/ppermute | solution.py:599
  7.9 6.2 %collective-permute-start.4 = (f32[2,512]{1,0:T(2,128)S(1)}, f32[2,512]{1,0:T(2,128)S(1)}, u32[]{:S(2)}, u32[]{:S(2)}) collective-permute-start(f32[2,512]{1,0:T(2,128)S(1)} %get-tuple-element.387), channel_id=1, source_target_pairs={{0,8},{8,16},{16,24},{24,0},{1,9},{9,17},{17,25},{25,1},{2,10},{10... | collective-permute-start | bytes 12296 | tf_op jit(solution)/shard_map/ppermute | solution.py:576
  14.1 9.9 %collective-permute-start.5 = (f32[32,8,256]{2,1,0:T(8,128)S(1)}, f32[32,8,256]{2,1,0:T(8,128)S(1)}, u32[]{:S(2)}, u32[]{:S(2)}) collective-permute-start(f32[32,8,256]{2,1,0:T(8,128)S(1)} %get-tuple-element.213), channel_id=1, source_target_pairs={{0,3},{1,2},{2,1},{3,0},{4,7},{5,6},{6,5},{7,4},{8,11},{9,10},{10,... | collective-permute-start | bytes 786440 | tf_op jit(solution)/shard_map/ppermute | solution.py:599
  14.2 10.2 %collective-permute-start.6 = (f32[32,8,256]{2,1,0:T(8,128)S(1)}, f32[32,8,256]{2,1,0:T(8,128)S(1)}, u32[]{:S(2)}, u32[]{:S(2)}) collective-permute-start(f32[32,8,256]{2,1,0:T(8,128)S(1)} %get-tuple-element.217), channel_id=1, source_target_pairs={{0,5},{1,4},{2,7},{3,6},{4,1},{5,0},{6,3},{7,2},{8,13},{9,12},{10,... | collective-permute-start | bytes 786440 | tf_op jit(solution)/shard_map/ppermute | solution.py:599
  17.1 9.7 %collective-permute-start.1 = (f32[32,8,256]{2,1,0:T(8,128)S(1)}, f32[32,8,256]{2,1,0:T(8,128)S(1)}, u32[]{:S(2)}, u32[]{:S(2)}) collective-permute-start(f32[32,8,256]{2,1,0:T(8,128)S(1)} %get-tuple-element.205), channel_id=1, source_target_pairs={{0,1},{1,0},{2,3},{3,2},{4,5},{5,4},{6,7},{7,6},{8,9},{9,8},{10,11... | collective-permute-start | bytes 786440 | tf_op jit(solution)/shard_map/ppermute | solution.py:599
  17.1 12.6 %collective-permute-start.8 = (f32[32,8,256]{2,1,0:T(8,128)S(1)}, f32[32,8,256]{2,1,0:T(8,128)S(1)}, u32[]{:S(2)}, u32[]{:S(2)}) collective-permute-start(f32[32,8,256]{2,1,0:T(8,128)S(1)} %get-tuple-element.223), channel_id=1, source_target_pairs={{0,7},{1,6},{2,5},{3,4},{4,3},{5,2},{6,1},{7,0},{8,15},{9,14},{10,... | collective-permute-start | bytes 786440 | tf_op jit(solution)/shard_map/ppermute | solution.py:599
  19.6 16.8 %collective-permute-start.11 = (f32[32,8,256]{2,1,0:T(8,128)S(1)}, f32[32,8,256]{2,1,0:T(8,128)S(1)}, u32[]{:S(2)}, u32[]{:S(2)}) collective-permute-start(f32[32,8,256]{2,1,0:T(8,128)S(1)} %get-tuple-element.241), channel_id=1, source_target_pairs={{0,2},{1,3},{2,0},{3,1},{4,6},{5,7},{6,4},{7,5},{8,10},{9,11},{10,... | collective-permute-start | bytes 786440 | tf_op jit(solution)/shard_map/ppermute | solution.py:599
  24.0 13.0 %collective-permute-start.9 = (f32[32,8,256]{2,1,0:T(8,128)S(1)}, f32[32,8,256]{2,1,0:T(8,128)S(1)}, u32[]{:S(2)}, u32[]{:S(2)}) collective-permute-start(f32[32,8,256]{2,1,0:T(8,128)S(1)} %get-tuple-element.237), channel_id=1, source_target_pairs={{0,4},{1,5},{2,6},{3,7},{4,0},{5,1},{6,2},{7,3},{8,12},{9,13},{10,... | collective-permute-start | bytes 786440 | tf_op jit(solution)/shard_map/ppermute | solution.py:599
  24.4 16.5 %collective-permute-start.14 = (f32[32,8,256]{2,1,0:T(8,128)S(1)}, f32[32,8,256]{2,1,0:T(8,128)S(1)}, u32[]{:S(2)}, u32[]{:S(2)}) collective-permute-start(f32[32,8,256]{2,1,0:T(8,128)S(1)} %get-tuple-element.251), channel_id=1, source_target_pairs={{0,6},{1,7},{2,4},{3,5},{4,2},{5,3},{6,0},{7,1},{8,14},{9,15},{10,... | collective-permute-start | bytes 786440 | tf_op jit(solution)/shard_map/ppermute | solution.py:599
  32.1 19.9 %collective-permute-start.13 = (f32[32,8,256]{2,1,0:T(8,128)S(1)}, f32[32,8,256]{2,1,0:T(8,128)S(1)}, u32[]{:S(2)}, u32[]{:S(2)}) collective-permute-start(f32[32,8,256]{2,1,0:T(8,128)S(1)} %get-tuple-element.248), channel_id=1, source_target_pairs={{0,5},{1,4},{2,7},{3,6},{4,1},{5,0},{6,3},{7,2},{8,13},{9,12},{10,... | collective-permute-start | bytes 786440 | tf_op jit(solution)/shard_map/ppermute | solution.py:599
  36.4 18.1 %collective-permute-start.15 = (f32[32,8,256]{2,1,0:T(8,128)S(1)}, f32[32,8,256]{2,1,0:T(8,128)S(1)}, u32[]{:S(2)}, u32[]{:S(2)}) collective-permute-start(f32[32,8,256]{2,1,0:T(8,128)S(1)} %get-tuple-element.254), channel_id=1, source_target_pairs={{0,7},{1,6},{2,5},{3,4},{4,3},{5,2},{6,1},{7,0},{8,15},{9,14},{10,... | collective-permute-start | bytes 786440 | tf_op jit(solution)/shard_map/ppermute | solution.py:599
  36.5 18.1 %collective-permute-start.12 = (f32[32,8,256]{2,1,0:T(8,128)S(1)}, f32[32,8,256]{2,1,0:T(8,128)S(1)}, u32[]{:S(2)}, u32[]{:S(2)}) collective-permute-start(f32[32,8,256]{2,1,0:T(8,128)S(1)} %get-tuple-element.244), channel_id=1, source_target_pairs={{0,3},{1,2},{2,1},{3,0},{4,7},{5,6},{6,5},{7,4},{8,11},{9,10},{10,... | collective-permute-start | bytes 786440 | tf_op jit(solution)/shard_map/ppermute | solution.py:599
  37.0 19.2 %collective-permute-start.10 = (f32[32,8,256]{2,1,0:T(8,128)S(1)}, f32[32,8,256]{2,1,0:T(8,128)S(1)}, u32[]{:S(2)}, u32[]{:S(2)}) collective-permute-start(f32[32,8,256]{2,1,0:T(8,128)S(1)} %get-tuple-element.238), channel_id=1, source_target_pairs={{0,1},{1,0},{2,3},{3,2},{4,5},{5,4},{6,7},{7,6},{8,9},{9,8},{10,11... | collective-permute-start | bytes 786440 | tf_op jit(solution)/shard_map/ppermute | solution.py:599
  41.0 19.2 %collective-permute-start.18 = (f32[32,8,256]{2,1,0:T(8,128)S(1)}, f32[32,8,256]{2,1,0:T(8,128)S(1)}, u32[]{:S(2)}, u32[]{:S(2)}) collective-permute-start(f32[32,8,256]{2,1,0:T(8,128)S(1)} %get-tuple-element.283), channel_id=1, source_target_pairs={{0,2},{1,3},{2,0},{3,1},{4,6},{5,7},{6,4},{7,5},{8,10},{9,11},{10,... | collective-permute-start | bytes 786440 | tf_op jit(solution)/shard_map/ppermute | solution.py:599
  52.0 11.4 %collective-permute-start.21 = (f32[32,8,256]{2,1,0:T(8,128)S(1)}, f32[32,8,256]{2,1,0:T(8,128)S(1)}, u32[]{:S(2)}, u32[]{:S(2)}) collective-permute-start(f32[32,8,256]{2,1,0:T(8,128)S(1)} %get-tuple-element.293), channel_id=1, source_target_pairs={{0,6},{1,7},{2,4},{3,5},{4,2},{5,3},{6,0},{7,1},{8,14},{9,15},{10,... | collective-permute-start | bytes 786440 | tf_op jit(solution)/shard_map/ppermute | solution.py:599
  54.5 14.6 %collective-permute-start.19 = (f32[32,8,256]{2,1,0:T(8,128)S(1)}, f32[32,8,256]{2,1,0:T(8,128)S(1)}, u32[]{:S(2)}, u32[]{:S(2)}) collective-permute-start(f32[32,8,256]{2,1,0:T(8,128)S(1)} %get-tuple-element.286), channel_id=1, source_target_pairs={{0,3},{1,2},{2,1},{3,0},{4,7},{5,6},{6,5},{7,4},{8,11},{9,10},{10,... | collective-permute-start | bytes 786440 | tf_op jit(solution)/shard_map/ppermute | solution.py:599
  54.5 15.0 %collective-permute-start.16 = (f32[32,8,256]{2,1,0:T(8,128)S(1)}, f32[32,8,256]{2,1,0:T(8,128)S(1)}, u32[]{:S(2)}, u32[]{:S(2)}) collective-permute-start(f32[32,8,256]{2,1,0:T(8,128)S(1)} %get-tuple-element.279), channel_id=1, source_target_pairs={{0,4},{1,5},{2,6},{3,7},{4,0},{5,1},{6,2},{7,3},{8,12},{9,13},{10,... | collective-permute-start | bytes 786440 | tf_op jit(solution)/shard_map/ppermute | solution.py:599
  56.2 24.0 %collective-permute-start.20 = (f32[32,8,256]{2,1,0:T(8,128)S(1)}, f32[32,8,256]{2,1,0:T(8,128)S(1)}, u32[]{:S(2)}, u32[]{:S(2)}) collective-permute-start(f32[32,8,256]{2,1,0:T(8,128)S(1)} %get-tuple-element.290), channel_id=1, source_target_pairs={{0,5},{1,4},{2,7},{3,6},{4,1},{5,0},{6,3},{7,2},{8,13},{9,12},{10,... | collective-permute-start | bytes 786440 | tf_op jit(solution)/shard_map/ppermute | solution.py:599
  60.2 21.3 %collective-permute-start.22 = (f32[32,8,256]{2,1,0:T(8,128)S(1)}, f32[32,8,256]{2,1,0:T(8,128)S(1)}, u32[]{:S(2)}, u32[]{:S(2)}) collective-permute-start(f32[32,8,256]{2,1,0:T(8,128)S(1)} %get-tuple-element.296), channel_id=1, source_target_pairs={{0,7},{1,6},{2,5},{3,4},{4,3},{5,2},{6,1},{7,0},{8,15},{9,14},{10,... | collective-permute-start | bytes 786440 | tf_op jit(solution)/shard_map/ppermute | solution.py:599
  63.5 18.2 %collective-permute-start.25 = (f32[32,8,256]{2,1,0:T(8,128)S(1)}, f32[32,8,256]{2,1,0:T(8,128)S(1)}, u32[]{:S(2)}, u32[]{:S(2)}) collective-permute-start(f32[32,8,256]{2,1,0:T(8,128)S(1)} %get-tuple-element.305), channel_id=1, source_target_pairs={{0,2},{1,3},{2,0},{3,1},{4,6},{5,7},{6,4},{7,5},{8,10},{9,11},{10,... | collective-permute-start | bytes 786440 | tf_op jit(solution)/shard_map/ppermute | solution.py:599
  69.1 22.3 %collective-permute-start.23 = (f32[32,8,256]{2,1,0:T(8,128)S(1)}, f32[32,8,256]{2,1,0:T(8,128)S(1)}, u32[]{:S(2)}, u32[]{:S(2)}) collective-permute-start(f32[32,8,256]{2,1,0:T(8,128)S(1)} %get-tuple-element.301), channel_id=1, source_target_pairs={{0,4},{1,5},{2,6},{3,7},{4,0},{5,1},{6,2},{7,3},{8,12},{9,13},{10,... | collective-permute-start | bytes 786440 | tf_op jit(solution)/shard_map/ppermute | solution.py:599
  69.5 22.0 %collective-permute-start.17 = (f32[32,8,256]{2,1,0:T(8,128)S(1)}, f32[32,8,256]{2,1,0:T(8,128)S(1)}, u32[]{:S(2)}, u32[]{:S(2)}) collective-permute-start(f32[32,8,256]{2,1,0:T(8,128)S(1)} %get-tuple-element.280), channel_id=1, source_target_pairs={{0,1},{1,0},{2,3},{3,2},{4,5},{5,4},{6,7},{7,6},{8,9},{9,8},{10,11... | collective-permute-start | bytes 786440 | tf_op jit(solution)/shard_map/ppermute | solution.py:599
  80.2 11.9 %collective-permute-start.28 = (f32[32,8,256]{2,1,0:T(8,128)S(1)}, f32[32,8,256]{2,1,0:T(8,128)S(1)}, u32[]{:S(2)}, u32[]{:S(2)}) collective-permute-start(f32[32,8,256]{2,1,0:T(8,128)S(1)} %get-tuple-element.315), channel_id=1, source_target_pairs={{0,6},{1,7},{2,4},{3,5},{4,2},{5,3},{6,0},{7,1},{8,14},{9,15},{10,... | collective-permute-start | bytes 786440 | tf_op jit(solution)/shard_map/ppermute | solution.py:599
  81.6 12.3 %collective-permute-start.26 = (f32[32,8,256]{2,1,0:T(8,128)S(1)}, f32[32,8,256]{2,1,0:T(8,128)S(1)}, u32[]{:S(2)}, u32[]{:S(2)}) collective-permute-start(f32[32,8,256]{2,1,0:T(8,128)S(1)} %get-tuple-element.308), channel_id=1, source_target_pairs={{0,3},{1,2},{2,1},{3,0},{4,7},{5,6},{6,5},{7,4},{8,11},{9,10},{10,... | collective-permute-start | bytes 786440 | tf_op jit(solution)/shard_map/ppermute | solution.py:599
  81.7 18.3 %collective-permute-start.29 = (f32[32,8,256]{2,1,0:T(8,128)S(1)}, f32[32,8,256]{2,1,0:T(8,128)S(1)}, u32[]{:S(2)}, u32[]{:S(2)}) collective-permute-start(f32[32,8,256]{2,1,0:T(8,128)S(1)} %get-tuple-element.318), channel_id=1, source_target_pairs={{0,7},{1,6},{2,5},{3,4},{4,3},{5,2},{6,1},{7,0},{8,15},{9,14},{10,... | collective-permute-start | bytes 786440 | tf_op jit(solution)/shard_map/ppermute | solution.py:599
  91.4 8.6 %collective-permute-start.24 = (f32[32,8,256]{2,1,0:T(8,128)S(1)}, f32[32,8,256]{2,1,0:T(8,128)S(1)}, u32[]{:S(2)}, u32[]{:S(2)}) collective-permute-start(f32[32,8,256]{2,1,0:T(8,128)S(1)} %get-tuple-element.302), channel_id=1, source_target_pairs={{0,1},{1,0},{2,3},{3,2},{4,5},{5,4},{6,7},{7,6},{8,9},{9,8},{10,11... | collective-permute-start | bytes 786440 | tf_op jit(solution)/shard_map/ppermute | solution.py:599
  91.5 13.8 %collective-permute-start.27 = (f32[32,8,256]{2,1,0:T(8,128)S(1)}, f32[32,8,256]{2,1,0:T(8,128)S(1)}, u32[]{:S(2)}, u32[]{:S(2)}) collective-permute-start(f32[32,8,256]{2,1,0:T(8,128)S(1)} %get-tuple-element.312), channel_id=1, source_target_pairs={{0,5},{1,4},{2,7},{3,6},{4,1},{5,0},{6,3},{7,2},{8,13},{9,12},{10,... | collective-permute-start | bytes 786440 | tf_op jit(solution)/shard_map/ppermute | solution.py:599
  92.0 20.6 %collective-permute-start.35 = (f32[32,8,256]{2,1,0:T(8,128)S(1)}, f32[32,8,256]{2,1,0:T(8,128)S(1)}, u32[]{:S(2)}, u32[]{:S(2)}) collective-permute-start(f32[32,8,256]{2,1,0:T(8,128)S(1)} %get-tuple-element.341), channel_id=1, source_target_pairs={{0,2},{1,3},{2,0},{3,1},{4,6},{5,7},{6,4},{7,5},{8,10},{9,11},{10,... | collective-permute-start | bytes 786440 | tf_op jit(solution)/shard_map/ppermute | solution.py:599
  93.9 23.3 %collective-permute-start.33 = (f32[32,8,256]{2,1,0:T(8,128)S(1)}, f32[32,8,256]{2,1,0:T(8,128)S(1)}, u32[]{:S(2)}, u32[]{:S(2)}) collective-permute-start(f32[32,8,256]{2,1,0:T(8,128)S(1)} %get-tuple-element.338), channel_id=1, source_target_pairs={{0,4},{1,5},{2,6},{3,7},{4,0},{5,1},{6,2},{7,3},{8,12},{9,13},{10,... | collective-permute-start | bytes 786440 | tf_op jit(solution)/shard_map/ppermute | solution.py:599
  105.3 13.6 %collective-permute-start.30 = (f32[32,8,256]{2,1,0:T(8,128)S(1)}, f32[32,8,256]{2,1,0:T(8,128)S(1)}, u32[]{:S(2)}, u32[]{:S(2)}) collective-permute-start(f32[32,8,256]{2,1,0:T(8,128)S(1)} %get-tuple-element.325), channel_id=1, source_target_pairs={{0,6},{1,7},{2,4},{3,5},{4,2},{5,3},{6,0},{7,1},{8,14},{9,15},{10,... | collective-permute-start | bytes 786440 | tf_op jit(solution)/shard_map/ppermute | solution.py:599
  110.7 7.8 %collective-permute-start.32 = (f32[2,32,512]{2,1,0:T(8,128)S(1)}, f32[2,32,512]{2,1,0:T(8,128)S(1)}, u32[]{:S(2)}, u32[]{:S(2)}) collective-permute-start(f32[2,32,512]{2,1,0:T(8,128)S(1)} %get-tuple-element.329.own_up_ref), channel_id=1, source_target_pairs={{0,8},{8,16},{16,24},{24,0},{1,9},{9,17},{17,25},{25,1},{2,10},{10... | collective-permute-start | bytes 393224 | tf_op jit(solution)/shard_map/ppermute | solution.py:576
  112.2 18.8 %collective-permute-start.36 = (f32[32,8,256]{2,1,0:T(8,128)S(1)}, f32[32,8,256]{2,1,0:T(8,128)S(1)}, u32[]{:S(2)}, u32[]{:S(2)}) collective-permute-start(f32[32,8,256]{2,1,0:T(8,128)S(1)} %get-tuple-element.343), channel_id=1, source_target_pairs={{0,3},{1,2},{2,1},{3,0},{4,7},{5,6},{6,5},{7,4},{8,11},{9,10},{10,... | collective-permute-start | bytes 786440 | tf_op jit(solution)/shard_map/ppermute | solution.py:599
  112.7 18.3 %collective-permute-start.37 = (f32[32,8,256]{2,1,0:T(8,128)S(1)}, f32[32,8,256]{2,1,0:T(8,128)S(1)}, u32[]{:S(2)}, u32[]{:S(2)}) collective-permute-start(f32[32,8,256]{2,1,0:T(8,128)S(1)} %get-tuple-element.345), channel_id=1, source_target_pairs={{0,5},{1,4},{2,7},{3,6},{4,1},{5,0},{6,3},{7,2},{8,13},{9,12},{10,... | collective-permute-start | bytes 786440 | tf_op jit(solution)/shard_map/ppermute | solution.py:599
  117.2 13.8 %collective-permute-start.38 = (f32[32,8,256]{2,1,0:T(8,128)S(1)}, f32[32,8,256]{2,1,0:T(8,128)S(1)}, u32[]{:S(2)}, u32[]{:S(2)}) collective-permute-start(f32[32,8,256]{2,1,0:T(8,128)S(1)} %get-tuple-element.347), channel_id=1, source_target_pairs={{0,7},{1,6},{2,5},{3,4},{4,3},{5,2},{6,1},{7,0},{8,15},{9,14},{10,... | collective-permute-start | bytes 786440 | tf_op jit(solution)/shard_map/ppermute | solution.py:599
  118.5 12.4 %collective-permute-start.34 = (f32[32,8,256]{2,1,0:T(8,128)S(1)}, f32[32,8,256]{2,1,0:T(8,128)S(1)}, u32[]{:S(2)}, u32[]{:S(2)}) collective-permute-start(f32[32,8,256]{2,1,0:T(8,128)S(1)} %get-tuple-element.339), channel_id=1, source_target_pairs={{0,1},{1,0},{2,3},{3,2},{4,5},{5,4},{6,7},{7,6},{8,9},{9,8},{10,11... | collective-permute-start | bytes 786440 | tf_op jit(solution)/shard_map/ppermute | solution.py:599
  118.9 6.5 %collective-permute-start.31 = (f32[2,32,512]{2,1,0:T(8,128)S(1)}, f32[2,32,512]{2,1,0:T(8,128)S(1)}, u32[]{:S(2)}, u32[]{:S(2)}) collective-permute-start(f32[2,32,512]{2,1,0:T(8,128)S(1)} %get-tuple-element.330.own_lo_ref), channel_id=1, source_target_pairs={{8,0},{16,8},{24,16},{0,24},{9,1},{17,9},{25,17},{1,25},{10,2},{18... | collective-permute-start | bytes 393224 | tf_op jit(solution)/shard_map/ppermute | solution.py:576
  133.5 7.9 %collective-permute-start.40 = (f32[32,8,256]{2,1,0:T(8,128)S(1)}, f32[32,8,256]{2,1,0:T(8,128)S(1)}, u32[]{:S(2)}, u32[]{:S(2)}) collective-permute-start(f32[32,8,256]{2,1,0:T(8,128)S(1)} %get-tuple-element.355), channel_id=1, source_target_pairs={{0,4},{1,5},{2,6},{3,7},{4,0},{5,1},{6,2},{7,3},{8,12},{9,13},{10,... | collective-permute-start | bytes 786440 | tf_op jit(solution)/shard_map/ppermute | solution.py:599
  135.2 9.0 %collective-permute-start.39 = (f32[32,8,256]{2,1,0:T(8,128)S(1)}, f32[32,8,256]{2,1,0:T(8,128)S(1)}, u32[]{:S(2)}, u32[]{:S(2)}) collective-permute-start(f32[32,8,256]{2,1,0:T(8,128)S(1)} %get-tuple-element.350), channel_id=1, source_target_pairs={{0,2},{1,3},{2,0},{3,1},{4,6},{5,7},{6,4},{7,5},{8,10},{9,11},{10,... | collective-permute-start | bytes 786440 | tf_op jit(solution)/shard_map/ppermute | solution.py:599
  135.8 8.5 %collective-permute-start.42 = (f32[2,32,512]{2,1,0:T(8,128)S(1)}, f32[2,32,512]{2,1,0:T(8,128)S(1)}, u32[]{:S(2)}, u32[]{:S(2)}) collective-permute-start(f32[2,32,512]{2,1,0:T(8,128)S(1)} %get-tuple-element.358.own_up_ref), channel_id=1, source_target_pairs={{0,8},{8,16},{16,24},{24,0},{1,9},{9,17},{17,25},{25,1},{2,10},{10... | collective-permute-start | bytes 393224 | tf_op jit(solution)/shard_map/ppermute | solution.py:576
  136.2 8.0 %collective-permute-start.41 = (f32[2,32,512]{2,1,0:T(8,128)S(1)}, f32[2,32,512]{2,1,0:T(8,128)S(1)}, u32[]{:S(2)}, u32[]{:S(2)}) collective-permute-start(f32[2,32,512]{2,1,0:T(8,128)S(1)} %get-tuple-element.359.own_lo_ref), channel_id=1, source_target_pairs={{8,0},{16,8},{24,16},{0,24},{9,1},{17,9},{25,17},{1,25},{10,2},{18... | collective-permute-start | bytes 393224 | tf_op jit(solution)/shard_map/ppermute | solution.py:576
  140.0 11.5 %collective-permute-start.44 = (f32[32,8,256]{2,1,0:T(8,128)S(1)}, f32[32,8,256]{2,1,0:T(8,128)S(1)}, u32[]{:S(2)}, u32[]{:S(2)}) collective-permute-start(f32[32,8,256]{2,1,0:T(8,128)S(1)} %get-tuple-element.367), channel_id=1, source_target_pairs={{0,6},{1,7},{2,4},{3,5},{4,2},{5,3},{6,0},{7,1},{8,14},{9,15},{10,... | collective-permute-start | bytes 786440 | tf_op jit(solution)/shard_map/ppermute | solution.py:599
  141.3 12.4 %collective-permute-start.45 = (f32[32,8,256]{2,1,0:T(8,128)S(1)}, f32[32,8,256]{2,1,0:T(8,128)S(1)}, u32[]{:S(2)}, u32[]{:S(2)}) collective-permute-start(f32[32,8,256]{2,1,0:T(8,128)S(1)} %get-tuple-element.371), channel_id=1, source_target_pairs={{0,3},{1,2},{2,1},{3,0},{4,7},{5,6},{6,5},{7,4},{8,11},{9,10},{10,... | collective-permute-start | bytes 786440 | tf_op jit(solution)/shard_map/ppermute | solution.py:599
  144.2 13.8 %collective-permute-start.43 = (f32[32,8,256]{2,1,0:T(8,128)S(1)}, f32[32,8,256]{2,1,0:T(8,128)S(1)}, u32[]{:S(2)}, u32[]{:S(2)}) collective-permute-start(f32[32,8,256]{2,1,0:T(8,128)S(1)} %get-tuple-element.362), channel_id=1, source_target_pairs={{0,5},{1,4},{2,7},{3,6},{4,1},{5,0},{6,3},{7,2},{8,13},{9,12},{10,... | collective-permute-start | bytes 786440 | tf_op jit(solution)/shard_map/ppermute | solution.py:599
  144.2 23.2 %collective-permute-start.48 = (f32[32,8,256]{2,1,0:T(8,128)S(1)}, f32[32,8,256]{2,1,0:T(8,128)S(1)}, u32[]{:S(2)}, u32[]{:S(2)}) collective-permute-start(f32[32,8,256]{2,1,0:T(8,128)S(1)} %get-tuple-element.380), channel_id=1, source_target_pairs={{0,1},{1,0},{2,3},{3,2},{4,5},{5,4},{6,7},{7,6},{8,9},{9,8},{10,11... | collective-permute-start | bytes 786440 | tf_op jit(solution)/shard_map/ppermute | solution.py:599
  144.3 23.2 %collective-permute-start.49 = (f32[32,8,256]{2,1,0:T(8,128)S(1)}, f32[32,8,256]{2,1,0:T(8,128)S(1)}, u32[]{:S(2)}, u32[]{:S(2)}) collective-permute-start(f32[32,8,256]{2,1,0:T(8,128)S(1)} %get-tuple-element.386), channel_id=1, source_target_pairs={{0,7},{1,6},{2,5},{3,4},{4,3},{5,2},{6,1},{7,0},{8,15},{9,14},{10,... | collective-permute-start | bytes 786440 | tf_op jit(solution)/shard_map/ppermute | solution.py:599
  153.7 6.2 %collective-permute-start.46 = (f32[1,32,512]{2,1,0:T(8,128)S(1)}, f32[1,32,512]{2,1,0:T(8,128)S(1)}, u32[]{:S(2)}, u32[]{:S(2)}) collective-permute-start(f32[1,32,512]{2,1,0:T(8,128)S(1)} %get-tuple-element.372), channel_id=1, source_target_pairs={{8,0},{16,8},{24,16},{0,24},{9,1},{17,9},{25,17},{1,25},{10,2},{18... | collective-permute-start | bytes 196616 | tf_op jit(solution)/shard_map/ppermute | solution.py:576
  (13 other events, 78.9 us)

commit v12 on v9

--- a/solution.py
+++ b/solution.py
@@ -292,8 +292,8 @@
     return (1.0 - RELAXATION) * pot + inverse * (source - applied)
 
 
-def coef_block(coefs):
-    return 8 if coefs % 8 == 0 else coefs
+def coef_block(coefs, block=8):
+    return block if coefs % block == 0 else coefs
 
 
 def start_kernel(
@@ -340,7 +340,7 @@
     coefs, part, elements = z[0].shape
     nodes = len(z) * part
     shared = gather.shape[2]
-    block = coef_block(coefs)
+    block = coef_block(coefs, 16)
     field = [pl.BlockSpec((block, part, elements), lambda i: (i, 0, 0))] * len(z)
     flat = pl.BlockSpec((block * nodes, elements), lambda i: (i, 0))
     face = pl.BlockSpec((2, block, shared), lambda i: (0, i, 0))
@@ -413,7 +413,7 @@
     elements = local.shape[1]
     coefs = local.shape[0] // nodes
     shared = gather.shape[2]
-    block = coef_block(coefs)
+    block = coef_block(coefs, 16)
     flat = pl.BlockSpec((block * nodes, elements), lambda i: (i, 0))
     one = pl.BlockSpec((1, block, shared), lambda i: (0, i, 0))
     two = pl.BlockSpec((2, block, shared), lambda i: (0, i, 0))
@@ -505,7 +505,7 @@
 def add_force(position, local, got, face, geometry, dpack, scatter, mask, px, pz):
     coefs, nodes, elements = px.shape
     shared = scatter.shape[1]
-    block = coef_block(coefs)
+    block = coef_block(coefs, 16)
     flat = pl.BlockSpec((block * nodes, elements), lambda i: (i, 0))
     one = pl.BlockSpec((1, block, shared), lambda i: (0, i, 0))
     part = pl.BlockSpec((block, nodes, elements), lambda i: (i, 0, 0))

time: 165 us -> 164 us (level)
  transfers between devices with their start and end apart: 50 -> 50, of which waited for: 25 -> 26; matrix products, arithmetic and copies ran while one was open for 0% -> 0% of each run, Pallas kernels for 20% -> 19%
where the time goes in v12:
time: 164 us
  waiting for transfers between devices  64.3 us (39%)
  starting transfers between devices  58.9 us (36%)
  Pallas kernels  40.1 us (24%)
    ppermute x42, waiting for transfers between devices, send(): self.flight.append(lax.ppermute(block, 'four', pairs))  56.9 us
    ppermute x42, starting transfers between devices, send(): self.flight.append(lax.ppermute(block, 'four', pairs))  42.3 us
    ppermute x8, starting transfers between devices, swap_faces(): return (lax.ppermute(lo, 'dom', down_way), lax.ppermute(up, 'dom', up_way))  16.6 us
    pallas_call x2, Pallas kernels, two_sweeps(): pl.pallas_call(functools.partial(sweeps_kernel, block, keep), out_shape=[...  11.6 us
    ppermute x8, waiting for transfers between devices, swap_faces(): return (lax.ppermute(lo, 'dom', down_way), lax.ppermute(up, 'dom', up_way))  7.35 us
    pallas_call x3, Pallas kernels, transform(): pl.pallas_call(functools.partial(transform_kernel, count), out_shape=[jax...  7.35 us
    pallas_call x3, Pallas kernels, pack(): pl.pallas_call(pack_kernel, out_shape=[jax.ShapeDtypeStruct((per, LINE, e...  4.88 us
    pallas_call x1, Pallas kernels, finish(): pl.pallas_call(functools.partial(finish_kernel, block, len(y)), out_shape...  3.99 us
  transfers between devices with their start and end apart: 50, of which 26 were waited for; matrix products, arithmetic and copies ran while one was open for 0% of the time, Pallas kernels for 19%

profile of v12, /device:TPU:0, one launch (start us, length us, event | category | flops | bytes accessed | tf_op | source)
XLA Modules:
  0.0 163.7 jit_solution(14594048086182716447)
XLA Ops:
  0.2 2.8 %pack.4 = (f32[32,8,256]{2,1,0:T(8,128)S(1)}, f32[32,8,256]{2,1,0:T(8,128)S(1)}, f32[32,8,256]{2,1,0:T(8,128)S(1)}, f32[32,8,256]{2,1,0:T(8,128)S(1)}, f32[32,8,...) custom-call(s32[2]{0:T(128)S(1)} %pad_add_fusion.pos_ref, ...), custom_call_target="tpu_custom_call" | custom-call | bytes 4194304 | tf_op jit(solution)/shard_map/pack/pallas_call | solution.py:149
  2.9 3.0 %collective-permute-start = (f32[32,8,256]{2,1,0:T(8,128)S(1)}, f32[32,8,256]{2,1,0:T(8,128)S(1)}, u32[]{:S(2)}, u32[]{:S(2)}) collective-permute-start(f32[32,8,256]{2,1,0:T(8,128)S(1)} %get-tuple-element.204), channel_id=1, source_target_pairs={{0,4},{1,5},{2,6},{3,7},{4,0},{5,1},{6,2},{7,3},{8,12},{9,13},{10,... | collective-permute-start | bytes 786440 | tf_op jit(solution)/shard_map/ppermute | solution.py:599
  6.0 1.5 collective-permute-start.2
  8.8 2.1 %collective-permute-start.4 = (f32[2,512]{1,0:T(2,128)S(1)}, f32[2,512]{1,0:T(2,128)S(1)}, u32[]{:S(2)}, u32[]{:S(2)}) collective-permute-start(f32[2,512]{1,0:T(2,128)S(1)} %get-tuple-element.387), channel_id=1, source_target_pairs={{0,8},{8,16},{16,24},{24,0},{1,9},{9,17},{17,25},{25,1},{2,10},{10... | collective-permute-start | bytes 12296 | tf_op jit(solution)/shard_map/ppermute | solution.py:576
  10.9 2.1 %collective-permute-start.3 = (f32[2,512]{1,0:T(2,128)S(1)}, f32[2,512]{1,0:T(2,128)S(1)}, u32[]{:S(2)}, u32[]{:S(2)}) collective-permute-start(f32[2,512]{1,0:T(2,128)S(1)} %get-tuple-element.388), channel_id=1, source_target_pairs={{8,0},{16,8},{24,16},{0,24},{9,1},{17,9},{25,17},{1,25},{10,2},{18... | collective-permute-start | bytes 12296 | tf_op jit(solution)/shard_map/ppermute | solution.py:576
  13.0 1.6 collective-permute-done.4.far_lo_ref
  14.6 2.9 %collective-permute-start.6 = (f32[32,8,256]{2,1,0:T(8,128)S(1)}, f32[32,8,256]{2,1,0:T(8,128)S(1)}, u32[]{:S(2)}, u32[]{:S(2)}) collective-permute-start(f32[32,8,256]{2,1,0:T(8,128)S(1)} %get-tuple-element.217), channel_id=1, source_target_pairs={{0,5},{1,4},{2,7},{3,6},{4,1},{5,0},{6,3},{7,2},{8,13},{9,12},{10,... | collective-permute-start | bytes 786440 | tf_op jit(solution)/shard_map/ppermute | solution.py:599
  19.9 1.7 %collective-permute-start.11 = (f32[32,8,256]{2,1,0:T(8,128)S(1)}, f32[32,8,256]{2,1,0:T(8,128)S(1)}, u32[]{:S(2)}, u32[]{:S(2)}) collective-permute-start(f32[32,8,256]{2,1,0:T(8,128)S(1)} %get-tuple-element.241), channel_id=1, source_target_pairs={{0,2},{1,3},{2,0},{3,1},{4,6},{5,7},{6,4},{7,5},{8,10},{9,11},{10,... | collective-permute-start | bytes 786440 | tf_op jit(solution)/shard_map/ppermute | solution.py:599
  21.7 3.8 %collective-permute-done.5.refs_3_ = f32[32,8,256]{2,1,0:T(8,128)S(1)} collective-permute-done((f32[32,8,256]{2,1,0:T(8,128)S(1)}, f32[32,8,256]{2,1,0:T(8,128)S(1)}, u32[]{:S(2)}, u32[]{:S(2)}) %collective-permute-start.5) | collective-permute-done | bytes 262176 | tf_op jit(solution)/shard_map/ppermute | solution.py:599
  25.4 2.7 %collective-permute-start.14 = (f32[32,8,256]{2,1,0:T(8,128)S(1)}, f32[32,8,256]{2,1,0:T(8,128)S(1)}, u32[]{:S(2)}, u32[]{:S(2)}) collective-permute-start(f32[32,8,256]{2,1,0:T(8,128)S(1)} %get-tuple-element.251), channel_id=1, source_target_pairs={{0,6},{1,7},{2,4},{3,5},{4,2},{5,3},{6,0},{7,1},{8,14},{9,15},{10,... | collective-permute-start | bytes 786440 | tf_op jit(solution)/shard_map/ppermute | solution.py:599
  28.8 2.3 %collective-permute-done.8.refs_7_ = f32[32,8,256]{2,1,0:T(8,128)S(1)} collective-permute-done((f32[32,8,256]{2,1,0:T(8,128)S(1)}, f32[32,8,256]{2,1,0:T(8,128)S(1)}, u32[]{:S(2)}, u32[]{:S(2)}) %collective-permute-start.8) | collective-permute-done | bytes 262176 | tf_op jit(solution)/shard_map/ppermute | solution.py:599
  32.0 2.4 %transform.3 = (f32[32,8,256]{2,1,0:T(8,128)S(1)}, f32[32,8,256]{2,1,0:T(8,128)S(1)}, f32[32,8,256]{2,1,0:T(8,128)S(1)}, f32[32,8,256]{2,1,0:T(8,128)S(1)}, f32[...) custom-call(bf16[512,256]{1,0:T(8,128)(2,1)S(1)} %permuted_table.1.tab, ...), custom_call_target="tpu_custom_call" | custom-call | flops 805306368 | bytes 4194304 | tf_op jit(solution)/shard_map/transform/pallas_call | solution.py:122
  34.5 3.2 %collective-permute-done.11.refs_2_ = f32[32,8,256]{2,1,0:T(8,128)S(1)} collective-permute-done((f32[32,8,256]{2,1,0:T(8,128)S(1)}, f32[32,8,256]{2,1,0:T(8,128)S(1)}, u32[]{:S(2)}, u32[]{:S(2)}) %collective-permute-start.11) | collective-permute-done | bytes 262176 | tf_op jit(solution)/shard_map/ppermute | solution.py:599
  38.3 4.0 %collective-permute-done.14.refs_6_ = f32[32,8,256]{2,1,0:T(8,128)S(1)} collective-permute-done((f32[32,8,256]{2,1,0:T(8,128)S(1)}, f32[32,8,256]{2,1,0:T(8,128)S(1)}, u32[]{:S(2)}, u32[]{:S(2)}) %collective-permute-start.14) | collective-permute-done | bytes 262176 | tf_op jit(solution)/shard_map/ppermute | solution.py:599
  42.4 1.5 collective-permute-start.18
  43.9 3.7 %collective-permute-done.13.refs_5_ = f32[32,8,256]{2,1,0:T(8,128)S(1)} collective-permute-done((f32[32,8,256]{2,1,0:T(8,128)S(1)}, f32[32,8,256]{2,1,0:T(8,128)S(1)}, u32[]{:S(2)}, u32[]{:S(2)}) %collective-permute-start.13) | collective-permute-done | bytes 262176 | tf_op jit(solution)/shard_map/ppermute | solution.py:599
  47.6 3.6 %collective-permute-start.21 = (f32[32,8,256]{2,1,0:T(8,128)S(1)}, f32[32,8,256]{2,1,0:T(8,128)S(1)}, u32[]{:S(2)}, u32[]{:S(2)}) collective-permute-start(f32[32,8,256]{2,1,0:T(8,128)S(1)} %get-tuple-element.293), channel_id=1, source_target_pairs={{0,6},{1,7},{2,4},{3,5},{4,2},{5,3},{6,0},{7,1},{8,14},{9,15},{10,... | collective-permute-start | bytes 786440 | tf_op jit(solution)/shard_map/ppermute | solution.py:599
  51.2 2.4 %collective-permute-done.15.refs_7_ = f32[32,8,256]{2,1,0:T(8,128)S(1)} collective-permute-done((f32[32,8,256]{2,1,0:T(8,128)S(1)}, f32[32,8,256]{2,1,0:T(8,128)S(1)}, u32[]{:S(2)}, u32[]{:S(2)}) %collective-permute-start.15) | collective-permute-done | bytes 262176 | tf_op jit(solution)/shard_map/ppermute | solution.py:599
  56.6 2.4 %transform.4 = (f32[32,8,256]{2,1,0:T(8,128)S(1)}, f32[32,8,256]{2,1,0:T(8,128)S(1)}, f32[32,8,256]{2,1,0:T(8,128)S(1)}, f32[32,8,256]{2,1,0:T(8,128)S(1)}, f32[...) custom-call(bf16[512,256]{1,0:T(8,128)(2,1)S(1)} %permuted_table.1.tab, ...), custom_call_target="tpu_custom_call" | custom-call | flops 805306368 | bytes 4194304 | tf_op jit(solution)/shard_map/transform/pallas_call | solution.py:122
  60.2 4.7 %collective-permute-done.21.refs_6_ = f32[32,8,256]{2,1,0:T(8,128)S(1)} collective-permute-done((f32[32,8,256]{2,1,0:T(8,128)S(1)}, f32[32,8,256]{2,1,0:T(8,128)S(1)}, u32[]{:S(2)}, u32[]{:S(2)}) %collective-permute-start.21) | collective-permute-done | bytes 262176 | tf_op jit(solution)/shard_map/ppermute | solution.py:599
  64.9 1.5 collective-permute-start.25
  66.4 4.1 %collective-permute-done.19.refs_3_ = f32[32,8,256]{2,1,0:T(8,128)S(1)} collective-permute-done((f32[32,8,256]{2,1,0:T(8,128)S(1)}, f32[32,8,256]{2,1,0:T(8,128)S(1)}, u32[]{:S(2)}, u32[]{:S(2)}) %collective-permute-start.19) | collective-permute-done | bytes 262176 | tf_op jit(solution)/shard_map/ppermute | solution.py:599
  70.8 2.3 %collective-permute-start.28 = (f32[32,8,256]{2,1,0:T(8,128)S(1)}, f32[32,8,256]{2,1,0:T(8,128)S(1)}, u32[]{:S(2)}, u32[]{:S(2)}) collective-permute-start(f32[32,8,256]{2,1,0:T(8,128)S(1)} %get-tuple-element.315), channel_id=1, source_target_pairs={{0,6},{1,7},{2,4},{3,5},{4,2},{5,3},{6,0},{7,1},{8,14},{9,15},{10,... | collective-permute-start | bytes 786440 | tf_op jit(solution)/shard_map/ppermute | solution.py:599
  73.1 3.1 %collective-permute-done.22.refs_7_ = f32[32,8,256]{2,1,0:T(8,128)S(1)} collective-permute-done((f32[32,8,256]{2,1,0:T(8,128)S(1)}, f32[32,8,256]{2,1,0:T(8,128)S(1)}, u32[]{:S(2)}, u32[]{:S(2)}) %collective-permute-start.22) | collective-permute-done | bytes 262176 | tf_op jit(solution)/shard_map/ppermute | solution.py:599
  77.1 5.7 %collective-permute-done.25.refs_10_ = f32[32,8,256]{2,1,0:T(8,128)S(1)} collective-permute-done((f32[32,8,256]{2,1,0:T(8,128)S(1)}, f32[32,8,256]{2,1,0:T(8,128)S(1)}, u32[]{:S(2)}, u32[]{:S(2)}) %collective-permute-start.25) | collective-permute-done | bytes 262176 | tf_op jit(solution)/shard_map/ppermute | solution.py:599
  82.7 2.7 %collective-permute-start.27 = (f32[32,8,256]{2,1,0:T(8,128)S(1)}, f32[32,8,256]{2,1,0:T(8,128)S(1)}, u32[]{:S(2)}, u32[]{:S(2)}) collective-permute-start(f32[32,8,256]{2,1,0:T(8,128)S(1)} %get-tuple-element.312), channel_id=1, source_target_pairs={{0,5},{1,4},{2,7},{3,6},{4,1},{5,0},{6,3},{7,2},{8,13},{9,12},{10,... | collective-permute-start | bytes 786440 | tf_op jit(solution)/shard_map/ppermute | solution.py:599
  85.4 1.9 %collective-permute-done.23.refs_12_ = f32[32,8,256]{2,1,0:T(8,128)S(1)} collective-permute-done((f32[32,8,256]{2,1,0:T(8,128)S(1)}, f32[32,8,256]{2,1,0:T(8,128)S(1)}, u32[]{:S(2)}, u32[]{:S(2)}) %collective-permute-start.23) | collective-permute-done | bytes 262176 | tf_op jit(solution)/shard_map/ppermute | solution.py:599
  88.9 4.1 %collective-permute-done.26.refs_11_ = f32[32,8,256]{2,1,0:T(8,128)S(1)} collective-permute-done((f32[32,8,256]{2,1,0:T(8,128)S(1)}, f32[32,8,256]{2,1,0:T(8,128)S(1)}, u32[]{:S(2)}, u32[]{:S(2)}) %collective-permute-start.26) | collective-permute-done | bytes 262176 | tf_op jit(solution)/shard_map/ppermute | solution.py:599
  93.0 5.7 %collective-permute-done.29.refs_15_ = f32[32,8,256]{2,1,0:T(8,128)S(1)} collective-permute-done((f32[32,8,256]{2,1,0:T(8,128)S(1)}, f32[32,8,256]{2,1,0:T(8,128)S(1)}, u32[]{:S(2)}, u32[]{:S(2)}) %collective-permute-start.29) | collective-permute-done | bytes 262176 | tf_op jit(solution)/shard_map/ppermute | solution.py:599
  99.2 3.9 %start_solve.1 = (f32[2048,256]{1,0:T(8,128)S(1)}, f32[2048,256]{1,0:T(8,128)S(1)}, f32[2048,256]{1,0:T(8,128)S(1)}, f32[2,32,512]{2,1,0:T(8,128)S(1)}, f32[2,32,512]{2,1,0:T(8,128)S(1)}) custom-call(s32[2]{0:T(128)S(1)} %pad_add_fusion.pos_ref, f32[2,256]{1,0:T(2,128)S(1)} %copy-done.5, f32[7,64,256]{2,1,0:T(8,128)S(1)} %get-tuple-element.196.diag_ref.coef_ref, ...), custom_call_target="tpu_custom_call" | custom-call | flops 1000000 | bytes 100000 | tf_op jit(solution)/shard_map/start_solve/pallas_call | solution.py:348
  103.1 1.6 collective-permute-start.32
  104.7 2.3 %collective-permute-start.36 = (f32[32,8,256]{2,1,0:T(8,128)S(1)}, f32[32,8,256]{2,1,0:T(8,128)S(1)}, u32[]{:S(2)}, u32[]{:S(2)}) collective-permute-start(f32[32,8,256]{2,1,0:T(8,128)S(1)} %get-tuple-element.343), channel_id=1, source_target_pairs={{0,3},{1,2},{2,1},{3,0},{4,7},{5,6},{6,5},{7,4},{8,11},{9,10},{10,... | collective-permute-start | bytes 786440 | tf_op jit(solution)/shard_map/ppermute | solution.py:599
  107.5 2.1 %collective-permute-done.33.refs_4_ = f32[32,8,256]{2,1,0:T(8,128)S(1)} collective-permute-done((f32[32,8,256]{2,1,0:T(8,128)S(1)}, f32[32,8,256]{2,1,0:T(8,128)S(1)}, u32[]{:S(2)}, u32[]{:S(2)}) %collective-permute-start.33) | collective-permute-done | bytes 262176 | tf_op jit(solution)/shard_map/ppermute | solution.py:599
  111.2 2.3 %collective-permute-start.31 = (f32[2,32,512]{2,1,0:T(8,128)S(1)}, f32[2,32,512]{2,1,0:T(8,128)S(1)}, u32[]{:S(2)}, u32[]{:S(2)}) collective-permute-start(f32[2,32,512]{2,1,0:T(8,128)S(1)} %get-tuple-element.330.own_lo_ref), channel_id=1, source_target_pairs={{8,0},{16,8},{24,16},{0,24},{9,1},{17,9},{25,17},{1,25},{10,2},{18... | collective-permute-start | bytes 393224 | tf_op jit(solution)/shard_map/ppermute | solution.py:576
  113.4 2.8 %partial_update.1 = (f32[32,64,256]{2,1,0:T(8,128)S(1)}, f32[32,64,256]{2,1,0:T(8,128)S(1)}, f32[32,64,256]{2,1,0:T(8,128)S(1)}) custom-call(f32[7,64,256]{2,1,0:T(8,128)S(1)} %get-tuple-element.196.diag_ref.coef_ref, bf16[128,192]{1,0:T(8,128)(2,1)S(1)} %get-tuple-element.197.dpack_ref, f32[32,8,256]{2,1,0:T(8,128)S(1)} %get-tuple-element.276.refs_0_, ...), custom_call_target="tpu_custom_call" | custom-call | flops 1000000 | bytes 100000 | tf_op jit(solution)/shard_map/partial_update/pallas_call | solution.py:468
  116.6 5.5 %two_sweeps.2 = (f32[2048,256]{1,0:T(8,128)S(1)}, f32[2,32,512]{2,1,0:T(8,128)S(1)}, f32[2,32,512]{2,1,0:T(8,128)S(1)}) custom-call(s32[2]{0:T(128)S(1)} %pad_add_fusion.pos_ref, f32[2048,256]{1,0:T(8,128)S(1)} %get-tuple-element.326.local_ref, f32[2048,256]{1,0:T(8,128)S(1)} %get-tuple-element.327.source_ref, ...), custom_call_target="tpu_custom_call" | custom-call | flops 1000000 | bytes 100000 | tf_op jit(solution)/shard_map/two_sweeps/pallas_call | solution.py:422
  122.1 2.5 %transform.5 = (f32[32,8,256]{2,1,0:T(8,128)S(1)}, f32[32,8,256]{2,1,0:T(8,128)S(1)}, f32[32,8,256]{2,1,0:T(8,128)S(1)}, f32[32,8,256]{2,1,0:T(8,128)S(1)}, f32[...) custom-call(bf16[512,256]{1,0:T(8,128)(2,1)S(1)} %permuted_table.1.tab, ...), custom_call_target="tpu_custom_call" | custom-call | flops 805306368 | bytes 4194304 | tf_op jit(solution)/shard_map/transform/pallas_call | solution.py:122
  124.6 1.7 %collective-permute-start.40 = (f32[32,8,256]{2,1,0:T(8,128)S(1)}, f32[32,8,256]{2,1,0:T(8,128)S(1)}, u32[]{:S(2)}, u32[]{:S(2)}) collective-permute-start(f32[32,8,256]{2,1,0:T(8,128)S(1)} %get-tuple-element.355), channel_id=1, source_target_pairs={{0,4},{1,5},{2,6},{3,7},{4,0},{5,1},{6,2},{7,3},{8,12},{9,13},{10,... | collective-permute-start | bytes 786440 | tf_op jit(solution)/shard_map/ppermute | solution.py:599
  126.3 1.6 collective-permute-start.39
  128.3 3.9 %collective-permute-start.41 = (f32[2,32,512]{2,1,0:T(8,128)S(1)}, f32[2,32,512]{2,1,0:T(8,128)S(1)}, u32[]{:S(2)}, u32[]{:S(2)}) collective-permute-start(f32[2,32,512]{2,1,0:T(8,128)S(1)} %get-tuple-element.359.own_lo_ref), channel_id=1, source_target_pairs={{8,0},{16,8},{24,16},{0,24},{9,1},{17,9},{25,17},{1,25},{10,2},{18... | collective-permute-start | bytes 393224 | tf_op jit(solution)/shard_map/ppermute | solution.py:576
  132.8 2.3 %collective-permute-done.39.refs_2_ = f32[32,8,256]{2,1,0:T(8,128)S(1)} collective-permute-done((f32[32,8,256]{2,1,0:T(8,128)S(1)}, f32[32,8,256]{2,1,0:T(8,128)S(1)}, u32[]{:S(2)}, u32[]{:S(2)}) %collective-permute-start.39) | collective-permute-done | bytes 262176 | tf_op jit(solution)/shard_map/ppermute | solution.py:599
  136.0 2.4 %collective-permute-start.49 = (f32[32,8,256]{2,1,0:T(8,128)S(1)}, f32[32,8,256]{2,1,0:T(8,128)S(1)}, u32[]{:S(2)}, u32[]{:S(2)}) collective-permute-start(f32[32,8,256]{2,1,0:T(8,128)S(1)} %get-tuple-element.386), channel_id=1, source_target_pairs={{0,7},{1,6},{2,5},{3,4},{4,3},{5,2},{6,1},{7,0},{8,15},{9,14},{10,... | collective-permute-start | bytes 786440 | tf_op jit(solution)/shard_map/ppermute | solution.py:599
  138.4 6.1 %two_sweeps.3 = (f32[2048,256]{1,0:T(8,128)S(1)}, f32[1,32,512]{2,1,0:T(8,128)S(1)}, f32[1,32,512]{2,1,0:T(8,128)S(1)}) custom-call(s32[2]{0:T(128)S(1)} %pad_add_fusion.pos_ref, f32[2048,256]{1,0:T(8,128)S(1)} %get-tuple-element.357.local_ref, f32[2048,256]{1,0:T(8,128)S(1)} %get-tuple-element.327.source_ref, ...), custom_call_target="tpu_custom_call" | custom-call | flops 1000000 | bytes 100000 | tf_op jit(solution)/shard_map/two_sweeps/pallas_call | solution.py:422
  145.9 4.3 %collective-permute-start.46 = (f32[1,32,512]{2,1,0:T(8,128)S(1)}, f32[1,32,512]{2,1,0:T(8,128)S(1)}, u32[]{:S(2)}, u32[]{:S(2)}) collective-permute-start(f32[1,32,512]{2,1,0:T(8,128)S(1)} %get-tuple-element.372), channel_id=1, source_target_pairs={{8,0},{16,8},{24,16},{0,24},{9,1},{17,9},{25,17},{1,25},{10,2},{18... | collective-permute-start | bytes 196616 | tf_op jit(solution)/shard_map/ppermute | solution.py:576
  151.1 1.5 collective-permute-done.46.got_up_ref
  152.6 3.7 %collective-permute-done.47.got_lo_ref = f32[1,32,512]{2,1,0:T(8,128)S(1)} collective-permute-done((f32[1,32,512]{2,1,0:T(8,128)S(1)}, f32[1,32,512]{2,1,0:T(8,128)S(1)}, u32[]{:S(2)}, u32[]{:S(2)}) %collective-permute-start.47) | collective-permute-done | bytes 65568 | tf_op jit(solution)/shard_map/ppermute | solution.py:576
  156.3 3.4 %add_force.1 = (f32[3,32,64,256]{3,2,1,0:T(8,128)}, f32[32,64,256]{2,1,0:T(8,128)S(1)}) custom-call(s32[2]{0:T(128)S(1)} %pad_add_fusion.pos_ref, f32[2048,256]{1,0:T(8,128)S(1)} %get-tuple-element.363.local_ref, f32[1,32,512]{2,1,0:T(8,128)S(1)} %collective-permute-done.46.got_up_ref, f32[1,32,512]{2,1,0:T(8,128)S(1)} %collective-permute-done.47.got_lo_ref, ...), custom_call_target="tpu_custom_call" | custom-call | flops 1000000 | bytes 100000 | tf_op jit(solution)/shard_map/add_force/pallas_call | solution.py:512
  159.7 4.0 %finish.1 = f32[3,32,64,256]{3,2,1,0:T(8,128)} custom-call(s32[2]{0:T(128)S(1)} %pad_add_fusion.pos_ref, f32[7,64,256]{2,1,0:T(8,128)S(1)} %get-tuple-element.196.diag_ref.coef_ref, bf16[128,192]{1,0:T(8,128)(2,1)S(1)} %get-tuple-element.197.dpack_ref, f32[32,64,256]{2,1,0:T(8,128)S(1)} %get-tuple-element.376.px_ref, ...), custom_call_target="tpu_custom_call", output_to_operand_aliasing={{}: (5, {})} | custom-call | flops 1000000 | bytes 100000 | tf_op jit(solution)/shard_map/finish/pallas_call | solution.py:552
  (91 shorter events, 20.1 us)
Async XLA Ops:
  2.9 14.5 %collective-permute-start = (f32[32,8,256]{2,1,0:T(8,128)S(1)}, f32[32,8,256]{2,1,0:T(8,128)S(1)}, u32[]{:S(2)}, u32[]{:S(2)}) collective-permute-start(f32[32,8,256]{2,1,0:T(8,128)S(1)} %get-tuple-element.204), channel_id=1, source_target_pairs={{0,4},{1,5},{2,6},{3,7},{4,0},{5,1},{6,2},{7,3},{8,12},{9,13},{10,... | collective-permute-start | bytes 786440 | tf_op jit(solution)/shard_map/ppermute | solution.py:599
  6.0 11.5 %collective-permute-start.2 = (f32[32,8,256]{2,1,0:T(8,128)S(1)}, f32[32,8,256]{2,1,0:T(8,128)S(1)}, u32[]{:S(2)}, u32[]{:S(2)}) collective-permute-start(f32[32,8,256]{2,1,0:T(8,128)S(1)} %get-tuple-element.208), channel_id=1, source_target_pairs={{0,2},{1,3},{2,0},{3,1},{4,6},{5,7},{6,4},{7,5},{8,10},{9,11},{10,... | collective-permute-start | bytes 786440 | tf_op jit(solution)/shard_map/ppermute | solution.py:599
  7.4 12.5 %collective-permute-start.7 = (f32[32,8,256]{2,1,0:T(8,128)S(1)}, f32[32,8,256]{2,1,0:T(8,128)S(1)}, u32[]{:S(2)}, u32[]{:S(2)}) collective-permute-start(f32[32,8,256]{2,1,0:T(8,128)S(1)} %get-tuple-element.220), channel_id=1, source_target_pairs={{0,6},{1,7},{2,4},{3,5},{4,2},{5,3},{6,0},{7,1},{8,14},{9,15},{10,... | collective-permute-start | bytes 786440 | tf_op jit(solution)/shard_map/ppermute | solution.py:599
  8.8 5.7 %collective-permute-start.4 = (f32[2,512]{1,0:T(2,128)S(1)}, f32[2,512]{1,0:T(2,128)S(1)}, u32[]{:S(2)}, u32[]{:S(2)}) collective-permute-start(f32[2,512]{1,0:T(2,128)S(1)} %get-tuple-element.387), channel_id=1, source_target_pairs={{0,8},{8,16},{16,24},{24,0},{1,9},{9,17},{17,25},{25,1},{2,10},{10... | collective-permute-start | bytes 12296 | tf_op jit(solution)/shard_map/ppermute | solution.py:576
  14.5 10.9 %collective-permute-start.5 = (f32[32,8,256]{2,1,0:T(8,128)S(1)}, f32[32,8,256]{2,1,0:T(8,128)S(1)}, u32[]{:S(2)}, u32[]{:S(2)}) collective-permute-start(f32[32,8,256]{2,1,0:T(8,128)S(1)} %get-tuple-element.213), channel_id=1, source_target_pairs={{0,3},{1,2},{2,1},{3,0},{4,7},{5,6},{6,5},{7,4},{8,11},{9,10},{10,... | collective-permute-start | bytes 786440 | tf_op jit(solution)/shard_map/ppermute | solution.py:599
  14.6 10.9 %collective-permute-start.6 = (f32[32,8,256]{2,1,0:T(8,128)S(1)}, f32[32,8,256]{2,1,0:T(8,128)S(1)}, u32[]{:S(2)}, u32[]{:S(2)}) collective-permute-start(f32[32,8,256]{2,1,0:T(8,128)S(1)} %get-tuple-element.217), channel_id=1, source_target_pairs={{0,5},{1,4},{2,7},{3,6},{4,1},{5,0},{6,3},{7,2},{8,13},{9,12},{10,... | collective-permute-start | bytes 786440 | tf_op jit(solution)/shard_map/ppermute | solution.py:599
  17.5 10.7 %collective-permute-start.1 = (f32[32,8,256]{2,1,0:T(8,128)S(1)}, f32[32,8,256]{2,1,0:T(8,128)S(1)}, u32[]{:S(2)}, u32[]{:S(2)}) collective-permute-start(f32[32,8,256]{2,1,0:T(8,128)S(1)} %get-tuple-element.205), channel_id=1, source_target_pairs={{0,1},{1,0},{2,3},{3,2},{4,5},{5,4},{6,7},{7,6},{8,9},{9,8},{10,11... | collective-permute-start | bytes 786440 | tf_op jit(solution)/shard_map/ppermute | solution.py:599
  17.5 13.6 %collective-permute-start.8 = (f32[32,8,256]{2,1,0:T(8,128)S(1)}, f32[32,8,256]{2,1,0:T(8,128)S(1)}, u32[]{:S(2)}, u32[]{:S(2)}) collective-permute-start(f32[32,8,256]{2,1,0:T(8,128)S(1)} %get-tuple-element.223), channel_id=1, source_target_pairs={{0,7},{1,6},{2,5},{3,4},{4,3},{5,2},{6,1},{7,0},{8,15},{9,14},{10,... | collective-permute-start | bytes 786440 | tf_op jit(solution)/shard_map/ppermute | solution.py:599
  19.9 17.7 %collective-permute-start.11 = (f32[32,8,256]{2,1,0:T(8,128)S(1)}, f32[32,8,256]{2,1,0:T(8,128)S(1)}, u32[]{:S(2)}, u32[]{:S(2)}) collective-permute-start(f32[32,8,256]{2,1,0:T(8,128)S(1)} %get-tuple-element.241), channel_id=1, source_target_pairs={{0,2},{1,3},{2,0},{3,1},{4,6},{5,7},{6,4},{7,5},{8,10},{9,11},{10,... | collective-permute-start | bytes 786440 | tf_op jit(solution)/shard_map/ppermute | solution.py:599
  25.4 12.2 %collective-permute-start.9 = (f32[32,8,256]{2,1,0:T(8,128)S(1)}, f32[32,8,256]{2,1,0:T(8,128)S(1)}, u32[]{:S(2)}, u32[]{:S(2)}) collective-permute-start(f32[32,8,256]{2,1,0:T(8,128)S(1)} %get-tuple-element.237), channel_id=1, source_target_pairs={{0,4},{1,5},{2,6},{3,7},{4,0},{5,1},{6,2},{7,3},{8,12},{9,13},{10,... | collective-permute-start | bytes 786440 | tf_op jit(solution)/shard_map/ppermute | solution.py:599
  25.4 16.9 %collective-permute-start.14 = (f32[32,8,256]{2,1,0:T(8,128)S(1)}, f32[32,8,256]{2,1,0:T(8,128)S(1)}, u32[]{:S(2)}, u32[]{:S(2)}) collective-permute-start(f32[32,8,256]{2,1,0:T(8,128)S(1)} %get-tuple-element.251), channel_id=1, source_target_pairs={{0,6},{1,7},{2,4},{3,5},{4,2},{5,3},{6,0},{7,1},{8,14},{9,15},{10,... | collective-permute-start | bytes 786440 | tf_op jit(solution)/shard_map/ppermute | solution.py:599
  28.1 19.4 %collective-permute-start.13 = (f32[32,8,256]{2,1,0:T(8,128)S(1)}, f32[32,8,256]{2,1,0:T(8,128)S(1)}, u32[]{:S(2)}, u32[]{:S(2)}) collective-permute-start(f32[32,8,256]{2,1,0:T(8,128)S(1)} %get-tuple-element.248), channel_id=1, source_target_pairs={{0,5},{1,4},{2,7},{3,6},{4,1},{5,0},{6,3},{7,2},{8,13},{9,12},{10,... | collective-permute-start | bytes 786440 | tf_op jit(solution)/shard_map/ppermute | solution.py:599
  31.1 20.1 %collective-permute-start.12 = (f32[32,8,256]{2,1,0:T(8,128)S(1)}, f32[32,8,256]{2,1,0:T(8,128)S(1)}, u32[]{:S(2)}, u32[]{:S(2)}) collective-permute-start(f32[32,8,256]{2,1,0:T(8,128)S(1)} %get-tuple-element.244), channel_id=1, source_target_pairs={{0,3},{1,2},{2,1},{3,0},{4,7},{5,6},{6,5},{7,4},{8,11},{9,10},{10,... | collective-permute-start | bytes 786440 | tf_op jit(solution)/shard_map/ppermute | solution.py:599
  37.7 15.9 %collective-permute-start.15 = (f32[32,8,256]{2,1,0:T(8,128)S(1)}, f32[32,8,256]{2,1,0:T(8,128)S(1)}, u32[]{:S(2)}, u32[]{:S(2)}) collective-permute-start(f32[32,8,256]{2,1,0:T(8,128)S(1)} %get-tuple-element.254), channel_id=1, source_target_pairs={{0,7},{1,6},{2,5},{3,4},{4,3},{5,2},{6,1},{7,0},{8,15},{9,14},{10,... | collective-permute-start | bytes 786440 | tf_op jit(solution)/shard_map/ppermute | solution.py:599
  37.7 17.9 %collective-permute-start.10 = (f32[32,8,256]{2,1,0:T(8,128)S(1)}, f32[32,8,256]{2,1,0:T(8,128)S(1)}, u32[]{:S(2)}, u32[]{:S(2)}) collective-permute-start(f32[32,8,256]{2,1,0:T(8,128)S(1)} %get-tuple-element.238), channel_id=1, source_target_pairs={{0,1},{1,0},{2,3},{3,2},{4,5},{5,4},{6,7},{7,6},{8,9},{9,8},{10,11... | collective-permute-start | bytes 786440 | tf_op jit(solution)/shard_map/ppermute | solution.py:599
  42.4 17.8 %collective-permute-start.18 = (f32[32,8,256]{2,1,0:T(8,128)S(1)}, f32[32,8,256]{2,1,0:T(8,128)S(1)}, u32[]{:S(2)}, u32[]{:S(2)}) collective-permute-start(f32[32,8,256]{2,1,0:T(8,128)S(1)} %get-tuple-element.283), channel_id=1, source_target_pairs={{0,2},{1,3},{2,0},{3,1},{4,6},{5,7},{6,4},{7,5},{8,10},{9,11},{10,... | collective-permute-start | bytes 786440 | tf_op jit(solution)/shard_map/ppermute | solution.py:599
  47.6 17.3 %collective-permute-start.21 = (f32[32,8,256]{2,1,0:T(8,128)S(1)}, f32[32,8,256]{2,1,0:T(8,128)S(1)}, u32[]{:S(2)}, u32[]{:S(2)}) collective-permute-start(f32[32,8,256]{2,1,0:T(8,128)S(1)} %get-tuple-element.293), channel_id=1, source_target_pairs={{0,6},{1,7},{2,4},{3,5},{4,2},{5,3},{6,0},{7,1},{8,14},{9,15},{10,... | collective-permute-start | bytes 786440 | tf_op jit(solution)/shard_map/ppermute | solution.py:599
  51.2 15.2 %collective-permute-start.16 = (f32[32,8,256]{2,1,0:T(8,128)S(1)}, f32[32,8,256]{2,1,0:T(8,128)S(1)}, u32[]{:S(2)}, u32[]{:S(2)}) collective-permute-start(f32[32,8,256]{2,1,0:T(8,128)S(1)} %get-tuple-element.279), channel_id=1, source_target_pairs={{0,4},{1,5},{2,6},{3,7},{4,0},{5,1},{6,2},{7,3},{8,12},{9,13},{10,... | collective-permute-start | bytes 786440 | tf_op jit(solution)/shard_map/ppermute | solution.py:599
  53.6 16.9 %collective-permute-start.19 = (f32[32,8,256]{2,1,0:T(8,128)S(1)}, f32[32,8,256]{2,1,0:T(8,128)S(1)}, u32[]{:S(2)}, u32[]{:S(2)}) collective-permute-start(f32[32,8,256]{2,1,0:T(8,128)S(1)} %get-tuple-element.286), channel_id=1, source_target_pairs={{0,3},{1,2},{2,1},{3,0},{4,7},{5,6},{6,5},{7,4},{8,11},{9,10},{10,... | collective-permute-start | bytes 786440 | tf_op jit(solution)/shard_map/ppermute | solution.py:599
  55.6 15.2 %collective-permute-start.20 = (f32[32,8,256]{2,1,0:T(8,128)S(1)}, f32[32,8,256]{2,1,0:T(8,128)S(1)}, u32[]{:S(2)}, u32[]{:S(2)}) collective-permute-start(f32[32,8,256]{2,1,0:T(8,128)S(1)} %get-tuple-element.290), channel_id=1, source_target_pairs={{0,5},{1,4},{2,7},{3,6},{4,1},{5,0},{6,3},{7,2},{8,13},{9,12},{10,... | collective-permute-start | bytes 786440 | tf_op jit(solution)/shard_map/ppermute | solution.py:599
  60.2 16.0 %collective-permute-start.22 = (f32[32,8,256]{2,1,0:T(8,128)S(1)}, f32[32,8,256]{2,1,0:T(8,128)S(1)}, u32[]{:S(2)}, u32[]{:S(2)}) collective-permute-start(f32[32,8,256]{2,1,0:T(8,128)S(1)} %get-tuple-element.296), channel_id=1, source_target_pairs={{0,7},{1,6},{2,5},{3,4},{4,3},{5,2},{6,1},{7,0},{8,15},{9,14},{10,... | collective-permute-start | bytes 786440 | tf_op jit(solution)/shard_map/ppermute | solution.py:599
  64.9 17.9 %collective-permute-start.25 = (f32[32,8,256]{2,1,0:T(8,128)S(1)}, f32[32,8,256]{2,1,0:T(8,128)S(1)}, u32[]{:S(2)}, u32[]{:S(2)}) collective-permute-start(f32[32,8,256]{2,1,0:T(8,128)S(1)} %get-tuple-element.305), channel_id=1, source_target_pairs={{0,2},{1,3},{2,0},{3,1},{4,6},{5,7},{6,4},{7,5},{8,10},{9,11},{10,... | collective-permute-start | bytes 786440 | tf_op jit(solution)/shard_map/ppermute | solution.py:599
  66.4 16.4 %collective-permute-start.17 = (f32[32,8,256]{2,1,0:T(8,128)S(1)}, f32[32,8,256]{2,1,0:T(8,128)S(1)}, u32[]{:S(2)}, u32[]{:S(2)}) collective-permute-start(f32[32,8,256]{2,1,0:T(8,128)S(1)} %get-tuple-element.280), channel_id=1, source_target_pairs={{0,1},{1,0},{2,3},{3,2},{4,5},{5,4},{6,7},{7,6},{8,9},{9,8},{10,11... | collective-permute-start | bytes 786440 | tf_op jit(solution)/shard_map/ppermute | solution.py:599
  70.5 16.8 %collective-permute-start.23 = (f32[32,8,256]{2,1,0:T(8,128)S(1)}, f32[32,8,256]{2,1,0:T(8,128)S(1)}, u32[]{:S(2)}, u32[]{:S(2)}) collective-permute-start(f32[32,8,256]{2,1,0:T(8,128)S(1)} %get-tuple-element.301), channel_id=1, source_target_pairs={{0,4},{1,5},{2,6},{3,7},{4,0},{5,1},{6,2},{7,3},{8,12},{9,13},{10,... | collective-permute-start | bytes 786440 | tf_op jit(solution)/shard_map/ppermute | solution.py:599
  70.8 16.6 %collective-permute-start.28 = (f32[32,8,256]{2,1,0:T(8,128)S(1)}, f32[32,8,256]{2,1,0:T(8,128)S(1)}, u32[]{:S(2)}, u32[]{:S(2)}) collective-permute-start(f32[32,8,256]{2,1,0:T(8,128)S(1)} %get-tuple-element.315), channel_id=1, source_target_pairs={{0,6},{1,7},{2,4},{3,5},{4,2},{5,3},{6,0},{7,1},{8,14},{9,15},{10,... | collective-permute-start | bytes 786440 | tf_op jit(solution)/shard_map/ppermute | solution.py:599
  76.2 16.9 %collective-permute-start.26 = (f32[32,8,256]{2,1,0:T(8,128)S(1)}, f32[32,8,256]{2,1,0:T(8,128)S(1)}, u32[]{:S(2)}, u32[]{:S(2)}) collective-permute-start(f32[32,8,256]{2,1,0:T(8,128)S(1)} %get-tuple-element.308), channel_id=1, source_target_pairs={{0,3},{1,2},{2,1},{3,0},{4,7},{5,6},{6,5},{7,4},{8,11},{9,10},{10,... | collective-permute-start | bytes 786440 | tf_op jit(solution)/shard_map/ppermute | solution.py:599
  82.7 15.9 %collective-permute-start.29 = (f32[32,8,256]{2,1,0:T(8,128)S(1)}, f32[32,8,256]{2,1,0:T(8,128)S(1)}, u32[]{:S(2)}, u32[]{:S(2)}) collective-permute-start(f32[32,8,256]{2,1,0:T(8,128)S(1)} %get-tuple-element.318), channel_id=1, source_target_pairs={{0,7},{1,6},{2,5},{3,4},{4,3},{5,2},{6,1},{7,0},{8,15},{9,14},{10,... | collective-permute-start | bytes 786440 | tf_op jit(solution)/shard_map/ppermute | solution.py:599
  82.7 15.9 %collective-permute-start.27 = (f32[32,8,256]{2,1,0:T(8,128)S(1)}, f32[32,8,256]{2,1,0:T(8,128)S(1)}, u32[]{:S(2)}, u32[]{:S(2)}) collective-permute-start(f32[32,8,256]{2,1,0:T(8,128)S(1)} %get-tuple-element.312), channel_id=1, source_target_pairs={{0,5},{1,4},{2,7},{3,6},{4,1},{5,0},{6,3},{7,2},{8,13},{9,12},{10,... | collective-permute-start | bytes 786440 | tf_op jit(solution)/shard_map/ppermute | solution.py:599
  87.3 11.9 %collective-permute-start.24 = (f32[32,8,256]{2,1,0:T(8,128)S(1)}, f32[32,8,256]{2,1,0:T(8,128)S(1)}, u32[]{:S(2)}, u32[]{:S(2)}) collective-permute-start(f32[32,8,256]{2,1,0:T(8,128)S(1)} %get-tuple-element.302), channel_id=1, source_target_pairs={{0,1},{1,0},{2,3},{3,2},{4,5},{5,4},{6,7},{7,6},{8,9},{9,8},{10,11... | collective-permute-start | bytes 786440 | tf_op jit(solution)/shard_map/ppermute | solution.py:599
  87.4 19.6 %collective-permute-start.35 = (f32[32,8,256]{2,1,0:T(8,128)S(1)}, f32[32,8,256]{2,1,0:T(8,128)S(1)}, u32[]{:S(2)}, u32[]{:S(2)}) collective-permute-start(f32[32,8,256]{2,1,0:T(8,128)S(1)} %get-tuple-element.341), channel_id=1, source_target_pairs={{0,2},{1,3},{2,0},{3,1},{4,6},{5,7},{6,4},{7,5},{8,10},{9,11},{10,... | collective-permute-start | bytes 786440 | tf_op jit(solution)/shard_map/ppermute | solution.py:599
  93.0 16.6 %collective-permute-start.33 = (f32[32,8,256]{2,1,0:T(8,128)S(1)}, f32[32,8,256]{2,1,0:T(8,128)S(1)}, u32[]{:S(2)}, u32[]{:S(2)}) collective-permute-start(f32[32,8,256]{2,1,0:T(8,128)S(1)} %get-tuple-element.338), channel_id=1, source_target_pairs={{0,4},{1,5},{2,6},{3,7},{4,0},{5,1},{6,2},{7,3},{8,12},{9,13},{10,... | collective-permute-start | bytes 786440 | tf_op jit(solution)/shard_map/ppermute | solution.py:599
  98.7 12.5 %collective-permute-start.30 = (f32[32,8,256]{2,1,0:T(8,128)S(1)}, f32[32,8,256]{2,1,0:T(8,128)S(1)}, u32[]{:S(2)}, u32[]{:S(2)}) collective-permute-start(f32[32,8,256]{2,1,0:T(8,128)S(1)} %get-tuple-element.325), channel_id=1, source_target_pairs={{0,6},{1,7},{2,4},{3,5},{4,2},{5,3},{6,0},{7,1},{8,14},{9,15},{10,... | collective-permute-start | bytes 786440 | tf_op jit(solution)/shard_map/ppermute | solution.py:599
  103.1 6.8 %collective-permute-start.32 = (f32[2,32,512]{2,1,0:T(8,128)S(1)}, f32[2,32,512]{2,1,0:T(8,128)S(1)}, u32[]{:S(2)}, u32[]{:S(2)}) collective-permute-start(f32[2,32,512]{2,1,0:T(8,128)S(1)} %get-tuple-element.329.own_up_ref), channel_id=1, source_target_pairs={{0,8},{8,16},{16,24},{24,0},{1,9},{9,17},{17,25},{25,1},{2,10},{10... | collective-permute-start | bytes 393224 | tf_op jit(solution)/shard_map/ppermute | solution.py:576
  104.7 17.4 %collective-permute-start.36 = (f32[32,8,256]{2,1,0:T(8,128)S(1)}, f32[32,8,256]{2,1,0:T(8,128)S(1)}, u32[]{:S(2)}, u32[]{:S(2)}) collective-permute-start(f32[32,8,256]{2,1,0:T(8,128)S(1)} %get-tuple-element.343), channel_id=1, source_target_pairs={{0,3},{1,2},{2,1},{3,0},{4,7},{5,6},{6,5},{7,4},{8,11},{9,10},{10,... | collective-permute-start | bytes 786440 | tf_op jit(solution)/shard_map/ppermute | solution.py:599
  107.0 15.1 %collective-permute-start.37 = (f32[32,8,256]{2,1,0:T(8,128)S(1)}, f32[32,8,256]{2,1,0:T(8,128)S(1)}, u32[]{:S(2)}, u32[]{:S(2)}) collective-permute-start(f32[32,8,256]{2,1,0:T(8,128)S(1)} %get-tuple-element.345), channel_id=1, source_target_pairs={{0,5},{1,4},{2,7},{3,6},{4,1},{5,0},{6,3},{7,2},{8,13},{9,12},{10,... | collective-permute-start | bytes 786440 | tf_op jit(solution)/shard_map/ppermute | solution.py:599
  109.6 12.5 %collective-permute-start.38 = (f32[32,8,256]{2,1,0:T(8,128)S(1)}, f32[32,8,256]{2,1,0:T(8,128)S(1)}, u32[]{:S(2)}, u32[]{:S(2)}) collective-permute-start(f32[32,8,256]{2,1,0:T(8,128)S(1)} %get-tuple-element.347), channel_id=1, source_target_pairs={{0,7},{1,6},{2,5},{3,4},{4,3},{5,2},{6,1},{7,0},{8,15},{9,14},{10,... | collective-permute-start | bytes 786440 | tf_op jit(solution)/shard_map/ppermute | solution.py:599
  109.9 12.2 %collective-permute-start.34 = (f32[32,8,256]{2,1,0:T(8,128)S(1)}, f32[32,8,256]{2,1,0:T(8,128)S(1)}, u32[]{:S(2)}, u32[]{:S(2)}) collective-permute-start(f32[32,8,256]{2,1,0:T(8,128)S(1)} %get-tuple-element.339), channel_id=1, source_target_pairs={{0,1},{1,0},{2,3},{3,2},{4,5},{5,4},{6,7},{7,6},{8,9},{9,8},{10,11... | collective-permute-start | bytes 786440 | tf_op jit(solution)/shard_map/ppermute | solution.py:599
  124.6 7.9 %collective-permute-start.40 = (f32[32,8,256]{2,1,0:T(8,128)S(1)}, f32[32,8,256]{2,1,0:T(8,128)S(1)}, u32[]{:S(2)}, u32[]{:S(2)}) collective-permute-start(f32[32,8,256]{2,1,0:T(8,128)S(1)} %get-tuple-element.355), channel_id=1, source_target_pairs={{0,4},{1,5},{2,6},{3,7},{4,0},{5,1},{6,2},{7,3},{8,12},{9,13},{10,... | collective-permute-start | bytes 786440 | tf_op jit(solution)/shard_map/ppermute | solution.py:599
  126.3 8.7 %collective-permute-start.39 = (f32[32,8,256]{2,1,0:T(8,128)S(1)}, f32[32,8,256]{2,1,0:T(8,128)S(1)}, u32[]{:S(2)}, u32[]{:S(2)}) collective-permute-start(f32[32,8,256]{2,1,0:T(8,128)S(1)} %get-tuple-element.350), channel_id=1, source_target_pairs={{0,2},{1,3},{2,0},{3,1},{4,6},{5,7},{6,4},{7,5},{8,10},{9,11},{10,... | collective-permute-start | bytes 786440 | tf_op jit(solution)/shard_map/ppermute | solution.py:599
  127.9 8.1 %collective-permute-start.42 = (f32[2,32,512]{2,1,0:T(8,128)S(1)}, f32[2,32,512]{2,1,0:T(8,128)S(1)}, u32[]{:S(2)}, u32[]{:S(2)}) collective-permute-start(f32[2,32,512]{2,1,0:T(8,128)S(1)} %get-tuple-element.358.own_up_ref), channel_id=1, source_target_pairs={{0,8},{8,16},{16,24},{24,0},{1,9},{9,17},{17,25},{25,1},{2,10},{10... | collective-permute-start | bytes 393224 | tf_op jit(solution)/shard_map/ppermute | solution.py:576
  128.3 7.7 %collective-permute-start.41 = (f32[2,32,512]{2,1,0:T(8,128)S(1)}, f32[2,32,512]{2,1,0:T(8,128)S(1)}, u32[]{:S(2)}, u32[]{:S(2)}) collective-permute-start(f32[2,32,512]{2,1,0:T(8,128)S(1)} %get-tuple-element.359.own_lo_ref), channel_id=1, source_target_pairs={{8,0},{16,8},{24,16},{0,24},{9,1},{17,9},{25,17},{1,25},{10,2},{18... | collective-permute-start | bytes 393224 | tf_op jit(solution)/shard_map/ppermute | solution.py:576
  132.2 12.3 %collective-permute-start.44 = (f32[32,8,256]{2,1,0:T(8,128)S(1)}, f32[32,8,256]{2,1,0:T(8,128)S(1)}, u32[]{:S(2)}, u32[]{:S(2)}) collective-permute-start(f32[32,8,256]{2,1,0:T(8,128)S(1)} %get-tuple-element.367), channel_id=1, source_target_pairs={{0,6},{1,7},{2,4},{3,5},{4,2},{5,3},{6,0},{7,1},{8,14},{9,15},{10,... | collective-permute-start | bytes 786440 | tf_op jit(solution)/shard_map/ppermute | solution.py:599
  132.5 13.4 %collective-permute-start.45 = (f32[32,8,256]{2,1,0:T(8,128)S(1)}, f32[32,8,256]{2,1,0:T(8,128)S(1)}, u32[]{:S(2)}, u32[]{:S(2)}) collective-permute-start(f32[32,8,256]{2,1,0:T(8,128)S(1)} %get-tuple-element.371), channel_id=1, source_target_pairs={{0,3},{1,2},{2,1},{3,0},{4,7},{5,6},{6,5},{7,4},{8,11},{9,10},{10,... | collective-permute-start | bytes 786440 | tf_op jit(solution)/shard_map/ppermute | solution.py:599
  135.1 16.0 %collective-permute-start.43 = (f32[32,8,256]{2,1,0:T(8,128)S(1)}, f32[32,8,256]{2,1,0:T(8,128)S(1)}, u32[]{:S(2)}, u32[]{:S(2)}) collective-permute-start(f32[32,8,256]{2,1,0:T(8,128)S(1)} %get-tuple-element.362), channel_id=1, source_target_pairs={{0,5},{1,4},{2,7},{3,6},{4,1},{5,0},{6,3},{7,2},{8,13},{9,12},{10,... | collective-permute-start | bytes 786440 | tf_op jit(solution)/shard_map/ppermute | solution.py:599
  136.0 23.7 %collective-permute-start.48 = (f32[32,8,256]{2,1,0:T(8,128)S(1)}, f32[32,8,256]{2,1,0:T(8,128)S(1)}, u32[]{:S(2)}, u32[]{:S(2)}) collective-permute-start(f32[32,8,256]{2,1,0:T(8,128)S(1)} %get-tuple-element.380), channel_id=1, source_target_pairs={{0,1},{1,0},{2,3},{3,2},{4,5},{5,4},{6,7},{7,6},{8,9},{9,8},{10,11... | collective-permute-start | bytes 786440 | tf_op jit(solution)/shard_map/ppermute | solution.py:599
  136.0 23.7 %collective-permute-start.49 = (f32[32,8,256]{2,1,0:T(8,128)S(1)}, f32[32,8,256]{2,1,0:T(8,128)S(1)}, u32[]{:S(2)}, u32[]{:S(2)}) collective-permute-start(f32[32,8,256]{2,1,0:T(8,128)S(1)} %get-tuple-element.386), channel_id=1, source_target_pairs={{0,7},{1,6},{2,5},{3,4},{4,3},{5,2},{6,1},{7,0},{8,15},{9,14},{10,... | collective-permute-start | bytes 786440 | tf_op jit(solution)/shard_map/ppermute | solution.py:599
  145.9 6.7 %collective-permute-start.46 = (f32[1,32,512]{2,1,0:T(8,128)S(1)}, f32[1,32,512]{2,1,0:T(8,128)S(1)}, u32[]{:S(2)}, u32[]{:S(2)}) collective-permute-start(f32[1,32,512]{2,1,0:T(8,128)S(1)} %get-tuple-element.372), channel_id=1, source_target_pairs={{8,0},{16,8},{24,16},{0,24},{9,1},{17,9},{25,17},{1,25},{10,2},{18... | collective-permute-start | bytes 196616 | tf_op jit(solution)/shard_map/ppermute | solution.py:576
  150.2 6.1 %collective-permute-start.47 = (f32[1,32,512]{2,1,0:T(8,128)S(1)}, f32[1,32,512]{2,1,0:T(8,128)S(1)}, u32[]{:S(2)}, u32[]{:S(2)}) collective-permute-start(f32[1,32,512]{2,1,0:T(8,128)S(1)} %get-tuple-element.373), channel_id=1, source_target_pairs={{0,8},{8,16},{16,24},{24,0},{1,9},{9,17},{17,25},{25,1},{2,10},{10... | collective-permute-start | bytes 196616 | tf_op jit(solution)/shard_map/ppermute | solution.py:576
  (13 other events, 105.6 us)

commit v13 on v12

--- a/solution.py
+++ b/solution.py
@@ -546,7 +546,7 @@
 def finish(position, y, coef, dpack, px, py, filled):
     coefs, part, elements = y[0].shape
     nodes = len(y) * part
-    block = coef_block(coefs)
+    block = coef_block(coefs, 16)
     field = pl.BlockSpec((block, part, elements), lambda i: (i, 0, 0))
     own = pl.BlockSpec((block, nodes, elements), lambda i: (i, 0, 0))
     return pl.pallas_call(

time: 164 us -> 164 us (level)
  no operation moved by 1% of the time
where the time goes in v13:
time: 164 us; the launch traced here: 163 us
  waiting for transfers between devices  64.3 us (39%)
  starting transfers between devices  58.9 us (36%)
  Pallas kernels  39.8 us (24%)
    ppermute x42, waiting for transfers between devices, send(): self.flight.append(lax.ppermute(block, 'four', pairs))  56.9 us
    ppermute x42, starting transfers between devices, send(): self.flight.append(lax.ppermute(block, 'four', pairs))  42.3 us
    ppermute x8, starting transfers between devices, swap_faces(): return (lax.ppermute(lo, 'dom', down_way), lax.ppermute(up, 'dom', up_way))  16.6 us
    pallas_call x2, Pallas kernels, two_sweeps(): pl.pallas_call(functools.partial(sweeps_kernel, block, keep), out_shape=[...  11.6 us
    ppermute x8, waiting for transfers between devices, swap_faces(): return (lax.ppermute(lo, 'dom', down_way), lax.ppermute(up, 'dom', up_way))  7.35 us
    pallas_call x3, Pallas kernels, transform(): pl.pallas_call(functools.partial(transform_kernel, count), out_shape=[jax...  7.35 us
    pallas_call x3, Pallas kernels, pack(): pl.pallas_call(pack_kernel, out_shape=[jax.ShapeDtypeStruct((per, LINE, e...  4.88 us
    pallas_call x1, Pallas kernels, start_solve(): pl.pallas_call(functools.partial(start_kernel, block, len(z)), out_shape=...  3.89 us
  transfers between devices with their start and end apart: 50, of which 26 were waited for; matrix products, arithmetic and copies ran while one was open for 0% of the time, Pallas kernels for 19%

profile of v13, /device:TPU:0, one launch (start us, length us, event | category | flops | bytes accessed | tf_op | source)
XLA Modules:
  0.0 163.4 jit_solution(9424626401458235922)
XLA Ops:
  0.2 2.8 %pack.4 = (f32[32,8,256]{2,1,0:T(8,128)S(1)}, f32[32,8,256]{2,1,0:T(8,128)S(1)}, f32[32,8,256]{2,1,0:T(8,128)S(1)}, f32[32,8,256]{2,1,0:T(8,128)S(1)}, f32[32,8,...) custom-call(s32[2]{0:T(128)S(1)} %pad_add_fusion.pos_ref, ...), custom_call_target="tpu_custom_call" | custom-call | bytes 4194304 | tf_op jit(solution)/shard_map/pack/pallas_call | solution.py:149
  2.9 3.0 %collective-permute-start = (f32[32,8,256]{2,1,0:T(8,128)S(1)}, f32[32,8,256]{2,1,0:T(8,128)S(1)}, u32[]{:S(2)}, u32[]{:S(2)}) collective-permute-start(f32[32,8,256]{2,1,0:T(8,128)S(1)} %get-tuple-element.204), channel_id=1, source_target_pairs={{0,4},{1,5},{2,6},{3,7},{4,0},{5,1},{6,2},{7,3},{8,12},{9,13},{10,... | collective-permute-start | bytes 786440 | tf_op jit(solution)/shard_map/ppermute | solution.py:599
  6.0 1.5 collective-permute-start.2
  8.8 2.1 %collective-permute-start.4 = (f32[2,512]{1,0:T(2,128)S(1)}, f32[2,512]{1,0:T(2,128)S(1)}, u32[]{:S(2)}, u32[]{:S(2)}) collective-permute-start(f32[2,512]{1,0:T(2,128)S(1)} %get-tuple-element.387), channel_id=1, source_target_pairs={{0,8},{8,16},{16,24},{24,0},{1,9},{9,17},{17,25},{25,1},{2,10},{10... | collective-permute-start | bytes 12296 | tf_op jit(solution)/shard_map/ppermute | solution.py:576
  10.9 2.1 %collective-permute-start.3 = (f32[2,512]{1,0:T(2,128)S(1)}, f32[2,512]{1,0:T(2,128)S(1)}, u32[]{:S(2)}, u32[]{:S(2)}) collective-permute-start(f32[2,512]{1,0:T(2,128)S(1)} %get-tuple-element.388), channel_id=1, source_target_pairs={{8,0},{16,8},{24,16},{0,24},{9,1},{17,9},{25,17},{1,25},{10,2},{18... | collective-permute-start | bytes 12296 | tf_op jit(solution)/shard_map/ppermute | solution.py:576
  13.0 1.6 collective-permute-done.4.far_lo_ref
  14.6 2.9 %collective-permute-start.6 = (f32[32,8,256]{2,1,0:T(8,128)S(1)}, f32[32,8,256]{2,1,0:T(8,128)S(1)}, u32[]{:S(2)}, u32[]{:S(2)}) collective-permute-start(f32[32,8,256]{2,1,0:T(8,128)S(1)} %get-tuple-element.217), channel_id=1, source_target_pairs={{0,5},{1,4},{2,7},{3,6},{4,1},{5,0},{6,3},{7,2},{8,13},{9,12},{10,... | collective-permute-start | bytes 786440 | tf_op jit(solution)/shard_map/ppermute | solution.py:599
  19.9 1.7 %collective-permute-start.11 = (f32[32,8,256]{2,1,0:T(8,128)S(1)}, f32[32,8,256]{2,1,0:T(8,128)S(1)}, u32[]{:S(2)}, u32[]{:S(2)}) collective-permute-start(f32[32,8,256]{2,1,0:T(8,128)S(1)} %get-tuple-element.241), channel_id=1, source_target_pairs={{0,2},{1,3},{2,0},{3,1},{4,6},{5,7},{6,4},{7,5},{8,10},{9,11},{10,... | collective-permute-start | bytes 786440 | tf_op jit(solution)/shard_map/ppermute | solution.py:599
  21.7 3.8 %collective-permute-done.5.refs_3_ = f32[32,8,256]{2,1,0:T(8,128)S(1)} collective-permute-done((f32[32,8,256]{2,1,0:T(8,128)S(1)}, f32[32,8,256]{2,1,0:T(8,128)S(1)}, u32[]{:S(2)}, u32[]{:S(2)}) %collective-permute-start.5) | collective-permute-done | bytes 262176 | tf_op jit(solution)/shard_map/ppermute | solution.py:599
  25.4 2.7 %collective-permute-start.14 = (f32[32,8,256]{2,1,0:T(8,128)S(1)}, f32[32,8,256]{2,1,0:T(8,128)S(1)}, u32[]{:S(2)}, u32[]{:S(2)}) collective-permute-start(f32[32,8,256]{2,1,0:T(8,128)S(1)} %get-tuple-element.251), channel_id=1, source_target_pairs={{0,6},{1,7},{2,4},{3,5},{4,2},{5,3},{6,0},{7,1},{8,14},{9,15},{10,... | collective-permute-start | bytes 786440 | tf_op jit(solution)/shard_map/ppermute | solution.py:599
  28.8 2.3 %collective-permute-done.8.refs_7_ = f32[32,8,256]{2,1,0:T(8,128)S(1)} collective-permute-done((f32[32,8,256]{2,1,0:T(8,128)S(1)}, f32[32,8,256]{2,1,0:T(8,128)S(1)}, u32[]{:S(2)}, u32[]{:S(2)}) %collective-permute-start.8) | collective-permute-done | bytes 262176 | tf_op jit(solution)/shard_map/ppermute | solution.py:599
  32.0 2.4 %transform.3 = (f32[32,8,256]{2,1,0:T(8,128)S(1)}, f32[32,8,256]{2,1,0:T(8,128)S(1)}, f32[32,8,256]{2,1,0:T(8,128)S(1)}, f32[32,8,256]{2,1,0:T(8,128)S(1)}, f32[...) custom-call(bf16[512,256]{1,0:T(8,128)(2,1)S(1)} %permuted_table.1.tab, ...), custom_call_target="tpu_custom_call" | custom-call | flops 805306368 | bytes 4194304 | tf_op jit(solution)/shard_map/transform/pallas_call | solution.py:122
  34.5 3.2 %collective-permute-done.11.refs_2_ = f32[32,8,256]{2,1,0:T(8,128)S(1)} collective-permute-done((f32[32,8,256]{2,1,0:T(8,128)S(1)}, f32[32,8,256]{2,1,0:T(8,128)S(1)}, u32[]{:S(2)}, u32[]{:S(2)}) %collective-permute-start.11) | collective-permute-done | bytes 262176 | tf_op jit(solution)/shard_map/ppermute | solution.py:599
  38.3 4.0 %collective-permute-done.14.refs_6_ = f32[32,8,256]{2,1,0:T(8,128)S(1)} collective-permute-done((f32[32,8,256]{2,1,0:T(8,128)S(1)}, f32[32,8,256]{2,1,0:T(8,128)S(1)}, u32[]{:S(2)}, u32[]{:S(2)}) %collective-permute-start.14) | collective-permute-done | bytes 262176 | tf_op jit(solution)/shard_map/ppermute | solution.py:599
  42.4 1.5 collective-permute-start.18
  43.9 3.7 %collective-permute-done.13.refs_5_ = f32[32,8,256]{2,1,0:T(8,128)S(1)} collective-permute-done((f32[32,8,256]{2,1,0:T(8,128)S(1)}, f32[32,8,256]{2,1,0:T(8,128)S(1)}, u32[]{:S(2)}, u32[]{:S(2)}) %collective-permute-start.13) | collective-permute-done | bytes 262176 | tf_op jit(solution)/shard_map/ppermute | solution.py:599
  47.6 3.6 %collective-permute-start.21 = (f32[32,8,256]{2,1,0:T(8,128)S(1)}, f32[32,8,256]{2,1,0:T(8,128)S(1)}, u32[]{:S(2)}, u32[]{:S(2)}) collective-permute-start(f32[32,8,256]{2,1,0:T(8,128)S(1)} %get-tuple-element.293), channel_id=1, source_target_pairs={{0,6},{1,7},{2,4},{3,5},{4,2},{5,3},{6,0},{7,1},{8,14},{9,15},{10,... | collective-permute-start | bytes 786440 | tf_op jit(solution)/shard_map/ppermute | solution.py:599
  51.2 2.4 %collective-permute-done.15.refs_7_ = f32[32,8,256]{2,1,0:T(8,128)S(1)} collective-permute-done((f32[32,8,256]{2,1,0:T(8,128)S(1)}, f32[32,8,256]{2,1,0:T(8,128)S(1)}, u32[]{:S(2)}, u32[]{:S(2)}) %collective-permute-start.15) | collective-permute-done | bytes 262176 | tf_op jit(solution)/shard_map/ppermute | solution.py:599
  56.6 2.4 %transform.4 = (f32[32,8,256]{2,1,0:T(8,128)S(1)}, f32[32,8,256]{2,1,0:T(8,128)S(1)}, f32[32,8,256]{2,1,0:T(8,128)S(1)}, f32[32,8,256]{2,1,0:T(8,128)S(1)}, f32[...) custom-call(bf16[512,256]{1,0:T(8,128)(2,1)S(1)} %permuted_table.1.tab, ...), custom_call_target="tpu_custom_call" | custom-call | flops 805306368 | bytes 4194304 | tf_op jit(solution)/shard_map/transform/pallas_call | solution.py:122
  60.2 4.7 %collective-permute-done.21.refs_6_ = f32[32,8,256]{2,1,0:T(8,128)S(1)} collective-permute-done((f32[32,8,256]{2,1,0:T(8,128)S(1)}, f32[32,8,256]{2,1,0:T(8,128)S(1)}, u32[]{:S(2)}, u32[]{:S(2)}) %collective-permute-start.21) | collective-permute-done | bytes 262176 | tf_op jit(solution)/shard_map/ppermute | solution.py:599
  64.9 1.5 collective-permute-start.25
  66.4 4.1 %collective-permute-done.19.refs_3_ = f32[32,8,256]{2,1,0:T(8,128)S(1)} collective-permute-done((f32[32,8,256]{2,1,0:T(8,128)S(1)}, f32[32,8,256]{2,1,0:T(8,128)S(1)}, u32[]{:S(2)}, u32[]{:S(2)}) %collective-permute-start.19) | collective-permute-done | bytes 262176 | tf_op jit(solution)/shard_map/ppermute | solution.py:599
  70.8 2.3 %collective-permute-start.28 = (f32[32,8,256]{2,1,0:T(8,128)S(1)}, f32[32,8,256]{2,1,0:T(8,128)S(1)}, u32[]{:S(2)}, u32[]{:S(2)}) collective-permute-start(f32[32,8,256]{2,1,0:T(8,128)S(1)} %get-tuple-element.315), channel_id=1, source_target_pairs={{0,6},{1,7},{2,4},{3,5},{4,2},{5,3},{6,0},{7,1},{8,14},{9,15},{10,... | collective-permute-start | bytes 786440 | tf_op jit(solution)/shard_map/ppermute | solution.py:599
  73.1 3.1 %collective-permute-done.22.refs_7_ = f32[32,8,256]{2,1,0:T(8,128)S(1)} collective-permute-done((f32[32,8,256]{2,1,0:T(8,128)S(1)}, f32[32,8,256]{2,1,0:T(8,128)S(1)}, u32[]{:S(2)}, u32[]{:S(2)}) %collective-permute-start.22) | collective-permute-done | bytes 262176 | tf_op jit(solution)/shard_map/ppermute | solution.py:599
  77.1 5.7 %collective-permute-done.25.refs_10_ = f32[32,8,256]{2,1,0:T(8,128)S(1)} collective-permute-done((f32[32,8,256]{2,1,0:T(8,128)S(1)}, f32[32,8,256]{2,1,0:T(8,128)S(1)}, u32[]{:S(2)}, u32[]{:S(2)}) %collective-permute-start.25) | collective-permute-done | bytes 262176 | tf_op jit(solution)/shard_map/ppermute | solution.py:599
  82.7 2.7 %collective-permute-start.27 = (f32[32,8,256]{2,1,0:T(8,128)S(1)}, f32[32,8,256]{2,1,0:T(8,128)S(1)}, u32[]{:S(2)}, u32[]{:S(2)}) collective-permute-start(f32[32,8,256]{2,1,0:T(8,128)S(1)} %get-tuple-element.312), channel_id=1, source_target_pairs={{0,5},{1,4},{2,7},{3,6},{4,1},{5,0},{6,3},{7,2},{8,13},{9,12},{10,... | collective-permute-start | bytes 786440 | tf_op jit(solution)/shard_map/ppermute | solution.py:599
  85.4 1.9 %collective-permute-done.23.refs_12_ = f32[32,8,256]{2,1,0:T(8,128)S(1)} collective-permute-done((f32[32,8,256]{2,1,0:T(8,128)S(1)}, f32[32,8,256]{2,1,0:T(8,128)S(1)}, u32[]{:S(2)}, u32[]{:S(2)}) %collective-permute-start.23) | collective-permute-done | bytes 262176 | tf_op jit(solution)/shard_map/ppermute | solution.py:599
  88.9 4.1 %collective-permute-done.26.refs_11_ = f32[32,8,256]{2,1,0:T(8,128)S(1)} collective-permute-done((f32[32,8,256]{2,1,0:T(8,128)S(1)}, f32[32,8,256]{2,1,0:T(8,128)S(1)}, u32[]{:S(2)}, u32[]{:S(2)}) %collective-permute-start.26) | collective-permute-done | bytes 262176 | tf_op jit(solution)/shard_map/ppermute | solution.py:599
  93.0 5.7 %collective-permute-done.29.refs_15_ = f32[32,8,256]{2,1,0:T(8,128)S(1)} collective-permute-done((f32[32,8,256]{2,1,0:T(8,128)S(1)}, f32[32,8,256]{2,1,0:T(8,128)S(1)}, u32[]{:S(2)}, u32[]{:S(2)}) %collective-permute-start.29) | collective-permute-done | bytes 262176 | tf_op jit(solution)/shard_map/ppermute | solution.py:599
  99.2 3.9 %start_solve.1 = (f32[2048,256]{1,0:T(8,128)S(1)}, f32[2048,256]{1,0:T(8,128)S(1)}, f32[2048,256]{1,0:T(8,128)S(1)}, f32[2,32,512]{2,1,0:T(8,128)S(1)}, f32[2,32,512]{2,1,0:T(8,128)S(1)}) custom-call(s32[2]{0:T(128)S(1)} %pad_add_fusion.pos_ref, f32[2,256]{1,0:T(2,128)S(1)} %copy-done.5, f32[7,64,256]{2,1,0:T(8,128)S(1)} %get-tuple-element.196.diag_ref.coef_ref, ...), custom_call_target="tpu_custom_call" | custom-call | flops 1000000 | bytes 100000 | tf_op jit(solution)/shard_map/start_solve/pallas_call | solution.py:348
  103.1 1.6 collective-permute-start.32
  104.7 2.3 %collective-permute-start.36 = (f32[32,8,256]{2,1,0:T(8,128)S(1)}, f32[32,8,256]{2,1,0:T(8,128)S(1)}, u32[]{:S(2)}, u32[]{:S(2)}) collective-permute-start(f32[32,8,256]{2,1,0:T(8,128)S(1)} %get-tuple-element.343), channel_id=1, source_target_pairs={{0,3},{1,2},{2,1},{3,0},{4,7},{5,6},{6,5},{7,4},{8,11},{9,10},{10,... | collective-permute-start | bytes 786440 | tf_op jit(solution)/shard_map/ppermute | solution.py:599
  107.5 2.1 %collective-permute-done.33.refs_4_ = f32[32,8,256]{2,1,0:T(8,128)S(1)} collective-permute-done((f32[32,8,256]{2,1,0:T(8,128)S(1)}, f32[32,8,256]{2,1,0:T(8,128)S(1)}, u32[]{:S(2)}, u32[]{:S(2)}) %collective-permute-start.33) | collective-permute-done | bytes 262176 | tf_op jit(solution)/shard_map/ppermute | solution.py:599
  111.2 2.3 %collective-permute-start.31 = (f32[2,32,512]{2,1,0:T(8,128)S(1)}, f32[2,32,512]{2,1,0:T(8,128)S(1)}, u32[]{:S(2)}, u32[]{:S(2)}) collective-permute-start(f32[2,32,512]{2,1,0:T(8,128)S(1)} %get-tuple-element.330.own_lo_ref), channel_id=1, source_target_pairs={{8,0},{16,8},{24,16},{0,24},{9,1},{17,9},{25,17},{1,25},{10,2},{18... | collective-permute-start | bytes 393224 | tf_op jit(solution)/shard_map/ppermute | solution.py:576
  113.4 2.8 %partial_update.1 = (f32[32,64,256]{2,1,0:T(8,128)S(1)}, f32[32,64,256]{2,1,0:T(8,128)S(1)}, f32[32,64,256]{2,1,0:T(8,128)S(1)}) custom-call(f32[7,64,256]{2,1,0:T(8,128)S(1)} %get-tuple-element.196.diag_ref.coef_ref, bf16[128,192]{1,0:T(8,128)(2,1)S(1)} %get-tuple-element.197.dpack_ref, f32[32,8,256]{2,1,0:T(8,128)S(1)} %get-tuple-element.276.refs_0_, ...), custom_call_target="tpu_custom_call" | custom-call | flops 1000000 | bytes 100000 | tf_op jit(solution)/shard_map/partial_update/pallas_call | solution.py:468
  116.6 5.5 %two_sweeps.2 = (f32[2048,256]{1,0:T(8,128)S(1)}, f32[2,32,512]{2,1,0:T(8,128)S(1)}, f32[2,32,512]{2,1,0:T(8,128)S(1)}) custom-call(s32[2]{0:T(128)S(1)} %pad_add_fusion.pos_ref, f32[2048,256]{1,0:T(8,128)S(1)} %get-tuple-element.326.local_ref, f32[2048,256]{1,0:T(8,128)S(1)} %get-tuple-element.327.source_ref, ...), custom_call_target="tpu_custom_call" | custom-call | flops 1000000 | bytes 100000 | tf_op jit(solution)/shard_map/two_sweeps/pallas_call | solution.py:422
  122.1 2.5 %transform.5 = (f32[32,8,256]{2,1,0:T(8,128)S(1)}, f32[32,8,256]{2,1,0:T(8,128)S(1)}, f32[32,8,256]{2,1,0:T(8,128)S(1)}, f32[32,8,256]{2,1,0:T(8,128)S(1)}, f32[...) custom-call(bf16[512,256]{1,0:T(8,128)(2,1)S(1)} %permuted_table.1.tab, ...), custom_call_target="tpu_custom_call" | custom-call | flops 805306368 | bytes 4194304 | tf_op jit(solution)/shard_map/transform/pallas_call | solution.py:122
  124.6 1.7 %collective-permute-start.40 = (f32[32,8,256]{2,1,0:T(8,128)S(1)}, f32[32,8,256]{2,1,0:T(8,128)S(1)}, u32[]{:S(2)}, u32[]{:S(2)}) collective-permute-start(f32[32,8,256]{2,1,0:T(8,128)S(1)} %get-tuple-element.355), channel_id=1, source_target_pairs={{0,4},{1,5},{2,6},{3,7},{4,0},{5,1},{6,2},{7,3},{8,12},{9,13},{10,... | collective-permute-start | bytes 786440 | tf_op jit(solution)/shard_map/ppermute | solution.py:599
  126.3 1.6 collective-permute-start.39
  128.3 3.9 %collective-permute-start.41 = (f32[2,32,512]{2,1,0:T(8,128)S(1)}, f32[2,32,512]{2,1,0:T(8,128)S(1)}, u32[]{:S(2)}, u32[]{:S(2)}) collective-permute-start(f32[2,32,512]{2,1,0:T(8,128)S(1)} %get-tuple-element.359.own_lo_ref), channel_id=1, source_target_pairs={{8,0},{16,8},{24,16},{0,24},{9,1},{17,9},{25,17},{1,25},{10,2},{18... | collective-permute-start | bytes 393224 | tf_op jit(solution)/shard_map/ppermute | solution.py:576
  132.8 2.3 %collective-permute-done.39.refs_2_ = f32[32,8,256]{2,1,0:T(8,128)S(1)} collective-permute-done((f32[32,8,256]{2,1,0:T(8,128)S(1)}, f32[32,8,256]{2,1,0:T(8,128)S(1)}, u32[]{:S(2)}, u32[]{:S(2)}) %collective-permute-start.39) | collective-permute-done | bytes 262176 | tf_op jit(solution)/shard_map/ppermute | solution.py:599
  136.0 2.4 %collective-permute-start.49 = (f32[32,8,256]{2,1,0:T(8,128)S(1)}, f32[32,8,256]{2,1,0:T(8,128)S(1)}, u32[]{:S(2)}, u32[]{:S(2)}) collective-permute-start(f32[32,8,256]{2,1,0:T(8,128)S(1)} %get-tuple-element.386), channel_id=1, source_target_pairs={{0,7},{1,6},{2,5},{3,4},{4,3},{5,2},{6,1},{7,0},{8,15},{9,14},{10,... | collective-permute-start | bytes 786440 | tf_op jit(solution)/shard_map/ppermute | solution.py:599
  138.4 6.1 %two_sweeps.3 = (f32[2048,256]{1,0:T(8,128)S(1)}, f32[1,32,512]{2,1,0:T(8,128)S(1)}, f32[1,32,512]{2,1,0:T(8,128)S(1)}) custom-call(s32[2]{0:T(128)S(1)} %pad_add_fusion.pos_ref, f32[2048,256]{1,0:T(8,128)S(1)} %get-tuple-element.357.local_ref, f32[2048,256]{1,0:T(8,128)S(1)} %get-tuple-element.327.source_ref, ...), custom_call_target="tpu_custom_call" | custom-call | flops 1000000 | bytes 100000 | tf_op jit(solution)/shard_map/two_sweeps/pallas_call | solution.py:422
  145.9 4.3 %collective-permute-start.46 = (f32[1,32,512]{2,1,0:T(8,128)S(1)}, f32[1,32,512]{2,1,0:T(8,128)S(1)}, u32[]{:S(2)}, u32[]{:S(2)}) collective-permute-start(f32[1,32,512]{2,1,0:T(8,128)S(1)} %get-tuple-element.372), channel_id=1, source_target_pairs={{8,0},{16,8},{24,16},{0,24},{9,1},{17,9},{25,17},{1,25},{10,2},{18... | collective-permute-start | bytes 196616 | tf_op jit(solution)/shard_map/ppermute | solution.py:576
  151.1 1.5 collective-permute-done.46.got_up_ref
  152.6 3.7 %collective-permute-done.47.got_lo_ref = f32[1,32,512]{2,1,0:T(8,128)S(1)} collective-permute-done((f32[1,32,512]{2,1,0:T(8,128)S(1)}, f32[1,32,512]{2,1,0:T(8,128)S(1)}, u32[]{:S(2)}, u32[]{:S(2)}) %collective-permute-start.47) | collective-permute-done | bytes 65568 | tf_op jit(solution)/shard_map/ppermute | solution.py:576
  156.3 3.4 %add_force.1 = (f32[3,32,64,256]{3,2,1,0:T(8,128)}, f32[32,64,256]{2,1,0:T(8,128)S(1)}) custom-call(s32[2]{0:T(128)S(1)} %pad_add_fusion.pos_ref, f32[2048,256]{1,0:T(8,128)S(1)} %get-tuple-element.363.local_ref, f32[1,32,512]{2,1,0:T(8,128)S(1)} %collective-permute-done.46.got_up_ref, f32[1,32,512]{2,1,0:T(8,128)S(1)} %collective-permute-done.47.got_lo_ref, ...), custom_call_target="tpu_custom_call" | custom-call | flops 1000000 | bytes 100000 | tf_op jit(solution)/shard_map/add_force/pallas_call | solution.py:512
  159.7 3.7 %finish.1 = f32[3,32,64,256]{3,2,1,0:T(8,128)} custom-call(s32[2]{0:T(128)S(1)} %pad_add_fusion.pos_ref, f32[7,64,256]{2,1,0:T(8,128)S(1)} %get-tuple-element.196.diag_ref.coef_ref, bf16[128,192]{1,0:T(8,128)(2,1)S(1)} %get-tuple-element.197.dpack_ref, f32[32,64,256]{2,1,0:T(8,128)S(1)} %get-tuple-element.376.px_ref, ...), custom_call_target="tpu_custom_call", output_to_operand_aliasing={{}: (5, {})} | custom-call | flops 1000000 | bytes 100000 | tf_op jit(solution)/shard_map/finish/pallas_call | solution.py:552
  (91 shorter events, 20.1 us)
Async XLA Ops:
  2.9 14.5 %collective-permute-start = (f32[32,8,256]{2,1,0:T(8,128)S(1)}, f32[32,8,256]{2,1,0:T(8,128)S(1)}, u32[]{:S(2)}, u32[]{:S(2)}) collective-permute-start(f32[32,8,256]{2,1,0:T(8,128)S(1)} %get-tuple-element.204), channel_id=1, source_target_pairs={{0,4},{1,5},{2,6},{3,7},{4,0},{5,1},{6,2},{7,3},{8,12},{9,13},{10,... | collective-permute-start | bytes 786440 | tf_op jit(solution)/shard_map/ppermute | solution.py:599
  6.0 11.5 %collective-permute-start.2 = (f32[32,8,256]{2,1,0:T(8,128)S(1)}, f32[32,8,256]{2,1,0:T(8,128)S(1)}, u32[]{:S(2)}, u32[]{:S(2)}) collective-permute-start(f32[32,8,256]{2,1,0:T(8,128)S(1)} %get-tuple-element.208), channel_id=1, source_target_pairs={{0,2},{1,3},{2,0},{3,1},{4,6},{5,7},{6,4},{7,5},{8,10},{9,11},{10,... | collective-permute-start | bytes 786440 | tf_op jit(solution)/shard_map/ppermute | solution.py:599
  7.4 12.5 %collective-permute-start.7 = (f32[32,8,256]{2,1,0:T(8,128)S(1)}, f32[32,8,256]{2,1,0:T(8,128)S(1)}, u32[]{:S(2)}, u32[]{:S(2)}) collective-permute-start(f32[32,8,256]{2,1,0:T(8,128)S(1)} %get-tuple-element.220), channel_id=1, source_target_pairs={{0,6},{1,7},{2,4},{3,5},{4,2},{5,3},{6,0},{7,1},{8,14},{9,15},{10,... | collective-permute-start | bytes 786440 | tf_op jit(solution)/shard_map/ppermute | solution.py:599
  8.8 5.7 %collective-permute-start.4 = (f32[2,512]{1,0:T(2,128)S(1)}, f32[2,512]{1,0:T(2,128)S(1)}, u32[]{:S(2)}, u32[]{:S(2)}) collective-permute-start(f32[2,512]{1,0:T(2,128)S(1)} %get-tuple-element.387), channel_id=1, source_target_pairs={{0,8},{8,16},{16,24},{24,0},{1,9},{9,17},{17,25},{25,1},{2,10},{10... | collective-permute-start | bytes 12296 | tf_op jit(solution)/shard_map/ppermute | solution.py:576
  14.5 10.9 %collective-permute-start.5 = (f32[32,8,256]{2,1,0:T(8,128)S(1)}, f32[32,8,256]{2,1,0:T(8,128)S(1)}, u32[]{:S(2)}, u32[]{:S(2)}) collective-permute-start(f32[32,8,256]{2,1,0:T(8,128)S(1)} %get-tuple-element.213), channel_id=1, source_target_pairs={{0,3},{1,2},{2,1},{3,0},{4,7},{5,6},{6,5},{7,4},{8,11},{9,10},{10,... | collective-permute-start | bytes 786440 | tf_op jit(solution)/shard_map/ppermute | solution.py:599
  14.6 10.9 %collective-permute-start.6 = (f32[32,8,256]{2,1,0:T(8,128)S(1)}, f32[32,8,256]{2,1,0:T(8,128)S(1)}, u32[]{:S(2)}, u32[]{:S(2)}) collective-permute-start(f32[32,8,256]{2,1,0:T(8,128)S(1)} %get-tuple-element.217), channel_id=1, source_target_pairs={{0,5},{1,4},{2,7},{3,6},{4,1},{5,0},{6,3},{7,2},{8,13},{9,12},{10,... | collective-permute-start | bytes 786440 | tf_op jit(solution)/shard_map/ppermute | solution.py:599
  17.5 10.7 %collective-permute-start.1 = (f32[32,8,256]{2,1,0:T(8,128)S(1)}, f32[32,8,256]{2,1,0:T(8,128)S(1)}, u32[]{:S(2)}, u32[]{:S(2)}) collective-permute-start(f32[32,8,256]{2,1,0:T(8,128)S(1)} %get-tuple-element.205), channel_id=1, source_target_pairs={{0,1},{1,0},{2,3},{3,2},{4,5},{5,4},{6,7},{7,6},{8,9},{9,8},{10,11... | collective-permute-start | bytes 786440 | tf_op jit(solution)/shard_map/ppermute | solution.py:599
  17.5 13.6 %collective-permute-start.8 = (f32[32,8,256]{2,1,0:T(8,128)S(1)}, f32[32,8,256]{2,1,0:T(8,128)S(1)}, u32[]{:S(2)}, u32[]{:S(2)}) collective-permute-start(f32[32,8,256]{2,1,0:T(8,128)S(1)} %get-tuple-element.223), channel_id=1, source_target_pairs={{0,7},{1,6},{2,5},{3,4},{4,3},{5,2},{6,1},{7,0},{8,15},{9,14},{10,... | collective-permute-start | bytes 786440 | tf_op jit(solution)/shard_map/ppermute | solution.py:599
  19.9 17.7 %collective-permute-start.11 = (f32[32,8,256]{2,1,0:T(8,128)S(1)}, f32[32,8,256]{2,1,0:T(8,128)S(1)}, u32[]{:S(2)}, u32[]{:S(2)}) collective-permute-start(f32[32,8,256]{2,1,0:T(8,128)S(1)} %get-tuple-element.241), channel_id=1, source_target_pairs={{0,2},{1,3},{2,0},{3,1},{4,6},{5,7},{6,4},{7,5},{8,10},{9,11},{10,... | collective-permute-start | bytes 786440 | tf_op jit(solution)/shard_map/ppermute | solution.py:599
  25.4 12.2 %collective-permute-start.9 = (f32[32,8,256]{2,1,0:T(8,128)S(1)}, f32[32,8,256]{2,1,0:T(8,128)S(1)}, u32[]{:S(2)}, u32[]{:S(2)}) collective-permute-start(f32[32,8,256]{2,1,0:T(8,128)S(1)} %get-tuple-element.237), channel_id=1, source_target_pairs={{0,4},{1,5},{2,6},{3,7},{4,0},{5,1},{6,2},{7,3},{8,12},{9,13},{10,... | collective-permute-start | bytes 786440 | tf_op jit(solution)/shard_map/ppermute | solution.py:599
  25.4 16.9 %collective-permute-start.14 = (f32[32,8,256]{2,1,0:T(8,128)S(1)}, f32[32,8,256]{2,1,0:T(8,128)S(1)}, u32[]{:S(2)}, u32[]{:S(2)}) collective-permute-start(f32[32,8,256]{2,1,0:T(8,128)S(1)} %get-tuple-element.251), channel_id=1, source_target_pairs={{0,6},{1,7},{2,4},{3,5},{4,2},{5,3},{6,0},{7,1},{8,14},{9,15},{10,... | collective-permute-start | bytes 786440 | tf_op jit(solution)/shard_map/ppermute | solution.py:599
  28.1 19.4 %collective-permute-start.13 = (f32[32,8,256]{2,1,0:T(8,128)S(1)}, f32[32,8,256]{2,1,0:T(8,128)S(1)}, u32[]{:S(2)}, u32[]{:S(2)}) collective-permute-start(f32[32,8,256]{2,1,0:T(8,128)S(1)} %get-tuple-element.248), channel_id=1, source_target_pairs={{0,5},{1,4},{2,7},{3,6},{4,1},{5,0},{6,3},{7,2},{8,13},{9,12},{10,... | collective-permute-start | bytes 786440 | tf_op jit(solution)/shard_map/ppermute | solution.py:599
  31.1 20.1 %collective-permute-start.12 = (f32[32,8,256]{2,1,0:T(8,128)S(1)}, f32[32,8,256]{2,1,0:T(8,128)S(1)}, u32[]{:S(2)}, u32[]{:S(2)}) collective-permute-start(f32[32,8,256]{2,1,0:T(8,128)S(1)} %get-tuple-element.244), channel_id=1, source_target_pairs={{0,3},{1,2},{2,1},{3,0},{4,7},{5,6},{6,5},{7,4},{8,11},{9,10},{10,... | collective-permute-start | bytes 786440 | tf_op jit(solution)/shard_map/ppermute | solution.py:599
  37.7 15.9 %collective-permute-start.15 = (f32[32,8,256]{2,1,0:T(8,128)S(1)}, f32[32,8,256]{2,1,0:T(8,128)S(1)}, u32[]{:S(2)}, u32[]{:S(2)}) collective-permute-start(f32[32,8,256]{2,1,0:T(8,128)S(1)} %get-tuple-element.254), channel_id=1, source_target_pairs={{0,7},{1,6},{2,5},{3,4},{4,3},{5,2},{6,1},{7,0},{8,15},{9,14},{10,... | collective-permute-start | bytes 786440 | tf_op jit(solution)/shard_map/ppermute | solution.py:599
  37.7 17.9 %collective-permute-start.10 = (f32[32,8,256]{2,1,0:T(8,128)S(1)}, f32[32,8,256]{2,1,0:T(8,128)S(1)}, u32[]{:S(2)}, u32[]{:S(2)}) collective-permute-start(f32[32,8,256]{2,1,0:T(8,128)S(1)} %get-tuple-element.238), channel_id=1, source_target_pairs={{0,1},{1,0},{2,3},{3,2},{4,5},{5,4},{6,7},{7,6},{8,9},{9,8},{10,11... | collective-permute-start | bytes 786440 | tf_op jit(solution)/shard_map/ppermute | solution.py:599
  42.4 17.8 %collective-permute-start.18 = (f32[32,8,256]{2,1,0:T(8,128)S(1)}, f32[32,8,256]{2,1,0:T(8,128)S(1)}, u32[]{:S(2)}, u32[]{:S(2)}) collective-permute-start(f32[32,8,256]{2,1,0:T(8,128)S(1)} %get-tuple-element.283), channel_id=1, source_target_pairs={{0,2},{1,3},{2,0},{3,1},{4,6},{5,7},{6,4},{7,5},{8,10},{9,11},{10,... | collective-permute-start | bytes 786440 | tf_op jit(solution)/shard_map/ppermute | solution.py:599
  47.6 17.3 %collective-permute-start.21 = (f32[32,8,256]{2,1,0:T(8,128)S(1)}, f32[32,8,256]{2,1,0:T(8,128)S(1)}, u32[]{:S(2)}, u32[]{:S(2)}) collective-permute-start(f32[32,8,256]{2,1,0:T(8,128)S(1)} %get-tuple-element.293), channel_id=1, source_target_pairs={{0,6},{1,7},{2,4},{3,5},{4,2},{5,3},{6,0},{7,1},{8,14},{9,15},{10,... | collective-permute-start | bytes 786440 | tf_op jit(solution)/shard_map/ppermute | solution.py:599
  51.2 15.2 %collective-permute-start.16 = (f32[32,8,256]{2,1,0:T(8,128)S(1)}, f32[32,8,256]{2,1,0:T(8,128)S(1)}, u32[]{:S(2)}, u32[]{:S(2)}) collective-permute-start(f32[32,8,256]{2,1,0:T(8,128)S(1)} %get-tuple-element.279), channel_id=1, source_target_pairs={{0,4},{1,5},{2,6},{3,7},{4,0},{5,1},{6,2},{7,3},{8,12},{9,13},{10,... | collective-permute-start | bytes 786440 | tf_op jit(solution)/shard_map/ppermute | solution.py:599
  53.6 16.9 %collective-permute-start.19 = (f32[32,8,256]{2,1,0:T(8,128)S(1)}, f32[32,8,256]{2,1,0:T(8,128)S(1)}, u32[]{:S(2)}, u32[]{:S(2)}) collective-permute-start(f32[32,8,256]{2,1,0:T(8,128)S(1)} %get-tuple-element.286), channel_id=1, source_target_pairs={{0,3},{1,2},{2,1},{3,0},{4,7},{5,6},{6,5},{7,4},{8,11},{9,10},{10,... | collective-permute-start | bytes 786440 | tf_op jit(solution)/shard_map/ppermute | solution.py:599
  55.6 15.2 %collective-permute-start.20 = (f32[32,8,256]{2,1,0:T(8,128)S(1)}, f32[32,8,256]{2,1,0:T(8,128)S(1)}, u32[]{:S(2)}, u32[]{:S(2)}) collective-permute-start(f32[32,8,256]{2,1,0:T(8,128)S(1)} %get-tuple-element.290), channel_id=1, source_target_pairs={{0,5},{1,4},{2,7},{3,6},{4,1},{5,0},{6,3},{7,2},{8,13},{9,12},{10,... | collective-permute-start | bytes 786440 | tf_op jit(solution)/shard_map/ppermute | solution.py:599
  60.2 16.0 %collective-permute-start.22 = (f32[32,8,256]{2,1,0:T(8,128)S(1)}, f32[32,8,256]{2,1,0:T(8,128)S(1)}, u32[]{:S(2)}, u32[]{:S(2)}) collective-permute-start(f32[32,8,256]{2,1,0:T(8,128)S(1)} %get-tuple-element.296), channel_id=1, source_target_pairs={{0,7},{1,6},{2,5},{3,4},{4,3},{5,2},{6,1},{7,0},{8,15},{9,14},{10,... | collective-permute-start | bytes 786440 | tf_op jit(solution)/shard_map/ppermute | solution.py:599
  64.9 17.9 %collective-permute-start.25 = (f32[32,8,256]{2,1,0:T(8,128)S(1)}, f32[32,8,256]{2,1,0:T(8,128)S(1)}, u32[]{:S(2)}, u32[]{:S(2)}) collective-permute-start(f32[32,8,256]{2,1,0:T(8,128)S(1)} %get-tuple-element.305), channel_id=1, source_target_pairs={{0,2},{1,3},{2,0},{3,1},{4,6},{5,7},{6,4},{7,5},{8,10},{9,11},{10,... | collective-permute-start | bytes 786440 | tf_op jit(solution)/shard_map/ppermute | solution.py:599
  66.4 16.4 %collective-permute-start.17 = (f32[32,8,256]{2,1,0:T(8,128)S(1)}, f32[32,8,256]{2,1,0:T(8,128)S(1)}, u32[]{:S(2)}, u32[]{:S(2)}) collective-permute-start(f32[32,8,256]{2,1,0:T(8,128)S(1)} %get-tuple-element.280), channel_id=1, source_target_pairs={{0,1},{1,0},{2,3},{3,2},{4,5},{5,4},{6,7},{7,6},{8,9},{9,8},{10,11... | collective-permute-start | bytes 786440 | tf_op jit(solution)/shard_map/ppermute | solution.py:599
  70.5 16.8 %collective-permute-start.23 = (f32[32,8,256]{2,1,0:T(8,128)S(1)}, f32[32,8,256]{2,1,0:T(8,128)S(1)}, u32[]{:S(2)}, u32[]{:S(2)}) collective-permute-start(f32[32,8,256]{2,1,0:T(8,128)S(1)} %get-tuple-element.301), channel_id=1, source_target_pairs={{0,4},{1,5},{2,6},{3,7},{4,0},{5,1},{6,2},{7,3},{8,12},{9,13},{10,... | collective-permute-start | bytes 786440 | tf_op jit(solution)/shard_map/ppermute | solution.py:599
  70.8 16.6 %collective-permute-start.28 = (f32[32,8,256]{2,1,0:T(8,128)S(1)}, f32[32,8,256]{2,1,0:T(8,128)S(1)}, u32[]{:S(2)}, u32[]{:S(2)}) collective-permute-start(f32[32,8,256]{2,1,0:T(8,128)S(1)} %get-tuple-element.315), channel_id=1, source_target_pairs={{0,6},{1,7},{2,4},{3,5},{4,2},{5,3},{6,0},{7,1},{8,14},{9,15},{10,... | collective-permute-start | bytes 786440 | tf_op jit(solution)/shard_map/ppermute | solution.py:599
  76.2 16.9 %collective-permute-start.26 = (f32[32,8,256]{2,1,0:T(8,128)S(1)}, f32[32,8,256]{2,1,0:T(8,128)S(1)}, u32[]{:S(2)}, u32[]{:S(2)}) collective-permute-start(f32[32,8,256]{2,1,0:T(8,128)S(1)} %get-tuple-element.308), channel_id=1, source_target_pairs={{0,3},{1,2},{2,1},{3,0},{4,7},{5,6},{6,5},{7,4},{8,11},{9,10},{10,... | collective-permute-start | bytes 786440 | tf_op jit(solution)/shard_map/ppermute | solution.py:599
  82.7 15.9 %collective-permute-start.29 = (f32[32,8,256]{2,1,0:T(8,128)S(1)}, f32[32,8,256]{2,1,0:T(8,128)S(1)}, u32[]{:S(2)}, u32[]{:S(2)}) collective-permute-start(f32[32,8,256]{2,1,0:T(8,128)S(1)} %get-tuple-element.318), channel_id=1, source_target_pairs={{0,7},{1,6},{2,5},{3,4},{4,3},{5,2},{6,1},{7,0},{8,15},{9,14},{10,... | collective-permute-start | bytes 786440 | tf_op jit(solution)/shard_map/ppermute | solution.py:599
  82.7 15.9 %collective-permute-start.27 = (f32[32,8,256]{2,1,0:T(8,128)S(1)}, f32[32,8,256]{2,1,0:T(8,128)S(1)}, u32[]{:S(2)}, u32[]{:S(2)}) collective-permute-start(f32[32,8,256]{2,1,0:T(8,128)S(1)} %get-tuple-element.312), channel_id=1, source_target_pairs={{0,5},{1,4},{2,7},{3,6},{4,1},{5,0},{6,3},{7,2},{8,13},{9,12},{10,... | collective-permute-start | bytes 786440 | tf_op jit(solution)/shard_map/ppermute | solution.py:599
  87.3 11.9 %collective-permute-start.24 = (f32[32,8,256]{2,1,0:T(8,128)S(1)}, f32[32,8,256]{2,1,0:T(8,128)S(1)}, u32[]{:S(2)}, u32[]{:S(2)}) collective-permute-start(f32[32,8,256]{2,1,0:T(8,128)S(1)} %get-tuple-element.302), channel_id=1, source_target_pairs={{0,1},{1,0},{2,3},{3,2},{4,5},{5,4},{6,7},{7,6},{8,9},{9,8},{10,11... | collective-permute-start | bytes 786440 | tf_op jit(solution)/shard_map/ppermute | solution.py:599
  87.4 19.6 %collective-permute-start.35 = (f32[32,8,256]{2,1,0:T(8,128)S(1)}, f32[32,8,256]{2,1,0:T(8,128)S(1)}, u32[]{:S(2)}, u32[]{:S(2)}) collective-permute-start(f32[32,8,256]{2,1,0:T(8,128)S(1)} %get-tuple-element.341), channel_id=1, source_target_pairs={{0,2},{1,3},{2,0},{3,1},{4,6},{5,7},{6,4},{7,5},{8,10},{9,11},{10,... | collective-permute-start | bytes 786440 | tf_op jit(solution)/shard_map/ppermute | solution.py:599
  93.0 16.6 %collective-permute-start.33 = (f32[32,8,256]{2,1,0:T(8,128)S(1)}, f32[32,8,256]{2,1,0:T(8,128)S(1)}, u32[]{:S(2)}, u32[]{:S(2)}) collective-permute-start(f32[32,8,256]{2,1,0:T(8,128)S(1)} %get-tuple-element.338), channel_id=1, source_target_pairs={{0,4},{1,5},{2,6},{3,7},{4,0},{5,1},{6,2},{7,3},{8,12},{9,13},{10,... | collective-permute-start | bytes 786440 | tf_op jit(solution)/shard_map/ppermute | solution.py:599
  98.7 12.5 %collective-permute-start.30 = (f32[32,8,256]{2,1,0:T(8,128)S(1)}, f32[32,8,256]{2,1,0:T(8,128)S(1)}, u32[]{:S(2)}, u32[]{:S(2)}) collective-permute-start(f32[32,8,256]{2,1,0:T(8,128)S(1)} %get-tuple-element.325), channel_id=1, source_target_pairs={{0,6},{1,7},{2,4},{3,5},{4,2},{5,3},{6,0},{7,1},{8,14},{9,15},{10,... | collective-permute-start | bytes 786440 | tf_op jit(solution)/shard_map/ppermute | solution.py:599
  103.1 6.8 %collective-permute-start.32 = (f32[2,32,512]{2,1,0:T(8,128)S(1)}, f32[2,32,512]{2,1,0:T(8,128)S(1)}, u32[]{:S(2)}, u32[]{:S(2)}) collective-permute-start(f32[2,32,512]{2,1,0:T(8,128)S(1)} %get-tuple-element.329.own_up_ref), channel_id=1, source_target_pairs={{0,8},{8,16},{16,24},{24,0},{1,9},{9,17},{17,25},{25,1},{2,10},{10... | collective-permute-start | bytes 393224 | tf_op jit(solution)/shard_map/ppermute | solution.py:576
  104.7 17.4 %collective-permute-start.36 = (f32[32,8,256]{2,1,0:T(8,128)S(1)}, f32[32,8,256]{2,1,0:T(8,128)S(1)}, u32[]{:S(2)}, u32[]{:S(2)}) collective-permute-start(f32[32,8,256]{2,1,0:T(8,128)S(1)} %get-tuple-element.343), channel_id=1, source_target_pairs={{0,3},{1,2},{2,1},{3,0},{4,7},{5,6},{6,5},{7,4},{8,11},{9,10},{10,... | collective-permute-start | bytes 786440 | tf_op jit(solution)/shard_map/ppermute | solution.py:599
  107.0 15.1 %collective-permute-start.37 = (f32[32,8,256]{2,1,0:T(8,128)S(1)}, f32[32,8,256]{2,1,0:T(8,128)S(1)}, u32[]{:S(2)}, u32[]{:S(2)}) collective-permute-start(f32[32,8,256]{2,1,0:T(8,128)S(1)} %get-tuple-element.345), channel_id=1, source_target_pairs={{0,5},{1,4},{2,7},{3,6},{4,1},{5,0},{6,3},{7,2},{8,13},{9,12},{10,... | collective-permute-start | bytes 786440 | tf_op jit(solution)/shard_map/ppermute | solution.py:599
  109.6 12.5 %collective-permute-start.38 = (f32[32,8,256]{2,1,0:T(8,128)S(1)}, f32[32,8,256]{2,1,0:T(8,128)S(1)}, u32[]{:S(2)}, u32[]{:S(2)}) collective-permute-start(f32[32,8,256]{2,1,0:T(8,128)S(1)} %get-tuple-element.347), channel_id=1, source_target_pairs={{0,7},{1,6},{2,5},{3,4},{4,3},{5,2},{6,1},{7,0},{8,15},{9,14},{10,... | collective-permute-start | bytes 786440 | tf_op jit(solution)/shard_map/ppermute | solution.py:599
  109.9 12.2 %collective-permute-start.34 = (f32[32,8,256]{2,1,0:T(8,128)S(1)}, f32[32,8,256]{2,1,0:T(8,128)S(1)}, u32[]{:S(2)}, u32[]{:S(2)}) collective-permute-start(f32[32,8,256]{2,1,0:T(8,128)S(1)} %get-tuple-element.339), channel_id=1, source_target_pairs={{0,1},{1,0},{2,3},{3,2},{4,5},{5,4},{6,7},{7,6},{8,9},{9,8},{10,11... | collective-permute-start | bytes 786440 | tf_op jit(solution)/shard_map/ppermute | solution.py:599
  124.6 7.9 %collective-permute-start.40 = (f32[32,8,256]{2,1,0:T(8,128)S(1)}, f32[32,8,256]{2,1,0:T(8,128)S(1)}, u32[]{:S(2)}, u32[]{:S(2)}) collective-permute-start(f32[32,8,256]{2,1,0:T(8,128)S(1)} %get-tuple-element.355), channel_id=1, source_target_pairs={{0,4},{1,5},{2,6},{3,7},{4,0},{5,1},{6,2},{7,3},{8,12},{9,13},{10,... | collective-permute-start | bytes 786440 | tf_op jit(solution)/shard_map/ppermute | solution.py:599
  126.3 8.7 %collective-permute-start.39 = (f32[32,8,256]{2,1,0:T(8,128)S(1)}, f32[32,8,256]{2,1,0:T(8,128)S(1)}, u32[]{:S(2)}, u32[]{:S(2)}) collective-permute-start(f32[32,8,256]{2,1,0:T(8,128)S(1)} %get-tuple-element.350), channel_id=1, source_target_pairs={{0,2},{1,3},{2,0},{3,1},{4,6},{5,7},{6,4},{7,5},{8,10},{9,11},{10,... | collective-permute-start | bytes 786440 | tf_op jit(solution)/shard_map/ppermute | solution.py:599
  127.9 8.1 %collective-permute-start.42 = (f32[2,32,512]{2,1,0:T(8,128)S(1)}, f32[2,32,512]{2,1,0:T(8,128)S(1)}, u32[]{:S(2)}, u32[]{:S(2)}) collective-permute-start(f32[2,32,512]{2,1,0:T(8,128)S(1)} %get-tuple-element.358.own_up_ref), channel_id=1, source_target_pairs={{0,8},{8,16},{16,24},{24,0},{1,9},{9,17},{17,25},{25,1},{2,10},{10... | collective-permute-start | bytes 393224 | tf_op jit(solution)/shard_map/ppermute | solution.py:576
  128.3 7.7 %collective-permute-start.41 = (f32[2,32,512]{2,1,0:T(8,128)S(1)}, f32[2,32,512]{2,1,0:T(8,128)S(1)}, u32[]{:S(2)}, u32[]{:S(2)}) collective-permute-start(f32[2,32,512]{2,1,0:T(8,128)S(1)} %get-tuple-element.359.own_lo_ref), channel_id=1, source_target_pairs={{8,0},{16,8},{24,16},{0,24},{9,1},{17,9},{25,17},{1,25},{10,2},{18... | collective-permute-start | bytes 393224 | tf_op jit(solution)/shard_map/ppermute | solution.py:576
  132.2 12.3 %collective-permute-start.44 = (f32[32,8,256]{2,1,0:T(8,128)S(1)}, f32[32,8,256]{2,1,0:T(8,128)S(1)}, u32[]{:S(2)}, u32[]{:S(2)}) collective-permute-start(f32[32,8,256]{2,1,0:T(8,128)S(1)} %get-tuple-element.367), channel_id=1, source_target_pairs={{0,6},{1,7},{2,4},{3,5},{4,2},{5,3},{6,0},{7,1},{8,14},{9,15},{10,... | collective-permute-start | bytes 786440 | tf_op jit(solution)/shard_map/ppermute | solution.py:599
  132.5 13.4 %collective-permute-start.45 = (f32[32,8,256]{2,1,0:T(8,128)S(1)}, f32[32,8,256]{2,1,0:T(8,128)S(1)}, u32[]{:S(2)}, u32[]{:S(2)}) collective-permute-start(f32[32,8,256]{2,1,0:T(8,128)S(1)} %get-tuple-element.371), channel_id=1, source_target_pairs={{0,3},{1,2},{2,1},{3,0},{4,7},{5,6},{6,5},{7,4},{8,11},{9,10},{10,... | collective-permute-start | bytes 786440 | tf_op jit(solution)/shard_map/ppermute | solution.py:599
  135.1 16.0 %collective-permute-start.43 = (f32[32,8,256]{2,1,0:T(8,128)S(1)}, f32[32,8,256]{2,1,0:T(8,128)S(1)}, u32[]{:S(2)}, u32[]{:S(2)}) collective-permute-start(f32[32,8,256]{2,1,0:T(8,128)S(1)} %get-tuple-element.362), channel_id=1, source_target_pairs={{0,5},{1,4},{2,7},{3,6},{4,1},{5,0},{6,3},{7,2},{8,13},{9,12},{10,... | collective-permute-start | bytes 786440 | tf_op jit(solution)/shard_map/ppermute | solution.py:599
  136.0 23.7 %collective-permute-start.48 = (f32[32,8,256]{2,1,0:T(8,128)S(1)}, f32[32,8,256]{2,1,0:T(8,128)S(1)}, u32[]{:S(2)}, u32[]{:S(2)}) collective-permute-start(f32[32,8,256]{2,1,0:T(8,128)S(1)} %get-tuple-element.380), channel_id=1, source_target_pairs={{0,1},{1,0},{2,3},{3,2},{4,5},{5,4},{6,7},{7,6},{8,9},{9,8},{10,11... | collective-permute-start | bytes 786440 | tf_op jit(solution)/shard_map/ppermute | solution.py:599
  136.0 23.7 %collective-permute-start.49 = (f32[32,8,256]{2,1,0:T(8,128)S(1)}, f32[32,8,256]{2,1,0:T(8,128)S(1)}, u32[]{:S(2)}, u32[]{:S(2)}) collective-permute-start(f32[32,8,256]{2,1,0:T(8,128)S(1)} %get-tuple-element.386), channel_id=1, source_target_pairs={{0,7},{1,6},{2,5},{3,4},{4,3},{5,2},{6,1},{7,0},{8,15},{9,14},{10,... | collective-permute-start | bytes 786440 | tf_op jit(solution)/shard_map/ppermute | solution.py:599
  145.9 6.7 %collective-permute-start.46 = (f32[1,32,512]{2,1,0:T(8,128)S(1)}, f32[1,32,512]{2,1,0:T(8,128)S(1)}, u32[]{:S(2)}, u32[]{:S(2)}) collective-permute-start(f32[1,32,512]{2,1,0:T(8,128)S(1)} %get-tuple-element.372), channel_id=1, source_target_pairs={{8,0},{16,8},{24,16},{0,24},{9,1},{17,9},{25,17},{1,25},{10,2},{18... | collective-permute-start | bytes 196616 | tf_op jit(solution)/shard_map/ppermute | solution.py:576
  150.2 6.1 %collective-permute-start.47 = (f32[1,32,512]{2,1,0:T(8,128)S(1)}, f32[1,32,512]{2,1,0:T(8,128)S(1)}, u32[]{:S(2)}, u32[]{:S(2)}) collective-permute-start(f32[1,32,512]{2,1,0:T(8,128)S(1)} %get-tuple-element.373), channel_id=1, source_target_pairs={{0,8},{8,16},{16,24},{24,0},{1,9},{9,17},{17,25},{25,1},{2,10},{10... | collective-permute-start | bytes 196616 | tf_op jit(solution)/shard_map/ppermute | solution.py:576
  (13 other events, 105.6 us)
